TPU v7x, 512 devices: a whole 4x4x16 slice. The times are simulated.
512 devices in a mesh: ctx: 64 (over z_hi, y, x, core), tp: 8 (over z_lo).
Axes of the slice: x: 4, y: 4, z: 16 (z_hi: 2, z_lo: 8; z = z_hi * 8 + z_lo), core: 2. Of those that a mesh axis runs over, the one named last changes fastest.
Arguments:
- tokens_in: bfloat16 [16384, 4096], P('ctx'), may hold values from -6 to 6
- pre_gain: bfloat16 [4096], replicated, may hold values from 0.099609375 to 1.8984375
- w_in: bfloat16 [4096, 3, 2048], P('ctx', None, 'tp'), may hold values from -0.09375 to 0.09375
- w_out: bfloat16 [2048, 4096], P('ctx', 'tp'), may hold values from -0.5 to 0.5
- long_filter: bfloat16 [16384, 2048], P('ctx', 'tp'), may hold values from -0.046875 to 0.046875
- w_unembed: bfloat16 [4096, 512], P('tp'), may hold values from -0.1875 to 0.1875
- target_ids: int32 [16384], P('ctx'), may hold values from 0 to 511
- score_mask: int32 [16384], P('ctx'), may hold values 0 or 1
Outputs:
- token_logprob: float32 [16384], P('ctx')
All inputs are finite; a program needn't handle non-finite values. No bound on the sum of `score_mask` on one device may be relied on, other than what follows from the above.
Results may differ from a plain program's by a relative error of at most 0.0045.
Values may be sent and summed in bfloat16 or wider, within the bound.
No kernel may reach another device: no remote copies, remote signals or barrier semaphores. Data moves between devices by JAX's collectives and lax.ppermute only.
A program may use at most 64 MiB of HBM per device.

v0:
```python
import math

import jax
import jax.numpy as jnp
from jax import lax
from jax.sharding import PartitionSpec as P

NORM_EPS = 1e-05
EXACT = lax.Precision.HIGHEST


def phase_table(rows_n, cols_n, period):
    row_index = lax.broadcasted_iota(jnp.int32, (rows_n, cols_n), 0)
    col_index = lax.broadcasted_iota(jnp.int32, (rows_n, cols_n), 1)
    angles = (row_index * col_index % period).astype(jnp.float32) * (2.0 * math.pi / period)
    return (jnp.cos(angles), jnp.sin(angles))


def forward_spectrum(values_in, tables):
    cos_p, sin_p, cos_tw, sin_tw, cos_q, sin_q = tables
    real_a = jnp.einsum("ap,cpq->caq", cos_p, values_in, precision=EXACT)
    imag_a = -jnp.einsum("ap,cpq->caq", sin_p, values_in, precision=EXACT)
    real_b = real_a * cos_tw + imag_a * sin_tw
    imag_b = imag_a * cos_tw - real_a * sin_tw
    real_x = jnp.einsum("caq,qb->cab", real_b, cos_q, precision=EXACT) + jnp.einsum(
        "caq,qb->cab", imag_b, sin_q, precision=EXACT
    )
    imag_x = jnp.einsum("caq,qb->cab", imag_b, cos_q, precision=EXACT) - jnp.einsum(
        "caq,qb->cab", real_b, sin_q, precision=EXACT
    )
    return (real_x, imag_x)


def inverse_spectrum(real_y, imag_y, tables, total_len):
    cos_p, sin_p, cos_tw, sin_tw, cos_q, sin_q = tables
    real_z = jnp.einsum("cab,qb->caq", real_y, cos_q, precision=EXACT) - jnp.einsum(
        "cab,qb->caq", imag_y, sin_q, precision=EXACT
    )
    imag_z = jnp.einsum("cab,qb->caq", imag_y, cos_q, precision=EXACT) + jnp.einsum(
        "cab,qb->caq", real_y, sin_q, precision=EXACT
    )
    real_w = real_z * cos_tw - imag_z * sin_tw
    imag_w = imag_z * cos_tw + real_z * sin_tw
    result = jnp.einsum("ap,caq->cpq", cos_p, real_w, precision=EXACT) - jnp.einsum(
        "ap,caq->cpq", sin_p, imag_w, precision=EXACT
    )
    return result / total_len


def long_convolution(signal, kernel, ctx_count):
    seq_len, chans = signal.shape
    period_p = 4 * ctx_count
    half_rows = period_p // 2
    period_q = seq_len // half_rows
    total_len = period_p * period_q
    cos_p, sin_p = phase_table(period_p, half_rows, period_p)
    cos_tw, sin_tw = phase_table(period_p, period_q, total_len)
    cos_q, sin_q = phase_table(period_q, period_q, period_q)
    tables = (cos_p, sin_p, cos_tw, sin_tw, cos_q, sin_q)
    signal_cube = signal.astype(jnp.float32).T.reshape(chans, half_rows, period_q)
    kernel_cube = kernel.astype(jnp.float32).T.reshape(chans, half_rows, period_q)
    real_s, imag_s = forward_spectrum(signal_cube, tables)
    real_k, imag_k = forward_spectrum(kernel_cube, tables)
    real_y = real_s * real_k - imag_s * imag_k
    imag_y = real_s * imag_k + imag_s * real_k
    result = inverse_spectrum(real_y, imag_y, tables, total_len)
    return result.reshape(chans, seq_len).T


def per_device(tokens_in, pre_gain, w_in, w_out, long_filter, w_unembed, target_ids, score_mask):
    ctx_count = lax.axis_size("ctx")
    stream = tokens_in.astype(jnp.float32)
    scale = lax.rsqrt(jnp.mean(stream * stream, axis=1, keepdims=True) + NORM_EPS)
    normed = (stream * scale * pre_gain.astype(jnp.float32)).astype(jnp.bfloat16)
    rows_here = normed.shape[0]
    block = normed
    proj = jnp.einsum(
        "td,dgc->tgc",
        block,
        lax.all_gather(w_in, "ctx", axis=0, tiled=True),
        preferred_element_type=jnp.float32,
    ).astype(jnp.bfloat16)
    gate_out = proj[:, 0].astype(jnp.float32)
    gated = (proj[:, 1].astype(jnp.float32) * proj[:, 2].astype(jnp.float32)).astype(jnp.bfloat16)
    signal, kernel = (
        lax.all_to_all(gated, "ctx", split_axis=1, concat_axis=0, tiled=True),
        lax.all_to_all(long_filter, "ctx", split_axis=1, concat_axis=0, tiled=True),
    )
    conv_chan = long_convolution(signal, kernel, ctx_count).astype(jnp.bfloat16)
    conv_tok = lax.all_to_all(conv_chan, "ctx", split_axis=0, concat_axis=1, tiled=True)
    mixed = (gate_out * conv_tok.astype(jnp.float32)).astype(jnp.bfloat16)
    mixed_full = lax.all_gather(mixed, "tp", axis=1, tiled=True)
    width_here = w_out.shape[1]
    block = mixed_full
    out = jnp.dot(
        block, lax.all_gather(w_out, "ctx", axis=0, tiled=True), preferred_element_type=jnp.float32
    ).astype(jnp.bfloat16)
    width_start = lax.axis_index("tp") * width_here
    stream_slice = lax.dynamic_slice_in_dim(tokens_in, width_start, width_here, 1).astype(
        jnp.float32
    )
    resid = (stream_slice + out.astype(jnp.float32)).astype(jnp.bfloat16)
    partial_logits = jnp.dot(resid, w_unembed, preferred_element_type=jnp.float32)
    vocab_all = partial_logits.shape[1]
    weight_mask = score_mask.astype(jnp.float32)
    logits = lax.psum(partial_logits, "tp")
    row_top = jnp.max(logits, axis=1)
    log_total = row_top + jnp.log(jnp.sum(jnp.exp(logits - row_top[:, None]), axis=1))
    vocab_index = lax.broadcasted_iota(jnp.int32, (rows_here, vocab_all), 1)
    picked = jnp.sum(jnp.where(vocab_index == target_ids[:, None], logits, 0.0), axis=1)
    return (picked - log_total) * weight_mask


def solution(mesh):
    return jax.shard_map(
        per_device,
        mesh=mesh,
        in_specs=(
            P("ctx", None),
            P(),
            P("ctx", None, "tp"),
            P("ctx", "tp"),
            P("ctx", "tp"),
            P("tp", None),
            P("ctx"),
            P("ctx"),
        ),
        out_specs=P("ctx"),
        check_vma=False,
    )
```

profile of v0, /device:TPU:6, one launch (start us, length us, event | category | flops | bytes accessed | tf_op | source)
XLA Modules:
  0.0 471.3 jit_solution(7691614836793345126)
XLA Ops:
  7.3 1.0 copy.42
  9.0 21.2 %all-to-all-start.1 = ((bf16[256,64,4]{0,2,1:T(4,128)(2,1)}), bf16[256,64,4]{0,2,1:T(4,128)(2,1)S(1)}, u32[]{:S(2)}, u32[]{:S(2)}) async-start(bf16[256,64,4]{0,2,1:T(4,128)(2,1)} %all_to_all.39), calls=%async_computation.1 | async-start | bytes 262144 | tf_op jit(solution)/shard_map/all_to_all | solution.py:87
  32.4 2.1 fusion
  34.5 11.7 %all-to-all-done.1 = bf16[256,64,4]{0,2,1:T(4,128)(2,1)S(1)} async-done(((bf16[256,64,4]{0,2,1:T(4,128)(2,1)}), bf16[256,64,4]{0,2,1:T(4,128)(2,1)S(1)}, u32[]{:S(2)}, u32[]{:S(2)}) %all-to-all-start.1) | async-done | bytes 131104 | tf_op jit(solution)/shard_map/all_to_all | solution.py:87
  47.8 0.8 fusion.23
  48.6 0.8 convolution_add_fusion.1
  49.4 120.6 %all-gather.4.cloned.1.call-done = bf16[4096,3,256]{2,0,1:T(8,128)(2,1)} async-done(((bf16[64,3,256]{2,0,1:T(8,128)(2,1)}), bf16[4096,3,256]{2,0,1:T(8,128)(2,1)}) %all-gather.4.cloned.1.call-update) | async-done | bytes 6291472 | tf_op jit(solution)/shard_map/all_gather | solution.py:80
  170.0 6.1 %fusion.8 = bf16[256,3,256]{0,2,1:T(8,128)(2,1)S(1)} fusion(bf16[4096,3,256]{2,0,1:T(8,128)(2,1)} %all-gather.4.cloned.1.call-done, bf16[256,4096]{1,0:T(8,128)(2,1)} %param.8, f32[4096]{0:T(1024)S(1)} %convert_element_type.148, f32[256]{0:T(256)S(1)} %add_rsqrt_fusion), kind=kOutput, calls=%fused_computation.9 | convolution fusion | flops 1615003648 | bytes 8799232 | tf_op jit(solution)/shard_map/td,dgc->tgc/dot_general | solution.py:77
  177.6 7.2 %all-to-all-start = ((bf16[256,64,4]{0,2,1:T(4,128)(2,1)}), bf16[256,64,4]{0,2,1:T(4,128)(2,1)S(1)}, u32[]{:S(2)}, u32[]{:S(2)}) async-start(bf16[256,64,4]{0,2,1:T(4,128)(2,1)} %convert_element_type.156), calls=%async_computation | async-start | bytes 262144 | tf_op jit(solution)/shard_map/all_to_all | solution.py:86
  185.0 0.8 fusion.19
  185.8 0.8 convolution_subtract_fusion.1
  186.7 15.5 %all-to-all-done = bf16[256,64,4]{0,2,1:T(4,128)(2,1)S(1)} async-done(((bf16[256,64,4]{0,2,1:T(4,128)(2,1)}), bf16[256,64,4]{0,2,1:T(4,128)(2,1)S(1)}, u32[]{:S(2)}, u32[]{:S(2)}) %all-to-all-start) | async-done | bytes 131104 | tf_op jit(solution)/shard_map/all_to_all | solution.py:86
  202.2 0.9 convolution_bitcast_fusion
  203.1 0.9 fusion.11
  204.0 1.2 fusion.82
  205.2 1.2 fusion.79
  206.4 1.2 convolution_add_fusion.2
  207.6 1.2 multiply_subtract_fusion
  208.9 0.9 fusion.76
  209.8 0.9 fusion.74
  210.6 0.9 convolution_subtract_fusion
  211.5 0.9 convolution_add_fusion
  212.4 1.3 fusion.28
  213.7 1.1 fusion.18
  215.1 22.3 %all_to_all.48 = bf16[64,256,4]{1,2,0:T(4,128)(2,1)S(1)} all-to-all(bf16[64,256,4]{1,2,0:T(4,128)(2,1)S(1)} %bitcast.118), channel_id=1, replica_groups=mesh['ctx'=64,'tp'=8] {'ctx'}, dimensions={0} | all-to-all | bytes 262144 | tf_op jit(solution)/shard_map/all_to_all | solution.py:90
  237.6 1.6 fusion.33
  239.2 41.4 %all-gather.8.cloned.1.call-done = bf16[2048,512]{1,0:T(8,128)(2,1)} async-done(((bf16[32,512]{1,0:T(8,128)(2,1)}), bf16[2048,512]{1,0:T(8,128)(2,1)}) %all-gather.8.cloned.1.call-update) | async-done | bytes 2097168 | tf_op jit(solution)/shard_map/all_gather | solution.py:96
  280.6 60.2 %all-gather.6.cloned.1.call-done = bf16[256,2048]{0,1:T(8,128)(2,1)} async-done(((bf16[256,256]{0,1:T(8,128)(2,1)}), bf16[256,2048]{0,1:T(8,128)(2,1)}) %all-gather.6.cloned.1.call-update) | async-done | bytes 1048592 | tf_op jit(solution)/shard_map/all_gather | solution.py:92
  340.8 3.7 fusion.16
  344.5 117.2 %all-reduce.2.cloned.1.call-done = f32[256,512]{1,0:T(8,128)} async-done(((f32[256,512]{1,0:T(8,128)}), f32[256,512]{1,0:T(8,128)}) %all-reduce.2.cloned.1.call-update) | async-done | bytes 524304 | tf_op jit(solution)/shard_map/psum | solution.py:106
  461.7 1.2 reduce_max.9
  462.9 1.3 exponential_reduce_fusion
  (31 shorter events, 7.9 us)
Async XLA Ops:
  6.5 334.3 %copy-start = (bf16[512,512]{1,0:T(8,128)(2,1)S(1)}, bf16[512,512]{1,0:T(8,128)(2,1)}, u32[]{:S(2)}) copy-start(bf16[512,512]{1,0:T(8,128)(2,1)} %param.13) | copy-start | bytes 1572868
  6.5 163.5 %all-gather.4.cloned.1.call-start = ((), (), s32[]{:S(2)}) async-start(), calls=%async_computation.3 | async-start | bytes 6389760 | tf_op jit(solution)/shard_map/all_gather | solution.py:80
  9.0 37.2 %all-to-all-start.1 = ((bf16[256,64,4]{0,2,1:T(4,128)(2,1)}), bf16[256,64,4]{0,2,1:T(4,128)(2,1)S(1)}, u32[]{:S(2)}, u32[]{:S(2)}) async-start(bf16[256,64,4]{0,2,1:T(4,128)(2,1)} %all_to_all.39), calls=%async_computation.1 | async-start | bytes 262144 | tf_op jit(solution)/shard_map/all_to_all | solution.py:87
  30.2 250.4 %all-gather.8.cloned.1.call-start = ((), (), s32[]{:S(2)}) async-start(), calls=%async_computation.5 | async-start | bytes 2129920 | tf_op jit(solution)/shard_map/all_gather | solution.py:96
  176.1 0.7 copy-start.1
  177.6 24.6 %all-to-all-start = ((bf16[256,64,4]{0,2,1:T(4,128)(2,1)}), bf16[256,64,4]{0,2,1:T(4,128)(2,1)S(1)}, u32[]{:S(2)}, u32[]{:S(2)}) async-start(bf16[256,64,4]{0,2,1:T(4,128)(2,1)} %convert_element_type.156), calls=%async_computation | async-start | bytes 262144 | tf_op jit(solution)/shard_map/all_to_all | solution.py:86
  184.8 156.0 %all-gather.6.cloned.1.call-start = ((), (), s32[]{:S(2)}) async-start(), calls=%async_computation.4 | async-start | bytes 1179648 | tf_op jit(solution)/shard_map/all_gather | solution.py:92
  239.2 222.5 %all-reduce.2.cloned.1.call-start = ((), (), s32[]{:S(2)}) async-start(), calls=%async_computation.6 | async-start | bytes 1048576 | tf_op jit(solution)/shard_map/psum | solution.py:106
  239.2 223.6 %copy-start.2 = (s32[256]{0:T(256)S(1)}, s32[256]{0:T(256)}, u32[]{:S(2)}) copy-start(s32[256]{0:T(256)} %param.14) | copy-start | bytes 3076
  239.2 225.0 %copy-start.3 = (s32[256]{0:T(256)S(1)}, s32[256]{0:T(256)}, u32[]{:S(2)}) copy-start(s32[256]{0:T(256)} %param.15) | copy-start | bytes 3076
Sparse Core Ops, SparseCore 0:
  12.0 158.0 all-gather.3
  174.6 106.0 all-gather.7
  282.7 58.0 all-gather.5
  344.6 117.0 all-reduce.1
where the time goes:
time: 472 us; the launch traced here: 471 us
  waiting for transfers between devices  368 us (78%)
  starting transfers between devices  28.7 us (6%)
  matrix products  27.2 us (6%)
  blocking collectives  22.3 us (5%)
  between operations  13.4 us (3%)
  other arithmetic  8.03 us (2%)
    all_gather x1, waiting for transfers between devices, per_device(): lax.all_gather(w_in, 'ctx', axis=0, tiled=True)  121 us
    psum x1, waiting for transfers between devices, per_device(): logits = lax.psum(partial_logits, 'tp')  117 us
    all_gather x1, waiting for transfers between devices, per_device(): mixed_full = lax.all_gather(mixed, 'tp', axis=1, tiled=True)  60.2 us
    all_gather x1, waiting for transfers between devices, per_device(): lax.all_gather(w_out, 'ctx', axis=0, tiled=True)  41.4 us
    all_to_all x1, blocking collectives, per_device(): lax.all_to_all(conv_chan, 'ctx', split_axis=0, concat_axis=1, tiled=True)  22.3 us
    all_to_all x1, starting transfers between devices, per_device(): lax.all_to_all(long_filter, 'ctx', split_axis=1, concat_axis=0, tiled=True)  21.2 us
    all_to_all x1, waiting for transfers between devices, per_device(): lax.all_to_all(gated, 'ctx', split_axis=1, concat_axis=0, tiled=True)  15.5 us
    all_to_all x1, waiting for transfers between devices, per_device(): lax.all_to_all(long_filter, 'ctx', split_axis=1, concat_axis=0, tiled=True)  11.7 us
  transfers between devices with their start and end apart: 6, of which 6 were waited for; matrix products, arithmetic and copies ran while one was open for 7% of the time, Pallas kernels for 0%

commit v1 on v0

v1 whole, which is shorter than its diff:
```python
import math

import jax
import jax.numpy as jnp
import numpy as np
from jax import lax
from jax.sharding import PartitionSpec as P

NORM_EPS = 1e-05
F32 = jnp.float32
BF16 = jnp.bfloat16

COORDS = [(z, y, x, c) for z in range(2) for y in range(4) for x in range(4) for c in range(2)]


def ctx_id(z, y, x, c):
    return ((z * 4 + y) * 4 + x) * 2 + c


def ctx_perm(move):
    return [(ctx_id(*at), ctx_id(*move(*at))) for at in COORDS]


PERM_CORE = ctx_perm(lambda z, y, x, c: (z, y, x, 1 - c))
PERM_Z = ctx_perm(lambda z, y, x, c: (1 - z, y, x, c))
PERM_Z_UP = [(i, i + 32) for i in range(32)]
GROUPS_X = [[ctx_id(z, y, x, c) for x in range(4)] for z in range(2) for y in range(4) for c in range(2)]
GROUPS_Y = [[ctx_id(z, y, x, c) for y in range(4)] for z in range(2) for x in range(4) for c in range(2)]
GROUPS_PLANE = [
    [ctx_id(z, y, x, c) for y in range(4) for x in range(4) for c in range(2)] for z in range(2)
]
GROUPS_CORE = [
    [ctx_id(z, y, x, c) for y in range(4) for x in range(4)] for z in range(2) for c in range(2)
]
GROUPS_TP = [[0, 1, 2, 3], [4, 5, 6, 7]]


def weight_routes(flip):
    pairs = []
    for i in range(64):
        for q in range(8):
            plane, core, chip, half = i // 8, (i % 8) // 4, (i % 4) * 4 + q // 2, q % 2
            z = half ^ flip
            pairs.append((i * 8 + q, (z * 32 + chip * 2 + core) * 8 + plane))
    return pairs


ROUTE_SAME, ROUTE_FLIP = weight_routes(0), weight_routes(1)


def tables():
    index = np.arange(128)
    inner = 2.0 * math.pi * (np.outer(index, index) % 128) / 128
    outer = 2.0 * math.pi * np.outer(index, index) / 16384
    return (np.cos(inner), np.sin(inner), np.cos(outer), np.sin(outer))


COS, SIN, COS_TW, SIN_TW = tables()


def mm(left, right):
    return jnp.dot(left, right, preferred_element_type=F32)


def spectrum(cube):
    rows, chans, _ = cube.shape
    flat = cube.reshape(rows, chans * 128)
    first = mm(jnp.asarray(np.concatenate([COS[:, :rows], SIN[:, :rows]]), BF16), flat)
    real = first[:128].reshape(128, chans, 128)
    imag = -first[128:].reshape(128, chans, 128)
    cos_tw, sin_tw = (jnp.asarray(t, F32)[:, None, :] for t in (COS_TW, SIN_TW))
    real_t = (real * cos_tw + imag * sin_tw).astype(BF16).reshape(128 * chans, 128)
    imag_t = (imag * cos_tw - real * sin_tw).astype(BF16).reshape(128 * chans, 128)
    both = jnp.asarray(np.concatenate([COS, SIN], axis=1), BF16)
    from_real, from_imag = mm(real_t, both), mm(imag_t, both)
    real_x = from_real[:, :128] + from_imag[:, 128:]
    imag_x = from_imag[:, :128] - from_real[:, 128:]
    return (real_x.reshape(128, chans, 128), imag_x.reshape(128, chans, 128))


def inverse(real_y, imag_y):
    chans = real_y.shape[1]
    both = jnp.asarray(np.concatenate([COS, SIN], axis=1), BF16)
    from_real = mm(real_y.astype(BF16).reshape(128 * chans, 128), both)
    from_imag = mm(imag_y.astype(BF16).reshape(128 * chans, 128), both)
    real_z = (from_real[:, :128] - from_imag[:, 128:]).reshape(128, chans, 128)
    imag_z = (from_imag[:, :128] + from_real[:, 128:]).reshape(128, chans, 128)
    cos_tw, sin_tw = (jnp.asarray(t, F32)[:, None, :] for t in (COS_TW, SIN_TW))
    real_w = (real_z * cos_tw - imag_z * sin_tw).astype(BF16).reshape(128, chans * 128)
    imag_w = (imag_z * cos_tw + real_z * sin_tw).astype(BF16).reshape(128, chans * 128)
    last = jnp.asarray(np.concatenate([COS[:64], -SIN[:64]], axis=1) / 16384.0, BF16)
    return mm(last, jnp.concatenate([real_w, imag_w])).reshape(64, chans, 128)


def by_position(own, other, place):
    return jnp.where(place == 0, jnp.stack([own, other]), jnp.stack([other, own]))


def per_device(tokens_in, pre_gain, w_in, w_out, long_filter, w_unembed, target_ids, score_mask):
    ctx, tp = lax.axis_index("ctx"), lax.axis_index("tp")
    core, z = ctx % 2, ctx // 32

    halves = w_in.reshape(64, 3, 2, 128)
    keep = lax.dynamic_index_in_dim(halves, core, 2, False).reshape(64, 384)
    give = lax.dynamic_index_in_dim(halves, 1 - core, 2, False).reshape(64, 384)
    got = lax.ppermute(give, "ctx", PERM_CORE)
    own = by_position(keep, got, core).reshape(128, 384)
    other = lax.ppermute(own, "ctx", PERM_Z)
    block = by_position(own, other, z).reshape(1, 256, 384)
    block = lax.all_to_all(
        jnp.broadcast_to(block, (4, 256, 384)), "ctx", 0, 0, axis_index_groups=GROUPS_X, tiled=True
    )
    block = lax.all_to_all(
        jnp.broadcast_to(block[None], (4, 4, 256, 384)), "ctx", 0, 0, axis_index_groups=GROUPS_Y, tiled=True
    )
    weights = block.reshape(4096, 384)

    stream = tokens_in.astype(F32)
    scale = lax.rsqrt(jnp.mean(stream * stream, axis=1, keepdims=True) + NORM_EPS)
    normed = (stream * scale * pre_gain.astype(F32)).astype(BF16)
    normed = normed.reshape(256, 2, 16, 128).transpose(0, 2, 1, 3).reshape(256, 4096)
    normed = by_position(normed, lax.ppermute(normed, "ctx", PERM_CORE), core).reshape(512, 4096)

    chans = long_filter.reshape(2, 128, 2, 16, 8).transpose(3, 2, 0, 4, 1).reshape(32, 2, 8, 128)
    chans = lax.all_to_all(chans, "ctx", 0, 0, axis_index_groups=GROUPS_PLANE, tiled=True)
    chans = chans.reshape(64, 8, 128)
    chans = by_position(chans, lax.ppermute(chans, "ctx", PERM_Z), z)
    low_real, low_imag = spectrum(chans[0])
    high_real, high_imag = spectrum(chans[1])
    sign = jnp.asarray(1.0 - 2.0 * (np.arange(128) % 2), F32)[:, None, None]
    all_real, all_imag = sign * low_real + high_real, sign * low_imag + high_imag

    partial = mm(w_out, w_unembed).astype(BF16).reshape(8, 16, 128)
    partial = lax.all_to_all(partial, "tp", 0, 0, tiled=True)
    piece = jnp.sum(partial.astype(F32), axis=0).astype(BF16)
    same = lax.ppermute(piece, ("ctx", "tp"), ROUTE_SAME)
    flip = lax.ppermute(piece, ("ctx", "tp"), ROUTE_FLIP)
    rows8 = by_position(same, flip, z).reshape(1, 8, 512)

    proj = mm(normed, weights).astype(BF16)
    gate = proj[:, :128]
    gated = (proj[:, 128:256].astype(F32) * proj[:, 256:].astype(F32)).astype(BF16)
    gate = gate.reshape(2, 256, 128)
    gate_keep = lax.dynamic_index_in_dim(gate, core, 0, False)
    gate_got = lax.ppermute(lax.dynamic_index_in_dim(gate, 1 - core, 0, False), "ctx", PERM_CORE)
    gate_all = by_position(gate_keep, gate_got, core).reshape(2, 2, 128, 16, 8).transpose(3, 0, 1, 4, 2)

    signal = gated.reshape(4, 128, 16, 8).transpose(2, 0, 3, 1)
    signal = lax.all_to_all(signal, "ctx", 0, 0, axis_index_groups=GROUPS_CORE, tiled=True)
    signal = signal.reshape(64, 8, 128)
    before = lax.ppermute(signal, "ctx", PERM_Z_UP)
    w_mix = lax.all_to_all(
        jnp.broadcast_to(rows8, (32, 8, 512)), "ctx", 0, 0, axis_index_groups=GROUPS_PLANE, tiled=True
    ).reshape(256, 512)
    own_real, own_imag = spectrum(signal)
    old_real, old_imag = spectrum(before)
    real_y = own_real * low_real - own_imag * low_imag + old_real * all_real - old_imag * all_imag
    imag_y = own_real * low_imag + own_imag * low_real + old_real * all_imag + old_imag * all_real
    conv = inverse(real_y, imag_y).astype(BF16)

    conv = conv.reshape(32, 2, 8, 128)
    conv = lax.all_to_all(conv, "ctx", 0, 0, axis_index_groups=GROUPS_PLANE, tiled=True)
    conv = conv.reshape(16, 2, 2, 8, 128)
    mixed = (gate_all.astype(F32) * conv.astype(F32)).astype(BF16)
    mixed = mixed.transpose(2, 4, 0, 1, 3).reshape(256, 256)

    width = w_unembed.shape[0]
    stream_slice = lax.dynamic_slice_in_dim(tokens_in, tp * width, width, 1)
    logits = mm(stream_slice, w_unembed) + mm(mixed, w_mix)
    logits = logits.astype(BF16).reshape(4, 64, 512)
    logits = lax.all_to_all(logits, "tp", 0, 0, axis_index_groups=GROUPS_TP, tiled=True)
    logits = jnp.sum(logits.astype(F32), axis=0).astype(BF16)
    far = lax.ppermute(logits, "tp", [(i, i ^ 4) for i in range(8)])
    logits = logits.astype(F32) + far.astype(F32)

    row_top = jnp.max(logits, axis=1, keepdims=True)
    log_total = row_top[:, 0] + jnp.log(jnp.sum(jnp.exp(logits - row_top), axis=1))
    ids = lax.dynamic_slice_in_dim(target_ids, (tp % 4) * 64, 64, 0)
    vocab_index = lax.broadcasted_iota(jnp.int32, (64, 512), 1)
    picked = jnp.sum(jnp.where(vocab_index == ids[:, None], logits, 0.0), axis=1)
    scores = jnp.broadcast_to((picked - log_total)[None, None, :], (4, 8, 64))
    scores = lax.all_to_all(scores, "tp", 0, 0, axis_index_groups=GROUPS_TP, tiled=True)
    return scores[:, 0].reshape(256) * score_mask.astype(F32)


def solution(mesh):
    return jax.shard_map(
        per_device,
        mesh=mesh,
        in_specs=(
            P("ctx", None),
            P(),
            P("ctx", None, "tp"),
            P("ctx", "tp"),
            P("ctx", "tp"),
            P("tp", None),
            P("ctx"),
            P("ctx"),
        ),
        out_specs=P("ctx"),
        check_vma=False,
    )
```

time: 472 us -> 223 us (0.47)
  waiting for transfers between devices: 368 us -> 38.9 us
  starting transfers between devices: 28.7 us -> 94.4 us
  local copies, waits for them, and re-layouts: 3.67 us -> 30.7 us
  between operations: 13.4 us -> 0.76 us
    all_gather x3 -> x0, waiting for transfers between devices: 222 us -> none  [the longest x1 121 us: per_device(): lax.all_gather(w_in, 'ctx', axis=0, tiled=True)]
    psum x1 -> x0, waiting for transfers between devices: 117 us -> none  [per_device(): logits = lax.psum(partial_logits, 'tp')]
    ppermute x0 -> x9, starting transfers between devices: none -> 54.6 us  [the longest x1 14 us: per_device(): other = lax.ppermute(own, 'ctx', PERM_Z)]
    all_to_all x2 -> x7, starting transfers between devices: 28.4 us -> 39.8 us  [the longest x1 9.39 us: per_device(): lax.all_to_all(chans, 'ctx', 0, 0, axis_index_groups=GROUPS_PLANE, tiled=...]
    ppermute x0 -> x9, waiting for transfers between devices: none -> 7.54 us  [the longest x1 7.52 us: per_device(): far = lax.ppermute(logits, 'tp', [(i, i ^ 4) for i in range(8)])]
    select_n x0 -> x2, local copies, waits for them, and re-layouts: none -> 6.41 us  [by_position(): jnp.where(place == 0, jnp.stack([own, other]), jnp.stack([other, own]))]
    reshape x0 -> x10, local copies, waits for them, and re-layouts: none -> 5.51 us  [the longest x4 3.02 us: spectrum(): real = first[:128].reshape(128, chans, 128)]
    unnamed x10 -> x51, local copies, waits for them, and re-layouts: 1.86 us -> 7.22 us
  transfers between devices with their start and end apart: 6 -> 16, of which waited for: 6 -> 6; matrix products, arithmetic and copies ran while one was open for 7% -> 26% of each run, Pallas kernels for 0% -> 0%
where the time goes in v1:
time: 223 us; the launch traced here: 221 us
  starting transfers between devices  94.4 us (42%)
  waiting for transfers between devices  38.9 us (17%)
  local copies, waits for them, and re-layouts  30.7 us (14%)
  blocking collectives  23 us (10%)
  matrix products  22.8 us (10%)
  other arithmetic  10.9 us (5%)
    dot_general x20, matrix products, mm(): return jnp.dot(left, right, preferred_element_type=F32)  22.8 us
    all_to_all x1, blocking collectives, per_device(): lax.all_to_all(logits, 'tp', 0, 0, axis_index_groups=GROUPS_TP, tiled=True)  15.1 us
    ppermute x1, starting transfers between devices, per_device(): other = lax.ppermute(own, 'ctx', PERM_Z)  14 us
    all_to_all x1, waiting for transfers between devices, per_device(): lax.all_to_all(jnp.broadcast_to(block[None], (4, 4, 256, 384)), 'ctx', 0,...  12.9 us
    ppermute x1, starting transfers between devices, per_device(): before = lax.ppermute(signal, 'ctx', PERM_Z_UP)  10.9 us
    all_to_all x1, starting transfers between devices, per_device(): lax.all_to_all(chans, 'ctx', 0, 0, axis_index_groups=GROUPS_PLANE, tiled=...  9.39 us
    ppermute x1, starting transfers between devices, per_device(): flip = lax.ppermute(piece, ('ctx', 'tp'), ROUTE_FLIP)  7.99 us
    all_to_all x1, blocking collectives, per_device(): lax.all_to_all(scores, 'tp', 0, 0, axis_index_groups=GROUPS_TP, tiled=True)  7.92 us
  transfers between devices with their start and end apart: 16, of which 6 were waited for; matrix products, arithmetic and copies ran while one was open for 26% of the time, Pallas kernels for 0%

profile of v1, /device:TPU:6, one launch (start us, length us, event | category | flops | bytes accessed | tf_op | source)
XLA Modules:
  0.0 221.4 jit_solution(13997172009057928057)
XLA Ops:
  5.0 9.4 %all-to-all-start.3 = ((bf16[32,2,8,128]{3,2,1,0:T(8,128)(2,1)}), bf16[32,2,8,128]{3,2,1,0:T(8,128)(2,1)S(1)}, u32[]{:S(2)}, u32[]{:S(2)}) async-start(bf16[32,2,8,128]{3,2,1,0:T(8,128)(2,1)} %bitcast.24), calls=%async_computation.3 | async-start | bytes 262144 | tf_op jit(solution)/shard_map/all_to_all | solution.py:125
  14.4 3.3 %copy.70 = bf16[256,4096]{0,1:T(8,128)(2,1)S(1)} copy(bf16[256,4096]{1,0:T(8,128)(2,1)} %param.29) | data formatting | bytes 4194304 | tf_op args[0]
  18.6 14.0 %collective-permute-start.2 = (bf16[128,384]{1,0:T(8,128)(2,1)S(1)}, bf16[128,384]{1,0:T(8,128)(2,1)S(1)}, u32[]{:S(2)}, u32[]{:S(2)}) collective-permute-start(bf16[128,384]{1,0:T(8,128)(2,1)S(1)} %bitcast.225), channel_id=1, source_target_pairs={{0,256},{8,264},{16,272},{24,280},{32,288},{40,296},{48,304},{56,3... | collective-permute-start | bytes 294920 | tf_op jit(solution)/shard_map/ppermute | solution.py:108
  33.3 5.0 %all-to-all-start.5 = ((bf16[8,16,128]{2,1,0:T(8,128)(2,1)}), bf16[8,16,128]{2,1,0:T(8,128)(2,1)S(1)}, u32[]{:S(2)}, u32[]{:S(2)}) async-start(bf16[8,16,128]{2,1,0:T(8,128)(2,1)} %reshape.266), calls=%async_computation.5 | async-start | bytes 65536 | tf_op jit(solution)/shard_map/all_to_all | solution.py:134
  38.3 6.3 %collective-permute-start.4 = (bf16[64,8,128]{2,1,0:T(8,128)(2,1)S(1)}, bf16[64,8,128]{2,1,0:T(8,128)(2,1)S(1)}, u32[]{:S(2)}, u32[]{:S(2)}) collective-permute-start(bf16[64,8,128]{2,1,0:T(8,128)(2,1)S(1)} %bitcast.215), channel_id=1, source_target_pairs={{0,256},{8,264},{16,272},{24,280},{32,288},{40,296},{48,304},{56,3... | collective-permute-start | bytes 393224 | tf_op jit(solution)/shard_map/ppermute | solution.py:127
  44.7 4.3 %all-to-all-done.5 = bf16[8,16,128]{2,1,0:T(8,128)(2,1)S(1)} async-done(((bf16[8,16,128]{2,1,0:T(8,128)(2,1)}), bf16[8,16,128]{2,1,0:T(8,128)(2,1)S(1)}, u32[]{:S(2)}, u32[]{:S(2)}) %all-to-all-start.5) | async-done | bytes 32800 | tf_op jit(solution)/shard_map/all_to_all | solution.py:134
  49.9 4.8 %all-to-all-start = ((bf16[4,256,384]{2,1,0:T(8,128)(2,1)}), bf16[4,256,384]{2,1,0:T(8,128)(2,1)}, u32[]{:S(2)}, u32[]{:S(2)}) async-start(bf16[4,256,384]{2,1,0:T(8,128)(2,1)} %broadcast_in_dim.11), calls=%async_computation | async-start | bytes 1572864 | tf_op jit(solution)/shard_map/all_to_all | solution.py:110
  57.7 4.4 %collective-permute-start.6 = (bf16[16,128]{1,0:T(8,128)(2,1)S(1)}, bf16[16,128]{1,0:T(8,128)(2,1)S(1)}, u32[]{:S(2)}, u32[]{:S(2)}) collective-permute-start(bf16[16,128]{1,0:T(8,128)(2,1)S(1)} %reduce_sum.52), channel_id=1, source_target_pairs={{0,0},{1,256},{2,16},{3,272},{4,32},{5,288},{6,48},{7,304},{8,64},... | collective-permute-start | bytes 12296 | tf_op jit(solution)/shard_map/ppermute | solution.py:136
  62.2 8.0 %collective-permute-start.7 = (bf16[16,128]{1,0:T(8,128)(2,1)S(1)}, bf16[16,128]{1,0:T(8,128)(2,1)S(1)}, u32[]{:S(2)}, u32[]{:S(2)}) collective-permute-start(bf16[16,128]{1,0:T(8,128)(2,1)S(1)} %reduce_sum.52), channel_id=1, source_target_pairs={{0,256},{1,0},{2,272},{3,16},{4,288},{5,32},{6,304},{7,48},{8,320}... | collective-permute-start | bytes 12296 | tf_op jit(solution)/shard_map/ppermute | solution.py:137
  70.3 3.3 %broadcast_in_dim.12 = bf16[4,4,256,384]{3,2,1,0:T(8,128)(2,1)} broadcast(bf16[4,256,384]{2,1,0:T(8,128)(2,1)} %all-to-all-done), dimensions={1,2,3} | broadcast | bytes 3932160 | tf_op jit(solution)/shard_map/broadcast_in_dim | solution.py:114
  73.5 4.6 %all-to-all-start.1 = ((bf16[4,4,256,384]{3,2,1,0:T(8,128)(2,1)}), bf16[4,4,256,384]{3,2,1,0:T(8,128)(2,1)}, u32[]{:S(2)}, u32[]{:S(2)}) async-start(bf16[4,4,256,384]{3,2,1,0:T(8,128)(2,1)} %broadcast_in_dim.12), calls=%async_computation.1 | async-start | bytes 6291456 | tf_op jit(solution)/shard_map/all_to_all | solution.py:113
  79.4 2.0 neg.35
  84.8 1.9 reshape.262
  86.7 2.6 %fusion.41 = f32[1024,256]{1,0:T(8,128)} fusion(bf16[128,256]{1,0:T(8,128)(2,1)S(1)} %copy-done.1, f32[1024,128]{1,0:T(8,128)} %neg.35, f32[1024,128]{1,0:T(8,128)} %reshape.258, f32[128,128]{1,0:T(8,128)S(1)} %copy-done.2, f32[128,128]{1,0:T(8,128)S(1)} %copy-done.3), kind=kOutput, calls=%fused_computation.78 | convolution fusion | flops 67633152 | bytes 2293760 | tf_op jit(solution)/shard_map/dot_general | solution.py:62
  89.3 2.5 %fusion.43 = f32[1024,256]{1,0:T(8,128)} fusion(bf16[128,256]{1,0:T(8,128)(2,1)S(1)} %copy-done.1, f32[1024,128]{1,0:T(8,128)} %reshape.258, f32[1024,128]{1,0:T(8,128)} %neg.35, f32[128,128]{1,0:T(8,128)S(1)} %copy-done.2, f32[128,128]{1,0:T(8,128)S(1)} %copy-done.3), kind=kOutput, calls=%fused_computation.79 | convolution fusion | flops 67633152 | bytes 2293760 | tf_op jit(solution)/shard_map/dot_general | solution.py:62
  93.1 4.6 %maximum_select_fusion = bf16[2,256,4096]{1,2,0:T(8,128)(2,1)} fusion(bf16[1,256,4096]{1,2,0:T(8,128)(2,1)} %bitcast.5, bf16[1,256,4096]{1,2,0:T(8,128)(2,1)S(1)} %bitcast.207, pred[]{:T(512)S(6)} %eq.23), kind=kLoop, calls=%fused_computation.5 | loop fusion | flops 6291456 | bytes 8388609 | tf_op jit(solution)/shard_map/jit(_where)/select_n | solution.py:96
  97.7 6.4 %copy.73 = bf16[2,256,4096]{2,1,0:T(8,128)(2,1)} copy(bf16[2,256,4096]{1,2,0:T(8,128)(2,1)} %maximum_select_fusion) | data formatting | bytes 8388608 | tf_op jit(solution)/shard_map/jit(_where)/select_n | solution.py:96
  104.1 12.9 %all-to-all-done.1 = bf16[4,4,256,384]{3,2,1,0:T(8,128)(2,1)} async-done(((bf16[4,4,256,384]{3,2,1,0:T(8,128)(2,1)}), bf16[4,4,256,384]{3,2,1,0:T(8,128)(2,1)}, u32[]{:S(2)}, u32[]{:S(2)}) %all-to-all-start.1) | async-done | bytes 3145760 | tf_op jit(solution)/shard_map/all_to_all | solution.py:113
  117.0 5.5 %convolution_convert_fusion = bf16[512,384]{1,0:T(8,128)(2,1)S(1)} fusion(bf16[512,4096]{1,0:T(8,128)(2,1)} %bitcast.212, bf16[4096,384]{1,0:T(8,128)(2,1)} %bitcast.12), kind=kOutput, calls=%fused_computation.22 | convolution fusion | flops 1610809344 | bytes 7733248 | tf_op jit(solution)/shard_map/dot_general | solution.py:62
  123.4 4.6 %all-to-all-start.2 = ((bf16[16,4,8,128]{3,1,2,0:T(4,128)(2,1)}), bf16[16,4,8,128]{3,1,2,0:T(4,128)(2,1)S(1)}, u32[]{:S(2)}, u32[]{:S(2)}) async-start(bf16[16,4,8,128]{3,1,2,0:T(4,128)(2,1)} %bitcast.20), calls=%async_computation.2 | async-start | bytes 262144 | tf_op jit(solution)/shard_map/all_to_all | solution.py:149
  129.2 4.6 %all-to-all-done.2 = bf16[16,4,8,128]{3,1,2,0:T(4,128)(2,1)S(1)} async-done(((bf16[16,4,8,128]{3,1,2,0:T(4,128)(2,1)}), bf16[16,4,8,128]{3,1,2,0:T(4,128)(2,1)S(1)}, u32[]{:S(2)}, u32[]{:S(2)}) %all-to-all-start.2) | async-done | bytes 131104 | tf_op jit(solution)/shard_map/all_to_all | solution.py:149
  133.8 10.9 %collective-permute-start.5 = (bf16[64,8,128]{2,1,0:T(8,128)(2,1)S(1)}, bf16[64,8,128]{2,1,0:T(8,128)(2,1)S(1)}, u32[]{:S(2)}, u32[]{:S(2)}) collective-permute-start(bf16[64,8,128]{2,1,0:T(8,128)(2,1)S(1)} %bitcast.217), channel_id=1, source_target_pairs={{0,256},{8,264},{16,272},{24,280},{32,288},{40,296},{48,304},{56,3... | collective-permute-start | bytes 393224 | tf_op jit(solution)/shard_map/ppermute | solution.py:151
  152.4 1.9 fusion.28
  157.6 5.8 %all-to-all-start.4 = ((bf16[32,2,8,128]{3,2,1,0:T(8,128)(2,1)}), bf16[32,2,8,128]{3,2,1,0:T(8,128)(2,1)S(1)}, u32[]{:S(2)}, u32[]{:S(2)}) async-start(bf16[32,2,8,128]{3,2,1,0:T(8,128)(2,1)} %bitcast.64), calls=%async_computation.4 | async-start | bytes 262144 | tf_op jit(solution)/shard_map/all_to_all | solution.py:162
  163.7 2.1 collective-permute-start.3
  165.8 3.9 %all-to-all-done.4 = bf16[32,2,8,128]{3,2,1,0:T(8,128)(2,1)S(1)} async-done(((bf16[32,2,8,128]{3,2,1,0:T(8,128)(2,1)}), bf16[32,2,8,128]{3,2,1,0:T(8,128)(2,1)S(1)}, u32[]{:S(2)}, u32[]{:S(2)}) %all-to-all-start.4) | async-done | bytes 131104 | tf_op jit(solution)/shard_map/all_to_all | solution.py:162
  170.4 5.5 %all-to-all-start.6 = ((bf16[32,8,512]{2,1,0:T(8,128)(2,1)}), bf16[32,8,512]{2,1,0:T(8,128)(2,1)S(1)}, u32[]{:S(2)}, u32[]{:S(2)}) async-start(bf16[32,8,512]{2,1,0:T(8,128)(2,1)} %broadcast_in_dim.13), calls=%async_computation.6 | async-start | bytes 524288 | tf_op jit(solution)/shard_map/all_to_all | solution.py:152
  177.3 5.6 %all-to-all-done.6 = bf16[32,8,512]{2,1,0:T(8,128)(2,1)S(1)} async-done(((bf16[32,8,512]{2,1,0:T(8,128)(2,1)}), bf16[32,8,512]{2,1,0:T(8,128)(2,1)S(1)}, u32[]{:S(2)}, u32[]{:S(2)}) %all-to-all-start.6) | async-done | bytes 262176 | tf_op jit(solution)/shard_map/all_to_all | solution.py:152
  183.2 15.1 %all_to_all.45 = bf16[4,64,512]{2,1,0:T(8,128)(2,1)S(1)} all-to-all(bf16[4,64,512]{2,1,0:T(8,128)(2,1)S(1)} %bitcast.213), channel_id=1, replica_groups={{0,1,2,3},{4,5,6,7},{8,9,10,11},{12,13,14,15},{16,17,18,19},{20,21,22,2..., dimensions={0} | all-to-all | bytes 524288 | tf_op jit(solution)/shard_map/all_to_all | solution.py:171
  198.4 5.1 %collective-permute-start.8 = (bf16[64,512]{1,0:T(8,128)(2,1)S(1)}, bf16[64,512]{1,0:T(8,128)(2,1)S(1)}, u32[]{:S(2)}, u32[]{:S(2)}) collective-permute-start(bf16[64,512]{1,0:T(8,128)(2,1)S(1)} %reduce_sum.53), channel_id=1, source_target_pairs={{0,4},{1,5},{2,6},{3,7},{4,0},{5,1},{6,2},{7,3},{8,12},{9,13},{10,... | collective-permute-start | bytes 196616 | tf_op jit(solution)/shard_map/ppermute | solution.py:173
  203.6 7.5 %collective-permute-done.8 = bf16[64,512]{1,0:T(8,128)(2,1)S(1)} collective-permute-done((bf16[64,512]{1,0:T(8,128)(2,1)S(1)}, bf16[64,512]{1,0:T(8,128)(2,1)S(1)}, u32[]{:S(2)}, u32[]{:S(2)}) %collective-permute-start.8) | collective-permute-done | bytes 65568 | tf_op jit(solution)/shard_map/ppermute | solution.py:173
  211.5 7.9 %all_to_all.46 = f32[4,1,512]{2,1,0:T(1,128)S(1)} all-to-all(f32[4,1,512]{2,1,0:T(1,128)S(1)} %reshape.277), channel_id=1, replica_groups={{0,1,2,3},{4,5,6,7},{8,9,10,11},{12,13,14,15},{16,17,18,19},{20,21,22,2..., dimensions={0} | all-to-all | bytes 16384 | tf_op jit(solution)/shard_map/all_to_all | solution.py:182
  (135 shorter events, 34.3 us)
Async XLA Ops:
  0.0 18.2 %copy-start = (bf16[512,512]{1,0:T(8,128)(2,1)S(1)}, bf16[512,512]{1,0:T(8,128)(2,1)}, u32[]{:S(2)}) copy-start(bf16[512,512]{1,0:T(8,128)(2,1)} %param.34) | copy-start | bytes 1572868
  0.0 18.2 %copy-start.14 = (bf16[32,512]{1,0:T(8,128)(2,1)S(1)}, bf16[32,512]{1,0:T(8,128)(2,1)}, u32[]{:S(2)}) copy-start(bf16[32,512]{1,0:T(8,128)(2,1)} %param.32) | copy-start | bytes 98308
  1.3 31.3 %copy-start.17 = (bf16[4096]{0:T(1024)(128)(2,1)S(1)}, bf16[4096]{0:T(1024)(128)(2,1)}, u32[]{:S(2)}) copy-start(bf16[4096]{0:T(1024)(128)(2,1)} %param.30) | copy-start | bytes 24580
  1.3 17.3 %collective-permute-start.1 = (bf16[64,384]{1,0:T(8,128)(2,1)S(1)}, bf16[64,384]{1,0:T(8,128)(2,1)S(1)}, u32[]{:S(2)}, u32[]{:S(2)}) collective-permute-start(bf16[64,384]{1,0:T(8,128)(2,1)S(1)} %bitcast.234), channel_id=1, source_target_pairs={{0,8},{8,0},{16,24},{24,16},{32,40},{40,32},{48,56},{56,48},{64,72... | collective-permute-start | bytes 147464 | tf_op jit(solution)/shard_map/ppermute | solution.py:106
  5.0 28.3 %all-to-all-start.3 = ((bf16[32,2,8,128]{3,2,1,0:T(8,128)(2,1)}), bf16[32,2,8,128]{3,2,1,0:T(8,128)(2,1)S(1)}, u32[]{:S(2)}, u32[]{:S(2)}) async-start(bf16[32,2,8,128]{3,2,1,0:T(8,128)(2,1)} %bitcast.24), calls=%async_computation.3 | async-start | bytes 262144 | tf_op jit(solution)/shard_map/all_to_all | solution.py:125
  18.6 26.1 %collective-permute-start.2 = (bf16[128,384]{1,0:T(8,128)(2,1)S(1)}, bf16[128,384]{1,0:T(8,128)(2,1)S(1)}, u32[]{:S(2)}, u32[]{:S(2)}) collective-permute-start(bf16[128,384]{1,0:T(8,128)(2,1)S(1)} %bitcast.225), channel_id=1, source_target_pairs={{0,256},{8,264},{16,272},{24,280},{32,288},{40,296},{48,304},{56,3... | collective-permute-start | bytes 294920 | tf_op jit(solution)/shard_map/ppermute | solution.py:108
  33.3 15.7 %all-to-all-start.5 = ((bf16[8,16,128]{2,1,0:T(8,128)(2,1)}), bf16[8,16,128]{2,1,0:T(8,128)(2,1)S(1)}, u32[]{:S(2)}, u32[]{:S(2)}) async-start(bf16[8,16,128]{2,1,0:T(8,128)(2,1)} %reshape.266), calls=%async_computation.5 | async-start | bytes 65536 | tf_op jit(solution)/shard_map/all_to_all | solution.py:134
  38.3 31.9 %collective-permute-start.4 = (bf16[64,8,128]{2,1,0:T(8,128)(2,1)S(1)}, bf16[64,8,128]{2,1,0:T(8,128)(2,1)S(1)}, u32[]{:S(2)}, u32[]{:S(2)}) collective-permute-start(bf16[64,8,128]{2,1,0:T(8,128)(2,1)S(1)} %bitcast.215), channel_id=1, source_target_pairs={{0,256},{8,264},{16,272},{24,280},{32,288},{40,296},{48,304},{56,3... | collective-permute-start | bytes 393224 | tf_op jit(solution)/shard_map/ppermute | solution.py:127
  49.9 20.3 %all-to-all-start = ((bf16[4,256,384]{2,1,0:T(8,128)(2,1)}), bf16[4,256,384]{2,1,0:T(8,128)(2,1)}, u32[]{:S(2)}, u32[]{:S(2)}) async-start(bf16[4,256,384]{2,1,0:T(8,128)(2,1)} %broadcast_in_dim.11), calls=%async_computation | async-start | bytes 1572864 | tf_op jit(solution)/shard_map/all_to_all | solution.py:110
  54.7 2.8 %copy-start.19 = (f32[128]{0:T(128)S(1)}, f32[128]{0:T(128)}, u32[]{:S(2)}) copy-start(f32[128]{0:T(128)} %constant.97.clone) | copy-start | bytes 1540
  55.6 37.5 %collective-permute-start = (bf16[256,4096]{0,1:T(8,128)(2,1)S(1)}, bf16[256,4096]{0,1:T(8,128)(2,1)}, u32[]{:S(2)}, u32[]{:S(2)}) collective-permute-start(bf16[256,4096]{0,1:T(8,128)(2,1)S(1)} %bitcast.206), channel_id=1, source_target_pairs={{0,8},{8,0},{16,24},{24,16},{32,40},{40,32},{48,56},{56,48},{64,72... | collective-permute-start | bytes 6291464 | tf_op jit(solution)/shard_map/ppermute | solution.py:122
  57.7 105.8 %collective-permute-start.6 = (bf16[16,128]{1,0:T(8,128)(2,1)S(1)}, bf16[16,128]{1,0:T(8,128)(2,1)S(1)}, u32[]{:S(2)}, u32[]{:S(2)}) collective-permute-start(bf16[16,128]{1,0:T(8,128)(2,1)S(1)} %reduce_sum.52), channel_id=1, source_target_pairs={{0,0},{1,256},{2,16},{3,272},{4,32},{5,288},{6,48},{7,304},{8,64},... | collective-permute-start | bytes 12296 | tf_op jit(solution)/shard_map/ppermute | solution.py:136
  62.2 101.3 %collective-permute-start.7 = (bf16[16,128]{1,0:T(8,128)(2,1)S(1)}, bf16[16,128]{1,0:T(8,128)(2,1)S(1)}, u32[]{:S(2)}, u32[]{:S(2)}) collective-permute-start(bf16[16,128]{1,0:T(8,128)(2,1)S(1)} %reduce_sum.52), channel_id=1, source_target_pairs={{0,256},{1,0},{2,272},{3,16},{4,288},{5,32},{6,304},{7,48},{8,320}... | collective-permute-start | bytes 12296 | tf_op jit(solution)/shard_map/ppermute | solution.py:137
  70.3 7.9 %copy-start.12 = (bf16[256,64]{1,0:T(8,128)(2,1)S(1)}, bf16[256,64]{1,0:T(8,128)(2,1)}, u32[]{:S(2)}) copy-start(bf16[256,64]{1,0:T(8,128)(2,1)} %constant.93.clone) | copy-start | bytes 98308
  73.5 43.4 %all-to-all-start.1 = ((bf16[4,4,256,384]{3,2,1,0:T(8,128)(2,1)}), bf16[4,4,256,384]{3,2,1,0:T(8,128)(2,1)}, u32[]{:S(2)}, u32[]{:S(2)}) async-start(bf16[4,4,256,384]{3,2,1,0:T(8,128)(2,1)} %broadcast_in_dim.12), calls=%async_computation.1 | async-start | bytes 6291456 | tf_op jit(solution)/shard_map/all_to_all | solution.py:113
  79.4 7.4 %copy-start.1 = (bf16[128,256]{1,0:T(8,128)(2,1)S(1)}, bf16[128,256]{1,0:T(8,128)(2,1)}, u32[]{:S(2)}) copy-start(bf16[128,256]{1,0:T(8,128)(2,1)} %constant.96.clone) | copy-start | bytes 196612
  79.4 7.4 %copy-start.2 = (f32[128,128]{1,0:T(8,128)S(1)}, f32[128,128]{1,0:T(8,128)}, u32[]{:S(2)}) copy-start(f32[128,128]{1,0:T(8,128)} %constant.95.clone) | copy-start | bytes 196612
  79.4 7.4 %copy-start.3 = (f32[128,128]{1,0:T(8,128)S(1)}, f32[128,128]{1,0:T(8,128)}, u32[]{:S(2)}) copy-start(f32[128,128]{1,0:T(8,128)} %constant.94.clone) | copy-start | bytes 196612
  86.7 5.1 %copy-start.4 = (f32[1024,128]{1,0:T(8,128)S(1)}, f32[1024,128]{1,0:T(8,128)}, u32[]{:S(2)}) copy-start(f32[1024,128]{1,0:T(8,128)} %reshape.262) | copy-start | bytes 1572868
  117.0 11.0 %copy-start.5 = (f32[1024,128]{1,0:T(8,128)S(1)}, f32[1024,128]{1,0:T(8,128)}, u32[]{:S(2)}) copy-start(f32[1024,128]{1,0:T(8,128)} %reshape.262) | copy-start | bytes 1572868
  122.5 22.2 %copy-start.13 = (bf16[512,384]{1,0:T(8,128)(2,1)}, bf16[512,384]{1,0:T(8,128)(2,1)S(1)}, u32[]{:S(2)}) copy-start(bf16[512,384]{1,0:T(8,128)(2,1)S(1)} %convolution_convert_fusion) | copy-start | bytes 1179652
  123.4 10.4 %all-to-all-start.2 = ((bf16[16,4,8,128]{3,1,2,0:T(4,128)(2,1)}), bf16[16,4,8,128]{3,1,2,0:T(4,128)(2,1)S(1)}, u32[]{:S(2)}, u32[]{:S(2)}) async-start(bf16[16,4,8,128]{3,1,2,0:T(4,128)(2,1)} %bitcast.20), calls=%async_computation.2 | async-start | bytes 262144 | tf_op jit(solution)/shard_map/all_to_all | solution.py:149
  133.8 14.0 %collective-permute-start.5 = (bf16[64,8,128]{2,1,0:T(8,128)(2,1)S(1)}, bf16[64,8,128]{2,1,0:T(8,128)(2,1)S(1)}, u32[]{:S(2)}, u32[]{:S(2)}) collective-permute-start(bf16[64,8,128]{2,1,0:T(8,128)(2,1)S(1)} %bitcast.217), channel_id=1, source_target_pairs={{0,256},{8,264},{16,272},{24,280},{32,288},{40,296},{48,304},{56,3... | collective-permute-start | bytes 393224 | tf_op jit(solution)/shard_map/ppermute | solution.py:151
  148.1 2.8 %copy-start.6 = (f32[1024,256]{1,0:T(8,128)S(1)}, f32[1024,256]{1,0:T(8,128)}, u32[]{:S(2)}) copy-start(f32[1024,256]{1,0:T(8,128)} %fusion.41) | copy-start | bytes 3145732
  150.6 3.8 %copy-start.11 = (f32[1024,256]{1,0:T(8,128)S(1)}, f32[1024,256]{1,0:T(8,128)}, u32[]{:S(2)}) copy-start(f32[1024,256]{1,0:T(8,128)} %fusion.45) | copy-start | bytes 3145732
  155.9 7.7 %slice-start = ((bf16[512,384]{1,0:T(8,128)(2,1)}), bf16[512,128]{1,0:T(8,128)(2,1)S(1)}, s32[]{:S(2)}) async-start(bf16[512,384]{1,0:T(8,128)(2,1)} %copy-done.13), calls=%async_computation.9 | async-start | bytes 262144 | tf_op jit(solution)/shard_map/slice | solution.py:141
  156.6 46.9 %copy-start.20 = (s32[256]{0:T(256)S(1)}, s32[256]{0:T(256)}, u32[]{:S(2)}) copy-start(s32[256]{0:T(256)} %param.35) | copy-start | bytes 3076
  156.6 64.2 %copy-start.18 = (s32[256]{0:T(256)S(1)}, s32[256]{0:T(256)}, u32[]{:S(2)}) copy-start(s32[256]{0:T(256)} %param.36) | copy-start | bytes 3076
  157.6 12.0 %all-to-all-start.4 = ((bf16[32,2,8,128]{3,2,1,0:T(8,128)(2,1)}), bf16[32,2,8,128]{3,2,1,0:T(8,128)(2,1)S(1)}, u32[]{:S(2)}, u32[]{:S(2)}) async-start(bf16[32,2,8,128]{3,2,1,0:T(8,128)(2,1)} %bitcast.64), calls=%async_computation.4 | async-start | bytes 262144 | tf_op jit(solution)/shard_map/all_to_all | solution.py:162
  163.7 13.6 %collective-permute-start.3 = (bf16[256,128]{0,1:T(8,128)(2,1)S(1)}, bf16[256,128]{0,1:T(8,128)(2,1)S(1)}, u32[]{:S(2)}, u32[]{:S(2)}) collective-permute-start(bf16[256,128]{0,1:T(8,128)(2,1)S(1)} %bitcast.232), channel_id=1, source_target_pairs={{0,8},{8,0},{16,24},{24,16},{32,40},{40,32},{48,56},{56,48},{64,72... | collective-permute-start | bytes 196616 | tf_op jit(solution)/shard_map/ppermute | solution.py:145
  170.4 12.6 %all-to-all-start.6 = ((bf16[32,8,512]{2,1,0:T(8,128)(2,1)}), bf16[32,8,512]{2,1,0:T(8,128)(2,1)S(1)}, u32[]{:S(2)}, u32[]{:S(2)}) async-start(bf16[32,8,512]{2,1,0:T(8,128)(2,1)} %broadcast_in_dim.13), calls=%async_computation.6 | async-start | bytes 524288 | tf_op jit(solution)/shard_map/all_to_all | solution.py:152
  198.4 12.7 %collective-permute-start.8 = (bf16[64,512]{1,0:T(8,128)(2,1)S(1)}, bf16[64,512]{1,0:T(8,128)(2,1)S(1)}, u32[]{:S(2)}, u32[]{:S(2)}) collective-permute-start(bf16[64,512]{1,0:T(8,128)(2,1)S(1)} %reduce_sum.53), channel_id=1, source_target_pairs={{0,4},{1,5},{2,6},{3,7},{4,0},{5,1},{6,2},{7,3},{8,12},{9,13},{10,... | collective-permute-start | bytes 196616 | tf_op jit(solution)/shard_map/ppermute | solution.py:173
  (6 other events, 8.5 us)

commit v2 on v1

v2 whole, which is shorter than its diff:
```python
import math

import jax
import jax.numpy as jnp
import numpy as np
from jax import lax
from jax.experimental import pallas as pl
from jax.experimental.pallas import tpu as pltpu
from jax.sharding import PartitionSpec as P

NORM_EPS = 1e-05
F32 = jnp.float32
BF16 = jnp.bfloat16

COORDS = [(z, y, x, c) for z in range(2) for y in range(4) for x in range(4) for c in range(2)]


def ctx_id(z, y, x, c):
    return ((z * 4 + y) * 4 + x) * 2 + c


def ctx_perm(move):
    return [(ctx_id(*at), ctx_id(*move(*at))) for at in COORDS]


PERM_CORE = ctx_perm(lambda z, y, x, c: (z, y, x, 1 - c))
PERM_Z = ctx_perm(lambda z, y, x, c: (1 - z, y, x, c))
PERM_Z_UP = [(i, i + 32) for i in range(32)]
PERM_X = [ctx_perm(lambda z, y, x, c, k=k: (z, y, (x + k) % 4, c)) for k in range(4)]
PERM_Y = [ctx_perm(lambda z, y, x, c, k=k: (z, (y + k) % 4, x, c)) for k in range(4)]
GROUPS_X = [[ctx_id(z, y, x, c) for x in range(4)] for z in range(2) for y in range(4) for c in range(2)]
GROUPS_Y = [[ctx_id(z, y, x, c) for y in range(4)] for z in range(2) for x in range(4) for c in range(2)]
GROUPS_PLANE = [
    [ctx_id(z, y, x, c) for y in range(4) for x in range(4) for c in range(2)] for z in range(2)
]
GROUPS_CORE = [
    [ctx_id(z, y, x, c) for z in range(2) for y in range(4) for x in range(4)] for c in range(2)
]
GROUPS_TP = [[0, 1, 2, 3], [4, 5, 6, 7]]


def weight_routes(flip):
    pairs = []
    for i in range(64):
        for q in range(8):
            plane, core, chip, half = i // 8, (i % 8) // 4, (i % 4) * 4 + q // 2, q % 2
            z = half ^ flip
            pairs.append((i * 8 + q, (z * 32 + chip * 2 + core) * 8 + plane))
    return pairs


ROUTE_SAME, ROUTE_FLIP = weight_routes(0), weight_routes(1)


def tables():
    index = np.arange(128)
    inner = 2.0 * math.pi * (np.outer(index, index) % 128) / 128
    outer = 2.0 * math.pi * np.outer(index, index) / 16384
    cos, sin = np.cos(inner), np.sin(inner)
    first = np.concatenate([cos[:, :64], -sin[:, :64]], axis=0)
    second = np.block([[cos, -sin], [sin, cos]])
    back = np.block([[cos, sin], [-sin, cos]])
    last = np.concatenate([cos[:64], -sin[:64]], axis=1) / 16384.0
    return (first, second, back, last, np.cos(outer), np.sin(outer))


FIRST, SECOND, BACK, LAST, COS_TW, SIN_TW = tables()


def mm(left, right):
    return jnp.dot(left, right, preferred_element_type=F32)


def whole(count):
    return [pl.BlockSpec(memory_space=pltpu.VMEM)] * count


SCALARS = pl.BlockSpec(memory_space=pltpu.SMEM)


def spectrum(rows, scratch, first, second, cos_tw, sin_tw):
    scratch[...] = rows
    cube = jnp.concatenate([scratch[pl.ds(c, 64, stride=8), :] for c in range(8)], axis=1)
    step = mm(first, cube.astype(BF16))
    parts = []
    for c in range(8):
        real, imag = step[:128, c * 128 : c * 128 + 128], step[128:, c * 128 : c * 128 + 128]
        parts.append(
            jnp.concatenate(
                [(real * cos_tw + imag * sin_tw).astype(BF16), (imag * cos_tw - real * sin_tw).astype(BF16)],
                axis=1,
            )
        )
    return mm(jnp.concatenate(parts, axis=0), second)


def filter_kernel(z_ref, own_ref, got_ref, first, second, cos_tw, sin_tw, low_ref, all_ref, scratch):
    upper = z_ref[0] == 1
    own, got = own_ref[...].astype(F32), got_ref[...].astype(F32)
    args = (scratch, first[...], second[...], cos_tw[...], sin_tw[...])
    low = spectrum(jnp.where(upper, got, own), *args)
    high = spectrum(own, *args)
    odd = lax.broadcasted_iota(jnp.int32, (1024, 256), 0) & 1
    low_ref[...] = low
    all_ref[...] = jnp.where(odd == 1, -low, low) + high


def conv_kernel(
    z_ref, sig_ref, low_ref, all_ref, piece_ref, first, second, back, last, cos_tw_ref, sin_tw_ref, out_ref, scratch
):
    z = z_ref[0]
    cos_tw, sin_tw = cos_tw_ref[...], sin_tw_ref[...]
    args = (scratch, first[...], second[...], cos_tw, sin_tw)
    own = spectrum(sig_ref[z].astype(F32), *args)
    old = spectrum(sig_ref[0].astype(F32) * z.astype(F32), *args)
    low, every = low_ref[...], all_ref[...]
    own_r, own_i, old_r, old_i = own[:, :128], own[:, 128:], old[:, :128], old[:, 128:]
    low_r, low_i, all_r, all_i = low[:, :128], low[:, 128:], every[:, :128], every[:, 128:]
    real = own_r * low_r - own_i * low_i + old_r * all_r - old_i * all_i
    imag = own_r * low_i + own_i * low_r + old_r * all_i + old_i * all_r
    half = mm(jnp.concatenate([real.astype(BF16), imag.astype(BF16)], axis=1), back[...])
    parts = []
    for c in range(8):
        real, imag = half[c * 128 : c * 128 + 128, :128], half[c * 128 : c * 128 + 128, 128:]
        parts.append(
            jnp.concatenate(
                [(real * cos_tw - imag * sin_tw).astype(BF16), (imag * cos_tw + real * sin_tw).astype(BF16)],
                axis=0,
            )
        )
    result = mm(last[...], jnp.concatenate(parts, axis=1))
    for c in range(8):
        scratch[pl.ds(c, 64, stride=8), :] = result[:, c * 128 : c * 128 + 128]
    piece = piece_ref[...]
    for d in range(32):
        out_ref[d, :16] = scratch[d * 16 : d * 16 + 16].astype(BF16)
        out_ref[d, 16:] = piece


def proj_kernel(at_ref, own_ref, other_ref, low_ref, b0, b1, b2, b3, sig_ref, gate_ref):
    y_at, x_at, core = at_ref[0], at_ref[1], at_ref[2]

    def block(ref, lead, row):
        return jnp.concatenate([ref[lead, row + 128 * g : row + 128 * g + 128, :] for g in range(3)], axis=1)

    for part, tokens in enumerate((own_ref, other_ref)):
        total = jnp.zeros((256, 384), F32)
        for y in range(4):
            for x in (0, 2):
                left = tokens[:, (y * 4 + x) * 128 : (y * 4 + x) * 128 + 256]
                right = jnp.concatenate([block(low_ref, y, x * 384), block(low_ref, y, x * 384 + 384)], axis=0)
                total += mm(left, right)
        for step, ref in enumerate((b0, b1, b2, b3)):
            x = lax.rem(x_at + 4 - step, 4)
            for k in (0, 2):
                starts = [2048 + (lax.rem(y_at + 4 - j, 4) * 4 + x) * 128 for j in (k, k + 1)]
                left = jnp.concatenate([tokens[:, pl.ds(pl.multiple_of(s, 128), 128)] for s in starts], axis=1)
                right = jnp.concatenate([block(ref, k, 0), block(ref, k + 1, 0)], axis=0)
                total += mm(left, right)
        proj = total.astype(BF16).astype(F32)
        gated = proj[:, 128:256] * proj[:, 256:]
        place = core if part == 0 else 1 - core
        first, second = gated[:128].T, gated[128:].T
        for p in range(16):
            rows = jnp.concatenate([first[p * 8 : p * 8 + 8], second[p * 8 : p * 8 + 8]], axis=0).astype(BF16)
            sig_ref[0, p, pl.ds(pl.multiple_of(place * 16, 16), 16), :] = rows
            sig_ref[1, p, pl.ds(pl.multiple_of(place * 16, 16), 16), :] = rows
        gate_ref[place, 0] = proj[:128, :128].T.astype(BF16)
        gate_ref[place, 1] = proj[128:, :128].T.astype(BF16)


def mix_kernel(core_ref, got_ref, keep_ref, other_ref, base_ref, out_ref):
    core = core_ref[0]
    keep, other = keep_ref[...].astype(F32), other_ref[...].astype(F32)
    conv = got_ref[:, :16, :].astype(F32)
    for rb in range(2):
        total = base_ref[rb * 128 : rb * 128 + 128, :]
        for c in range(2):
            cube = jnp.concatenate([conv[p * 2 + c, rb * 8 : rb * 8 + 8] for p in range(16)], axis=0)
            gate = jnp.where(core == c, keep[rb], other[rb])
            mixed = (gate * cube).T.astype(BF16)
            weights = []
            for p in range(16):
                piece = got_ref[p * 2 + c, 16:, :].astype(F32)
                weights.append(jnp.concatenate([piece[v * 8 : v * 8 + 8] for v in range(4)], axis=1))
            total += mm(mixed, jnp.concatenate(weights, axis=0).astype(BF16))
        out_ref[rb * 128 : rb * 128 + 128, :] = total.astype(BF16)


def call(kernel, outs, specs, scratch, flops, args):
    return pl.pallas_call(
        kernel,
        out_shape=outs,
        in_specs=specs,
        out_specs=jax.tree.map(lambda _: pl.BlockSpec(memory_space=pltpu.VMEM), outs),
        scratch_shapes=scratch,
        compiler_params=pltpu.CompilerParams(vmem_limit_bytes=40 * 2**20),
        cost_estimate=pl.CostEstimate(flops=flops, bytes_accessed=4 * 2**20, transcendentals=0),
    )(*args)


def shape(dims, dtype):
    return jax.ShapeDtypeStruct(dims, dtype)


def by_position(own, other, place):
    return jnp.where(place == 0, jnp.stack([own, other]), jnp.stack([other, own]))


def filter_spectra(z, own, got):
    consts = (jnp.asarray(FIRST, BF16), jnp.asarray(SECOND, BF16), jnp.asarray(COS_TW, F32), jnp.asarray(SIN_TW, F32))
    return call(
        filter_kernel,
        (shape((1024, 256), F32), shape((1024, 256), F32)),
        [SCALARS] + whole(6),
        [pltpu.VMEM((512, 128), F32)],
        4 * 10**8,
        (z, own, got, *consts),
    )


def convolve(z, signal, low, every, piece):
    consts = [jnp.asarray(t, BF16) for t in (FIRST, SECOND, BACK, LAST)]
    consts += [jnp.asarray(t, F32) for t in (COS_TW, SIN_TW)]
    return call(
        conv_kernel,
        shape((32, 48, 128), BF16),
        [SCALARS] + whole(10),
        [pltpu.VMEM((512, 128), F32)],
        6 * 10**8,
        (z, signal, low, every, piece, *consts),
    )


def gather_weights(w_in, long_filter, ctx):
    core, z = ctx % 2, ctx // 32
    halves = w_in.transpose(1, 0, 2).reshape(3, 64, 2, 128)
    taps = long_filter.reshape(256, 2, 128)

    def half_of(which):
        weights = lax.dynamic_index_in_dim(halves, which, 2, False).reshape(192, 128)
        return jnp.concatenate([weights, lax.dynamic_index_in_dim(taps, which, 1, False)], axis=0)

    keep = half_of(core)
    got = lax.ppermute(half_of(1 - core), "ctx", PERM_CORE)
    both = by_position(keep, got, core)
    own = both[:, :192].reshape(2, 3, 64, 128).transpose(1, 0, 2, 3).reshape(384, 128)
    taps = both[:, 192:].reshape(2, 2, 128, 4, 4, 8).transpose(4, 3, 0, 1, 5, 2).reshape(4, 128, 128)
    other = lax.ppermute(own, "ctx", PERM_Z)
    low = jnp.where(z == 0, own, other)
    high = jnp.where(z == 0, other, own)

    along_y = jnp.stack([high] + [lax.ppermute(high, "ctx", PERM_Y[k]) for k in (1, 2, 3)])
    low = jnp.concatenate([jnp.broadcast_to(low, (4, 384, 128)), taps], axis=1)
    low = lax.all_to_all(low, "ctx", 0, 0, axis_index_groups=GROUPS_X, tiled=True)
    taps = low[:, 384:].reshape(4, 4, 32, 128).transpose(1, 0, 2, 3).reshape(4, 128, 128)
    low = jnp.broadcast_to(low[:, :384].reshape(1, 1536, 128), (4, 1536, 128))
    low = jnp.concatenate([low, taps], axis=1)
    low = lax.all_to_all(low, "ctx", 0, 0, axis_index_groups=GROUPS_Y, tiled=True)
    highs = [along_y] + [lax.ppermute(along_y, "ctx", PERM_X[k]) for k in (1, 2, 3)]
    return low, highs, low[:, 1536:].reshape(512, 128)


def output_weights(w_out, w_unembed, z):
    partial = mm(w_out, w_unembed)
    piece = lax.psum_scatter(partial, "tp", scatter_dimension=0, tiled=True).astype(BF16).reshape(16, 128)
    same = lax.ppermute(piece, ("ctx", "tp"), ROUTE_SAME)
    flip = lax.ppermute(piece, ("ctx", "tp"), ROUTE_FLIP)
    return by_position(same, flip, z).reshape(8, 4, 128).transpose(1, 0, 2).reshape(32, 128)


def per_device(tokens_in, pre_gain, w_in, w_out, long_filter, w_unembed, target_ids, score_mask):
    ctx, tp = lax.axis_index("ctx"), lax.axis_index("tp")
    core, z = ctx % 2, ctx // 32
    z_at = z.reshape(1).astype(jnp.int32)
    low, highs, taps = gather_weights(w_in, long_filter, ctx)
    piece = output_weights(w_out, w_unembed, z)

    stream = tokens_in.astype(F32)
    scale = lax.rsqrt(jnp.mean(stream * stream, axis=1, keepdims=True) + NORM_EPS)
    normed = (stream * scale * pre_gain.astype(F32)).astype(BF16)
    beside = lax.ppermute(normed, "ctx", PERM_CORE)

    at = jnp.stack([(ctx // 8) % 4, (ctx // 2) % 4, core]).astype(jnp.int32)
    signal, gate = call(
        proj_kernel,
        (shape((2, 16, 32, 128), BF16), shape((2, 2, 128, 128), BF16)),
        [SCALARS] + whole(7),
        [],
        16 * 10**8,
        (at, normed, beside, low, *highs),
    )
    signal = lax.all_to_all(
        signal.reshape(32, 32, 128), "ctx", 0, 0, axis_index_groups=GROUPS_CORE, tiled=True
    ).reshape(2, 512, 128)
    gate_keep = lax.dynamic_index_in_dim(gate, core, 0, False)
    gate_got = lax.ppermute(lax.dynamic_index_in_dim(gate, 1 - core, 0, False), "ctx", PERM_CORE)

    spectra = filter_spectra(z_at, taps, lax.ppermute(taps, "ctx", PERM_Z_UP))
    conv = convolve(z_at, signal, *spectra, piece)
    conv = lax.all_to_all(conv, "ctx", 0, 0, axis_index_groups=GROUPS_PLANE, tiled=True)

    width = w_unembed.shape[0]
    base = mm(lax.dynamic_slice_in_dim(tokens_in, tp * width, width, 1), w_unembed)
    logits = call(
        mix_kernel,
        shape((256, 512), BF16),
        [SCALARS] + whole(4),
        [],
        10**8,
        (core.reshape(1).astype(jnp.int32), conv, gate_keep, gate_got, base),
    )
    logits = lax.all_to_all(logits.reshape(4, 64, 512), "tp", 0, 0, axis_index_groups=GROUPS_TP, tiled=True)
    logits = jnp.sum(logits.astype(F32), axis=0).astype(BF16)
    far = lax.ppermute(logits, "tp", [(i, i ^ 4) for i in range(8)])
    logits = logits.astype(F32) + far.astype(F32)

    row_top = jnp.max(logits, axis=1, keepdims=True)
    log_total = row_top[:, 0] + jnp.log(jnp.sum(jnp.exp(logits - row_top), axis=1))
    ids = lax.dynamic_slice_in_dim(target_ids, (tp % 4) * 64, 64, 0)
    vocab_index = lax.broadcasted_iota(jnp.int32, (64, 512), 1)
    picked = jnp.sum(jnp.where(vocab_index == ids[:, None], logits, 0.0), axis=1)
    scores = jnp.broadcast_to((picked - log_total)[None, None, :], (4, 8, 64))
    scores = lax.all_to_all(scores, "tp", 0, 0, axis_index_groups=GROUPS_TP, tiled=True)
    return scores[:, 0].reshape(256) * score_mask.astype(F32)


def solution(mesh):
    return jax.shard_map(
        per_device,
        mesh=mesh,
        in_specs=(
            P("ctx", None),
            P(),
            P("ctx", None, "tp"),
            P("ctx", "tp"),
            P("ctx", "tp"),
            P("tp", None),
            P("ctx"),
            P("ctx"),
        ),
        out_specs=P("ctx"),
        check_vma=False,
    )
```

time: 223 us -> 268 us (1.20)
  blocking collectives: 23 us -> 88.9 us
  matrix products: 22.8 us -> 2.19 us
  local copies, waits for them, and re-layouts: 30.7 us -> 11.5 us
  waiting for transfers between devices: 38.9 us -> 54.2 us
  Pallas kernels: 0 us -> 8.11 us
  other arithmetic: 10.9 us -> 8.21 us
    unnamed x0 -> x1, blocking collectives: none -> 55.8 us
    ppermute x7 -> x12, waiting for transfers between devices: 0.02 us -> 41.5 us  [the longest x3 15.2 us: gather_weights(): lax.ppermute(along_y, 'ctx', PERM_X[k])]
    all_to_all x6 -> x2, waiting for transfers between devices: 27.4 us -> 0.01 us  [the longest x1 0.01 us: gather_weights(): lax.all_to_all(low, 'ctx', 0, 0, axis_index_groups=GROUPS_Y, tiled=True)]
    dot_general x20 -> x2, matrix products: 22.8 us -> 2.19 us  [mm(): return jnp.dot(left, right, preferred_element_type=F32)]
    all_to_all x6 -> x2, starting transfers between devices: 33.9 us -> 19.3 us  [the longest x1 14.8 us: per_device(): lax.all_to_all(signal.reshape(32, 32, 128), 'ctx', 0, 0, axis_index_group...]
    all_to_all x1 -> x2, blocking collectives: 15.1 us -> 25.1 us  [the longest x1 12.7 us: per_device(): lax.all_to_all(logits.reshape(4, 64, 512), 'tp', 0, 0, axis_index_groups=...]
    ppermute x7 -> x12, starting transfers between devices: 47.5 us -> 55.6 us  [the longest x1 15.7 us: gather_weights(): other = lax.ppermute(own, 'ctx', PERM_Z)]
    pallas_call x0 -> x4, Pallas kernels: none -> 8.11 us  [call(): pl.pallas_call(kernel, out_shape=outs, in_specs=specs, out_specs=jax.tree...]
  transfers between devices with their start and end apart: 16 -> 17, of which waited for: 6 -> 10; matrix products, arithmetic and copies ran while one was open for 26% -> 4% of each run, Pallas kernels for 0% -> 0%
where the time goes in v2:
time: 268 us; the launch traced here: 267 us
  starting transfers between devices  92.5 us (35%)
  blocking collectives  88.9 us (33%)
  waiting for transfers between devices  54.2 us (20%)
  local copies, waits for them, and re-layouts  11.5 us (4%)
  other arithmetic  8.21 us (3%)
  Pallas kernels  8.11 us (3%)
    unnamed x1, blocking collectives  55.8 us
    ppermute x1, starting transfers between devices, gather_weights(): other = lax.ppermute(own, 'ctx', PERM_Z)  15.7 us
    ppermute x3, waiting for transfers between devices, gather_weights(): lax.ppermute(along_y, 'ctx', PERM_X[k])  15.2 us
    ppermute x3, waiting for transfers between devices, gather_weights(): lax.ppermute(high, 'ctx', PERM_Y[k])  14.9 us
    all_to_all x1, starting transfers between devices, per_device(): lax.all_to_all(signal.reshape(32, 32, 128), 'ctx', 0, 0, axis_index_group...  14.8 us
    all_to_all x1, blocking collectives, per_device(): lax.all_to_all(logits.reshape(4, 64, 512), 'tp', 0, 0, axis_index_groups=...  12.7 us
    all_to_all x1, blocking collectives, gather_weights(): lax.all_to_all(low, 'ctx', 0, 0, axis_index_groups=GROUPS_X, tiled=True)  12.4 us
    ppermute x1, starting transfers between devices, per_device(): spectra = filter_spectra(z_at, taps, lax.ppermute(taps, 'ctx', PERM_Z_UP))  12.1 us
  transfers between devices with their start and end apart: 17, of which 10 were waited for; matrix products, arithmetic and copies ran while one was open for 4% of the time, Pallas kernels for 0%

profile of v2, /device:TPU:6, one launch (start us, length us, event | category | flops | bytes accessed | tf_op | source)
XLA Modules:
  0.0 266.7 jit_solution(6340158696244533123)
XLA Ops:
  2.4 1.9 collective-permute-start.1
  5.0 2.1 fusion
  7.4 15.7 %collective-permute-start.2 = (bf16[384,128]{1,0:T(8,128)(2,1)S(1)}, bf16[384,128]{1,0:T(8,128)(2,1)S(1)}, u32[]{:S(2)}, u32[]{:S(2)}) collective-permute-start(bf16[384,128]{1,0:T(8,128)(2,1)S(1)} %bitcast.66), channel_id=1, source_target_pairs={{0,256},{8,264},{16,272},{24,280},{32,288},{40,296},{48,304},{56,3... | collective-permute-start | bytes 294920 | tf_op jit(solution)/shard_map/ppermute | solution.py:249
  23.1 2.2 fusion.2.own_ref
  25.3 2.1 collective-permute-start
  27.8 12.4 %all_to_all.30 = bf16[4,512,128]{2,1,0:T(8,128)(2,1)S(1)} all-to-all(bf16[4,512,128]{2,1,0:T(8,128)(2,1)S(1)} %pad_maximum_fusion.1), channel_id=1, replica_groups={{0,16,32,48},{8,24,40,56},{64,80,96,112},{72,88,104,120},{128,144,160,1..., dimensions={0} | all-to-all | bytes 1048576 | tf_op jit(solution)/shard_map/all_to_all | solution.py:255
  41.9 4.5 %all-to-all-start.1 = ((bf16[4,1664,128]{2,1,0:T(8,128)(2,1)}), bf16[4,1664,128]{2,1,0:T(8,128)(2,1)}, u32[]{:S(2)}, u32[]{:S(2)}) async-start(bf16[4,1664,128]{2,1,0:T(8,128)(2,1)} %pad_maximum_fusion), calls=%async_computation.1 | async-start | bytes 3407872 | tf_op jit(solution)/shard_map/all_to_all | solution.py:259
  46.4 5.1 %collective-permute-start.5 = (bf16[384,128]{1,0:T(8,128)(2,1)S(1)}, bf16[384,128]{1,0:T(8,128)(2,1)S(1)}, u32[]{:S(2)}, u32[]{:S(2)}) collective-permute-start(bf16[384,128]{1,0:T(8,128)(2,1)S(1)} %get-tuple-element.15), channel_id=1, source_target_pairs={{0,192},{8,200},{16,208},{24,216},{32,224},{40,232},{48,240},{56,2... | collective-permute-start | bytes 294920 | tf_op jit(solution)/shard_map/ppermute | solution.py:253
  51.5 2.8 %collective-permute-start.4 = (bf16[384,128]{1,0:T(8,128)(2,1)S(1)}, bf16[384,128]{1,0:T(8,128)(2,1)S(1)}, u32[]{:S(2)}, u32[]{:S(2)}) collective-permute-start(bf16[384,128]{1,0:T(8,128)(2,1)S(1)} %get-tuple-element.15), channel_id=1, source_target_pairs={{0,128},{8,136},{16,144},{24,152},{32,160},{40,168},{48,176},{56,1... | collective-permute-start | bytes 294920 | tf_op jit(solution)/shard_map/ppermute | solution.py:253
  54.3 2.8 %collective-permute-start.3 = (bf16[384,128]{1,0:T(8,128)(2,1)S(1)}, bf16[384,128]{1,0:T(8,128)(2,1)S(1)}, u32[]{:S(2)}, u32[]{:S(2)}) collective-permute-start(bf16[384,128]{1,0:T(8,128)(2,1)S(1)} %get-tuple-element.15), channel_id=1, source_target_pairs={{0,64},{8,72},{16,80},{24,88},{32,96},{40,104},{48,112},{56,120},{... | collective-permute-start | bytes 294920 | tf_op jit(solution)/shard_map/ppermute | solution.py:253
  57.0 12.6 %collective-permute-done.5 = bf16[384,128]{1,0:T(8,128)(2,1)S(1)} collective-permute-done((bf16[384,128]{1,0:T(8,128)(2,1)S(1)}, bf16[384,128]{1,0:T(8,128)(2,1)S(1)}, u32[]{:S(2)}, u32[]{:S(2)}) %collective-permute-start.5) | collective-permute-done | bytes 98336 | tf_op jit(solution)/shard_map/ppermute | solution.py:253
  69.7 1.6 collective-permute-done.4
  72.0 4.0 %collective-permute-start.6 = (bf16[4,384,128]{2,1,0:T(8,128)(2,1)S(1)}, bf16[4,384,128]{2,1,0:T(8,128)(2,1)S(1)}, u32[]{:S(2)}, u32[]{:S(2)}) collective-permute-start(bf16[4,384,128]{2,1,0:T(8,128)(2,1)S(1)} %pad_maximum_fusion.2.b0), channel_id=1, source_target_pairs={{0,16},{8,24},{16,32},{24,40},{32,48},{40,56},{48,0},{56,8},{64,80... | collective-permute-start | bytes 1179656 | tf_op jit(solution)/shard_map/ppermute | solution.py:260
  76.0 1.9 collective-permute-start.7
  77.9 3.3 %collective-permute-start.8 = (bf16[4,384,128]{2,1,0:T(8,128)(2,1)S(1)}, bf16[4,384,128]{2,1,0:T(8,128)(2,1)}, u32[]{:S(2)}, u32[]{:S(2)}) collective-permute-start(bf16[4,384,128]{2,1,0:T(8,128)(2,1)S(1)} %pad_maximum_fusion.2.b0), channel_id=1, source_target_pairs={{0,48},{8,56},{16,0},{24,8},{32,16},{40,24},{48,32},{56,40},{64,11... | collective-permute-start | bytes 1179656 | tf_op jit(solution)/shard_map/ppermute | solution.py:260
  81.4 9.5 %collective-permute-done.6.b1 = bf16[4,384,128]{2,1,0:T(8,128)(2,1)S(1)} collective-permute-done((bf16[4,384,128]{2,1,0:T(8,128)(2,1)S(1)}, bf16[4,384,128]{2,1,0:T(8,128)(2,1)S(1)}, u32[]{:S(2)}, u32[]{:S(2)}) %collective-permute-start.6) | collective-permute-done | bytes 393248 | tf_op jit(solution)/shard_map/ppermute | solution.py:260
  91.6 5.0 %collective-permute-done.8.b3 = bf16[4,384,128]{2,1,0:T(8,128)(2,1)} collective-permute-done((bf16[4,384,128]{2,1,0:T(8,128)(2,1)S(1)}, bf16[4,384,128]{2,1,0:T(8,128)(2,1)}, u32[]{:S(2)}, u32[]{:S(2)}) %collective-permute-start.8) | collective-permute-done | bytes 393248 | tf_op jit(solution)/shard_map/ppermute | solution.py:260
  96.6 4.7 %shard_map.172 = (bf16[2,16,32,128]{3,2,1,0:T(8,128)(2,1)S(1)}, bf16[2,2,128,128]{3,2,1,0:T(8,128)(2,1)S(1)}) custom-call(s32[3]{0:T(128)S(1)} %pad_add_fusion.at_ref, bf16[256,4096]{1,0:T(8,128)(2,1)S(1)} %fusion.2.own_ref, bf16[256,4096]{1,0:T(8,128)(2,1)} %collective-permute-done.other_ref, bf16[4,1664,128]{2,1,0:T(8,128)(2,1)} %all-to-all-done.1.low_ref, ...), custom_call_target="tpu_custom_call" | custom-call | flops 1600000000 | bytes 4194304 | tf_op jit(solution)/shard_map/pallas_call | solution.py:191
  102.7 14.8 %all-to-all-start.2 = ((bf16[32,32,128]{2,1,0:T(8,128)(2,1)}), bf16[32,32,128]{2,1,0:T(8,128)(2,1)S(1)}, u32[]{:S(2)}, u32[]{:S(2)}) async-start(bf16[32,32,128]{2,1,0:T(8,128)(2,1)} %bitcast.54), calls=%async_computation.2 | async-start | bytes 524288 | tf_op jit(solution)/shard_map/all_to_all | solution.py:293
  120.2 55.8 %all-reduce = bf16[32,512]{1,0:T(8,128)(2,1)S(1)} all-reduce(f32[32,512]{1,0:T(8,128)S(1)} %fusion.7), channel_id=2, replica_groups=mesh['ctx'=64,'tp'=8] {'tp'}, use_global_device_ids=true, to_apply=%region_1.2.clone | all-reduce | flops 16384 | bytes 98304
  177.0 12.1 %collective-permute-start.9 = (bf16[512,128]{1,0:T(8,128)(2,1)S(1)}, bf16[512,128]{1,0:T(8,128)(2,1)S(1)}, u32[]{:S(2)}, u32[]{:S(2)}) collective-permute-start(bf16[512,128]{1,0:T(8,128)(2,1)S(1)} %bitcast.55), channel_id=1, source_target_pairs={{0,256},{8,264},{16,272},{24,280},{32,288},{40,296},{48,304},{56,3... | collective-permute-start | bytes 393224 | tf_op jit(solution)/shard_map/ppermute | solution.py:299
  189.2 1.9 collective-permute-start.11
  191.1 1.9 collective-permute-start.10
  193.0 10.4 %collective-permute-done.11 = bf16[16,128]{1,0:T(8,128)(2,1)S(1)} collective-permute-done((bf16[16,128]{1,0:T(8,128)(2,1)S(1)}, bf16[16,128]{1,0:T(8,128)(2,1)S(1)}, u32[]{:S(2)}, u32[]{:S(2)}) %collective-permute-start.11) | collective-permute-done | bytes 4128 | tf_op jit(solution)/shard_map/ppermute | solution.py:268
  209.6 2.0 shard_map.174
  211.6 10.3 %all-to-all-start.3 = ((bf16[32,48,128]{2,1,0:T(8,128)(2,1)}), bf16[32,48,128]{2,1,0:T(8,128)(2,1)S(1)}, u32[]{:S(2)}, u32[]{:S(2)}) async-start(bf16[32,48,128]{2,1,0:T(8,128)(2,1)} %shard_map.174), calls=%async_computation.3 | async-start | bytes 786432 | tf_op jit(solution)/shard_map/all_to_all | solution.py:301
  222.0 2.1 collective-permute-start.12
  225.4 4.7 %all-to-all-done.3.got_ref = bf16[32,48,128]{2,1,0:T(8,128)(2,1)S(1)} async-done(((bf16[32,48,128]{2,1,0:T(8,128)(2,1)}), bf16[32,48,128]{2,1,0:T(8,128)(2,1)S(1)}, u32[]{:S(2)}, u32[]{:S(2)}) %all-to-all-start.3) | async-done | bytes 393248 | tf_op jit(solution)/shard_map/all_to_all | solution.py:301
  230.4 12.7 %all_to_all.31 = bf16[4,64,512]{2,1,0:T(8,128)(2,1)S(1)} all-to-all(bf16[4,64,512]{2,1,0:T(8,128)(2,1)S(1)} %bitcast.52), channel_id=1, replica_groups={{0,1,2,3},{4,5,6,7},{8,9,10,11},{12,13,14,15},{16,17,18,19},{20,21,22,2..., dimensions={0} | all-to-all | bytes 524288 | tf_op jit(solution)/shard_map/all_to_all | solution.py:313
  243.1 5.3 %collective-permute-start.13 = (bf16[64,512]{1,0:T(8,128)(2,1)S(1)}, bf16[64,512]{1,0:T(8,128)(2,1)S(1)}, u32[]{:S(2)}, u32[]{:S(2)}) collective-permute-start(bf16[64,512]{1,0:T(8,128)(2,1)S(1)} %reduce_sum.40), channel_id=1, source_target_pairs={{0,4},{1,5},{2,6},{3,7},{4,0},{5,1},{6,2},{7,3},{8,12},{9,13},{10,... | collective-permute-start | bytes 196616 | tf_op jit(solution)/shard_map/ppermute | solution.py:315
  248.5 8.0 %collective-permute-done.13 = bf16[64,512]{1,0:T(8,128)(2,1)S(1)} collective-permute-done((bf16[64,512]{1,0:T(8,128)(2,1)S(1)}, bf16[64,512]{1,0:T(8,128)(2,1)S(1)}, u32[]{:S(2)}, u32[]{:S(2)}) %collective-permute-start.13) | collective-permute-done | bytes 65568 | tf_op jit(solution)/shard_map/ppermute | solution.py:315
  256.9 7.9 %all_to_all.32 = f32[4,1,512]{2,1,0:T(1,128)S(1)} all-to-all(f32[4,1,512]{2,1,0:T(1,128)S(1)} %reshape.109), channel_id=1, replica_groups={{0,1,2,3},{4,5,6,7},{8,9,10,11},{12,13,14,15},{16,17,18,19},{20,21,22,2..., dimensions={0} | all-to-all | bytes 16384 | tf_op jit(solution)/shard_map/all_to_all | solution.py:324
  (95 shorter events, 21.4 us)
Async XLA Ops:
  0.0 119.3 %copy-start = (bf16[512,512]{1,0:T(8,128)(2,1)S(1)}, bf16[512,512]{1,0:T(8,128)(2,1)}, u32[]{:S(2)}) copy-start(bf16[512,512]{1,0:T(8,128)(2,1)} %param.23) | copy-start | bytes 1572868
  2.4 4.9 %collective-permute-start.1 = (bf16[448,128]{1,0:T(8,128)(2,1)S(1)}, bf16[448,128]{1,0:T(8,128)(2,1)S(1)}, u32[]{:S(2)}, u32[]{:S(2)}) collective-permute-start(bf16[448,128]{1,0:T(8,128)(2,1)S(1)} %pad_maximum_fusion.3), channel_id=1, source_target_pairs={{0,8},{8,0},{16,24},{24,16},{32,40},{40,32},{48,56},{56,48},{64,72... | collective-permute-start | bytes 344072 | tf_op jit(solution)/shard_map/ppermute | solution.py:245
  7.4 20.3 %collective-permute-start.2 = (bf16[384,128]{1,0:T(8,128)(2,1)S(1)}, bf16[384,128]{1,0:T(8,128)(2,1)S(1)}, u32[]{:S(2)}, u32[]{:S(2)}) collective-permute-start(bf16[384,128]{1,0:T(8,128)(2,1)S(1)} %bitcast.66), channel_id=1, source_target_pairs={{0,256},{8,264},{16,272},{24,280},{32,288},{40,296},{48,304},{56,3... | collective-permute-start | bytes 294920 | tf_op jit(solution)/shard_map/ppermute | solution.py:249
  25.3 71.3 %collective-permute-start = (bf16[256,4096]{1,0:T(8,128)(2,1)S(1)}, bf16[256,4096]{1,0:T(8,128)(2,1)}, u32[]{:S(2)}, u32[]{:S(2)}) collective-permute-start(bf16[256,4096]{1,0:T(8,128)(2,1)S(1)} %fusion.2.own_ref), channel_id=1, source_target_pairs={{0,8},{8,0},{16,24},{24,16},{32,40},{40,32},{48,56},{56,48},{64,72... | collective-permute-start | bytes 6291464 | tf_op jit(solution)/shard_map/ppermute | solution.py:282
  41.9 54.7 %all-to-all-start.1 = ((bf16[4,1664,128]{2,1,0:T(8,128)(2,1)}), bf16[4,1664,128]{2,1,0:T(8,128)(2,1)}, u32[]{:S(2)}, u32[]{:S(2)}) async-start(bf16[4,1664,128]{2,1,0:T(8,128)(2,1)} %pad_maximum_fusion), calls=%async_computation.1 | async-start | bytes 3407872 | tf_op jit(solution)/shard_map/all_to_all | solution.py:259
  46.4 23.3 %collective-permute-start.5 = (bf16[384,128]{1,0:T(8,128)(2,1)S(1)}, bf16[384,128]{1,0:T(8,128)(2,1)S(1)}, u32[]{:S(2)}, u32[]{:S(2)}) collective-permute-start(bf16[384,128]{1,0:T(8,128)(2,1)S(1)} %get-tuple-element.15), channel_id=1, source_target_pairs={{0,192},{8,200},{16,208},{24,216},{32,224},{40,232},{48,240},{56,2... | collective-permute-start | bytes 294920 | tf_op jit(solution)/shard_map/ppermute | solution.py:253
  51.5 19.7 %collective-permute-start.4 = (bf16[384,128]{1,0:T(8,128)(2,1)S(1)}, bf16[384,128]{1,0:T(8,128)(2,1)S(1)}, u32[]{:S(2)}, u32[]{:S(2)}) collective-permute-start(bf16[384,128]{1,0:T(8,128)(2,1)S(1)} %get-tuple-element.15), channel_id=1, source_target_pairs={{0,128},{8,136},{16,144},{24,152},{32,160},{40,168},{48,176},{56,1... | collective-permute-start | bytes 294920 | tf_op jit(solution)/shard_map/ppermute | solution.py:253
  54.3 17.7 %collective-permute-start.3 = (bf16[384,128]{1,0:T(8,128)(2,1)S(1)}, bf16[384,128]{1,0:T(8,128)(2,1)S(1)}, u32[]{:S(2)}, u32[]{:S(2)}) collective-permute-start(bf16[384,128]{1,0:T(8,128)(2,1)S(1)} %get-tuple-element.15), channel_id=1, source_target_pairs={{0,64},{8,72},{16,80},{24,88},{32,96},{40,104},{48,112},{56,120},{... | collective-permute-start | bytes 294920 | tf_op jit(solution)/shard_map/ppermute | solution.py:253
  72.0 18.9 %collective-permute-start.6 = (bf16[4,384,128]{2,1,0:T(8,128)(2,1)S(1)}, bf16[4,384,128]{2,1,0:T(8,128)(2,1)S(1)}, u32[]{:S(2)}, u32[]{:S(2)}) collective-permute-start(bf16[4,384,128]{2,1,0:T(8,128)(2,1)S(1)} %pad_maximum_fusion.2.b0), channel_id=1, source_target_pairs={{0,16},{8,24},{16,32},{24,40},{32,48},{40,56},{48,0},{56,8},{64,80... | collective-permute-start | bytes 1179656 | tf_op jit(solution)/shard_map/ppermute | solution.py:260
  76.0 15.6 %collective-permute-start.7 = (bf16[4,384,128]{2,1,0:T(8,128)(2,1)S(1)}, bf16[4,384,128]{2,1,0:T(8,128)(2,1)}, u32[]{:S(2)}, u32[]{:S(2)}) collective-permute-start(bf16[4,384,128]{2,1,0:T(8,128)(2,1)S(1)} %pad_maximum_fusion.2.b0), channel_id=1, source_target_pairs={{0,32},{8,40},{16,48},{24,56},{32,0},{40,8},{48,16},{56,24},{64,96... | collective-permute-start | bytes 1179656 | tf_op jit(solution)/shard_map/ppermute | solution.py:260
  77.9 18.7 %collective-permute-start.8 = (bf16[4,384,128]{2,1,0:T(8,128)(2,1)S(1)}, bf16[4,384,128]{2,1,0:T(8,128)(2,1)}, u32[]{:S(2)}, u32[]{:S(2)}) collective-permute-start(bf16[4,384,128]{2,1,0:T(8,128)(2,1)S(1)} %pad_maximum_fusion.2.b0), channel_id=1, source_target_pairs={{0,48},{8,56},{16,0},{24,8},{32,16},{40,24},{48,32},{56,40},{64,11... | collective-permute-start | bytes 1179656 | tf_op jit(solution)/shard_map/ppermute | solution.py:260
  81.4 123.7 %copy-start.2 = (bf16[256,256]{1,0:T(8,128)(2,1)S(1)}, bf16[256,256]{1,0:T(8,128)(2,1)}, u32[]{:S(2)}) copy-start(bf16[256,256]{1,0:T(8,128)(2,1)} %constant.129.clone.second) | copy-start | bytes 393220
  101.3 0.7 copy-start.1
  102.0 0.6 copy-start.4
  102.6 106.9 %copy-start.3 = (bf16[256,256]{1,0:T(8,128)(2,1)S(1)}, bf16[256,256]{1,0:T(8,128)(2,1)}, u32[]{:S(2)}) copy-start(bf16[256,256]{1,0:T(8,128)(2,1)} %constant.132.clone.back) | copy-start | bytes 393220
  102.6 106.9 %copy-start.7 = (bf16[256,64]{1,0:T(8,128)(2,1)S(1)}, bf16[256,64]{1,0:T(8,128)(2,1)}, u32[]{:S(2)}) copy-start(bf16[256,64]{1,0:T(8,128)(2,1)} %constant.128.clone.first) | copy-start | bytes 98308
  102.7 106.9 %copy-start.9 = (f32[128,128]{1,0:T(8,128)S(1)}, f32[128,128]{1,0:T(8,128)}, u32[]{:S(2)}) copy-start(f32[128,128]{1,0:T(8,128)} %constant.130.clone.cos_tw.cos_tw_ref) | copy-start | bytes 196612
  102.7 106.9 %copy-start.11 = (bf16[64,256]{1,0:T(8,128)(2,1)S(1)}, bf16[64,256]{1,0:T(8,128)(2,1)}, u32[]{:S(2)}) copy-start(bf16[64,256]{1,0:T(8,128)(2,1)} %constant.133.clone.last) | copy-start | bytes 98308
  102.7 106.9 %all-to-all-start.2 = ((bf16[32,32,128]{2,1,0:T(8,128)(2,1)}), bf16[32,32,128]{2,1,0:T(8,128)(2,1)S(1)}, u32[]{:S(2)}, u32[]{:S(2)}) async-start(bf16[32,32,128]{2,1,0:T(8,128)(2,1)} %bitcast.54), calls=%async_computation.2 | async-start | bytes 524288 | tf_op jit(solution)/shard_map/all_to_all | solution.py:293
  177.0 27.4 %collective-permute-start.9 = (bf16[512,128]{1,0:T(8,128)(2,1)S(1)}, bf16[512,128]{1,0:T(8,128)(2,1)S(1)}, u32[]{:S(2)}, u32[]{:S(2)}) collective-permute-start(bf16[512,128]{1,0:T(8,128)(2,1)S(1)} %bitcast.55), channel_id=1, source_target_pairs={{0,256},{8,264},{16,272},{24,280},{32,288},{40,296},{48,304},{56,3... | collective-permute-start | bytes 393224 | tf_op jit(solution)/shard_map/ppermute | solution.py:299
  189.2 14.2 %collective-permute-start.11 = (bf16[16,128]{1,0:T(8,128)(2,1)S(1)}, bf16[16,128]{1,0:T(8,128)(2,1)S(1)}, u32[]{:S(2)}, u32[]{:S(2)}) collective-permute-start(bf16[16,128]{1,0:T(8,128)(2,1)S(1)} %reshape.98), channel_id=1, source_target_pairs={{0,256},{1,0},{2,272},{3,16},{4,288},{5,32},{6,304},{7,48},{8,320}... | collective-permute-start | bytes 12296 | tf_op jit(solution)/shard_map/ppermute | solution.py:268
  191.1 13.3 %collective-permute-start.10 = (bf16[16,128]{1,0:T(8,128)(2,1)S(1)}, bf16[16,128]{1,0:T(8,128)(2,1)S(1)}, u32[]{:S(2)}, u32[]{:S(2)}) collective-permute-start(bf16[16,128]{1,0:T(8,128)(2,1)S(1)} %reshape.98), channel_id=1, source_target_pairs={{0,0},{1,256},{2,16},{3,272},{4,32},{5,288},{6,48},{7,304},{8,64},... | collective-permute-start | bytes 12296 | tf_op jit(solution)/shard_map/ppermute | solution.py:267
  205.1 0.8 copy-start.6
  205.9 0.8 copy-start.8
  206.8 0.8 copy-start.10
  207.6 0.9 copy-start.13
  209.5 12.5 %copy-start.5 = (bf16[2,2,128,128]{3,2,1,0:T(8,128)(2,1)S(1)}, bf16[2,2,128,128]{3,2,1,0:T(8,128)(2,1)}, u32[]{:S(2)}) copy-start(bf16[2,2,128,128]{3,2,1,0:T(8,128)(2,1)} %copy-done.4) | copy-start | bytes 393220
  211.6 36.8 %copy-start.15 = (s32[256]{0:T(256)S(1)}, s32[256]{0:T(256)}, u32[]{:S(2)}) copy-start(s32[256]{0:T(256)} %param.24) | copy-start | bytes 3076
  211.6 18.4 %all-to-all-start.3 = ((bf16[32,48,128]{2,1,0:T(8,128)(2,1)}), bf16[32,48,128]{2,1,0:T(8,128)(2,1)S(1)}, u32[]{:S(2)}, u32[]{:S(2)}) async-start(bf16[32,48,128]{2,1,0:T(8,128)(2,1)} %shard_map.174), calls=%async_computation.3 | async-start | bytes 786432 | tf_op jit(solution)/shard_map/all_to_all | solution.py:301
  222.0 44.2 %copy-start.14 = (s32[256]{0:T(256)S(1)}, s32[256]{0:T(256)}, u32[]{:S(2)}) copy-start(s32[256]{0:T(256)} %param.25) | copy-start | bytes 3076
  222.0 3.3 %collective-permute-start.12 = (bf16[2,128,128]{2,1,0:T(8,128)(2,1)S(1)}, bf16[2,128,128]{2,1,0:T(8,128)(2,1)S(1)}, u32[]{:S(2)}, u32[]{:S(2)}) collective-permute-start(bf16[2,128,128]{2,1,0:T(8,128)(2,1)S(1)} %get-tuple-element.17), channel_id=1, source_target_pairs={{0,8},{8,0},{16,24},{24,16},{32,40},{40,32},{48,56},{56,48},{64,72... | collective-permute-start | bytes 196616 | tf_op jit(solution)/shard_map/ppermute | solution.py:297
  243.1 13.4 %collective-permute-start.13 = (bf16[64,512]{1,0:T(8,128)(2,1)S(1)}, bf16[64,512]{1,0:T(8,128)(2,1)S(1)}, u32[]{:S(2)}, u32[]{:S(2)}) collective-permute-start(bf16[64,512]{1,0:T(8,128)(2,1)S(1)} %reduce_sum.40), channel_id=1, source_target_pairs={{0,4},{1,5},{2,6},{3,7},{4,0},{5,1},{6,2},{7,3},{8,12},{9,13},{10,... | collective-permute-start | bytes 196616 | tf_op jit(solution)/shard_map/ppermute | solution.py:315
  (1 other events, 0.6 us)

commit v3 on v2

--- a/solution.py
+++ b/solution.py
@@ -34,22 +34,21 @@
     [ctx_id(z, y, x, c) for y in range(4) for x in range(4) for c in range(2)] for z in range(2)
 ]
 GROUPS_CORE = [
-    [ctx_id(z, y, x, c) for z in range(2) for y in range(4) for x in range(4)] for c in range(2)
+    [ctx_id(z, y, x, c) for y in range(4) for x in range(4)] for z in range(2) for c in range(2)
 ]
 GROUPS_TP = [[0, 1, 2, 3], [4, 5, 6, 7]]
 
 
-def weight_routes(flip):
+def weight_route():
     pairs = []
     for i in range(64):
-        for q in range(8):
-            plane, core, chip, half = i // 8, (i % 8) // 4, (i % 4) * 4 + q // 2, q % 2
-            z = half ^ flip
-            pairs.append((i * 8 + q, (z * 32 + chip * 2 + core) * 8 + plane))
+        for j in range(8):
+            plane, core, chip, z = i // 8, (i % 8) // 4, (i % 4) * 4 + j // 2, j % 2
+            pairs.append((i * 8 + j, (z * 32 + chip * 2 + core) * 8 + plane))
     return pairs
 
 
-ROUTE_SAME, ROUTE_FLIP = weight_routes(0), weight_routes(1)
+ROUTE = weight_route()
 
 
 def tables():
@@ -106,13 +105,12 @@
 
 
 def conv_kernel(
-    z_ref, sig_ref, low_ref, all_ref, piece_ref, first, second, back, last, cos_tw_ref, sin_tw_ref, out_ref, scratch
+    z_ref, sig_ref, before_ref, low_ref, all_ref, piece_ref, first, second, back, last, cos_tw_ref, sin_tw_ref, out_ref, scratch
 ):
-    z = z_ref[0]
     cos_tw, sin_tw = cos_tw_ref[...], sin_tw_ref[...]
     args = (scratch, first[...], second[...], cos_tw, sin_tw)
-    own = spectrum(sig_ref[z].astype(F32), *args)
-    old = spectrum(sig_ref[0].astype(F32) * z.astype(F32), *args)
+    own = spectrum(sig_ref[...].astype(F32), *args)
+    old = spectrum(jnp.where(z_ref[0] == 1, before_ref[...].astype(F32), 0.0), *args)
     low, every = low_ref[...], all_ref[...]
     own_r, own_i, old_r, old_i = own[:, :128], own[:, 128:], old[:, :128], old[:, 128:]
     low_r, low_i, all_r, all_i = low[:, :128], low[:, 128:], every[:, :128], every[:, 128:]
@@ -137,34 +135,44 @@
         out_ref[d, 16:] = piece
 
 
-def proj_kernel(at_ref, own_ref, other_ref, low_ref, b0, b1, b2, b3, sig_ref, gate_ref):
-    y_at, x_at, core = at_ref[0], at_ref[1], at_ref[2]
-
-    def block(ref, lead, row):
-        return jnp.concatenate([ref[lead, row + 128 * g : row + 128 * g + 128, :] for g in range(3)], axis=1)
-
-    for part, tokens in enumerate((own_ref, other_ref)):
+def weight_block(ref, lead, row):
+    return jnp.concatenate([ref[lead, row + 128 * g : row + 128 * g + 128, :] for g in range(3)], axis=1)
+
+
+def columns(ref, start, count):
+    return ref[:, pl.ds(pl.multiple_of(start, 128), count)]
+
+
+def near_kernel(at_ref, own_ref, beside_ref, near_ref, out_ref):
+    start = at_ref[3] * 2048
+    for part, tokens in enumerate((own_ref, beside_ref)):
         total = jnp.zeros((256, 384), F32)
         for y in range(4):
             for x in (0, 2):
-                left = tokens[:, (y * 4 + x) * 128 : (y * 4 + x) * 128 + 256]
-                right = jnp.concatenate([block(low_ref, y, x * 384), block(low_ref, y, x * 384 + 384)], axis=0)
-                total += mm(left, right)
-        for step, ref in enumerate((b0, b1, b2, b3)):
+                left = columns(tokens, start + (y * 4 + x) * 128, 256)
+                right = [weight_block(near_ref, y, x * 384), weight_block(near_ref, y, x * 384 + 384)]
+                total += mm(left, jnp.concatenate(right, axis=0))
+        out_ref[part] = total
+
+
+def proj_kernel(at_ref, own_ref, beside_ref, near_ref, f0, f1, f2, f3, sig_ref, gate_ref):
+    y_at, x_at, core = at_ref[0], at_ref[1], at_ref[2]
+    start = 2048 - at_ref[3] * 2048
+    for part, tokens in enumerate((own_ref, beside_ref)):
+        total = near_ref[part]
+        for step, ref in enumerate((f0, f1, f2, f3)):
             x = lax.rem(x_at + 4 - step, 4)
             for k in (0, 2):
-                starts = [2048 + (lax.rem(y_at + 4 - j, 4) * 4 + x) * 128 for j in (k, k + 1)]
-                left = jnp.concatenate([tokens[:, pl.ds(pl.multiple_of(s, 128), 128)] for s in starts], axis=1)
-                right = jnp.concatenate([block(ref, k, 0), block(ref, k + 1, 0)], axis=0)
-                total += mm(left, right)
+                left = [columns(tokens, start + (lax.rem(y_at + 4 - j, 4) * 4 + x) * 128, 128) for j in (k, k + 1)]
+                right = [weight_block(ref, k, 0), weight_block(ref, k + 1, 0)]
+                total += mm(jnp.concatenate(left, axis=1), jnp.concatenate(right, axis=0))
         proj = total.astype(BF16).astype(F32)
         gated = proj[:, 128:256] * proj[:, 256:]
         place = core if part == 0 else 1 - core
         first, second = gated[:128].T, gated[128:].T
         for p in range(16):
             rows = jnp.concatenate([first[p * 8 : p * 8 + 8], second[p * 8 : p * 8 + 8]], axis=0).astype(BF16)
-            sig_ref[0, p, pl.ds(pl.multiple_of(place * 16, 16), 16), :] = rows
-            sig_ref[1, p, pl.ds(pl.multiple_of(place * 16, 16), 16), :] = rows
+            sig_ref[p, pl.ds(pl.multiple_of(place * 16, 16), 16), :] = rows
         gate_ref[place, 0] = proj[:128, :128].T.astype(BF16)
         gate_ref[place, 1] = proj[128:, :128].T.astype(BF16)
 
@@ -219,21 +227,21 @@
     )
 
 
-def convolve(z, signal, low, every, piece):
+def convolve(z, signal, before, low, every, piece):
     consts = [jnp.asarray(t, BF16) for t in (FIRST, SECOND, BACK, LAST)]
     consts += [jnp.asarray(t, F32) for t in (COS_TW, SIN_TW)]
     return call(
         conv_kernel,
         shape((32, 48, 128), BF16),
-        [SCALARS] + whole(10),
+        [SCALARS] + whole(11),
         [pltpu.VMEM((512, 128), F32)],
         6 * 10**8,
-        (z, signal, low, every, piece, *consts),
+        (z, signal, before, low, every, piece, *consts),
     )
 
 
 def gather_weights(w_in, long_filter, ctx):
-    core, z = ctx % 2, ctx // 32
+    core = ctx % 2
     halves = w_in.transpose(1, 0, 2).reshape(3, 64, 2, 128)
     taps = long_filter.reshape(256, 2, 128)
 
@@ -244,60 +252,61 @@
     keep = half_of(core)
     got = lax.ppermute(half_of(1 - core), "ctx", PERM_CORE)
     both = by_position(keep, got, core)
-    own = both[:, :192].reshape(2, 3, 64, 128).transpose(1, 0, 2, 3).reshape(384, 128)
+    near = both[:, :192].reshape(2, 3, 64, 128).transpose(1, 0, 2, 3).reshape(384, 128)
+    far = lax.ppermute(near, "ctx", PERM_Z)
     taps = both[:, 192:].reshape(2, 2, 128, 4, 4, 8).transpose(4, 3, 0, 1, 5, 2).reshape(4, 128, 128)
-    other = lax.ppermute(own, "ctx", PERM_Z)
-    low = jnp.where(z == 0, own, other)
-    high = jnp.where(z == 0, other, own)
-
-    along_y = jnp.stack([high] + [lax.ppermute(high, "ctx", PERM_Y[k]) for k in (1, 2, 3)])
-    low = jnp.concatenate([jnp.broadcast_to(low, (4, 384, 128)), taps], axis=1)
-    low = lax.all_to_all(low, "ctx", 0, 0, axis_index_groups=GROUPS_X, tiled=True)
-    taps = low[:, 384:].reshape(4, 4, 32, 128).transpose(1, 0, 2, 3).reshape(4, 128, 128)
-    low = jnp.broadcast_to(low[:, :384].reshape(1, 1536, 128), (4, 1536, 128))
-    low = jnp.concatenate([low, taps], axis=1)
-    low = lax.all_to_all(low, "ctx", 0, 0, axis_index_groups=GROUPS_Y, tiled=True)
-    highs = [along_y] + [lax.ppermute(along_y, "ctx", PERM_X[k]) for k in (1, 2, 3)]
-    return low, highs, low[:, 1536:].reshape(512, 128)
-
-
-def output_weights(w_out, w_unembed, z):
+
+    near = jnp.concatenate([jnp.broadcast_to(near, (4, 384, 128)), taps], axis=1)
+    near = lax.all_to_all(near, "ctx", 0, 0, axis_index_groups=GROUPS_X, tiled=True)
+    taps = near[:, 384:].reshape(4, 4, 32, 128).transpose(1, 0, 2, 3).reshape(4, 128, 128)
+    near = jnp.broadcast_to(near[:, :384].reshape(1, 1536, 128), (4, 1536, 128))
+    near = jnp.concatenate([near, taps], axis=1)
+    near = lax.all_to_all(near, "ctx", 0, 0, axis_index_groups=GROUPS_Y, tiled=True)
+
+    along_y = jnp.stack([far] + [lax.ppermute(far, "ctx", PERM_Y[k]) for k in (1, 2, 3)])
+    fars = [along_y] + [lax.ppermute(along_y, "ctx", PERM_X[k]) for k in (1, 2, 3)]
+    return near, fars, near[:, 1536:].reshape(512, 128)
+
+
+def output_weights(w_out, w_unembed, tp):
     partial = mm(w_out, w_unembed)
-    piece = lax.psum_scatter(partial, "tp", scatter_dimension=0, tiled=True).astype(BF16).reshape(16, 128)
-    same = lax.ppermute(piece, ("ctx", "tp"), ROUTE_SAME)
-    flip = lax.ppermute(piece, ("ctx", "tp"), ROUTE_FLIP)
-    return by_position(same, flip, z).reshape(8, 4, 128).transpose(1, 0, 2).reshape(32, 128)
+    partial = lax.all_gather(jnp.concatenate([partial, partial]), "tp", axis=0)
+    rows = lax.dynamic_slice_in_dim(partial, (tp // 2) * 8, 8, 1)
+    rows = jnp.sum(rows, axis=0).astype(BF16).reshape(8, 4, 128).transpose(1, 0, 2).reshape(32, 128)
+    return lax.ppermute(rows, ("ctx", "tp"), ROUTE)
 
 
 def per_device(tokens_in, pre_gain, w_in, w_out, long_filter, w_unembed, target_ids, score_mask):
     ctx, tp = lax.axis_index("ctx"), lax.axis_index("tp")
     core, z = ctx % 2, ctx // 32
     z_at = z.reshape(1).astype(jnp.int32)
-    low, highs, taps = gather_weights(w_in, long_filter, ctx)
-    piece = output_weights(w_out, w_unembed, z)
+    near, fars, taps = gather_weights(w_in, long_filter, ctx)
+    piece = output_weights(w_out, w_unembed, tp)
 
     stream = tokens_in.astype(F32)
     scale = lax.rsqrt(jnp.mean(stream * stream, axis=1, keepdims=True) + NORM_EPS)
     normed = (stream * scale * pre_gain.astype(F32)).astype(BF16)
     beside = lax.ppermute(normed, "ctx", PERM_CORE)
 
-    at = jnp.stack([(ctx // 8) % 4, (ctx // 2) % 4, core]).astype(jnp.int32)
+    at = jnp.stack([(ctx // 8) % 4, (ctx // 2) % 4, core, z]).astype(jnp.int32)
+    sums = call(
+        near_kernel, shape((2, 256, 384), F32), [SCALARS] + whole(3), [], 8 * 10**8, (at, normed, beside, near)
+    )
     signal, gate = call(
         proj_kernel,
-        (shape((2, 16, 32, 128), BF16), shape((2, 2, 128, 128), BF16)),
+        (shape((16, 32, 128), BF16), shape((2, 2, 128, 128), BF16)),
         [SCALARS] + whole(7),
         [],
-        16 * 10**8,
-        (at, normed, beside, low, *highs),
-    )
-    signal = lax.all_to_all(
-        signal.reshape(32, 32, 128), "ctx", 0, 0, axis_index_groups=GROUPS_CORE, tiled=True
-    ).reshape(2, 512, 128)
+        8 * 10**8,
+        (at, normed, beside, sums, *fars),
+    )
+    signal = lax.all_to_all(signal, "ctx", 0, 0, axis_index_groups=GROUPS_CORE, tiled=True).reshape(512, 128)
+    before = lax.ppermute(signal, "ctx", PERM_Z_UP)
     gate_keep = lax.dynamic_index_in_dim(gate, core, 0, False)
     gate_got = lax.ppermute(lax.dynamic_index_in_dim(gate, 1 - core, 0, False), "ctx", PERM_CORE)
 
     spectra = filter_spectra(z_at, taps, lax.ppermute(taps, "ctx", PERM_Z_UP))
-    conv = convolve(z_at, signal, *spectra, piece)
+    conv = convolve(z_at, signal, before, *spectra, piece)
     conv = lax.all_to_all(conv, "ctx", 0, 0, axis_index_groups=GROUPS_PLANE, tiled=True)
 
     width = w_unembed.shape[0]

time: 268 us -> 216 us (0.81)
  blocking collectives: 88.9 us -> 24.5 us
  between operations: 1.2 us -> 14.1 us
  waiting for transfers between devices: 54.2 us -> 45.9 us
  starting transfers between devices: 92.5 us -> 100 us
    unnamed x1 -> x0, blocking collectives: 55.8 us -> none
    all_to_all x1 -> x0, blocking collectives: 12.4 us -> none  [gather_weights(): lax.all_to_all(low, 'ctx', 0, 0, axis_index_groups=GROUPS_X, tiled=True)]
    ppermute x6, waiting for transfers between devices: 26.3 us -> 18.2 us  [the longest x1 8.93 us: output_weights(): return lax.ppermute(rows, ('ctx', 'tp'), ROUTE)]
    ppermute x1, starting transfers between devices: 5.28 us -> 12.8 us  [per_device(): far = lax.ppermute(logits, 'tp', [(i, i ^ 4) for i in range(8)])]
    all_to_all x2 -> x3, waiting for transfers between devices: 0.01 us -> 7.1 us  [the longest x1 7.1 us: gather_weights(): lax.all_to_all(near, 'ctx', 0, 0, axis_index_groups=GROUPS_X, tiled=True)]
    ppermute x3, waiting for transfers between devices: 15.2 us -> 9.22 us  [gather_weights(): lax.ppermute(along_y, 'ctx', PERM_X[k])]
    all_to_all x1, blocking collectives: 12.7 us -> 16.6 us  [per_device(): lax.all_to_all(logits.reshape(4, 64, 512), 'tp', 0, 0, axis_index_groups=...]
    pallas_call x4 -> x5, Pallas kernels: 8.11 us -> 9.88 us  [call(): pl.pallas_call(kernel, out_shape=outs, in_specs=specs, out_specs=jax.tree...]
  transfers between devices with their start and end apart: 17 -> 19, of which waited for: 10 -> 11; matrix products, arithmetic and copies ran while one was open for 4% -> 3% of each run, Pallas kernels for 0% -> 3%
where the time goes in v3:
time: 216 us; the launch traced here: 215 us
  starting transfers between devices  100 us (46%)
  waiting for transfers between devices  45.9 us (21%)
  blocking collectives  24.5 us (11%)
  between operations  14.1 us (7%)
  local copies, waits for them, and re-layouts  10 us (5%)
  Pallas kernels  9.88 us (5%)
  other arithmetic  9.12 us (4%)
    all_to_all x1, blocking collectives, per_device(): lax.all_to_all(logits.reshape(4, 64, 512), 'tp', 0, 0, axis_index_groups=...  16.6 us
    ppermute x1, starting transfers between devices, per_device(): spectra = filter_spectra(z_at, taps, lax.ppermute(taps, 'ctx', PERM_Z_UP))  13.5 us
    ppermute x1, starting transfers between devices, per_device(): far = lax.ppermute(logits, 'tp', [(i, i ^ 4) for i in range(8)])  12.8 us
    ppermute x1, starting transfers between devices, gather_weights(): far = lax.ppermute(near, 'ctx', PERM_Z)  11 us
    ppermute x3, starting transfers between devices, gather_weights(): lax.ppermute(far, 'ctx', PERM_Y[k])  10.6 us
    ppermute x3, starting transfers between devices, gather_weights(): lax.ppermute(along_y, 'ctx', PERM_X[k])  10.2 us
    pallas_call x5, Pallas kernels, call(): pl.pallas_call(kernel, out_shape=outs, in_specs=specs, out_specs=jax.tree...  9.88 us
    all_to_all x1, starting transfers between devices, gather_weights(): lax.all_to_all(near, 'ctx', 0, 0, axis_index_groups=GROUPS_X, tiled=True)  9.29 us
  transfers between devices with their start and end apart: 19, of which 11 were waited for; matrix products, arithmetic and copies ran while one was open for 3% of the time, Pallas kernels for 3%

profile of v3, /device:TPU:6, one launch (start us, length us, event | category | flops | bytes accessed | tf_op | source)
XLA Modules:
  0.0 215.1 jit_solution(4620467596958891272)
XLA Ops:
  7.4 2.1 fusion
  10.2 1.9 collective-permute-start
  12.7 2.4 %collective-permute-start.1 = (bf16[448,128]{1,0:T(8,128)(2,1)S(1)}, bf16[448,128]{1,0:T(8,128)(2,1)S(1)}, u32[]{:S(2)}, u32[]{:S(2)}) collective-permute-start(bf16[448,128]{1,0:T(8,128)(2,1)S(1)} %pad_maximum_fusion.4), channel_id=1, source_target_pairs={{0,8},{8,0},{16,24},{24,16},{32,40},{40,32},{48,56},{56,48},{64,72... | collective-permute-start | bytes 344072 | tf_op jit(solution)/shard_map/ppermute | solution.py:253
  17.6 9.3 %all-to-all-start = ((bf16[4,512,128]{2,1,0:T(8,128)(2,1)}), bf16[4,512,128]{2,1,0:T(8,128)(2,1)S(1)}, u32[]{:S(2)}, u32[]{:S(2)}) async-start(bf16[4,512,128]{2,1,0:T(8,128)(2,1)} %pad_maximum_fusion.1), calls=%async_computation | async-start | bytes 1048576 | tf_op jit(solution)/shard_map/all_to_all | solution.py:260
  27.7 7.1 %all-to-all-done = bf16[4,512,128]{2,1,0:T(8,128)(2,1)S(1)} async-done(((bf16[4,512,128]{2,1,0:T(8,128)(2,1)}), bf16[4,512,128]{2,1,0:T(8,128)(2,1)S(1)}, u32[]{:S(2)}, u32[]{:S(2)}) %all-to-all-start) | async-done | bytes 524320 | tf_op jit(solution)/shard_map/all_to_all | solution.py:260
  36.4 4.4 %all-to-all-start.1 = ((bf16[4,1664,128]{2,1,0:T(8,128)(2,1)}), bf16[4,1664,128]{2,1,0:T(8,128)(2,1)}, u32[]{:S(2)}, u32[]{:S(2)}) async-start(bf16[4,1664,128]{2,1,0:T(8,128)(2,1)} %pad_maximum_fusion), calls=%async_computation.1 | async-start | bytes 3407872 | tf_op jit(solution)/shard_map/all_to_all | solution.py:264
  40.8 11.0 %collective-permute-start.2 = (bf16[384,128]{1,0:T(8,128)(2,1)S(1)}, bf16[384,128]{1,0:T(8,128)(2,1)S(1)}, u32[]{:S(2)}, u32[]{:S(2)}) collective-permute-start(bf16[384,128]{1,0:T(8,128)(2,1)S(1)} %bitcast.61), channel_id=1, source_target_pairs={{0,256},{8,264},{16,272},{24,280},{32,288},{40,296},{48,304},{56,3... | collective-permute-start | bytes 294920 | tf_op jit(solution)/shard_map/ppermute | solution.py:256
  51.8 4.4 %collective-permute-done.2 = bf16[384,128]{1,0:T(8,128)(2,1)S(1)} collective-permute-done((bf16[384,128]{1,0:T(8,128)(2,1)S(1)}, bf16[384,128]{1,0:T(8,128)(2,1)S(1)}, u32[]{:S(2)}, u32[]{:S(2)}) %collective-permute-start.2) | collective-permute-done | bytes 98336 | tf_op jit(solution)/shard_map/ppermute | solution.py:256
  56.2 5.1 %collective-permute-start.5 = (bf16[384,128]{1,0:T(8,128)(2,1)S(1)}, bf16[384,128]{1,0:T(8,128)(2,1)S(1)}, u32[]{:S(2)}, u32[]{:S(2)}) collective-permute-start(bf16[384,128]{1,0:T(8,128)(2,1)S(1)} %collective-permute-done.2), channel_id=1, source_target_pairs={{0,192},{8,200},{16,208},{24,216},{32,224},{40,232},{48,240},{56,2... | collective-permute-start | bytes 294920 | tf_op jit(solution)/shard_map/ppermute | solution.py:266
  61.3 2.8 %collective-permute-start.4 = (bf16[384,128]{1,0:T(8,128)(2,1)S(1)}, bf16[384,128]{1,0:T(8,128)(2,1)S(1)}, u32[]{:S(2)}, u32[]{:S(2)}) collective-permute-start(bf16[384,128]{1,0:T(8,128)(2,1)S(1)} %collective-permute-done.2), channel_id=1, source_target_pairs={{0,128},{8,136},{16,144},{24,152},{32,160},{40,168},{48,176},{56,1... | collective-permute-start | bytes 294920 | tf_op jit(solution)/shard_map/ppermute | solution.py:266
  64.1 2.8 %collective-permute-start.3 = (bf16[384,128]{1,0:T(8,128)(2,1)S(1)}, bf16[384,128]{1,0:T(8,128)(2,1)S(1)}, u32[]{:S(2)}, u32[]{:S(2)}) collective-permute-start(bf16[384,128]{1,0:T(8,128)(2,1)S(1)} %collective-permute-done.2), channel_id=1, source_target_pairs={{0,64},{8,72},{16,80},{24,88},{32,96},{40,104},{48,112},{56,120},{... | collective-permute-start | bytes 294920 | tf_op jit(solution)/shard_map/ppermute | solution.py:266
  66.8 2.5 %collective-permute-done.4 = bf16[384,128]{1,0:T(8,128)(2,1)S(1)} collective-permute-done((bf16[384,128]{1,0:T(8,128)(2,1)S(1)}, bf16[384,128]{1,0:T(8,128)(2,1)S(1)}, u32[]{:S(2)}, u32[]{:S(2)}) %collective-permute-start.4) | collective-permute-done | bytes 98336 | tf_op jit(solution)/shard_map/ppermute | solution.py:266
  69.3 2.5 %collective-permute-done.3 = bf16[384,128]{1,0:T(8,128)(2,1)S(1)} collective-permute-done((bf16[384,128]{1,0:T(8,128)(2,1)S(1)}, bf16[384,128]{1,0:T(8,128)(2,1)S(1)}, u32[]{:S(2)}, u32[]{:S(2)}) %collective-permute-start.3) | collective-permute-done | bytes 98336 | tf_op jit(solution)/shard_map/ppermute | solution.py:266
  71.8 5.5 %collective-permute-start.6 = (bf16[4,384,128]{2,1,0:T(8,128)(2,1)S(1)}, bf16[4,384,128]{2,1,0:T(8,128)(2,1)S(1)}, u32[]{:S(2)}, u32[]{:S(2)}) collective-permute-start(bf16[4,384,128]{2,1,0:T(8,128)(2,1)S(1)} %pad_maximum_fusion.2.f0), channel_id=1, source_target_pairs={{0,16},{8,24},{16,32},{24,40},{32,48},{40,56},{48,0},{56,8},{64,80... | collective-permute-start | bytes 1179656 | tf_op jit(solution)/shard_map/ppermute | solution.py:267
  79.2 2.8 %collective-permute-start.8 = (bf16[4,384,128]{2,1,0:T(8,128)(2,1)S(1)}, bf16[4,384,128]{2,1,0:T(8,128)(2,1)}, u32[]{:S(2)}, u32[]{:S(2)}) collective-permute-start(bf16[4,384,128]{2,1,0:T(8,128)(2,1)S(1)} %pad_maximum_fusion.2.f0), channel_id=1, source_target_pairs={{0,48},{8,56},{16,0},{24,8},{32,16},{40,24},{48,32},{56,40},{64,11... | collective-permute-start | bytes 1179656 | tf_op jit(solution)/shard_map/ppermute | solution.py:267
  82.2 3.3 %shard_map.172.near_ref = f32[2,256,384]{2,1,0:T(8,128)S(1)} custom-call(s32[4]{0:T(128)S(1)} %pad_add_fusion.at_ref, bf16[256,4096]{1,0:T(8,128)(2,1)S(1)} %fusion.2.own_ref, bf16[256,4096]{1,0:T(8,128)(2,1)} %collective-permute-done.beside_ref, bf16[4,1664,128]{2,1,0:T(8,128)(2,1)} %all-to-all-done.1.near_ref), custom_call_target="tpu_custom_call" | custom-call | flops 800000000 | bytes 4194304 | tf_op jit(solution)/shard_map/pallas_call | solution.py:199
  85.5 4.3 %collective-permute-done.6.f1 = bf16[4,384,128]{2,1,0:T(8,128)(2,1)S(1)} collective-permute-done((bf16[4,384,128]{2,1,0:T(8,128)(2,1)S(1)}, bf16[4,384,128]{2,1,0:T(8,128)(2,1)S(1)}, u32[]{:S(2)}, u32[]{:S(2)}) %collective-permute-start.6) | collective-permute-done | bytes 393248 | tf_op jit(solution)/shard_map/ppermute | solution.py:267
  90.6 4.1 %collective-permute-done.8.f3 = bf16[4,384,128]{2,1,0:T(8,128)(2,1)} collective-permute-done((bf16[4,384,128]{2,1,0:T(8,128)(2,1)S(1)}, bf16[4,384,128]{2,1,0:T(8,128)(2,1)}, u32[]{:S(2)}, u32[]{:S(2)}) %collective-permute-start.8) | collective-permute-done | bytes 393248 | tf_op jit(solution)/shard_map/ppermute | solution.py:267
  94.8 3.1 %shard_map.173 = (bf16[16,32,128]{2,1,0:T(8,128)(2,1)S(1)}, bf16[2,2,128,128]{3,2,1,0:T(8,128)(2,1)S(1)}) custom-call(s32[4]{0:T(128)S(1)} %pad_add_fusion.at_ref, bf16[256,4096]{1,0:T(8,128)(2,1)S(1)} %fusion.2.own_ref, bf16[256,4096]{1,0:T(8,128)(2,1)} %collective-permute-done.beside_ref, f32[2,256,384]{2,1,0:T(8,128)S(1)} %shard_map.172.near_ref, ...), custom_call_target="tpu_custom_call" | custom-call | flops 800000000 | bytes 4194304 | tf_op jit(solution)/shard_map/pallas_call | solution.py:199
  99.2 5.9 %all-to-all-start.2 = ((bf16[16,32,128]{2,1,0:T(8,128)(2,1)}), bf16[16,32,128]{2,1,0:T(8,128)(2,1)S(1)}, u32[]{:S(2)}, u32[]{:S(2)}) async-start(bf16[16,32,128]{2,1,0:T(8,128)(2,1)} %copy-done.5), calls=%async_computation.2 | async-start | bytes 262144 | tf_op jit(solution)/shard_map/all_to_all | solution.py:303
  106.0 13.5 %collective-permute-start.10 = (bf16[512,128]{1,0:T(8,128)(2,1)S(1)}, bf16[512,128]{1,0:T(8,128)(2,1)S(1)}, u32[]{:S(2)}, u32[]{:S(2)}) collective-permute-start(bf16[512,128]{1,0:T(8,128)(2,1)S(1)} %bitcast.51), channel_id=1, source_target_pairs={{0,256},{8,264},{16,272},{24,280},{32,288},{40,296},{48,304},{56,3... | collective-permute-start | bytes 393224 | tf_op jit(solution)/shard_map/ppermute | solution.py:308
  119.4 4.8 %collective-permute-start.9 = (bf16[512,128]{1,0:T(8,128)(2,1)S(1)}, bf16[512,128]{1,0:T(8,128)(2,1)S(1)}, u32[]{:S(2)}, u32[]{:S(2)}) collective-permute-start(bf16[512,128]{1,0:T(8,128)(2,1)S(1)} %bitcast.49), channel_id=1, source_target_pairs={{0,256},{8,264},{16,272},{24,280},{32,288},{40,296},{48,304},{56,3... | collective-permute-start | bytes 393224 | tf_op jit(solution)/shard_map/ppermute | solution.py:304
  125.3 2.7 %collective-permute-start.11 = (bf16[32,128]{1,0:T(8,128)(2,1)S(1)}, bf16[32,128]{1,0:T(8,128)(2,1)S(1)}, u32[]{:S(2)}, u32[]{:S(2)}) collective-permute-start(bf16[32,128]{1,0:T(8,128)(2,1)S(1)} %bitcast.73), channel_id=1, source_target_pairs={{0,0},{1,256},{2,16},{3,272},{4,32},{5,288},{6,48},{7,304},{8,64},... | collective-permute-start | bytes 24584 | tf_op jit(solution)/shard_map/ppermute | solution.py:276
  131.5 8.9 %collective-permute-done.11.piece_ref = bf16[32,128]{1,0:T(8,128)(2,1)S(1)} collective-permute-done((bf16[32,128]{1,0:T(8,128)(2,1)S(1)}, bf16[32,128]{1,0:T(8,128)(2,1)S(1)}, u32[]{:S(2)}, u32[]{:S(2)}) %collective-permute-start.11) | collective-permute-done | bytes 8224 | tf_op jit(solution)/shard_map/ppermute | solution.py:276
  143.7 2.1 shard_map.175
  145.8 8.8 %all-to-all-start.3 = ((bf16[32,48,128]{2,1,0:T(8,128)(2,1)}), bf16[32,48,128]{2,1,0:T(8,128)(2,1)S(1)}, u32[]{:S(2)}, u32[]{:S(2)}) async-start(bf16[32,48,128]{2,1,0:T(8,128)(2,1)} %shard_map.175), calls=%async_computation.3 | async-start | bytes 786432 | tf_op jit(solution)/shard_map/all_to_all | solution.py:310
  154.6 2.1 collective-permute-start.12
  158.0 4.7 %all-to-all-done.3.got_ref = bf16[32,48,128]{2,1,0:T(8,128)(2,1)S(1)} async-done(((bf16[32,48,128]{2,1,0:T(8,128)(2,1)}), bf16[32,48,128]{2,1,0:T(8,128)(2,1)S(1)}, u32[]{:S(2)}, u32[]{:S(2)}) %all-to-all-start.3) | async-done | bytes 393248 | tf_op jit(solution)/shard_map/all_to_all | solution.py:310
  163.0 16.6 %all_to_all.30 = bf16[4,64,512]{2,1,0:T(8,128)(2,1)S(1)} all-to-all(bf16[4,64,512]{2,1,0:T(8,128)(2,1)S(1)} %bitcast.48), channel_id=1, replica_groups={{0,1,2,3},{4,5,6,7},{8,9,10,11},{12,13,14,15},{16,17,18,19},{20,21,22,2..., dimensions={0} | all-to-all | bytes 524288 | tf_op jit(solution)/shard_map/all_to_all | solution.py:322
  179.6 12.8 %collective-permute-start.13 = (bf16[64,512]{1,0:T(8,128)(2,1)S(1)}, bf16[64,512]{1,0:T(8,128)(2,1)S(1)}, u32[]{:S(2)}, u32[]{:S(2)}) collective-permute-start(bf16[64,512]{1,0:T(8,128)(2,1)S(1)} %reduce_sum.50), channel_id=1, source_target_pairs={{0,4},{1,5},{2,6},{3,7},{4,0},{5,1},{6,2},{7,3},{8,12},{9,13},{10,... | collective-permute-start | bytes 196616 | tf_op jit(solution)/shard_map/ppermute | solution.py:324
  192.5 5.5 %collective-permute-done.13 = bf16[64,512]{1,0:T(8,128)(2,1)S(1)} collective-permute-done((bf16[64,512]{1,0:T(8,128)(2,1)S(1)}, bf16[64,512]{1,0:T(8,128)(2,1)S(1)}, u32[]{:S(2)}, u32[]{:S(2)}) %collective-permute-start.13) | collective-permute-done | bytes 65568 | tf_op jit(solution)/shard_map/ppermute | solution.py:324
  198.4 7.9 %all_to_all.31 = f32[4,1,512]{2,1,0:T(1,128)S(1)} all-to-all(f32[4,1,512]{2,1,0:T(1,128)S(1)} %reshape.99), channel_id=1, replica_groups={{0,1,2,3},{4,5,6,7},{8,9,10,11},{12,13,14,15},{16,17,18,19},{20,21,22,2..., dimensions={0} | all-to-all | bytes 16384 | tf_op jit(solution)/shard_map/all_to_all | solution.py:333
  (101 shorter events, 23.8 us)
Async XLA Ops:
  6.5 20.3 %copy-start = (bf16[512,512]{1,0:T(8,128)(2,1)S(1)}, bf16[512,512]{1,0:T(8,128)(2,1)}, u32[]{:S(2)}) copy-start(bf16[512,512]{1,0:T(8,128)(2,1)} %param.23) | copy-start | bytes 1572868
  6.5 2.9 %copy-start.13 = (bf16[256,4096]{1,0:T(8,128)(2,1)S(1)}, bf16[256,4096]{1,0:T(8,128)(2,1)}, u32[]{:S(2)}) copy-start(bf16[256,4096]{1,0:T(8,128)(2,1)} %param.18) | copy-start | bytes 6291460
  9.5 2.6 %copy-start.14 = (bf16[256,256]{1,0:T(8,128)(2,1)S(1)}, bf16[256,256]{1,0:T(8,128)(2,1)}, u32[]{:S(2)}) copy-start(bf16[256,256]{1,0:T(8,128)(2,1)} %param.22) | copy-start | bytes 393220
  9.5 2.9 %copy-start.15 = (bf16[64,3,256]{2,0,1:T(8,128)(2,1)S(1)}, bf16[64,3,256]{2,0,1:T(8,128)(2,1)}, u32[]{:S(2)}) copy-start(bf16[64,3,256]{2,0,1:T(8,128)(2,1)} %param.20) | copy-start | bytes 294916
  10.2 72.0 %collective-permute-start = (bf16[256,4096]{1,0:T(8,128)(2,1)S(1)}, bf16[256,4096]{1,0:T(8,128)(2,1)}, u32[]{:S(2)}, u32[]{:S(2)}) collective-permute-start(bf16[256,4096]{1,0:T(8,128)(2,1)S(1)} %fusion.2.own_ref), channel_id=1, source_target_pairs={{0,8},{8,0},{16,24},{24,16},{32,40},{40,32},{48,56},{56,48},{64,72... | collective-permute-start | bytes 6291464 | tf_op jit(solution)/shard_map/ppermute | solution.py:289
  12.7 3.7 %collective-permute-start.1 = (bf16[448,128]{1,0:T(8,128)(2,1)S(1)}, bf16[448,128]{1,0:T(8,128)(2,1)S(1)}, u32[]{:S(2)}, u32[]{:S(2)}) collective-permute-start(bf16[448,128]{1,0:T(8,128)(2,1)S(1)} %pad_maximum_fusion.4), channel_id=1, source_target_pairs={{0,8},{8,0},{16,24},{24,16},{32,40},{40,32},{48,56},{56,48},{64,72... | collective-permute-start | bytes 344072 | tf_op jit(solution)/shard_map/ppermute | solution.py:253
  16.4 10.5 %copy-start.16 = (bf16[32,512]{1,0:T(8,128)(2,1)S(1)}, bf16[32,512]{1,0:T(8,128)(2,1)}, u32[]{:S(2)}) copy-start(bf16[32,512]{1,0:T(8,128)(2,1)} %param.21) | copy-start | bytes 98308
  17.6 17.3 %all-to-all-start = ((bf16[4,512,128]{2,1,0:T(8,128)(2,1)}), bf16[4,512,128]{2,1,0:T(8,128)(2,1)S(1)}, u32[]{:S(2)}, u32[]{:S(2)}) async-start(bf16[4,512,128]{2,1,0:T(8,128)(2,1)} %pad_maximum_fusion.1), calls=%async_computation | async-start | bytes 1048576 | tf_op jit(solution)/shard_map/all_to_all | solution.py:260
  26.9 97.5 %all-gather.3.cloned.1.call-start = ((), (), s32[]{:S(2)}) async-start(), calls=%async_computation.6 | async-start | bytes 1179648 | tf_op jit(solution)/shard_map/all_gather | solution.py:273
  36.4 45.7 %all-to-all-start.1 = ((bf16[4,1664,128]{2,1,0:T(8,128)(2,1)}), bf16[4,1664,128]{2,1,0:T(8,128)(2,1)}, u32[]{:S(2)}, u32[]{:S(2)}) async-start(bf16[4,1664,128]{2,1,0:T(8,128)(2,1)} %pad_maximum_fusion), calls=%async_computation.1 | async-start | bytes 3407872 | tf_op jit(solution)/shard_map/all_to_all | solution.py:264
  40.8 15.4 %collective-permute-start.2 = (bf16[384,128]{1,0:T(8,128)(2,1)S(1)}, bf16[384,128]{1,0:T(8,128)(2,1)S(1)}, u32[]{:S(2)}, u32[]{:S(2)}) collective-permute-start(bf16[384,128]{1,0:T(8,128)(2,1)S(1)} %bitcast.61), channel_id=1, source_target_pairs={{0,256},{8,264},{16,272},{24,280},{32,288},{40,296},{48,304},{56,3... | collective-permute-start | bytes 294920 | tf_op jit(solution)/shard_map/ppermute | solution.py:256
  56.2 10.6 %collective-permute-start.5 = (bf16[384,128]{1,0:T(8,128)(2,1)S(1)}, bf16[384,128]{1,0:T(8,128)(2,1)S(1)}, u32[]{:S(2)}, u32[]{:S(2)}) collective-permute-start(bf16[384,128]{1,0:T(8,128)(2,1)S(1)} %collective-permute-done.2), channel_id=1, source_target_pairs={{0,192},{8,200},{16,208},{24,216},{32,224},{40,232},{48,240},{56,2... | collective-permute-start | bytes 294920 | tf_op jit(solution)/shard_map/ppermute | solution.py:266
  61.3 8.0 %collective-permute-start.4 = (bf16[384,128]{1,0:T(8,128)(2,1)S(1)}, bf16[384,128]{1,0:T(8,128)(2,1)S(1)}, u32[]{:S(2)}, u32[]{:S(2)}) collective-permute-start(bf16[384,128]{1,0:T(8,128)(2,1)S(1)} %collective-permute-done.2), channel_id=1, source_target_pairs={{0,128},{8,136},{16,144},{24,152},{32,160},{40,168},{48,176},{56,1... | collective-permute-start | bytes 294920 | tf_op jit(solution)/shard_map/ppermute | solution.py:266
  64.1 7.7 %collective-permute-start.3 = (bf16[384,128]{1,0:T(8,128)(2,1)S(1)}, bf16[384,128]{1,0:T(8,128)(2,1)S(1)}, u32[]{:S(2)}, u32[]{:S(2)}) collective-permute-start(bf16[384,128]{1,0:T(8,128)(2,1)S(1)} %collective-permute-done.2), channel_id=1, source_target_pairs={{0,64},{8,72},{16,80},{24,88},{32,96},{40,104},{48,112},{56,120},{... | collective-permute-start | bytes 294920 | tf_op jit(solution)/shard_map/ppermute | solution.py:266
  71.8 18.0 %collective-permute-start.6 = (bf16[4,384,128]{2,1,0:T(8,128)(2,1)S(1)}, bf16[4,384,128]{2,1,0:T(8,128)(2,1)S(1)}, u32[]{:S(2)}, u32[]{:S(2)}) collective-permute-start(bf16[4,384,128]{2,1,0:T(8,128)(2,1)S(1)} %pad_maximum_fusion.2.f0), channel_id=1, source_target_pairs={{0,16},{8,24},{16,32},{24,40},{32,48},{40,56},{48,0},{56,8},{64,80... | collective-permute-start | bytes 1179656 | tf_op jit(solution)/shard_map/ppermute | solution.py:267
  77.3 13.3 %collective-permute-start.7 = (bf16[4,384,128]{2,1,0:T(8,128)(2,1)S(1)}, bf16[4,384,128]{2,1,0:T(8,128)(2,1)}, u32[]{:S(2)}, u32[]{:S(2)}) collective-permute-start(bf16[4,384,128]{2,1,0:T(8,128)(2,1)S(1)} %pad_maximum_fusion.2.f0), channel_id=1, source_target_pairs={{0,32},{8,40},{16,48},{24,56},{32,0},{40,8},{48,16},{56,24},{64,96... | collective-permute-start | bytes 1179656 | tf_op jit(solution)/shard_map/ppermute | solution.py:267
  79.2 15.5 %collective-permute-start.8 = (bf16[4,384,128]{2,1,0:T(8,128)(2,1)S(1)}, bf16[4,384,128]{2,1,0:T(8,128)(2,1)}, u32[]{:S(2)}, u32[]{:S(2)}) collective-permute-start(bf16[4,384,128]{2,1,0:T(8,128)(2,1)S(1)} %pad_maximum_fusion.2.f0), channel_id=1, source_target_pairs={{0,48},{8,56},{16,0},{24,8},{32,16},{40,24},{48,32},{56,40},{64,11... | collective-permute-start | bytes 1179656 | tf_op jit(solution)/shard_map/ppermute | solution.py:267
  85.5 42.4 %copy-start.1 = (bf16[256,256]{1,0:T(8,128)(2,1)S(1)}, bf16[256,256]{1,0:T(8,128)(2,1)}, u32[]{:S(2)}) copy-start(bf16[256,256]{1,0:T(8,128)(2,1)} %constant.135.clone.second) | copy-start | bytes 393220
  99.2 41.3 %copy-start.2 = (bf16[256,256]{1,0:T(8,128)(2,1)S(1)}, bf16[256,256]{1,0:T(8,128)(2,1)}, u32[]{:S(2)}) copy-start(bf16[256,256]{1,0:T(8,128)(2,1)} %constant.138.clone.back) | copy-start | bytes 393220
  99.2 20.3 %all-to-all-start.2 = ((bf16[16,32,128]{2,1,0:T(8,128)(2,1)}), bf16[16,32,128]{2,1,0:T(8,128)(2,1)S(1)}, u32[]{:S(2)}, u32[]{:S(2)}) async-start(bf16[16,32,128]{2,1,0:T(8,128)(2,1)} %copy-done.5), calls=%async_computation.2 | async-start | bytes 262144 | tf_op jit(solution)/shard_map/all_to_all | solution.py:303
  106.0 22.0 %collective-permute-start.10 = (bf16[512,128]{1,0:T(8,128)(2,1)S(1)}, bf16[512,128]{1,0:T(8,128)(2,1)S(1)}, u32[]{:S(2)}, u32[]{:S(2)}) collective-permute-start(bf16[512,128]{1,0:T(8,128)(2,1)S(1)} %bitcast.51), channel_id=1, source_target_pairs={{0,256},{8,264},{16,272},{24,280},{32,288},{40,296},{48,304},{56,3... | collective-permute-start | bytes 393224 | tf_op jit(solution)/shard_map/ppermute | solution.py:308
  119.4 21.0 %collective-permute-start.9 = (bf16[512,128]{1,0:T(8,128)(2,1)S(1)}, bf16[512,128]{1,0:T(8,128)(2,1)S(1)}, u32[]{:S(2)}, u32[]{:S(2)}) collective-permute-start(bf16[512,128]{1,0:T(8,128)(2,1)S(1)} %bitcast.49), channel_id=1, source_target_pairs={{0,256},{8,264},{16,272},{24,280},{32,288},{40,296},{48,304},{56,3... | collective-permute-start | bytes 393224 | tf_op jit(solution)/shard_map/ppermute | solution.py:304
  125.3 15.2 %collective-permute-start.11 = (bf16[32,128]{1,0:T(8,128)(2,1)S(1)}, bf16[32,128]{1,0:T(8,128)(2,1)S(1)}, u32[]{:S(2)}, u32[]{:S(2)}) collective-permute-start(bf16[32,128]{1,0:T(8,128)(2,1)S(1)} %bitcast.73), channel_id=1, source_target_pairs={{0,0},{1,256},{2,16},{3,272},{4,32},{5,288},{6,48},{7,304},{8,64},... | collective-permute-start | bytes 24584 | tf_op jit(solution)/shard_map/ppermute | solution.py:276
  128.0 0.8 copy-start.6
  128.8 0.8 copy-start.8
  131.5 23.1 %copy-start.4 = (bf16[2,2,128,128]{3,2,1,0:T(8,128)(2,1)S(1)}, bf16[2,2,128,128]{3,2,1,0:T(8,128)(2,1)}, u32[]{:S(2)}) copy-start(bf16[2,2,128,128]{3,2,1,0:T(8,128)(2,1)} %copy-done.3) | copy-start | bytes 393220
  140.4 0.8 copy-start.7
  145.8 46.7 %copy-start.18 = (s32[256]{0:T(256)S(1)}, s32[256]{0:T(256)}, u32[]{:S(2)}) copy-start(s32[256]{0:T(256)} %param.24) | copy-start | bytes 3076
  145.8 16.9 %all-to-all-start.3 = ((bf16[32,48,128]{2,1,0:T(8,128)(2,1)}), bf16[32,48,128]{2,1,0:T(8,128)(2,1)S(1)}, u32[]{:S(2)}, u32[]{:S(2)}) async-start(bf16[32,48,128]{2,1,0:T(8,128)(2,1)} %shard_map.175), calls=%async_computation.3 | async-start | bytes 786432 | tf_op jit(solution)/shard_map/all_to_all | solution.py:310
  154.6 53.1 %copy-start.17 = (s32[256]{0:T(256)S(1)}, s32[256]{0:T(256)}, u32[]{:S(2)}) copy-start(s32[256]{0:T(256)} %param.25) | copy-start | bytes 3076
  154.6 3.3 %collective-permute-start.12 = (bf16[2,128,128]{2,1,0:T(8,128)(2,1)S(1)}, bf16[2,128,128]{2,1,0:T(8,128)(2,1)S(1)}, u32[]{:S(2)}, u32[]{:S(2)}) collective-permute-start(bf16[2,128,128]{2,1,0:T(8,128)(2,1)S(1)} %get-tuple-element.15), channel_id=1, source_target_pairs={{0,8},{8,0},{16,24},{24,16},{32,40},{40,32},{48,56},{56,48},{64,72... | collective-permute-start | bytes 196616 | tf_op jit(solution)/shard_map/ppermute | solution.py:306
  179.6 18.4 %collective-permute-start.13 = (bf16[64,512]{1,0:T(8,128)(2,1)S(1)}, bf16[64,512]{1,0:T(8,128)(2,1)S(1)}, u32[]{:S(2)}, u32[]{:S(2)}) collective-permute-start(bf16[64,512]{1,0:T(8,128)(2,1)S(1)} %reduce_sum.50), channel_id=1, source_target_pairs={{0,4},{1,5},{2,6},{3,7},{4,0},{5,1},{6,2},{7,3},{8,12},{9,13},{10,... | collective-permute-start | bytes 196616 | tf_op jit(solution)/shard_map/ppermute | solution.py:324
  (6 other events, 4.6 us)
Sparse Core Ops, SparseCore 0:
  29.8 69.3 all-gather.2

commit v4 on v3

--- a/solution.py
+++ b/solution.py
@@ -64,6 +64,8 @@
 
 
 FIRST, SECOND, BACK, LAST, COS_TW, SIN_TW = tables()
+MATRICES = np.concatenate([np.pad(FIRST, ((0, 0), (0, 192))), SECOND, BACK, LAST])
+TWIDDLES = np.concatenate([COS_TW, SIN_TW], axis=1)
 
 
 def mm(left, right):
@@ -77,10 +79,10 @@
 SCALARS = pl.BlockSpec(memory_space=pltpu.SMEM)
 
 
-def spectrum(rows, scratch, first, second, cos_tw, sin_tw):
-    scratch[...] = rows
+def spectrum(scratch, matrices, twiddles):
+    cos_tw, sin_tw = twiddles[:, :128], twiddles[:, 128:]
     cube = jnp.concatenate([scratch[pl.ds(c, 64, stride=8), :] for c in range(8)], axis=1)
-    step = mm(first, cube.astype(BF16))
+    step = mm(matrices[:256, :64], cube.astype(BF16))
     parts = []
     for c in range(8):
         real, imag = step[:128, c * 128 : c * 128 + 128], step[128:, c * 128 : c * 128 + 128]
@@ -90,33 +92,34 @@
                 axis=1,
             )
         )
-    return mm(jnp.concatenate(parts, axis=0), second)
-
-
-def filter_kernel(z_ref, own_ref, got_ref, first, second, cos_tw, sin_tw, low_ref, all_ref, scratch):
+    return mm(jnp.concatenate(parts, axis=0), matrices[256:512, :])
+
+
+def filter_kernel(z_ref, got_ref, matrices, twiddles, low_ref, all_ref, scratch):
     upper = z_ref[0] == 1
-    own, got = own_ref[...].astype(F32), got_ref[...].astype(F32)
-    args = (scratch, first[...], second[...], cos_tw[...], sin_tw[...])
-    low = spectrum(jnp.where(upper, got, own), *args)
-    high = spectrum(own, *args)
+    for p in range(16):
+        scratch[p * 32 : p * 32 + 32] = got_ref[p, 32:64].astype(F32)
+    high = spectrum(scratch, matrices, twiddles)
+    for p in range(16):
+        scratch[p * 32 : p * 32 + 32] = jnp.where(upper, got_ref[p, 64:].astype(F32), got_ref[p, 32:64].astype(F32))
+    low = spectrum(scratch, matrices, twiddles)
     odd = lax.broadcasted_iota(jnp.int32, (1024, 256), 0) & 1
     low_ref[...] = low
     all_ref[...] = jnp.where(odd == 1, -low, low) + high
 
 
-def conv_kernel(
-    z_ref, sig_ref, before_ref, low_ref, all_ref, piece_ref, first, second, back, last, cos_tw_ref, sin_tw_ref, out_ref, scratch
-):
-    cos_tw, sin_tw = cos_tw_ref[...], sin_tw_ref[...]
-    args = (scratch, first[...], second[...], cos_tw, sin_tw)
-    own = spectrum(sig_ref[...].astype(F32), *args)
-    old = spectrum(jnp.where(z_ref[0] == 1, before_ref[...].astype(F32), 0.0), *args)
+def conv_kernel(z_ref, sig_ref, before_ref, low_ref, all_ref, piece_ref, matrices, twiddles, out_ref, scratch):
+    cos_tw, sin_tw = twiddles[:, :128], twiddles[:, 128:]
+    scratch[...] = sig_ref[...].astype(F32)
+    own = spectrum(scratch, matrices, twiddles)
+    scratch[...] = jnp.where(z_ref[0] == 1, before_ref[...].astype(F32), 0.0)
+    old = spectrum(scratch, matrices, twiddles)
     low, every = low_ref[...], all_ref[...]
     own_r, own_i, old_r, old_i = own[:, :128], own[:, 128:], old[:, :128], old[:, 128:]
     low_r, low_i, all_r, all_i = low[:, :128], low[:, 128:], every[:, :128], every[:, 128:]
     real = own_r * low_r - own_i * low_i + old_r * all_r - old_i * all_i
     imag = own_r * low_i + own_i * low_r + old_r * all_i + old_i * all_r
-    half = mm(jnp.concatenate([real.astype(BF16), imag.astype(BF16)], axis=1), back[...])
+    half = mm(jnp.concatenate([real.astype(BF16), imag.astype(BF16)], axis=1), matrices[512:768, :])
     parts = []
     for c in range(8):
         real, imag = half[c * 128 : c * 128 + 128, :128], half[c * 128 : c * 128 + 128, 128:]
@@ -126,7 +129,7 @@
                 axis=0,
             )
         )
-    result = mm(last[...], jnp.concatenate(parts, axis=1))
+    result = mm(matrices[768:, :], jnp.concatenate(parts, axis=1))
     for c in range(8):
         scratch[pl.ds(c, 64, stride=8), :] = result[:, c * 128 : c * 128 + 128]
     piece = piece_ref[...]
@@ -155,7 +158,7 @@
         out_ref[part] = total
 
 
-def proj_kernel(at_ref, own_ref, beside_ref, near_ref, f0, f1, f2, f3, sig_ref, gate_ref):
+def proj_kernel(at_ref, own_ref, beside_ref, near_ref, taps_ref, f0, f1, f2, f3, sig_ref, gate_ref):
     y_at, x_at, core = at_ref[0], at_ref[1], at_ref[2]
     start = 2048 - at_ref[3] * 2048
     for part, tokens in enumerate((own_ref, beside_ref)):
@@ -175,6 +178,8 @@
             sig_ref[p, pl.ds(pl.multiple_of(place * 16, 16), 16), :] = rows
         gate_ref[place, 0] = proj[:128, :128].T.astype(BF16)
         gate_ref[place, 1] = proj[128:, :128].T.astype(BF16)
+    for p in range(16):
+        sig_ref[p, 32:, :] = taps_ref[p]
 
 
 def mix_kernel(core_ref, got_ref, keep_ref, other_ref, base_ref, out_ref):
@@ -215,73 +220,75 @@
     return jnp.where(place == 0, jnp.stack([own, other]), jnp.stack([other, own]))
 
 
-def filter_spectra(z, own, got):
-    consts = (jnp.asarray(FIRST, BF16), jnp.asarray(SECOND, BF16), jnp.asarray(COS_TW, F32), jnp.asarray(SIN_TW, F32))
+def filter_spectra(z, got):
     return call(
         filter_kernel,
         (shape((1024, 256), F32), shape((1024, 256), F32)),
-        [SCALARS] + whole(6),
+        [SCALARS] + whole(3),
         [pltpu.VMEM((512, 128), F32)],
         4 * 10**8,
-        (z, own, got, *consts),
+        (z, got, jnp.asarray(MATRICES, BF16), jnp.asarray(TWIDDLES, F32)),
     )
 
 
 def convolve(z, signal, before, low, every, piece):
-    consts = [jnp.asarray(t, BF16) for t in (FIRST, SECOND, BACK, LAST)]
-    consts += [jnp.asarray(t, F32) for t in (COS_TW, SIN_TW)]
     return call(
         conv_kernel,
         shape((32, 48, 128), BF16),
-        [SCALARS] + whole(11),
+        [SCALARS] + whole(7),
         [pltpu.VMEM((512, 128), F32)],
         6 * 10**8,
-        (z, signal, before, low, every, piece, *consts),
-    )
-
-
-def gather_weights(w_in, long_filter, ctx):
+        (z, signal, before, low, every, piece, jnp.asarray(MATRICES, BF16), jnp.asarray(TWIDDLES, F32)),
+    )
+
+
+def gather_weights(w_in, ctx):
     core = ctx % 2
     halves = w_in.transpose(1, 0, 2).reshape(3, 64, 2, 128)
-    taps = long_filter.reshape(256, 2, 128)
-
-    def half_of(which):
-        weights = lax.dynamic_index_in_dim(halves, which, 2, False).reshape(192, 128)
-        return jnp.concatenate([weights, lax.dynamic_index_in_dim(taps, which, 1, False)], axis=0)
-
-    keep = half_of(core)
-    got = lax.ppermute(half_of(1 - core), "ctx", PERM_CORE)
-    both = by_position(keep, got, core)
-    near = both[:, :192].reshape(2, 3, 64, 128).transpose(1, 0, 2, 3).reshape(384, 128)
+    keep = lax.dynamic_index_in_dim(halves, core, 2, False)
+    got = lax.ppermute(lax.dynamic_index_in_dim(halves, 1 - core, 2, False), "ctx", PERM_CORE)
+    near = jnp.concatenate(
+        [jnp.where(core == 0, keep, got), jnp.where(core == 0, got, keep)], axis=1
+    ).reshape(384, 128)
     far = lax.ppermute(near, "ctx", PERM_Z)
-    taps = both[:, 192:].reshape(2, 2, 128, 4, 4, 8).transpose(4, 3, 0, 1, 5, 2).reshape(4, 128, 128)
-
-    near = jnp.concatenate([jnp.broadcast_to(near, (4, 384, 128)), taps], axis=1)
-    near = lax.all_to_all(near, "ctx", 0, 0, axis_index_groups=GROUPS_X, tiled=True)
-    taps = near[:, 384:].reshape(4, 4, 32, 128).transpose(1, 0, 2, 3).reshape(4, 128, 128)
-    near = jnp.broadcast_to(near[:, :384].reshape(1, 1536, 128), (4, 1536, 128))
-    near = jnp.concatenate([near, taps], axis=1)
+
+    near = lax.all_to_all(
+        jnp.broadcast_to(near, (4, 384, 128)), "ctx", 0, 0, axis_index_groups=GROUPS_X, tiled=True
+    )
+    near, far = lax.optimization_barrier((near, far))
+    near = jnp.broadcast_to(near.reshape(1, 1536, 128), (4, 1536, 128))
     near = lax.all_to_all(near, "ctx", 0, 0, axis_index_groups=GROUPS_Y, tiled=True)
 
     along_y = jnp.stack([far] + [lax.ppermute(far, "ctx", PERM_Y[k]) for k in (1, 2, 3)])
     fars = [along_y] + [lax.ppermute(along_y, "ctx", PERM_X[k]) for k in (1, 2, 3)]
-    return near, fars, near[:, 1536:].reshape(512, 128)
-
-
-def output_weights(w_out, w_unembed, tp):
-    partial = mm(w_out, w_unembed)
-    partial = lax.all_gather(jnp.concatenate([partial, partial]), "tp", axis=0)
-    rows = lax.dynamic_slice_in_dim(partial, (tp // 2) * 8, 8, 1)
-    rows = jnp.sum(rows, axis=0).astype(BF16).reshape(8, 4, 128).transpose(1, 0, 2).reshape(32, 128)
-    return lax.ppermute(rows, ("ctx", "tp"), ROUTE)
+    return near, fars, got
+
+
+def gather_filter(long_filter, ctx):
+    core = ctx % 2
+    taps = long_filter.reshape(256, 2, 128)
+    keep = lax.dynamic_index_in_dim(taps, core, 1, False)
+    got = lax.ppermute(lax.dynamic_index_in_dim(taps, 1 - core, 1, False), "ctx", PERM_CORE)
+    taps = by_position(keep, got, core).reshape(2, 2, 128, 16, 8).transpose(3, 0, 1, 4, 2).reshape(16, 32, 128)
+    return jnp.concatenate([taps, lax.ppermute(taps, "ctx", PERM_Z_UP)], axis=1)
+
+
+def output_weights(w_out, w_unembed, near):
+    partial = mm(w_out, w_unembed).astype(BF16).reshape(4, 1, 8, 4, 128).transpose(0, 1, 3, 2, 4)
+    partial = jnp.broadcast_to(partial.reshape(4, 1, 32, 128), (4, 2, 32, 128)).reshape(8, 32, 128)
+    partial, _ = lax.optimization_barrier((partial, near))
+    partial = lax.all_to_all(partial, "tp", 0, 0, tiled=True)
+    return jnp.sum(partial.astype(F32), axis=0).astype(BF16)
 
 
 def per_device(tokens_in, pre_gain, w_in, w_out, long_filter, w_unembed, target_ids, score_mask):
     ctx, tp = lax.axis_index("ctx"), lax.axis_index("tp")
     core, z = ctx % 2, ctx // 32
     z_at = z.reshape(1).astype(jnp.int32)
-    near, fars, taps = gather_weights(w_in, long_filter, ctx)
-    piece = output_weights(w_out, w_unembed, tp)
+    near, fars, first = gather_weights(w_in, ctx)
+    tokens_in, long_filter, w_out, _ = lax.optimization_barrier((tokens_in, long_filter, w_out, first))
+    taps = gather_filter(long_filter, ctx)
+    piece = output_weights(w_out, w_unembed, near)
 
     stream = tokens_in.astype(F32)
     scale = lax.rsqrt(jnp.mean(stream * stream, axis=1, keepdims=True) + NORM_EPS)
@@ -294,18 +301,21 @@
     )
     signal, gate = call(
         proj_kernel,
-        (shape((16, 32, 128), BF16), shape((2, 2, 128, 128), BF16)),
-        [SCALARS] + whole(7),
+        (shape((16, 96, 128), BF16), shape((2, 2, 128, 128), BF16)),
+        [SCALARS] + whole(8),
         [],
         8 * 10**8,
-        (at, normed, beside, sums, *fars),
-    )
-    signal = lax.all_to_all(signal, "ctx", 0, 0, axis_index_groups=GROUPS_CORE, tiled=True).reshape(512, 128)
+        (at, normed, beside, sums, taps, *fars),
+    )
+    signal, piece = lax.optimization_barrier((signal, piece))
+    piece = lax.ppermute(piece, ("ctx", "tp"), ROUTE)
+    got = lax.all_to_all(signal, "ctx", 0, 0, axis_index_groups=GROUPS_CORE, tiled=True)
+    signal = got[:, :32].reshape(512, 128)
     before = lax.ppermute(signal, "ctx", PERM_Z_UP)
     gate_keep = lax.dynamic_index_in_dim(gate, core, 0, False)
     gate_got = lax.ppermute(lax.dynamic_index_in_dim(gate, 1 - core, 0, False), "ctx", PERM_CORE)
 
-    spectra = filter_spectra(z_at, taps, lax.ppermute(taps, "ctx", PERM_Z_UP))
+    spectra = filter_spectra(z_at, got)
     conv = convolve(z_at, signal, before, *spectra, piece)
     conv = lax.all_to_all(conv, "ctx", 0, 0, axis_index_groups=GROUPS_PLANE, tiled=True)
 

time: 216 us -> 196 us (0.907)
  between operations: 14.1 us -> 0.56 us
  waiting for transfers between devices: 45.9 us -> 37.8 us
  blocking collectives: 24.5 us -> 32.3 us
  local copies, waits for them, and re-layouts: 10 us -> 5.33 us
  other arithmetic: 9.12 us -> 6.33 us
    all_to_all x0 -> x1, blocking collectives: none -> 11.8 us  [per_device(): lax.all_to_all(signal, 'ctx', 0, 0, axis_index_groups=GROUPS_CORE, tiled=...]
    ppermute x3, waiting for transfers between devices: 9.22 us -> 0.01 us  [gather_weights(): lax.ppermute(along_y, 'ctx', PERM_X[k])]
    unnamed x43 -> x19, local copies, waits for them, and re-layouts: 7.4 us -> 0.21 us
    ppermute x1, starting transfers between devices: 12.8 us -> 6.33 us  [per_device(): far = lax.ppermute(logits, 'tp', [(i, i ^ 4) for i in range(8)])]
    ppermute x3, waiting for transfers between devices: 4.94 us -> 0.01 us  [gather_weights(): lax.ppermute(far, 'ctx', PERM_Y[k])]
    all_to_all x1, blocking collectives: 16.6 us -> 12.7 us  [per_device(): lax.all_to_all(logits.reshape(4, 64, 512), 'tp', 0, 0, axis_index_groups=...]
    all_to_all x2, starting transfers between devices: 15.2 us -> 18.9 us  [the longest x1 9.65 us: output_weights(): partial = lax.all_to_all(partial, 'tp', 0, 0, tiled=True)]
    all_to_all x2, waiting for transfers between devices: 7.1 us -> 9.89 us  [the longest x1 9.89 us: output_weights(): partial = lax.all_to_all(partial, 'tp', 0, 0, tiled=True)]
  transfers between devices with their start and end apart: 19 -> 19, of which waited for: 11 -> 7; matrix products, arithmetic and copies ran while one was open for 3% -> 3% of each run, Pallas kernels for 3% -> 2%
where the time goes in v4:
time: 196 us; the launch traced here: 194 us
  starting transfers between devices  101 us (52%)
  waiting for transfers between devices  37.8 us (19%)
  blocking collectives  32.3 us (16%)
  Pallas kernels  10.1 us (5%)
  other arithmetic  6.33 us (3%)
  local copies, waits for them, and re-layouts  5.33 us (3%)
    ppermute x1, starting transfers between devices, gather_filter(): return jnp.concatenate([taps, lax.ppermute(taps, 'ctx', PERM_Z_UP)], axis=1)  12.9 us
    all_to_all x1, blocking collectives, per_device(): lax.all_to_all(logits.reshape(4, 64, 512), 'tp', 0, 0, axis_index_groups=...  12.7 us
    ppermute x3, starting transfers between devices, gather_weights(): lax.ppermute(far, 'ctx', PERM_Y[k])  11.8 us
    all_to_all x1, blocking collectives, per_device(): lax.all_to_all(signal, 'ctx', 0, 0, axis_index_groups=GROUPS_CORE, tiled=...  11.8 us
    ppermute x1, starting transfers between devices, gather_weights(): far = lax.ppermute(near, 'ctx', PERM_Z)  11.2 us
    ppermute x1, waiting for transfers between devices, per_device(): piece = lax.ppermute(piece, ('ctx', 'tp'), ROUTE)  10.4 us
    pallas_call x5, Pallas kernels, call(): pl.pallas_call(kernel, out_shape=outs, in_specs=specs, out_specs=jax.tree...  10.1 us
    all_to_all x1, waiting for transfers between devices, output_weights(): partial = lax.all_to_all(partial, 'tp', 0, 0, tiled=True)  9.89 us
  transfers between devices with their start and end apart: 19, of which 7 were waited for; matrix products, arithmetic and copies ran while one was open for 3% of the time, Pallas kernels for 2%

profile of v4, /device:TPU:6, one launch (start us, length us, event | category | flops | bytes accessed | tf_op | source)
XLA Modules:
  0.0 194.4 jit_solution(17615026350657414308)
XLA Ops:
  1.2 2.1 %collective-permute-start = (bf16[3,64,128]{2,1,0:T(8,128)(2,1)S(1)}, bf16[3,64,128]{2,1,0:T(8,128)(2,1)S(1)}, u32[]{:S(2)}, u32[]{:S(2)}) collective-permute-start(bf16[3,64,128]{2,1,0:T(8,128)(2,1)S(1)} %bitcast.57), channel_id=1, source_target_pairs={{0,8},{8,0},{16,24},{24,16},{32,40},{40,32},{48,56},{56,48},{64,72... | collective-permute-start | bytes 147464 | tf_op jit(solution)/shard_map/ppermute | solution.py:249
  4.5 2.1 %fusion = f32[256]{0:T(256)S(1)} fusion(bf16[256,4096]{1,0:T(8,128)(2,1)} %param.12), kind=kLoop, calls=%fused_computation.2 | loop fusion | flops 3145472 | bytes 2098176 | tf_op jit(solution)/shard_map/reduce_sum | solution.py:294
  7.2 2.1 %collective-permute-start.1 = (bf16[256,4096]{1,0:T(8,128)(2,1)S(1)}, bf16[256,4096]{1,0:T(8,128)(2,1)}, u32[]{:S(2)}, u32[]{:S(2)}) collective-permute-start(bf16[256,4096]{1,0:T(8,128)(2,1)S(1)} %fusion.2.own_ref), channel_id=1, source_target_pairs={{0,8},{8,0},{16,24},{24,16},{32,40},{40,32},{48,56},{56,48},{64,72... | collective-permute-start | bytes 6291464 | tf_op jit(solution)/shard_map/ppermute | solution.py:296
  10.2 9.3 %all-to-all-start = ((bf16[4,384,128]{2,1,0:T(8,128)(2,1)}), bf16[4,384,128]{2,1,0:T(8,128)(2,1)S(1)}, u32[]{:S(2)}, u32[]{:S(2)}) async-start(bf16[4,384,128]{2,1,0:T(8,128)(2,1)} %broadcast_in_dim.16), calls=%async_computation | async-start | bytes 786432 | tf_op jit(solution)/shard_map/all_to_all | solution.py:255
  19.4 11.2 %collective-permute-start.2 = (bf16[384,128]{1,0:T(8,128)(2,1)S(1)}, bf16[384,128]{1,0:T(8,128)(2,1)S(1)}, u32[]{:S(2)}, u32[]{:S(2)}) collective-permute-start(bf16[384,128]{1,0:T(8,128)(2,1)S(1)} %bitcast.50), channel_id=1, source_target_pairs={{0,256},{8,264},{16,272},{24,280},{32,288},{40,296},{48,304},{56,3... | collective-permute-start | bytes 294920 | tf_op jit(solution)/shard_map/ppermute | solution.py:253
  30.7 4.3 %collective-permute-done.2 = bf16[384,128]{1,0:T(8,128)(2,1)S(1)} collective-permute-done((bf16[384,128]{1,0:T(8,128)(2,1)S(1)}, bf16[384,128]{1,0:T(8,128)(2,1)S(1)}, u32[]{:S(2)}, u32[]{:S(2)}) %collective-permute-start.2) | collective-permute-done | bytes 98336 | tf_op jit(solution)/shard_map/ppermute | solution.py:253
  34.9 1.4 broadcast_in_dim.33
  36.3 4.5 %all-to-all-start.1 = ((bf16[4,1536,128]{2,1,0:T(8,128)(2,1)}), bf16[4,1536,128]{2,1,0:T(8,128)(2,1)}, u32[]{:S(2)}, u32[]{:S(2)}) async-start(bf16[4,1536,128]{2,1,0:T(8,128)(2,1)} %broadcast_in_dim.33), calls=%async_computation.1 | async-start | bytes 3145728 | tf_op jit(solution)/shard_map/all_to_all | solution.py:260
  41.0 1.9 collective-permute-start.3
  44.3 3.9 %collective-permute-start.5 = (bf16[384,128]{1,0:T(8,128)(2,1)S(1)}, bf16[384,128]{1,0:T(8,128)(2,1)S(1)}, u32[]{:S(2)}, u32[]{:S(2)}) collective-permute-start(bf16[384,128]{1,0:T(8,128)(2,1)S(1)} %collective-permute-done.2), channel_id=1, source_target_pairs={{0,64},{8,72},{16,80},{24,88},{32,96},{40,104},{48,112},{56,120},{... | collective-permute-start | bytes 294920 | tf_op jit(solution)/shard_map/ppermute | solution.py:262
  48.2 4.6 %collective-permute-start.6 = (bf16[384,128]{1,0:T(8,128)(2,1)S(1)}, bf16[384,128]{1,0:T(8,128)(2,1)S(1)}, u32[]{:S(2)}, u32[]{:S(2)}) collective-permute-start(bf16[384,128]{1,0:T(8,128)(2,1)S(1)} %collective-permute-done.2), channel_id=1, source_target_pairs={{0,128},{8,136},{16,144},{24,152},{32,160},{40,168},{48,176},{56,1... | collective-permute-start | bytes 294920 | tf_op jit(solution)/shard_map/ppermute | solution.py:262
  52.8 3.4 %collective-permute-start.7 = (bf16[384,128]{1,0:T(8,128)(2,1)S(1)}, bf16[384,128]{1,0:T(8,128)(2,1)S(1)}, u32[]{:S(2)}, u32[]{:S(2)}) collective-permute-start(bf16[384,128]{1,0:T(8,128)(2,1)S(1)} %collective-permute-done.2), channel_id=1, source_target_pairs={{0,192},{8,200},{16,208},{24,216},{32,224},{40,232},{48,240},{56,2... | collective-permute-start | bytes 294920 | tf_op jit(solution)/shard_map/ppermute | solution.py:262
  56.4 12.9 %collective-permute-start.4 = (bf16[16,32,128]{2,1,0:T(8,128)(2,1)S(1)}, bf16[16,32,128]{2,1,0:T(8,128)(2,1)}, u32[]{:S(2)}, u32[]{:S(2)}) collective-permute-start(bf16[16,32,128]{2,1,0:T(8,128)(2,1)S(1)} %bitcast.47), channel_id=1, source_target_pairs={{0,256},{8,264},{16,272},{24,280},{32,288},{40,296},{48,304},{56,3... | collective-permute-start | bytes 393224 | tf_op jit(solution)/shard_map/ppermute | solution.py:273
  69.4 2.8 %collective-permute-start.10 = (bf16[4,384,128]{2,1,0:T(8,128)(2,1)S(1)}, bf16[4,384,128]{2,1,0:T(8,128)(2,1)}, u32[]{:S(2)}, u32[]{:S(2)}) collective-permute-start(bf16[4,384,128]{2,1,0:T(8,128)(2,1)S(1)} %pad_maximum_fusion.f0), channel_id=1, source_target_pairs={{0,48},{8,56},{16,0},{24,8},{32,16},{40,24},{48,32},{56,40},{64,11... | collective-permute-start | bytes 1179656 | tf_op jit(solution)/shard_map/ppermute | solution.py:263
  72.1 4.3 %collective-permute-start.8 = (bf16[4,384,128]{2,1,0:T(8,128)(2,1)S(1)}, bf16[4,384,128]{2,1,0:T(8,128)(2,1)}, u32[]{:S(2)}, u32[]{:S(2)}) collective-permute-start(bf16[4,384,128]{2,1,0:T(8,128)(2,1)S(1)} %pad_maximum_fusion.f0), channel_id=1, source_target_pairs={{0,16},{8,24},{16,32},{24,40},{32,48},{40,56},{48,0},{56,8},{64,80... | collective-permute-start | bytes 1179656 | tf_op jit(solution)/shard_map/ppermute | solution.py:263
  76.4 2.2 %collective-permute-start.9 = (bf16[4,384,128]{2,1,0:T(8,128)(2,1)S(1)}, bf16[4,384,128]{2,1,0:T(8,128)(2,1)}, u32[]{:S(2)}, u32[]{:S(2)}) collective-permute-start(bf16[4,384,128]{2,1,0:T(8,128)(2,1)S(1)} %pad_maximum_fusion.f0), channel_id=1, source_target_pairs={{0,32},{8,40},{16,48},{24,56},{32,0},{40,8},{48,16},{56,24},{64,96... | collective-permute-start | bytes 1179656 | tf_op jit(solution)/shard_map/ppermute | solution.py:263
  79.5 9.7 %all-to-all-start.2 = ((bf16[8,32,128]{2,1,0:T(8,128)(2,1)}), bf16[8,32,128]{2,1,0:T(8,128)(2,1)S(1)}, u32[]{:S(2)}, u32[]{:S(2)}) async-start(bf16[8,32,128]{2,1,0:T(8,128)(2,1)} %bitcast.18), calls=%async_computation.2 | async-start | bytes 131072 | tf_op jit(solution)/shard_map/all_to_all | solution.py:280
  90.1 9.9 %all-to-all-done.2 = bf16[8,32,128]{2,1,0:T(8,128)(2,1)S(1)} async-done(((bf16[8,32,128]{2,1,0:T(8,128)(2,1)}), bf16[8,32,128]{2,1,0:T(8,128)(2,1)S(1)}, u32[]{:S(2)}, u32[]{:S(2)}) %all-to-all-start.2) | async-done | bytes 65568 | tf_op jit(solution)/shard_map/all_to_all | solution.py:280
  100.0 3.3 %shard_map.118.near_ref = f32[2,256,384]{2,1,0:T(8,128)S(1)} custom-call(s32[4]{0:T(128)S(1)} %pad_add_fusion.at_ref, bf16[256,4096]{1,0:T(8,128)(2,1)S(1)} %fusion.2.own_ref, bf16[256,4096]{1,0:T(8,128)(2,1)} %collective-permute-done.1.beside_ref, bf16[4,1536,128]{2,1,0:T(8,128)(2,1)} %all-to-all-done.1.near_ref), custom_call_target="tpu_custom_call" | custom-call | flops 800000000 | bytes 4194304 | tf_op jit(solution)/shard_map/pallas_call | solution.py:204
  103.4 3.3 %shard_map.119 = (bf16[16,96,128]{2,1,0:T(8,128)(2,1)S(1)}, bf16[2,2,128,128]{3,2,1,0:T(8,128)(2,1)S(1)}) custom-call(s32[4]{0:T(128)S(1)} %pad_add_fusion.at_ref, bf16[256,4096]{1,0:T(8,128)(2,1)S(1)} %fusion.2.own_ref, bf16[256,4096]{1,0:T(8,128)(2,1)} %collective-permute-done.1.beside_ref, f32[2,256,384]{2,1,0:T(8,128)S(1)} %shard_map.118.near_ref, ...), custom_call_target="tpu_custom_call" | custom-call | flops 800000000 | bytes 4194304 | tf_op jit(solution)/shard_map/pallas_call | solution.py:204
  106.7 11.8 %all_to_all.35.got_ref = bf16[16,96,128]{2,1,0:T(8,128)(2,1)S(1)} all-to-all(bf16[16,96,128]{2,1,0:T(8,128)(2,1)S(1)} %get-tuple-element.24), channel_id=1, replica_groups={{0,16,32,48,64,80,96,112,128,144,160,176,192,208,224,240},{8,24,40,56,7..., dimensions={0} | all-to-all | bytes 786432 | tf_op jit(solution)/shard_map/all_to_all | solution.py:312
  118.5 7.3 %collective-permute-start.11 = (bf16[512,128]{1,0:T(8,128)(2,1)S(1)}, bf16[512,128]{1,0:T(8,128)(2,1)S(1)}, u32[]{:S(2)}, u32[]{:S(2)}) collective-permute-start(bf16[512,128]{1,0:T(8,128)(2,1)S(1)} %bitcast.43), channel_id=1, source_target_pairs={{0,256},{8,264},{16,272},{24,280},{32,288},{40,296},{48,304},{56,3... | collective-permute-start | bytes 393224 | tf_op jit(solution)/shard_map/ppermute | solution.py:314
  125.8 1.9 collective-permute-start.12
  128.8 10.4 %collective-permute-done.12.piece_ref = bf16[32,128]{1,0:T(8,128)(2,1)S(1)} collective-permute-done((bf16[32,128]{1,0:T(8,128)(2,1)S(1)}, bf16[32,128]{1,0:T(8,128)(2,1)S(1)}, u32[]{:S(2)}, u32[]{:S(2)}) %collective-permute-start.12) | collective-permute-done | bytes 8224 | tf_op jit(solution)/shard_map/ppermute | solution.py:311
  139.2 2.1 %shard_map.121 = bf16[32,48,128]{2,1,0:T(8,128)(2,1)} custom-call(s32[1]{0:T(128)} %bitcast.1.z_ref, bf16[512,128]{1,0:T(8,128)(2,1)S(1)} %bitcast.44, bf16[512,128]{1,0:T(8,128)(2,1)S(1)} %collective-permute-done.11.before_ref, f32[1024,256]{1,0:T(8,128)S(1)} %get-tuple-element.25.low_ref, f32[1024,256]{1,0:T(8,128)S(1)} %get-tuple-element.26.all_ref, ...), custom_call_target="tpu_custom_call" | custom-call | flops 600000000 | bytes 4194304 | tf_op jit(solution)/shard_map/pallas_call | solution.py:204
  141.3 8.4 %all-to-all-start.4 = ((bf16[32,48,128]{2,1,0:T(8,128)(2,1)}), bf16[32,48,128]{2,1,0:T(8,128)(2,1)S(1)}, u32[]{:S(2)}, u32[]{:S(2)}) async-start(bf16[32,48,128]{2,1,0:T(8,128)(2,1)} %shard_map.121), calls=%async_computation.4 | async-start | bytes 786432 | tf_op jit(solution)/shard_map/all_to_all | solution.py:320
  149.7 2.1 %collective-permute-start.13 = (bf16[2,128,128]{2,1,0:T(8,128)(2,1)S(1)}, bf16[2,128,128]{2,1,0:T(8,128)(2,1)S(1)}, u32[]{:S(2)}, u32[]{:S(2)}) collective-permute-start(bf16[2,128,128]{2,1,0:T(8,128)(2,1)S(1)} %get-tuple-element.33), channel_id=1, source_target_pairs={{0,8},{8,0},{16,24},{24,16},{32,40},{40,32},{48,56},{56,48},{64,72... | collective-permute-start | bytes 196616 | tf_op jit(solution)/shard_map/ppermute | solution.py:316
  153.0 4.7 %all-to-all-done.4.got_ref = bf16[32,48,128]{2,1,0:T(8,128)(2,1)S(1)} async-done(((bf16[32,48,128]{2,1,0:T(8,128)(2,1)}), bf16[32,48,128]{2,1,0:T(8,128)(2,1)S(1)}, u32[]{:S(2)}, u32[]{:S(2)}) %all-to-all-start.4) | async-done | bytes 393248 | tf_op jit(solution)/shard_map/all_to_all | solution.py:320
  158.1 12.7 %all_to_all.36 = bf16[4,64,512]{2,1,0:T(8,128)(2,1)S(1)} all-to-all(bf16[4,64,512]{2,1,0:T(8,128)(2,1)S(1)} %bitcast.42), channel_id=1, replica_groups={{0,1,2,3},{4,5,6,7},{8,9,10,11},{12,13,14,15},{16,17,18,19},{20,21,22,2..., dimensions={0} | all-to-all | bytes 524288 | tf_op jit(solution)/shard_map/all_to_all | solution.py:332
  170.8 6.3 %collective-permute-start.14 = (bf16[64,512]{1,0:T(8,128)(2,1)S(1)}, bf16[64,512]{1,0:T(8,128)(2,1)S(1)}, u32[]{:S(2)}, u32[]{:S(2)}) collective-permute-start(bf16[64,512]{1,0:T(8,128)(2,1)S(1)} %reduce_sum.53), channel_id=1, source_target_pairs={{0,4},{1,5},{2,6},{3,7},{4,0},{5,1},{6,2},{7,3},{8,12},{9,13},{10,... | collective-permute-start | bytes 196616 | tf_op jit(solution)/shard_map/ppermute | solution.py:334
  177.2 6.9 %collective-permute-done.14 = bf16[64,512]{1,0:T(8,128)(2,1)S(1)} collective-permute-done((bf16[64,512]{1,0:T(8,128)(2,1)S(1)}, bf16[64,512]{1,0:T(8,128)(2,1)S(1)}, u32[]{:S(2)}, u32[]{:S(2)}) %collective-permute-start.14) | collective-permute-done | bytes 65568 | tf_op jit(solution)/shard_map/ppermute | solution.py:334
  184.6 7.9 %all_to_all.37 = f32[4,1,512]{2,1,0:T(1,128)S(1)} all-to-all(f32[4,1,512]{2,1,0:T(1,128)S(1)} %reshape.81), channel_id=1, replica_groups={{0,1,2,3},{4,5,6,7},{8,9,10,11},{12,13,14,15},{16,17,18,19},{20,21,22,2..., dimensions={0} | all-to-all | bytes 16384 | tf_op jit(solution)/shard_map/all_to_all | solution.py:343
  (71 shorter events, 12.7 us)
Async XLA Ops:
  0.0 78.6 %copy-start = (bf16[512,512]{1,0:T(8,128)(2,1)S(1)}, bf16[512,512]{1,0:T(8,128)(2,1)}, u32[]{:S(2)}) copy-start(bf16[512,512]{1,0:T(8,128)(2,1)} %param.17) | copy-start | bytes 1572868
  1.0 5.6 %copy-start.3 = (bf16[256,4096]{1,0:T(8,128)(2,1)S(1)}, bf16[256,4096]{1,0:T(8,128)(2,1)}, u32[]{:S(2)}) copy-start(bf16[256,4096]{1,0:T(8,128)(2,1)} %param.12) | copy-start | bytes 6291460
  1.2 3.3 %collective-permute-start = (bf16[3,64,128]{2,1,0:T(8,128)(2,1)S(1)}, bf16[3,64,128]{2,1,0:T(8,128)(2,1)S(1)}, u32[]{:S(2)}, u32[]{:S(2)}) collective-permute-start(bf16[3,64,128]{2,1,0:T(8,128)(2,1)S(1)} %bitcast.57), channel_id=1, source_target_pairs={{0,8},{8,0},{16,24},{24,16},{32,40},{40,32},{48,56},{56,48},{64,72... | collective-permute-start | bytes 147464 | tf_op jit(solution)/shard_map/ppermute | solution.py:249
  7.2 92.8 %collective-permute-start.1 = (bf16[256,4096]{1,0:T(8,128)(2,1)S(1)}, bf16[256,4096]{1,0:T(8,128)(2,1)}, u32[]{:S(2)}, u32[]{:S(2)}) collective-permute-start(bf16[256,4096]{1,0:T(8,128)(2,1)S(1)} %fusion.2.own_ref), channel_id=1, source_target_pairs={{0,8},{8,0},{16,24},{24,16},{32,40},{40,32},{48,56},{56,48},{64,72... | collective-permute-start | bytes 6291464 | tf_op jit(solution)/shard_map/ppermute | solution.py:296
  10.2 24.8 %all-to-all-start = ((bf16[4,384,128]{2,1,0:T(8,128)(2,1)}), bf16[4,384,128]{2,1,0:T(8,128)(2,1)S(1)}, u32[]{:S(2)}, u32[]{:S(2)}) async-start(bf16[4,384,128]{2,1,0:T(8,128)(2,1)} %broadcast_in_dim.16), calls=%async_computation | async-start | bytes 786432 | tf_op jit(solution)/shard_map/all_to_all | solution.py:255
  19.4 15.5 %collective-permute-start.2 = (bf16[384,128]{1,0:T(8,128)(2,1)S(1)}, bf16[384,128]{1,0:T(8,128)(2,1)S(1)}, u32[]{:S(2)}, u32[]{:S(2)}) collective-permute-start(bf16[384,128]{1,0:T(8,128)(2,1)S(1)} %bitcast.50), channel_id=1, source_target_pairs={{0,256},{8,264},{16,272},{24,280},{32,288},{40,296},{48,304},{56,3... | collective-permute-start | bytes 294920 | tf_op jit(solution)/shard_map/ppermute | solution.py:253
  34.9 5.9 %copy-start.4 = (bf16[256,256]{1,0:T(8,128)(2,1)S(1)}, bf16[256,256]{1,0:T(8,128)(2,1)}, u32[]{:S(2)}) copy-start(bf16[256,256]{1,0:T(8,128)(2,1)} %param.16) | copy-start | bytes 393220
  36.3 42.3 %copy-start.5 = (bf16[32,512]{1,0:T(8,128)(2,1)S(1)}, bf16[32,512]{1,0:T(8,128)(2,1)}, u32[]{:S(2)}) copy-start(bf16[32,512]{1,0:T(8,128)(2,1)} %param.15) | copy-start | bytes 98308
  36.3 42.5 %all-to-all-start.1 = ((bf16[4,1536,128]{2,1,0:T(8,128)(2,1)}), bf16[4,1536,128]{2,1,0:T(8,128)(2,1)}, u32[]{:S(2)}, u32[]{:S(2)}) async-start(bf16[4,1536,128]{2,1,0:T(8,128)(2,1)} %broadcast_in_dim.33), calls=%async_computation.1 | async-start | bytes 3145728 | tf_op jit(solution)/shard_map/all_to_all | solution.py:260
  41.0 3.1 %collective-permute-start.3 = (bf16[256,128]{1,0:T(8,128)(2,1)S(1)}, bf16[256,128]{1,0:T(8,128)(2,1)S(1)}, u32[]{:S(2)}, u32[]{:S(2)}) collective-permute-start(bf16[256,128]{1,0:T(8,128)(2,1)S(1)} %bitcast.56), channel_id=1, source_target_pairs={{0,8},{8,0},{16,24},{24,16},{32,40},{40,32},{48,56},{56,48},{64,72... | collective-permute-start | bytes 196616 | tf_op jit(solution)/shard_map/ppermute | solution.py:271
  44.3 25.0 %collective-permute-start.5 = (bf16[384,128]{1,0:T(8,128)(2,1)S(1)}, bf16[384,128]{1,0:T(8,128)(2,1)S(1)}, u32[]{:S(2)}, u32[]{:S(2)}) collective-permute-start(bf16[384,128]{1,0:T(8,128)(2,1)S(1)} %collective-permute-done.2), channel_id=1, source_target_pairs={{0,64},{8,72},{16,80},{24,88},{32,96},{40,104},{48,112},{56,120},{... | collective-permute-start | bytes 294920 | tf_op jit(solution)/shard_map/ppermute | solution.py:262
  48.2 21.1 %collective-permute-start.6 = (bf16[384,128]{1,0:T(8,128)(2,1)S(1)}, bf16[384,128]{1,0:T(8,128)(2,1)S(1)}, u32[]{:S(2)}, u32[]{:S(2)}) collective-permute-start(bf16[384,128]{1,0:T(8,128)(2,1)S(1)} %collective-permute-done.2), channel_id=1, source_target_pairs={{0,128},{8,136},{16,144},{24,152},{32,160},{40,168},{48,176},{56,1... | collective-permute-start | bytes 294920 | tf_op jit(solution)/shard_map/ppermute | solution.py:262
  52.8 16.5 %collective-permute-start.7 = (bf16[384,128]{1,0:T(8,128)(2,1)S(1)}, bf16[384,128]{1,0:T(8,128)(2,1)S(1)}, u32[]{:S(2)}, u32[]{:S(2)}) collective-permute-start(bf16[384,128]{1,0:T(8,128)(2,1)S(1)} %collective-permute-done.2), channel_id=1, source_target_pairs={{0,192},{8,200},{16,208},{24,216},{32,224},{40,232},{48,240},{56,2... | collective-permute-start | bytes 294920 | tf_op jit(solution)/shard_map/ppermute | solution.py:262
  56.4 32.8 %collective-permute-start.4 = (bf16[16,32,128]{2,1,0:T(8,128)(2,1)S(1)}, bf16[16,32,128]{2,1,0:T(8,128)(2,1)}, u32[]{:S(2)}, u32[]{:S(2)}) collective-permute-start(bf16[16,32,128]{2,1,0:T(8,128)(2,1)S(1)} %bitcast.47), channel_id=1, source_target_pairs={{0,256},{8,264},{16,272},{24,280},{32,288},{40,296},{48,304},{56,3... | collective-permute-start | bytes 393224 | tf_op jit(solution)/shard_map/ppermute | solution.py:273
  69.4 34.0 %collective-permute-start.10 = (bf16[4,384,128]{2,1,0:T(8,128)(2,1)S(1)}, bf16[4,384,128]{2,1,0:T(8,128)(2,1)}, u32[]{:S(2)}, u32[]{:S(2)}) collective-permute-start(bf16[4,384,128]{2,1,0:T(8,128)(2,1)S(1)} %pad_maximum_fusion.f0), channel_id=1, source_target_pairs={{0,48},{8,56},{16,0},{24,8},{32,16},{40,24},{48,32},{56,40},{64,11... | collective-permute-start | bytes 1179656 | tf_op jit(solution)/shard_map/ppermute | solution.py:263
  72.1 31.3 %collective-permute-start.8 = (bf16[4,384,128]{2,1,0:T(8,128)(2,1)S(1)}, bf16[4,384,128]{2,1,0:T(8,128)(2,1)}, u32[]{:S(2)}, u32[]{:S(2)}) collective-permute-start(bf16[4,384,128]{2,1,0:T(8,128)(2,1)S(1)} %pad_maximum_fusion.f0), channel_id=1, source_target_pairs={{0,16},{8,24},{16,32},{24,40},{32,48},{40,56},{48,0},{56,8},{64,80... | collective-permute-start | bytes 1179656 | tf_op jit(solution)/shard_map/ppermute | solution.py:263
  76.4 27.0 %collective-permute-start.9 = (bf16[4,384,128]{2,1,0:T(8,128)(2,1)S(1)}, bf16[4,384,128]{2,1,0:T(8,128)(2,1)}, u32[]{:S(2)}, u32[]{:S(2)}) collective-permute-start(bf16[4,384,128]{2,1,0:T(8,128)(2,1)S(1)} %pad_maximum_fusion.f0), channel_id=1, source_target_pairs={{0,32},{8,40},{16,48},{24,56},{32,0},{40,8},{48,16},{56,24},{64,96... | collective-permute-start | bytes 1179656 | tf_op jit(solution)/shard_map/ppermute | solution.py:263
  79.5 20.6 %all-to-all-start.2 = ((bf16[8,32,128]{2,1,0:T(8,128)(2,1)}), bf16[8,32,128]{2,1,0:T(8,128)(2,1)S(1)}, u32[]{:S(2)}, u32[]{:S(2)}) async-start(bf16[8,32,128]{2,1,0:T(8,128)(2,1)} %bitcast.18), calls=%async_computation.2 | async-start | bytes 131072 | tf_op jit(solution)/shard_map/all_to_all | solution.py:280
  103.3 24.4 %copy-start.1 = (bf16[832,256]{1,0:T(8,128)(2,1)S(1)}, bf16[832,256]{1,0:T(8,128)(2,1)}, u32[]{:S(2)}) copy-start(bf16[832,256]{1,0:T(8,128)(2,1)} %constant.121.clone.matrices) | copy-start | bytes 1277956
  103.4 24.4 %copy-start.2 = (f32[128,256]{1,0:T(8,128)S(1)}, f32[128,256]{1,0:T(8,128)}, u32[]{:S(2)}) copy-start(f32[128,256]{1,0:T(8,128)} %constant.122.clone.twiddles) | copy-start | bytes 393220
  118.5 20.7 %collective-permute-start.11 = (bf16[512,128]{1,0:T(8,128)(2,1)S(1)}, bf16[512,128]{1,0:T(8,128)(2,1)S(1)}, u32[]{:S(2)}, u32[]{:S(2)}) collective-permute-start(bf16[512,128]{1,0:T(8,128)(2,1)S(1)} %bitcast.43), channel_id=1, source_target_pairs={{0,256},{8,264},{16,272},{24,280},{32,288},{40,296},{48,304},{56,3... | collective-permute-start | bytes 393224 | tf_op jit(solution)/shard_map/ppermute | solution.py:314
  125.8 13.4 %collective-permute-start.12 = (bf16[32,128]{1,0:T(8,128)(2,1)S(1)}, bf16[32,128]{1,0:T(8,128)(2,1)S(1)}, u32[]{:S(2)}, u32[]{:S(2)}) collective-permute-start(bf16[32,128]{1,0:T(8,128)(2,1)S(1)} %reduce_sum.52), channel_id=1, source_target_pairs={{0,0},{1,256},{2,16},{3,272},{4,32},{5,288},{6,48},{7,304},{8,64},... | collective-permute-start | bytes 24584 | tf_op jit(solution)/shard_map/ppermute | solution.py:311
  141.3 35.8 %copy-start.7 = (s32[256]{0:T(256)S(1)}, s32[256]{0:T(256)}, u32[]{:S(2)}) copy-start(s32[256]{0:T(256)} %param.18) | copy-start | bytes 3076
  141.3 16.4 %all-to-all-start.4 = ((bf16[32,48,128]{2,1,0:T(8,128)(2,1)}), bf16[32,48,128]{2,1,0:T(8,128)(2,1)S(1)}, u32[]{:S(2)}, u32[]{:S(2)}) async-start(bf16[32,48,128]{2,1,0:T(8,128)(2,1)} %shard_map.121), calls=%async_computation.4 | async-start | bytes 786432 | tf_op jit(solution)/shard_map/all_to_all | solution.py:320
  149.7 44.2 %copy-start.6 = (s32[256]{0:T(256)S(1)}, s32[256]{0:T(256)}, u32[]{:S(2)}) copy-start(s32[256]{0:T(256)} %param.19) | copy-start | bytes 3076
  149.7 3.3 %collective-permute-start.13 = (bf16[2,128,128]{2,1,0:T(8,128)(2,1)S(1)}, bf16[2,128,128]{2,1,0:T(8,128)(2,1)S(1)}, u32[]{:S(2)}, u32[]{:S(2)}) collective-permute-start(bf16[2,128,128]{2,1,0:T(8,128)(2,1)S(1)} %get-tuple-element.33), channel_id=1, source_target_pairs={{0,8},{8,0},{16,24},{24,16},{32,40},{40,32},{48,56},{56,48},{64,72... | collective-permute-start | bytes 196616 | tf_op jit(solution)/shard_map/ppermute | solution.py:316
  170.8 13.4 %collective-permute-start.14 = (bf16[64,512]{1,0:T(8,128)(2,1)S(1)}, bf16[64,512]{1,0:T(8,128)(2,1)S(1)}, u32[]{:S(2)}, u32[]{:S(2)}) collective-permute-start(bf16[64,512]{1,0:T(8,128)(2,1)S(1)} %reduce_sum.53), channel_id=1, source_target_pairs={{0,4},{1,5},{2,6},{3,7},{4,0},{5,1},{6,2},{7,3},{8,12},{9,13},{10,... | collective-permute-start | bytes 196616 | tf_op jit(solution)/shard_map/ppermute | solution.py:334

commit v5 on v4

--- a/solution.py
+++ b/solution.py
@@ -242,58 +242,66 @@
     )
 
 
-def gather_weights(w_in, ctx):
-    core = ctx % 2
-    halves = w_in.transpose(1, 0, 2).reshape(3, 64, 2, 128)
-    keep = lax.dynamic_index_in_dim(halves, core, 2, False)
-    got = lax.ppermute(lax.dynamic_index_in_dim(halves, 1 - core, 2, False), "ctx", PERM_CORE)
-    near = jnp.concatenate(
-        [jnp.where(core == 0, keep, got), jnp.where(core == 0, got, keep)], axis=1
-    ).reshape(384, 128)
-    far = lax.ppermute(near, "ctx", PERM_Z)
-
-    near = lax.all_to_all(
-        jnp.broadcast_to(near, (4, 384, 128)), "ctx", 0, 0, axis_index_groups=GROUPS_X, tiled=True
-    )
-    near, far = lax.optimization_barrier((near, far))
-    near = jnp.broadcast_to(near.reshape(1, 1536, 128), (4, 1536, 128))
-    near = lax.all_to_all(near, "ctx", 0, 0, axis_index_groups=GROUPS_Y, tiled=True)
-
-    along_y = jnp.stack([far] + [lax.ppermute(far, "ctx", PERM_Y[k]) for k in (1, 2, 3)])
-    fars = [along_y] + [lax.ppermute(along_y, "ctx", PERM_X[k]) for k in (1, 2, 3)]
-    return near, fars, got
-
-
-def gather_filter(long_filter, ctx):
-    core = ctx % 2
-    taps = long_filter.reshape(256, 2, 128)
-    keep = lax.dynamic_index_in_dim(taps, core, 1, False)
-    got = lax.ppermute(lax.dynamic_index_in_dim(taps, 1 - core, 1, False), "ctx", PERM_CORE)
-    taps = by_position(keep, got, core).reshape(2, 2, 128, 16, 8).transpose(3, 0, 1, 4, 2).reshape(16, 32, 128)
-    return jnp.concatenate([taps, lax.ppermute(taps, "ctx", PERM_Z_UP)], axis=1)
-
-
-def output_weights(w_out, w_unembed, near):
+def halves_of(array, axis, core):
+    keep = lax.dynamic_slice_in_dim(array, core * 128, 128, axis)
+    return keep, lax.dynamic_slice_in_dim(array, 128 - core * 128, 128, axis)
+
+
+def product(w_out, w_unembed):
     partial = mm(w_out, w_unembed).astype(BF16).reshape(4, 1, 8, 4, 128).transpose(0, 1, 3, 2, 4)
-    partial = jnp.broadcast_to(partial.reshape(4, 1, 32, 128), (4, 2, 32, 128)).reshape(8, 32, 128)
-    partial, _ = lax.optimization_barrier((partial, near))
-    partial = lax.all_to_all(partial, "tp", 0, 0, tiled=True)
-    return jnp.sum(partial.astype(F32), axis=0).astype(BF16)
+    return jnp.broadcast_to(partial.reshape(4, 1, 32, 128), (4, 2, 32, 128)).reshape(8, 32, 128)
+
+
+def filter_pieces(own, low, core):
+    keep, give = halves_of(jnp.stack([own, low]), 2, core)
+    taps = by_position(keep, lax.ppermute(give, "ctx", PERM_CORE), core)
+    return taps.reshape(2, 2, 2, 128, 16, 8).transpose(4, 1, 0, 2, 5, 3).reshape(16, 64, 128)
+
+
+def norm_kernel(tokens_ref, gain_ref, out_ref):
+    stream = tokens_ref[...].astype(F32)
+    scale = lax.rsqrt(jnp.mean(stream * stream, axis=1, keepdims=True) + NORM_EPS)
+    out_ref[...] = (stream * scale * gain_ref[...].astype(F32)).astype(BF16)
+
+
+def norm(tokens, gain):
+    return pl.pallas_call(
+        norm_kernel,
+        out_shape=shape((256, 4096), BF16),
+        grid=(4,),
+        in_specs=[pl.BlockSpec((64, 4096), lambda i: (i, 0)), pl.BlockSpec((1, 4096), lambda i: (0, 0))],
+        out_specs=pl.BlockSpec((64, 4096), lambda i: (i, 0)),
+        cost_estimate=pl.CostEstimate(flops=5 * 2**20, bytes_accessed=4 * 2**20, transcendentals=256),
+    )(tokens, gain.reshape(1, 4096))
 
 
 def per_device(tokens_in, pre_gain, w_in, w_out, long_filter, w_unembed, target_ids, score_mask):
     ctx, tp = lax.axis_index("ctx"), lax.axis_index("tp")
     core, z = ctx % 2, ctx // 32
     z_at = z.reshape(1).astype(jnp.int32)
-    near, fars, first = gather_weights(w_in, ctx)
-    tokens_in, long_filter, w_out, _ = lax.optimization_barrier((tokens_in, long_filter, w_out, first))
-    taps = gather_filter(long_filter, ctx)
-    piece = output_weights(w_out, w_unembed, near)
-
-    stream = tokens_in.astype(F32)
-    scale = lax.rsqrt(jnp.mean(stream * stream, axis=1, keepdims=True) + NORM_EPS)
-    normed = (stream * scale * pre_gain.astype(F32)).astype(BF16)
+
+    keep, give = halves_of(w_in.transpose(1, 0, 2), 2, core)
+    got = lax.ppermute(give, "ctx", PERM_CORE)
+    near = jnp.concatenate([jnp.where(core == 0, keep, got), jnp.where(core == 0, got, keep)], axis=1)
+    near = near.reshape(384, 128)
+    far = lax.ppermute(near, "ctx", PERM_Z)
+    low_taps = lax.ppermute(long_filter, "ctx", PERM_Z_UP)
+    terms = lax.all_to_all(product(w_out, w_unembed), "tp", 0, 0, tiled=True)
+    near, far, low_taps, terms, tokens_in = lax.optimization_barrier((near, far, low_taps, terms, tokens_in))
+
+    near = lax.all_to_all(
+        jnp.broadcast_to(near, (4, 384, 128)), "ctx", 0, 0, axis_index_groups=GROUPS_X, tiled=True
+    )
+    far = jnp.stack([far] + [lax.ppermute(far, "ctx", PERM_Y[k]) for k in (1, 2, 3)])
+    near, far, low_taps, terms, tokens_in = lax.optimization_barrier((near, far, low_taps, terms, tokens_in))
+
+    near = jnp.broadcast_to(near.reshape(1, 1536, 128), (4, 1536, 128))
+    near = lax.all_to_all(near, "ctx", 0, 0, axis_index_groups=GROUPS_Y, tiled=True)
+    fars = [far] + [lax.ppermute(far, "ctx", PERM_X[k]) for k in (1, 2, 3)]
+    normed = norm(tokens_in, pre_gain)
     beside = lax.ppermute(normed, "ctx", PERM_CORE)
+    piece = lax.ppermute(jnp.sum(terms.astype(F32), axis=0).astype(BF16), ("ctx", "tp"), ROUTE)
+    taps = filter_pieces(long_filter, low_taps, core)
 
     at = jnp.stack([(ctx // 8) % 4, (ctx // 2) % 4, core, z]).astype(jnp.int32)
     sums = call(
@@ -307,8 +315,6 @@
         8 * 10**8,
         (at, normed, beside, sums, taps, *fars),
     )
-    signal, piece = lax.optimization_barrier((signal, piece))
-    piece = lax.ppermute(piece, ("ctx", "tp"), ROUTE)
     got = lax.all_to_all(signal, "ctx", 0, 0, axis_index_groups=GROUPS_CORE, tiled=True)
     signal = got[:, :32].reshape(512, 128)
     before = lax.ppermute(signal, "ctx", PERM_Z_UP)
@@ -337,11 +343,13 @@
     row_top = jnp.max(logits, axis=1, keepdims=True)
     log_total = row_top[:, 0] + jnp.log(jnp.sum(jnp.exp(logits - row_top), axis=1))
     ids = lax.dynamic_slice_in_dim(target_ids, (tp % 4) * 64, 64, 0)
+    mask = lax.dynamic_slice_in_dim(score_mask, (tp % 4) * 64, 64, 0)
     vocab_index = lax.broadcasted_iota(jnp.int32, (64, 512), 1)
     picked = jnp.sum(jnp.where(vocab_index == ids[:, None], logits, 0.0), axis=1)
-    scores = jnp.broadcast_to((picked - log_total)[None, None, :], (4, 8, 64))
+    scores = (picked - log_total) * mask.astype(F32)
+    scores = jnp.broadcast_to(scores[None, :], (4, 64))
     scores = lax.all_to_all(scores, "tp", 0, 0, axis_index_groups=GROUPS_TP, tiled=True)
-    return scores[:, 0].reshape(256) * score_mask.astype(F32)
+    return scores.reshape(256)
 
 
 def solution(mesh):

time: 196 us -> 199 us (1.015)
  starting transfers between devices: 101 us -> 79.8 us
  waiting for transfers between devices: 37.8 us -> 53.7 us
  blocking collectives: 32.3 us -> 37.3 us
  Pallas kernels: 10.1 us -> 14.4 us
  other arithmetic: 6.33 us -> 3.36 us
    ppermute x11, waiting for transfers between devices: 16.3 us -> 34.6 us  [the longest x1 19.7 us: per_device(): far = lax.ppermute(near, 'ctx', PERM_Z)]
    all_to_all x3, starting transfers between devices: 23.4 us -> 14.1 us  [the longest x1 5.02 us: per_device(): terms = lax.all_to_all(product(w_out, w_unembed), 'tp', 0, 0, tiled=True)]
    ppermute x11, starting transfers between devices: 51 us -> 43.3 us  [the longest x1 15.7 us: per_device(): low_taps = lax.ppermute(long_filter, 'ctx', PERM_Z_UP)]
    ppermute x1, starting transfers between devices: 7.32 us -> 1.3 us  [per_device(): before = lax.ppermute(signal, 'ctx', PERM_Z_UP)]
    pallas_call x0 -> x1, Pallas kernels: none -> 4.34 us  [norm(): pl.pallas_call(norm_kernel, out_shape=shape((256, 4096), BF16), grid=(4,)...]
    all_to_all x1, blocking collectives: 11.8 us -> 14.6 us  [per_device(): lax.all_to_all(signal, 'ctx', 0, 0, axis_index_groups=GROUPS_CORE, tiled=...]
    ppermute x1, starting transfers between devices: 6.33 us -> 9.2 us  [per_device(): far = lax.ppermute(logits, 'tp', [(i, i ^ 4) for i in range(8)])]
    all_to_all x1, blocking collectives: 12.7 us -> 14.8 us  [per_device(): lax.all_to_all(logits.reshape(4, 64, 512), 'tp', 0, 0, axis_index_groups=...]
  transfers between devices with their start and end apart: 19 -> 19, of which waited for: 7 -> 9; matrix products, arithmetic and copies ran while one was open for 3% -> 4% of each run, Pallas kernels for 2% -> 2%
where the time goes in v5:
time: 199 us; the launch traced here: 198 us
  starting transfers between devices  79.8 us (40%)
  waiting for transfers between devices  53.7 us (27%)
  blocking collectives  37.3 us (19%)
  Pallas kernels  14.4 us (7%)
  local copies, waits for them, and re-layouts  6.95 us (3%)
  other arithmetic  3.36 us (2%)
  matrix products  2.19 us (1%)
    ppermute x1, waiting for transfers between devices, per_device(): far = lax.ppermute(near, 'ctx', PERM_Z)  19.7 us
    ppermute x1, starting transfers between devices, per_device(): low_taps = lax.ppermute(long_filter, 'ctx', PERM_Z_UP)  15.7 us
    all_to_all x1, blocking collectives, per_device(): lax.all_to_all(logits.reshape(4, 64, 512), 'tp', 0, 0, axis_index_groups=...  14.8 us
    all_to_all x1, blocking collectives, per_device(): lax.all_to_all(signal, 'ctx', 0, 0, axis_index_groups=GROUPS_CORE, tiled=...  14.6 us
    ppermute x3, starting transfers between devices, per_device(): lax.ppermute(far, 'ctx', PERM_Y[k])  10.3 us
    pallas_call x5, Pallas kernels, call(): pl.pallas_call(kernel, out_shape=outs, in_specs=specs, out_specs=jax.tree...  10.1 us
    ppermute x1, starting transfers between devices, per_device(): far = lax.ppermute(logits, 'tp', [(i, i ^ 4) for i in range(8)])  9.2 us
    ppermute x1, waiting for transfers between devices, per_device(): lax.ppermute(jnp.sum(terms.astype(F32), axis=0).astype(BF16), ('ctx', 'tp...  9.2 us
  transfers between devices with their start and end apart: 19, of which 9 were waited for; matrix products, arithmetic and copies ran while one was open for 4% of the time, Pallas kernels for 2%

profile of v5, /device:TPU:6, one launch (start us, length us, event | category | flops | bytes accessed | tf_op | source)
XLA Modules:
  0.0 198.2 jit_solution(5314691162660034529)
XLA Ops:
  0.9 1.9 collective-permute-start
  2.8 15.7 %collective-permute-start.2 = (bf16[256,256]{1,0:T(8,128)(2,1)}, bf16[256,256]{1,0:T(8,128)(2,1)S(1)}, u32[]{:S(2)}, u32[]{:S(2)}) collective-permute-start(bf16[256,256]{1,0:T(8,128)(2,1)} %param.16), channel_id=1, source_target_pairs={{0,256},{8,264},{16,272},{24,280},{32,288},{40,296},{48,304},{56,3... | collective-permute-start | bytes 393224 | tf_op jit(solution)/shard_map/ppermute | solution.py:288
  20.1 5.0 %all-to-all-start = ((bf16[8,32,128]{2,1,0:T(8,128)(2,1)}), bf16[8,32,128]{2,1,0:T(8,128)(2,1)S(1)}, u32[]{:S(2)}, u32[]{:S(2)}) async-start(bf16[8,32,128]{2,1,0:T(8,128)(2,1)} %bitcast.10), calls=%async_computation | async-start | bytes 131072 | tf_op jit(solution)/shard_map/all_to_all | solution.py:289
  26.0 1.9 collective-permute-start.1
  27.9 19.7 %collective-permute-done.1 = bf16[384,128]{1,0:T(8,128)(2,1)S(1)} collective-permute-done((bf16[384,128]{1,0:T(8,128)(2,1)S(1)}, bf16[384,128]{1,0:T(8,128)(2,1)S(1)}, u32[]{:S(2)}, u32[]{:S(2)}) %collective-permute-start.1) | collective-permute-done | bytes 98336 | tf_op jit(solution)/shard_map/ppermute | solution.py:287
  48.4 4.8 %all-to-all-start.1 = ((bf16[4,384,128]{2,1,0:T(8,128)(2,1)}), bf16[4,384,128]{2,1,0:T(8,128)(2,1)S(1)}, u32[]{:S(2)}, u32[]{:S(2)}) async-start(bf16[4,384,128]{2,1,0:T(8,128)(2,1)} %broadcast_in_dim.31), calls=%async_computation.1 | async-start | bytes 786432 | tf_op jit(solution)/shard_map/all_to_all | solution.py:292
  53.2 4.9 %collective-permute-start.5 = (bf16[384,128]{1,0:T(8,128)(2,1)S(1)}, bf16[384,128]{1,0:T(8,128)(2,1)S(1)}, u32[]{:S(2)}, u32[]{:S(2)}) collective-permute-start(bf16[384,128]{1,0:T(8,128)(2,1)S(1)} %collective-permute-done.1), channel_id=1, source_target_pairs={{0,192},{8,200},{16,208},{24,216},{32,224},{40,232},{48,240},{56,2... | collective-permute-start | bytes 294920 | tf_op jit(solution)/shard_map/ppermute | solution.py:295
  58.1 2.5 %collective-permute-start.4 = (bf16[384,128]{1,0:T(8,128)(2,1)S(1)}, bf16[384,128]{1,0:T(8,128)(2,1)S(1)}, u32[]{:S(2)}, u32[]{:S(2)}) collective-permute-start(bf16[384,128]{1,0:T(8,128)(2,1)S(1)} %collective-permute-done.1), channel_id=1, source_target_pairs={{0,128},{8,136},{16,144},{24,152},{32,160},{40,168},{48,176},{56,1... | collective-permute-start | bytes 294920 | tf_op jit(solution)/shard_map/ppermute | solution.py:295
  60.6 2.9 %collective-permute-start.3 = (bf16[384,128]{1,0:T(8,128)(2,1)S(1)}, bf16[384,128]{1,0:T(8,128)(2,1)S(1)}, u32[]{:S(2)}, u32[]{:S(2)}) collective-permute-start(bf16[384,128]{1,0:T(8,128)(2,1)S(1)} %collective-permute-done.1), channel_id=1, source_target_pairs={{0,64},{8,72},{16,80},{24,88},{32,96},{40,104},{48,112},{56,120},{... | collective-permute-start | bytes 294920 | tf_op jit(solution)/shard_map/ppermute | solution.py:295
  64.1 2.0 collective-permute-done.4
  66.1 2.3 %collective-permute-done.3 = bf16[384,128]{1,0:T(8,128)(2,1)S(1)} collective-permute-done((bf16[384,128]{1,0:T(8,128)(2,1)S(1)}, bf16[384,128]{1,0:T(8,128)(2,1)S(1)}, u32[]{:S(2)}, u32[]{:S(2)}) %collective-permute-start.3) | collective-permute-done | bytes 98336 | tf_op jit(solution)/shard_map/ppermute | solution.py:295
  68.4 4.3 %shard_map.118.own_ref = bf16[256,4096]{1,0:T(8,128)(2,1)} custom-call(bf16[256,4096]{1,0:T(8,128)(2,1)} %tokens_ref, bf16[1,4096]{1,0:T(2,128)(2,1)} %reshape.57.gain_ref), custom_call_target="tpu_custom_call" | custom-call | flops 5242880 | bytes 4194304 | tf_op jit(solution)/shard_map/pallas_call | solution.py:268
  72.8 1.9 collective-permute-start.6
  76.1 4.3 %all-to-all-start.2 = ((bf16[4,1536,128]{2,1,0:T(8,128)(2,1)}), bf16[4,1536,128]{2,1,0:T(8,128)(2,1)}, u32[]{:S(2)}, u32[]{:S(2)}) async-start(bf16[4,1536,128]{2,1,0:T(8,128)(2,1)} %broadcast_in_dim.33), calls=%async_computation.2 | async-start | bytes 3145728 | tf_op jit(solution)/shard_map/all_to_all | solution.py:299
  80.4 2.1 %collective-permute-start.8 = (bf16[4,384,128]{2,1,0:T(8,128)(2,1)S(1)}, bf16[4,384,128]{2,1,0:T(8,128)(2,1)}, u32[]{:S(2)}, u32[]{:S(2)}) collective-permute-start(bf16[4,384,128]{2,1,0:T(8,128)(2,1)S(1)} %pad_maximum_fusion.f0), channel_id=1, source_target_pairs={{0,16},{8,24},{16,32},{24,40},{32,48},{40,56},{48,0},{56,8},{64,80... | collective-permute-start | bytes 1179656 | tf_op jit(solution)/shard_map/ppermute | solution.py:300
  82.5 4.8 %collective-permute-start.9 = (bf16[4,384,128]{2,1,0:T(8,128)(2,1)S(1)}, bf16[4,384,128]{2,1,0:T(8,128)(2,1)}, u32[]{:S(2)}, u32[]{:S(2)}) collective-permute-start(bf16[4,384,128]{2,1,0:T(8,128)(2,1)S(1)} %pad_maximum_fusion.f0), channel_id=1, source_target_pairs={{0,32},{8,40},{16,48},{24,56},{32,0},{40,8},{48,16},{56,24},{64,96... | collective-permute-start | bytes 1179656 | tf_op jit(solution)/shard_map/ppermute | solution.py:300
  87.3 1.9 collective-permute-start.10
  89.3 1.9 collective-permute-start.7
  93.2 9.0 %all-to-all-done.2.near_ref = bf16[4,1536,128]{2,1,0:T(8,128)(2,1)} async-done(((bf16[4,1536,128]{2,1,0:T(8,128)(2,1)}), bf16[4,1536,128]{2,1,0:T(8,128)(2,1)}, u32[]{:S(2)}, u32[]{:S(2)}) %all-to-all-start.2) | async-done | bytes 1572896 | tf_op jit(solution)/shard_map/all_to_all | solution.py:299
  102.1 3.3 %shard_map.119.near_ref = f32[2,256,384]{2,1,0:T(8,128)S(1)} custom-call(s32[4]{0:T(128)S(1)} %pad_add_fusion.at_ref, bf16[256,4096]{1,0:T(8,128)(2,1)S(1)} %copy-done.1, bf16[256,4096]{1,0:T(8,128)(2,1)} %collective-permute-done.6.beside_ref, bf16[4,1536,128]{2,1,0:T(8,128)(2,1)} %all-to-all-done.2.near_ref), custom_call_target="tpu_custom_call" | custom-call | flops 800000000 | bytes 4194304 | tf_op jit(solution)/shard_map/pallas_call | solution.py:204
  105.9 3.3 %shard_map.120 = (bf16[16,96,128]{2,1,0:T(8,128)(2,1)S(1)}, bf16[2,2,128,128]{3,2,1,0:T(8,128)(2,1)S(1)}) custom-call(s32[4]{0:T(128)S(1)} %pad_add_fusion.at_ref, bf16[256,4096]{1,0:T(8,128)(2,1)S(1)} %copy-done.1, bf16[256,4096]{1,0:T(8,128)(2,1)} %collective-permute-done.6.beside_ref, f32[2,256,384]{2,1,0:T(8,128)S(1)} %shard_map.119.near_ref, ...), custom_call_target="tpu_custom_call" | custom-call | flops 800000000 | bytes 4194304 | tf_op jit(solution)/shard_map/pallas_call | solution.py:204
  109.2 14.6 %all_to_all.36.got_ref = bf16[16,96,128]{2,1,0:T(8,128)(2,1)S(1)} all-to-all(bf16[16,96,128]{2,1,0:T(8,128)(2,1)S(1)} %get-tuple-element.28), channel_id=1, replica_groups={{0,16,32,48,64,80,96,112,128,144,160,176,192,208,224,240},{8,24,40,56,7..., dimensions={0} | all-to-all | bytes 786432 | tf_op jit(solution)/shard_map/all_to_all | solution.py:318
  126.0 2.7 %collective-permute-start.12 = (bf16[32,128]{1,0:T(8,128)(2,1)S(1)}, bf16[32,128]{1,0:T(8,128)(2,1)S(1)}, u32[]{:S(2)}, u32[]{:S(2)}) collective-permute-start(bf16[32,128]{1,0:T(8,128)(2,1)S(1)} %reduce_sum.42), channel_id=1, source_target_pairs={{0,0},{1,256},{2,16},{3,272},{4,32},{5,288},{6,48},{7,304},{8,64},... | collective-permute-start | bytes 24584 | tf_op jit(solution)/shard_map/ppermute | solution.py:303
  130.8 9.2 %collective-permute-done.12.piece_ref = bf16[32,128]{1,0:T(8,128)(2,1)S(1)} collective-permute-done((bf16[32,128]{1,0:T(8,128)(2,1)S(1)}, bf16[32,128]{1,0:T(8,128)(2,1)S(1)}, u32[]{:S(2)}, u32[]{:S(2)}) %collective-permute-start.12) | collective-permute-done | bytes 8224 | tf_op jit(solution)/shard_map/ppermute | solution.py:303
  140.0 2.1 %shard_map.122 = bf16[32,48,128]{2,1,0:T(8,128)(2,1)} custom-call(s32[1]{0:T(128)} %bitcast.1.z_ref, bf16[512,128]{1,0:T(8,128)(2,1)S(1)} %bitcast.43, bf16[512,128]{1,0:T(8,128)(2,1)S(1)} %collective-permute-done.11.before_ref, f32[1024,256]{1,0:T(8,128)S(1)} %get-tuple-element.29.low_ref, f32[1024,256]{1,0:T(8,128)S(1)} %get-tuple-element.30.all_ref, ...), custom_call_target="tpu_custom_call" | custom-call | flops 600000000 | bytes 4194304 | tf_op jit(solution)/shard_map/pallas_call | solution.py:204
  142.1 7.9 %all-to-all-start.4 = ((bf16[32,48,128]{2,1,0:T(8,128)(2,1)}), bf16[32,48,128]{2,1,0:T(8,128)(2,1)S(1)}, u32[]{:S(2)}, u32[]{:S(2)}) async-start(bf16[32,48,128]{2,1,0:T(8,128)(2,1)} %shard_map.122), calls=%async_computation.4 | async-start | bytes 786432 | tf_op jit(solution)/shard_map/all_to_all | solution.py:326
  150.1 2.1 %collective-permute-start.13 = (bf16[2,128,128]{2,1,0:T(8,128)(2,1)S(1)}, bf16[2,128,128]{2,1,0:T(8,128)(2,1)S(1)}, u32[]{:S(2)}, u32[]{:S(2)}) collective-permute-start(bf16[2,128,128]{2,1,0:T(8,128)(2,1)S(1)} %get-tuple-element.39), channel_id=1, source_target_pairs={{0,8},{8,0},{16,24},{24,16},{32,40},{40,32},{48,56},{56,48},{64,72... | collective-permute-start | bytes 196616 | tf_op jit(solution)/shard_map/ppermute | solution.py:322
  153.4 4.7 %all-to-all-done.4.got_ref = bf16[32,48,128]{2,1,0:T(8,128)(2,1)S(1)} async-done(((bf16[32,48,128]{2,1,0:T(8,128)(2,1)}), bf16[32,48,128]{2,1,0:T(8,128)(2,1)S(1)}, u32[]{:S(2)}, u32[]{:S(2)}) %all-to-all-start.4) | async-done | bytes 393248 | tf_op jit(solution)/shard_map/all_to_all | solution.py:326
  158.4 14.8 %all_to_all.37 = bf16[4,64,512]{2,1,0:T(8,128)(2,1)S(1)} all-to-all(bf16[4,64,512]{2,1,0:T(8,128)(2,1)S(1)} %bitcast.41), channel_id=1, replica_groups={{0,1,2,3},{4,5,6,7},{8,9,10,11},{12,13,14,15},{16,17,18,19},{20,21,22,2..., dimensions={0} | all-to-all | bytes 524288 | tf_op jit(solution)/shard_map/all_to_all | solution.py:338
  173.3 9.2 %collective-permute-start.14 = (bf16[64,512]{1,0:T(8,128)(2,1)S(1)}, bf16[64,512]{1,0:T(8,128)(2,1)S(1)}, u32[]{:S(2)}, u32[]{:S(2)}) collective-permute-start(bf16[64,512]{1,0:T(8,128)(2,1)S(1)} %reduce_sum.43), channel_id=1, source_target_pairs={{0,4},{1,5},{2,6},{3,7},{4,0},{5,1},{6,2},{7,3},{8,12},{9,13},{10,... | collective-permute-start | bytes 196616 | tf_op jit(solution)/shard_map/ppermute | solution.py:340
  182.6 5.5 %collective-permute-done.14 = bf16[64,512]{1,0:T(8,128)(2,1)S(1)} collective-permute-done((bf16[64,512]{1,0:T(8,128)(2,1)S(1)}, bf16[64,512]{1,0:T(8,128)(2,1)S(1)}, u32[]{:S(2)}, u32[]{:S(2)}) %collective-permute-start.14) | collective-permute-done | bytes 65568 | tf_op jit(solution)/shard_map/ppermute | solution.py:340
  188.5 7.9 %all_to_all.38 = f32[4,1,64]{2,1,0:T(1,128)S(1)} all-to-all(f32[4,1,64]{2,1,0:T(1,128)S(1)} %broadcast_in_dim.35), channel_id=1, replica_groups={{0,1,2,3},{4,5,6,7},{8,9,10,11},{12,13,14,15},{16,17,18,19},{20,21,22,2..., dimensions={0} | all-to-all | bytes 2048 | tf_op jit(solution)/shard_map/all_to_all | solution.py:351
  (63 shorter events, 16.7 us)
Async XLA Ops:
  0.0 18.5 %copy-start = (bf16[512,512]{1,0:T(8,128)(2,1)S(1)}, bf16[512,512]{1,0:T(8,128)(2,1)}, u32[]{:S(2)}) copy-start(bf16[512,512]{1,0:T(8,128)(2,1)} %param.17) | copy-start | bytes 1572868
  0.0 63.5 %copy-start.6 = (bf16[4096]{0:T(1024)(128)(2,1)S(1)}, bf16[4096]{0:T(1024)(128)(2,1)}, u32[]{:S(2)}) copy-start(bf16[4096]{0:T(1024)(128)(2,1)} %param.13) | copy-start | bytes 24580
  0.9 24.3 %collective-permute-start = (bf16[3,64,128]{2,1,0:T(8,128)(2,1)S(1)}, bf16[3,64,128]{2,1,0:T(8,128)(2,1)S(1)}, u32[]{:S(2)}, u32[]{:S(2)}) collective-permute-start(bf16[3,64,128]{2,1,0:T(8,128)(2,1)S(1)} %dynamic-slice_bitcast_fusion.2), channel_id=1, source_target_pairs={{0,8},{8,0},{16,24},{24,16},{32,40},{40,32},{48,56},{56,48},{64,72... | collective-permute-start | bytes 147464 | tf_op jit(solution)/shard_map/ppermute | solution.py:284
  2.8 25.1 %collective-permute-start.2 = (bf16[256,256]{1,0:T(8,128)(2,1)}, bf16[256,256]{1,0:T(8,128)(2,1)S(1)}, u32[]{:S(2)}, u32[]{:S(2)}) collective-permute-start(bf16[256,256]{1,0:T(8,128)(2,1)} %param.16), channel_id=1, source_target_pairs={{0,256},{8,264},{16,272},{24,280},{32,288},{40,296},{48,304},{56,3... | collective-permute-start | bytes 393224 | tf_op jit(solution)/shard_map/ppermute | solution.py:288
  20.1 27.5 %all-to-all-start = ((bf16[8,32,128]{2,1,0:T(8,128)(2,1)}), bf16[8,32,128]{2,1,0:T(8,128)(2,1)S(1)}, u32[]{:S(2)}, u32[]{:S(2)}) async-start(bf16[8,32,128]{2,1,0:T(8,128)(2,1)} %bitcast.10), calls=%async_computation | async-start | bytes 131072 | tf_op jit(solution)/shard_map/all_to_all | solution.py:289
  26.0 21.6 %collective-permute-start.1 = (bf16[384,128]{1,0:T(8,128)(2,1)S(1)}, bf16[384,128]{1,0:T(8,128)(2,1)S(1)}, u32[]{:S(2)}, u32[]{:S(2)}) collective-permute-start(bf16[384,128]{1,0:T(8,128)(2,1)S(1)} %bitcast.45), channel_id=1, source_target_pairs={{0,256},{8,264},{16,272},{24,280},{32,288},{40,296},{48,304},{56,3... | collective-permute-start | bytes 294920 | tf_op jit(solution)/shard_map/ppermute | solution.py:287
  47.6 20.8 %copy-start.4 = (bf16[8,32,128]{2,1,0:T(8,128)(2,1)}, bf16[8,32,128]{2,1,0:T(8,128)(2,1)S(1)}, u32[]{:S(2)}) copy-start(bf16[8,32,128]{2,1,0:T(8,128)(2,1)S(1)} %all-to-all-done) | copy-start | bytes 196612
  48.4 20.0 %all-to-all-start.1 = ((bf16[4,384,128]{2,1,0:T(8,128)(2,1)}), bf16[4,384,128]{2,1,0:T(8,128)(2,1)S(1)}, u32[]{:S(2)}, u32[]{:S(2)}) async-start(bf16[4,384,128]{2,1,0:T(8,128)(2,1)} %broadcast_in_dim.31), calls=%async_computation.1 | async-start | bytes 786432 | tf_op jit(solution)/shard_map/all_to_all | solution.py:292
  53.2 11.0 %collective-permute-start.5 = (bf16[384,128]{1,0:T(8,128)(2,1)S(1)}, bf16[384,128]{1,0:T(8,128)(2,1)S(1)}, u32[]{:S(2)}, u32[]{:S(2)}) collective-permute-start(bf16[384,128]{1,0:T(8,128)(2,1)S(1)} %collective-permute-done.1), channel_id=1, source_target_pairs={{0,192},{8,200},{16,208},{24,216},{32,224},{40,232},{48,240},{56,2... | collective-permute-start | bytes 294920 | tf_op jit(solution)/shard_map/ppermute | solution.py:295
  58.1 8.0 %collective-permute-start.4 = (bf16[384,128]{1,0:T(8,128)(2,1)S(1)}, bf16[384,128]{1,0:T(8,128)(2,1)S(1)}, u32[]{:S(2)}, u32[]{:S(2)}) collective-permute-start(bf16[384,128]{1,0:T(8,128)(2,1)S(1)} %collective-permute-done.1), channel_id=1, source_target_pairs={{0,128},{8,136},{16,144},{24,152},{32,160},{40,168},{48,176},{56,1... | collective-permute-start | bytes 294920 | tf_op jit(solution)/shard_map/ppermute | solution.py:295
  60.6 7.7 %collective-permute-start.3 = (bf16[384,128]{1,0:T(8,128)(2,1)S(1)}, bf16[384,128]{1,0:T(8,128)(2,1)S(1)}, u32[]{:S(2)}, u32[]{:S(2)}) collective-permute-start(bf16[384,128]{1,0:T(8,128)(2,1)S(1)} %collective-permute-done.1), channel_id=1, source_target_pairs={{0,64},{8,72},{16,80},{24,88},{32,96},{40,104},{48,112},{56,120},{... | collective-permute-start | bytes 294920 | tf_op jit(solution)/shard_map/ppermute | solution.py:295
  72.8 29.4 %collective-permute-start.6 = (bf16[256,4096]{1,0:T(8,128)(2,1)}, bf16[256,4096]{1,0:T(8,128)(2,1)}, u32[]{:S(2)}, u32[]{:S(2)}) collective-permute-start(bf16[256,4096]{1,0:T(8,128)(2,1)} %shard_map.118.own_ref), channel_id=1, source_target_pairs={{0,8},{8,0},{16,24},{24,16},{32,40},{40,32},{48,56},{56,48},{64,72... | collective-permute-start | bytes 6291464 | tf_op jit(solution)/shard_map/ppermute | solution.py:302
  74.7 14.6 %copy-start.5 = (bf16[256,256]{1,0:T(8,128)(2,1)S(1)}, bf16[256,256]{1,0:T(8,128)(2,1)}, u32[]{:S(2)}) copy-start(bf16[256,256]{1,0:T(8,128)(2,1)} %param.16) | copy-start | bytes 393220
  76.1 26.1 %all-to-all-start.2 = ((bf16[4,1536,128]{2,1,0:T(8,128)(2,1)}), bf16[4,1536,128]{2,1,0:T(8,128)(2,1)}, u32[]{:S(2)}, u32[]{:S(2)}) async-start(bf16[4,1536,128]{2,1,0:T(8,128)(2,1)} %broadcast_in_dim.33), calls=%async_computation.2 | async-start | bytes 3145728 | tf_op jit(solution)/shard_map/all_to_all | solution.py:299
  80.4 21.7 %copy-start.1 = (bf16[256,4096]{1,0:T(8,128)(2,1)S(1)}, bf16[256,4096]{1,0:T(8,128)(2,1)}, u32[]{:S(2)}) copy-start(bf16[256,4096]{1,0:T(8,128)(2,1)} %shard_map.118.own_ref) | copy-start | bytes 6291460
  80.4 25.0 %collective-permute-start.8 = (bf16[4,384,128]{2,1,0:T(8,128)(2,1)S(1)}, bf16[4,384,128]{2,1,0:T(8,128)(2,1)}, u32[]{:S(2)}, u32[]{:S(2)}) collective-permute-start(bf16[4,384,128]{2,1,0:T(8,128)(2,1)S(1)} %pad_maximum_fusion.f0), channel_id=1, source_target_pairs={{0,16},{8,24},{16,32},{24,40},{32,48},{40,56},{48,0},{56,8},{64,80... | collective-permute-start | bytes 1179656 | tf_op jit(solution)/shard_map/ppermute | solution.py:300
  82.5 23.0 %collective-permute-start.9 = (bf16[4,384,128]{2,1,0:T(8,128)(2,1)S(1)}, bf16[4,384,128]{2,1,0:T(8,128)(2,1)}, u32[]{:S(2)}, u32[]{:S(2)}) collective-permute-start(bf16[4,384,128]{2,1,0:T(8,128)(2,1)S(1)} %pad_maximum_fusion.f0), channel_id=1, source_target_pairs={{0,32},{8,40},{16,48},{24,56},{32,0},{40,8},{48,16},{56,24},{64,96... | collective-permute-start | bytes 1179656 | tf_op jit(solution)/shard_map/ppermute | solution.py:300
  87.3 18.6 %collective-permute-start.10 = (bf16[4,384,128]{2,1,0:T(8,128)(2,1)S(1)}, bf16[4,384,128]{2,1,0:T(8,128)(2,1)}, u32[]{:S(2)}, u32[]{:S(2)}) collective-permute-start(bf16[4,384,128]{2,1,0:T(8,128)(2,1)S(1)} %pad_maximum_fusion.f0), channel_id=1, source_target_pairs={{0,48},{8,56},{16,0},{24,8},{32,16},{40,24},{48,32},{56,40},{64,11... | collective-permute-start | bytes 1179656 | tf_op jit(solution)/shard_map/ppermute | solution.py:300
  89.3 3.2 %collective-permute-start.7 = (bf16[2,256,128]{2,1,0:T(8,128)(2,1)S(1)}, bf16[2,256,128]{2,1,0:T(8,128)(2,1)S(1)}, u32[]{:S(2)}, u32[]{:S(2)}) collective-permute-start(bf16[2,256,128]{2,1,0:T(8,128)(2,1)S(1)} %get-tuple-element.36), channel_id=1, source_target_pairs={{0,8},{8,0},{16,24},{24,16},{32,40},{40,32},{48,56},{56,48},{64,72... | collective-permute-start | bytes 393224 | tf_op jit(solution)/shard_map/ppermute | solution.py:257
  105.9 22.8 %copy-start.3 = (f32[128,256]{1,0:T(8,128)S(1)}, f32[128,256]{1,0:T(8,128)}, u32[]{:S(2)}) copy-start(f32[128,256]{1,0:T(8,128)} %constant.107.clone.twiddles) | copy-start | bytes 393220
  123.9 16.1 %collective-permute-start.11 = (bf16[512,128]{1,0:T(8,128)(2,1)S(1)}, bf16[512,128]{1,0:T(8,128)(2,1)S(1)}, u32[]{:S(2)}, u32[]{:S(2)}) collective-permute-start(bf16[512,128]{1,0:T(8,128)(2,1)S(1)} %bitcast.42), channel_id=1, source_target_pairs={{0,256},{8,264},{16,272},{24,280},{32,288},{40,296},{48,304},{56,3... | collective-permute-start | bytes 393224 | tf_op jit(solution)/shard_map/ppermute | solution.py:320
  126.0 14.0 %collective-permute-start.12 = (bf16[32,128]{1,0:T(8,128)(2,1)S(1)}, bf16[32,128]{1,0:T(8,128)(2,1)S(1)}, u32[]{:S(2)}, u32[]{:S(2)}) collective-permute-start(bf16[32,128]{1,0:T(8,128)(2,1)S(1)} %reduce_sum.42), channel_id=1, source_target_pairs={{0,0},{1,256},{2,16},{3,272},{4,32},{5,288},{6,48},{7,304},{8,64},... | collective-permute-start | bytes 24584 | tf_op jit(solution)/shard_map/ppermute | solution.py:303
  128.8 1.0 copy-start.2
  142.1 40.4 %copy-start.8 = (s32[256]{0:T(256)S(1)}, s32[256]{0:T(256)}, u32[]{:S(2)}) copy-start(s32[256]{0:T(256)} %param.18) | copy-start | bytes 3076
  142.1 16.0 %all-to-all-start.4 = ((bf16[32,48,128]{2,1,0:T(8,128)(2,1)}), bf16[32,48,128]{2,1,0:T(8,128)(2,1)S(1)}, u32[]{:S(2)}, u32[]{:S(2)}) async-start(bf16[32,48,128]{2,1,0:T(8,128)(2,1)} %shard_map.122), calls=%async_computation.4 | async-start | bytes 786432 | tf_op jit(solution)/shard_map/all_to_all | solution.py:326
  150.0 38.3 %copy-start.7 = (s32[256]{0:T(256)S(1)}, s32[256]{0:T(256)}, u32[]{:S(2)}) copy-start(s32[256]{0:T(256)} %param.19) | copy-start | bytes 3076
  150.1 3.3 %collective-permute-start.13 = (bf16[2,128,128]{2,1,0:T(8,128)(2,1)S(1)}, bf16[2,128,128]{2,1,0:T(8,128)(2,1)S(1)}, u32[]{:S(2)}, u32[]{:S(2)}) collective-permute-start(bf16[2,128,128]{2,1,0:T(8,128)(2,1)S(1)} %get-tuple-element.39), channel_id=1, source_target_pairs={{0,8},{8,0},{16,24},{24,16},{32,40},{40,32},{48,56},{56,48},{64,72... | collective-permute-start | bytes 196616 | tf_op jit(solution)/shard_map/ppermute | solution.py:322
  173.3 14.8 %collective-permute-start.14 = (bf16[64,512]{1,0:T(8,128)(2,1)S(1)}, bf16[64,512]{1,0:T(8,128)(2,1)S(1)}, u32[]{:S(2)}, u32[]{:S(2)}) collective-permute-start(bf16[64,512]{1,0:T(8,128)(2,1)S(1)} %reduce_sum.43), channel_id=1, source_target_pairs={{0,4},{1,5},{2,6},{3,7},{4,0},{5,1},{6,2},{7,3},{8,12},{9,13},{10,... | collective-permute-start | bytes 196616 | tf_op jit(solution)/shard_map/ppermute | solution.py:340

commit v6 on v5

--- a/solution.py
+++ b/solution.py
@@ -142,31 +142,37 @@
     return jnp.concatenate([ref[lead, row + 128 * g : row + 128 * g + 128, :] for g in range(3)], axis=1)
 
 
-def columns(ref, start, count):
-    return ref[:, pl.ds(pl.multiple_of(start, 128), count)]
-
-
-def near_kernel(at_ref, own_ref, beside_ref, near_ref, out_ref):
+def near_kernel(at_ref, own_ref, beside_ref, gain_ref, near_ref, normed_ref, out_ref):
     start = at_ref[3] * 2048
+    gain = gain_ref[...].astype(F32)
     for part, tokens in enumerate((own_ref, beside_ref)):
+
+        @pl.loop(0, 8)
+        def _(i):
+            rows = pl.ds(pl.multiple_of(i * 32, 32), 32)
+            stream = tokens[rows, :].astype(F32)
+            scale = lax.rsqrt(jnp.mean(stream * stream, axis=1, keepdims=True) + NORM_EPS)
+            normed_ref[part, rows, :] = (stream * scale * gain).astype(BF16)
+
         total = jnp.zeros((256, 384), F32)
         for y in range(4):
             for x in (0, 2):
-                left = columns(tokens, start + (y * 4 + x) * 128, 256)
+                left = normed_ref[part, :, pl.ds(pl.multiple_of(start + (y * 4 + x) * 128, 128), 256)]
                 right = [weight_block(near_ref, y, x * 384), weight_block(near_ref, y, x * 384 + 384)]
                 total += mm(left, jnp.concatenate(right, axis=0))
         out_ref[part] = total
 
 
-def proj_kernel(at_ref, own_ref, beside_ref, near_ref, taps_ref, f0, f1, f2, f3, sig_ref, gate_ref):
+def proj_kernel(at_ref, normed_ref, near_ref, taps_ref, f0, f1, f2, f3, sig_ref, gate_ref):
     y_at, x_at, core = at_ref[0], at_ref[1], at_ref[2]
     start = 2048 - at_ref[3] * 2048
-    for part, tokens in enumerate((own_ref, beside_ref)):
+    for part in range(2):
         total = near_ref[part]
         for step, ref in enumerate((f0, f1, f2, f3)):
             x = lax.rem(x_at + 4 - step, 4)
             for k in (0, 2):
-                left = [columns(tokens, start + (lax.rem(y_at + 4 - j, 4) * 4 + x) * 128, 128) for j in (k, k + 1)]
+                starts = [start + (lax.rem(y_at + 4 - j, 4) * 4 + x) * 128 for j in (k, k + 1)]
+                left = [normed_ref[part, :, pl.ds(pl.multiple_of(at, 128), 128)] for at in starts]
                 right = [weight_block(ref, k, 0), weight_block(ref, k + 1, 0)]
                 total += mm(jnp.concatenate(left, axis=1), jnp.concatenate(right, axis=0))
         proj = total.astype(BF16).astype(F32)
@@ -258,23 +264,6 @@
     return taps.reshape(2, 2, 2, 128, 16, 8).transpose(4, 1, 0, 2, 5, 3).reshape(16, 64, 128)
 
 
-def norm_kernel(tokens_ref, gain_ref, out_ref):
-    stream = tokens_ref[...].astype(F32)
-    scale = lax.rsqrt(jnp.mean(stream * stream, axis=1, keepdims=True) + NORM_EPS)
-    out_ref[...] = (stream * scale * gain_ref[...].astype(F32)).astype(BF16)
-
-
-def norm(tokens, gain):
-    return pl.pallas_call(
-        norm_kernel,
-        out_shape=shape((256, 4096), BF16),
-        grid=(4,),
-        in_specs=[pl.BlockSpec((64, 4096), lambda i: (i, 0)), pl.BlockSpec((1, 4096), lambda i: (0, 0))],
-        out_specs=pl.BlockSpec((64, 4096), lambda i: (i, 0)),
-        cost_estimate=pl.CostEstimate(flops=5 * 2**20, bytes_accessed=4 * 2**20, transcendentals=256),
-    )(tokens, gain.reshape(1, 4096))
-
-
 def per_device(tokens_in, pre_gain, w_in, w_out, long_filter, w_unembed, target_ids, score_mask):
     ctx, tp = lax.axis_index("ctx"), lax.axis_index("tp")
     core, z = ctx % 2, ctx // 32
@@ -283,38 +272,44 @@
     keep, give = halves_of(w_in.transpose(1, 0, 2), 2, core)
     got = lax.ppermute(give, "ctx", PERM_CORE)
     near = jnp.concatenate([jnp.where(core == 0, keep, got), jnp.where(core == 0, got, keep)], axis=1)
-    near = near.reshape(384, 128)
+    near, filter_in, tokens = lax.optimization_barrier((near.reshape(384, 128), long_filter, tokens_in))
     far = lax.ppermute(near, "ctx", PERM_Z)
-    low_taps = lax.ppermute(long_filter, "ctx", PERM_Z_UP)
-    terms = lax.all_to_all(product(w_out, w_unembed), "tp", 0, 0, tiled=True)
-    near, far, low_taps, terms, tokens_in = lax.optimization_barrier((near, far, low_taps, terms, tokens_in))
-
+    low_taps = lax.ppermute(filter_in, "ctx", PERM_Z_UP)
     near = lax.all_to_all(
         jnp.broadcast_to(near, (4, 384, 128)), "ctx", 0, 0, axis_index_groups=GROUPS_X, tiled=True
     )
-    far = jnp.stack([far] + [lax.ppermute(far, "ctx", PERM_Y[k]) for k in (1, 2, 3)])
-    near, far, low_taps, terms, tokens_in = lax.optimization_barrier((near, far, low_taps, terms, tokens_in))
+    near, far, low_taps, tokens = lax.optimization_barrier((near, far, low_taps, tokens))
 
     near = jnp.broadcast_to(near.reshape(1, 1536, 128), (4, 1536, 128))
     near = lax.all_to_all(near, "ctx", 0, 0, axis_index_groups=GROUPS_Y, tiled=True)
+    far = jnp.stack([far] + [lax.ppermute(far, "ctx", PERM_Y[k]) for k in (1, 2, 3)])
+    far, tokens, low_taps = lax.optimization_barrier((far, tokens, low_taps))
+
     fars = [far] + [lax.ppermute(far, "ctx", PERM_X[k]) for k in (1, 2, 3)]
-    normed = norm(tokens_in, pre_gain)
-    beside = lax.ppermute(normed, "ctx", PERM_CORE)
-    piece = lax.ppermute(jnp.sum(terms.astype(F32), axis=0).astype(BF16), ("ctx", "tp"), ROUTE)
+    beside = lax.ppermute(tokens, "ctx", PERM_CORE)
+    terms, near, low_taps = lax.optimization_barrier((product(w_out, w_unembed), near, low_taps))
+    terms = lax.all_to_all(terms, "tp", 0, 0, tiled=True)
     taps = filter_pieces(long_filter, low_taps, core)
 
     at = jnp.stack([(ctx // 8) % 4, (ctx // 2) % 4, core, z]).astype(jnp.int32)
-    sums = call(
-        near_kernel, shape((2, 256, 384), F32), [SCALARS] + whole(3), [], 8 * 10**8, (at, normed, beside, near)
+    normed, sums = call(
+        near_kernel,
+        (shape((2, 256, 4096), BF16), shape((2, 256, 384), F32)),
+        [SCALARS] + whole(4),
+        [],
+        8 * 10**8,
+        (at, tokens_in, beside, pre_gain.reshape(1, 4096), near),
     )
     signal, gate = call(
         proj_kernel,
         (shape((16, 96, 128), BF16), shape((2, 2, 128, 128), BF16)),
-        [SCALARS] + whole(8),
+        [SCALARS] + whole(7),
         [],
         8 * 10**8,
-        (at, normed, beside, sums, taps, *fars),
-    )
+        (at, normed, sums, taps, *fars),
+    )
+    signal, terms = lax.optimization_barrier((signal, terms))
+    piece = lax.ppermute(jnp.sum(terms.astype(F32), axis=0).astype(BF16), ("ctx", "tp"), ROUTE)
     got = lax.all_to_all(signal, "ctx", 0, 0, axis_index_groups=GROUPS_CORE, tiled=True)
     signal = got[:, :32].reshape(512, 128)
     before = lax.ppermute(signal, "ctx", PERM_Z_UP)

time: 199 us -> 212 us (1.065)
  starting transfers between devices: 79.8 us -> 96.1 us
  blocking collectives: 37.3 us -> 33.6 us
  local copies, waits for them, and re-layouts: 6.95 us -> 9.96 us
  Pallas kernels: 14.4 us -> 12.2 us
    ppermute x1, starting transfers between devices: 1.3 us -> 11.7 us  [per_device(): before = lax.ppermute(signal, 'ctx', PERM_Z_UP)]
    ppermute x1, waiting for transfers between devices: 19.7 us -> 13.6 us  [per_device(): far = lax.ppermute(near, 'ctx', PERM_Z)]
    all_to_all x1, starting transfers between devices: 5.02 us -> 10 us  [per_device(): terms = lax.all_to_all(terms, 'tp', 0, 0, tiled=True)]
    all_to_all x1, starting transfers between devices: 4.77 us -> 9.28 us  [per_device(): lax.all_to_all(jnp.broadcast_to(near, (4, 384, 128)), 'ctx', 0, 0, axis_i...]
    ppermute x2, starting transfers between devices: 17.6 us -> 13.1 us  [the longest x1 11.2 us: per_device(): low_taps = lax.ppermute(filter_in, 'ctx', PERM_Z_UP)]
    pallas_call x1 -> x0, Pallas kernels: 4.34 us -> none  [norm(): pl.pallas_call(norm_kernel, out_shape=shape((256, 4096), BF16), grid=(4,)...]
    all_to_all x1, waiting for transfers between devices: 8.97 us -> 12.7 us  [per_device(): lax.all_to_all(near, 'ctx', 0, 0, axis_index_groups=GROUPS_Y, tiled=True)]
    another operation x2, local copies, waits for them, and re-layouts: 0.07 us -> 2.53 us  [by_position(): jnp.stack([own, other])]
  transfers between devices with their start and end apart: 19 -> 19, of which waited for: 9 -> 8; matrix products, arithmetic and copies ran while one was open for 4% -> 6% of each run, Pallas kernels for 2% -> 5%
where the time goes in v6:
time: 212 us; the launch traced here: 211 us
  starting transfers between devices  96.1 us (45%)
  waiting for transfers between devices  52.1 us (25%)
  blocking collectives  33.6 us (16%)
  Pallas kernels  12.2 us (6%)
  local copies, waits for them, and re-layouts  9.96 us (5%)
  other arithmetic  5.18 us (2%)
    ppermute x1, waiting for transfers between devices, per_device(): far = lax.ppermute(near, 'ctx', PERM_Z)  13.6 us
    all_to_all x1, blocking collectives, per_device(): lax.all_to_all(signal, 'ctx', 0, 0, axis_index_groups=GROUPS_CORE, tiled=...  13.1 us
    all_to_all x1, waiting for transfers between devices, per_device(): lax.all_to_all(near, 'ctx', 0, 0, axis_index_groups=GROUPS_Y, tiled=True)  12.7 us
    all_to_all x1, blocking collectives, per_device(): lax.all_to_all(logits.reshape(4, 64, 512), 'tp', 0, 0, axis_index_groups=...  12.7 us
    pallas_call x5, Pallas kernels, call(): pl.pallas_call(kernel, out_shape=outs, in_specs=specs, out_specs=jax.tree...  12.2 us
    ppermute x1, starting transfers between devices, per_device(): before = lax.ppermute(signal, 'ctx', PERM_Z_UP)  11.7 us
    ppermute x1, starting transfers between devices, per_device(): low_taps = lax.ppermute(filter_in, 'ctx', PERM_Z_UP)  11.2 us
    ppermute x3, starting transfers between devices, per_device(): lax.ppermute(far, 'ctx', PERM_Y[k])  10.3 us
  transfers between devices with their start and end apart: 19, of which 8 were waited for; matrix products, arithmetic and copies ran while one was open for 6% of the time, Pallas kernels for 5%

profile of v6, /device:TPU:6, one launch (start us, length us, event | category | flops | bytes accessed | tf_op | source)
XLA Modules:
  0.0 211.2 jit_solution(8593907492330014230)
XLA Ops:
  0.9 1.9 collective-permute-start
  5.6 9.3 %all-to-all-start = ((bf16[4,384,128]{2,1,0:T(8,128)(2,1)}), bf16[4,384,128]{2,1,0:T(8,128)(2,1)S(1)}, u32[]{:S(2)}, u32[]{:S(2)}) async-start(bf16[4,384,128]{2,1,0:T(8,128)(2,1)} %broadcast_in_dim.29), calls=%async_computation | async-start | bytes 786432 | tf_op jit(solution)/shard_map/all_to_all | solution.py:278
  14.9 11.2 %collective-permute-start.2 = (bf16[256,256]{1,0:T(8,128)(2,1)}, bf16[256,256]{1,0:T(8,128)(2,1)S(1)}, u32[]{:S(2)}, u32[]{:S(2)}) collective-permute-start(bf16[256,256]{1,0:T(8,128)(2,1)} %param.16), channel_id=1, source_target_pairs={{0,256},{8,264},{16,272},{24,280},{32,288},{40,296},{48,304},{56,3... | collective-permute-start | bytes 393224 | tf_op jit(solution)/shard_map/ppermute | solution.py:277
  26.1 1.9 collective-permute-start.1
  28.0 13.6 %collective-permute-done.1 = bf16[384,128]{1,0:T(8,128)(2,1)S(1)} collective-permute-done((bf16[384,128]{1,0:T(8,128)(2,1)S(1)}, bf16[384,128]{1,0:T(8,128)(2,1)S(1)}, u32[]{:S(2)}, u32[]{:S(2)}) %collective-permute-start.1) | collective-permute-done | bytes 98336 | tf_op jit(solution)/shard_map/ppermute | solution.py:276
  41.7 4.9 %collective-permute-start.5 = (bf16[384,128]{1,0:T(8,128)(2,1)S(1)}, bf16[384,128]{1,0:T(8,128)(2,1)S(1)}, u32[]{:S(2)}, u32[]{:S(2)}) collective-permute-start(bf16[384,128]{1,0:T(8,128)(2,1)S(1)} %collective-permute-done.1), channel_id=1, source_target_pairs={{0,192},{8,200},{16,208},{24,216},{32,224},{40,232},{48,240},{56,2... | collective-permute-start | bytes 294920 | tf_op jit(solution)/shard_map/ppermute | solution.py:285
  46.6 2.5 %collective-permute-start.4 = (bf16[384,128]{1,0:T(8,128)(2,1)S(1)}, bf16[384,128]{1,0:T(8,128)(2,1)S(1)}, u32[]{:S(2)}, u32[]{:S(2)}) collective-permute-start(bf16[384,128]{1,0:T(8,128)(2,1)S(1)} %collective-permute-done.1), channel_id=1, source_target_pairs={{0,128},{8,136},{16,144},{24,152},{32,160},{40,168},{48,176},{56,1... | collective-permute-start | bytes 294920 | tf_op jit(solution)/shard_map/ppermute | solution.py:285
  49.1 2.9 %collective-permute-start.3 = (bf16[384,128]{1,0:T(8,128)(2,1)S(1)}, bf16[384,128]{1,0:T(8,128)(2,1)S(1)}, u32[]{:S(2)}, u32[]{:S(2)}) collective-permute-start(bf16[384,128]{1,0:T(8,128)(2,1)S(1)} %collective-permute-done.1), channel_id=1, source_target_pairs={{0,64},{8,72},{16,80},{24,88},{32,96},{40,104},{48,112},{56,120},{... | collective-permute-start | bytes 294920 | tf_op jit(solution)/shard_map/ppermute | solution.py:285
  52.0 2.6 %collective-permute-done.4 = bf16[384,128]{1,0:T(8,128)(2,1)S(1)} collective-permute-done((bf16[384,128]{1,0:T(8,128)(2,1)S(1)}, bf16[384,128]{1,0:T(8,128)(2,1)S(1)}, u32[]{:S(2)}, u32[]{:S(2)}) %collective-permute-start.4) | collective-permute-done | bytes 98336 | tf_op jit(solution)/shard_map/ppermute | solution.py:285
  54.6 2.3 %collective-permute-done.3 = bf16[384,128]{1,0:T(8,128)(2,1)S(1)} collective-permute-done((bf16[384,128]{1,0:T(8,128)(2,1)S(1)}, bf16[384,128]{1,0:T(8,128)(2,1)S(1)}, u32[]{:S(2)}, u32[]{:S(2)}) %collective-permute-start.3) | collective-permute-done | bytes 98336 | tf_op jit(solution)/shard_map/ppermute | solution.py:285
  56.9 1.9 collective-permute-start.6
  60.2 3.7 %all-to-all-start.1 = ((bf16[4,1536,128]{2,1,0:T(8,128)(2,1)}), bf16[4,1536,128]{2,1,0:T(8,128)(2,1)S(1)}, u32[]{:S(2)}, u32[]{:S(2)}) async-start(bf16[4,1536,128]{2,1,0:T(8,128)(2,1)} %broadcast_in_dim.33), calls=%async_computation.1 | async-start | bytes 3145728 | tf_op jit(solution)/shard_map/all_to_all | solution.py:284
  64.1 1.9 collective-permute-start.8
  66.0 4.8 %collective-permute-start.9 = (bf16[4,384,128]{2,1,0:T(8,128)(2,1)S(1)}, bf16[4,384,128]{2,1,0:T(8,128)(2,1)S(1)}, u32[]{:S(2)}, u32[]{:S(2)}) collective-permute-start(bf16[4,384,128]{2,1,0:T(8,128)(2,1)S(1)} %pad_maximum_fusion.f0), channel_id=1, source_target_pairs={{0,32},{8,40},{16,48},{24,56},{32,0},{40,8},{48,16},{56,24},{64,96... | collective-permute-start | bytes 1179656 | tf_op jit(solution)/shard_map/ppermute | solution.py:288
  70.9 1.9 collective-permute-start.10
  72.8 12.7 %all-to-all-done.1.near_ref = bf16[4,1536,128]{2,1,0:T(8,128)(2,1)S(1)} async-done(((bf16[4,1536,128]{2,1,0:T(8,128)(2,1)}), bf16[4,1536,128]{2,1,0:T(8,128)(2,1)S(1)}, u32[]{:S(2)}, u32[]{:S(2)}) %all-to-all-start.1) | async-done | bytes 1572896 | tf_op jit(solution)/shard_map/all_to_all | solution.py:284
  87.8 1.9 collective-permute-start.7
  91.6 10.0 %all-to-all-start.2 = ((bf16[8,32,128]{2,1,0:T(8,128)(2,1)}), bf16[8,32,128]{2,1,0:T(8,128)(2,1)S(1)}, u32[]{:S(2)}, u32[]{:S(2)}) async-start(bf16[8,32,128]{2,1,0:T(8,128)(2,1)} %bitcast.14), calls=%async_computation.2 | async-start | bytes 131072 | tf_op jit(solution)/shard_map/all_to_all | solution.py:291
  106.4 6.4 %shard_map.118 = (bf16[2,256,4096]{2,1,0:T(8,128)(2,1)S(1)}, f32[2,256,384]{2,1,0:T(8,128)S(1)}) custom-call(s32[4]{0:T(128)S(1)} %pad_add_fusion.at_ref, bf16[256,4096]{1,0:T(8,128)(2,1)} %own_ref.1, bf16[256,4096]{1,0:T(8,128)(2,1)} %collective-permute-done.6.beside_ref, bf16[1,4096]{1,0:T(2,128)(2,1)S(1)} %reshape.55.gain_ref, ...), custom_call_target="tpu_custom_call" | custom-call | flops 800000000 | bytes 4194304 | tf_op jit(solution)/shard_map/pallas_call | solution.py:210
  112.8 2.4 %shard_map.119 = (bf16[16,96,128]{2,1,0:T(8,128)(2,1)S(1)}, bf16[2,2,128,128]{3,2,1,0:T(8,128)(2,1)S(1)}) custom-call(s32[4]{0:T(128)S(1)} %pad_add_fusion.at_ref, bf16[2,256,4096]{2,1,0:T(8,128)(2,1)S(1)} %get-tuple-element.36.normed_ref, f32[2,256,384]{2,1,0:T(8,128)S(1)} %get-tuple-element.37.near_ref, bf16[16,64,128]{2,1,0:T(8,128)(2,1)S(1)} %bitcast.40, ...), custom_call_target="tpu_custom_call" | custom-call | flops 800000000 | bytes 4194304 | tf_op jit(solution)/shard_map/pallas_call | solution.py:210
  115.3 13.1 %all_to_all.36.got_ref = bf16[16,96,128]{2,1,0:T(8,128)(2,1)S(1)} all-to-all(bf16[16,96,128]{2,1,0:T(8,128)(2,1)S(1)} %get-tuple-element.42), channel_id=1, replica_groups={{0,16,32,48,64,80,96,112,128,144,160,176,192,208,224,240},{8,24,40,56,7..., dimensions={0} | all-to-all | bytes 786432 | tf_op jit(solution)/shard_map/all_to_all | solution.py:313
  128.4 11.7 %collective-permute-start.11 = (bf16[512,128]{1,0:T(8,128)(2,1)S(1)}, bf16[512,128]{1,0:T(8,128)(2,1)S(1)}, u32[]{:S(2)}, u32[]{:S(2)}) collective-permute-start(bf16[512,128]{1,0:T(8,128)(2,1)S(1)} %bitcast.42), channel_id=1, source_target_pairs={{0,256},{8,264},{16,272},{24,280},{32,288},{40,296},{48,304},{56,3... | collective-permute-start | bytes 393224 | tf_op jit(solution)/shard_map/ppermute | solution.py:315
  140.2 3.1 %collective-permute-start.12 = (bf16[32,128]{1,0:T(8,128)(2,1)S(1)}, bf16[32,128]{1,0:T(8,128)(2,1)S(1)}, u32[]{:S(2)}, u32[]{:S(2)}) collective-permute-start(bf16[32,128]{1,0:T(8,128)(2,1)S(1)} %reduce_sum.42), channel_id=1, source_target_pairs={{0,0},{1,256},{2,16},{3,272},{4,32},{5,288},{6,48},{7,304},{8,64},... | collective-permute-start | bytes 24584 | tf_op jit(solution)/shard_map/ppermute | solution.py:312
  144.3 9.6 %collective-permute-done.12.piece_ref = bf16[32,128]{1,0:T(8,128)(2,1)S(1)} collective-permute-done((bf16[32,128]{1,0:T(8,128)(2,1)S(1)}, bf16[32,128]{1,0:T(8,128)(2,1)S(1)}, u32[]{:S(2)}, u32[]{:S(2)}) %collective-permute-start.12) | collective-permute-done | bytes 8224 | tf_op jit(solution)/shard_map/ppermute | solution.py:312
  154.0 2.0 shard_map.121
  156.0 8.1 %all-to-all-start.4 = ((bf16[32,48,128]{2,1,0:T(8,128)(2,1)}), bf16[32,48,128]{2,1,0:T(8,128)(2,1)S(1)}, u32[]{:S(2)}, u32[]{:S(2)}) async-start(bf16[32,48,128]{2,1,0:T(8,128)(2,1)} %shard_map.121), calls=%async_computation.4 | async-start | bytes 786432 | tf_op jit(solution)/shard_map/all_to_all | solution.py:321
  164.1 2.1 collective-permute-start.13
  167.5 4.7 %all-to-all-done.4.got_ref = bf16[32,48,128]{2,1,0:T(8,128)(2,1)S(1)} async-done(((bf16[32,48,128]{2,1,0:T(8,128)(2,1)}), bf16[32,48,128]{2,1,0:T(8,128)(2,1)S(1)}, u32[]{:S(2)}, u32[]{:S(2)}) %all-to-all-start.4) | async-done | bytes 393248 | tf_op jit(solution)/shard_map/all_to_all | solution.py:321
  172.5 12.7 %all_to_all.37 = bf16[4,64,512]{2,1,0:T(8,128)(2,1)S(1)} all-to-all(bf16[4,64,512]{2,1,0:T(8,128)(2,1)S(1)} %bitcast.41), channel_id=1, replica_groups={{0,1,2,3},{4,5,6,7},{8,9,10,11},{12,13,14,15},{16,17,18,19},{20,21,22,2..., dimensions={0} | all-to-all | bytes 524288 | tf_op jit(solution)/shard_map/all_to_all | solution.py:333
  185.2 10.3 %collective-permute-start.14 = (bf16[64,512]{1,0:T(8,128)(2,1)S(1)}, bf16[64,512]{1,0:T(8,128)(2,1)S(1)}, u32[]{:S(2)}, u32[]{:S(2)}) collective-permute-start(bf16[64,512]{1,0:T(8,128)(2,1)S(1)} %reduce_sum.43), channel_id=1, source_target_pairs={{0,4},{1,5},{2,6},{3,7},{4,0},{5,1},{6,2},{7,3},{8,12},{9,13},{10,... | collective-permute-start | bytes 196616 | tf_op jit(solution)/shard_map/ppermute | solution.py:335
  195.6 5.5 %collective-permute-done.14 = bf16[64,512]{1,0:T(8,128)(2,1)S(1)} collective-permute-done((bf16[64,512]{1,0:T(8,128)(2,1)S(1)}, bf16[64,512]{1,0:T(8,128)(2,1)S(1)}, u32[]{:S(2)}, u32[]{:S(2)}) %collective-permute-start.14) | collective-permute-done | bytes 65568 | tf_op jit(solution)/shard_map/ppermute | solution.py:335
  201.5 7.9 %all_to_all.38 = f32[4,1,64]{2,1,0:T(1,128)S(1)} all-to-all(f32[4,1,64]{2,1,0:T(1,128)S(1)} %broadcast_in_dim.35), channel_id=1, replica_groups={{0,1,2,3},{4,5,6,7},{8,9,10,11},{12,13,14,15},{16,17,18,19},{20,21,22,2..., dimensions={0} | all-to-all | bytes 2048 | tf_op jit(solution)/shard_map/all_to_all | solution.py:346
  (60 shorter events, 19.1 us)
Async XLA Ops:
  0.0 63.9 %copy-start = (bf16[512,512]{1,0:T(8,128)(2,1)S(1)}, bf16[512,512]{1,0:T(8,128)(2,1)}, u32[]{:S(2)}) copy-start(bf16[512,512]{1,0:T(8,128)(2,1)} %param.17) | copy-start | bytes 1572868
  0.9 3.1 %collective-permute-start = (bf16[3,64,128]{2,1,0:T(8,128)(2,1)S(1)}, bf16[3,64,128]{2,1,0:T(8,128)(2,1)S(1)}, u32[]{:S(2)}, u32[]{:S(2)}) collective-permute-start(bf16[3,64,128]{2,1,0:T(8,128)(2,1)S(1)} %dynamic-slice_bitcast_fusion.2), channel_id=1, source_target_pairs={{0,8},{8,0},{16,24},{24,16},{32,40},{40,32},{48,56},{56,48},{64,72... | collective-permute-start | bytes 147464 | tf_op jit(solution)/shard_map/ppermute | solution.py:273
  5.6 36.0 %all-to-all-start = ((bf16[4,384,128]{2,1,0:T(8,128)(2,1)}), bf16[4,384,128]{2,1,0:T(8,128)(2,1)S(1)}, u32[]{:S(2)}, u32[]{:S(2)}) async-start(bf16[4,384,128]{2,1,0:T(8,128)(2,1)} %broadcast_in_dim.29), calls=%async_computation | async-start | bytes 786432 | tf_op jit(solution)/shard_map/all_to_all | solution.py:278
  14.9 26.7 %collective-permute-start.2 = (bf16[256,256]{1,0:T(8,128)(2,1)}, bf16[256,256]{1,0:T(8,128)(2,1)S(1)}, u32[]{:S(2)}, u32[]{:S(2)}) collective-permute-start(bf16[256,256]{1,0:T(8,128)(2,1)} %param.16), channel_id=1, source_target_pairs={{0,256},{8,264},{16,272},{24,280},{32,288},{40,296},{48,304},{56,3... | collective-permute-start | bytes 393224 | tf_op jit(solution)/shard_map/ppermute | solution.py:277
  26.1 15.5 %collective-permute-start.1 = (bf16[384,128]{1,0:T(8,128)(2,1)S(1)}, bf16[384,128]{1,0:T(8,128)(2,1)S(1)}, u32[]{:S(2)}, u32[]{:S(2)}) collective-permute-start(bf16[384,128]{1,0:T(8,128)(2,1)S(1)} %bitcast.46), channel_id=1, source_target_pairs={{0,256},{8,264},{16,272},{24,280},{32,288},{40,296},{48,304},{56,3... | collective-permute-start | bytes 294920 | tf_op jit(solution)/shard_map/ppermute | solution.py:276
  41.6 18.6 %copy-start.3 = (bf16[256,256]{1,0:T(8,128)(2,1)}, bf16[256,256]{1,0:T(8,128)(2,1)S(1)}, u32[]{:S(2)}) copy-start(bf16[256,256]{1,0:T(8,128)(2,1)S(1)} %collective-permute-done.2) | copy-start | bytes 393220
  41.7 10.4 %collective-permute-start.5 = (bf16[384,128]{1,0:T(8,128)(2,1)S(1)}, bf16[384,128]{1,0:T(8,128)(2,1)S(1)}, u32[]{:S(2)}, u32[]{:S(2)}) collective-permute-start(bf16[384,128]{1,0:T(8,128)(2,1)S(1)} %collective-permute-done.1), channel_id=1, source_target_pairs={{0,192},{8,200},{16,208},{24,216},{32,224},{40,232},{48,240},{56,2... | collective-permute-start | bytes 294920 | tf_op jit(solution)/shard_map/ppermute | solution.py:285
  46.6 8.0 %collective-permute-start.4 = (bf16[384,128]{1,0:T(8,128)(2,1)S(1)}, bf16[384,128]{1,0:T(8,128)(2,1)S(1)}, u32[]{:S(2)}, u32[]{:S(2)}) collective-permute-start(bf16[384,128]{1,0:T(8,128)(2,1)S(1)} %collective-permute-done.1), channel_id=1, source_target_pairs={{0,128},{8,136},{16,144},{24,152},{32,160},{40,168},{48,176},{56,1... | collective-permute-start | bytes 294920 | tf_op jit(solution)/shard_map/ppermute | solution.py:285
  49.1 7.7 %collective-permute-start.3 = (bf16[384,128]{1,0:T(8,128)(2,1)S(1)}, bf16[384,128]{1,0:T(8,128)(2,1)S(1)}, u32[]{:S(2)}, u32[]{:S(2)}) collective-permute-start(bf16[384,128]{1,0:T(8,128)(2,1)S(1)} %collective-permute-done.1), channel_id=1, source_target_pairs={{0,64},{8,72},{16,80},{24,88},{32,96},{40,104},{48,112},{56,120},{... | collective-permute-start | bytes 294920 | tf_op jit(solution)/shard_map/ppermute | solution.py:285
  56.9 49.5 %collective-permute-start.6 = (bf16[256,4096]{1,0:T(8,128)(2,1)}, bf16[256,4096]{1,0:T(8,128)(2,1)}, u32[]{:S(2)}, u32[]{:S(2)}) collective-permute-start(bf16[256,4096]{1,0:T(8,128)(2,1)} %own_ref.1), channel_id=1, source_target_pairs={{0,8},{8,0},{16,24},{24,16},{32,40},{40,32},{48,56},{56,48},{64,72... | collective-permute-start | bytes 6291464 | tf_op jit(solution)/shard_map/ppermute | solution.py:289
  58.8 5.1 %copy-start.4 = (bf16[32,512]{1,0:T(8,128)(2,1)S(1)}, bf16[32,512]{1,0:T(8,128)(2,1)}, u32[]{:S(2)}) copy-start(bf16[32,512]{1,0:T(8,128)(2,1)} %param.15) | copy-start | bytes 98308
  60.2 29.5 %copy-start.5 = (bf16[4096]{0:T(1024)(128)(2,1)S(1)}, bf16[4096]{0:T(1024)(128)(2,1)}, u32[]{:S(2)}) copy-start(bf16[4096]{0:T(1024)(128)(2,1)} %param.13) | copy-start | bytes 24580
  60.2 25.3 %all-to-all-start.1 = ((bf16[4,1536,128]{2,1,0:T(8,128)(2,1)}), bf16[4,1536,128]{2,1,0:T(8,128)(2,1)S(1)}, u32[]{:S(2)}, u32[]{:S(2)}) async-start(bf16[4,1536,128]{2,1,0:T(8,128)(2,1)} %broadcast_in_dim.33), calls=%async_computation.1 | async-start | bytes 3145728 | tf_op jit(solution)/shard_map/all_to_all | solution.py:284
  64.1 48.7 %collective-permute-start.8 = (bf16[4,384,128]{2,1,0:T(8,128)(2,1)S(1)}, bf16[4,384,128]{2,1,0:T(8,128)(2,1)S(1)}, u32[]{:S(2)}, u32[]{:S(2)}) collective-permute-start(bf16[4,384,128]{2,1,0:T(8,128)(2,1)S(1)} %pad_maximum_fusion.f0), channel_id=1, source_target_pairs={{0,16},{8,24},{16,32},{24,40},{32,48},{40,56},{48,0},{56,8},{64,80... | collective-permute-start | bytes 1179656 | tf_op jit(solution)/shard_map/ppermute | solution.py:288
  66.0 46.8 %collective-permute-start.9 = (bf16[4,384,128]{2,1,0:T(8,128)(2,1)S(1)}, bf16[4,384,128]{2,1,0:T(8,128)(2,1)S(1)}, u32[]{:S(2)}, u32[]{:S(2)}) collective-permute-start(bf16[4,384,128]{2,1,0:T(8,128)(2,1)S(1)} %pad_maximum_fusion.f0), channel_id=1, source_target_pairs={{0,32},{8,40},{16,48},{24,56},{32,0},{40,8},{48,16},{56,24},{64,96... | collective-permute-start | bytes 1179656 | tf_op jit(solution)/shard_map/ppermute | solution.py:288
  70.9 41.9 %collective-permute-start.10 = (bf16[4,384,128]{2,1,0:T(8,128)(2,1)S(1)}, bf16[4,384,128]{2,1,0:T(8,128)(2,1)}, u32[]{:S(2)}, u32[]{:S(2)}) collective-permute-start(bf16[4,384,128]{2,1,0:T(8,128)(2,1)S(1)} %pad_maximum_fusion.f0), channel_id=1, source_target_pairs={{0,48},{8,56},{16,0},{24,8},{32,16},{40,24},{48,32},{56,40},{64,11... | collective-permute-start | bytes 1179656 | tf_op jit(solution)/shard_map/ppermute | solution.py:288
  87.8 13.8 %collective-permute-start.7 = (bf16[2,256,128]{2,1,0:T(8,128)(2,1)}, bf16[2,256,128]{2,1,0:T(8,128)(2,1)}, u32[]{:S(2)}, u32[]{:S(2)}) collective-permute-start(bf16[2,256,128]{2,1,0:T(8,128)(2,1)} %get-tuple-element.50), channel_id=1, source_target_pairs={{0,8},{8,0},{16,24},{24,16},{32,40},{40,32},{48,56},{56,48},{64,72... | collective-permute-start | bytes 393224 | tf_op jit(solution)/shard_map/ppermute | solution.py:263
  91.6 23.7 %all-to-all-start.2 = ((bf16[8,32,128]{2,1,0:T(8,128)(2,1)}), bf16[8,32,128]{2,1,0:T(8,128)(2,1)S(1)}, u32[]{:S(2)}, u32[]{:S(2)}) async-start(bf16[8,32,128]{2,1,0:T(8,128)(2,1)} %bitcast.14), calls=%async_computation.2 | async-start | bytes 131072 | tf_op jit(solution)/shard_map/all_to_all | solution.py:291
  112.8 30.5 %copy-start.1 = (bf16[832,256]{1,0:T(8,128)(2,1)S(1)}, bf16[832,256]{1,0:T(8,128)(2,1)}, u32[]{:S(2)}) copy-start(bf16[832,256]{1,0:T(8,128)(2,1)} %constant.106.clone.matrices) | copy-start | bytes 1277956
  112.8 30.5 %copy-start.2 = (f32[128,256]{1,0:T(8,128)S(1)}, f32[128,256]{1,0:T(8,128)}, u32[]{:S(2)}) copy-start(f32[128,256]{1,0:T(8,128)} %constant.107.clone.twiddles) | copy-start | bytes 393220
  128.4 25.6 %collective-permute-start.11 = (bf16[512,128]{1,0:T(8,128)(2,1)S(1)}, bf16[512,128]{1,0:T(8,128)(2,1)S(1)}, u32[]{:S(2)}, u32[]{:S(2)}) collective-permute-start(bf16[512,128]{1,0:T(8,128)(2,1)S(1)} %bitcast.42), channel_id=1, source_target_pairs={{0,256},{8,264},{16,272},{24,280},{32,288},{40,296},{48,304},{56,3... | collective-permute-start | bytes 393224 | tf_op jit(solution)/shard_map/ppermute | solution.py:315
  140.2 13.8 %collective-permute-start.12 = (bf16[32,128]{1,0:T(8,128)(2,1)S(1)}, bf16[32,128]{1,0:T(8,128)(2,1)S(1)}, u32[]{:S(2)}, u32[]{:S(2)}) collective-permute-start(bf16[32,128]{1,0:T(8,128)(2,1)S(1)} %reduce_sum.42), channel_id=1, source_target_pairs={{0,0},{1,256},{2,16},{3,272},{4,32},{5,288},{6,48},{7,304},{8,64},... | collective-permute-start | bytes 24584 | tf_op jit(solution)/shard_map/ppermute | solution.py:312
  156.0 39.5 %copy-start.7 = (s32[256]{0:T(256)S(1)}, s32[256]{0:T(256)}, u32[]{:S(2)}) copy-start(s32[256]{0:T(256)} %param.18) | copy-start | bytes 3076
  156.0 16.1 %all-to-all-start.4 = ((bf16[32,48,128]{2,1,0:T(8,128)(2,1)}), bf16[32,48,128]{2,1,0:T(8,128)(2,1)S(1)}, u32[]{:S(2)}, u32[]{:S(2)}) async-start(bf16[32,48,128]{2,1,0:T(8,128)(2,1)} %shard_map.121), calls=%async_computation.4 | async-start | bytes 786432 | tf_op jit(solution)/shard_map/all_to_all | solution.py:321
  164.1 37.3 %copy-start.6 = (s32[256]{0:T(256)S(1)}, s32[256]{0:T(256)}, u32[]{:S(2)}) copy-start(s32[256]{0:T(256)} %param.19) | copy-start | bytes 3076
  164.1 3.3 %collective-permute-start.13 = (bf16[2,128,128]{2,1,0:T(8,128)(2,1)S(1)}, bf16[2,128,128]{2,1,0:T(8,128)(2,1)S(1)}, u32[]{:S(2)}, u32[]{:S(2)}) collective-permute-start(bf16[2,128,128]{2,1,0:T(8,128)(2,1)S(1)} %get-tuple-element.53), channel_id=1, source_target_pairs={{0,8},{8,0},{16,24},{24,16},{32,40},{40,32},{48,56},{56,48},{64,72... | collective-permute-start | bytes 196616 | tf_op jit(solution)/shard_map/ppermute | solution.py:317
  185.2 15.9 %collective-permute-start.14 = (bf16[64,512]{1,0:T(8,128)(2,1)S(1)}, bf16[64,512]{1,0:T(8,128)(2,1)S(1)}, u32[]{:S(2)}, u32[]{:S(2)}) collective-permute-start(bf16[64,512]{1,0:T(8,128)(2,1)S(1)} %reduce_sum.43), channel_id=1, source_target_pairs={{0,4},{1,5},{2,6},{3,7},{4,0},{5,1},{6,2},{7,3},{8,12},{9,13},{10,... | collective-permute-start | bytes 196616 | tf_op jit(solution)/shard_map/ppermute | solution.py:335

commit v7 on v6

--- a/solution.py
+++ b/solution.py
@@ -95,26 +95,28 @@
     return mm(jnp.concatenate(parts, axis=0), matrices[256:512, :])
 
 
-def filter_kernel(z_ref, got_ref, matrices, twiddles, low_ref, all_ref, scratch):
+def rows_of(scratch, ref, at):
+    for p in range(16):
+        scratch[p * 32 : p * 32 + 32] = ref[p, at : at + 32].astype(F32)
+
+
+def spectra_kernel(got_ref, matrices, twiddles, signal_ref, filter_ref, scratch):
+    rows_of(scratch, got_ref, 0)
+    signal_ref[...] = spectrum(scratch, matrices, twiddles)
+    rows_of(scratch, got_ref, 32)
+    filter_ref[...] = spectrum(scratch, matrices, twiddles)
+
+
+def conv_kernel(z_ref, signal_ref, filter_ref, before_ref, piece_ref, matrices, twiddles, out_ref, scratch):
     upper = z_ref[0] == 1
-    for p in range(16):
-        scratch[p * 32 : p * 32 + 32] = got_ref[p, 32:64].astype(F32)
-    high = spectrum(scratch, matrices, twiddles)
-    for p in range(16):
-        scratch[p * 32 : p * 32 + 32] = jnp.where(upper, got_ref[p, 64:].astype(F32), got_ref[p, 32:64].astype(F32))
-    low = spectrum(scratch, matrices, twiddles)
+    cos_tw, sin_tw = twiddles[:, :128], twiddles[:, 128:]
+    own, high = signal_ref[...], filter_ref[...]
+    rows_of(scratch, before_ref, 0)
+    old = jnp.where(upper, spectrum(scratch, matrices, twiddles), 0.0)
+    rows_of(scratch, before_ref, 32)
+    low = jnp.where(upper, spectrum(scratch, matrices, twiddles), high)
     odd = lax.broadcasted_iota(jnp.int32, (1024, 256), 0) & 1
-    low_ref[...] = low
-    all_ref[...] = jnp.where(odd == 1, -low, low) + high
-
-
-def conv_kernel(z_ref, sig_ref, before_ref, low_ref, all_ref, piece_ref, matrices, twiddles, out_ref, scratch):
-    cos_tw, sin_tw = twiddles[:, :128], twiddles[:, 128:]
-    scratch[...] = sig_ref[...].astype(F32)
-    own = spectrum(scratch, matrices, twiddles)
-    scratch[...] = jnp.where(z_ref[0] == 1, before_ref[...].astype(F32), 0.0)
-    old = spectrum(scratch, matrices, twiddles)
-    low, every = low_ref[...], all_ref[...]
+    every = jnp.where(odd == 1, -low, low) + high
     own_r, own_i, old_r, old_i = own[:, :128], own[:, 128:], old[:, :128], old[:, 128:]
     low_r, low_i, all_r, all_i = low[:, :128], low[:, 128:], every[:, :128], every[:, 128:]
     real = own_r * low_r - own_i * low_i + old_r * all_r - old_i * all_i
@@ -163,7 +165,14 @@
         out_ref[part] = total
 
 
-def proj_kernel(at_ref, normed_ref, near_ref, taps_ref, f0, f1, f2, f3, sig_ref, gate_ref):
+def put_pieces(ref, row, place, block):
+    first, second = block[:128].T, block[128:].T
+    for p in range(16):
+        rows = jnp.concatenate([first[p * 8 : p * 8 + 8], second[p * 8 : p * 8 + 8]], axis=0).astype(BF16)
+        ref[p, pl.ds(pl.multiple_of(row + place * 16, 16), 16), :] = rows
+
+
+def proj_kernel(at_ref, normed_ref, near_ref, keep_ref, got_ref, f0, f1, f2, f3, sig_ref, gate_ref):
     y_at, x_at, core = at_ref[0], at_ref[1], at_ref[2]
     start = 2048 - at_ref[3] * 2048
     for part in range(2):
@@ -176,16 +185,11 @@
                 right = [weight_block(ref, k, 0), weight_block(ref, k + 1, 0)]
                 total += mm(jnp.concatenate(left, axis=1), jnp.concatenate(right, axis=0))
         proj = total.astype(BF16).astype(F32)
-        gated = proj[:, 128:256] * proj[:, 256:]
         place = core if part == 0 else 1 - core
-        first, second = gated[:128].T, gated[128:].T
-        for p in range(16):
-            rows = jnp.concatenate([first[p * 8 : p * 8 + 8], second[p * 8 : p * 8 + 8]], axis=0).astype(BF16)
-            sig_ref[p, pl.ds(pl.multiple_of(place * 16, 16), 16), :] = rows
+        put_pieces(sig_ref, 0, place, proj[:, 128:256] * proj[:, 256:])
+        put_pieces(sig_ref, 32, place, (keep_ref if part == 0 else got_ref)[...].astype(F32))
         gate_ref[place, 0] = proj[:128, :128].T.astype(BF16)
         gate_ref[place, 1] = proj[128:, :128].T.astype(BF16)
-    for p in range(16):
-        sig_ref[p, 32:, :] = taps_ref[p]
 
 
 def mix_kernel(core_ref, got_ref, keep_ref, other_ref, base_ref, out_ref):
@@ -226,25 +230,25 @@
     return jnp.where(place == 0, jnp.stack([own, other]), jnp.stack([other, own]))
 
 
-def filter_spectra(z, got):
+def spectra(got):
     return call(
-        filter_kernel,
+        spectra_kernel,
         (shape((1024, 256), F32), shape((1024, 256), F32)),
-        [SCALARS] + whole(3),
+        whole(3),
         [pltpu.VMEM((512, 128), F32)],
         4 * 10**8,
-        (z, got, jnp.asarray(MATRICES, BF16), jnp.asarray(TWIDDLES, F32)),
-    )
-
-
-def convolve(z, signal, before, low, every, piece):
+        (got, jnp.asarray(MATRICES, BF16), jnp.asarray(TWIDDLES, F32)),
+    )
+
+
+def convolve(z, signal, taps, before, piece):
     return call(
         conv_kernel,
         shape((32, 48, 128), BF16),
-        [SCALARS] + whole(7),
+        [SCALARS] + whole(6),
         [pltpu.VMEM((512, 128), F32)],
         6 * 10**8,
-        (z, signal, before, low, every, piece, jnp.asarray(MATRICES, BF16), jnp.asarray(TWIDDLES, F32)),
+        (z, signal, taps, before, piece, jnp.asarray(MATRICES, BF16), jnp.asarray(TWIDDLES, F32)),
     )
 
 
@@ -256,12 +260,6 @@
 def product(w_out, w_unembed):
     partial = mm(w_out, w_unembed).astype(BF16).reshape(4, 1, 8, 4, 128).transpose(0, 1, 3, 2, 4)
     return jnp.broadcast_to(partial.reshape(4, 1, 32, 128), (4, 2, 32, 128)).reshape(8, 32, 128)
-
-
-def filter_pieces(own, low, core):
-    keep, give = halves_of(jnp.stack([own, low]), 2, core)
-    taps = by_position(keep, lax.ppermute(give, "ctx", PERM_CORE), core)
-    return taps.reshape(2, 2, 2, 128, 16, 8).transpose(4, 1, 0, 2, 5, 3).reshape(16, 64, 128)
 
 
 def per_device(tokens_in, pre_gain, w_in, w_out, long_filter, w_unembed, target_ids, score_mask):
@@ -272,24 +270,24 @@
     keep, give = halves_of(w_in.transpose(1, 0, 2), 2, core)
     got = lax.ppermute(give, "ctx", PERM_CORE)
     near = jnp.concatenate([jnp.where(core == 0, keep, got), jnp.where(core == 0, got, keep)], axis=1)
-    near, filter_in, tokens = lax.optimization_barrier((near.reshape(384, 128), long_filter, tokens_in))
+    near, w_out, tokens = lax.optimization_barrier((near.reshape(384, 128), w_out, tokens_in))
+    beside = lax.ppermute(tokens, "ctx", PERM_CORE)
+    terms = lax.all_to_all(product(w_out, w_unembed), "tp", 0, 0, tiled=True)
     far = lax.ppermute(near, "ctx", PERM_Z)
-    low_taps = lax.ppermute(filter_in, "ctx", PERM_Z_UP)
+    near, far, terms, beside = lax.optimization_barrier((near, far, terms, beside))
+
     near = lax.all_to_all(
         jnp.broadcast_to(near, (4, 384, 128)), "ctx", 0, 0, axis_index_groups=GROUPS_X, tiled=True
     )
-    near, far, low_taps, tokens = lax.optimization_barrier((near, far, low_taps, tokens))
+    far = jnp.stack([far] + [lax.ppermute(far, "ctx", PERM_Y[k]) for k in (1, 2, 3)])
+    near, far, terms, long_filter = lax.optimization_barrier((near, far, terms, long_filter))
 
     near = jnp.broadcast_to(near.reshape(1, 1536, 128), (4, 1536, 128))
     near = lax.all_to_all(near, "ctx", 0, 0, axis_index_groups=GROUPS_Y, tiled=True)
-    far = jnp.stack([far] + [lax.ppermute(far, "ctx", PERM_Y[k]) for k in (1, 2, 3)])
-    far, tokens, low_taps = lax.optimization_barrier((far, tokens, low_taps))
-
     fars = [far] + [lax.ppermute(far, "ctx", PERM_X[k]) for k in (1, 2, 3)]
-    beside = lax.ppermute(tokens, "ctx", PERM_CORE)
-    terms, near, low_taps = lax.optimization_barrier((product(w_out, w_unembed), near, low_taps))
-    terms = lax.all_to_all(terms, "tp", 0, 0, tiled=True)
-    taps = filter_pieces(long_filter, low_taps, core)
+    taps, give = halves_of(long_filter, 1, core)
+    taps_got = lax.ppermute(give, "ctx", PERM_CORE)
+    piece = lax.ppermute(jnp.sum(terms.astype(F32), axis=0).astype(BF16), ("ctx", "tp"), ROUTE)
 
     at = jnp.stack([(ctx // 8) % 4, (ctx // 2) % 4, core, z]).astype(jnp.int32)
     normed, sums = call(
@@ -302,22 +300,18 @@
     )
     signal, gate = call(
         proj_kernel,
-        (shape((16, 96, 128), BF16), shape((2, 2, 128, 128), BF16)),
-        [SCALARS] + whole(7),
+        (shape((16, 64, 128), BF16), shape((2, 2, 128, 128), BF16)),
+        [SCALARS] + whole(8),
         [],
         8 * 10**8,
-        (at, normed, sums, taps, *fars),
-    )
-    signal, terms = lax.optimization_barrier((signal, terms))
-    piece = lax.ppermute(jnp.sum(terms.astype(F32), axis=0).astype(BF16), ("ctx", "tp"), ROUTE)
+        (at, normed, sums, taps, taps_got, *fars),
+    )
     got = lax.all_to_all(signal, "ctx", 0, 0, axis_index_groups=GROUPS_CORE, tiled=True)
-    signal = got[:, :32].reshape(512, 128)
-    before = lax.ppermute(signal, "ctx", PERM_Z_UP)
+    before = lax.ppermute(got, "ctx", PERM_Z_UP)
     gate_keep = lax.dynamic_index_in_dim(gate, core, 0, False)
     gate_got = lax.ppermute(lax.dynamic_index_in_dim(gate, 1 - core, 0, False), "ctx", PERM_CORE)
 
-    spectra = filter_spectra(z_at, got)
-    conv = convolve(z_at, signal, before, *spectra, piece)
+    conv = convolve(z_at, *spectra(got), before, piece)
     conv = lax.all_to_all(conv, "ctx", 0, 0, axis_index_groups=GROUPS_PLANE, tiled=True)
 
     width = w_unembed.shape[0]

time: 212 us -> 193 us (0.910)
  waiting for transfers between devices: 52.1 us -> 44.3 us
  starting transfers between devices: 96.1 us -> 89.3 us
  other arithmetic: 5.18 us -> 2.98 us
    ppermute x3 -> x2, starting transfers between devices: 24.8 us -> 10.1 us  [the longest x1 8.23 us: per_device(): before = lax.ppermute(got, 'ctx', PERM_Z_UP)]
    all_to_all x1, waiting for transfers between devices: 12.7 us -> 5.39 us  [per_device(): lax.all_to_all(near, 'ctx', 0, 0, axis_index_groups=GROUPS_Y, tiled=True)]
    ppermute x1, waiting for transfers between devices: 9.65 us -> 16.9 us  [per_device(): lax.ppermute(jnp.sum(terms.astype(F32), axis=0).astype(BF16), ('ctx', 'tp...]
    ppermute x1, starting transfers between devices: 1.92 us -> 8.21 us  [per_device(): far = lax.ppermute(near, 'ctx', PERM_Z)]
    ppermute x1, waiting for transfers between devices: 13.6 us -> 7.45 us  [per_device(): far = lax.ppermute(near, 'ctx', PERM_Z)]
    all_to_all x1, starting transfers between devices: 9.28 us -> 4.77 us  [per_device(): lax.all_to_all(jnp.broadcast_to(near, (4, 384, 128)), 'ctx', 0, 0, axis_i...]
    unnamed x16 -> x20, local copies, waits for them, and re-layouts: 0.04 us -> 3.22 us
    ppermute x1, starting transfers between devices: 10.3 us -> 13.1 us  [per_device(): far = lax.ppermute(logits, 'tp', [(i, i ^ 4) for i in range(8)])]
  transfers between devices with their start and end apart: 19 -> 18, of which waited for: 8 -> 7; matrix products, arithmetic and copies ran while one was open for 6% -> 3% of each run, Pallas kernels for 5% -> 3%
where the time goes in v7:
time: 193 us; the launch traced here: 192 us
  starting transfers between devices  89.3 us (46%)
  waiting for transfers between devices  44.3 us (23%)
  blocking collectives  32.1 us (17%)
  Pallas kernels  10.7 us (6%)
  local copies, waits for them, and re-layouts  9.71 us (5%)
  other arithmetic  2.98 us (2%)
  matrix products  2.19 us (1%)
    ppermute x1, waiting for transfers between devices, per_device(): lax.ppermute(jnp.sum(terms.astype(F32), axis=0).astype(BF16), ('ctx', 'tp...  16.9 us
    ppermute x1, starting transfers between devices, per_device(): far = lax.ppermute(logits, 'tp', [(i, i ^ 4) for i in range(8)])  13.1 us
    all_to_all x1, blocking collectives, per_device(): lax.all_to_all(logits.reshape(4, 64, 512), 'tp', 0, 0, axis_index_groups=...  12.7 us
    all_to_all x1, starting transfers between devices, per_device(): terms = lax.all_to_all(product(w_out, w_unembed), 'tp', 0, 0, tiled=True)  12.5 us
    ppermute x3, starting transfers between devices, per_device(): lax.ppermute(far, 'ctx', PERM_Y[k])  11.5 us
    all_to_all x1, blocking collectives, per_device(): lax.all_to_all(signal, 'ctx', 0, 0, axis_index_groups=GROUPS_CORE, tiled=...  11.5 us
    pallas_call x5, Pallas kernels, call(): pl.pallas_call(kernel, out_shape=outs, in_specs=specs, out_specs=jax.tree...  10.7 us
    ppermute x3, starting transfers between devices, per_device(): fars = [far] + [lax.ppermute(far, 'ctx', PERM_X[k]) for k in (1, 2, 3)]  8.65 us
  transfers between devices with their start and end apart: 18, of which 7 were waited for; matrix products, arithmetic and copies ran while one was open for 3% of the time, Pallas kernels for 3%

profile of v7, /device:TPU:6, one launch (start us, length us, event | category | flops | bytes accessed | tf_op | source)
XLA Modules:
  0.0 191.8 jit_solution(15580030953428858133)
XLA Ops:
  0.9 1.9 collective-permute-start
  4.8 2.1 %collective-permute-start.2 = (bf16[256,4096]{1,0:T(8,128)(2,1)}, bf16[256,4096]{1,0:T(8,128)(2,1)S(1)}, u32[]{:S(2)}, u32[]{:S(2)}) collective-permute-start(bf16[256,4096]{1,0:T(8,128)(2,1)} %own_ref.1), channel_id=1, source_target_pairs={{0,8},{8,0},{16,24},{24,16},{32,40},{40,32},{48,56},{56,48},{64,72... | collective-permute-start | bytes 6291464 | tf_op jit(solution)/shard_map/ppermute | solution.py:274
  8.5 12.5 %all-to-all-start = ((bf16[8,32,128]{2,1,0:T(8,128)(2,1)}), bf16[8,32,128]{2,1,0:T(8,128)(2,1)S(1)}, u32[]{:S(2)}, u32[]{:S(2)}) async-start(bf16[8,32,128]{2,1,0:T(8,128)(2,1)} %bitcast.10), calls=%async_computation | async-start | bytes 131072 | tf_op jit(solution)/shard_map/all_to_all | solution.py:275
  21.0 8.2 %collective-permute-start.1 = (bf16[384,128]{1,0:T(8,128)(2,1)S(1)}, bf16[384,128]{1,0:T(8,128)(2,1)S(1)}, u32[]{:S(2)}, u32[]{:S(2)}) collective-permute-start(bf16[384,128]{1,0:T(8,128)(2,1)S(1)} %bitcast.32), channel_id=1, source_target_pairs={{0,256},{8,264},{16,272},{24,280},{32,288},{40,296},{48,304},{56,3... | collective-permute-start | bytes 294920 | tf_op jit(solution)/shard_map/ppermute | solution.py:276
  29.2 7.4 %collective-permute-done.1 = bf16[384,128]{1,0:T(8,128)(2,1)S(1)} collective-permute-done((bf16[384,128]{1,0:T(8,128)(2,1)S(1)}, bf16[384,128]{1,0:T(8,128)(2,1)S(1)}, u32[]{:S(2)}, u32[]{:S(2)}) %collective-permute-start.1) | collective-permute-done | bytes 98336 | tf_op jit(solution)/shard_map/ppermute | solution.py:276
  37.6 4.8 %all-to-all-start.1 = ((bf16[4,384,128]{2,1,0:T(8,128)(2,1)}), bf16[4,384,128]{2,1,0:T(8,128)(2,1)S(1)}, u32[]{:S(2)}, u32[]{:S(2)}) async-start(bf16[4,384,128]{2,1,0:T(8,128)(2,1)} %broadcast_in_dim.31), calls=%async_computation.1 | async-start | bytes 786432 | tf_op jit(solution)/shard_map/all_to_all | solution.py:279
  42.4 3.5 %collective-permute-start.3 = (bf16[384,128]{1,0:T(8,128)(2,1)S(1)}, bf16[384,128]{1,0:T(8,128)(2,1)S(1)}, u32[]{:S(2)}, u32[]{:S(2)}) collective-permute-start(bf16[384,128]{1,0:T(8,128)(2,1)S(1)} %collective-permute-done.1), channel_id=1, source_target_pairs={{0,64},{8,72},{16,80},{24,88},{32,96},{40,104},{48,112},{56,120},{... | collective-permute-start | bytes 294920 | tf_op jit(solution)/shard_map/ppermute | solution.py:282
  45.8 4.8 %collective-permute-start.4 = (bf16[384,128]{1,0:T(8,128)(2,1)S(1)}, bf16[384,128]{1,0:T(8,128)(2,1)S(1)}, u32[]{:S(2)}, u32[]{:S(2)}) collective-permute-start(bf16[384,128]{1,0:T(8,128)(2,1)S(1)} %collective-permute-done.1), channel_id=1, source_target_pairs={{0,128},{8,136},{16,144},{24,152},{32,160},{40,168},{48,176},{56,1... | collective-permute-start | bytes 294920 | tf_op jit(solution)/shard_map/ppermute | solution.py:282
  50.7 3.3 %collective-permute-start.5 = (bf16[384,128]{1,0:T(8,128)(2,1)S(1)}, bf16[384,128]{1,0:T(8,128)(2,1)S(1)}, u32[]{:S(2)}, u32[]{:S(2)}) collective-permute-start(bf16[384,128]{1,0:T(8,128)(2,1)S(1)} %collective-permute-done.1), channel_id=1, source_target_pairs={{0,192},{8,200},{16,208},{24,216},{32,224},{40,232},{48,240},{56,2... | collective-permute-start | bytes 294920 | tf_op jit(solution)/shard_map/ppermute | solution.py:282
  53.9 3.2 %collective-permute-done.5 = bf16[384,128]{1,0:T(8,128)(2,1)S(1)} collective-permute-done((bf16[384,128]{1,0:T(8,128)(2,1)S(1)}, bf16[384,128]{1,0:T(8,128)(2,1)S(1)}, u32[]{:S(2)}, u32[]{:S(2)}) %collective-permute-start.5) | collective-permute-done | bytes 98336 | tf_op jit(solution)/shard_map/ppermute | solution.py:282
  59.5 4.0 %all-to-all-start.2 = ((bf16[4,1536,128]{2,1,0:T(8,128)(2,1)}), bf16[4,1536,128]{2,1,0:T(8,128)(2,1)S(1)}, u32[]{:S(2)}, u32[]{:S(2)}) async-start(bf16[4,1536,128]{2,1,0:T(8,128)(2,1)} %broadcast_in_dim.33), calls=%async_computation.2 | async-start | bytes 3145728 | tf_op jit(solution)/shard_map/all_to_all | solution.py:286
  63.4 1.9 collective-permute-start.7
  65.3 4.8 %collective-permute-start.8 = (bf16[4,384,128]{2,1,0:T(8,128)(2,1)S(1)}, bf16[4,384,128]{2,1,0:T(8,128)(2,1)S(1)}, u32[]{:S(2)}, u32[]{:S(2)}) collective-permute-start(bf16[4,384,128]{2,1,0:T(8,128)(2,1)S(1)} %pad_maximum_fusion.f0), channel_id=1, source_target_pairs={{0,32},{8,40},{16,48},{24,56},{32,0},{40,8},{48,16},{56,24},{64,96... | collective-permute-start | bytes 1179656 | tf_op jit(solution)/shard_map/ppermute | solution.py:287
  70.2 1.9 %collective-permute-start.9 = (bf16[4,384,128]{2,1,0:T(8,128)(2,1)S(1)}, bf16[4,384,128]{2,1,0:T(8,128)(2,1)}, u32[]{:S(2)}, u32[]{:S(2)}) collective-permute-start(bf16[4,384,128]{2,1,0:T(8,128)(2,1)S(1)} %pad_maximum_fusion.f0), channel_id=1, source_target_pairs={{0,48},{8,56},{16,0},{24,8},{32,16},{40,24},{48,32},{56,40},{64,11... | collective-permute-start | bytes 1179656 | tf_op jit(solution)/shard_map/ppermute | solution.py:287
  73.8 1.9 collective-permute-start.6
  75.7 5.4 %all-to-all-done.2.near_ref = bf16[4,1536,128]{2,1,0:T(8,128)(2,1)S(1)} async-done(((bf16[4,1536,128]{2,1,0:T(8,128)(2,1)}), bf16[4,1536,128]{2,1,0:T(8,128)(2,1)S(1)}, u32[]{:S(2)}, u32[]{:S(2)}) %all-to-all-start.2) | async-done | bytes 1572896 | tf_op jit(solution)/shard_map/all_to_all | solution.py:286
  81.1 1.6 copy-done.1
  82.7 1.6 copy-done.3
  84.3 4.7 %shard_map.118 = (bf16[2,256,4096]{2,1,0:T(8,128)(2,1)S(1)}, f32[2,256,384]{2,1,0:T(8,128)S(1)}) custom-call(s32[4]{0:T(128)S(1)} %pad_add_fusion.at_ref, bf16[256,4096]{1,0:T(8,128)(2,1)S(1)} %copy-done.1, bf16[256,4096]{1,0:T(8,128)(2,1)S(1)} %copy-done.3, bf16[1,4096]{1,0:T(2,128)(2,1)S(1)} %reshape.42.gain_ref, ...), custom_call_target="tpu_custom_call" | custom-call | flops 800000000 | bytes 4194304 | tf_op jit(solution)/shard_map/pallas_call | solution.py:214
  89.0 2.5 %shard_map.119 = (bf16[16,64,128]{2,1,0:T(8,128)(2,1)S(1)}, bf16[2,2,128,128]{3,2,1,0:T(8,128)(2,1)S(1)}) custom-call(s32[4]{0:T(128)S(1)} %pad_add_fusion.at_ref, bf16[2,256,4096]{2,1,0:T(8,128)(2,1)S(1)} %get-tuple-element.30.normed_ref, f32[2,256,384]{2,1,0:T(8,128)S(1)} %get-tuple-element.31.near_ref, bf16[256,128]{1,0:T(8,128)(2,1)S(1)} %get-tuple-element.46.keep_ref, ...), custom_call_target="tpu_custom_call" | custom-call | flops 800000000 | bytes 4194304 | tf_op jit(solution)/shard_map/pallas_call | solution.py:214
  91.5 11.5 %all_to_all.36.got_ref = bf16[16,64,128]{2,1,0:T(8,128)(2,1)S(1)} all-to-all(bf16[16,64,128]{2,1,0:T(8,128)(2,1)S(1)} %get-tuple-element.34), channel_id=1, replica_groups={{0,16,32,48,64,80,96,112,128,144,160,176,192,208,224,240},{8,24,40,56,7..., dimensions={0} | all-to-all | bytes 524288 | tf_op jit(solution)/shard_map/all_to_all | solution.py:309
  103.0 8.2 %collective-permute-start.10 = (bf16[16,64,128]{2,1,0:T(8,128)(2,1)S(1)}, bf16[16,64,128]{2,1,0:T(8,128)(2,1)S(1)}, u32[]{:S(2)}, u32[]{:S(2)}) collective-permute-start(bf16[16,64,128]{2,1,0:T(8,128)(2,1)S(1)} %all_to_all.36.got_ref), channel_id=1, source_target_pairs={{0,256},{8,264},{16,272},{24,280},{32,288},{40,296},{48,304},{56,3... | collective-permute-start | bytes 786440 | tf_op jit(solution)/shard_map/ppermute | solution.py:310
  111.3 1.9 %collective-permute-start.11 = (bf16[32,128]{1,0:T(8,128)(2,1)S(1)}, bf16[32,128]{1,0:T(8,128)(2,1)S(1)}, u32[]{:S(2)}, u32[]{:S(2)}) collective-permute-start(bf16[32,128]{1,0:T(8,128)(2,1)S(1)} %reduce_sum.42), channel_id=1, source_target_pairs={{0,0},{1,256},{2,16},{3,272},{4,32},{5,288},{6,48},{7,304},{8,64},... | collective-permute-start | bytes 24584 | tf_op jit(solution)/shard_map/ppermute | solution.py:290
  114.2 16.9 %collective-permute-done.11.piece_ref = bf16[32,128]{1,0:T(8,128)(2,1)S(1)} collective-permute-done((bf16[32,128]{1,0:T(8,128)(2,1)S(1)}, bf16[32,128]{1,0:T(8,128)(2,1)S(1)}, u32[]{:S(2)}, u32[]{:S(2)}) %collective-permute-start.11) | collective-permute-done | bytes 8224 | tf_op jit(solution)/shard_map/ppermute | solution.py:290
  131.1 2.3 %shard_map.121 = bf16[32,48,128]{2,1,0:T(8,128)(2,1)} custom-call(s32[1]{0:T(128)} %bitcast.1.z_ref, f32[1024,256]{1,0:T(8,128)S(1)} %get-tuple-element.35.signal_ref, f32[1024,256]{1,0:T(8,128)S(1)} %get-tuple-element.36.filter_ref, bf16[16,64,128]{2,1,0:T(8,128)(2,1)S(1)} %collective-permute-done.10.before_ref, ...), custom_call_target="tpu_custom_call" | custom-call | flops 600000000 | bytes 4194304 | tf_op jit(solution)/shard_map/pallas_call | solution.py:214
  133.4 8.4 %all-to-all-start.4 = ((bf16[32,48,128]{2,1,0:T(8,128)(2,1)}), bf16[32,48,128]{2,1,0:T(8,128)(2,1)S(1)}, u32[]{:S(2)}, u32[]{:S(2)}) async-start(bf16[32,48,128]{2,1,0:T(8,128)(2,1)} %shard_map.121), calls=%async_computation.4 | async-start | bytes 786432 | tf_op jit(solution)/shard_map/all_to_all | solution.py:315
  141.9 2.1 %collective-permute-start.12 = (bf16[2,128,128]{2,1,0:T(8,128)(2,1)S(1)}, bf16[2,128,128]{2,1,0:T(8,128)(2,1)S(1)}, u32[]{:S(2)}, u32[]{:S(2)}) collective-permute-start(bf16[2,128,128]{2,1,0:T(8,128)(2,1)S(1)} %get-tuple-element.43), channel_id=1, source_target_pairs={{0,8},{8,0},{16,24},{24,16},{32,40},{40,32},{48,56},{56,48},{64,72... | collective-permute-start | bytes 196616 | tf_op jit(solution)/shard_map/ppermute | solution.py:312
  145.2 4.7 %all-to-all-done.4.got_ref = bf16[32,48,128]{2,1,0:T(8,128)(2,1)S(1)} async-done(((bf16[32,48,128]{2,1,0:T(8,128)(2,1)}), bf16[32,48,128]{2,1,0:T(8,128)(2,1)S(1)}, u32[]{:S(2)}, u32[]{:S(2)}) %all-to-all-start.4) | async-done | bytes 393248 | tf_op jit(solution)/shard_map/all_to_all | solution.py:315
  150.2 12.7 %all_to_all.37 = bf16[4,64,512]{2,1,0:T(8,128)(2,1)S(1)} all-to-all(bf16[4,64,512]{2,1,0:T(8,128)(2,1)S(1)} %bitcast.30), channel_id=1, replica_groups={{0,1,2,3},{4,5,6,7},{8,9,10,11},{12,13,14,15},{16,17,18,19},{20,21,22,2..., dimensions={0} | all-to-all | bytes 524288 | tf_op jit(solution)/shard_map/all_to_all | solution.py:327
  163.0 13.1 %collective-permute-start.13 = (bf16[64,512]{1,0:T(8,128)(2,1)S(1)}, bf16[64,512]{1,0:T(8,128)(2,1)S(1)}, u32[]{:S(2)}, u32[]{:S(2)}) collective-permute-start(bf16[64,512]{1,0:T(8,128)(2,1)S(1)} %reduce_sum.43), channel_id=1, source_target_pairs={{0,4},{1,5},{2,6},{3,7},{4,0},{5,1},{6,2},{7,3},{8,12},{9,13},{10,... | collective-permute-start | bytes 196616 | tf_op jit(solution)/shard_map/ppermute | solution.py:329
  176.2 5.4 %collective-permute-done.13 = bf16[64,512]{1,0:T(8,128)(2,1)S(1)} collective-permute-done((bf16[64,512]{1,0:T(8,128)(2,1)S(1)}, bf16[64,512]{1,0:T(8,128)(2,1)S(1)}, u32[]{:S(2)}, u32[]{:S(2)}) %collective-permute-start.13) | collective-permute-done | bytes 65568 | tf_op jit(solution)/shard_map/ppermute | solution.py:329
  182.1 7.9 %all_to_all.38 = f32[4,1,64]{2,1,0:T(1,128)S(1)} all-to-all(f32[4,1,64]{2,1,0:T(1,128)S(1)} %broadcast_in_dim.35), channel_id=1, replica_groups={{0,1,2,3},{4,5,6,7},{8,9,10,11},{12,13,14,15},{16,17,18,19},{20,21,22,2..., dimensions={0} | all-to-all | bytes 2048 | tf_op jit(solution)/shard_map/all_to_all | solution.py:340
  (55 shorter events, 14.2 us)
Async XLA Ops:
  0.0 6.9 %copy-start = (bf16[512,512]{1,0:T(8,128)(2,1)S(1)}, bf16[512,512]{1,0:T(8,128)(2,1)}, u32[]{:S(2)}) copy-start(bf16[512,512]{1,0:T(8,128)(2,1)} %param.17) | copy-start | bytes 1572868
  0.9 3.1 %collective-permute-start = (bf16[3,64,128]{2,1,0:T(8,128)(2,1)S(1)}, bf16[3,64,128]{2,1,0:T(8,128)(2,1)S(1)}, u32[]{:S(2)}, u32[]{:S(2)}) collective-permute-start(bf16[3,64,128]{2,1,0:T(8,128)(2,1)S(1)} %dynamic-slice_bitcast_fusion.2), channel_id=1, source_target_pairs={{0,8},{8,0},{16,24},{24,16},{32,40},{40,32},{48,56},{56,48},{64,72... | collective-permute-start | bytes 147464 | tf_op jit(solution)/shard_map/ppermute | solution.py:271
  4.8 31.9 %collective-permute-start.2 = (bf16[256,4096]{1,0:T(8,128)(2,1)}, bf16[256,4096]{1,0:T(8,128)(2,1)S(1)}, u32[]{:S(2)}, u32[]{:S(2)}) collective-permute-start(bf16[256,4096]{1,0:T(8,128)(2,1)} %own_ref.1), channel_id=1, source_target_pairs={{0,8},{8,0},{16,24},{24,16},{32,40},{40,32},{48,56},{56,48},{64,72... | collective-permute-start | bytes 6291464 | tf_op jit(solution)/shard_map/ppermute | solution.py:274
  8.5 28.2 %all-to-all-start = ((bf16[8,32,128]{2,1,0:T(8,128)(2,1)}), bf16[8,32,128]{2,1,0:T(8,128)(2,1)S(1)}, u32[]{:S(2)}, u32[]{:S(2)}) async-start(bf16[8,32,128]{2,1,0:T(8,128)(2,1)} %bitcast.10), calls=%async_computation | async-start | bytes 131072 | tf_op jit(solution)/shard_map/all_to_all | solution.py:275
  21.0 15.7 %collective-permute-start.1 = (bf16[384,128]{1,0:T(8,128)(2,1)S(1)}, bf16[384,128]{1,0:T(8,128)(2,1)S(1)}, u32[]{:S(2)}, u32[]{:S(2)}) collective-permute-start(bf16[384,128]{1,0:T(8,128)(2,1)S(1)} %bitcast.32), channel_id=1, source_target_pairs={{0,256},{8,264},{16,272},{24,280},{32,288},{40,296},{48,304},{56,3... | collective-permute-start | bytes 294920 | tf_op jit(solution)/shard_map/ppermute | solution.py:276
  36.7 20.5 %copy-start.6 = (bf16[384,128]{1,0:T(8,128)(2,1)}, bf16[384,128]{1,0:T(8,128)(2,1)S(1)}, u32[]{:S(2)}) copy-start(bf16[384,128]{1,0:T(8,128)(2,1)S(1)} %collective-permute-done.1) | copy-start | bytes 294916
  36.7 22.8 %copy-start.2 = (bf16[256,4096]{1,0:T(8,128)(2,1)}, bf16[256,4096]{1,0:T(8,128)(2,1)S(1)}, u32[]{:S(2)}) copy-start(bf16[256,4096]{1,0:T(8,128)(2,1)S(1)} %collective-permute-done.2.beside_ref) | copy-start | bytes 6291460
  37.6 20.5 %all-to-all-start.1 = ((bf16[4,384,128]{2,1,0:T(8,128)(2,1)}), bf16[4,384,128]{2,1,0:T(8,128)(2,1)S(1)}, u32[]{:S(2)}, u32[]{:S(2)}) async-start(bf16[4,384,128]{2,1,0:T(8,128)(2,1)} %broadcast_in_dim.31), calls=%async_computation.1 | async-start | bytes 786432 | tf_op jit(solution)/shard_map/all_to_all | solution.py:279
  42.4 11.6 %collective-permute-start.3 = (bf16[384,128]{1,0:T(8,128)(2,1)S(1)}, bf16[384,128]{1,0:T(8,128)(2,1)S(1)}, u32[]{:S(2)}, u32[]{:S(2)}) collective-permute-start(bf16[384,128]{1,0:T(8,128)(2,1)S(1)} %collective-permute-done.1), channel_id=1, source_target_pairs={{0,64},{8,72},{16,80},{24,88},{32,96},{40,104},{48,112},{56,120},{... | collective-permute-start | bytes 294920 | tf_op jit(solution)/shard_map/ppermute | solution.py:282
  45.8 8.1 %collective-permute-start.4 = (bf16[384,128]{1,0:T(8,128)(2,1)S(1)}, bf16[384,128]{1,0:T(8,128)(2,1)S(1)}, u32[]{:S(2)}, u32[]{:S(2)}) collective-permute-start(bf16[384,128]{1,0:T(8,128)(2,1)S(1)} %collective-permute-done.1), channel_id=1, source_target_pairs={{0,128},{8,136},{16,144},{24,152},{32,160},{40,168},{48,176},{56,1... | collective-permute-start | bytes 294920 | tf_op jit(solution)/shard_map/ppermute | solution.py:282
  50.7 6.5 %collective-permute-start.5 = (bf16[384,128]{1,0:T(8,128)(2,1)S(1)}, bf16[384,128]{1,0:T(8,128)(2,1)S(1)}, u32[]{:S(2)}, u32[]{:S(2)}) collective-permute-start(bf16[384,128]{1,0:T(8,128)(2,1)S(1)} %collective-permute-done.1), channel_id=1, source_target_pairs={{0,192},{8,200},{16,208},{24,216},{32,224},{40,232},{48,240},{56,2... | collective-permute-start | bytes 294920 | tf_op jit(solution)/shard_map/ppermute | solution.py:282
  59.5 12.7 %copy-start.7 = (bf16[4096]{0:T(1024)(128)(2,1)S(1)}, bf16[4096]{0:T(1024)(128)(2,1)}, u32[]{:S(2)}) copy-start(bf16[4096]{0:T(1024)(128)(2,1)} %param.13) | copy-start | bytes 24580
  59.5 21.6 %all-to-all-start.2 = ((bf16[4,1536,128]{2,1,0:T(8,128)(2,1)}), bf16[4,1536,128]{2,1,0:T(8,128)(2,1)S(1)}, u32[]{:S(2)}, u32[]{:S(2)}) async-start(bf16[4,1536,128]{2,1,0:T(8,128)(2,1)} %broadcast_in_dim.33), calls=%async_computation.2 | async-start | bytes 3145728 | tf_op jit(solution)/shard_map/all_to_all | solution.py:286
  63.4 25.6 %collective-permute-start.7 = (bf16[4,384,128]{2,1,0:T(8,128)(2,1)S(1)}, bf16[4,384,128]{2,1,0:T(8,128)(2,1)S(1)}, u32[]{:S(2)}, u32[]{:S(2)}) collective-permute-start(bf16[4,384,128]{2,1,0:T(8,128)(2,1)S(1)} %pad_maximum_fusion.f0), channel_id=1, source_target_pairs={{0,16},{8,24},{16,32},{24,40},{32,48},{40,56},{48,0},{56,8},{64,80... | collective-permute-start | bytes 1179656 | tf_op jit(solution)/shard_map/ppermute | solution.py:287
  65.3 23.6 %collective-permute-start.8 = (bf16[4,384,128]{2,1,0:T(8,128)(2,1)S(1)}, bf16[4,384,128]{2,1,0:T(8,128)(2,1)S(1)}, u32[]{:S(2)}, u32[]{:S(2)}) collective-permute-start(bf16[4,384,128]{2,1,0:T(8,128)(2,1)S(1)} %pad_maximum_fusion.f0), channel_id=1, source_target_pairs={{0,32},{8,40},{16,48},{24,56},{32,0},{40,8},{48,16},{56,24},{64,96... | collective-permute-start | bytes 1179656 | tf_op jit(solution)/shard_map/ppermute | solution.py:287
  70.2 18.8 %collective-permute-start.9 = (bf16[4,384,128]{2,1,0:T(8,128)(2,1)S(1)}, bf16[4,384,128]{2,1,0:T(8,128)(2,1)}, u32[]{:S(2)}, u32[]{:S(2)}) collective-permute-start(bf16[4,384,128]{2,1,0:T(8,128)(2,1)S(1)} %pad_maximum_fusion.f0), channel_id=1, source_target_pairs={{0,48},{8,56},{16,0},{24,8},{32,16},{40,24},{48,32},{56,40},{64,11... | collective-permute-start | bytes 1179656 | tf_op jit(solution)/shard_map/ppermute | solution.py:287
  73.8 15.2 %collective-permute-start.6 = (bf16[256,128]{1,0:T(8,128)(2,1)}, bf16[256,128]{1,0:T(8,128)(2,1)S(1)}, u32[]{:S(2)}, u32[]{:S(2)}) collective-permute-start(bf16[256,128]{1,0:T(8,128)(2,1)} %get-tuple-element.45), channel_id=1, source_target_pairs={{0,8},{8,0},{16,24},{24,16},{32,40},{40,32},{48,56},{56,48},{64,72... | collective-permute-start | bytes 196616 | tf_op jit(solution)/shard_map/ppermute | solution.py:289
  81.1 1.6 copy-start.1
  82.7 1.6 copy-start.3
  89.0 24.2 %copy-start.4 = (bf16[832,256]{1,0:T(8,128)(2,1)S(1)}, bf16[832,256]{1,0:T(8,128)(2,1)}, u32[]{:S(2)}) copy-start(bf16[832,256]{1,0:T(8,128)(2,1)} %constant.106.clone.matrices) | copy-start | bytes 1277956
  89.0 24.2 %copy-start.5 = (f32[128,256]{1,0:T(8,128)S(1)}, f32[128,256]{1,0:T(8,128)}, u32[]{:S(2)}) copy-start(f32[128,256]{1,0:T(8,128)} %constant.107.clone.twiddles) | copy-start | bytes 393220
  103.0 28.1 %collective-permute-start.10 = (bf16[16,64,128]{2,1,0:T(8,128)(2,1)S(1)}, bf16[16,64,128]{2,1,0:T(8,128)(2,1)S(1)}, u32[]{:S(2)}, u32[]{:S(2)}) collective-permute-start(bf16[16,64,128]{2,1,0:T(8,128)(2,1)S(1)} %all_to_all.36.got_ref), channel_id=1, source_target_pairs={{0,256},{8,264},{16,272},{24,280},{32,288},{40,296},{48,304},{56,3... | collective-permute-start | bytes 786440 | tf_op jit(solution)/shard_map/ppermute | solution.py:310
  111.3 19.8 %collective-permute-start.11 = (bf16[32,128]{1,0:T(8,128)(2,1)S(1)}, bf16[32,128]{1,0:T(8,128)(2,1)S(1)}, u32[]{:S(2)}, u32[]{:S(2)}) collective-permute-start(bf16[32,128]{1,0:T(8,128)(2,1)S(1)} %reduce_sum.42), channel_id=1, source_target_pairs={{0,0},{1,256},{2,16},{3,272},{4,32},{5,288},{6,48},{7,304},{8,64},... | collective-permute-start | bytes 24584 | tf_op jit(solution)/shard_map/ppermute | solution.py:290
  133.4 42.7 %copy-start.9 = (s32[256]{0:T(256)S(1)}, s32[256]{0:T(256)}, u32[]{:S(2)}) copy-start(s32[256]{0:T(256)} %param.18) | copy-start | bytes 3076
  133.4 16.5 %all-to-all-start.4 = ((bf16[32,48,128]{2,1,0:T(8,128)(2,1)}), bf16[32,48,128]{2,1,0:T(8,128)(2,1)S(1)}, u32[]{:S(2)}, u32[]{:S(2)}) async-start(bf16[32,48,128]{2,1,0:T(8,128)(2,1)} %shard_map.121), calls=%async_computation.4 | async-start | bytes 786432 | tf_op jit(solution)/shard_map/all_to_all | solution.py:315
  141.9 40.1 %copy-start.8 = (s32[256]{0:T(256)S(1)}, s32[256]{0:T(256)}, u32[]{:S(2)}) copy-start(s32[256]{0:T(256)} %param.19) | copy-start | bytes 3076
  141.9 3.3 %collective-permute-start.12 = (bf16[2,128,128]{2,1,0:T(8,128)(2,1)S(1)}, bf16[2,128,128]{2,1,0:T(8,128)(2,1)S(1)}, u32[]{:S(2)}, u32[]{:S(2)}) collective-permute-start(bf16[2,128,128]{2,1,0:T(8,128)(2,1)S(1)} %get-tuple-element.43), channel_id=1, source_target_pairs={{0,8},{8,0},{16,24},{24,16},{32,40},{40,32},{48,56},{56,48},{64,72... | collective-permute-start | bytes 196616 | tf_op jit(solution)/shard_map/ppermute | solution.py:312
  163.0 18.7 %collective-permute-start.13 = (bf16[64,512]{1,0:T(8,128)(2,1)S(1)}, bf16[64,512]{1,0:T(8,128)(2,1)S(1)}, u32[]{:S(2)}, u32[]{:S(2)}) collective-permute-start(bf16[64,512]{1,0:T(8,128)(2,1)S(1)} %reduce_sum.43), channel_id=1, source_target_pairs={{0,4},{1,5},{2,6},{3,7},{4,0},{5,1},{6,2},{7,3},{8,12},{9,13},{10,... | collective-permute-start | bytes 196616 | tf_op jit(solution)/shard_map/ppermute | solution.py:329

commit v8 on v7

--- a/solution.py
+++ b/solution.py
@@ -39,16 +39,17 @@
 GROUPS_TP = [[0, 1, 2, 3], [4, 5, 6, 7]]
 
 
-def weight_route():
+def term_route(flip):
     pairs = []
     for i in range(64):
         for j in range(8):
-            plane, core, chip, z = i // 8, (i % 8) // 4, (i % 4) * 4 + j // 2, j % 2
-            pairs.append((i * 8 + j, (z * 32 + chip * 2 + core) * 8 + plane))
+            to = ctx_id((j % 2) ^ flip, j // 2, i % 4, (i % 8) // 4)
+            pairs.append((i * 8 + j, to * 8 + i // 8))
     return pairs
 
 
-ROUTE = weight_route()
+ROUTES = [term_route(0), term_route(1)]
+BLOCK = [(p % 4) * 4 + p // 4 for p in range(16)]
 
 
 def tables():
@@ -144,50 +145,56 @@
     return jnp.concatenate([ref[lead, row + 128 * g : row + 128 * g + 128, :] for g in range(3)], axis=1)
 
 
-def near_kernel(at_ref, own_ref, beside_ref, gain_ref, near_ref, normed_ref, out_ref):
+def near_kernel(at_ref, own_ref, beside_ref, gain_ref, near_ref, gained_ref, scale_ref, out_ref, piece_ref):
     start = at_ref[3] * 2048
-    gain = gain_ref[...].astype(F32)
+    gain = gain_ref[...]
     for part, tokens in enumerate((own_ref, beside_ref)):
 
         @pl.loop(0, 8)
         def _(i):
             rows = pl.ds(pl.multiple_of(i * 32, 32), 32)
-            stream = tokens[rows, :].astype(F32)
-            scale = lax.rsqrt(jnp.mean(stream * stream, axis=1, keepdims=True) + NORM_EPS)
-            normed_ref[part, rows, :] = (stream * scale * gain).astype(BF16)
+            block = tokens[rows, :]
+            stream = block.astype(F32)
+            mean = jnp.mean(stream * stream, axis=1, keepdims=True)
+            scale_ref[part, rows, :] = jnp.broadcast_to(lax.rsqrt(mean + NORM_EPS), (32, 128))
+            gained_ref[part, rows, :] = block * gain
 
         total = jnp.zeros((256, 384), F32)
         for y in range(4):
             for x in (0, 2):
-                left = normed_ref[part, :, pl.ds(pl.multiple_of(start + (y * 4 + x) * 128, 128), 256)]
+                left = gained_ref[part, :, pl.ds(pl.multiple_of(start + (y * 4 + x) * 128, 128), 256)]
                 right = [weight_block(near_ref, y, x * 384), weight_block(near_ref, y, x * 384 + 384)]
                 total += mm(left, jnp.concatenate(right, axis=0))
         out_ref[part] = total
+    piece_ref[...] = sum(near_ref[y, 1536:, :].astype(F32) for y in range(4)).astype(BF16)
 
 
 def put_pieces(ref, row, place, block):
     first, second = block[:128].T, block[128:].T
     for p in range(16):
-        rows = jnp.concatenate([first[p * 8 : p * 8 + 8], second[p * 8 : p * 8 + 8]], axis=0).astype(BF16)
+        b = BLOCK[p] * 8
+        rows = jnp.concatenate([first[b : b + 8], second[b : b + 8]], axis=0).astype(BF16)
         ref[p, pl.ds(pl.multiple_of(row + place * 16, 16), 16), :] = rows
 
 
-def proj_kernel(at_ref, normed_ref, near_ref, keep_ref, got_ref, f0, f1, f2, f3, sig_ref, gate_ref):
+def proj_kernel(at_ref, gained_ref, scale_ref, near_ref, own_taps, got_taps, f0, f1, f2, f3, sig_ref, gate_ref):
     y_at, x_at, core = at_ref[0], at_ref[1], at_ref[2]
     start = 2048 - at_ref[3] * 2048
+    half = pl.ds(pl.multiple_of(core * 128, 128), 128)
     for part in range(2):
         total = near_ref[part]
         for step, ref in enumerate((f0, f1, f2, f3)):
             x = lax.rem(x_at + 4 - step, 4)
             for k in (0, 2):
                 starts = [start + (lax.rem(y_at + 4 - j, 4) * 4 + x) * 128 for j in (k, k + 1)]
-                left = [normed_ref[part, :, pl.ds(pl.multiple_of(at, 128), 128)] for at in starts]
+                left = [gained_ref[part, :, pl.ds(pl.multiple_of(at, 128), 128)] for at in starts]
                 right = [weight_block(ref, k, 0), weight_block(ref, k + 1, 0)]
                 total += mm(jnp.concatenate(left, axis=1), jnp.concatenate(right, axis=0))
-        proj = total.astype(BF16).astype(F32)
+        scale = scale_ref[part]
+        proj = (total * jnp.concatenate([scale, scale, scale], axis=1)).astype(BF16).astype(F32)
         place = core if part == 0 else 1 - core
         put_pieces(sig_ref, 0, place, proj[:, 128:256] * proj[:, 256:])
-        put_pieces(sig_ref, 32, place, (keep_ref if part == 0 else got_ref)[...].astype(F32))
+        put_pieces(sig_ref, 32, place, (own_taps if part == 0 else got_taps)[:, half].astype(F32))
         gate_ref[place, 0] = proj[:128, :128].T.astype(BF16)
         gate_ref[place, 1] = proj[128:, :128].T.astype(BF16)
 
@@ -199,12 +206,12 @@
     for rb in range(2):
         total = base_ref[rb * 128 : rb * 128 + 128, :]
         for c in range(2):
-            cube = jnp.concatenate([conv[p * 2 + c, rb * 8 : rb * 8 + 8] for p in range(16)], axis=0)
+            cube = jnp.concatenate([conv[BLOCK[b] * 2 + c, rb * 8 : rb * 8 + 8] for b in range(16)], axis=0)
             gate = jnp.where(core == c, keep[rb], other[rb])
             mixed = (gate * cube).T.astype(BF16)
             weights = []
-            for p in range(16):
-                piece = got_ref[p * 2 + c, 16:, :].astype(F32)
+            for b in range(16):
+                piece = got_ref[BLOCK[b] * 2 + c, 16:, :].astype(F32)
                 weights.append(jnp.concatenate([piece[v * 8 : v * 8 + 8] for v in range(4)], axis=1))
             total += mm(mixed, jnp.concatenate(weights, axis=0).astype(BF16))
         out_ref[rb * 128 : rb * 128 + 128, :] = total.astype(BF16)
@@ -252,14 +259,13 @@
     )
 
 
-def halves_of(array, axis, core):
-    keep = lax.dynamic_slice_in_dim(array, core * 128, 128, axis)
-    return keep, lax.dynamic_slice_in_dim(array, 128 - core * 128, 128, axis)
+def half_of(array, axis, which):
+    return lax.dynamic_slice_in_dim(array, which * 128, 128, axis)
 
 
 def product(w_out, w_unembed):
-    partial = mm(w_out, w_unembed).astype(BF16).reshape(4, 1, 8, 4, 128).transpose(0, 1, 3, 2, 4)
-    return jnp.broadcast_to(partial.reshape(4, 1, 32, 128), (4, 2, 32, 128)).reshape(8, 32, 128)
+    partial = mm(w_out, w_unembed).astype(BF16).reshape(4, 8, 4, 128)
+    return partial.transpose(0, 2, 1, 3).reshape(128, 128)
 
 
 def per_device(tokens_in, pre_gain, w_in, w_out, long_filter, w_unembed, target_ids, score_mask):
@@ -267,32 +273,33 @@
     core, z = ctx % 2, ctx // 32
     z_at = z.reshape(1).astype(jnp.int32)
 
-    keep, give = halves_of(w_in.transpose(1, 0, 2), 2, core)
-    got = lax.ppermute(give, "ctx", PERM_CORE)
+    w_in = w_in.transpose(1, 0, 2)
+    got = half_of(lax.ppermute(w_in, "ctx", PERM_CORE), 2, core)
+    keep = half_of(w_in, 2, core)
     near = jnp.concatenate([jnp.where(core == 0, keep, got), jnp.where(core == 0, got, keep)], axis=1)
-    near, w_out, tokens = lax.optimization_barrier((near.reshape(384, 128), w_out, tokens_in))
+    near, tokens = lax.optimization_barrier((near.reshape(384, 128), tokens_in))
     beside = lax.ppermute(tokens, "ctx", PERM_CORE)
-    terms = lax.all_to_all(product(w_out, w_unembed), "tp", 0, 0, tiled=True)
     far = lax.ppermute(near, "ctx", PERM_Z)
-    near, far, terms, beside = lax.optimization_barrier((near, far, terms, beside))
-
+    near, w_out, taps, beside = lax.optimization_barrier((near, w_out, long_filter, beside))
+    taps_got = lax.ppermute(taps, "ctx", PERM_CORE)
+    term = product(w_out, w_unembed)
+    terms = [lax.ppermute(term, ("ctx", "tp"), route) for route in ROUTES]
     near = lax.all_to_all(
         jnp.broadcast_to(near, (4, 384, 128)), "ctx", 0, 0, axis_index_groups=GROUPS_X, tiled=True
     )
+
     far = jnp.stack([far] + [lax.ppermute(far, "ctx", PERM_Y[k]) for k in (1, 2, 3)])
-    near, far, terms, long_filter = lax.optimization_barrier((near, far, terms, long_filter))
-
-    near = jnp.broadcast_to(near.reshape(1, 1536, 128), (4, 1536, 128))
+    pieces = (terms[0].astype(F32) + terms[1].astype(F32)).astype(BF16).reshape(4, 32, 128)
+    near, far, pieces = lax.optimization_barrier((near, far, pieces))
+
+    near = jnp.concatenate([jnp.broadcast_to(near.reshape(1, 1536, 128), (4, 1536, 128)), pieces], axis=1)
     near = lax.all_to_all(near, "ctx", 0, 0, axis_index_groups=GROUPS_Y, tiled=True)
     fars = [far] + [lax.ppermute(far, "ctx", PERM_X[k]) for k in (1, 2, 3)]
-    taps, give = halves_of(long_filter, 1, core)
-    taps_got = lax.ppermute(give, "ctx", PERM_CORE)
-    piece = lax.ppermute(jnp.sum(terms.astype(F32), axis=0).astype(BF16), ("ctx", "tp"), ROUTE)
 
     at = jnp.stack([(ctx // 8) % 4, (ctx // 2) % 4, core, z]).astype(jnp.int32)
-    normed, sums = call(
+    gained, scale, sums, piece = call(
         near_kernel,
-        (shape((2, 256, 4096), BF16), shape((2, 256, 384), F32)),
+        (shape((2, 256, 4096), BF16), shape((2, 256, 128), F32), shape((2, 256, 384), F32), shape((32, 128), BF16)),
         [SCALARS] + whole(4),
         [],
         8 * 10**8,
@@ -301,10 +308,10 @@
     signal, gate = call(
         proj_kernel,
         (shape((16, 64, 128), BF16), shape((2, 2, 128, 128), BF16)),
-        [SCALARS] + whole(8),
+        [SCALARS] + whole(9),
         [],
         8 * 10**8,
-        (at, normed, sums, taps, taps_got, *fars),
+        (at, gained, scale, sums, taps, taps_got, *fars),
     )
     got = lax.all_to_all(signal, "ctx", 0, 0, axis_index_groups=GROUPS_CORE, tiled=True)
     before = lax.ppermute(got, "ctx", PERM_Z_UP)

time: 193 us -> 199 us (1.031)
  blocking collectives: 32.1 us -> 48.2 us
  waiting for transfers between devices: 44.3 us -> 36.6 us
  local copies, waits for them, and re-layouts: 9.71 us -> 6.8 us
    ppermute x3 -> x4, waiting for transfers between devices: 18.1 us -> 1.46 us  [the longest x1 1.46 us: per_device(): got = half_of(lax.ppermute(w_in, 'ctx', PERM_CORE), 2, core)]
    all_to_all x1, blocking collectives: 12.7 us -> 28.7 us  [per_device(): lax.all_to_all(logits.reshape(4, 64, 512), 'tp', 0, 0, axis_index_groups=...]
    ppermute x3 -> x4, starting transfers between devices: 5.74 us -> 19.1 us  [the longest x2 15.2 us: per_device(): terms = [lax.ppermute(term, ('ctx', 'tp'), route) for route in ROUTES]]
    all_to_all x1 -> x0, starting transfers between devices: 12.5 us -> none  [per_device(): terms = lax.all_to_all(product(w_out, w_unembed), 'tp', 0, 0, tiled=True)]
    ppermute x1, starting transfers between devices: 13.1 us -> 3.7 us  [per_device(): far = lax.ppermute(logits, 'tp', [(i, i ^ 4) for i in range(8)])]
    ppermute x1, starting transfers between devices: 8.21 us -> 15.7 us  [per_device(): far = lax.ppermute(near, 'ctx', PERM_Z)]
    all_to_all x1, waiting for transfers between devices: 0.01 us -> 6.85 us  [per_device(): lax.all_to_all(jnp.broadcast_to(near, (4, 384, 128)), 'ctx', 0, 0, axis_i...]
    ppermute x1, waiting for transfers between devices: 5.45 us -> 9.31 us  [per_device(): far = lax.ppermute(logits, 'tp', [(i, i ^ 4) for i in range(8)])]
  transfers between devices with their start and end apart: 18 -> 18, of which waited for: 7 -> 7; matrix products, arithmetic and copies ran while one was open for 3% -> 2% of each run, Pallas kernels for 3% -> 3%
where the time goes in v8:
time: 199 us; the launch traced here: 198 us
  starting transfers between devices  90 us (45%)
  blocking collectives  48.2 us (24%)
  waiting for transfers between devices  36.6 us (18%)
  Pallas kernels  10.5 us (5%)
  local copies, waits for them, and re-layouts  6.8 us (3%)
  other arithmetic  3.35 us (2%)
  matrix products  2.19 us (1%)
    all_to_all x1, blocking collectives, per_device(): lax.all_to_all(logits.reshape(4, 64, 512), 'tp', 0, 0, axis_index_groups=...  28.7 us
    ppermute x1, starting transfers between devices, per_device(): far = lax.ppermute(near, 'ctx', PERM_Z)  15.7 us
    ppermute x2, starting transfers between devices, per_device(): terms = [lax.ppermute(term, ('ctx', 'tp'), route) for route in ROUTES]  15.2 us
    all_to_all x1, blocking collectives, per_device(): lax.all_to_all(signal, 'ctx', 0, 0, axis_index_groups=GROUPS_CORE, tiled=...  11.6 us
    ppermute x3, starting transfers between devices, per_device(): fars = [far] + [lax.ppermute(far, 'ctx', PERM_X[k]) for k in (1, 2, 3)]  11 us
    ppermute x3, starting transfers between devices, per_device(): lax.ppermute(far, 'ctx', PERM_Y[k])  10.9 us
    pallas_call x5, Pallas kernels, call(): pl.pallas_call(kernel, out_shape=outs, in_specs=specs, out_specs=jax.tree...  10.5 us
    ppermute x1, waiting for transfers between devices, per_device(): far = lax.ppermute(logits, 'tp', [(i, i ^ 4) for i in range(8)])  9.31 us
  transfers between devices with their start and end apart: 18, of which 7 were waited for; matrix products, arithmetic and copies ran while one was open for 2% of the time, Pallas kernels for 3%

profile of v8, /device:TPU:6, one launch (start us, length us, event | category | flops | bytes accessed | tf_op | source)
XLA Modules:
  0.0 198.2 jit_solution(6931146274543876026)
XLA Ops:
  0.0 2.0 %collective-permute-start = (bf16[3,64,256]{2,1,0:T(8,128)(2,1)}, bf16[3,64,256]{2,1,0:T(8,128)(2,1)S(1)}, u32[]{:S(2)}, u32[]{:S(2)}) collective-permute-start(bf16[3,64,256]{2,1,0:T(8,128)(2,1)} %bitcast.39), channel_id=1, source_target_pairs={{0,8},{8,0},{16,24},{24,16},{32,40},{40,32},{48,56},{56,48},{64,72... | collective-permute-start | bytes 294920 | tf_op jit(solution)/shard_map/ppermute | solution.py:277
  4.4 2.1 %collective-permute-start.1 = (bf16[256,4096]{1,0:T(8,128)(2,1)}, bf16[256,4096]{1,0:T(8,128)(2,1)S(1)}, u32[]{:S(2)}, u32[]{:S(2)}) collective-permute-start(bf16[256,4096]{1,0:T(8,128)(2,1)} %own_ref.1), channel_id=1, source_target_pairs={{0,8},{8,0},{16,24},{24,16},{32,40},{40,32},{48,56},{56,48},{64,72... | collective-permute-start | bytes 6291464 | tf_op jit(solution)/shard_map/ppermute | solution.py:281
  6.4 15.7 %collective-permute-start.2 = (bf16[384,128]{1,0:T(8,128)(2,1)S(1)}, bf16[384,128]{1,0:T(8,128)(2,1)S(1)}, u32[]{:S(2)}, u32[]{:S(2)}) collective-permute-start(bf16[384,128]{1,0:T(8,128)(2,1)S(1)} %bitcast.30), channel_id=1, source_target_pairs={{0,256},{8,264},{16,272},{24,280},{32,288},{40,296},{48,304},{56,3... | collective-permute-start | bytes 294920 | tf_op jit(solution)/shard_map/ppermute | solution.py:282
  22.2 3.6 %collective-permute-done.2 = bf16[384,128]{1,0:T(8,128)(2,1)S(1)} collective-permute-done((bf16[384,128]{1,0:T(8,128)(2,1)S(1)}, bf16[384,128]{1,0:T(8,128)(2,1)S(1)}, u32[]{:S(2)}, u32[]{:S(2)}) %collective-permute-start.2) | collective-permute-done | bytes 98336 | tf_op jit(solution)/shard_map/ppermute | solution.py:282
  25.8 4.9 %collective-permute-start.5 = (bf16[384,128]{1,0:T(8,128)(2,1)S(1)}, bf16[384,128]{1,0:T(8,128)(2,1)S(1)}, u32[]{:S(2)}, u32[]{:S(2)}) collective-permute-start(bf16[384,128]{1,0:T(8,128)(2,1)S(1)} %collective-permute-done.2), channel_id=1, source_target_pairs={{0,192},{8,200},{16,208},{24,216},{32,224},{40,232},{48,240},{56,2... | collective-permute-start | bytes 294920 | tf_op jit(solution)/shard_map/ppermute | solution.py:291
  30.7 1.9 collective-permute-start.3
  32.6 4.1 %collective-permute-start.4 = (bf16[384,128]{1,0:T(8,128)(2,1)S(1)}, bf16[384,128]{1,0:T(8,128)(2,1)S(1)}, u32[]{:S(2)}, u32[]{:S(2)}) collective-permute-start(bf16[384,128]{1,0:T(8,128)(2,1)S(1)} %collective-permute-done.2), channel_id=1, source_target_pairs={{0,128},{8,136},{16,144},{24,152},{32,160},{40,168},{48,176},{56,1... | collective-permute-start | bytes 294920 | tf_op jit(solution)/shard_map/ppermute | solution.py:291
  39.0 1.9 collective-permute-start.6
  40.9 13.3 %collective-permute-start.7 = (bf16[128,128]{1,0:T(8,128)(2,1)S(1)}, bf16[128,128]{1,0:T(8,128)(2,1)S(1)}, u32[]{:S(2)}, u32[]{:S(2)}) collective-permute-start(bf16[128,128]{1,0:T(8,128)(2,1)S(1)} %bitcast.38), channel_id=1, source_target_pairs={{0,256},{1,0},{2,320},{3,64},{4,384},{5,128},{6,448},{7,192},{8,27... | collective-permute-start | bytes 98312 | tf_op jit(solution)/shard_map/ppermute | solution.py:286
  55.0 7.4 %all-to-all-start = ((bf16[4,384,128]{2,1,0:T(8,128)(2,1)}), bf16[4,384,128]{2,1,0:T(8,128)(2,1)S(1)}, u32[]{:S(2)}, u32[]{:S(2)}) async-start(bf16[4,384,128]{2,1,0:T(8,128)(2,1)} %broadcast_in_dim.22), calls=%async_computation | async-start | bytes 786432 | tf_op jit(solution)/shard_map/all_to_all | solution.py:287
  62.5 6.9 %all-to-all-done = bf16[4,384,128]{2,1,0:T(8,128)(2,1)S(1)} async-done(((bf16[4,384,128]{2,1,0:T(8,128)(2,1)}), bf16[4,384,128]{2,1,0:T(8,128)(2,1)S(1)}, u32[]{:S(2)}, u32[]{:S(2)}) %all-to-all-start) | async-done | bytes 393248 | tf_op jit(solution)/shard_map/all_to_all | solution.py:287
  70.8 5.7 %all-to-all-start.1 = ((bf16[4,1568,128]{2,1,0:T(8,128)(2,1)}), bf16[4,1568,128]{2,1,0:T(8,128)(2,1)S(1)}, u32[]{:S(2)}, u32[]{:S(2)}) async-start(bf16[4,1568,128]{2,1,0:T(8,128)(2,1)} %pad_maximum_fusion), calls=%async_computation.1 | async-start | bytes 3211264 | tf_op jit(solution)/shard_map/all_to_all | solution.py:296
  76.5 4.0 %collective-permute-start.10 = (bf16[4,384,128]{2,1,0:T(8,128)(2,1)S(1)}, bf16[4,384,128]{2,1,0:T(8,128)(2,1)S(1)}, u32[]{:S(2)}, u32[]{:S(2)}) collective-permute-start(bf16[4,384,128]{2,1,0:T(8,128)(2,1)S(1)} %pad_maximum_fusion.1.f0), channel_id=1, source_target_pairs={{0,32},{8,40},{16,48},{24,56},{32,0},{40,8},{48,16},{56,24},{64,96... | collective-permute-start | bytes 1179656 | tf_op jit(solution)/shard_map/ppermute | solution.py:297
  80.5 2.8 %collective-permute-start.11 = (bf16[4,384,128]{2,1,0:T(8,128)(2,1)S(1)}, bf16[4,384,128]{2,1,0:T(8,128)(2,1)S(1)}, u32[]{:S(2)}, u32[]{:S(2)}) collective-permute-start(bf16[4,384,128]{2,1,0:T(8,128)(2,1)S(1)} %pad_maximum_fusion.1.f0), channel_id=1, source_target_pairs={{0,48},{8,56},{16,0},{24,8},{32,16},{40,24},{48,32},{56,40},{64,11... | collective-permute-start | bytes 1179656 | tf_op jit(solution)/shard_map/ppermute | solution.py:297
  83.2 4.3 %collective-permute-start.9 = (bf16[4,384,128]{2,1,0:T(8,128)(2,1)S(1)}, bf16[4,384,128]{2,1,0:T(8,128)(2,1)}, u32[]{:S(2)}, u32[]{:S(2)}) collective-permute-start(bf16[4,384,128]{2,1,0:T(8,128)(2,1)S(1)} %pad_maximum_fusion.1.f0), channel_id=1, source_target_pairs={{0,16},{8,24},{16,32},{24,40},{32,48},{40,56},{48,0},{56,8},{64,80... | collective-permute-start | bytes 1179656 | tf_op jit(solution)/shard_map/ppermute | solution.py:297
  87.6 1.9 collective-permute-start.8
  89.6 7.8 %all-to-all-done.1.near_ref = bf16[4,1568,128]{2,1,0:T(8,128)(2,1)S(1)} async-done(((bf16[4,1568,128]{2,1,0:T(8,128)(2,1)}), bf16[4,1568,128]{2,1,0:T(8,128)(2,1)S(1)}, u32[]{:S(2)}, u32[]{:S(2)}) %all-to-all-start.1) | async-done | bytes 1605664 | tf_op jit(solution)/shard_map/all_to_all | solution.py:296
  97.5 1.6 copy-done.1
  99.1 1.6 copy-done.3
  100.7 4.4 %shard_map.118 = (bf16[2,256,4096]{2,1,0:T(8,128)(2,1)S(1)}, f32[2,256,128]{2,1,0:T(8,128)S(1)}, f32[2,256,384]{2,1,0:T(8,128)S(1)}, bf16[32,128]{1,0:T(8,128)(2,1)S(1)}) custom-call(s32[4]{0:T(128)S(1)} %pad_add_fusion.at_ref, bf16[256,4096]{1,0:T(8,128)(2,1)S(1)} %copy-done.1, bf16[256,4096]{1,0:T(8,128)(2,1)S(1)} %copy-done.3, ...), custom_call_target="tpu_custom_call" | custom-call | flops 800000000 | bytes 4194304 | tf_op jit(solution)/shard_map/pallas_call | solution.py:221
  105.1 2.5 %shard_map.119 = (bf16[16,64,128]{2,1,0:T(8,128)(2,1)S(1)}, bf16[2,2,128,128]{3,2,1,0:T(8,128)(2,1)S(1)}) custom-call(s32[4]{0:T(128)S(1)} %pad_add_fusion.at_ref, bf16[2,256,4096]{2,1,0:T(8,128)(2,1)S(1)} %get-tuple-element.29.gained_ref, f32[2,256,128]{2,1,0:T(8,128)S(1)} %get-tuple-element.30.scale_ref, f32[2,256,384]{2,1,0:T(8,128)S(1)} %get-tuple-element.31.near_ref, ...), custom_call_target="tpu_custom_call" | custom-call | flops 800000000 | bytes 4194304 | tf_op jit(solution)/shard_map/pallas_call | solution.py:221
  107.6 11.6 %all_to_all.31.got_ref = bf16[16,64,128]{2,1,0:T(8,128)(2,1)S(1)} all-to-all(bf16[16,64,128]{2,1,0:T(8,128)(2,1)S(1)} %get-tuple-element.34), channel_id=1, replica_groups={{0,16,32,48,64,80,96,112,128,144,160,176,192,208,224,240},{8,24,40,56,7..., dimensions={0} | all-to-all | bytes 524288 | tf_op jit(solution)/shard_map/all_to_all | solution.py:316
  119.2 6.1 %collective-permute-start.12 = (bf16[16,64,128]{2,1,0:T(8,128)(2,1)S(1)}, bf16[16,64,128]{2,1,0:T(8,128)(2,1)S(1)}, u32[]{:S(2)}, u32[]{:S(2)}) collective-permute-start(bf16[16,64,128]{2,1,0:T(8,128)(2,1)S(1)} %all_to_all.31.got_ref), channel_id=1, source_target_pairs={{0,256},{8,264},{16,272},{24,280},{32,288},{40,296},{48,304},{56,3... | collective-permute-start | bytes 786440 | tf_op jit(solution)/shard_map/ppermute | solution.py:317
  126.3 2.8 %collective-permute-done.12.before_ref = bf16[16,64,128]{2,1,0:T(8,128)(2,1)S(1)} collective-permute-done((bf16[16,64,128]{2,1,0:T(8,128)(2,1)S(1)}, bf16[16,64,128]{2,1,0:T(8,128)(2,1)S(1)}, u32[]{:S(2)}, u32[]{:S(2)}) %collective-permute-start.12) | collective-permute-done | bytes 262176 | tf_op jit(solution)/shard_map/ppermute | solution.py:317
  129.2 2.3 %shard_map.121 = bf16[32,48,128]{2,1,0:T(8,128)(2,1)} custom-call(s32[1]{0:T(128)} %bitcast.1.z_ref, f32[1024,256]{1,0:T(8,128)S(1)} %get-tuple-element.35.signal_ref, f32[1024,256]{1,0:T(8,128)S(1)} %get-tuple-element.36.filter_ref, bf16[16,64,128]{2,1,0:T(8,128)(2,1)S(1)} %collective-permute-done.12.before_ref, ...), custom_call_target="tpu_custom_call" | custom-call | flops 600000000 | bytes 4194304 | tf_op jit(solution)/shard_map/pallas_call | solution.py:221
  131.5 6.2 %all-to-all-start.3 = ((bf16[32,48,128]{2,1,0:T(8,128)(2,1)}), bf16[32,48,128]{2,1,0:T(8,128)(2,1)S(1)}, u32[]{:S(2)}, u32[]{:S(2)}) async-start(bf16[32,48,128]{2,1,0:T(8,128)(2,1)} %shard_map.121), calls=%async_computation.3 | async-start | bytes 786432 | tf_op jit(solution)/shard_map/all_to_all | solution.py:322
  137.7 2.1 %collective-permute-start.13 = (bf16[2,128,128]{2,1,0:T(8,128)(2,1)S(1)}, bf16[2,128,128]{2,1,0:T(8,128)(2,1)S(1)}, u32[]{:S(2)}, u32[]{:S(2)}) collective-permute-start(bf16[2,128,128]{2,1,0:T(8,128)(2,1)S(1)} %get-tuple-element.43), channel_id=1, source_target_pairs={{0,8},{8,0},{16,24},{24,16},{32,40},{40,32},{48,56},{56,48},{64,72... | collective-permute-start | bytes 196616 | tf_op jit(solution)/shard_map/ppermute | solution.py:319
  141.1 4.7 %all-to-all-done.3.got_ref = bf16[32,48,128]{2,1,0:T(8,128)(2,1)S(1)} async-done(((bf16[32,48,128]{2,1,0:T(8,128)(2,1)}), bf16[32,48,128]{2,1,0:T(8,128)(2,1)S(1)}, u32[]{:S(2)}, u32[]{:S(2)}) %all-to-all-start.3) | async-done | bytes 393248 | tf_op jit(solution)/shard_map/all_to_all | solution.py:322
  146.2 28.7 %all_to_all.32 = bf16[4,64,512]{2,1,0:T(8,128)(2,1)S(1)} all-to-all(bf16[4,64,512]{2,1,0:T(8,128)(2,1)S(1)} %bitcast.28), channel_id=1, replica_groups={{0,1,2,3},{4,5,6,7},{8,9,10,11},{12,13,14,15},{16,17,18,19},{20,21,22,2..., dimensions={0} | all-to-all | bytes 524288 | tf_op jit(solution)/shard_map/all_to_all | solution.py:334
  174.9 3.7 %collective-permute-start.14 = (bf16[64,512]{1,0:T(8,128)(2,1)S(1)}, bf16[64,512]{1,0:T(8,128)(2,1)S(1)}, u32[]{:S(2)}, u32[]{:S(2)}) collective-permute-start(bf16[64,512]{1,0:T(8,128)(2,1)S(1)} %reduce_sum.30), channel_id=1, source_target_pairs={{0,4},{1,5},{2,6},{3,7},{4,0},{5,1},{6,2},{7,3},{8,12},{9,13},{10,... | collective-permute-start | bytes 196616 | tf_op jit(solution)/shard_map/ppermute | solution.py:336
  178.7 9.3 %collective-permute-done.14 = bf16[64,512]{1,0:T(8,128)(2,1)S(1)} collective-permute-done((bf16[64,512]{1,0:T(8,128)(2,1)S(1)}, bf16[64,512]{1,0:T(8,128)(2,1)S(1)}, u32[]{:S(2)}, u32[]{:S(2)}) %collective-permute-start.14) | collective-permute-done | bytes 65568 | tf_op jit(solution)/shard_map/ppermute | solution.py:336
  188.5 7.9 %all_to_all.33 = f32[4,1,64]{2,1,0:T(1,128)S(1)} all-to-all(f32[4,1,64]{2,1,0:T(1,128)S(1)} %broadcast_in_dim.26), channel_id=1, replica_groups={{0,1,2,3},{4,5,6,7},{8,9,10,11},{12,13,14,15},{16,17,18,19},{20,21,22,2..., dimensions={0} | all-to-all | bytes 2048 | tf_op jit(solution)/shard_map/all_to_all | solution.py:347
  (53 shorter events, 12.0 us)
Async XLA Ops:
  0.0 38.1 %copy-start = (bf16[512,512]{1,0:T(8,128)(2,1)S(1)}, bf16[512,512]{1,0:T(8,128)(2,1)}, u32[]{:S(2)}) copy-start(bf16[512,512]{1,0:T(8,128)(2,1)} %param.17) | copy-start | bytes 1572868
  0.0 3.5 %collective-permute-start = (bf16[3,64,256]{2,1,0:T(8,128)(2,1)}, bf16[3,64,256]{2,1,0:T(8,128)(2,1)S(1)}, u32[]{:S(2)}, u32[]{:S(2)}) collective-permute-start(bf16[3,64,256]{2,1,0:T(8,128)(2,1)} %bitcast.39), channel_id=1, source_target_pairs={{0,8},{8,0},{16,24},{24,16},{32,40},{40,32},{48,56},{56,48},{64,72... | collective-permute-start | bytes 294920 | tf_op jit(solution)/shard_map/ppermute | solution.py:277
  4.4 32.4 %collective-permute-start.1 = (bf16[256,4096]{1,0:T(8,128)(2,1)}, bf16[256,4096]{1,0:T(8,128)(2,1)S(1)}, u32[]{:S(2)}, u32[]{:S(2)}) collective-permute-start(bf16[256,4096]{1,0:T(8,128)(2,1)} %own_ref.1), channel_id=1, source_target_pairs={{0,8},{8,0},{16,24},{24,16},{32,40},{40,32},{48,56},{56,48},{64,72... | collective-permute-start | bytes 6291464 | tf_op jit(solution)/shard_map/ppermute | solution.py:281
  6.4 19.3 %collective-permute-start.2 = (bf16[384,128]{1,0:T(8,128)(2,1)S(1)}, bf16[384,128]{1,0:T(8,128)(2,1)S(1)}, u32[]{:S(2)}, u32[]{:S(2)}) collective-permute-start(bf16[384,128]{1,0:T(8,128)(2,1)S(1)} %bitcast.30), channel_id=1, source_target_pairs={{0,256},{8,264},{16,272},{24,280},{32,288},{40,296},{48,304},{56,3... | collective-permute-start | bytes 294920 | tf_op jit(solution)/shard_map/ppermute | solution.py:282
  25.8 36.6 %collective-permute-start.5 = (bf16[384,128]{1,0:T(8,128)(2,1)S(1)}, bf16[384,128]{1,0:T(8,128)(2,1)S(1)}, u32[]{:S(2)}, u32[]{:S(2)}) collective-permute-start(bf16[384,128]{1,0:T(8,128)(2,1)S(1)} %collective-permute-done.2), channel_id=1, source_target_pairs={{0,192},{8,200},{16,208},{24,216},{32,224},{40,232},{48,240},{56,2... | collective-permute-start | bytes 294920 | tf_op jit(solution)/shard_map/ppermute | solution.py:291
  30.7 31.7 %collective-permute-start.3 = (bf16[384,128]{1,0:T(8,128)(2,1)S(1)}, bf16[384,128]{1,0:T(8,128)(2,1)S(1)}, u32[]{:S(2)}, u32[]{:S(2)}) collective-permute-start(bf16[384,128]{1,0:T(8,128)(2,1)S(1)} %collective-permute-done.2), channel_id=1, source_target_pairs={{0,64},{8,72},{16,80},{24,88},{32,96},{40,104},{48,112},{56,120},{... | collective-permute-start | bytes 294920 | tf_op jit(solution)/shard_map/ppermute | solution.py:291
  32.6 29.8 %collective-permute-start.4 = (bf16[384,128]{1,0:T(8,128)(2,1)S(1)}, bf16[384,128]{1,0:T(8,128)(2,1)S(1)}, u32[]{:S(2)}, u32[]{:S(2)}) collective-permute-start(bf16[384,128]{1,0:T(8,128)(2,1)S(1)} %collective-permute-done.2), channel_id=1, source_target_pairs={{0,128},{8,136},{16,144},{24,152},{32,160},{40,168},{48,176},{56,1... | collective-permute-start | bytes 294920 | tf_op jit(solution)/shard_map/ppermute | solution.py:291
  36.7 1.3 copy-start.2
  39.0 23.4 %collective-permute-start.6 = (bf16[128,128]{1,0:T(8,128)(2,1)S(1)}, bf16[128,128]{1,0:T(8,128)(2,1)S(1)}, u32[]{:S(2)}, u32[]{:S(2)}) collective-permute-start(bf16[128,128]{1,0:T(8,128)(2,1)S(1)} %bitcast.37), channel_id=1, source_target_pairs={{0,0},{1,256},{2,64},{3,320},{4,128},{5,384},{6,192},{7,448},{8,16... | collective-permute-start | bytes 98312 | tf_op jit(solution)/shard_map/ppermute | solution.py:286
  40.9 21.5 %collective-permute-start.7 = (bf16[128,128]{1,0:T(8,128)(2,1)S(1)}, bf16[128,128]{1,0:T(8,128)(2,1)S(1)}, u32[]{:S(2)}, u32[]{:S(2)}) collective-permute-start(bf16[128,128]{1,0:T(8,128)(2,1)S(1)} %bitcast.38), channel_id=1, source_target_pairs={{0,256},{1,0},{2,320},{3,64},{4,384},{5,128},{6,448},{7,192},{8,27... | collective-permute-start | bytes 98312 | tf_op jit(solution)/shard_map/ppermute | solution.py:286
  55.0 14.3 %all-to-all-start = ((bf16[4,384,128]{2,1,0:T(8,128)(2,1)}), bf16[4,384,128]{2,1,0:T(8,128)(2,1)S(1)}, u32[]{:S(2)}, u32[]{:S(2)}) async-start(bf16[4,384,128]{2,1,0:T(8,128)(2,1)} %broadcast_in_dim.22), calls=%async_computation | async-start | bytes 786432 | tf_op jit(solution)/shard_map/all_to_all | solution.py:287
  70.8 16.8 %copy-start.5 = (bf16[256,256]{1,0:T(8,128)(2,1)S(1)}, bf16[256,256]{1,0:T(8,128)(2,1)}, u32[]{:S(2)}) copy-start(bf16[256,256]{1,0:T(8,128)(2,1)} %own_taps) | copy-start | bytes 393220
  70.8 18.8 %copy-start.7 = (bf16[4096]{0:T(1024)(128)(2,1)S(1)}, bf16[4096]{0:T(1024)(128)(2,1)}, u32[]{:S(2)}) copy-start(bf16[4096]{0:T(1024)(128)(2,1)} %param.13) | copy-start | bytes 24580
  70.8 26.7 %all-to-all-start.1 = ((bf16[4,1568,128]{2,1,0:T(8,128)(2,1)}), bf16[4,1568,128]{2,1,0:T(8,128)(2,1)S(1)}, u32[]{:S(2)}, u32[]{:S(2)}) async-start(bf16[4,1568,128]{2,1,0:T(8,128)(2,1)} %pad_maximum_fusion), calls=%async_computation.1 | async-start | bytes 3211264 | tf_op jit(solution)/shard_map/all_to_all | solution.py:296
  76.5 28.5 %collective-permute-start.10 = (bf16[4,384,128]{2,1,0:T(8,128)(2,1)S(1)}, bf16[4,384,128]{2,1,0:T(8,128)(2,1)S(1)}, u32[]{:S(2)}, u32[]{:S(2)}) collective-permute-start(bf16[4,384,128]{2,1,0:T(8,128)(2,1)S(1)} %pad_maximum_fusion.1.f0), channel_id=1, source_target_pairs={{0,32},{8,40},{16,48},{24,56},{32,0},{40,8},{48,16},{56,24},{64,96... | collective-permute-start | bytes 1179656 | tf_op jit(solution)/shard_map/ppermute | solution.py:297
  80.5 24.5 %collective-permute-start.11 = (bf16[4,384,128]{2,1,0:T(8,128)(2,1)S(1)}, bf16[4,384,128]{2,1,0:T(8,128)(2,1)S(1)}, u32[]{:S(2)}, u32[]{:S(2)}) collective-permute-start(bf16[4,384,128]{2,1,0:T(8,128)(2,1)S(1)} %pad_maximum_fusion.1.f0), channel_id=1, source_target_pairs={{0,48},{8,56},{16,0},{24,8},{32,16},{40,24},{48,32},{56,40},{64,11... | collective-permute-start | bytes 1179656 | tf_op jit(solution)/shard_map/ppermute | solution.py:297
  83.2 21.8 %collective-permute-start.9 = (bf16[4,384,128]{2,1,0:T(8,128)(2,1)S(1)}, bf16[4,384,128]{2,1,0:T(8,128)(2,1)}, u32[]{:S(2)}, u32[]{:S(2)}) collective-permute-start(bf16[4,384,128]{2,1,0:T(8,128)(2,1)S(1)} %pad_maximum_fusion.1.f0), channel_id=1, source_target_pairs={{0,16},{8,24},{16,32},{24,40},{32,48},{40,56},{48,0},{56,8},{64,80... | collective-permute-start | bytes 1179656 | tf_op jit(solution)/shard_map/ppermute | solution.py:297
  87.6 17.4 %collective-permute-start.8 = (bf16[256,256]{1,0:T(8,128)(2,1)S(1)}, bf16[256,256]{1,0:T(8,128)(2,1)}, u32[]{:S(2)}, u32[]{:S(2)}) collective-permute-start(bf16[256,256]{1,0:T(8,128)(2,1)S(1)} %copy-done.5), channel_id=1, source_target_pairs={{0,8},{8,0},{16,24},{24,16},{32,40},{40,32},{48,56},{56,48},{64,72... | collective-permute-start | bytes 393224 | tf_op jit(solution)/shard_map/ppermute | solution.py:284
  97.5 1.6 copy-start.1
  99.1 1.6 copy-start.3
  105.0 20.3 %copy-start.4 = (bf16[832,256]{1,0:T(8,128)(2,1)S(1)}, bf16[832,256]{1,0:T(8,128)(2,1)}, u32[]{:S(2)}) copy-start(bf16[832,256]{1,0:T(8,128)(2,1)} %constant.103.clone.matrices) | copy-start | bytes 1277956
  105.1 20.3 %copy-start.6 = (f32[128,256]{1,0:T(8,128)S(1)}, f32[128,256]{1,0:T(8,128)}, u32[]{:S(2)}) copy-start(f32[128,256]{1,0:T(8,128)} %constant.104.clone.twiddles) | copy-start | bytes 393220
  119.2 9.9 %collective-permute-start.12 = (bf16[16,64,128]{2,1,0:T(8,128)(2,1)S(1)}, bf16[16,64,128]{2,1,0:T(8,128)(2,1)S(1)}, u32[]{:S(2)}, u32[]{:S(2)}) collective-permute-start(bf16[16,64,128]{2,1,0:T(8,128)(2,1)S(1)} %all_to_all.31.got_ref), channel_id=1, source_target_pairs={{0,256},{8,264},{16,272},{24,280},{32,288},{40,296},{48,304},{56,3... | collective-permute-start | bytes 786440 | tf_op jit(solution)/shard_map/ppermute | solution.py:317
  131.5 47.2 %copy-start.9 = (s32[256]{0:T(256)S(1)}, s32[256]{0:T(256)}, u32[]{:S(2)}) copy-start(s32[256]{0:T(256)} %param.18) | copy-start | bytes 3076
  131.5 14.3 %all-to-all-start.3 = ((bf16[32,48,128]{2,1,0:T(8,128)(2,1)}), bf16[32,48,128]{2,1,0:T(8,128)(2,1)S(1)}, u32[]{:S(2)}, u32[]{:S(2)}) async-start(bf16[32,48,128]{2,1,0:T(8,128)(2,1)} %shard_map.121), calls=%async_computation.3 | async-start | bytes 786432 | tf_op jit(solution)/shard_map/all_to_all | solution.py:322
  137.7 50.7 %copy-start.8 = (s32[256]{0:T(256)S(1)}, s32[256]{0:T(256)}, u32[]{:S(2)}) copy-start(s32[256]{0:T(256)} %param.19) | copy-start | bytes 3076
  137.7 3.3 %collective-permute-start.13 = (bf16[2,128,128]{2,1,0:T(8,128)(2,1)S(1)}, bf16[2,128,128]{2,1,0:T(8,128)(2,1)S(1)}, u32[]{:S(2)}, u32[]{:S(2)}) collective-permute-start(bf16[2,128,128]{2,1,0:T(8,128)(2,1)S(1)} %get-tuple-element.43), channel_id=1, source_target_pairs={{0,8},{8,0},{16,24},{24,16},{32,40},{40,32},{48,56},{56,48},{64,72... | collective-permute-start | bytes 196616 | tf_op jit(solution)/shard_map/ppermute | solution.py:319
  174.9 13.1 %collective-permute-start.14 = (bf16[64,512]{1,0:T(8,128)(2,1)S(1)}, bf16[64,512]{1,0:T(8,128)(2,1)S(1)}, u32[]{:S(2)}, u32[]{:S(2)}) collective-permute-start(bf16[64,512]{1,0:T(8,128)(2,1)S(1)} %reduce_sum.30), channel_id=1, source_target_pairs={{0,4},{1,5},{2,6},{3,7},{4,0},{5,1},{6,2},{7,3},{8,12},{9,13},{10,... | collective-permute-start | bytes 196616 | tf_op jit(solution)/shard_map/ppermute | solution.py:336

commit v9 on v8

--- a/solution.py
+++ b/solution.py
@@ -37,19 +37,6 @@
     [ctx_id(z, y, x, c) for y in range(4) for x in range(4)] for z in range(2) for c in range(2)
 ]
 GROUPS_TP = [[0, 1, 2, 3], [4, 5, 6, 7]]
-
-
-def term_route(flip):
-    pairs = []
-    for i in range(64):
-        for j in range(8):
-            to = ctx_id((j % 2) ^ flip, j // 2, i % 4, (i % 8) // 4)
-            pairs.append((i * 8 + j, to * 8 + i // 8))
-    return pairs
-
-
-ROUTES = [term_route(0), term_route(1)]
-BLOCK = [(p % 4) * 4 + p // 4 for p in range(16)]
 
 
 def tables():
@@ -135,7 +122,7 @@
     result = mm(matrices[768:, :], jnp.concatenate(parts, axis=1))
     for c in range(8):
         scratch[pl.ds(c, 64, stride=8), :] = result[:, c * 128 : c * 128 + 128]
-    piece = piece_ref[...]
+    piece = sum(piece_ref[j].astype(F32) for j in range(8)).astype(BF16)
     for d in range(32):
         out_ref[d, :16] = scratch[d * 16 : d * 16 + 16].astype(BF16)
         out_ref[d, 16:] = piece
@@ -145,20 +132,30 @@
     return jnp.concatenate([ref[lead, row + 128 * g : row + 128 * g + 128, :] for g in range(3)], axis=1)
 
 
-def near_kernel(at_ref, own_ref, beside_ref, gain_ref, near_ref, gained_ref, scale_ref, out_ref, piece_ref):
-    start = at_ref[3] * 2048
+def norm_kernel(own_hbm, beside_hbm, gain_ref, gained_ref, scale_ref, tokens, sems):
     gain = gain_ref[...]
-    for part, tokens in enumerate((own_ref, beside_ref)):
-
-        @pl.loop(0, 8)
-        def _(i):
-            rows = pl.ds(pl.multiple_of(i * 32, 32), 32)
-            block = tokens[rows, :]
+    copies = []
+    for part, ref in enumerate((own_hbm, beside_hbm)):
+        for i in range(4):
+            rows = slice(i * 64, i * 64 + 64)
+            copies.append(pltpu.make_async_copy(ref.at[rows], tokens.at[part, rows], sems.at[part, i]))
+    for copy in copies:
+        copy.start()
+    for k, copy in enumerate(copies):
+        copy.wait()
+        part, i = k // 4, k % 4
+        for half in range(2):
+            rows = slice(i * 64 + half * 32, i * 64 + half * 32 + 32)
+            block = tokens[part, rows, :]
             stream = block.astype(F32)
             mean = jnp.mean(stream * stream, axis=1, keepdims=True)
             scale_ref[part, rows, :] = jnp.broadcast_to(lax.rsqrt(mean + NORM_EPS), (32, 128))
             gained_ref[part, rows, :] = block * gain
 
+
+def near_kernel(at_ref, gained_ref, near_ref, out_ref):
+    start = at_ref[3] * 2048
+    for part in range(2):
         total = jnp.zeros((256, 384), F32)
         for y in range(4):
             for x in (0, 2):
@@ -166,13 +163,24 @@
                 right = [weight_block(near_ref, y, x * 384), weight_block(near_ref, y, x * 384 + 384)]
                 total += mm(left, jnp.concatenate(right, axis=0))
         out_ref[part] = total
-    piece_ref[...] = sum(near_ref[y, 1536:, :].astype(F32) for y in range(4)).astype(BF16)
+
+
+def product_kernel(rows_ref, unembed_ref, out_ref):
+    blocks = []
+    for z in range(2):
+        for y in range(4):
+            block = rows_ref[y, 1536 + z * 32 : 1568 + z * 32, :].astype(F32)
+            blocks.append(jnp.concatenate([block[v * 8 : v * 8 + 8] for v in range(4)], axis=1))
+    terms = mm(jnp.concatenate(blocks, axis=0).astype(BF16), unembed_ref[...])
+    for j in range(8):
+        parts = [terms[j * 8 : j * 8 + 8, v * 128 : v * 128 + 128] for v in range(4)]
+        out_ref[j] = jnp.concatenate(parts, axis=0).astype(BF16)
 
 
 def put_pieces(ref, row, place, block):
     first, second = block[:128].T, block[128:].T
     for p in range(16):
-        b = BLOCK[p] * 8
+        b = p * 8
         rows = jnp.concatenate([first[b : b + 8], second[b : b + 8]], axis=0).astype(BF16)
         ref[p, pl.ds(pl.multiple_of(row + place * 16, 16), 16), :] = rows
 
@@ -206,12 +214,13 @@
     for rb in range(2):
         total = base_ref[rb * 128 : rb * 128 + 128, :]
         for c in range(2):
-            cube = jnp.concatenate([conv[BLOCK[b] * 2 + c, rb * 8 : rb * 8 + 8] for b in range(16)], axis=0)
+            cube = jnp.concatenate([conv[b * 2 + c, rb * 8 : rb * 8 + 8] for b in range(16)], axis=0)
             gate = jnp.where(core == c, keep[rb], other[rb])
             mixed = (gate * cube).T.astype(BF16)
             weights = []
             for b in range(16):
-                piece = got_ref[BLOCK[b] * 2 + c, 16:, :].astype(F32)
+                x, holder, y = (c * 16 + b) // 8, b % 8 // 4, b % 4
+                piece = got_ref[(y * 4 + x) * 2 + holder, 16:, :].astype(F32)
                 weights.append(jnp.concatenate([piece[v * 8 : v * 8 + 8] for v in range(4)], axis=1))
             total += mm(mixed, jnp.concatenate(weights, axis=0).astype(BF16))
         out_ref[rb * 128 : rb * 128 + 128, :] = total.astype(BF16)
@@ -263,11 +272,6 @@
     return lax.dynamic_slice_in_dim(array, which * 128, 128, axis)
 
 
-def product(w_out, w_unembed):
-    partial = mm(w_out, w_unembed).astype(BF16).reshape(4, 8, 4, 128)
-    return partial.transpose(0, 2, 1, 3).reshape(128, 128)
-
-
 def per_device(tokens_in, pre_gain, w_in, w_out, long_filter, w_unembed, target_ids, score_mask):
     ctx, tp = lax.axis_index("ctx"), lax.axis_index("tp")
     core, z = ctx % 2, ctx // 32
@@ -277,33 +281,37 @@
     got = half_of(lax.ppermute(w_in, "ctx", PERM_CORE), 2, core)
     keep = half_of(w_in, 2, core)
     near = jnp.concatenate([jnp.where(core == 0, keep, got), jnp.where(core == 0, got, keep)], axis=1)
-    near, tokens = lax.optimization_barrier((near.reshape(384, 128), tokens_in))
+    near, taps = lax.optimization_barrier((near.reshape(384, 128), long_filter))
+    taps_got = lax.ppermute(taps, "ctx", PERM_CORE)
+    rows = w_out.reshape(4, 8, 4, 128).transpose(0, 2, 1, 3).reshape(128, 128)
+    far = lax.ppermute(jnp.concatenate([near, rows]), "ctx", PERM_Z)
+    near, tokens, taps_got = lax.optimization_barrier((near, tokens_in, taps_got))
     beside = lax.ppermute(tokens, "ctx", PERM_CORE)
-    far = lax.ppermute(near, "ctx", PERM_Z)
-    near, w_out, taps, beside = lax.optimization_barrier((near, w_out, long_filter, beside))
-    taps_got = lax.ppermute(taps, "ctx", PERM_CORE)
-    term = product(w_out, w_unembed)
-    terms = [lax.ppermute(term, ("ctx", "tp"), route) for route in ROUTES]
     near = lax.all_to_all(
         jnp.broadcast_to(near, (4, 384, 128)), "ctx", 0, 0, axis_index_groups=GROUPS_X, tiled=True
     )
 
+    rows = by_position(rows.reshape(4, 32, 128), far[384:].reshape(4, 32, 128), z)
+    far = far[:384]
     far = jnp.stack([far] + [lax.ppermute(far, "ctx", PERM_Y[k]) for k in (1, 2, 3)])
-    pieces = (terms[0].astype(F32) + terms[1].astype(F32)).astype(BF16).reshape(4, 32, 128)
-    near, far, pieces = lax.optimization_barrier((near, far, pieces))
-
-    near = jnp.concatenate([jnp.broadcast_to(near.reshape(1, 1536, 128), (4, 1536, 128)), pieces], axis=1)
+    near, far, rows = lax.optimization_barrier((near, far, rows))
+
+    near = jnp.broadcast_to(near.reshape(1, 1536, 128), (4, 1536, 128))
+    near = jnp.concatenate([near, rows[0], rows[1]], axis=1)
     near = lax.all_to_all(near, "ctx", 0, 0, axis_index_groups=GROUPS_Y, tiled=True)
     fars = [far] + [lax.ppermute(far, "ctx", PERM_X[k]) for k in (1, 2, 3)]
 
     at = jnp.stack([(ctx // 8) % 4, (ctx // 2) % 4, core, z]).astype(jnp.int32)
-    gained, scale, sums, piece = call(
-        near_kernel,
-        (shape((2, 256, 4096), BF16), shape((2, 256, 128), F32), shape((2, 256, 384), F32), shape((32, 128), BF16)),
-        [SCALARS] + whole(4),
-        [],
-        8 * 10**8,
-        (at, tokens_in, beside, pre_gain.reshape(1, 4096), near),
+    gained, scale = call(
+        norm_kernel,
+        (shape((2, 256, 4096), BF16), shape((2, 256, 128), F32)),
+        [pl.BlockSpec(memory_space=pl.ANY)] * 2 + whole(1),
+        [pltpu.VMEM((2, 256, 4096), BF16), pltpu.SemaphoreType.DMA((2, 4))],
+        10**7,
+        (tokens_in, beside, pre_gain.reshape(1, 4096)),
+    )
+    sums = call(
+        near_kernel, shape((2, 256, 384), F32), [SCALARS] + whole(2), [], 8 * 10**8, (at, gained, near)
     )
     signal, gate = call(
         proj_kernel,
@@ -315,6 +323,9 @@
     )
     got = lax.all_to_all(signal, "ctx", 0, 0, axis_index_groups=GROUPS_CORE, tiled=True)
     before = lax.ppermute(got, "ctx", PERM_Z_UP)
+    terms = call(product_kernel, shape((8, 32, 128), BF16), whole(2), [], 4 * 10**7, (near, w_unembed))
+    terms, _ = lax.optimization_barrier((terms, got))
+    piece = lax.all_to_all(terms, "tp", 0, 0, tiled=True)
     gate_keep = lax.dynamic_index_in_dim(gate, core, 0, False)
     gate_got = lax.ppermute(lax.dynamic_index_in_dim(gate, 1 - core, 0, False), "ctx", PERM_CORE)
 

time: 199 us -> 182 us (0.915)
  blocking collectives: 48.2 us -> 33.3 us
  local copies, waits for them, and re-layouts: 6.8 us -> 14.3 us
  starting transfers between devices: 90 us -> 83.7 us
  waiting for transfers between devices: 36.6 us -> 32.6 us
    all_to_all x1, blocking collectives: 28.7 us -> 12.7 us  [per_device(): lax.all_to_all(logits.reshape(4, 64, 512), 'tp', 0, 0, axis_index_groups=...]
    ppermute x3 -> x1, starting transfers between devices: 30.9 us -> 15.7 us  [per_device(): far = lax.ppermute(jnp.concatenate([near, rows]), 'ctx', PERM_Z)]
    all_to_all x0 -> x1, starting transfers between devices: none -> 12.4 us  [per_device(): piece = lax.all_to_all(terms, 'tp', 0, 0, tiled=True)]
    all_to_all x0 -> x1, waiting for transfers between devices: none -> 8 us  [per_device(): piece = lax.all_to_all(terms, 'tp', 0, 0, tiled=True)]
    unnamed x20 -> x38, local copies, waits for them, and re-layouts: 4.54 us -> 12 us
    all_to_all x1, waiting for transfers between devices: 6.85 us -> 0.01 us  [per_device(): lax.all_to_all(jnp.broadcast_to(near, (4, 384, 128)), 'ctx', 0, 0, axis_i...]
    ppermute x3 -> x1, waiting for transfers between devices: 3.59 us -> 0.01 us  [per_device(): far = lax.ppermute(jnp.concatenate([near, rows]), 'ctx', PERM_Z)]
    ppermute x3, waiting for transfers between devices: 0.01 us -> 3.22 us  [per_device(): lax.ppermute(far, 'ctx', PERM_Y[k])]
  transfers between devices with their start and end apart: 18 -> 17, of which waited for: 7 -> 7; matrix products, arithmetic and copies ran while one was open for 2% -> 3% of each run, Pallas kernels for 3% -> 3%
where the time goes in v9:
time: 182 us; the launch traced here: 181 us
  starting transfers between devices  83.7 us (46%)
  blocking collectives  33.3 us (18%)
  waiting for transfers between devices  32.6 us (18%)
  local copies, waits for them, and re-layouts  14.3 us (8%)
  Pallas kernels  11.1 us (6%)
  other arithmetic  4.14 us (2%)
    ppermute x1, starting transfers between devices, per_device(): far = lax.ppermute(jnp.concatenate([near, rows]), 'ctx', PERM_Z)  15.7 us
    all_to_all x1, blocking collectives, per_device(): lax.all_to_all(signal, 'ctx', 0, 0, axis_index_groups=GROUPS_CORE, tiled=...  12.8 us
    all_to_all x1, blocking collectives, per_device(): lax.all_to_all(logits.reshape(4, 64, 512), 'tp', 0, 0, axis_index_groups=...  12.7 us
    all_to_all x1, starting transfers between devices, per_device(): piece = lax.all_to_all(terms, 'tp', 0, 0, tiled=True)  12.4 us
    unnamed x38, local copies, waits for them, and re-layouts  12 us
    ppermute x3, starting transfers between devices, per_device(): lax.ppermute(far, 'ctx', PERM_Y[k])  11.6 us
    pallas_call x7, Pallas kernels, call(): pl.pallas_call(kernel, out_shape=outs, in_specs=specs, out_specs=jax.tree...  11.1 us
    ppermute x1, waiting for transfers between devices, per_device(): far = lax.ppermute(logits, 'tp', [(i, i ^ 4) for i in range(8)])  9.68 us
  transfers between devices with their start and end apart: 17, of which 7 were waited for; matrix products, arithmetic and copies ran while one was open for 3% of the time, Pallas kernels for 3%

profile of v9, /device:TPU:6, one launch (start us, length us, event | category | flops | bytes accessed | tf_op | source)
XLA Modules:
  0.0 181.0 jit_solution(32116711003316062)
XLA Ops:
  0.0 2.0 %collective-permute-start = (bf16[3,64,256]{2,1,0:T(8,128)(2,1)}, bf16[3,64,256]{2,1,0:T(8,128)(2,1)S(1)}, u32[]{:S(2)}, u32[]{:S(2)}) collective-permute-start(bf16[3,64,256]{2,1,0:T(8,128)(2,1)} %bitcast.43), channel_id=1, source_target_pairs={{0,8},{8,0},{16,24},{24,16},{32,40},{40,32},{48,56},{56,48},{64,72... | collective-permute-start | bytes 294920 | tf_op jit(solution)/shard_map/ppermute | solution.py:281
  4.4 2.1 %collective-permute-start.1 = (bf16[256,256]{1,0:T(8,128)(2,1)}, bf16[256,256]{1,0:T(8,128)(2,1)S(1)}, u32[]{:S(2)}, u32[]{:S(2)}) collective-permute-start(bf16[256,256]{1,0:T(8,128)(2,1)} %own_taps), channel_id=1, source_target_pairs={{0,8},{8,0},{16,24},{24,16},{32,40},{40,32},{48,56},{56,48},{64,72... | collective-permute-start | bytes 393224 | tf_op jit(solution)/shard_map/ppermute | solution.py:285
  7.2 15.7 %collective-permute-start.3 = (bf16[512,128]{1,0:T(8,128)(2,1)S(1)}, bf16[512,128]{1,0:T(8,128)(2,1)S(1)}, u32[]{:S(2)}, u32[]{:S(2)}) collective-permute-start(bf16[512,128]{1,0:T(8,128)(2,1)S(1)} %pad_maximum_fusion.2), channel_id=1, source_target_pairs={{0,256},{8,264},{16,272},{24,280},{32,288},{40,296},{48,304},{56,3... | collective-permute-start | bytes 393224 | tf_op jit(solution)/shard_map/ppermute | solution.py:287
  23.8 4.8 %all-to-all-start = ((bf16[4,384,128]{2,1,0:T(8,128)(2,1)}), bf16[4,384,128]{2,1,0:T(8,128)(2,1)S(1)}, u32[]{:S(2)}, u32[]{:S(2)}) async-start(bf16[4,384,128]{2,1,0:T(8,128)(2,1)} %broadcast_in_dim.22), calls=%async_computation | async-start | bytes 786432 | tf_op jit(solution)/shard_map/all_to_all | solution.py:290
  28.6 1.9 %collective-permute-start.2 = (bf16[256,4096]{1,0:T(8,128)(2,1)}, bf16[256,4096]{1,0:T(8,128)(2,1)}, u32[]{:S(2)}, u32[]{:S(2)}) collective-permute-start(bf16[256,4096]{1,0:T(8,128)(2,1)} %own_hbm.1), channel_id=1, source_target_pairs={{0,8},{8,0},{16,24},{24,16},{32,40},{40,32},{48,56},{56,48},{64,72... | collective-permute-start | bytes 6291464 | tf_op jit(solution)/shard_map/ppermute | solution.py:289
  30.5 3.5 %collective-permute-start.4 = (bf16[384,128]{1,0:T(8,128)(2,1)S(1)}, bf16[384,128]{1,0:T(8,128)(2,1)S(1)}, u32[]{:S(2)}, u32[]{:S(2)}) collective-permute-start(bf16[384,128]{1,0:T(8,128)(2,1)S(1)} %get-tuple-element.42), channel_id=1, source_target_pairs={{0,64},{8,72},{16,80},{24,88},{32,96},{40,104},{48,112},{56,120},{... | collective-permute-start | bytes 294920 | tf_op jit(solution)/shard_map/ppermute | solution.py:296
  34.0 4.8 %collective-permute-start.5 = (bf16[384,128]{1,0:T(8,128)(2,1)S(1)}, bf16[384,128]{1,0:T(8,128)(2,1)S(1)}, u32[]{:S(2)}, u32[]{:S(2)}) collective-permute-start(bf16[384,128]{1,0:T(8,128)(2,1)S(1)} %get-tuple-element.42), channel_id=1, source_target_pairs={{0,128},{8,136},{16,144},{24,152},{32,160},{40,168},{48,176},{56,1... | collective-permute-start | bytes 294920 | tf_op jit(solution)/shard_map/ppermute | solution.py:296
  38.8 3.3 %collective-permute-start.6 = (bf16[384,128]{1,0:T(8,128)(2,1)S(1)}, bf16[384,128]{1,0:T(8,128)(2,1)S(1)}, u32[]{:S(2)}, u32[]{:S(2)}) collective-permute-start(bf16[384,128]{1,0:T(8,128)(2,1)S(1)} %get-tuple-element.42), channel_id=1, source_target_pairs={{0,192},{8,200},{16,208},{24,216},{32,224},{40,232},{48,240},{56,2... | collective-permute-start | bytes 294920 | tf_op jit(solution)/shard_map/ppermute | solution.py:296
  42.3 3.0 %collective-permute-done.6 = bf16[384,128]{1,0:T(8,128)(2,1)S(1)} collective-permute-done((bf16[384,128]{1,0:T(8,128)(2,1)S(1)}, bf16[384,128]{1,0:T(8,128)(2,1)S(1)}, u32[]{:S(2)}, u32[]{:S(2)}) %collective-permute-start.6) | collective-permute-done | bytes 98336 | tf_op jit(solution)/shard_map/ppermute | solution.py:296
  46.9 4.0 %all-to-all-start.1 = ((bf16[4,1600,128]{2,1,0:T(8,128)(2,1)}), bf16[4,1600,128]{2,1,0:T(8,128)(2,1)S(1)}, u32[]{:S(2)}, u32[]{:S(2)}) async-start(bf16[4,1600,128]{2,1,0:T(8,128)(2,1)} %pad_maximum_fusion), calls=%async_computation.1 | async-start | bytes 3276800 | tf_op jit(solution)/shard_map/all_to_all | solution.py:301
  50.9 1.9 %collective-permute-start.7 = (bf16[4,384,128]{2,1,0:T(8,128)(2,1)S(1)}, bf16[4,384,128]{2,1,0:T(8,128)(2,1)S(1)}, u32[]{:S(2)}, u32[]{:S(2)}) collective-permute-start(bf16[4,384,128]{2,1,0:T(8,128)(2,1)S(1)} %pad_maximum_fusion.1.f0), channel_id=1, source_target_pairs={{0,16},{8,24},{16,32},{24,40},{32,48},{40,56},{48,0},{56,8},{64,80... | collective-permute-start | bytes 1179656 | tf_op jit(solution)/shard_map/ppermute | solution.py:302
  52.8 4.8 %collective-permute-start.8 = (bf16[4,384,128]{2,1,0:T(8,128)(2,1)S(1)}, bf16[4,384,128]{2,1,0:T(8,128)(2,1)S(1)}, u32[]{:S(2)}, u32[]{:S(2)}) collective-permute-start(bf16[4,384,128]{2,1,0:T(8,128)(2,1)S(1)} %pad_maximum_fusion.1.f0), channel_id=1, source_target_pairs={{0,32},{8,40},{16,48},{24,56},{32,0},{40,8},{48,16},{56,24},{64,96... | collective-permute-start | bytes 1179656 | tf_op jit(solution)/shard_map/ppermute | solution.py:302
  57.6 1.9 %collective-permute-start.9 = (bf16[4,384,128]{2,1,0:T(8,128)(2,1)S(1)}, bf16[4,384,128]{2,1,0:T(8,128)(2,1)S(1)}, u32[]{:S(2)}, u32[]{:S(2)}) collective-permute-start(bf16[4,384,128]{2,1,0:T(8,128)(2,1)S(1)} %pad_maximum_fusion.1.f0), channel_id=1, source_target_pairs={{0,48},{8,56},{16,0},{24,8},{32,16},{40,24},{48,32},{56,40},{64,11... | collective-permute-start | bytes 1179656 | tf_op jit(solution)/shard_map/ppermute | solution.py:302
  59.8 1.6 copy-done.2
  61.3 2.1 %shard_map.118 = (bf16[2,256,4096]{2,1,0:T(8,128)(2,1)S(1)}, f32[2,256,128]{2,1,0:T(8,128)S(1)}) custom-call(bf16[256,4096]{1,0:T(8,128)(2,1)S(1)} %copy-done.2, bf16[256,4096]{1,0:T(8,128)(2,1)} %collective-permute-done.2.beside_hbm, bf16[1,4096]{1,0:T(2,128)(2,1)S(1)} %reshape.38.gain_ref), custom_call_target="tpu_custom_call" | custom-call | flops 10000000 | bytes 4194304 | tf_op jit(solution)/shard_map/pallas_call | solution.py:230
  63.4 1.9 %copy-done = bf16[2,256,4096]{2,1,0:T(8,128)(2,1)} copy-done((bf16[2,256,4096]{2,1,0:T(8,128)(2,1)}, bf16[2,256,4096]{2,1,0:T(8,128)(2,1)S(1)}, u32[]{:S(2)}) %copy-start) | copy-done | bytes 4194328
  66.1 5.5 %all-to-all-done.1.near_ref.rows_ref = bf16[4,1600,128]{2,1,0:T(8,128)(2,1)S(1)} async-done(((bf16[4,1600,128]{2,1,0:T(8,128)(2,1)}), bf16[4,1600,128]{2,1,0:T(8,128)(2,1)S(1)}, u32[]{:S(2)}, u32[]{:S(2)}) %all-to-all-start.1) | async-done | bytes 1638432 | tf_op jit(solution)/shard_map/all_to_all | solution.py:301
  71.6 2.2 %copy-done.1 = bf16[2,256,4096]{2,1,0:T(8,128)(2,1)S(1)} copy-done((bf16[2,256,4096]{2,1,0:T(8,128)(2,1)S(1)}, bf16[2,256,4096]{2,1,0:T(8,128)(2,1)}, u32[]{:S(2)}) %copy-start.1) | copy-done | bytes 4194328
  73.8 1.8 shard_map.119.near_ref
  77.3 1.9 %shard_map.120 = (bf16[16,64,128]{2,1,0:T(8,128)(2,1)S(1)}, bf16[2,2,128,128]{3,2,1,0:T(8,128)(2,1)S(1)}) custom-call(s32[4]{0:T(128)S(1)} %pad_add_fusion.at_ref, bf16[2,256,4096]{2,1,0:T(8,128)(2,1)S(1)} %copy-done.1, f32[2,256,128]{2,1,0:T(8,128)S(1)} %copy-done.9, f32[2,256,384]{2,1,0:T(8,128)S(1)} %shard_map.119.near_ref, ...), custom_call_target="tpu_custom_call" | custom-call | flops 800000000 | bytes 4194304 | tf_op jit(solution)/shard_map/pallas_call | solution.py:230
  79.3 12.8 %all_to_all.36.got_ref = bf16[16,64,128]{2,1,0:T(8,128)(2,1)S(1)} all-to-all(bf16[16,64,128]{2,1,0:T(8,128)(2,1)S(1)} %get-tuple-element.30), channel_id=1, replica_groups={{0,16,32,48,64,80,96,112,128,144,160,176,192,208,224,240},{8,24,40,56,7..., dimensions={0} | all-to-all | bytes 524288 | tf_op jit(solution)/shard_map/all_to_all | solution.py:324
  92.1 8.7 %collective-permute-start.10 = (bf16[16,64,128]{2,1,0:T(8,128)(2,1)S(1)}, bf16[16,64,128]{2,1,0:T(8,128)(2,1)}, u32[]{:S(2)}, u32[]{:S(2)}) collective-permute-start(bf16[16,64,128]{2,1,0:T(8,128)(2,1)S(1)} %all_to_all.36.got_ref), channel_id=1, source_target_pairs={{0,256},{8,264},{16,272},{24,280},{32,288},{40,296},{48,304},{56,3... | collective-permute-start | bytes 786440 | tf_op jit(solution)/shard_map/ppermute | solution.py:325
  101.7 12.4 %all-to-all-start.3 = ((bf16[8,32,128]{2,1,0:T(8,128)(2,1)}), bf16[8,32,128]{2,1,0:T(8,128)(2,1)S(1)}, u32[]{:S(2)}, u32[]{:S(2)}) async-start(bf16[8,32,128]{2,1,0:T(8,128)(2,1)} %shard_map.122), calls=%async_computation.3 | async-start | bytes 131072 | tf_op jit(solution)/shard_map/all_to_all | solution.py:328
  117.0 8.0 %all-to-all-done.3.piece_ref = bf16[8,32,128]{2,1,0:T(8,128)(2,1)S(1)} async-done(((bf16[8,32,128]{2,1,0:T(8,128)(2,1)}), bf16[8,32,128]{2,1,0:T(8,128)(2,1)S(1)}, u32[]{:S(2)}, u32[]{:S(2)}) %all-to-all-start.3) | async-done | bytes 65568 | tf_op jit(solution)/shard_map/all_to_all | solution.py:328
  126.9 3.2 %shard_map.123 = bf16[32,48,128]{2,1,0:T(8,128)(2,1)} custom-call(s32[1]{0:T(128)} %bitcast.1.z_ref, f32[1024,256]{1,0:T(8,128)S(1)} %get-tuple-element.31.signal_ref, f32[1024,256]{1,0:T(8,128)S(1)} %get-tuple-element.32.filter_ref, bf16[16,64,128]{2,1,0:T(8,128)(2,1)} %collective-permute-done.10.before_ref, ...), custom_call_target="tpu_custom_call" | custom-call | flops 600000000 | bytes 4194304 | tf_op jit(solution)/shard_map/pallas_call | solution.py:230
  130.1 6.2 %all-to-all-start.4 = ((bf16[32,48,128]{2,1,0:T(8,128)(2,1)}), bf16[32,48,128]{2,1,0:T(8,128)(2,1)S(1)}, u32[]{:S(2)}, u32[]{:S(2)}) async-start(bf16[32,48,128]{2,1,0:T(8,128)(2,1)} %shard_map.123), calls=%async_computation.4 | async-start | bytes 786432 | tf_op jit(solution)/shard_map/all_to_all | solution.py:333
  136.4 2.1 %collective-permute-start.11 = (bf16[2,128,128]{2,1,0:T(8,128)(2,1)S(1)}, bf16[2,128,128]{2,1,0:T(8,128)(2,1)S(1)}, u32[]{:S(2)}, u32[]{:S(2)}) collective-permute-start(bf16[2,128,128]{2,1,0:T(8,128)(2,1)S(1)} %get-tuple-element.39), channel_id=1, source_target_pairs={{0,8},{8,0},{16,24},{24,16},{32,40},{40,32},{48,56},{56,48},{64,72... | collective-permute-start | bytes 196616 | tf_op jit(solution)/shard_map/ppermute | solution.py:330
  139.7 4.7 %all-to-all-done.4.got_ref = bf16[32,48,128]{2,1,0:T(8,128)(2,1)S(1)} async-done(((bf16[32,48,128]{2,1,0:T(8,128)(2,1)}), bf16[32,48,128]{2,1,0:T(8,128)(2,1)S(1)}, u32[]{:S(2)}, u32[]{:S(2)}) %all-to-all-start.4) | async-done | bytes 393248 | tf_op jit(solution)/shard_map/all_to_all | solution.py:333
  144.8 12.7 %all_to_all.37 = bf16[4,64,512]{2,1,0:T(8,128)(2,1)S(1)} all-to-all(bf16[4,64,512]{2,1,0:T(8,128)(2,1)S(1)} %bitcast.33), channel_id=1, replica_groups={{0,1,2,3},{4,5,6,7},{8,9,10,11},{12,13,14,15},{16,17,18,19},{20,21,22,2..., dimensions={0} | all-to-all | bytes 524288 | tf_op jit(solution)/shard_map/all_to_all | solution.py:345
  157.5 3.6 %collective-permute-start.12 = (bf16[64,512]{1,0:T(8,128)(2,1)S(1)}, bf16[64,512]{1,0:T(8,128)(2,1)S(1)}, u32[]{:S(2)}, u32[]{:S(2)}) collective-permute-start(bf16[64,512]{1,0:T(8,128)(2,1)S(1)} %reduce_sum.30), channel_id=1, source_target_pairs={{0,4},{1,5},{2,6},{3,7},{4,0},{5,1},{6,2},{7,3},{8,12},{9,13},{10,... | collective-permute-start | bytes 196616 | tf_op jit(solution)/shard_map/ppermute | solution.py:347
  161.2 9.7 %collective-permute-done.12 = bf16[64,512]{1,0:T(8,128)(2,1)S(1)} collective-permute-done((bf16[64,512]{1,0:T(8,128)(2,1)S(1)}, bf16[64,512]{1,0:T(8,128)(2,1)S(1)}, u32[]{:S(2)}, u32[]{:S(2)}) %collective-permute-start.12) | collective-permute-done | bytes 65568 | tf_op jit(solution)/shard_map/ppermute | solution.py:347
  171.3 7.9 %all_to_all.38 = f32[4,1,64]{2,1,0:T(1,128)S(1)} all-to-all(f32[4,1,64]{2,1,0:T(1,128)S(1)} %broadcast_in_dim.26), channel_id=1, replica_groups={{0,1,2,3},{4,5,6,7},{8,9,10,11},{12,13,14,15},{16,17,18,19},{20,21,22,2..., dimensions={0} | all-to-all | bytes 2048 | tf_op jit(solution)/shard_map/all_to_all | solution.py:358
  (74 shorter events, 17.8 us)
Async XLA Ops:
  0.0 42.1 %copy-start.15 = (bf16[32,512]{1,0:T(8,128)(2,1)S(1)}, bf16[32,512]{1,0:T(8,128)(2,1)}, u32[]{:S(2)}) copy-start(bf16[32,512]{1,0:T(8,128)(2,1)} %param.15) | copy-start | bytes 98308
  0.0 3.5 %collective-permute-start = (bf16[3,64,256]{2,1,0:T(8,128)(2,1)}, bf16[3,64,256]{2,1,0:T(8,128)(2,1)S(1)}, u32[]{:S(2)}, u32[]{:S(2)}) collective-permute-start(bf16[3,64,256]{2,1,0:T(8,128)(2,1)} %bitcast.43), channel_id=1, source_target_pairs={{0,8},{8,0},{16,24},{24,16},{32,40},{40,32},{48,56},{56,48},{64,72... | collective-permute-start | bytes 294920 | tf_op jit(solution)/shard_map/ppermute | solution.py:281
  4.4 18.6 %collective-permute-start.1 = (bf16[256,256]{1,0:T(8,128)(2,1)}, bf16[256,256]{1,0:T(8,128)(2,1)S(1)}, u32[]{:S(2)}, u32[]{:S(2)}) collective-permute-start(bf16[256,256]{1,0:T(8,128)(2,1)} %own_taps), channel_id=1, source_target_pairs={{0,8},{8,0},{16,24},{24,16},{32,40},{40,32},{48,56},{56,48},{64,72... | collective-permute-start | bytes 393224 | tf_op jit(solution)/shard_map/ppermute | solution.py:285
  7.2 23.3 %collective-permute-start.3 = (bf16[512,128]{1,0:T(8,128)(2,1)S(1)}, bf16[512,128]{1,0:T(8,128)(2,1)S(1)}, u32[]{:S(2)}, u32[]{:S(2)}) collective-permute-start(bf16[512,128]{1,0:T(8,128)(2,1)S(1)} %pad_maximum_fusion.2), channel_id=1, source_target_pairs={{0,256},{8,264},{16,272},{24,280},{32,288},{40,296},{48,304},{56,3... | collective-permute-start | bytes 393224 | tf_op jit(solution)/shard_map/ppermute | solution.py:287
  23.8 21.6 %all-to-all-start = ((bf16[4,384,128]{2,1,0:T(8,128)(2,1)}), bf16[4,384,128]{2,1,0:T(8,128)(2,1)S(1)}, u32[]{:S(2)}, u32[]{:S(2)}) async-start(bf16[4,384,128]{2,1,0:T(8,128)(2,1)} %broadcast_in_dim.22), calls=%async_computation | async-start | bytes 786432 | tf_op jit(solution)/shard_map/all_to_all | solution.py:290
  28.6 31.2 %collective-permute-start.2 = (bf16[256,4096]{1,0:T(8,128)(2,1)}, bf16[256,4096]{1,0:T(8,128)(2,1)}, u32[]{:S(2)}, u32[]{:S(2)}) collective-permute-start(bf16[256,4096]{1,0:T(8,128)(2,1)} %own_hbm.1), channel_id=1, source_target_pairs={{0,8},{8,0},{16,24},{24,16},{32,40},{40,32},{48,56},{56,48},{64,72... | collective-permute-start | bytes 6291464 | tf_op jit(solution)/shard_map/ppermute | solution.py:289
  30.5 11.6 %collective-permute-start.4 = (bf16[384,128]{1,0:T(8,128)(2,1)S(1)}, bf16[384,128]{1,0:T(8,128)(2,1)S(1)}, u32[]{:S(2)}, u32[]{:S(2)}) collective-permute-start(bf16[384,128]{1,0:T(8,128)(2,1)S(1)} %get-tuple-element.42), channel_id=1, source_target_pairs={{0,64},{8,72},{16,80},{24,88},{32,96},{40,104},{48,112},{56,120},{... | collective-permute-start | bytes 294920 | tf_op jit(solution)/shard_map/ppermute | solution.py:296
  34.0 8.3 %collective-permute-start.5 = (bf16[384,128]{1,0:T(8,128)(2,1)S(1)}, bf16[384,128]{1,0:T(8,128)(2,1)S(1)}, u32[]{:S(2)}, u32[]{:S(2)}) collective-permute-start(bf16[384,128]{1,0:T(8,128)(2,1)S(1)} %get-tuple-element.42), channel_id=1, source_target_pairs={{0,128},{8,136},{16,144},{24,152},{32,160},{40,168},{48,176},{56,1... | collective-permute-start | bytes 294920 | tf_op jit(solution)/shard_map/ppermute | solution.py:296
  38.8 6.5 %collective-permute-start.6 = (bf16[384,128]{1,0:T(8,128)(2,1)S(1)}, bf16[384,128]{1,0:T(8,128)(2,1)S(1)}, u32[]{:S(2)}, u32[]{:S(2)}) collective-permute-start(bf16[384,128]{1,0:T(8,128)(2,1)S(1)} %get-tuple-element.42), channel_id=1, source_target_pairs={{0,192},{8,200},{16,208},{24,216},{32,224},{40,232},{48,240},{56,2... | collective-permute-start | bytes 294920 | tf_op jit(solution)/shard_map/ppermute | solution.py:296
  46.9 12.7 %copy-start.16 = (bf16[4096]{0:T(1024)(128)(2,1)S(1)}, bf16[4096]{0:T(1024)(128)(2,1)}, u32[]{:S(2)}) copy-start(bf16[4096]{0:T(1024)(128)(2,1)} %param.13) | copy-start | bytes 24580
  46.9 24.6 %all-to-all-start.1 = ((bf16[4,1600,128]{2,1,0:T(8,128)(2,1)}), bf16[4,1600,128]{2,1,0:T(8,128)(2,1)S(1)}, u32[]{:S(2)}, u32[]{:S(2)}) async-start(bf16[4,1600,128]{2,1,0:T(8,128)(2,1)} %pad_maximum_fusion), calls=%async_computation.1 | async-start | bytes 3276800 | tf_op jit(solution)/shard_map/all_to_all | solution.py:301
  50.9 24.6 %collective-permute-start.7 = (bf16[4,384,128]{2,1,0:T(8,128)(2,1)S(1)}, bf16[4,384,128]{2,1,0:T(8,128)(2,1)S(1)}, u32[]{:S(2)}, u32[]{:S(2)}) collective-permute-start(bf16[4,384,128]{2,1,0:T(8,128)(2,1)S(1)} %pad_maximum_fusion.1.f0), channel_id=1, source_target_pairs={{0,16},{8,24},{16,32},{24,40},{32,48},{40,56},{48,0},{56,8},{64,80... | collective-permute-start | bytes 1179656 | tf_op jit(solution)/shard_map/ppermute | solution.py:302
  52.8 22.7 %collective-permute-start.8 = (bf16[4,384,128]{2,1,0:T(8,128)(2,1)S(1)}, bf16[4,384,128]{2,1,0:T(8,128)(2,1)S(1)}, u32[]{:S(2)}, u32[]{:S(2)}) collective-permute-start(bf16[4,384,128]{2,1,0:T(8,128)(2,1)S(1)} %pad_maximum_fusion.1.f0), channel_id=1, source_target_pairs={{0,32},{8,40},{16,48},{24,56},{32,0},{40,8},{48,16},{56,24},{64,96... | collective-permute-start | bytes 1179656 | tf_op jit(solution)/shard_map/ppermute | solution.py:302
  57.6 17.9 %collective-permute-start.9 = (bf16[4,384,128]{2,1,0:T(8,128)(2,1)S(1)}, bf16[4,384,128]{2,1,0:T(8,128)(2,1)S(1)}, u32[]{:S(2)}, u32[]{:S(2)}) collective-permute-start(bf16[4,384,128]{2,1,0:T(8,128)(2,1)S(1)} %pad_maximum_fusion.1.f0), channel_id=1, source_target_pairs={{0,48},{8,56},{16,0},{24,8},{32,16},{40,24},{48,32},{56,40},{64,11... | collective-permute-start | bytes 1179656 | tf_op jit(solution)/shard_map/ppermute | solution.py:302
  59.8 1.6 copy-start.2
  63.4 2.0 %copy-start = (bf16[2,256,4096]{2,1,0:T(8,128)(2,1)}, bf16[2,256,4096]{2,1,0:T(8,128)(2,1)S(1)}, u32[]{:S(2)}) copy-start(bf16[2,256,4096]{2,1,0:T(8,128)(2,1)S(1)} %get-tuple-element.23.gained_ref) | copy-start | bytes 12582916
  71.6 2.2 %copy-start.1 = (bf16[2,256,4096]{2,1,0:T(8,128)(2,1)S(1)}, bf16[2,256,4096]{2,1,0:T(8,128)(2,1)}, u32[]{:S(2)}) copy-start(bf16[2,256,4096]{2,1,0:T(8,128)(2,1)} %copy-done) | copy-start | bytes 12582916
  73.7 2.6 %copy-start.9 = (f32[2,256,128]{2,1,0:T(8,128)S(1)}, f32[2,256,128]{2,1,0:T(8,128)}, u32[]{:S(2)}) copy-start(f32[2,256,128]{2,1,0:T(8,128)} %copy-done.8) | copy-start | bytes 786436
  73.8 2.6 %copy-start.10 = (bf16[256,256]{1,0:T(8,128)(2,1)S(1)}, bf16[256,256]{1,0:T(8,128)(2,1)}, u32[]{:S(2)}) copy-start(bf16[256,256]{1,0:T(8,128)(2,1)} %own_taps) | copy-start | bytes 393220
  76.3 1.0 copy-start.7
  77.3 23.5 %copy-start.3 = (bf16[512,512]{1,0:T(8,128)(2,1)S(1)}, bf16[512,512]{1,0:T(8,128)(2,1)}, u32[]{:S(2)}) copy-start(bf16[512,512]{1,0:T(8,128)(2,1)} %unembed_ref.1) | copy-start | bytes 1572868
  79.3 12.8 %copy-start.13 = (bf16[2,2,128,128]{3,2,1,0:T(8,128)(2,1)}, bf16[2,2,128,128]{3,2,1,0:T(8,128)(2,1)S(1)}, u32[]{:S(2)}) copy-start(bf16[2,2,128,128]{3,2,1,0:T(8,128)(2,1)S(1)} %get-tuple-element.34) | copy-start | bytes 393220
  92.1 32.9 %collective-permute-start.10 = (bf16[16,64,128]{2,1,0:T(8,128)(2,1)S(1)}, bf16[16,64,128]{2,1,0:T(8,128)(2,1)}, u32[]{:S(2)}, u32[]{:S(2)}) collective-permute-start(bf16[16,64,128]{2,1,0:T(8,128)(2,1)S(1)} %all_to_all.36.got_ref), channel_id=1, source_target_pairs={{0,256},{8,264},{16,272},{24,280},{32,288},{40,296},{48,304},{56,3... | collective-permute-start | bytes 786440 | tf_op jit(solution)/shard_map/ppermute | solution.py:325
  101.7 23.3 %all-to-all-start.3 = ((bf16[8,32,128]{2,1,0:T(8,128)(2,1)}), bf16[8,32,128]{2,1,0:T(8,128)(2,1)S(1)}, u32[]{:S(2)}, u32[]{:S(2)}) async-start(bf16[8,32,128]{2,1,0:T(8,128)(2,1)} %shard_map.122), calls=%async_computation.3 | async-start | bytes 131072 | tf_op jit(solution)/shard_map/all_to_all | solution.py:328
  114.1 1.0 copy-start.4
  116.0 20.3 %copy-start.14 = (bf16[2,2,128,128]{3,2,1,0:T(8,128)(2,1)S(1)}, bf16[2,2,128,128]{3,2,1,0:T(8,128)(2,1)}, u32[]{:S(2)}) copy-start(bf16[2,2,128,128]{3,2,1,0:T(8,128)(2,1)} %copy-done.13) | copy-start | bytes 393220
  125.0 1.0 copy-start.5
  130.1 31.0 %copy-start.18 = (s32[256]{0:T(256)S(1)}, s32[256]{0:T(256)}, u32[]{:S(2)}) copy-start(s32[256]{0:T(256)} %param.18) | copy-start | bytes 3076
  130.1 14.3 %all-to-all-start.4 = ((bf16[32,48,128]{2,1,0:T(8,128)(2,1)}), bf16[32,48,128]{2,1,0:T(8,128)(2,1)S(1)}, u32[]{:S(2)}, u32[]{:S(2)}) async-start(bf16[32,48,128]{2,1,0:T(8,128)(2,1)} %shard_map.123), calls=%async_computation.4 | async-start | bytes 786432 | tf_op jit(solution)/shard_map/all_to_all | solution.py:333
  136.3 34.9 %copy-start.17 = (s32[256]{0:T(256)S(1)}, s32[256]{0:T(256)}, u32[]{:S(2)}) copy-start(s32[256]{0:T(256)} %param.19) | copy-start | bytes 3076
  136.4 3.3 %collective-permute-start.11 = (bf16[2,128,128]{2,1,0:T(8,128)(2,1)S(1)}, bf16[2,128,128]{2,1,0:T(8,128)(2,1)S(1)}, u32[]{:S(2)}, u32[]{:S(2)}) collective-permute-start(bf16[2,128,128]{2,1,0:T(8,128)(2,1)S(1)} %get-tuple-element.39), channel_id=1, source_target_pairs={{0,8},{8,0},{16,24},{24,16},{32,40},{40,32},{48,56},{56,48},{64,72... | collective-permute-start | bytes 196616 | tf_op jit(solution)/shard_map/ppermute | solution.py:330
  157.5 13.4 %collective-permute-start.12 = (bf16[64,512]{1,0:T(8,128)(2,1)S(1)}, bf16[64,512]{1,0:T(8,128)(2,1)S(1)}, u32[]{:S(2)}, u32[]{:S(2)}) collective-permute-start(bf16[64,512]{1,0:T(8,128)(2,1)S(1)} %reduce_sum.30), channel_id=1, source_target_pairs={{0,4},{1,5},{2,6},{3,7},{4,0},{5,1},{6,2},{7,3},{8,12},{9,13},{10,... | collective-permute-start | bytes 196616 | tf_op jit(solution)/shard_map/ppermute | solution.py:347
  (4 other events, 3.2 us)

commit v10 on v9

--- a/solution.py
+++ b/solution.py
@@ -226,14 +226,14 @@
         out_ref[rb * 128 : rb * 128 + 128, :] = total.astype(BF16)
 
 
-def call(kernel, outs, specs, scratch, flops, args):
+def call(kernel, outs, specs, scratch, flops, args, mib=8):
     return pl.pallas_call(
         kernel,
         out_shape=outs,
         in_specs=specs,
         out_specs=jax.tree.map(lambda _: pl.BlockSpec(memory_space=pltpu.VMEM), outs),
         scratch_shapes=scratch,
-        compiler_params=pltpu.CompilerParams(vmem_limit_bytes=40 * 2**20),
+        compiler_params=pltpu.CompilerParams(vmem_limit_bytes=mib * 2**20),
         cost_estimate=pl.CostEstimate(flops=flops, bytes_accessed=4 * 2**20, transcendentals=0),
     )(*args)
 
@@ -265,6 +265,7 @@
         [pltpu.VMEM((512, 128), F32)],
         6 * 10**8,
         (z, signal, taps, before, piece, jnp.asarray(MATRICES, BF16), jnp.asarray(TWIDDLES, F32)),
+        mib=16,
     )
 
 
@@ -281,25 +282,28 @@
     got = half_of(lax.ppermute(w_in, "ctx", PERM_CORE), 2, core)
     keep = half_of(w_in, 2, core)
     near = jnp.concatenate([jnp.where(core == 0, keep, got), jnp.where(core == 0, got, keep)], axis=1)
-    near, taps = lax.optimization_barrier((near.reshape(384, 128), long_filter))
-    taps_got = lax.ppermute(taps, "ctx", PERM_CORE)
+    near = lax.optimization_barrier(near.reshape(384, 128))
     rows = w_out.reshape(4, 8, 4, 128).transpose(0, 2, 1, 3).reshape(128, 128)
     far = lax.ppermute(jnp.concatenate([near, rows]), "ctx", PERM_Z)
-    near, tokens, taps_got = lax.optimization_barrier((near, tokens_in, taps_got))
-    beside = lax.ppermute(tokens, "ctx", PERM_CORE)
     near = lax.all_to_all(
         jnp.broadcast_to(near, (4, 384, 128)), "ctx", 0, 0, axis_index_groups=GROUPS_X, tiled=True
     )
+    near, tokens, taps = lax.optimization_barrier((near, tokens_in, long_filter))
+    beside = lax.ppermute(tokens, "ctx", PERM_CORE)
+    taps_got = lax.ppermute(taps, "ctx", PERM_CORE)
+    near, far = lax.optimization_barrier((near, far))
 
     rows = by_position(rows.reshape(4, 32, 128), far[384:].reshape(4, 32, 128), z)
-    far = far[:384]
-    far = jnp.stack([far] + [lax.ppermute(far, "ctx", PERM_Y[k]) for k in (1, 2, 3)])
-    near, far, rows = lax.optimization_barrier((near, far, rows))
-
     near = jnp.broadcast_to(near.reshape(1, 1536, 128), (4, 1536, 128))
     near = jnp.concatenate([near, rows[0], rows[1]], axis=1)
     near = lax.all_to_all(near, "ctx", 0, 0, axis_index_groups=GROUPS_Y, tiled=True)
+    far = far[:384]
+    far = jnp.stack([far] + [lax.ppermute(far, "ctx", PERM_Y[k]) for k in (1, 2, 3)])
+
+    far = lax.optimization_barrier(far)
     fars = [far] + [lax.ppermute(far, "ctx", PERM_X[k]) for k in (1, 2, 3)]
+    terms = call(product_kernel, shape((8, 32, 128), BF16), whole(2), [], 4 * 10**7, (near, w_unembed))
+    piece = lax.all_to_all(terms, "tp", 0, 0, tiled=True)
 
     at = jnp.stack([(ctx // 8) % 4, (ctx // 2) % 4, core, z]).astype(jnp.int32)
     gained, scale = call(
@@ -321,11 +325,9 @@
         8 * 10**8,
         (at, gained, scale, sums, taps, taps_got, *fars),
     )
+    signal, piece = lax.optimization_barrier((signal, piece))
     got = lax.all_to_all(signal, "ctx", 0, 0, axis_index_groups=GROUPS_CORE, tiled=True)
     before = lax.ppermute(got, "ctx", PERM_Z_UP)
-    terms = call(product_kernel, shape((8, 32, 128), BF16), whole(2), [], 4 * 10**7, (near, w_unembed))
-    terms, _ = lax.optimization_barrier((terms, got))
-    piece = lax.all_to_all(terms, "tp", 0, 0, tiled=True)
     gate_keep = lax.dynamic_index_in_dim(gate, core, 0, False)
     gate_got = lax.ppermute(lax.dynamic_index_in_dim(gate, 1 - core, 0, False), "ctx", PERM_CORE)
 

time: 182 us -> 206 us (1.13)
  blocking collectives: 33.3 us -> 63.4 us
  local copies, waits for them, and re-layouts: 14.3 us -> 3.17 us
  waiting for transfers between devices: 32.6 us -> 35.8 us
    all_to_all x1, blocking collectives: 12.7 us -> 28 us  [per_device(): lax.all_to_all(logits.reshape(4, 64, 512), 'tp', 0, 0, axis_index_groups=...]
    all_to_all x0 -> x1, blocking collectives: none -> 14.8 us  [per_device(): lax.all_to_all(jnp.broadcast_to(near, (4, 384, 128)), 'ctx', 0, 0, axis_i...]
    unnamed x38 -> x18, local copies, waits for them, and re-layouts: 12 us -> 1.62 us
    ppermute x3, waiting for transfers between devices: 3.22 us -> 13.5 us  [per_device(): lax.ppermute(far, 'ctx', PERM_Y[k])]
    all_to_all x1, waiting for transfers between devices: 5.5 us -> 0.01 us  [per_device(): lax.all_to_all(near, 'ctx', 0, 0, axis_index_groups=GROUPS_Y, tiled=True)]
    all_to_all x1, waiting for transfers between devices: 8 us -> 2.74 us  [per_device(): piece = lax.all_to_all(terms, 'tp', 0, 0, tiled=True)]
    ppermute x1, waiting for transfers between devices: 0.01 us -> 5.01 us  [per_device(): far = lax.ppermute(jnp.concatenate([near, rows]), 'ctx', PERM_Z)]
    all_to_all x1 -> x0, starting transfers between devices: 4.77 us -> none  [per_device(): lax.all_to_all(jnp.broadcast_to(near, (4, 384, 128)), 'ctx', 0, 0, axis_i...]
  transfers between devices with their start and end apart: 17 -> 16, of which waited for: 7 -> 8; matrix products, arithmetic and copies ran while one was open for 3% -> 2% of each run, Pallas kernels for 3% -> 4%
where the time goes in v10:
time: 206 us; the launch traced here: 203 us
  starting transfers between devices  84 us (41%)
  blocking collectives  63.4 us (31%)
  waiting for transfers between devices  35.8 us (17%)
  Pallas kernels  10.8 us (5%)
  other arithmetic  4.11 us (2%)
  local copies, waits for them, and re-layouts  3.17 us (2%)
    all_to_all x1, blocking collectives, per_device(): lax.all_to_all(logits.reshape(4, 64, 512), 'tp', 0, 0, axis_index_groups=...  28 us
    all_to_all x1, starting transfers between devices, per_device(): piece = lax.all_to_all(terms, 'tp', 0, 0, tiled=True)  15.5 us
    all_to_all x1, blocking collectives, per_device(): lax.all_to_all(jnp.broadcast_to(near, (4, 384, 128)), 'ctx', 0, 0, axis_i...  14.8 us
    ppermute x3, waiting for transfers between devices, per_device(): lax.ppermute(far, 'ctx', PERM_Y[k])  13.5 us
    all_to_all x1, blocking collectives, per_device(): lax.all_to_all(signal, 'ctx', 0, 0, axis_index_groups=GROUPS_CORE, tiled=...  12.7 us
    ppermute x3, starting transfers between devices, per_device(): lax.ppermute(far, 'ctx', PERM_Y[k])  11.9 us
    ppermute x1, starting transfers between devices, per_device(): far = lax.ppermute(jnp.concatenate([near, rows]), 'ctx', PERM_Z)  11.8 us
    pallas_call x7, Pallas kernels, call(): pl.pallas_call(kernel, out_shape=outs, in_specs=specs, out_specs=jax.tree...  10.8 us
  transfers between devices with their start and end apart: 16, of which 8 were waited for; matrix products, arithmetic and copies ran while one was open for 2% of the time, Pallas kernels for 4%

profile of v10, /device:TPU:6, one launch (start us, length us, event | category | flops | bytes accessed | tf_op | source)
XLA Modules:
  0.0 203.0 jit_solution(10166826943802565282)
XLA Ops:
  0.0 2.0 %collective-permute-start = (bf16[3,64,256]{2,1,0:T(8,128)(2,1)}, bf16[3,64,256]{2,1,0:T(8,128)(2,1)S(1)}, u32[]{:S(2)}, u32[]{:S(2)}) collective-permute-start(bf16[3,64,256]{2,1,0:T(8,128)(2,1)} %bitcast.43), channel_id=1, source_target_pairs={{0,8},{8,0},{16,24},{24,16},{32,40},{40,32},{48,56},{56,48},{64,72... | collective-permute-start | bytes 294920 | tf_op jit(solution)/shard_map/ppermute | solution.py:282
  2.1 1.5 collective-permute-done
  4.4 14.8 %all_to_all.36 = bf16[4,384,128]{2,1,0:T(8,128)(2,1)S(1)} all-to-all(bf16[4,384,128]{2,1,0:T(8,128)(2,1)S(1)} %broadcast_in_dim.22), channel_id=1, replica_groups={{0,16,32,48},{8,24,40,56},{64,80,96,112},{72,88,104,120},{128,144,160,1..., dimensions={0} | all-to-all | bytes 786432 | tf_op jit(solution)/shard_map/all_to_all | solution.py:288
  19.3 1.9 collective-permute-start.1
  22.0 11.8 %collective-permute-start.2 = (bf16[512,128]{1,0:T(8,128)(2,1)S(1)}, bf16[512,128]{1,0:T(8,128)(2,1)S(1)}, u32[]{:S(2)}, u32[]{:S(2)}) collective-permute-start(bf16[512,128]{1,0:T(8,128)(2,1)S(1)} %pad_maximum_fusion.2), channel_id=1, source_target_pairs={{0,256},{8,264},{16,272},{24,280},{32,288},{40,296},{48,304},{56,3... | collective-permute-start | bytes 393224 | tf_op jit(solution)/shard_map/ppermute | solution.py:287
  33.8 5.0 %collective-permute-done.2 = bf16[512,128]{1,0:T(8,128)(2,1)S(1)} collective-permute-done((bf16[512,128]{1,0:T(8,128)(2,1)S(1)}, bf16[512,128]{1,0:T(8,128)(2,1)S(1)}, u32[]{:S(2)}, u32[]{:S(2)}) %collective-permute-start.2) | collective-permute-done | bytes 131104 | tf_op jit(solution)/shard_map/ppermute | solution.py:287
  40.3 4.0 %all-to-all-start.1 = ((bf16[4,1600,128]{2,1,0:T(8,128)(2,1)}), bf16[4,1600,128]{2,1,0:T(8,128)(2,1)S(1)}, u32[]{:S(2)}, u32[]{:S(2)}) async-start(bf16[4,1600,128]{2,1,0:T(8,128)(2,1)} %pad_maximum_fusion), calls=%async_computation.1 | async-start | bytes 3276800 | tf_op jit(solution)/shard_map/all_to_all | solution.py:299
  44.3 3.9 %collective-permute-start.4 = (bf16[384,128]{1,0:T(8,128)(2,1)S(1)}, bf16[384,128]{1,0:T(8,128)(2,1)S(1)}, u32[]{:S(2)}, u32[]{:S(2)}) collective-permute-start(bf16[384,128]{1,0:T(8,128)(2,1)S(1)} %get-tuple-element.38), channel_id=1, source_target_pairs={{0,64},{8,72},{16,80},{24,88},{32,96},{40,104},{48,112},{56,120},{... | collective-permute-start | bytes 294920 | tf_op jit(solution)/shard_map/ppermute | solution.py:301
  48.3 4.6 %collective-permute-start.5 = (bf16[384,128]{1,0:T(8,128)(2,1)S(1)}, bf16[384,128]{1,0:T(8,128)(2,1)S(1)}, u32[]{:S(2)}, u32[]{:S(2)}) collective-permute-start(bf16[384,128]{1,0:T(8,128)(2,1)S(1)} %get-tuple-element.38), channel_id=1, source_target_pairs={{0,128},{8,136},{16,144},{24,152},{32,160},{40,168},{48,176},{56,1... | collective-permute-start | bytes 294920 | tf_op jit(solution)/shard_map/ppermute | solution.py:301
  52.9 3.4 %collective-permute-start.6 = (bf16[384,128]{1,0:T(8,128)(2,1)S(1)}, bf16[384,128]{1,0:T(8,128)(2,1)S(1)}, u32[]{:S(2)}, u32[]{:S(2)}) collective-permute-start(bf16[384,128]{1,0:T(8,128)(2,1)S(1)} %get-tuple-element.38), channel_id=1, source_target_pairs={{0,192},{8,200},{16,208},{24,216},{32,224},{40,232},{48,240},{56,2... | collective-permute-start | bytes 294920 | tf_op jit(solution)/shard_map/ppermute | solution.py:301
  56.2 12.1 %collective-permute-done.4 = bf16[384,128]{1,0:T(8,128)(2,1)S(1)} collective-permute-done((bf16[384,128]{1,0:T(8,128)(2,1)S(1)}, bf16[384,128]{1,0:T(8,128)(2,1)S(1)}, u32[]{:S(2)}, u32[]{:S(2)}) %collective-permute-start.4) | collective-permute-done | bytes 98336 | tf_op jit(solution)/shard_map/ppermute | solution.py:301
  69.8 4.0 %collective-permute-start.7 = (bf16[4,384,128]{2,1,0:T(8,128)(2,1)S(1)}, bf16[4,384,128]{2,1,0:T(8,128)(2,1)S(1)}, u32[]{:S(2)}, u32[]{:S(2)}) collective-permute-start(bf16[4,384,128]{2,1,0:T(8,128)(2,1)S(1)} %pad_maximum_fusion.1.f0), channel_id=1, source_target_pairs={{0,16},{8,24},{16,32},{24,40},{32,48},{40,56},{48,0},{56,8},{64,80... | collective-permute-start | bytes 1179656 | tf_op jit(solution)/shard_map/ppermute | solution.py:304
  73.8 2.1 %collective-permute-start.8 = (bf16[4,384,128]{2,1,0:T(8,128)(2,1)S(1)}, bf16[4,384,128]{2,1,0:T(8,128)(2,1)S(1)}, u32[]{:S(2)}, u32[]{:S(2)}) collective-permute-start(bf16[4,384,128]{2,1,0:T(8,128)(2,1)S(1)} %pad_maximum_fusion.1.f0), channel_id=1, source_target_pairs={{0,32},{8,40},{16,48},{24,56},{32,0},{40,8},{48,16},{56,24},{64,96... | collective-permute-start | bytes 1179656 | tf_op jit(solution)/shard_map/ppermute | solution.py:304
  75.9 3.1 %collective-permute-start.9 = (bf16[4,384,128]{2,1,0:T(8,128)(2,1)S(1)}, bf16[4,384,128]{2,1,0:T(8,128)(2,1)}, u32[]{:S(2)}, u32[]{:S(2)}) collective-permute-start(bf16[4,384,128]{2,1,0:T(8,128)(2,1)S(1)} %pad_maximum_fusion.1.f0), channel_id=1, source_target_pairs={{0,48},{8,56},{16,0},{24,8},{32,16},{40,24},{48,32},{56,40},{64,11... | collective-permute-start | bytes 1179656 | tf_op jit(solution)/shard_map/ppermute | solution.py:304
  79.1 1.9 collective-permute-start.3
  81.9 15.5 %all-to-all-start.2 = ((bf16[8,32,128]{2,1,0:T(8,128)(2,1)}), bf16[8,32,128]{2,1,0:T(8,128)(2,1)S(1)}, u32[]{:S(2)}, u32[]{:S(2)}) async-start(bf16[8,32,128]{2,1,0:T(8,128)(2,1)} %shard_map.121), calls=%async_computation.2 | async-start | bytes 131072 | tf_op jit(solution)/shard_map/all_to_all | solution.py:306
  97.5 1.6 copy-done
  99.1 2.1 %shard_map.118 = (bf16[2,256,4096]{2,1,0:T(8,128)(2,1)S(1)}, f32[2,256,128]{2,1,0:T(8,128)S(1)}) custom-call(bf16[256,4096]{1,0:T(8,128)(2,1)S(1)} %copy-done, bf16[256,4096]{1,0:T(8,128)(2,1)} %collective-permute-done.1.beside_hbm, bf16[1,4096]{1,0:T(2,128)(2,1)S(1)} %reshape.38.gain_ref), custom_call_target="tpu_custom_call" | custom-call | flops 10000000 | bytes 4194304 | tf_op jit(solution)/shard_map/pallas_call | solution.py:230
  101.1 1.8 shard_map.119.near_ref
  103.0 2.5 %shard_map.120 = (bf16[16,64,128]{2,1,0:T(8,128)(2,1)S(1)}, bf16[2,2,128,128]{3,2,1,0:T(8,128)(2,1)S(1)}) custom-call(s32[4]{0:T(128)S(1)} %pad_add_fusion.at_ref, bf16[2,256,4096]{2,1,0:T(8,128)(2,1)S(1)} %get-tuple-element.19.gained_ref, f32[2,256,128]{2,1,0:T(8,128)S(1)} %get-tuple-element.20.scale_ref, f32[2,256,384]{2,1,0:T(8,128)S(1)} %shard_map.119.near_ref, ...), custom_call_target="tpu_custom_call" | custom-call | flops 800000000 | bytes 4194304 | tf_op jit(solution)/shard_map/pallas_call | solution.py:230
  105.5 2.7 %all-to-all-done.2.piece_ref = bf16[8,32,128]{2,1,0:T(8,128)(2,1)S(1)} async-done(((bf16[8,32,128]{2,1,0:T(8,128)(2,1)}), bf16[8,32,128]{2,1,0:T(8,128)(2,1)S(1)}, u32[]{:S(2)}, u32[]{:S(2)}) %all-to-all-start.2) | async-done | bytes 65568 | tf_op jit(solution)/shard_map/all_to_all | solution.py:306
  108.3 12.7 %all_to_all.37.got_ref = bf16[16,64,128]{2,1,0:T(8,128)(2,1)S(1)} all-to-all(bf16[16,64,128]{2,1,0:T(8,128)(2,1)S(1)} %get-tuple-element.26), channel_id=1, replica_groups={{0,16,32,48,64,80,96,112,128,144,160,176,192,208,224,240},{8,24,40,56,7..., dimensions={0} | all-to-all | bytes 524288 | tf_op jit(solution)/shard_map/all_to_all | solution.py:329
  121.0 9.7 %collective-permute-start.10 = (bf16[16,64,128]{2,1,0:T(8,128)(2,1)S(1)}, bf16[16,64,128]{2,1,0:T(8,128)(2,1)S(1)}, u32[]{:S(2)}, u32[]{:S(2)}) collective-permute-start(bf16[16,64,128]{2,1,0:T(8,128)(2,1)S(1)} %all_to_all.37.got_ref), channel_id=1, source_target_pairs={{0,256},{8,264},{16,272},{24,280},{32,288},{40,296},{48,304},{56,3... | collective-permute-start | bytes 786440 | tf_op jit(solution)/shard_map/ppermute | solution.py:330
  131.7 2.8 %collective-permute-done.10.before_ref = bf16[16,64,128]{2,1,0:T(8,128)(2,1)S(1)} collective-permute-done((bf16[16,64,128]{2,1,0:T(8,128)(2,1)S(1)}, bf16[16,64,128]{2,1,0:T(8,128)(2,1)S(1)}, u32[]{:S(2)}, u32[]{:S(2)}) %collective-permute-start.10) | collective-permute-done | bytes 262176 | tf_op jit(solution)/shard_map/ppermute | solution.py:330
  134.5 2.3 %shard_map.123 = bf16[32,48,128]{2,1,0:T(8,128)(2,1)} custom-call(s32[1]{0:T(128)} %bitcast.1.z_ref, f32[1024,256]{1,0:T(8,128)S(1)} %get-tuple-element.27.signal_ref, f32[1024,256]{1,0:T(8,128)S(1)} %get-tuple-element.28.filter_ref, bf16[16,64,128]{2,1,0:T(8,128)(2,1)S(1)} %collective-permute-done.10.before_ref, ...), custom_call_target="tpu_custom_call" | custom-call | flops 600000000 | bytes 4194304 | tf_op jit(solution)/shard_map/pallas_call | solution.py:230
  136.8 6.2 %all-to-all-start.4 = ((bf16[32,48,128]{2,1,0:T(8,128)(2,1)}), bf16[32,48,128]{2,1,0:T(8,128)(2,1)S(1)}, u32[]{:S(2)}, u32[]{:S(2)}) async-start(bf16[32,48,128]{2,1,0:T(8,128)(2,1)} %shard_map.123), calls=%async_computation.4 | async-start | bytes 786432 | tf_op jit(solution)/shard_map/all_to_all | solution.py:335
  143.0 2.1 %collective-permute-start.11 = (bf16[2,128,128]{2,1,0:T(8,128)(2,1)S(1)}, bf16[2,128,128]{2,1,0:T(8,128)(2,1)S(1)}, u32[]{:S(2)}, u32[]{:S(2)}) collective-permute-start(bf16[2,128,128]{2,1,0:T(8,128)(2,1)S(1)} %get-tuple-element.35), channel_id=1, source_target_pairs={{0,8},{8,0},{16,24},{24,16},{32,40},{40,32},{48,56},{56,48},{64,72... | collective-permute-start | bytes 196616 | tf_op jit(solution)/shard_map/ppermute | solution.py:332
  146.4 4.7 %all-to-all-done.4.got_ref = bf16[32,48,128]{2,1,0:T(8,128)(2,1)S(1)} async-done(((bf16[32,48,128]{2,1,0:T(8,128)(2,1)}), bf16[32,48,128]{2,1,0:T(8,128)(2,1)S(1)}, u32[]{:S(2)}, u32[]{:S(2)}) %all-to-all-start.4) | async-done | bytes 393248 | tf_op jit(solution)/shard_map/all_to_all | solution.py:335
  151.5 28.0 %all_to_all.38 = bf16[4,64,512]{2,1,0:T(8,128)(2,1)S(1)} all-to-all(bf16[4,64,512]{2,1,0:T(8,128)(2,1)S(1)} %bitcast.33), channel_id=1, replica_groups={{0,1,2,3},{4,5,6,7},{8,9,10,11},{12,13,14,15},{16,17,18,19},{20,21,22,2..., dimensions={0} | all-to-all | bytes 524288 | tf_op jit(solution)/shard_map/all_to_all | solution.py:347
  179.5 7.9 %collective-permute-start.12 = (bf16[64,512]{1,0:T(8,128)(2,1)S(1)}, bf16[64,512]{1,0:T(8,128)(2,1)S(1)}, u32[]{:S(2)}, u32[]{:S(2)}) collective-permute-start(bf16[64,512]{1,0:T(8,128)(2,1)S(1)} %reduce_sum.30), channel_id=1, source_target_pairs={{0,4},{1,5},{2,6},{3,7},{4,0},{5,1},{6,2},{7,3},{8,12},{9,13},{10,... | collective-permute-start | bytes 196616 | tf_op jit(solution)/shard_map/ppermute | solution.py:349
  187.4 5.5 %collective-permute-done.12 = bf16[64,512]{1,0:T(8,128)(2,1)S(1)} collective-permute-done((bf16[64,512]{1,0:T(8,128)(2,1)S(1)}, bf16[64,512]{1,0:T(8,128)(2,1)S(1)}, u32[]{:S(2)}, u32[]{:S(2)}) %collective-permute-start.12) | collective-permute-done | bytes 65568 | tf_op jit(solution)/shard_map/ppermute | solution.py:349
  193.3 7.9 %all_to_all.39 = f32[4,1,64]{2,1,0:T(1,128)S(1)} all-to-all(f32[4,1,64]{2,1,0:T(1,128)S(1)} %broadcast_in_dim.26), channel_id=1, replica_groups={{0,1,2,3},{4,5,6,7},{8,9,10,11},{12,13,14,15},{16,17,18,19},{20,21,22,2..., dimensions={0} | all-to-all | bytes 2048 | tf_op jit(solution)/shard_map/all_to_all | solution.py:360
  (53 shorter events, 10.5 us)
Async XLA Ops:
  0.0 38.8 %copy-start.5 = (bf16[32,512]{1,0:T(8,128)(2,1)S(1)}, bf16[32,512]{1,0:T(8,128)(2,1)}, u32[]{:S(2)}) copy-start(bf16[32,512]{1,0:T(8,128)(2,1)} %param.15) | copy-start | bytes 98308
  0.0 3.5 %collective-permute-start = (bf16[3,64,256]{2,1,0:T(8,128)(2,1)}, bf16[3,64,256]{2,1,0:T(8,128)(2,1)S(1)}, u32[]{:S(2)}, u32[]{:S(2)}) collective-permute-start(bf16[3,64,256]{2,1,0:T(8,128)(2,1)} %bitcast.43), channel_id=1, source_target_pairs={{0,8},{8,0},{16,24},{24,16},{32,40},{40,32},{48,56},{56,48},{64,72... | collective-permute-start | bytes 294920 | tf_op jit(solution)/shard_map/ppermute | solution.py:282
  19.3 78.2 %collective-permute-start.1 = (bf16[256,4096]{1,0:T(8,128)(2,1)}, bf16[256,4096]{1,0:T(8,128)(2,1)}, u32[]{:S(2)}, u32[]{:S(2)}) collective-permute-start(bf16[256,4096]{1,0:T(8,128)(2,1)} %own_hbm.1), channel_id=1, source_target_pairs={{0,8},{8,0},{16,24},{24,16},{32,40},{40,32},{48,56},{56,48},{64,72... | collective-permute-start | bytes 6291464 | tf_op jit(solution)/shard_map/ppermute | solution.py:292
  22.0 16.8 %collective-permute-start.2 = (bf16[512,128]{1,0:T(8,128)(2,1)S(1)}, bf16[512,128]{1,0:T(8,128)(2,1)S(1)}, u32[]{:S(2)}, u32[]{:S(2)}) collective-permute-start(bf16[512,128]{1,0:T(8,128)(2,1)S(1)} %pad_maximum_fusion.2), channel_id=1, source_target_pairs={{0,256},{8,264},{16,272},{24,280},{32,288},{40,296},{48,304},{56,3... | collective-permute-start | bytes 393224 | tf_op jit(solution)/shard_map/ppermute | solution.py:287
  40.3 38.8 %copy-start.3 = (bf16[256,256]{1,0:T(8,128)(2,1)S(1)}, bf16[256,256]{1,0:T(8,128)(2,1)}, u32[]{:S(2)}) copy-start(bf16[256,256]{1,0:T(8,128)(2,1)} %own_taps) | copy-start | bytes 393220
  40.3 40.8 %copy-start.1 = (bf16[512,512]{1,0:T(8,128)(2,1)S(1)}, bf16[512,512]{1,0:T(8,128)(2,1)}, u32[]{:S(2)}) copy-start(bf16[512,512]{1,0:T(8,128)(2,1)} %unembed_ref.1) | copy-start | bytes 1572868
  40.3 40.8 %all-to-all-start.1 = ((bf16[4,1600,128]{2,1,0:T(8,128)(2,1)}), bf16[4,1600,128]{2,1,0:T(8,128)(2,1)S(1)}, u32[]{:S(2)}, u32[]{:S(2)}) async-start(bf16[4,1600,128]{2,1,0:T(8,128)(2,1)} %pad_maximum_fusion), calls=%async_computation.1 | async-start | bytes 3276800 | tf_op jit(solution)/shard_map/all_to_all | solution.py:299
  44.3 53.1 %copy-start.6 = (bf16[4096]{0:T(1024)(128)(2,1)S(1)}, bf16[4096]{0:T(1024)(128)(2,1)}, u32[]{:S(2)}) copy-start(bf16[4096]{0:T(1024)(128)(2,1)} %param.13) | copy-start | bytes 24580
  44.3 24.1 %collective-permute-start.4 = (bf16[384,128]{1,0:T(8,128)(2,1)S(1)}, bf16[384,128]{1,0:T(8,128)(2,1)S(1)}, u32[]{:S(2)}, u32[]{:S(2)}) collective-permute-start(bf16[384,128]{1,0:T(8,128)(2,1)S(1)} %get-tuple-element.38), channel_id=1, source_target_pairs={{0,64},{8,72},{16,80},{24,88},{32,96},{40,104},{48,112},{56,120},{... | collective-permute-start | bytes 294920 | tf_op jit(solution)/shard_map/ppermute | solution.py:301
  48.3 21.5 %collective-permute-start.5 = (bf16[384,128]{1,0:T(8,128)(2,1)S(1)}, bf16[384,128]{1,0:T(8,128)(2,1)S(1)}, u32[]{:S(2)}, u32[]{:S(2)}) collective-permute-start(bf16[384,128]{1,0:T(8,128)(2,1)S(1)} %get-tuple-element.38), channel_id=1, source_target_pairs={{0,128},{8,136},{16,144},{24,152},{32,160},{40,168},{48,176},{56,1... | collective-permute-start | bytes 294920 | tf_op jit(solution)/shard_map/ppermute | solution.py:301
  52.9 16.9 %collective-permute-start.6 = (bf16[384,128]{1,0:T(8,128)(2,1)S(1)}, bf16[384,128]{1,0:T(8,128)(2,1)S(1)}, u32[]{:S(2)}, u32[]{:S(2)}) collective-permute-start(bf16[384,128]{1,0:T(8,128)(2,1)S(1)} %get-tuple-element.38), channel_id=1, source_target_pairs={{0,192},{8,200},{16,208},{24,216},{32,224},{40,232},{48,240},{56,2... | collective-permute-start | bytes 294920 | tf_op jit(solution)/shard_map/ppermute | solution.py:301
  69.8 33.1 %collective-permute-start.7 = (bf16[4,384,128]{2,1,0:T(8,128)(2,1)S(1)}, bf16[4,384,128]{2,1,0:T(8,128)(2,1)S(1)}, u32[]{:S(2)}, u32[]{:S(2)}) collective-permute-start(bf16[4,384,128]{2,1,0:T(8,128)(2,1)S(1)} %pad_maximum_fusion.1.f0), channel_id=1, source_target_pairs={{0,16},{8,24},{16,32},{24,40},{32,48},{40,56},{48,0},{56,8},{64,80... | collective-permute-start | bytes 1179656 | tf_op jit(solution)/shard_map/ppermute | solution.py:304
  73.8 29.1 %collective-permute-start.8 = (bf16[4,384,128]{2,1,0:T(8,128)(2,1)S(1)}, bf16[4,384,128]{2,1,0:T(8,128)(2,1)S(1)}, u32[]{:S(2)}, u32[]{:S(2)}) collective-permute-start(bf16[4,384,128]{2,1,0:T(8,128)(2,1)S(1)} %pad_maximum_fusion.1.f0), channel_id=1, source_target_pairs={{0,32},{8,40},{16,48},{24,56},{32,0},{40,8},{48,16},{56,24},{64,96... | collective-permute-start | bytes 1179656 | tf_op jit(solution)/shard_map/ppermute | solution.py:304
  75.9 27.0 %collective-permute-start.9 = (bf16[4,384,128]{2,1,0:T(8,128)(2,1)S(1)}, bf16[4,384,128]{2,1,0:T(8,128)(2,1)}, u32[]{:S(2)}, u32[]{:S(2)}) collective-permute-start(bf16[4,384,128]{2,1,0:T(8,128)(2,1)S(1)} %pad_maximum_fusion.1.f0), channel_id=1, source_target_pairs={{0,48},{8,56},{16,0},{24,8},{32,16},{40,24},{48,32},{56,40},{64,11... | collective-permute-start | bytes 1179656 | tf_op jit(solution)/shard_map/ppermute | solution.py:304
  79.1 23.8 %collective-permute-start.3 = (bf16[256,256]{1,0:T(8,128)(2,1)S(1)}, bf16[256,256]{1,0:T(8,128)(2,1)}, u32[]{:S(2)}, u32[]{:S(2)}) collective-permute-start(bf16[256,256]{1,0:T(8,128)(2,1)S(1)} %copy-done.3), channel_id=1, source_target_pairs={{0,8},{8,0},{16,24},{24,16},{32,40},{40,32},{48,56},{56,48},{64,72... | collective-permute-start | bytes 393224 | tf_op jit(solution)/shard_map/ppermute | solution.py:293
  81.9 26.4 %all-to-all-start.2 = ((bf16[8,32,128]{2,1,0:T(8,128)(2,1)}), bf16[8,32,128]{2,1,0:T(8,128)(2,1)S(1)}, u32[]{:S(2)}, u32[]{:S(2)}) async-start(bf16[8,32,128]{2,1,0:T(8,128)(2,1)} %shard_map.121), calls=%async_computation.2 | async-start | bytes 131072 | tf_op jit(solution)/shard_map/all_to_all | solution.py:306
  97.5 1.6 copy-start
  103.0 27.7 %copy-start.2 = (bf16[832,256]{1,0:T(8,128)(2,1)S(1)}, bf16[832,256]{1,0:T(8,128)(2,1)}, u32[]{:S(2)}) copy-start(bf16[832,256]{1,0:T(8,128)(2,1)} %constant.103.clone.matrices) | copy-start | bytes 1277956
  103.0 27.7 %copy-start.4 = (f32[128,256]{1,0:T(8,128)S(1)}, f32[128,256]{1,0:T(8,128)}, u32[]{:S(2)}) copy-start(f32[128,256]{1,0:T(8,128)} %constant.104.clone.twiddles) | copy-start | bytes 393220
  121.0 13.5 %collective-permute-start.10 = (bf16[16,64,128]{2,1,0:T(8,128)(2,1)S(1)}, bf16[16,64,128]{2,1,0:T(8,128)(2,1)S(1)}, u32[]{:S(2)}, u32[]{:S(2)}) collective-permute-start(bf16[16,64,128]{2,1,0:T(8,128)(2,1)S(1)} %all_to_all.37.got_ref), channel_id=1, source_target_pairs={{0,256},{8,264},{16,272},{24,280},{32,288},{40,296},{48,304},{56,3... | collective-permute-start | bytes 786440 | tf_op jit(solution)/shard_map/ppermute | solution.py:330
  136.8 50.6 %copy-start.8 = (s32[256]{0:T(256)S(1)}, s32[256]{0:T(256)}, u32[]{:S(2)}) copy-start(s32[256]{0:T(256)} %param.18) | copy-start | bytes 3076
  136.8 14.3 %all-to-all-start.4 = ((bf16[32,48,128]{2,1,0:T(8,128)(2,1)}), bf16[32,48,128]{2,1,0:T(8,128)(2,1)S(1)}, u32[]{:S(2)}, u32[]{:S(2)}) async-start(bf16[32,48,128]{2,1,0:T(8,128)(2,1)} %shard_map.123), calls=%async_computation.4 | async-start | bytes 786432 | tf_op jit(solution)/shard_map/all_to_all | solution.py:335
  143.0 50.2 %copy-start.7 = (s32[256]{0:T(256)S(1)}, s32[256]{0:T(256)}, u32[]{:S(2)}) copy-start(s32[256]{0:T(256)} %param.19) | copy-start | bytes 3076
  143.0 3.3 %collective-permute-start.11 = (bf16[2,128,128]{2,1,0:T(8,128)(2,1)S(1)}, bf16[2,128,128]{2,1,0:T(8,128)(2,1)S(1)}, u32[]{:S(2)}, u32[]{:S(2)}) collective-permute-start(bf16[2,128,128]{2,1,0:T(8,128)(2,1)S(1)} %get-tuple-element.35), channel_id=1, source_target_pairs={{0,8},{8,0},{16,24},{24,16},{32,40},{40,32},{48,56},{56,48},{64,72... | collective-permute-start | bytes 196616 | tf_op jit(solution)/shard_map/ppermute | solution.py:332
  179.5 13.4 %collective-permute-start.12 = (bf16[64,512]{1,0:T(8,128)(2,1)S(1)}, bf16[64,512]{1,0:T(8,128)(2,1)S(1)}, u32[]{:S(2)}, u32[]{:S(2)}) collective-permute-start(bf16[64,512]{1,0:T(8,128)(2,1)S(1)} %reduce_sum.30), channel_id=1, source_target_pairs={{0,4},{1,5},{2,6},{3,7},{4,0},{5,1},{6,2},{7,3},{8,12},{9,13},{10,... | collective-permute-start | bytes 196616 | tf_op jit(solution)/shard_map/ppermute | solution.py:349

commit v11 on v9

--- a/solution.py
+++ b/solution.py
@@ -226,14 +226,14 @@
         out_ref[rb * 128 : rb * 128 + 128, :] = total.astype(BF16)
 
 
-def call(kernel, outs, specs, scratch, flops, args):
+def call(kernel, outs, specs, scratch, flops, args, mib=8):
     return pl.pallas_call(
         kernel,
         out_shape=outs,
         in_specs=specs,
         out_specs=jax.tree.map(lambda _: pl.BlockSpec(memory_space=pltpu.VMEM), outs),
         scratch_shapes=scratch,
-        compiler_params=pltpu.CompilerParams(vmem_limit_bytes=40 * 2**20),
+        compiler_params=pltpu.CompilerParams(vmem_limit_bytes=mib * 2**20),
         cost_estimate=pl.CostEstimate(flops=flops, bytes_accessed=4 * 2**20, transcendentals=0),
     )(*args)
 
@@ -265,6 +265,7 @@
         [pltpu.VMEM((512, 128), F32)],
         6 * 10**8,
         (z, signal, taps, before, piece, jnp.asarray(MATRICES, BF16), jnp.asarray(TWIDDLES, F32)),
+        mib=16,
     )
 
 

time: 182 us -> 182 us (level)
  no operation moved by 1% of the time
where the time goes in v11:
time: 182 us; the launch traced here: 181 us
  starting transfers between devices  83.7 us (46%)
  blocking collectives  33.3 us (18%)
  waiting for transfers between devices  32.6 us (18%)
  local copies, waits for them, and re-layouts  14.3 us (8%)
  Pallas kernels  11.1 us (6%)
  other arithmetic  4.14 us (2%)
    ppermute x1, starting transfers between devices, per_device(): far = lax.ppermute(jnp.concatenate([near, rows]), 'ctx', PERM_Z)  15.7 us
    all_to_all x1, blocking collectives, per_device(): lax.all_to_all(signal, 'ctx', 0, 0, axis_index_groups=GROUPS_CORE, tiled=...  12.8 us
    all_to_all x1, blocking collectives, per_device(): lax.all_to_all(logits.reshape(4, 64, 512), 'tp', 0, 0, axis_index_groups=...  12.7 us
    all_to_all x1, starting transfers between devices, per_device(): piece = lax.all_to_all(terms, 'tp', 0, 0, tiled=True)  12.4 us
    unnamed x38, local copies, waits for them, and re-layouts  12 us
    ppermute x3, starting transfers between devices, per_device(): lax.ppermute(far, 'ctx', PERM_Y[k])  11.6 us
    pallas_call x7, Pallas kernels, call(): pl.pallas_call(kernel, out_shape=outs, in_specs=specs, out_specs=jax.tree...  11.1 us
    ppermute x1, waiting for transfers between devices, per_device(): far = lax.ppermute(logits, 'tp', [(i, i ^ 4) for i in range(8)])  9.68 us
  transfers between devices with their start and end apart: 17, of which 7 were waited for; matrix products, arithmetic and copies ran while one was open for 3% of the time, Pallas kernels for 3%

profile of v11, /device:TPU:6, one launch (start us, length us, event | category | flops | bytes accessed | tf_op | source)
XLA Modules:
  0.0 181.0 jit_solution(15424886134205893755)
XLA Ops:
  0.0 2.0 %collective-permute-start = (bf16[3,64,256]{2,1,0:T(8,128)(2,1)}, bf16[3,64,256]{2,1,0:T(8,128)(2,1)S(1)}, u32[]{:S(2)}, u32[]{:S(2)}) collective-permute-start(bf16[3,64,256]{2,1,0:T(8,128)(2,1)} %bitcast.43), channel_id=1, source_target_pairs={{0,8},{8,0},{16,24},{24,16},{32,40},{40,32},{48,56},{56,48},{64,72... | collective-permute-start | bytes 294920 | tf_op jit(solution)/shard_map/ppermute | solution.py:282
  4.4 2.1 %collective-permute-start.1 = (bf16[256,256]{1,0:T(8,128)(2,1)}, bf16[256,256]{1,0:T(8,128)(2,1)S(1)}, u32[]{:S(2)}, u32[]{:S(2)}) collective-permute-start(bf16[256,256]{1,0:T(8,128)(2,1)} %own_taps), channel_id=1, source_target_pairs={{0,8},{8,0},{16,24},{24,16},{32,40},{40,32},{48,56},{56,48},{64,72... | collective-permute-start | bytes 393224 | tf_op jit(solution)/shard_map/ppermute | solution.py:286
  7.2 15.7 %collective-permute-start.3 = (bf16[512,128]{1,0:T(8,128)(2,1)S(1)}, bf16[512,128]{1,0:T(8,128)(2,1)S(1)}, u32[]{:S(2)}, u32[]{:S(2)}) collective-permute-start(bf16[512,128]{1,0:T(8,128)(2,1)S(1)} %pad_maximum_fusion.2), channel_id=1, source_target_pairs={{0,256},{8,264},{16,272},{24,280},{32,288},{40,296},{48,304},{56,3... | collective-permute-start | bytes 393224 | tf_op jit(solution)/shard_map/ppermute | solution.py:288
  23.8 4.8 %all-to-all-start = ((bf16[4,384,128]{2,1,0:T(8,128)(2,1)}), bf16[4,384,128]{2,1,0:T(8,128)(2,1)S(1)}, u32[]{:S(2)}, u32[]{:S(2)}) async-start(bf16[4,384,128]{2,1,0:T(8,128)(2,1)} %broadcast_in_dim.22), calls=%async_computation | async-start | bytes 786432 | tf_op jit(solution)/shard_map/all_to_all | solution.py:291
  28.6 1.9 %collective-permute-start.2 = (bf16[256,4096]{1,0:T(8,128)(2,1)}, bf16[256,4096]{1,0:T(8,128)(2,1)}, u32[]{:S(2)}, u32[]{:S(2)}) collective-permute-start(bf16[256,4096]{1,0:T(8,128)(2,1)} %own_hbm.1), channel_id=1, source_target_pairs={{0,8},{8,0},{16,24},{24,16},{32,40},{40,32},{48,56},{56,48},{64,72... | collective-permute-start | bytes 6291464 | tf_op jit(solution)/shard_map/ppermute | solution.py:290
  30.5 3.5 %collective-permute-start.4 = (bf16[384,128]{1,0:T(8,128)(2,1)S(1)}, bf16[384,128]{1,0:T(8,128)(2,1)S(1)}, u32[]{:S(2)}, u32[]{:S(2)}) collective-permute-start(bf16[384,128]{1,0:T(8,128)(2,1)S(1)} %get-tuple-element.42), channel_id=1, source_target_pairs={{0,64},{8,72},{16,80},{24,88},{32,96},{40,104},{48,112},{56,120},{... | collective-permute-start | bytes 294920 | tf_op jit(solution)/shard_map/ppermute | solution.py:297
  34.0 4.8 %collective-permute-start.5 = (bf16[384,128]{1,0:T(8,128)(2,1)S(1)}, bf16[384,128]{1,0:T(8,128)(2,1)S(1)}, u32[]{:S(2)}, u32[]{:S(2)}) collective-permute-start(bf16[384,128]{1,0:T(8,128)(2,1)S(1)} %get-tuple-element.42), channel_id=1, source_target_pairs={{0,128},{8,136},{16,144},{24,152},{32,160},{40,168},{48,176},{56,1... | collective-permute-start | bytes 294920 | tf_op jit(solution)/shard_map/ppermute | solution.py:297
  38.8 3.3 %collective-permute-start.6 = (bf16[384,128]{1,0:T(8,128)(2,1)S(1)}, bf16[384,128]{1,0:T(8,128)(2,1)S(1)}, u32[]{:S(2)}, u32[]{:S(2)}) collective-permute-start(bf16[384,128]{1,0:T(8,128)(2,1)S(1)} %get-tuple-element.42), channel_id=1, source_target_pairs={{0,192},{8,200},{16,208},{24,216},{32,224},{40,232},{48,240},{56,2... | collective-permute-start | bytes 294920 | tf_op jit(solution)/shard_map/ppermute | solution.py:297
  42.3 3.0 %collective-permute-done.6 = bf16[384,128]{1,0:T(8,128)(2,1)S(1)} collective-permute-done((bf16[384,128]{1,0:T(8,128)(2,1)S(1)}, bf16[384,128]{1,0:T(8,128)(2,1)S(1)}, u32[]{:S(2)}, u32[]{:S(2)}) %collective-permute-start.6) | collective-permute-done | bytes 98336 | tf_op jit(solution)/shard_map/ppermute | solution.py:297
  46.9 4.0 %all-to-all-start.1 = ((bf16[4,1600,128]{2,1,0:T(8,128)(2,1)}), bf16[4,1600,128]{2,1,0:T(8,128)(2,1)S(1)}, u32[]{:S(2)}, u32[]{:S(2)}) async-start(bf16[4,1600,128]{2,1,0:T(8,128)(2,1)} %pad_maximum_fusion), calls=%async_computation.1 | async-start | bytes 3276800 | tf_op jit(solution)/shard_map/all_to_all | solution.py:302
  50.9 1.9 %collective-permute-start.7 = (bf16[4,384,128]{2,1,0:T(8,128)(2,1)S(1)}, bf16[4,384,128]{2,1,0:T(8,128)(2,1)S(1)}, u32[]{:S(2)}, u32[]{:S(2)}) collective-permute-start(bf16[4,384,128]{2,1,0:T(8,128)(2,1)S(1)} %pad_maximum_fusion.1.f0), channel_id=1, source_target_pairs={{0,16},{8,24},{16,32},{24,40},{32,48},{40,56},{48,0},{56,8},{64,80... | collective-permute-start | bytes 1179656 | tf_op jit(solution)/shard_map/ppermute | solution.py:303
  52.8 4.8 %collective-permute-start.8 = (bf16[4,384,128]{2,1,0:T(8,128)(2,1)S(1)}, bf16[4,384,128]{2,1,0:T(8,128)(2,1)S(1)}, u32[]{:S(2)}, u32[]{:S(2)}) collective-permute-start(bf16[4,384,128]{2,1,0:T(8,128)(2,1)S(1)} %pad_maximum_fusion.1.f0), channel_id=1, source_target_pairs={{0,32},{8,40},{16,48},{24,56},{32,0},{40,8},{48,16},{56,24},{64,96... | collective-permute-start | bytes 1179656 | tf_op jit(solution)/shard_map/ppermute | solution.py:303
  57.6 1.9 %collective-permute-start.9 = (bf16[4,384,128]{2,1,0:T(8,128)(2,1)S(1)}, bf16[4,384,128]{2,1,0:T(8,128)(2,1)S(1)}, u32[]{:S(2)}, u32[]{:S(2)}) collective-permute-start(bf16[4,384,128]{2,1,0:T(8,128)(2,1)S(1)} %pad_maximum_fusion.1.f0), channel_id=1, source_target_pairs={{0,48},{8,56},{16,0},{24,8},{32,16},{40,24},{48,32},{56,40},{64,11... | collective-permute-start | bytes 1179656 | tf_op jit(solution)/shard_map/ppermute | solution.py:303
  59.8 1.6 copy-done.2
  61.3 2.1 %shard_map.118 = (bf16[2,256,4096]{2,1,0:T(8,128)(2,1)S(1)}, f32[2,256,128]{2,1,0:T(8,128)S(1)}) custom-call(bf16[256,4096]{1,0:T(8,128)(2,1)S(1)} %copy-done.2, bf16[256,4096]{1,0:T(8,128)(2,1)} %collective-permute-done.2.beside_hbm, bf16[1,4096]{1,0:T(2,128)(2,1)S(1)} %reshape.38.gain_ref), custom_call_target="tpu_custom_call" | custom-call | flops 10000000 | bytes 4194304 | tf_op jit(solution)/shard_map/pallas_call | solution.py:230
  63.4 1.9 %copy-done = bf16[2,256,4096]{2,1,0:T(8,128)(2,1)} copy-done((bf16[2,256,4096]{2,1,0:T(8,128)(2,1)}, bf16[2,256,4096]{2,1,0:T(8,128)(2,1)S(1)}, u32[]{:S(2)}) %copy-start) | copy-done | bytes 4194328
  66.1 5.5 %all-to-all-done.1.near_ref.rows_ref = bf16[4,1600,128]{2,1,0:T(8,128)(2,1)S(1)} async-done(((bf16[4,1600,128]{2,1,0:T(8,128)(2,1)}), bf16[4,1600,128]{2,1,0:T(8,128)(2,1)S(1)}, u32[]{:S(2)}, u32[]{:S(2)}) %all-to-all-start.1) | async-done | bytes 1638432 | tf_op jit(solution)/shard_map/all_to_all | solution.py:302
  71.6 2.2 %copy-done.1 = bf16[2,256,4096]{2,1,0:T(8,128)(2,1)S(1)} copy-done((bf16[2,256,4096]{2,1,0:T(8,128)(2,1)S(1)}, bf16[2,256,4096]{2,1,0:T(8,128)(2,1)}, u32[]{:S(2)}) %copy-start.1) | copy-done | bytes 4194328
  73.8 1.8 shard_map.119.near_ref
  77.3 1.9 %shard_map.120 = (bf16[16,64,128]{2,1,0:T(8,128)(2,1)S(1)}, bf16[2,2,128,128]{3,2,1,0:T(8,128)(2,1)S(1)}) custom-call(s32[4]{0:T(128)S(1)} %pad_add_fusion.at_ref, bf16[2,256,4096]{2,1,0:T(8,128)(2,1)S(1)} %copy-done.1, f32[2,256,128]{2,1,0:T(8,128)S(1)} %copy-done.9, f32[2,256,384]{2,1,0:T(8,128)S(1)} %shard_map.119.near_ref, ...), custom_call_target="tpu_custom_call" | custom-call | flops 800000000 | bytes 4194304 | tf_op jit(solution)/shard_map/pallas_call | solution.py:230
  79.3 12.8 %all_to_all.36.got_ref = bf16[16,64,128]{2,1,0:T(8,128)(2,1)S(1)} all-to-all(bf16[16,64,128]{2,1,0:T(8,128)(2,1)S(1)} %get-tuple-element.30), channel_id=1, replica_groups={{0,16,32,48,64,80,96,112,128,144,160,176,192,208,224,240},{8,24,40,56,7..., dimensions={0} | all-to-all | bytes 524288 | tf_op jit(solution)/shard_map/all_to_all | solution.py:325
  92.1 8.7 %collective-permute-start.10 = (bf16[16,64,128]{2,1,0:T(8,128)(2,1)S(1)}, bf16[16,64,128]{2,1,0:T(8,128)(2,1)}, u32[]{:S(2)}, u32[]{:S(2)}) collective-permute-start(bf16[16,64,128]{2,1,0:T(8,128)(2,1)S(1)} %all_to_all.36.got_ref), channel_id=1, source_target_pairs={{0,256},{8,264},{16,272},{24,280},{32,288},{40,296},{48,304},{56,3... | collective-permute-start | bytes 786440 | tf_op jit(solution)/shard_map/ppermute | solution.py:326
  101.7 12.4 %all-to-all-start.3 = ((bf16[8,32,128]{2,1,0:T(8,128)(2,1)}), bf16[8,32,128]{2,1,0:T(8,128)(2,1)S(1)}, u32[]{:S(2)}, u32[]{:S(2)}) async-start(bf16[8,32,128]{2,1,0:T(8,128)(2,1)} %shard_map.122), calls=%async_computation.3 | async-start | bytes 131072 | tf_op jit(solution)/shard_map/all_to_all | solution.py:329
  117.0 8.0 %all-to-all-done.3.piece_ref = bf16[8,32,128]{2,1,0:T(8,128)(2,1)S(1)} async-done(((bf16[8,32,128]{2,1,0:T(8,128)(2,1)}), bf16[8,32,128]{2,1,0:T(8,128)(2,1)S(1)}, u32[]{:S(2)}, u32[]{:S(2)}) %all-to-all-start.3) | async-done | bytes 65568 | tf_op jit(solution)/shard_map/all_to_all | solution.py:329
  126.9 3.2 %shard_map.123 = bf16[32,48,128]{2,1,0:T(8,128)(2,1)} custom-call(s32[1]{0:T(128)} %bitcast.1.z_ref, f32[1024,256]{1,0:T(8,128)S(1)} %get-tuple-element.31.signal_ref, f32[1024,256]{1,0:T(8,128)S(1)} %get-tuple-element.32.filter_ref, bf16[16,64,128]{2,1,0:T(8,128)(2,1)} %collective-permute-done.10.before_ref, ...), custom_call_target="tpu_custom_call" | custom-call | flops 600000000 | bytes 4194304 | tf_op jit(solution)/shard_map/pallas_call | solution.py:230
  130.1 6.2 %all-to-all-start.4 = ((bf16[32,48,128]{2,1,0:T(8,128)(2,1)}), bf16[32,48,128]{2,1,0:T(8,128)(2,1)S(1)}, u32[]{:S(2)}, u32[]{:S(2)}) async-start(bf16[32,48,128]{2,1,0:T(8,128)(2,1)} %shard_map.123), calls=%async_computation.4 | async-start | bytes 786432 | tf_op jit(solution)/shard_map/all_to_all | solution.py:334
  136.4 2.1 %collective-permute-start.11 = (bf16[2,128,128]{2,1,0:T(8,128)(2,1)S(1)}, bf16[2,128,128]{2,1,0:T(8,128)(2,1)S(1)}, u32[]{:S(2)}, u32[]{:S(2)}) collective-permute-start(bf16[2,128,128]{2,1,0:T(8,128)(2,1)S(1)} %get-tuple-element.39), channel_id=1, source_target_pairs={{0,8},{8,0},{16,24},{24,16},{32,40},{40,32},{48,56},{56,48},{64,72... | collective-permute-start | bytes 196616 | tf_op jit(solution)/shard_map/ppermute | solution.py:331
  139.7 4.7 %all-to-all-done.4.got_ref = bf16[32,48,128]{2,1,0:T(8,128)(2,1)S(1)} async-done(((bf16[32,48,128]{2,1,0:T(8,128)(2,1)}), bf16[32,48,128]{2,1,0:T(8,128)(2,1)S(1)}, u32[]{:S(2)}, u32[]{:S(2)}) %all-to-all-start.4) | async-done | bytes 393248 | tf_op jit(solution)/shard_map/all_to_all | solution.py:334
  144.8 12.7 %all_to_all.37 = bf16[4,64,512]{2,1,0:T(8,128)(2,1)S(1)} all-to-all(bf16[4,64,512]{2,1,0:T(8,128)(2,1)S(1)} %bitcast.33), channel_id=1, replica_groups={{0,1,2,3},{4,5,6,7},{8,9,10,11},{12,13,14,15},{16,17,18,19},{20,21,22,2..., dimensions={0} | all-to-all | bytes 524288 | tf_op jit(solution)/shard_map/all_to_all | solution.py:346
  157.5 3.6 %collective-permute-start.12 = (bf16[64,512]{1,0:T(8,128)(2,1)S(1)}, bf16[64,512]{1,0:T(8,128)(2,1)S(1)}, u32[]{:S(2)}, u32[]{:S(2)}) collective-permute-start(bf16[64,512]{1,0:T(8,128)(2,1)S(1)} %reduce_sum.30), channel_id=1, source_target_pairs={{0,4},{1,5},{2,6},{3,7},{4,0},{5,1},{6,2},{7,3},{8,12},{9,13},{10,... | collective-permute-start | bytes 196616 | tf_op jit(solution)/shard_map/ppermute | solution.py:348
  161.2 9.7 %collective-permute-done.12 = bf16[64,512]{1,0:T(8,128)(2,1)S(1)} collective-permute-done((bf16[64,512]{1,0:T(8,128)(2,1)S(1)}, bf16[64,512]{1,0:T(8,128)(2,1)S(1)}, u32[]{:S(2)}, u32[]{:S(2)}) %collective-permute-start.12) | collective-permute-done | bytes 65568 | tf_op jit(solution)/shard_map/ppermute | solution.py:348
  171.3 7.9 %all_to_all.38 = f32[4,1,64]{2,1,0:T(1,128)S(1)} all-to-all(f32[4,1,64]{2,1,0:T(1,128)S(1)} %broadcast_in_dim.26), channel_id=1, replica_groups={{0,1,2,3},{4,5,6,7},{8,9,10,11},{12,13,14,15},{16,17,18,19},{20,21,22,2..., dimensions={0} | all-to-all | bytes 2048 | tf_op jit(solution)/shard_map/all_to_all | solution.py:359
  (74 shorter events, 17.8 us)
Async XLA Ops:
  0.0 42.1 %copy-start.15 = (bf16[32,512]{1,0:T(8,128)(2,1)S(1)}, bf16[32,512]{1,0:T(8,128)(2,1)}, u32[]{:S(2)}) copy-start(bf16[32,512]{1,0:T(8,128)(2,1)} %param.15) | copy-start | bytes 98308
  0.0 3.5 %collective-permute-start = (bf16[3,64,256]{2,1,0:T(8,128)(2,1)}, bf16[3,64,256]{2,1,0:T(8,128)(2,1)S(1)}, u32[]{:S(2)}, u32[]{:S(2)}) collective-permute-start(bf16[3,64,256]{2,1,0:T(8,128)(2,1)} %bitcast.43), channel_id=1, source_target_pairs={{0,8},{8,0},{16,24},{24,16},{32,40},{40,32},{48,56},{56,48},{64,72... | collective-permute-start | bytes 294920 | tf_op jit(solution)/shard_map/ppermute | solution.py:282
  4.4 18.6 %collective-permute-start.1 = (bf16[256,256]{1,0:T(8,128)(2,1)}, bf16[256,256]{1,0:T(8,128)(2,1)S(1)}, u32[]{:S(2)}, u32[]{:S(2)}) collective-permute-start(bf16[256,256]{1,0:T(8,128)(2,1)} %own_taps), channel_id=1, source_target_pairs={{0,8},{8,0},{16,24},{24,16},{32,40},{40,32},{48,56},{56,48},{64,72... | collective-permute-start | bytes 393224 | tf_op jit(solution)/shard_map/ppermute | solution.py:286
  7.2 23.3 %collective-permute-start.3 = (bf16[512,128]{1,0:T(8,128)(2,1)S(1)}, bf16[512,128]{1,0:T(8,128)(2,1)S(1)}, u32[]{:S(2)}, u32[]{:S(2)}) collective-permute-start(bf16[512,128]{1,0:T(8,128)(2,1)S(1)} %pad_maximum_fusion.2), channel_id=1, source_target_pairs={{0,256},{8,264},{16,272},{24,280},{32,288},{40,296},{48,304},{56,3... | collective-permute-start | bytes 393224 | tf_op jit(solution)/shard_map/ppermute | solution.py:288
  23.8 21.6 %all-to-all-start = ((bf16[4,384,128]{2,1,0:T(8,128)(2,1)}), bf16[4,384,128]{2,1,0:T(8,128)(2,1)S(1)}, u32[]{:S(2)}, u32[]{:S(2)}) async-start(bf16[4,384,128]{2,1,0:T(8,128)(2,1)} %broadcast_in_dim.22), calls=%async_computation | async-start | bytes 786432 | tf_op jit(solution)/shard_map/all_to_all | solution.py:291
  28.6 31.2 %collective-permute-start.2 = (bf16[256,4096]{1,0:T(8,128)(2,1)}, bf16[256,4096]{1,0:T(8,128)(2,1)}, u32[]{:S(2)}, u32[]{:S(2)}) collective-permute-start(bf16[256,4096]{1,0:T(8,128)(2,1)} %own_hbm.1), channel_id=1, source_target_pairs={{0,8},{8,0},{16,24},{24,16},{32,40},{40,32},{48,56},{56,48},{64,72... | collective-permute-start | bytes 6291464 | tf_op jit(solution)/shard_map/ppermute | solution.py:290
  30.5 11.6 %collective-permute-start.4 = (bf16[384,128]{1,0:T(8,128)(2,1)S(1)}, bf16[384,128]{1,0:T(8,128)(2,1)S(1)}, u32[]{:S(2)}, u32[]{:S(2)}) collective-permute-start(bf16[384,128]{1,0:T(8,128)(2,1)S(1)} %get-tuple-element.42), channel_id=1, source_target_pairs={{0,64},{8,72},{16,80},{24,88},{32,96},{40,104},{48,112},{56,120},{... | collective-permute-start | bytes 294920 | tf_op jit(solution)/shard_map/ppermute | solution.py:297
  34.0 8.3 %collective-permute-start.5 = (bf16[384,128]{1,0:T(8,128)(2,1)S(1)}, bf16[384,128]{1,0:T(8,128)(2,1)S(1)}, u32[]{:S(2)}, u32[]{:S(2)}) collective-permute-start(bf16[384,128]{1,0:T(8,128)(2,1)S(1)} %get-tuple-element.42), channel_id=1, source_target_pairs={{0,128},{8,136},{16,144},{24,152},{32,160},{40,168},{48,176},{56,1... | collective-permute-start | bytes 294920 | tf_op jit(solution)/shard_map/ppermute | solution.py:297
  38.8 6.5 %collective-permute-start.6 = (bf16[384,128]{1,0:T(8,128)(2,1)S(1)}, bf16[384,128]{1,0:T(8,128)(2,1)S(1)}, u32[]{:S(2)}, u32[]{:S(2)}) collective-permute-start(bf16[384,128]{1,0:T(8,128)(2,1)S(1)} %get-tuple-element.42), channel_id=1, source_target_pairs={{0,192},{8,200},{16,208},{24,216},{32,224},{40,232},{48,240},{56,2... | collective-permute-start | bytes 294920 | tf_op jit(solution)/shard_map/ppermute | solution.py:297
  46.9 12.7 %copy-start.16 = (bf16[4096]{0:T(1024)(128)(2,1)S(1)}, bf16[4096]{0:T(1024)(128)(2,1)}, u32[]{:S(2)}) copy-start(bf16[4096]{0:T(1024)(128)(2,1)} %param.13) | copy-start | bytes 24580
  46.9 24.6 %all-to-all-start.1 = ((bf16[4,1600,128]{2,1,0:T(8,128)(2,1)}), bf16[4,1600,128]{2,1,0:T(8,128)(2,1)S(1)}, u32[]{:S(2)}, u32[]{:S(2)}) async-start(bf16[4,1600,128]{2,1,0:T(8,128)(2,1)} %pad_maximum_fusion), calls=%async_computation.1 | async-start | bytes 3276800 | tf_op jit(solution)/shard_map/all_to_all | solution.py:302
  50.9 24.6 %collective-permute-start.7 = (bf16[4,384,128]{2,1,0:T(8,128)(2,1)S(1)}, bf16[4,384,128]{2,1,0:T(8,128)(2,1)S(1)}, u32[]{:S(2)}, u32[]{:S(2)}) collective-permute-start(bf16[4,384,128]{2,1,0:T(8,128)(2,1)S(1)} %pad_maximum_fusion.1.f0), channel_id=1, source_target_pairs={{0,16},{8,24},{16,32},{24,40},{32,48},{40,56},{48,0},{56,8},{64,80... | collective-permute-start | bytes 1179656 | tf_op jit(solution)/shard_map/ppermute | solution.py:303
  52.8 22.7 %collective-permute-start.8 = (bf16[4,384,128]{2,1,0:T(8,128)(2,1)S(1)}, bf16[4,384,128]{2,1,0:T(8,128)(2,1)S(1)}, u32[]{:S(2)}, u32[]{:S(2)}) collective-permute-start(bf16[4,384,128]{2,1,0:T(8,128)(2,1)S(1)} %pad_maximum_fusion.1.f0), channel_id=1, source_target_pairs={{0,32},{8,40},{16,48},{24,56},{32,0},{40,8},{48,16},{56,24},{64,96... | collective-permute-start | bytes 1179656 | tf_op jit(solution)/shard_map/ppermute | solution.py:303
  57.6 17.9 %collective-permute-start.9 = (bf16[4,384,128]{2,1,0:T(8,128)(2,1)S(1)}, bf16[4,384,128]{2,1,0:T(8,128)(2,1)S(1)}, u32[]{:S(2)}, u32[]{:S(2)}) collective-permute-start(bf16[4,384,128]{2,1,0:T(8,128)(2,1)S(1)} %pad_maximum_fusion.1.f0), channel_id=1, source_target_pairs={{0,48},{8,56},{16,0},{24,8},{32,16},{40,24},{48,32},{56,40},{64,11... | collective-permute-start | bytes 1179656 | tf_op jit(solution)/shard_map/ppermute | solution.py:303
  59.8 1.6 copy-start.2
  63.4 2.0 %copy-start = (bf16[2,256,4096]{2,1,0:T(8,128)(2,1)}, bf16[2,256,4096]{2,1,0:T(8,128)(2,1)S(1)}, u32[]{:S(2)}) copy-start(bf16[2,256,4096]{2,1,0:T(8,128)(2,1)S(1)} %get-tuple-element.23.gained_ref) | copy-start | bytes 12582916
  71.6 2.2 %copy-start.1 = (bf16[2,256,4096]{2,1,0:T(8,128)(2,1)S(1)}, bf16[2,256,4096]{2,1,0:T(8,128)(2,1)}, u32[]{:S(2)}) copy-start(bf16[2,256,4096]{2,1,0:T(8,128)(2,1)} %copy-done) | copy-start | bytes 12582916
  73.7 2.6 %copy-start.9 = (f32[2,256,128]{2,1,0:T(8,128)S(1)}, f32[2,256,128]{2,1,0:T(8,128)}, u32[]{:S(2)}) copy-start(f32[2,256,128]{2,1,0:T(8,128)} %copy-done.8) | copy-start | bytes 786436
  73.8 2.6 %copy-start.10 = (bf16[256,256]{1,0:T(8,128)(2,1)S(1)}, bf16[256,256]{1,0:T(8,128)(2,1)}, u32[]{:S(2)}) copy-start(bf16[256,256]{1,0:T(8,128)(2,1)} %own_taps) | copy-start | bytes 393220
  76.3 1.0 copy-start.7
  77.3 23.5 %copy-start.3 = (bf16[512,512]{1,0:T(8,128)(2,1)S(1)}, bf16[512,512]{1,0:T(8,128)(2,1)}, u32[]{:S(2)}) copy-start(bf16[512,512]{1,0:T(8,128)(2,1)} %unembed_ref.1) | copy-start | bytes 1572868
  79.3 12.8 %copy-start.13 = (bf16[2,2,128,128]{3,2,1,0:T(8,128)(2,1)}, bf16[2,2,128,128]{3,2,1,0:T(8,128)(2,1)S(1)}, u32[]{:S(2)}) copy-start(bf16[2,2,128,128]{3,2,1,0:T(8,128)(2,1)S(1)} %get-tuple-element.34) | copy-start | bytes 393220
  92.1 32.9 %collective-permute-start.10 = (bf16[16,64,128]{2,1,0:T(8,128)(2,1)S(1)}, bf16[16,64,128]{2,1,0:T(8,128)(2,1)}, u32[]{:S(2)}, u32[]{:S(2)}) collective-permute-start(bf16[16,64,128]{2,1,0:T(8,128)(2,1)S(1)} %all_to_all.36.got_ref), channel_id=1, source_target_pairs={{0,256},{8,264},{16,272},{24,280},{32,288},{40,296},{48,304},{56,3... | collective-permute-start | bytes 786440 | tf_op jit(solution)/shard_map/ppermute | solution.py:326
  101.7 23.3 %all-to-all-start.3 = ((bf16[8,32,128]{2,1,0:T(8,128)(2,1)}), bf16[8,32,128]{2,1,0:T(8,128)(2,1)S(1)}, u32[]{:S(2)}, u32[]{:S(2)}) async-start(bf16[8,32,128]{2,1,0:T(8,128)(2,1)} %shard_map.122), calls=%async_computation.3 | async-start | bytes 131072 | tf_op jit(solution)/shard_map/all_to_all | solution.py:329
  114.1 1.0 copy-start.4
  116.0 20.3 %copy-start.14 = (bf16[2,2,128,128]{3,2,1,0:T(8,128)(2,1)S(1)}, bf16[2,2,128,128]{3,2,1,0:T(8,128)(2,1)}, u32[]{:S(2)}) copy-start(bf16[2,2,128,128]{3,2,1,0:T(8,128)(2,1)} %copy-done.13) | copy-start | bytes 393220
  125.0 1.0 copy-start.5
  130.1 31.0 %copy-start.18 = (s32[256]{0:T(256)S(1)}, s32[256]{0:T(256)}, u32[]{:S(2)}) copy-start(s32[256]{0:T(256)} %param.18) | copy-start | bytes 3076
  130.1 14.3 %all-to-all-start.4 = ((bf16[32,48,128]{2,1,0:T(8,128)(2,1)}), bf16[32,48,128]{2,1,0:T(8,128)(2,1)S(1)}, u32[]{:S(2)}, u32[]{:S(2)}) async-start(bf16[32,48,128]{2,1,0:T(8,128)(2,1)} %shard_map.123), calls=%async_computation.4 | async-start | bytes 786432 | tf_op jit(solution)/shard_map/all_to_all | solution.py:334
  136.3 34.9 %copy-start.17 = (s32[256]{0:T(256)S(1)}, s32[256]{0:T(256)}, u32[]{:S(2)}) copy-start(s32[256]{0:T(256)} %param.19) | copy-start | bytes 3076
  136.4 3.3 %collective-permute-start.11 = (bf16[2,128,128]{2,1,0:T(8,128)(2,1)S(1)}, bf16[2,128,128]{2,1,0:T(8,128)(2,1)S(1)}, u32[]{:S(2)}, u32[]{:S(2)}) collective-permute-start(bf16[2,128,128]{2,1,0:T(8,128)(2,1)S(1)} %get-tuple-element.39), channel_id=1, source_target_pairs={{0,8},{8,0},{16,24},{24,16},{32,40},{40,32},{48,56},{56,48},{64,72... | collective-permute-start | bytes 196616 | tf_op jit(solution)/shard_map/ppermute | solution.py:331
  157.5 13.4 %collective-permute-start.12 = (bf16[64,512]{1,0:T(8,128)(2,1)S(1)}, bf16[64,512]{1,0:T(8,128)(2,1)S(1)}, u32[]{:S(2)}, u32[]{:S(2)}) collective-permute-start(bf16[64,512]{1,0:T(8,128)(2,1)S(1)} %reduce_sum.30), channel_id=1, source_target_pairs={{0,4},{1,5},{2,6},{3,7},{4,0},{5,1},{6,2},{7,3},{8,12},{9,13},{10,... | collective-permute-start | bytes 196616 | tf_op jit(solution)/shard_map/ppermute | solution.py:348
  (4 other events, 3.2 us)

commit v12 on v11

--- a/solution.py
+++ b/solution.py
@@ -95,7 +95,7 @@
     filter_ref[...] = spectrum(scratch, matrices, twiddles)
 
 
-def conv_kernel(z_ref, signal_ref, filter_ref, before_ref, piece_ref, matrices, twiddles, out_ref, scratch):
+def conv_kernel(z_ref, signal_ref, filter_ref, before_ref, matrices, twiddles, out_ref, scratch):
     upper = z_ref[0] == 1
     cos_tw, sin_tw = twiddles[:, :128], twiddles[:, 128:]
     own, high = signal_ref[...], filter_ref[...]
@@ -122,17 +122,42 @@
     result = mm(matrices[768:, :], jnp.concatenate(parts, axis=1))
     for c in range(8):
         scratch[pl.ds(c, 64, stride=8), :] = result[:, c * 128 : c * 128 + 128]
-    piece = sum(piece_ref[j].astype(F32) for j in range(8)).astype(BF16)
     for d in range(32):
-        out_ref[d, :16] = scratch[d * 16 : d * 16 + 16].astype(BF16)
+        out_ref[d] = scratch[d * 16 : d * 16 + 16].astype(BF16)
+
+
+def pack_kernel(conv_ref, terms_ref, out_ref):
+    piece = sum(terms_ref[j].astype(F32) for j in range(8)).astype(BF16)
+    for d in range(32):
+        out_ref[d, :16] = conv_ref[d]
         out_ref[d, 16:] = piece
+
+
+def first_kernel(core_ref, own_ref, got_ref, rows_ref, out_ref):
+    core = core_ref[0]
+    half = pl.ds(pl.multiple_of(core * 128, 128), 128)
+    for g in range(3):
+        own, got = own_ref[g, :, half], got_ref[g, :, half]
+        out_ref[g * 128 : g * 128 + 64] = jnp.where(core == 0, own, got)
+        out_ref[g * 128 + 64 : g * 128 + 128] = jnp.where(core == 0, got, own)
+    rows = rows_ref[...].astype(F32)
+    blocks = [rows[y * 8 : y * 8 + 8, v * 128 : v * 128 + 128] for y in range(4) for v in range(4)]
+    out_ref[384:] = jnp.concatenate(blocks, axis=0).astype(BF16)
+
+
+def copies_kernel(first_ref, out_ref):
+    for k in range(4):
+        out_ref[k] = first_ref[:384]
 
 
 def weight_block(ref, lead, row):
     return jnp.concatenate([ref[lead, row + 128 * g : row + 128 * g + 128, :] for g in range(3)], axis=1)
 
 
-def norm_kernel(own_hbm, beside_hbm, gain_ref, gained_ref, scale_ref, tokens, sems):
+def near_kernel(
+    at_ref, own_hbm, beside_hbm, gain_ref, near_ref, gained_ref, scale_ref, out_ref, tokens, sems
+):
+    start = at_ref[3] * 2048
     gain = gain_ref[...]
     copies = []
     for part, ref in enumerate((own_hbm, beside_hbm)):
@@ -141,21 +166,16 @@
             copies.append(pltpu.make_async_copy(ref.at[rows], tokens.at[part, rows], sems.at[part, i]))
     for copy in copies:
         copy.start()
-    for k, copy in enumerate(copies):
-        copy.wait()
-        part, i = k // 4, k % 4
-        for half in range(2):
-            rows = slice(i * 64 + half * 32, i * 64 + half * 32 + 32)
-            block = tokens[part, rows, :]
-            stream = block.astype(F32)
-            mean = jnp.mean(stream * stream, axis=1, keepdims=True)
-            scale_ref[part, rows, :] = jnp.broadcast_to(lax.rsqrt(mean + NORM_EPS), (32, 128))
-            gained_ref[part, rows, :] = block * gain
-
-
-def near_kernel(at_ref, gained_ref, near_ref, out_ref):
-    start = at_ref[3] * 2048
     for part in range(2):
+        for i in range(4):
+            copies[part * 4 + i].wait()
+            for half in range(2):
+                rows = slice(i * 64 + half * 32, i * 64 + half * 32 + 32)
+                block = tokens[part, rows, :]
+                stream = block.astype(F32)
+                mean = jnp.mean(stream * stream, axis=1, keepdims=True)
+                scale_ref[part, rows, :] = jnp.broadcast_to(lax.rsqrt(mean + NORM_EPS), (32, 128))
+                gained_ref[part, rows, :] = block * gain
         total = jnp.zeros((256, 384), F32)
         for y in range(4):
             for x in (0, 2):
@@ -257,20 +277,16 @@
     )
 
 
-def convolve(z, signal, taps, before, piece):
+def convolve(z, signal, taps, before):
     return call(
         conv_kernel,
-        shape((32, 48, 128), BF16),
-        [SCALARS] + whole(6),
+        shape((32, 16, 128), BF16),
+        [SCALARS] + whole(5),
         [pltpu.VMEM((512, 128), F32)],
         6 * 10**8,
-        (z, signal, taps, before, piece, jnp.asarray(MATRICES, BF16), jnp.asarray(TWIDDLES, F32)),
+        (z, signal, taps, before, jnp.asarray(MATRICES, BF16), jnp.asarray(TWIDDLES, F32)),
         mib=16,
     )
-
-
-def half_of(array, axis, which):
-    return lax.dynamic_slice_in_dim(array, which * 128, 128, axis)
 
 
 def per_device(tokens_in, pre_gain, w_in, w_out, long_filter, w_unembed, target_ids, score_mask):
@@ -278,41 +294,41 @@
     core, z = ctx % 2, ctx // 32
     z_at = z.reshape(1).astype(jnp.int32)
 
+    core_at = core.reshape(1).astype(jnp.int32)
     w_in = w_in.transpose(1, 0, 2)
-    got = half_of(lax.ppermute(w_in, "ctx", PERM_CORE), 2, core)
-    keep = half_of(w_in, 2, core)
-    near = jnp.concatenate([jnp.where(core == 0, keep, got), jnp.where(core == 0, got, keep)], axis=1)
-    near, taps = lax.optimization_barrier((near.reshape(384, 128), long_filter))
-    taps_got = lax.ppermute(taps, "ctx", PERM_CORE)
-    rows = w_out.reshape(4, 8, 4, 128).transpose(0, 2, 1, 3).reshape(128, 128)
-    far = lax.ppermute(jnp.concatenate([near, rows]), "ctx", PERM_Z)
-    near, tokens, taps_got = lax.optimization_barrier((near, tokens_in, taps_got))
+    first = call(
+        first_kernel,
+        shape((512, 128), BF16),
+        [SCALARS] + whole(3),
+        [],
+        10**5,
+        (core_at, w_in, lax.ppermute(w_in, "ctx", PERM_CORE), w_out),
+    )
+    near = call(copies_kernel, shape((4, 384, 128), BF16), whole(1), [], 10**10, (first,))
+    near, tokens = lax.optimization_barrier((near, tokens_in))
     beside = lax.ppermute(tokens, "ctx", PERM_CORE)
-    near = lax.all_to_all(
-        jnp.broadcast_to(near, (4, 384, 128)), "ctx", 0, 0, axis_index_groups=GROUPS_X, tiled=True
-    )
-
-    rows = by_position(rows.reshape(4, 32, 128), far[384:].reshape(4, 32, 128), z)
+    near = lax.all_to_all(near, "ctx", 0, 0, axis_index_groups=GROUPS_X, tiled=True)
+    far = lax.ppermute(first, "ctx", PERM_Z)
+
+    rows = by_position(first[384:].reshape(4, 32, 128), far[384:].reshape(4, 32, 128), z)
     far = far[:384]
     far = jnp.stack([far] + [lax.ppermute(far, "ctx", PERM_Y[k]) for k in (1, 2, 3)])
-    near, far, rows = lax.optimization_barrier((near, far, rows))
+    near, far, rows, taps = lax.optimization_barrier((near, far, rows, long_filter))
 
     near = jnp.broadcast_to(near.reshape(1, 1536, 128), (4, 1536, 128))
     near = jnp.concatenate([near, rows[0], rows[1]], axis=1)
     near = lax.all_to_all(near, "ctx", 0, 0, axis_index_groups=GROUPS_Y, tiled=True)
     fars = [far] + [lax.ppermute(far, "ctx", PERM_X[k]) for k in (1, 2, 3)]
+    taps_got = lax.ppermute(taps, "ctx", PERM_CORE)
 
     at = jnp.stack([(ctx // 8) % 4, (ctx // 2) % 4, core, z]).astype(jnp.int32)
-    gained, scale = call(
-        norm_kernel,
-        (shape((2, 256, 4096), BF16), shape((2, 256, 128), F32)),
-        [pl.BlockSpec(memory_space=pl.ANY)] * 2 + whole(1),
+    gained, scale, sums = call(
+        near_kernel,
+        (shape((2, 256, 4096), BF16), shape((2, 256, 128), F32), shape((2, 256, 384), F32)),
+        [SCALARS] + [pl.BlockSpec(memory_space=pl.ANY)] * 2 + whole(2),
         [pltpu.VMEM((2, 256, 4096), BF16), pltpu.SemaphoreType.DMA((2, 4))],
-        10**7,
-        (tokens_in, beside, pre_gain.reshape(1, 4096)),
-    )
-    sums = call(
-        near_kernel, shape((2, 256, 384), F32), [SCALARS] + whole(2), [], 8 * 10**8, (at, gained, near)
+        8 * 10**8,
+        (at, tokens_in, beside, pre_gain.reshape(1, 4096), near),
     )
     signal, gate = call(
         proj_kernel,
@@ -326,11 +342,12 @@
     before = lax.ppermute(got, "ctx", PERM_Z_UP)
     terms = call(product_kernel, shape((8, 32, 128), BF16), whole(2), [], 4 * 10**7, (near, w_unembed))
     terms, _ = lax.optimization_barrier((terms, got))
-    piece = lax.all_to_all(terms, "tp", 0, 0, tiled=True)
+    terms = lax.all_to_all(terms, "tp", 0, 0, tiled=True)
     gate_keep = lax.dynamic_index_in_dim(gate, core, 0, False)
     gate_got = lax.ppermute(lax.dynamic_index_in_dim(gate, 1 - core, 0, False), "ctx", PERM_CORE)
 
-    conv = convolve(z_at, *spectra(got), before, piece)
+    conv = convolve(z_at, *spectra(got), before)
+    conv = call(pack_kernel, shape((32, 48, 128), BF16), whole(2), [], 10**5, (conv, terms))
     conv = lax.all_to_all(conv, "ctx", 0, 0, axis_index_groups=GROUPS_PLANE, tiled=True)
 
     width = w_unembed.shape[0]
@@ -341,7 +358,7 @@
         [SCALARS] + whole(4),
         [],
         10**8,
-        (core.reshape(1).astype(jnp.int32), conv, gate_keep, gate_got, base),
+        (core_at, conv, gate_keep, gate_got, base),
     )
     logits = lax.all_to_all(logits.reshape(4, 64, 512), "tp", 0, 0, axis_index_groups=GROUPS_TP, tiled=True)
     logits = jnp.sum(logits.astype(F32), axis=0).astype(BF16)

time: 182 us -> 179 us (0.984)
  waiting for transfers between devices: 32.6 us -> 41.3 us
  local copies, waits for them, and re-layouts: 14.3 us -> 6.48 us
  starting transfers between devices: 83.7 us -> 81.4 us
    unnamed x38 -> x30, local copies, waits for them, and re-layouts: 12 us -> 4.98 us
    all_to_all x1, waiting for transfers between devices: 5.5 us -> 9.9 us  [per_device(): lax.all_to_all(near, 'ctx', 0, 0, axis_index_groups=GROUPS_Y, tiled=True)]
    all_to_all x2, waiting for transfers between devices: 8 us -> 11.4 us  [the longest x1 11.4 us: per_device(): terms = lax.all_to_all(terms, 'tp', 0, 0, tiled=True)]
    pallas_call x7 -> x9, Pallas kernels: 11.1 us -> 11.6 us  [call(): pl.pallas_call(kernel, out_shape=outs, in_specs=specs, out_specs=jax.tree...]
  transfers between devices with their start and end apart: 17 -> 17, of which waited for: 7 -> 7; matrix products, arithmetic and copies ran while one was open for 3% -> 2% of each run, Pallas kernels for 3% -> 5%
where the time goes in v12:
time: 179 us; the launch traced here: 177 us
  starting transfers between devices  81.4 us (45%)
  waiting for transfers between devices  41.3 us (23%)
  blocking collectives  32.4 us (18%)
  Pallas kernels  11.6 us (6%)
  local copies, waits for them, and re-layouts  6.48 us (4%)
  other arithmetic  2.52 us (1%)
    ppermute x1, starting transfers between devices, per_device(): far = lax.ppermute(first, 'ctx', PERM_Z)  15.7 us
    all_to_all x1, blocking collectives, per_device(): lax.all_to_all(logits.reshape(4, 64, 512), 'tp', 0, 0, axis_index_groups=...  12.7 us
    all_to_all x1, starting transfers between devices, per_device(): terms = lax.all_to_all(terms, 'tp', 0, 0, tiled=True)  12.2 us
    all_to_all x1, blocking collectives, per_device(): lax.all_to_all(signal, 'ctx', 0, 0, axis_index_groups=GROUPS_CORE, tiled=...  11.9 us
    pallas_call x9, Pallas kernels, call(): pl.pallas_call(kernel, out_shape=outs, in_specs=specs, out_specs=jax.tree...  11.6 us
    ppermute x3, starting transfers between devices, per_device(): lax.ppermute(far, 'ctx', PERM_Y[k])  11.6 us
    all_to_all x1, waiting for transfers between devices, per_device(): terms = lax.all_to_all(terms, 'tp', 0, 0, tiled=True)  11.4 us
    ppermute x1, waiting for transfers between devices, per_device(): far = lax.ppermute(logits, 'tp', [(i, i ^ 4) for i in range(8)])  10.6 us
  transfers between devices with their start and end apart: 17, of which 7 were waited for; matrix products, arithmetic and copies ran while one was open for 2% of the time, Pallas kernels for 5%

profile of v12, /device:TPU:6, one launch (start us, length us, event | category | flops | bytes accessed | tf_op | source)
XLA Modules:
  0.0 177.5 jit_solution(12644802171866286429)
XLA Ops:
  0.0 1.9 %collective-permute-start = (bf16[3,64,256]{2,1,0:T(8,128)(2,1)}, bf16[3,64,256]{2,1,0:T(8,128)(2,1)S(1)}, u32[]{:S(2)}, u32[]{:S(2)}) collective-permute-start(bf16[3,64,256]{2,1,0:T(8,128)(2,1)} %bitcast.24), channel_id=1, source_target_pairs={{0,8},{8,0},{16,24},{24,16},{32,40},{40,32},{48,56},{56,48},{64,72... | collective-permute-start | bytes 294920 | tf_op jit(solution)/shard_map/ppermute | solution.py:305
  1.9 1.4 collective-permute-done.got_ref
  5.1 15.7 %collective-permute-start.2 = (bf16[512,128]{1,0:T(8,128)(2,1)S(1)}, bf16[512,128]{1,0:T(8,128)(2,1)S(1)}, u32[]{:S(2)}, u32[]{:S(2)}) collective-permute-start(bf16[512,128]{1,0:T(8,128)(2,1)S(1)} %shard_map.118.first_ref), channel_id=1, source_target_pairs={{0,256},{8,264},{16,272},{24,280},{32,288},{40,296},{48,304},{56,3... | collective-permute-start | bytes 393224 | tf_op jit(solution)/shard_map/ppermute | solution.py:311
  21.6 4.8 %all-to-all-start = ((bf16[4,384,128]{2,1,0:T(8,128)(2,1)}), bf16[4,384,128]{2,1,0:T(8,128)(2,1)S(1)}, u32[]{:S(2)}, u32[]{:S(2)}) async-start(bf16[4,384,128]{2,1,0:T(8,128)(2,1)} %shard_map.119), calls=%async_computation | async-start | bytes 786432 | tf_op jit(solution)/shard_map/all_to_all | solution.py:310
  26.4 1.9 %collective-permute-start.1 = (bf16[256,4096]{1,0:T(8,128)(2,1)}, bf16[256,4096]{1,0:T(8,128)(2,1)}, u32[]{:S(2)}, u32[]{:S(2)}) collective-permute-start(bf16[256,4096]{1,0:T(8,128)(2,1)} %own_hbm.1), channel_id=1, source_target_pairs={{0,8},{8,0},{16,24},{24,16},{32,40},{40,32},{48,56},{56,48},{64,72... | collective-permute-start | bytes 6291464 | tf_op jit(solution)/shard_map/ppermute | solution.py:309
  28.3 3.5 %collective-permute-start.3 = (bf16[384,128]{1,0:T(8,128)(2,1)S(1)}, bf16[384,128]{1,0:T(8,128)(2,1)S(1)}, u32[]{:S(2)}, u32[]{:S(2)}) collective-permute-start(bf16[384,128]{1,0:T(8,128)(2,1)S(1)} %get-tuple-element.38), channel_id=1, source_target_pairs={{0,64},{8,72},{16,80},{24,88},{32,96},{40,104},{48,112},{56,120},{... | collective-permute-start | bytes 294920 | tf_op jit(solution)/shard_map/ppermute | solution.py:315
  31.8 4.8 %collective-permute-start.4 = (bf16[384,128]{1,0:T(8,128)(2,1)S(1)}, bf16[384,128]{1,0:T(8,128)(2,1)S(1)}, u32[]{:S(2)}, u32[]{:S(2)}) collective-permute-start(bf16[384,128]{1,0:T(8,128)(2,1)S(1)} %get-tuple-element.38), channel_id=1, source_target_pairs={{0,128},{8,136},{16,144},{24,152},{32,160},{40,168},{48,176},{56,1... | collective-permute-start | bytes 294920 | tf_op jit(solution)/shard_map/ppermute | solution.py:315
  36.6 3.3 %collective-permute-start.5 = (bf16[384,128]{1,0:T(8,128)(2,1)S(1)}, bf16[384,128]{1,0:T(8,128)(2,1)S(1)}, u32[]{:S(2)}, u32[]{:S(2)}) collective-permute-start(bf16[384,128]{1,0:T(8,128)(2,1)S(1)} %get-tuple-element.38), channel_id=1, source_target_pairs={{0,192},{8,200},{16,208},{24,216},{32,224},{40,232},{48,240},{56,2... | collective-permute-start | bytes 294920 | tf_op jit(solution)/shard_map/ppermute | solution.py:315
  40.1 3.0 %collective-permute-done.5 = bf16[384,128]{1,0:T(8,128)(2,1)S(1)} collective-permute-done((bf16[384,128]{1,0:T(8,128)(2,1)S(1)}, bf16[384,128]{1,0:T(8,128)(2,1)S(1)}, u32[]{:S(2)}, u32[]{:S(2)}) %collective-permute-start.5) | collective-permute-done | bytes 98336 | tf_op jit(solution)/shard_map/ppermute | solution.py:315
  43.5 1.3 pad_maximum_fusion
  44.7 4.0 %all-to-all-start.1 = ((bf16[4,1600,128]{2,1,0:T(8,128)(2,1)}), bf16[4,1600,128]{2,1,0:T(8,128)(2,1)S(1)}, u32[]{:S(2)}, u32[]{:S(2)}) async-start(bf16[4,1600,128]{2,1,0:T(8,128)(2,1)} %pad_maximum_fusion), calls=%async_computation.1 | async-start | bytes 3276800 | tf_op jit(solution)/shard_map/all_to_all | solution.py:320
  48.7 1.9 %collective-permute-start.7 = (bf16[4,384,128]{2,1,0:T(8,128)(2,1)S(1)}, bf16[4,384,128]{2,1,0:T(8,128)(2,1)S(1)}, u32[]{:S(2)}, u32[]{:S(2)}) collective-permute-start(bf16[4,384,128]{2,1,0:T(8,128)(2,1)S(1)} %pad_maximum_fusion.1.f0), channel_id=1, source_target_pairs={{0,16},{8,24},{16,32},{24,40},{32,48},{40,56},{48,0},{56,8},{64,80... | collective-permute-start | bytes 1179656 | tf_op jit(solution)/shard_map/ppermute | solution.py:321
  50.6 4.8 %collective-permute-start.8 = (bf16[4,384,128]{2,1,0:T(8,128)(2,1)S(1)}, bf16[4,384,128]{2,1,0:T(8,128)(2,1)S(1)}, u32[]{:S(2)}, u32[]{:S(2)}) collective-permute-start(bf16[4,384,128]{2,1,0:T(8,128)(2,1)S(1)} %pad_maximum_fusion.1.f0), channel_id=1, source_target_pairs={{0,32},{8,40},{16,48},{24,56},{32,0},{40,8},{48,16},{56,24},{64,96... | collective-permute-start | bytes 1179656 | tf_op jit(solution)/shard_map/ppermute | solution.py:321
  55.4 1.9 %collective-permute-start.9 = (bf16[4,384,128]{2,1,0:T(8,128)(2,1)S(1)}, bf16[4,384,128]{2,1,0:T(8,128)(2,1)S(1)}, u32[]{:S(2)}, u32[]{:S(2)}) collective-permute-start(bf16[4,384,128]{2,1,0:T(8,128)(2,1)S(1)} %pad_maximum_fusion.1.f0), channel_id=1, source_target_pairs={{0,48},{8,56},{16,0},{24,8},{32,16},{40,24},{48,32},{56,40},{64,11... | collective-permute-start | bytes 1179656 | tf_op jit(solution)/shard_map/ppermute | solution.py:321
  57.4 1.9 %collective-permute-start.6 = (bf16[256,256]{1,0:T(8,128)(2,1)S(1)}, bf16[256,256]{1,0:T(8,128)(2,1)S(1)}, u32[]{:S(2)}, u32[]{:S(2)}) collective-permute-start(bf16[256,256]{1,0:T(8,128)(2,1)S(1)} %copy-done.4), channel_id=1, source_target_pairs={{0,8},{8,0},{16,24},{24,16},{32,40},{40,32},{48,56},{56,48},{64,72... | collective-permute-start | bytes 393224 | tf_op jit(solution)/shard_map/ppermute | solution.py:322
  59.5 9.9 %all-to-all-done.1.near_ref.rows_ref = bf16[4,1600,128]{2,1,0:T(8,128)(2,1)S(1)} async-done(((bf16[4,1600,128]{2,1,0:T(8,128)(2,1)}), bf16[4,1600,128]{2,1,0:T(8,128)(2,1)S(1)}, u32[]{:S(2)}, u32[]{:S(2)}) %all-to-all-start.1) | async-done | bytes 1638432 | tf_op jit(solution)/shard_map/all_to_all | solution.py:320
  69.4 4.4 %shard_map.120 = (bf16[2,256,4096]{2,1,0:T(8,128)(2,1)S(1)}, f32[2,256,128]{2,1,0:T(8,128)S(1)}, f32[2,256,384]{2,1,0:T(8,128)S(1)}) custom-call(s32[4]{0:T(128)S(1)} %pad_add_fusion.at_ref, bf16[256,4096]{1,0:T(8,128)(2,1)} %own_hbm.1, bf16[256,4096]{1,0:T(8,128)(2,1)} %collective-permute-done.1.beside_hbm, bf16[1,4096]{1,0:T(2,128)(2,1)S(1)} %reshape.28.gain_ref, ...), custom_call_target="tpu_custom_call" | custom-call | flops 800000000 | bytes 4194304 | tf_op jit(solution)/shard_map/pallas_call | solution.py:250
  75.2 1.0 copy-done.3
  77.1 1.9 %shard_map.121 = (bf16[16,64,128]{2,1,0:T(8,128)(2,1)S(1)}, bf16[2,2,128,128]{3,2,1,0:T(8,128)(2,1)S(1)}) custom-call(s32[4]{0:T(128)S(1)} %pad_add_fusion.at_ref, bf16[2,256,4096]{2,1,0:T(8,128)(2,1)S(1)} %get-tuple-element.23.gained_ref, f32[2,256,128]{2,1,0:T(8,128)S(1)} %get-tuple-element.24.scale_ref, f32[2,256,384]{2,1,0:T(8,128)S(1)} %get-tuple-element.25.near_ref, ...), custom_call_target="tpu_custom_call" | custom-call | flops 800000000 | bytes 4194304 | tf_op jit(solution)/shard_map/pallas_call | solution.py:250
  79.1 11.9 %all_to_all.36.got_ref = bf16[16,64,128]{2,1,0:T(8,128)(2,1)S(1)} all-to-all(bf16[16,64,128]{2,1,0:T(8,128)(2,1)S(1)} %get-tuple-element.28), channel_id=1, replica_groups={{0,16,32,48,64,80,96,112,128,144,160,176,192,208,224,240},{8,24,40,56,7..., dimensions={0} | all-to-all | bytes 524288 | tf_op jit(solution)/shard_map/all_to_all | solution.py:341
  91.0 7.9 %collective-permute-start.10 = (bf16[16,64,128]{2,1,0:T(8,128)(2,1)S(1)}, bf16[16,64,128]{2,1,0:T(8,128)(2,1)S(1)}, u32[]{:S(2)}, u32[]{:S(2)}) collective-permute-start(bf16[16,64,128]{2,1,0:T(8,128)(2,1)S(1)} %all_to_all.36.got_ref), channel_id=1, source_target_pairs={{0,256},{8,264},{16,272},{24,280},{32,288},{40,296},{48,304},{56,3... | collective-permute-start | bytes 786440 | tf_op jit(solution)/shard_map/ppermute | solution.py:342
  99.7 12.2 %all-to-all-start.3 = ((bf16[8,32,128]{2,1,0:T(8,128)(2,1)}), bf16[8,32,128]{2,1,0:T(8,128)(2,1)S(1)}, u32[]{:S(2)}, u32[]{:S(2)}) async-start(bf16[8,32,128]{2,1,0:T(8,128)(2,1)} %shard_map.124), calls=%async_computation.3 | async-start | bytes 131072 | tf_op jit(solution)/shard_map/all_to_all | solution.py:345
  113.0 1.5 shard_map.123.conv_ref
  114.5 11.4 %all-to-all-done.3.terms_ref = bf16[8,32,128]{2,1,0:T(8,128)(2,1)S(1)} async-done(((bf16[8,32,128]{2,1,0:T(8,128)(2,1)}), bf16[8,32,128]{2,1,0:T(8,128)(2,1)S(1)}, u32[]{:S(2)}, u32[]{:S(2)}) %all-to-all-start.3) | async-done | bytes 65568 | tf_op jit(solution)/shard_map/all_to_all | solution.py:345
  126.7 6.2 %all-to-all-start.4 = ((bf16[32,48,128]{2,1,0:T(8,128)(2,1)}), bf16[32,48,128]{2,1,0:T(8,128)(2,1)S(1)}, u32[]{:S(2)}, u32[]{:S(2)}) async-start(bf16[32,48,128]{2,1,0:T(8,128)(2,1)} %shard_map.125), calls=%async_computation.4 | async-start | bytes 786432 | tf_op jit(solution)/shard_map/all_to_all | solution.py:351
  132.9 2.1 %collective-permute-start.11 = (bf16[2,128,128]{2,1,0:T(8,128)(2,1)S(1)}, bf16[2,128,128]{2,1,0:T(8,128)(2,1)S(1)}, u32[]{:S(2)}, u32[]{:S(2)}) collective-permute-start(bf16[2,128,128]{2,1,0:T(8,128)(2,1)S(1)} %get-tuple-element.35), channel_id=1, source_target_pairs={{0,8},{8,0},{16,24},{24,16},{32,40},{40,32},{48,56},{56,48},{64,72... | collective-permute-start | bytes 196616 | tf_op jit(solution)/shard_map/ppermute | solution.py:347
  135.0 1.2 fusion.base_ref
  136.2 4.7 %all-to-all-done.4.got_ref = bf16[32,48,128]{2,1,0:T(8,128)(2,1)S(1)} async-done(((bf16[32,48,128]{2,1,0:T(8,128)(2,1)}), bf16[32,48,128]{2,1,0:T(8,128)(2,1)S(1)}, u32[]{:S(2)}, u32[]{:S(2)}) %all-to-all-start.4) | async-done | bytes 393248 | tf_op jit(solution)/shard_map/all_to_all | solution.py:351
  141.3 12.7 %all_to_all.37 = bf16[4,64,512]{2,1,0:T(8,128)(2,1)S(1)} all-to-all(bf16[4,64,512]{2,1,0:T(8,128)(2,1)S(1)} %bitcast.23), channel_id=1, replica_groups={{0,1,2,3},{4,5,6,7},{8,9,10,11},{12,13,14,15},{16,17,18,19},{20,21,22,2..., dimensions={0} | all-to-all | bytes 524288 | tf_op jit(solution)/shard_map/all_to_all | solution.py:363
  154.0 2.7 %collective-permute-start.12 = (bf16[64,512]{1,0:T(8,128)(2,1)S(1)}, bf16[64,512]{1,0:T(8,128)(2,1)S(1)}, u32[]{:S(2)}, u32[]{:S(2)}) collective-permute-start(bf16[64,512]{1,0:T(8,128)(2,1)S(1)} %reduce_sum.30), channel_id=1, source_target_pairs={{0,4},{1,5},{2,6},{3,7},{4,0},{5,1},{6,2},{7,3},{8,12},{9,13},{10,... | collective-permute-start | bytes 196616 | tf_op jit(solution)/shard_map/ppermute | solution.py:365
  156.8 10.6 %collective-permute-done.12 = bf16[64,512]{1,0:T(8,128)(2,1)S(1)} collective-permute-done((bf16[64,512]{1,0:T(8,128)(2,1)S(1)}, bf16[64,512]{1,0:T(8,128)(2,1)S(1)}, u32[]{:S(2)}, u32[]{:S(2)}) %collective-permute-start.12) | collective-permute-done | bytes 65568 | tf_op jit(solution)/shard_map/ppermute | solution.py:365
  167.8 7.9 %all_to_all.38 = f32[4,1,64]{2,1,0:T(1,128)S(1)} all-to-all(f32[4,1,64]{2,1,0:T(1,128)S(1)} %broadcast_in_dim.22), channel_id=1, replica_groups={{0,1,2,3},{4,5,6,7},{8,9,10,11},{12,13,14,15},{16,17,18,19},{20,21,22,2..., dimensions={0} | all-to-all | bytes 2048 | tf_op jit(solution)/shard_map/all_to_all | solution.py:376
  (65 shorter events, 10.7 us)
Async XLA Ops:
  0.0 3.4 %collective-permute-start = (bf16[3,64,256]{2,1,0:T(8,128)(2,1)}, bf16[3,64,256]{2,1,0:T(8,128)(2,1)S(1)}, u32[]{:S(2)}, u32[]{:S(2)}) collective-permute-start(bf16[3,64,256]{2,1,0:T(8,128)(2,1)} %bitcast.24), channel_id=1, source_target_pairs={{0,8},{8,0},{16,24},{24,16},{32,40},{40,32},{48,56},{56,48},{64,72... | collective-permute-start | bytes 294920 | tf_op jit(solution)/shard_map/ppermute | solution.py:305
  3.4 0.9 copy-start.10
  4.3 0.8 copy-start.11
  5.1 23.2 %collective-permute-start.2 = (bf16[512,128]{1,0:T(8,128)(2,1)S(1)}, bf16[512,128]{1,0:T(8,128)(2,1)S(1)}, u32[]{:S(2)}, u32[]{:S(2)}) collective-permute-start(bf16[512,128]{1,0:T(8,128)(2,1)S(1)} %shard_map.118.first_ref), channel_id=1, source_target_pairs={{0,256},{8,264},{16,272},{24,280},{32,288},{40,296},{48,304},{56,3... | collective-permute-start | bytes 393224 | tf_op jit(solution)/shard_map/ppermute | solution.py:311
  21.6 21.6 %all-to-all-start = ((bf16[4,384,128]{2,1,0:T(8,128)(2,1)}), bf16[4,384,128]{2,1,0:T(8,128)(2,1)S(1)}, u32[]{:S(2)}, u32[]{:S(2)}) async-start(bf16[4,384,128]{2,1,0:T(8,128)(2,1)} %shard_map.119), calls=%async_computation | async-start | bytes 786432 | tf_op jit(solution)/shard_map/all_to_all | solution.py:310
  26.4 43.0 %collective-permute-start.1 = (bf16[256,4096]{1,0:T(8,128)(2,1)}, bf16[256,4096]{1,0:T(8,128)(2,1)}, u32[]{:S(2)}, u32[]{:S(2)}) collective-permute-start(bf16[256,4096]{1,0:T(8,128)(2,1)} %own_hbm.1), channel_id=1, source_target_pairs={{0,8},{8,0},{16,24},{24,16},{32,40},{40,32},{48,56},{56,48},{64,72... | collective-permute-start | bytes 6291464 | tf_op jit(solution)/shard_map/ppermute | solution.py:309
  28.3 11.6 %collective-permute-start.3 = (bf16[384,128]{1,0:T(8,128)(2,1)S(1)}, bf16[384,128]{1,0:T(8,128)(2,1)S(1)}, u32[]{:S(2)}, u32[]{:S(2)}) collective-permute-start(bf16[384,128]{1,0:T(8,128)(2,1)S(1)} %get-tuple-element.38), channel_id=1, source_target_pairs={{0,64},{8,72},{16,80},{24,88},{32,96},{40,104},{48,112},{56,120},{... | collective-permute-start | bytes 294920 | tf_op jit(solution)/shard_map/ppermute | solution.py:315
  31.8 8.3 %collective-permute-start.4 = (bf16[384,128]{1,0:T(8,128)(2,1)S(1)}, bf16[384,128]{1,0:T(8,128)(2,1)S(1)}, u32[]{:S(2)}, u32[]{:S(2)}) collective-permute-start(bf16[384,128]{1,0:T(8,128)(2,1)S(1)} %get-tuple-element.38), channel_id=1, source_target_pairs={{0,128},{8,136},{16,144},{24,152},{32,160},{40,168},{48,176},{56,1... | collective-permute-start | bytes 294920 | tf_op jit(solution)/shard_map/ppermute | solution.py:315
  36.6 6.5 %collective-permute-start.5 = (bf16[384,128]{1,0:T(8,128)(2,1)S(1)}, bf16[384,128]{1,0:T(8,128)(2,1)S(1)}, u32[]{:S(2)}, u32[]{:S(2)}) collective-permute-start(bf16[384,128]{1,0:T(8,128)(2,1)S(1)} %get-tuple-element.38), channel_id=1, source_target_pairs={{0,192},{8,200},{16,208},{24,216},{32,224},{40,232},{48,240},{56,2... | collective-permute-start | bytes 294920 | tf_op jit(solution)/shard_map/ppermute | solution.py:315
  44.7 12.7 %copy-start.4 = (bf16[256,256]{1,0:T(8,128)(2,1)S(1)}, bf16[256,256]{1,0:T(8,128)(2,1)}, u32[]{:S(2)}) copy-start(bf16[256,256]{1,0:T(8,128)(2,1)} %own_taps) | copy-start | bytes 393220
  44.7 14.7 %copy-start.12 = (bf16[4096]{0:T(1024)(128)(2,1)S(1)}, bf16[4096]{0:T(1024)(128)(2,1)}, u32[]{:S(2)}) copy-start(bf16[4096]{0:T(1024)(128)(2,1)} %param.13) | copy-start | bytes 24580
  44.7 24.6 %all-to-all-start.1 = ((bf16[4,1600,128]{2,1,0:T(8,128)(2,1)}), bf16[4,1600,128]{2,1,0:T(8,128)(2,1)S(1)}, u32[]{:S(2)}, u32[]{:S(2)}) async-start(bf16[4,1600,128]{2,1,0:T(8,128)(2,1)} %pad_maximum_fusion), calls=%async_computation.1 | async-start | bytes 3276800 | tf_op jit(solution)/shard_map/all_to_all | solution.py:320
  48.7 25.7 %collective-permute-start.7 = (bf16[4,384,128]{2,1,0:T(8,128)(2,1)S(1)}, bf16[4,384,128]{2,1,0:T(8,128)(2,1)S(1)}, u32[]{:S(2)}, u32[]{:S(2)}) collective-permute-start(bf16[4,384,128]{2,1,0:T(8,128)(2,1)S(1)} %pad_maximum_fusion.1.f0), channel_id=1, source_target_pairs={{0,16},{8,24},{16,32},{24,40},{32,48},{40,56},{48,0},{56,8},{64,80... | collective-permute-start | bytes 1179656 | tf_op jit(solution)/shard_map/ppermute | solution.py:321
  50.6 23.8 %collective-permute-start.8 = (bf16[4,384,128]{2,1,0:T(8,128)(2,1)S(1)}, bf16[4,384,128]{2,1,0:T(8,128)(2,1)S(1)}, u32[]{:S(2)}, u32[]{:S(2)}) collective-permute-start(bf16[4,384,128]{2,1,0:T(8,128)(2,1)S(1)} %pad_maximum_fusion.1.f0), channel_id=1, source_target_pairs={{0,32},{8,40},{16,48},{24,56},{32,0},{40,8},{48,16},{56,24},{64,96... | collective-permute-start | bytes 1179656 | tf_op jit(solution)/shard_map/ppermute | solution.py:321
  55.4 19.0 %collective-permute-start.9 = (bf16[4,384,128]{2,1,0:T(8,128)(2,1)S(1)}, bf16[4,384,128]{2,1,0:T(8,128)(2,1)S(1)}, u32[]{:S(2)}, u32[]{:S(2)}) collective-permute-start(bf16[4,384,128]{2,1,0:T(8,128)(2,1)S(1)} %pad_maximum_fusion.1.f0), channel_id=1, source_target_pairs={{0,48},{8,56},{16,0},{24,8},{32,16},{40,24},{48,32},{56,40},{64,11... | collective-permute-start | bytes 1179656 | tf_op jit(solution)/shard_map/ppermute | solution.py:321
  57.4 16.3 %collective-permute-start.6 = (bf16[256,256]{1,0:T(8,128)(2,1)S(1)}, bf16[256,256]{1,0:T(8,128)(2,1)S(1)}, u32[]{:S(2)}, u32[]{:S(2)}) collective-permute-start(bf16[256,256]{1,0:T(8,128)(2,1)S(1)} %copy-done.4), channel_id=1, source_target_pairs={{0,8},{8,0},{16,24},{24,16},{32,40},{40,32},{48,56},{56,48},{64,72... | collective-permute-start | bytes 393224 | tf_op jit(solution)/shard_map/ppermute | solution.py:322
  73.8 0.7 copy-start.5
  74.4 0.8 copy-start.2
  75.2 1.0 copy-start.3
  76.2 0.9 copy-start.6
  77.1 21.8 %copy-start = (bf16[512,512]{1,0:T(8,128)(2,1)S(1)}, bf16[512,512]{1,0:T(8,128)(2,1)}, u32[]{:S(2)}) copy-start(bf16[512,512]{1,0:T(8,128)(2,1)} %unembed_ref.1) | copy-start | bytes 1572868
  79.0 11.9 %copy-start.8 = (bf16[2,2,128,128]{3,2,1,0:T(8,128)(2,1)}, bf16[2,2,128,128]{3,2,1,0:T(8,128)(2,1)S(1)}, u32[]{:S(2)}) copy-start(bf16[2,2,128,128]{3,2,1,0:T(8,128)(2,1)S(1)} %get-tuple-element.32) | copy-start | bytes 393220
  79.1 32.9 %copy-start.1 = (bf16[832,256]{1,0:T(8,128)(2,1)S(1)}, bf16[832,256]{1,0:T(8,128)(2,1)}, u32[]{:S(2)}) copy-start(bf16[832,256]{1,0:T(8,128)(2,1)} %constant.101.clone.matrices) | copy-start | bytes 1277956
  79.1 32.9 %copy-start.7 = (f32[128,256]{1,0:T(8,128)S(1)}, f32[128,256]{1,0:T(8,128)}, u32[]{:S(2)}) copy-start(f32[128,256]{1,0:T(8,128)} %constant.102.clone.twiddles) | copy-start | bytes 393220
  91.0 22.0 %collective-permute-start.10 = (bf16[16,64,128]{2,1,0:T(8,128)(2,1)S(1)}, bf16[16,64,128]{2,1,0:T(8,128)(2,1)S(1)}, u32[]{:S(2)}, u32[]{:S(2)}) collective-permute-start(bf16[16,64,128]{2,1,0:T(8,128)(2,1)S(1)} %all_to_all.36.got_ref), channel_id=1, source_target_pairs={{0,256},{8,264},{16,272},{24,280},{32,288},{40,296},{48,304},{56,3... | collective-permute-start | bytes 786440 | tf_op jit(solution)/shard_map/ppermute | solution.py:342
  99.7 26.2 %all-to-all-start.3 = ((bf16[8,32,128]{2,1,0:T(8,128)(2,1)}), bf16[8,32,128]{2,1,0:T(8,128)(2,1)S(1)}, u32[]{:S(2)}, u32[]{:S(2)}) async-start(bf16[8,32,128]{2,1,0:T(8,128)(2,1)} %shard_map.124), calls=%async_computation.3 | async-start | bytes 131072 | tf_op jit(solution)/shard_map/all_to_all | solution.py:345
  112.9 19.9 %copy-start.9 = (bf16[2,2,128,128]{3,2,1,0:T(8,128)(2,1)S(1)}, bf16[2,2,128,128]{3,2,1,0:T(8,128)(2,1)}, u32[]{:S(2)}) copy-start(bf16[2,2,128,128]{3,2,1,0:T(8,128)(2,1)} %copy-done.8) | copy-start | bytes 393220
  126.7 30.0 %copy-start.14 = (s32[256]{0:T(256)S(1)}, s32[256]{0:T(256)}, u32[]{:S(2)}) copy-start(s32[256]{0:T(256)} %param.18) | copy-start | bytes 3076
  126.7 14.3 %all-to-all-start.4 = ((bf16[32,48,128]{2,1,0:T(8,128)(2,1)}), bf16[32,48,128]{2,1,0:T(8,128)(2,1)S(1)}, u32[]{:S(2)}, u32[]{:S(2)}) async-start(bf16[32,48,128]{2,1,0:T(8,128)(2,1)} %shard_map.125), calls=%async_computation.4 | async-start | bytes 786432 | tf_op jit(solution)/shard_map/all_to_all | solution.py:351
  132.8 34.9 %copy-start.13 = (s32[256]{0:T(256)S(1)}, s32[256]{0:T(256)}, u32[]{:S(2)}) copy-start(s32[256]{0:T(256)} %param.19) | copy-start | bytes 3076
  132.9 3.3 %collective-permute-start.11 = (bf16[2,128,128]{2,1,0:T(8,128)(2,1)S(1)}, bf16[2,128,128]{2,1,0:T(8,128)(2,1)S(1)}, u32[]{:S(2)}, u32[]{:S(2)}) collective-permute-start(bf16[2,128,128]{2,1,0:T(8,128)(2,1)S(1)} %get-tuple-element.35), channel_id=1, source_target_pairs={{0,8},{8,0},{16,24},{24,16},{32,40},{40,32},{48,56},{56,48},{64,72... | collective-permute-start | bytes 196616 | tf_op jit(solution)/shard_map/ppermute | solution.py:347
  154.0 13.4 %collective-permute-start.12 = (bf16[64,512]{1,0:T(8,128)(2,1)S(1)}, bf16[64,512]{1,0:T(8,128)(2,1)S(1)}, u32[]{:S(2)}, u32[]{:S(2)}) collective-permute-start(bf16[64,512]{1,0:T(8,128)(2,1)S(1)} %reduce_sum.30), channel_id=1, source_target_pairs={{0,4},{1,5},{2,6},{3,7},{4,0},{5,1},{6,2},{7,3},{8,12},{9,13},{10,... | collective-permute-start | bytes 196616 | tf_op jit(solution)/shard_map/ppermute | solution.py:365

commit v13 on v12

--- a/solution.py
+++ b/solution.py
@@ -133,21 +133,8 @@
         out_ref[d, 16:] = piece
 
 
-def first_kernel(core_ref, own_ref, got_ref, rows_ref, out_ref):
-    core = core_ref[0]
-    half = pl.ds(pl.multiple_of(core * 128, 128), 128)
-    for g in range(3):
-        own, got = own_ref[g, :, half], got_ref[g, :, half]
-        out_ref[g * 128 : g * 128 + 64] = jnp.where(core == 0, own, got)
-        out_ref[g * 128 + 64 : g * 128 + 128] = jnp.where(core == 0, got, own)
-    rows = rows_ref[...].astype(F32)
-    blocks = [rows[y * 8 : y * 8 + 8, v * 128 : v * 128 + 128] for y in range(4) for v in range(4)]
-    out_ref[384:] = jnp.concatenate(blocks, axis=0).astype(BF16)
-
-
-def copies_kernel(first_ref, out_ref):
-    for k in range(4):
-        out_ref[k] = first_ref[:384]
+def copy_kernel(first_ref, out_ref):
+    out_ref[...] = first_ref[:384]
 
 
 def weight_block(ref, lead, row):
@@ -155,15 +142,17 @@
 
 
 def near_kernel(
-    at_ref, own_hbm, beside_hbm, gain_ref, near_ref, gained_ref, scale_ref, out_ref, tokens, sems
+    at_ref, own_hbm, beside_hbm, gain_ref, n0, n1, n2, n3, gained_ref, scale_ref, out_ref, tokens, blocks, sems
 ):
-    start = at_ref[3] * 2048
+    y_at, x_at, start = at_ref[0], at_ref[1], at_ref[3] * 2048
     gain = gain_ref[...]
     copies = []
     for part, ref in enumerate((own_hbm, beside_hbm)):
         for i in range(4):
             rows = slice(i * 64, i * 64 + 64)
             copies.append(pltpu.make_async_copy(ref.at[rows], tokens.at[part, rows], sems.at[part, i]))
+    for step, ref in enumerate((n0, n1, n2, n3)):
+        copies.append(pltpu.make_async_copy(ref, blocks.at[step], sems.at[2, step]))
     for copy in copies:
         copy.start()
     for part in range(2):
@@ -176,12 +165,17 @@
                 mean = jnp.mean(stream * stream, axis=1, keepdims=True)
                 scale_ref[part, rows, :] = jnp.broadcast_to(lax.rsqrt(mean + NORM_EPS), (32, 128))
                 gained_ref[part, rows, :] = block * gain
+    for step in range(4):
+        copies[8 + step].wait()
+    for part in range(2):
         total = jnp.zeros((256, 384), F32)
-        for y in range(4):
-            for x in (0, 2):
-                left = gained_ref[part, :, pl.ds(pl.multiple_of(start + (y * 4 + x) * 128, 128), 256)]
-                right = [weight_block(near_ref, y, x * 384), weight_block(near_ref, y, x * 384 + 384)]
-                total += mm(left, jnp.concatenate(right, axis=0))
+        for step in range(4):
+            y = lax.rem(y_at + 4 - step, 4)
+            for k in (0, 2):
+                starts = [start + (y * 4 + lax.rem(x_at + 4 - j, 4)) * 128 for j in (k, k + 1)]
+                left = [gained_ref[part, :, pl.ds(pl.multiple_of(at, 128), 128)] for at in starts]
+                right = [weight_block(blocks.at[step], k, 0), weight_block(blocks.at[step], k + 1, 0)]
+                total += mm(jnp.concatenate(left, axis=1), jnp.concatenate(right, axis=0))
         out_ref[part] = total
 
 
@@ -189,7 +183,7 @@
     blocks = []
     for z in range(2):
         for y in range(4):
-            block = rows_ref[y, 1536 + z * 32 : 1568 + z * 32, :].astype(F32)
+            block = rows_ref[y, 384 + z * 32 : 416 + z * 32, :].astype(F32)
             blocks.append(jnp.concatenate([block[v * 8 : v * 8 + 8] for v in range(4)], axis=1))
     terms = mm(jnp.concatenate(blocks, axis=0).astype(BF16), unembed_ref[...])
     for j in range(8):
@@ -205,24 +199,33 @@
         ref[p, pl.ds(pl.multiple_of(row + place * 16, 16), 16), :] = rows
 
 
-def proj_kernel(at_ref, gained_ref, scale_ref, near_ref, own_taps, got_taps, f0, f1, f2, f3, sig_ref, gate_ref):
-    y_at, x_at, core = at_ref[0], at_ref[1], at_ref[2]
+def proj_kernel(
+    at_ref, gained_ref, scale_ref, near_ref, own_hbm, got_hbm, far_hbm, sig_ref, gate_ref, taps, far, sems
+):
+    core = at_ref[2]
     start = 2048 - at_ref[3] * 2048
     half = pl.ds(pl.multiple_of(core * 128, 128), 128)
+    copies = [pltpu.make_async_copy(far_hbm.at[x], far.at[x], sems.at[x]) for x in range(4)]
+    copies.append(pltpu.make_async_copy(own_hbm, taps.at[0], sems.at[4]))
+    copies.append(pltpu.make_async_copy(got_hbm, taps.at[1], sems.at[5]))
+    for copy in copies:
+        copy.start()
     for part in range(2):
         total = near_ref[part]
-        for step, ref in enumerate((f0, f1, f2, f3)):
-            x = lax.rem(x_at + 4 - step, 4)
-            for k in (0, 2):
-                starts = [start + (lax.rem(y_at + 4 - j, 4) * 4 + x) * 128 for j in (k, k + 1)]
+        for x in range(4):
+            if part == 0:
+                copies[x].wait()
+            for y in (0, 2):
+                starts = [start + (k * 4 + x) * 128 for k in (y, y + 1)]
                 left = [gained_ref[part, :, pl.ds(pl.multiple_of(at, 128), 128)] for at in starts]
-                right = [weight_block(ref, k, 0), weight_block(ref, k + 1, 0)]
+                right = [weight_block(far, x, y * 384), weight_block(far, x, y * 384 + 384)]
                 total += mm(jnp.concatenate(left, axis=1), jnp.concatenate(right, axis=0))
         scale = scale_ref[part]
         proj = (total * jnp.concatenate([scale, scale, scale], axis=1)).astype(BF16).astype(F32)
         place = core if part == 0 else 1 - core
         put_pieces(sig_ref, 0, place, proj[:, 128:256] * proj[:, 256:])
-        put_pieces(sig_ref, 32, place, (own_taps if part == 0 else got_taps)[:, half].astype(F32))
+        copies[4 + part].wait()
+        put_pieces(sig_ref, 32, place, taps[part, :, half].astype(F32))
         gate_ref[place, 0] = proj[:128, :128].T.astype(BF16)
         gate_ref[place, 1] = proj[128:, :128].T.astype(BF16)
 
@@ -296,51 +299,53 @@
 
     core_at = core.reshape(1).astype(jnp.int32)
     w_in = w_in.transpose(1, 0, 2)
-    first = call(
-        first_kernel,
-        shape((512, 128), BF16),
-        [SCALARS] + whole(3),
-        [],
-        10**5,
-        (core_at, w_in, lax.ppermute(w_in, "ctx", PERM_CORE), w_out),
-    )
-    near = call(copies_kernel, shape((4, 384, 128), BF16), whole(1), [], 10**10, (first,))
+    keep = lax.dynamic_slice_in_dim(w_in, core * 128, 128, 2)
+    got = lax.dynamic_slice_in_dim(lax.ppermute(w_in, "ctx", PERM_CORE), core * 128, 128, 2)
+    near = jnp.concatenate([jnp.where(core == 0, keep, got), jnp.where(core == 0, got, keep)], axis=1)
+    rows = w_out.reshape(4, 8, 4, 128).transpose(0, 2, 1, 3).reshape(128, 128)
+    first = jnp.concatenate([near.reshape(384, 128), rows])
+    near = call(copy_kernel, shape((384, 128), BF16), whole(1), [], 10**10, (first,))
     near, tokens = lax.optimization_barrier((near, tokens_in))
     beside = lax.ppermute(tokens, "ctx", PERM_CORE)
-    near = lax.all_to_all(near, "ctx", 0, 0, axis_index_groups=GROUPS_X, tiled=True)
+    near = jnp.stack([near] + [lax.ppermute(near, "ctx", PERM_X[k]) for k in (1, 2, 3)])
     far = lax.ppermute(first, "ctx", PERM_Z)
 
     rows = by_position(first[384:].reshape(4, 32, 128), far[384:].reshape(4, 32, 128), z)
-    far = far[:384]
-    far = jnp.stack([far] + [lax.ppermute(far, "ctx", PERM_Y[k]) for k in (1, 2, 3)])
-    near, far, rows, taps = lax.optimization_barrier((near, far, rows, long_filter))
-
-    near = jnp.broadcast_to(near.reshape(1, 1536, 128), (4, 1536, 128))
-    near = jnp.concatenate([near, rows[0], rows[1]], axis=1)
-    near = lax.all_to_all(near, "ctx", 0, 0, axis_index_groups=GROUPS_Y, tiled=True)
-    fars = [far] + [lax.ppermute(far, "ctx", PERM_X[k]) for k in (1, 2, 3)]
+    far = jnp.concatenate([jnp.broadcast_to(far[:384], (4, 384, 128)), rows[0], rows[1]], axis=1)
+    rows = lax.all_to_all(far, "ctx", 0, 0, axis_index_groups=GROUPS_Y, tiled=True)
+    near, rows, taps = lax.optimization_barrier((near, rows, long_filter))
+
+    far = jnp.broadcast_to(rows[:, :384].reshape(1, 1536, 128), (4, 1536, 128))
+    far = lax.all_to_all(far, "ctx", 0, 0, axis_index_groups=GROUPS_X, tiled=True)
+    nears = [near] + [lax.ppermute(near, "ctx", PERM_Y[k]) for k in (1, 2, 3)]
     taps_got = lax.ppermute(taps, "ctx", PERM_CORE)
 
     at = jnp.stack([(ctx // 8) % 4, (ctx // 2) % 4, core, z]).astype(jnp.int32)
+    anywhere = pl.BlockSpec(memory_space=pl.ANY)
     gained, scale, sums = call(
         near_kernel,
         (shape((2, 256, 4096), BF16), shape((2, 256, 128), F32), shape((2, 256, 384), F32)),
-        [SCALARS] + [pl.BlockSpec(memory_space=pl.ANY)] * 2 + whole(2),
-        [pltpu.VMEM((2, 256, 4096), BF16), pltpu.SemaphoreType.DMA((2, 4))],
+        [SCALARS, anywhere, anywhere] + whole(1) + [anywhere] * 4,
+        [
+            pltpu.VMEM((2, 256, 4096), BF16),
+            pltpu.VMEM((4, 4, 384, 128), BF16),
+            pltpu.SemaphoreType.DMA((3, 4)),
+        ],
         8 * 10**8,
-        (at, tokens_in, beside, pre_gain.reshape(1, 4096), near),
+        (at, tokens_in, beside, pre_gain.reshape(1, 4096), *nears),
+        mib=12,
     )
     signal, gate = call(
         proj_kernel,
         (shape((16, 64, 128), BF16), shape((2, 2, 128, 128), BF16)),
-        [SCALARS] + whole(9),
-        [],
+        [SCALARS] + whole(3) + [anywhere] * 3,
+        [pltpu.VMEM((2, 256, 256), BF16), pltpu.VMEM((4, 1536, 128), BF16), pltpu.SemaphoreType.DMA((6,))],
         8 * 10**8,
-        (at, gained, scale, sums, taps, taps_got, *fars),
+        (at, gained, scale, sums, taps, taps_got, far),
     )
     got = lax.all_to_all(signal, "ctx", 0, 0, axis_index_groups=GROUPS_CORE, tiled=True)
     before = lax.ppermute(got, "ctx", PERM_Z_UP)
-    terms = call(product_kernel, shape((8, 32, 128), BF16), whole(2), [], 4 * 10**7, (near, w_unembed))
+    terms = call(product_kernel, shape((8, 32, 128), BF16), whole(2), [], 4 * 10**7, (rows, w_unembed))
     terms, _ = lax.optimization_barrier((terms, got))
     terms = lax.all_to_all(terms, "tp", 0, 0, tiled=True)
     gate_keep = lax.dynamic_index_in_dim(gate, core, 0, False)

time: 179 us -> 197 us (1.10)
  local copies, waits for them, and re-layouts: 6.48 us -> 15.6 us
  starting transfers between devices: 81.4 us -> 90.2 us
  waiting for transfers between devices: 41.3 us -> 36.9 us
    all_to_all x2, waiting for transfers between devices: 9.9 us -> 0.01 us  [the longest x1 0.01 us: per_device(): lax.all_to_all(far, 'ctx', 0, 0, axis_index_groups=GROUPS_Y, tiled=True)]
    ppermute x6, waiting for transfers between devices: 3.24 us -> 12.8 us  [the longest x3 6.98 us: per_device(): nears = [near] + [lax.ppermute(near, 'ctx', PERM_Y[k]) for k in (1, 2, 3)]]
    unnamed x30 -> x44, local copies, waits for them, and re-layouts: 4.98 us -> 12.8 us
    all_to_all x1, waiting for transfers between devices: 11.4 us -> 6.43 us  [per_device(): terms = lax.all_to_all(terms, 'tp', 0, 0, tiled=True)]
    ppermute x1, starting transfers between devices: 7.89 us -> 12.3 us  [per_device(): before = lax.ppermute(got, 'ctx', PERM_Z_UP)]
    ppermute x1, waiting for transfers between devices: 0.01 us -> 4.27 us  [per_device(): far = lax.ppermute(first, 'ctx', PERM_Z)]
    ppermute x1, waiting for transfers between devices: 10.6 us -> 7.19 us  [per_device(): far = lax.ppermute(logits, 'tp', [(i, i ^ 4) for i in range(8)])]
    ppermute x1, starting transfers between devices: 2.66 us -> 6.07 us  [per_device(): far = lax.ppermute(logits, 'tp', [(i, i ^ 4) for i in range(8)])]
  transfers between devices with their start and end apart: 17 -> 17, of which waited for: 7 -> 10; matrix products, arithmetic and copies ran while one was open for 2% -> 2% of each run, Pallas kernels for 5% -> 4%
where the time goes in v13:
time: 197 us; the launch traced here: 195 us
  starting transfers between devices  90.2 us (46%)
  waiting for transfers between devices  36.9 us (19%)
  blocking collectives  34.3 us (17%)
  local copies, waits for them, and re-layouts  15.6 us (8%)
  Pallas kernels  12.9 us (7%)
  other arithmetic  3.66 us (2%)
    ppermute x1, starting transfers between devices, per_device(): far = lax.ppermute(first, 'ctx', PERM_Z)  15.7 us
    all_to_all x1, blocking collectives, per_device(): lax.all_to_all(signal, 'ctx', 0, 0, axis_index_groups=GROUPS_CORE, tiled=...  13.8 us
    pallas_call x8, Pallas kernels, call(): pl.pallas_call(kernel, out_shape=outs, in_specs=specs, out_specs=jax.tree...  12.9 us
    unnamed x44, local copies, waits for them, and re-layouts  12.8 us
    all_to_all x1, blocking collectives, per_device(): lax.all_to_all(logits.reshape(4, 64, 512), 'tp', 0, 0, axis_index_groups=...  12.7 us
    all_to_all x1, starting transfers between devices, per_device(): terms = lax.all_to_all(terms, 'tp', 0, 0, tiled=True)  12.3 us
    ppermute x1, starting transfers between devices, per_device(): before = lax.ppermute(got, 'ctx', PERM_Z_UP)  12.3 us
    ppermute x3, starting transfers between devices, per_device(): nears = [near] + [lax.ppermute(near, 'ctx', PERM_Y[k]) for k in (1, 2, 3)]  11.9 us
  transfers between devices with their start and end apart: 17, of which 10 were waited for; matrix products, arithmetic and copies ran while one was open for 2% of the time, Pallas kernels for 4%

profile of v13, /device:TPU:6, one launch (start us, length us, event | category | flops | bytes accessed | tf_op | source)
XLA Modules:
  0.0 195.2 jit_solution(11539937554785979578)
XLA Ops:
  0.0 1.9 collective-permute-start
  5.0 2.1 %collective-permute-start.1 = (bf16[256,4096]{1,0:T(8,128)(2,1)}, bf16[256,4096]{1,0:T(8,128)(2,1)}, u32[]{:S(2)}, u32[]{:S(2)}) collective-permute-start(bf16[256,4096]{1,0:T(8,128)(2,1)} %own_hbm.1), channel_id=1, source_target_pairs={{0,8},{8,0},{16,24},{24,16},{32,40},{40,32},{48,56},{56,48},{64,72... | collective-permute-start | bytes 6291464 | tf_op jit(solution)/shard_map/ppermute | solution.py:309
  7.1 15.7 %collective-permute-start.5 = (bf16[512,128]{1,0:T(8,128)(2,1)S(1)}, bf16[512,128]{1,0:T(8,128)(2,1)S(1)}, u32[]{:S(2)}, u32[]{:S(2)}) collective-permute-start(bf16[512,128]{1,0:T(8,128)(2,1)S(1)} %pad_maximum_fusion.2.first_ref), channel_id=1, source_target_pairs={{0,256},{8,264},{16,272},{24,280},{32,288},{40,296},{48,304},{56,3... | collective-permute-start | bytes 393224 | tf_op jit(solution)/shard_map/ppermute | solution.py:311
  22.9 4.3 %collective-permute-done.5 = bf16[512,128]{1,0:T(8,128)(2,1)S(1)} collective-permute-done((bf16[512,128]{1,0:T(8,128)(2,1)S(1)}, bf16[512,128]{1,0:T(8,128)(2,1)S(1)}, u32[]{:S(2)}, u32[]{:S(2)}) %collective-permute-start.5) | collective-permute-done | bytes 131104 | tf_op jit(solution)/shard_map/ppermute | solution.py:311
  28.1 4.5 %all-to-all-start = ((bf16[4,448,128]{2,1,0:T(8,128)(2,1)}), bf16[4,448,128]{2,1,0:T(8,128)(2,1)S(1)}, u32[]{:S(2)}, u32[]{:S(2)}) async-start(bf16[4,448,128]{2,1,0:T(8,128)(2,1)} %pad_maximum_fusion), calls=%async_computation | async-start | bytes 917504 | tf_op jit(solution)/shard_map/all_to_all | solution.py:315
  32.5 3.2 %collective-permute-start.2 = (bf16[384,128]{1,0:T(8,128)(2,1)S(1)}, bf16[384,128]{1,0:T(8,128)(2,1)S(1)}, u32[]{:S(2)}, u32[]{:S(2)}) collective-permute-start(bf16[384,128]{1,0:T(8,128)(2,1)S(1)} %shard_map.118), channel_id=1, source_target_pairs={{0,16},{8,24},{16,32},{24,40},{32,48},{40,56},{48,0},{56,8},{64,80... | collective-permute-start | bytes 294920 | tf_op jit(solution)/shard_map/ppermute | solution.py:310
  35.8 3.5 %collective-permute-start.3 = (bf16[384,128]{1,0:T(8,128)(2,1)S(1)}, bf16[384,128]{1,0:T(8,128)(2,1)S(1)}, u32[]{:S(2)}, u32[]{:S(2)}) collective-permute-start(bf16[384,128]{1,0:T(8,128)(2,1)S(1)} %shard_map.118), channel_id=1, source_target_pairs={{0,32},{8,40},{16,48},{24,56},{32,0},{40,8},{48,16},{56,24},{64,96... | collective-permute-start | bytes 294920 | tf_op jit(solution)/shard_map/ppermute | solution.py:310
  39.3 1.9 collective-permute-start.4
  41.2 2.7 %collective-permute-done.3 = bf16[384,128]{1,0:T(8,128)(2,1)S(1)} collective-permute-done((bf16[384,128]{1,0:T(8,128)(2,1)S(1)}, bf16[384,128]{1,0:T(8,128)(2,1)S(1)}, u32[]{:S(2)}, u32[]{:S(2)}) %collective-permute-start.3) | collective-permute-done | bytes 98336 | tf_op jit(solution)/shard_map/ppermute | solution.py:310
  44.0 3.0 %collective-permute-done.4 = bf16[384,128]{1,0:T(8,128)(2,1)S(1)} collective-permute-done((bf16[384,128]{1,0:T(8,128)(2,1)S(1)}, bf16[384,128]{1,0:T(8,128)(2,1)S(1)}, u32[]{:S(2)}, u32[]{:S(2)}) %collective-permute-start.4) | collective-permute-done | bytes 98336 | tf_op jit(solution)/shard_map/ppermute | solution.py:310
  48.5 4.6 %all-to-all-start.1 = ((bf16[4,1536,128]{2,1,0:T(8,128)(2,1)}), bf16[4,1536,128]{2,1,0:T(8,128)(2,1)S(1)}, u32[]{:S(2)}, u32[]{:S(2)}) async-start(bf16[4,1536,128]{2,1,0:T(8,128)(2,1)} %broadcast_in_dim.24), calls=%async_computation.1 | async-start | bytes 3145728 | tf_op jit(solution)/shard_map/all_to_all | solution.py:319
  53.1 3.9 %collective-permute-start.6 = (bf16[4,384,128]{2,1,0:T(8,128)(2,1)S(1)}, bf16[4,384,128]{2,1,0:T(8,128)(2,1)S(1)}, u32[]{:S(2)}, u32[]{:S(2)}) collective-permute-start(bf16[4,384,128]{2,1,0:T(8,128)(2,1)S(1)} %pad_maximum_fusion.1.n0), channel_id=1, source_target_pairs={{0,64},{8,72},{16,80},{24,88},{32,96},{40,104},{48,112},{56,120},{... | collective-permute-start | bytes 1179656 | tf_op jit(solution)/shard_map/ppermute | solution.py:320
  57.0 4.6 %collective-permute-start.7 = (bf16[4,384,128]{2,1,0:T(8,128)(2,1)S(1)}, bf16[4,384,128]{2,1,0:T(8,128)(2,1)S(1)}, u32[]{:S(2)}, u32[]{:S(2)}) collective-permute-start(bf16[4,384,128]{2,1,0:T(8,128)(2,1)S(1)} %pad_maximum_fusion.1.n0), channel_id=1, source_target_pairs={{0,128},{8,136},{16,144},{24,152},{32,160},{40,168},{48,176},{56,1... | collective-permute-start | bytes 1179656 | tf_op jit(solution)/shard_map/ppermute | solution.py:320
  61.6 3.4 %collective-permute-start.8 = (bf16[4,384,128]{2,1,0:T(8,128)(2,1)S(1)}, bf16[4,384,128]{2,1,0:T(8,128)(2,1)}, u32[]{:S(2)}, u32[]{:S(2)}) collective-permute-start(bf16[4,384,128]{2,1,0:T(8,128)(2,1)S(1)} %pad_maximum_fusion.1.n0), channel_id=1, source_target_pairs={{0,192},{8,200},{16,208},{24,216},{32,224},{40,232},{48,240},{56,2... | collective-permute-start | bytes 1179656 | tf_op jit(solution)/shard_map/ppermute | solution.py:320
  65.0 1.9 collective-permute-start.9
  68.1 6.0 %collective-permute-done.7.n2 = bf16[4,384,128]{2,1,0:T(8,128)(2,1)S(1)} collective-permute-done((bf16[4,384,128]{2,1,0:T(8,128)(2,1)S(1)}, bf16[4,384,128]{2,1,0:T(8,128)(2,1)S(1)}, u32[]{:S(2)}, u32[]{:S(2)}) %collective-permute-start.7) | collective-permute-done | bytes 393248 | tf_op jit(solution)/shard_map/ppermute | solution.py:320
  77.6 4.6 %shard_map.119 = (bf16[2,256,4096]{2,1,0:T(8,128)(2,1)S(1)}, f32[2,256,128]{2,1,0:T(8,128)S(1)}, f32[2,256,384]{2,1,0:T(8,128)S(1)}) custom-call(s32[4]{0:T(128)S(1)} %pad_add_fusion.at_ref, bf16[256,4096]{1,0:T(8,128)(2,1)} %own_hbm.1, bf16[256,4096]{1,0:T(8,128)(2,1)} %collective-permute-done.1.beside_hbm, bf16[1,4096]{1,0:T(2,128)(2,1)S(1)} %reshape.40.gain_ref, ...), custom_call_target="tpu_custom_call" | custom-call | flops 800000000 | bytes 4194304 | tf_op jit(solution)/shard_map/pallas_call | solution.py:253
  82.2 2.0 %copy-done = bf16[2,256,4096]{2,1,0:T(8,128)(2,1)} copy-done((bf16[2,256,4096]{2,1,0:T(8,128)(2,1)}, bf16[2,256,4096]{2,1,0:T(8,128)(2,1)S(1)}, u32[]{:S(2)}) %copy-start) | copy-done | bytes 4194328
  85.5 2.2 %copy-done.1 = bf16[2,256,4096]{2,1,0:T(8,128)(2,1)S(1)} copy-done((bf16[2,256,4096]{2,1,0:T(8,128)(2,1)S(1)}, bf16[2,256,4096]{2,1,0:T(8,128)(2,1)}, u32[]{:S(2)}) %copy-start.1) | copy-done | bytes 4194328
  89.5 3.8 %shard_map.120 = (bf16[16,64,128]{2,1,0:T(8,128)(2,1)S(1)}, bf16[2,2,128,128]{3,2,1,0:T(8,128)(2,1)S(1)}) custom-call(s32[4]{0:T(128)S(1)} %pad_add_fusion.at_ref, bf16[2,256,4096]{2,1,0:T(8,128)(2,1)S(1)} %copy-done.1, f32[2,256,128]{2,1,0:T(8,128)S(1)} %copy-done.10, f32[2,256,384]{2,1,0:T(8,128)S(1)} %get-tuple-element.23.near_ref, ...), custom_call_target="tpu_custom_call" | custom-call | flops 800000000 | bytes 4194304 | tf_op jit(solution)/shard_map/pallas_call | solution.py:253
  93.4 13.8 %all_to_all.36.got_ref = bf16[16,64,128]{2,1,0:T(8,128)(2,1)S(1)} all-to-all(bf16[16,64,128]{2,1,0:T(8,128)(2,1)S(1)} %get-tuple-element.26), channel_id=1, replica_groups={{0,16,32,48,64,80,96,112,128,144,160,176,192,208,224,240},{8,24,40,56,7..., dimensions={0} | all-to-all | bytes 524288 | tf_op jit(solution)/shard_map/all_to_all | solution.py:346
  107.2 12.3 %collective-permute-start.10 = (bf16[16,64,128]{2,1,0:T(8,128)(2,1)S(1)}, bf16[16,64,128]{2,1,0:T(8,128)(2,1)S(1)}, u32[]{:S(2)}, u32[]{:S(2)}) collective-permute-start(bf16[16,64,128]{2,1,0:T(8,128)(2,1)S(1)} %all_to_all.36.got_ref), channel_id=1, source_target_pairs={{0,256},{8,264},{16,272},{24,280},{32,288},{40,296},{48,304},{56,3... | collective-permute-start | bytes 786440 | tf_op jit(solution)/shard_map/ppermute | solution.py:347
  120.4 12.3 %all-to-all-start.3 = ((bf16[8,32,128]{2,1,0:T(8,128)(2,1)}), bf16[8,32,128]{2,1,0:T(8,128)(2,1)S(1)}, u32[]{:S(2)}, u32[]{:S(2)}) async-start(bf16[8,32,128]{2,1,0:T(8,128)(2,1)} %shard_map.123), calls=%async_computation.3 | async-start | bytes 131072 | tf_op jit(solution)/shard_map/all_to_all | solution.py:350
  135.7 1.5 shard_map.122.conv_ref
  137.2 6.4 %all-to-all-done.3.terms_ref = bf16[8,32,128]{2,1,0:T(8,128)(2,1)S(1)} async-done(((bf16[8,32,128]{2,1,0:T(8,128)(2,1)}), bf16[8,32,128]{2,1,0:T(8,128)(2,1)S(1)}, u32[]{:S(2)}, u32[]{:S(2)}) %all-to-all-start.3) | async-done | bytes 65568 | tf_op jit(solution)/shard_map/all_to_all | solution.py:350
  144.4 6.2 %all-to-all-start.4 = ((bf16[32,48,128]{2,1,0:T(8,128)(2,1)}), bf16[32,48,128]{2,1,0:T(8,128)(2,1)S(1)}, u32[]{:S(2)}, u32[]{:S(2)}) async-start(bf16[32,48,128]{2,1,0:T(8,128)(2,1)} %shard_map.124), calls=%async_computation.4 | async-start | bytes 786432 | tf_op jit(solution)/shard_map/all_to_all | solution.py:356
  150.6 2.1 %collective-permute-start.11 = (bf16[2,128,128]{2,1,0:T(8,128)(2,1)S(1)}, bf16[2,128,128]{2,1,0:T(8,128)(2,1)S(1)}, u32[]{:S(2)}, u32[]{:S(2)}) collective-permute-start(bf16[2,128,128]{2,1,0:T(8,128)(2,1)S(1)} %get-tuple-element.35), channel_id=1, source_target_pairs={{0,8},{8,0},{16,24},{24,16},{32,40},{40,32},{48,56},{56,48},{64,72... | collective-permute-start | bytes 196616 | tf_op jit(solution)/shard_map/ppermute | solution.py:352
  154.0 4.7 %all-to-all-done.4.got_ref = bf16[32,48,128]{2,1,0:T(8,128)(2,1)S(1)} async-done(((bf16[32,48,128]{2,1,0:T(8,128)(2,1)}), bf16[32,48,128]{2,1,0:T(8,128)(2,1)S(1)}, u32[]{:S(2)}, u32[]{:S(2)}) %all-to-all-start.4) | async-done | bytes 393248 | tf_op jit(solution)/shard_map/all_to_all | solution.py:356
  159.1 12.7 %all_to_all.37 = bf16[4,64,512]{2,1,0:T(8,128)(2,1)S(1)} all-to-all(bf16[4,64,512]{2,1,0:T(8,128)(2,1)S(1)} %bitcast.32), channel_id=1, replica_groups={{0,1,2,3},{4,5,6,7},{8,9,10,11},{12,13,14,15},{16,17,18,19},{20,21,22,2..., dimensions={0} | all-to-all | bytes 524288 | tf_op jit(solution)/shard_map/all_to_all | solution.py:368
  171.7 6.1 %collective-permute-start.12 = (bf16[64,512]{1,0:T(8,128)(2,1)S(1)}, bf16[64,512]{1,0:T(8,128)(2,1)S(1)}, u32[]{:S(2)}, u32[]{:S(2)}) collective-permute-start(bf16[64,512]{1,0:T(8,128)(2,1)S(1)} %reduce_sum.30), channel_id=1, source_target_pairs={{0,4},{1,5},{2,6},{3,7},{4,0},{5,1},{6,2},{7,3},{8,12},{9,13},{10,... | collective-permute-start | bytes 196616 | tf_op jit(solution)/shard_map/ppermute | solution.py:370
  177.9 7.2 %collective-permute-done.12 = bf16[64,512]{1,0:T(8,128)(2,1)S(1)} collective-permute-done((bf16[64,512]{1,0:T(8,128)(2,1)S(1)}, bf16[64,512]{1,0:T(8,128)(2,1)S(1)}, u32[]{:S(2)}, u32[]{:S(2)}) %collective-permute-start.12) | collective-permute-done | bytes 65568 | tf_op jit(solution)/shard_map/ppermute | solution.py:370
  185.5 7.9 %all_to_all.38 = f32[4,1,64]{2,1,0:T(1,128)S(1)} all-to-all(f32[4,1,64]{2,1,0:T(1,128)S(1)} %broadcast_in_dim.26), channel_id=1, replica_groups={{0,1,2,3},{4,5,6,7},{8,9,10,11},{12,13,14,15},{16,17,18,19},{20,21,22,2..., dimensions={0} | all-to-all | bytes 2048 | tf_op jit(solution)/shard_map/all_to_all | solution.py:381
  (82 shorter events, 21.7 us)
Async XLA Ops:
  0.0 3.4 %collective-permute-start = (bf16[3,64,256]{2,1,0:T(8,128)(2,1)}, bf16[3,64,256]{2,1,0:T(8,128)(2,1)S(1)}, u32[]{:S(2)}, u32[]{:S(2)}) collective-permute-start(bf16[3,64,256]{2,1,0:T(8,128)(2,1)} %bitcast.42), channel_id=1, source_target_pairs={{0,8},{8,0},{16,24},{24,16},{32,40},{40,32},{48,56},{56,48},{64,72... | collective-permute-start | bytes 294920 | tf_op jit(solution)/shard_map/ppermute | solution.py:303
  5.0 22.2 %copy-start.18 = (bf16[32,512]{1,0:T(8,128)(2,1)S(1)}, bf16[32,512]{1,0:T(8,128)(2,1)}, u32[]{:S(2)}) copy-start(bf16[32,512]{1,0:T(8,128)(2,1)} %param.15) | copy-start | bytes 98308
  5.0 70.5 %collective-permute-start.1 = (bf16[256,4096]{1,0:T(8,128)(2,1)}, bf16[256,4096]{1,0:T(8,128)(2,1)}, u32[]{:S(2)}, u32[]{:S(2)}) collective-permute-start(bf16[256,4096]{1,0:T(8,128)(2,1)} %own_hbm.1), channel_id=1, source_target_pairs={{0,8},{8,0},{16,24},{24,16},{32,40},{40,32},{48,56},{56,48},{64,72... | collective-permute-start | bytes 6291464 | tf_op jit(solution)/shard_map/ppermute | solution.py:309
  7.1 20.0 %collective-permute-start.5 = (bf16[512,128]{1,0:T(8,128)(2,1)S(1)}, bf16[512,128]{1,0:T(8,128)(2,1)S(1)}, u32[]{:S(2)}, u32[]{:S(2)}) collective-permute-start(bf16[512,128]{1,0:T(8,128)(2,1)S(1)} %pad_maximum_fusion.2.first_ref), channel_id=1, source_target_pairs={{0,256},{8,264},{16,272},{24,280},{32,288},{40,296},{48,304},{56,3... | collective-permute-start | bytes 393224 | tf_op jit(solution)/shard_map/ppermute | solution.py:311
  28.1 19.0 %all-to-all-start = ((bf16[4,448,128]{2,1,0:T(8,128)(2,1)}), bf16[4,448,128]{2,1,0:T(8,128)(2,1)S(1)}, u32[]{:S(2)}, u32[]{:S(2)}) async-start(bf16[4,448,128]{2,1,0:T(8,128)(2,1)} %pad_maximum_fusion), calls=%async_computation | async-start | bytes 917504 | tf_op jit(solution)/shard_map/all_to_all | solution.py:315
  32.5 8.6 %collective-permute-start.2 = (bf16[384,128]{1,0:T(8,128)(2,1)S(1)}, bf16[384,128]{1,0:T(8,128)(2,1)S(1)}, u32[]{:S(2)}, u32[]{:S(2)}) collective-permute-start(bf16[384,128]{1,0:T(8,128)(2,1)S(1)} %shard_map.118), channel_id=1, source_target_pairs={{0,16},{8,24},{16,32},{24,40},{32,48},{40,56},{48,0},{56,8},{64,80... | collective-permute-start | bytes 294920 | tf_op jit(solution)/shard_map/ppermute | solution.py:310
  35.8 8.2 %collective-permute-start.3 = (bf16[384,128]{1,0:T(8,128)(2,1)S(1)}, bf16[384,128]{1,0:T(8,128)(2,1)S(1)}, u32[]{:S(2)}, u32[]{:S(2)}) collective-permute-start(bf16[384,128]{1,0:T(8,128)(2,1)S(1)} %shard_map.118), channel_id=1, source_target_pairs={{0,32},{8,40},{16,48},{24,56},{32,0},{40,8},{48,16},{56,24},{64,96... | collective-permute-start | bytes 294920 | tf_op jit(solution)/shard_map/ppermute | solution.py:310
  39.3 7.7 %collective-permute-start.4 = (bf16[384,128]{1,0:T(8,128)(2,1)S(1)}, bf16[384,128]{1,0:T(8,128)(2,1)S(1)}, u32[]{:S(2)}, u32[]{:S(2)}) collective-permute-start(bf16[384,128]{1,0:T(8,128)(2,1)S(1)} %shard_map.118), channel_id=1, source_target_pairs={{0,48},{8,56},{16,0},{24,8},{32,16},{40,24},{48,32},{56,40},{64,11... | collective-permute-start | bytes 294920 | tf_op jit(solution)/shard_map/ppermute | solution.py:310
  48.4 16.6 %copy-start.11 = (bf16[256,256]{1,0:T(8,128)(2,1)S(1)}, bf16[256,256]{1,0:T(8,128)(2,1)}, u32[]{:S(2)}) copy-start(bf16[256,256]{1,0:T(8,128)(2,1)} %own_hbm.2) | copy-start | bytes 393220
  48.4 18.6 %copy-start.19 = (bf16[4096]{0:T(1024)(128)(2,1)S(1)}, bf16[4096]{0:T(1024)(128)(2,1)}, u32[]{:S(2)}) copy-start(bf16[4096]{0:T(1024)(128)(2,1)} %param.13) | copy-start | bytes 24580
  48.5 37.0 %all-to-all-start.1 = ((bf16[4,1536,128]{2,1,0:T(8,128)(2,1)}), bf16[4,1536,128]{2,1,0:T(8,128)(2,1)S(1)}, u32[]{:S(2)}, u32[]{:S(2)}) async-start(bf16[4,1536,128]{2,1,0:T(8,128)(2,1)} %broadcast_in_dim.24), calls=%async_computation.1 | async-start | bytes 3145728 | tf_op jit(solution)/shard_map/all_to_all | solution.py:319
  53.1 14.3 %collective-permute-start.6 = (bf16[4,384,128]{2,1,0:T(8,128)(2,1)S(1)}, bf16[4,384,128]{2,1,0:T(8,128)(2,1)S(1)}, u32[]{:S(2)}, u32[]{:S(2)}) collective-permute-start(bf16[4,384,128]{2,1,0:T(8,128)(2,1)S(1)} %pad_maximum_fusion.1.n0), channel_id=1, source_target_pairs={{0,64},{8,72},{16,80},{24,88},{32,96},{40,104},{48,112},{56,120},{... | collective-permute-start | bytes 1179656 | tf_op jit(solution)/shard_map/ppermute | solution.py:320
  57.0 17.1 %collective-permute-start.7 = (bf16[4,384,128]{2,1,0:T(8,128)(2,1)S(1)}, bf16[4,384,128]{2,1,0:T(8,128)(2,1)S(1)}, u32[]{:S(2)}, u32[]{:S(2)}) collective-permute-start(bf16[4,384,128]{2,1,0:T(8,128)(2,1)S(1)} %pad_maximum_fusion.1.n0), channel_id=1, source_target_pairs={{0,128},{8,136},{16,144},{24,152},{32,160},{40,168},{48,176},{56,1... | collective-permute-start | bytes 1179656 | tf_op jit(solution)/shard_map/ppermute | solution.py:320
  61.6 14.0 %collective-permute-start.8 = (bf16[4,384,128]{2,1,0:T(8,128)(2,1)S(1)}, bf16[4,384,128]{2,1,0:T(8,128)(2,1)}, u32[]{:S(2)}, u32[]{:S(2)}) collective-permute-start(bf16[4,384,128]{2,1,0:T(8,128)(2,1)S(1)} %pad_maximum_fusion.1.n0), channel_id=1, source_target_pairs={{0,192},{8,200},{16,208},{24,216},{32,224},{40,232},{48,240},{56,2... | collective-permute-start | bytes 1179656 | tf_op jit(solution)/shard_map/ppermute | solution.py:320
  65.0 19.8 %collective-permute-start.9 = (bf16[256,256]{1,0:T(8,128)(2,1)S(1)}, bf16[256,256]{1,0:T(8,128)(2,1)S(1)}, u32[]{:S(2)}, u32[]{:S(2)}) collective-permute-start(bf16[256,256]{1,0:T(8,128)(2,1)S(1)} %copy-done.11), channel_id=1, source_target_pairs={{0,8},{8,0},{16,24},{24,16},{32,40},{40,32},{48,56},{56,48},{64,72... | collective-permute-start | bytes 393224 | tf_op jit(solution)/shard_map/ppermute | solution.py:321
  75.6 1.0 copy-start.6
  76.6 1.0 copy-start.8
  82.2 2.0 %copy-start = (bf16[2,256,4096]{2,1,0:T(8,128)(2,1)}, bf16[2,256,4096]{2,1,0:T(8,128)(2,1)S(1)}, u32[]{:S(2)}) copy-start(bf16[2,256,4096]{2,1,0:T(8,128)(2,1)S(1)} %get-tuple-element.21.gained_ref) | copy-start | bytes 12582916
  85.5 2.2 %copy-start.1 = (bf16[2,256,4096]{2,1,0:T(8,128)(2,1)S(1)}, bf16[2,256,4096]{2,1,0:T(8,128)(2,1)}, u32[]{:S(2)}) copy-start(bf16[2,256,4096]{2,1,0:T(8,128)(2,1)} %copy-done) | copy-start | bytes 12582916
  89.5 30.0 %copy-start.2 = (bf16[512,512]{1,0:T(8,128)(2,1)S(1)}, bf16[512,512]{1,0:T(8,128)(2,1)}, u32[]{:S(2)}) copy-start(bf16[512,512]{1,0:T(8,128)(2,1)} %unembed_ref.1) | copy-start | bytes 1572868
  93.4 13.8 %copy-start.16 = (bf16[2,2,128,128]{3,2,1,0:T(8,128)(2,1)}, bf16[2,2,128,128]{3,2,1,0:T(8,128)(2,1)S(1)}, u32[]{:S(2)}) copy-start(bf16[2,2,128,128]{3,2,1,0:T(8,128)(2,1)S(1)} %get-tuple-element.30) | copy-start | bytes 393220
  93.4 42.2 %copy-start.4 = (bf16[832,256]{1,0:T(8,128)(2,1)S(1)}, bf16[832,256]{1,0:T(8,128)(2,1)}, u32[]{:S(2)}) copy-start(bf16[832,256]{1,0:T(8,128)(2,1)} %constant.103.clone.matrices) | copy-start | bytes 1277956
  93.4 42.2 %copy-start.15 = (f32[128,256]{1,0:T(8,128)S(1)}, f32[128,256]{1,0:T(8,128)}, u32[]{:S(2)}) copy-start(f32[128,256]{1,0:T(8,128)} %constant.104.clone.twiddles) | copy-start | bytes 393220
  107.2 28.4 %collective-permute-start.10 = (bf16[16,64,128]{2,1,0:T(8,128)(2,1)S(1)}, bf16[16,64,128]{2,1,0:T(8,128)(2,1)S(1)}, u32[]{:S(2)}, u32[]{:S(2)}) collective-permute-start(bf16[16,64,128]{2,1,0:T(8,128)(2,1)S(1)} %all_to_all.36.got_ref), channel_id=1, source_target_pairs={{0,256},{8,264},{16,272},{24,280},{32,288},{40,296},{48,304},{56,3... | collective-permute-start | bytes 786440 | tf_op jit(solution)/shard_map/ppermute | solution.py:347
  120.4 23.2 %all-to-all-start.3 = ((bf16[8,32,128]{2,1,0:T(8,128)(2,1)}), bf16[8,32,128]{2,1,0:T(8,128)(2,1)S(1)}, u32[]{:S(2)}, u32[]{:S(2)}) async-start(bf16[8,32,128]{2,1,0:T(8,128)(2,1)} %shard_map.123), calls=%async_computation.3 | async-start | bytes 131072 | tf_op jit(solution)/shard_map/all_to_all | solution.py:350
  132.7 1.0 copy-start.3
  135.6 15.0 %copy-start.17 = (bf16[2,2,128,128]{3,2,1,0:T(8,128)(2,1)S(1)}, bf16[2,2,128,128]{3,2,1,0:T(8,128)(2,1)}, u32[]{:S(2)}) copy-start(bf16[2,2,128,128]{3,2,1,0:T(8,128)(2,1)} %copy-done.16) | copy-start | bytes 393220
  144.4 33.5 %copy-start.21 = (s32[256]{0:T(256)S(1)}, s32[256]{0:T(256)}, u32[]{:S(2)}) copy-start(s32[256]{0:T(256)} %param.18) | copy-start | bytes 3076
  144.4 14.3 %all-to-all-start.4 = ((bf16[32,48,128]{2,1,0:T(8,128)(2,1)}), bf16[32,48,128]{2,1,0:T(8,128)(2,1)S(1)}, u32[]{:S(2)}, u32[]{:S(2)}) async-start(bf16[32,48,128]{2,1,0:T(8,128)(2,1)} %shard_map.124), calls=%async_computation.4 | async-start | bytes 786432 | tf_op jit(solution)/shard_map/all_to_all | solution.py:356
  150.6 34.9 %copy-start.20 = (s32[256]{0:T(256)S(1)}, s32[256]{0:T(256)}, u32[]{:S(2)}) copy-start(s32[256]{0:T(256)} %param.19) | copy-start | bytes 3076
  150.6 3.3 %collective-permute-start.11 = (bf16[2,128,128]{2,1,0:T(8,128)(2,1)S(1)}, bf16[2,128,128]{2,1,0:T(8,128)(2,1)S(1)}, u32[]{:S(2)}, u32[]{:S(2)}) collective-permute-start(bf16[2,128,128]{2,1,0:T(8,128)(2,1)S(1)} %get-tuple-element.35), channel_id=1, source_target_pairs={{0,8},{8,0},{16,24},{24,16},{32,40},{40,32},{48,56},{56,48},{64,72... | collective-permute-start | bytes 196616 | tf_op jit(solution)/shard_map/ppermute | solution.py:352
  171.7 13.4 %collective-permute-start.12 = (bf16[64,512]{1,0:T(8,128)(2,1)S(1)}, bf16[64,512]{1,0:T(8,128)(2,1)S(1)}, u32[]{:S(2)}, u32[]{:S(2)}) collective-permute-start(bf16[64,512]{1,0:T(8,128)(2,1)S(1)} %reduce_sum.30), channel_id=1, source_target_pairs={{0,4},{1,5},{2,6},{3,7},{4,0},{5,1},{6,2},{7,3},{8,12},{9,13},{10,... | collective-permute-start | bytes 196616 | tf_op jit(solution)/shard_map/ppermute | solution.py:370
  (7 other events, 5.6 us)

commit v14 on v12

--- a/solution.py
+++ b/solution.py
@@ -65,6 +65,7 @@
 
 
 SCALARS = pl.BlockSpec(memory_space=pltpu.SMEM)
+ANYWHERE = pl.BlockSpec(memory_space=pl.ANY)
 
 
 def spectrum(scratch, matrices, twiddles):
@@ -133,7 +134,15 @@
         out_ref[d, 16:] = piece
 
 
-def first_kernel(core_ref, own_ref, got_ref, rows_ref, out_ref):
+def first_kernel(core_ref, own_hbm, got_ref, rows_hbm, out_ref, own_ref, rows_ref, sems):
+    copies = [
+        pltpu.make_async_copy(own_hbm, own_ref, sems.at[0]),
+        pltpu.make_async_copy(rows_hbm, rows_ref, sems.at[1]),
+    ]
+    for copy in copies:
+        copy.start()
+    for copy in copies:
+        copy.wait()
     core = core_ref[0]
     half = pl.ds(pl.multiple_of(core * 128, 128), 128)
     for g in range(3):
@@ -154,47 +163,69 @@
     return jnp.concatenate([ref[lead, row + 128 * g : row + 128 * g + 128, :] for g in range(3)], axis=1)
 
 
-def near_kernel(
-    at_ref, own_hbm, beside_hbm, gain_ref, near_ref, gained_ref, scale_ref, out_ref, tokens, sems
-):
-    start = at_ref[3] * 2048
+def norm_kernel(own_hbm, beside_hbm, gain_ref, gained_hbm, scale_ref, tokens, gained, sems):
     gain = gain_ref[...]
-    copies = []
+    copies, stores = [], []
     for part, ref in enumerate((own_hbm, beside_hbm)):
         for i in range(4):
-            rows = slice(i * 64, i * 64 + 64)
-            copies.append(pltpu.make_async_copy(ref.at[rows], tokens.at[part, rows], sems.at[part, i]))
+            rows = pl.ds(i * 64, 64)
+            copies.append(pltpu.make_async_copy(ref.at[rows], tokens.at[part, rows], sems.at[0, part, i]))
+            stores.append(
+                pltpu.make_async_copy(gained.at[part, rows], gained_hbm.at[part, rows], sems.at[1, part, i])
+            )
     for copy in copies:
         copy.start()
-    for part in range(2):
-        for i in range(4):
-            copies[part * 4 + i].wait()
-            for half in range(2):
-                rows = slice(i * 64 + half * 32, i * 64 + half * 32 + 32)
-                block = tokens[part, rows, :]
-                stream = block.astype(F32)
-                mean = jnp.mean(stream * stream, axis=1, keepdims=True)
-                scale_ref[part, rows, :] = jnp.broadcast_to(lax.rsqrt(mean + NORM_EPS), (32, 128))
-                gained_ref[part, rows, :] = block * gain
-        total = jnp.zeros((256, 384), F32)
+    for k in range(8):
+        copies[k].wait()
+        part, i = k // 4, k % 4
+        for half in range(2):
+            rows = slice(i * 64 + half * 32, i * 64 + half * 32 + 32)
+            block = tokens[part, rows, :]
+            stream = block.astype(F32)
+            mean = jnp.mean(stream * stream, axis=1, keepdims=True)
+            scale_ref[part, rows, :] = jnp.broadcast_to(lax.rsqrt(mean + NORM_EPS), (32, 128))
+            gained[part, rows, :] = block * gain
+        stores[k].start()
+    for store in stores:
+        store.wait()
+
+
+def near_kernel(
+    at_ref, gained_hbm, own_taps, got_taps, near_ref, unembed_ref, out_ref, terms_ref, pieces_ref, gained, taps, sems
+):
+    core, z = at_ref[2], at_ref[3]
+    columns = pl.ds(pl.multiple_of(z * 2048, 2048), 2048)
+    copies = [
+        pltpu.make_async_copy(gained_hbm.at[part, :, columns], gained.at[part], sems.at[part]) for part in range(2)
+    ]
+    copies.append(pltpu.make_async_copy(own_taps, taps.at[0], sems.at[2]))
+    copies.append(pltpu.make_async_copy(got_taps, taps.at[1], sems.at[3]))
+    for copy in copies:
+        copy.start()
+
+    blocks = []
+    for plane in range(2):
         for y in range(4):
-            for x in (0, 2):
-                left = gained_ref[part, :, pl.ds(pl.multiple_of(start + (y * 4 + x) * 128, 128), 256)]
-                right = [weight_block(near_ref, y, x * 384), weight_block(near_ref, y, x * 384 + 384)]
-                total += mm(left, jnp.concatenate(right, axis=0))
-        out_ref[part] = total
-
-
-def product_kernel(rows_ref, unembed_ref, out_ref):
-    blocks = []
-    for z in range(2):
-        for y in range(4):
-            block = rows_ref[y, 1536 + z * 32 : 1568 + z * 32, :].astype(F32)
+            block = near_ref[y, 1536 + plane * 32 : 1568 + plane * 32, :].astype(F32)
             blocks.append(jnp.concatenate([block[v * 8 : v * 8 + 8] for v in range(4)], axis=1))
     terms = mm(jnp.concatenate(blocks, axis=0).astype(BF16), unembed_ref[...])
     for j in range(8):
         parts = [terms[j * 8 : j * 8 + 8, v * 128 : v * 128 + 128] for v in range(4)]
-        out_ref[j] = jnp.concatenate(parts, axis=0).astype(BF16)
+        terms_ref[j] = jnp.concatenate(parts, axis=0).astype(BF16)
+
+    for part in range(2):
+        copies[part].wait()
+        total = jnp.zeros((256, 384), F32)
+        for y in range(4):
+            for x in (0, 2):
+                left = gained[part, :, (y * 4 + x) * 128 : (y * 4 + x) * 128 + 256]
+                right = [weight_block(near_ref, y, x * 384), weight_block(near_ref, y, x * 384 + 384)]
+                total += mm(left, jnp.concatenate(right, axis=0))
+        out_ref[part] = total
+    half = pl.ds(pl.multiple_of(core * 128, 128), 128)
+    for part in range(2):
+        copies[2 + part].wait()
+        put_pieces(pieces_ref, 0, core if part == 0 else 1 - core, taps[part, :, half].astype(F32))
 
 
 def put_pieces(ref, row, place, block):
@@ -205,26 +236,37 @@
         ref[p, pl.ds(pl.multiple_of(row + place * 16, 16), 16), :] = rows
 
 
-def proj_kernel(at_ref, gained_ref, scale_ref, near_ref, own_taps, got_taps, f0, f1, f2, f3, sig_ref, gate_ref):
+def proj_kernel(
+    at_ref, gained_hbm, scale_ref, near_ref, pieces_ref, f0, f1, f2, f3, sig_ref, gate_ref, gained, fars, sems
+):
     y_at, x_at, core = at_ref[0], at_ref[1], at_ref[2]
-    start = 2048 - at_ref[3] * 2048
-    half = pl.ds(pl.multiple_of(core * 128, 128), 128)
+    columns = pl.ds(pl.multiple_of(2048 - at_ref[3] * 2048, 2048), 2048)
+    copies = [
+        pltpu.make_async_copy(gained_hbm.at[part, :, columns], gained.at[part], sems.at[part]) for part in range(2)
+    ]
+    copies += [pltpu.make_async_copy(f, fars.at[k], sems.at[2 + k]) for k, f in enumerate((f0, f1, f2, f3))]
+    for k in (0, 2, 3, 4, 5, 1):
+        copies[k].start()
     for part in range(2):
+        copies[part].wait()
         total = near_ref[part]
-        for step, ref in enumerate((f0, f1, f2, f3)):
+        for step in range(4):
+            if part == 0:
+                copies[2 + step].wait()
             x = lax.rem(x_at + 4 - step, 4)
             for k in (0, 2):
-                starts = [start + (lax.rem(y_at + 4 - j, 4) * 4 + x) * 128 for j in (k, k + 1)]
-                left = [gained_ref[part, :, pl.ds(pl.multiple_of(at, 128), 128)] for at in starts]
-                right = [weight_block(ref, k, 0), weight_block(ref, k + 1, 0)]
+                starts = [(lax.rem(y_at + 4 - j, 4) * 4 + x) * 128 for j in (k, k + 1)]
+                left = [gained[part, :, pl.ds(pl.multiple_of(at, 128), 128)] for at in starts]
+                right = [weight_block(fars.at[step], k, 0), weight_block(fars.at[step], k + 1, 0)]
                 total += mm(jnp.concatenate(left, axis=1), jnp.concatenate(right, axis=0))
         scale = scale_ref[part]
         proj = (total * jnp.concatenate([scale, scale, scale], axis=1)).astype(BF16).astype(F32)
         place = core if part == 0 else 1 - core
         put_pieces(sig_ref, 0, place, proj[:, 128:256] * proj[:, 256:])
-        put_pieces(sig_ref, 32, place, (own_taps if part == 0 else got_taps)[:, half].astype(F32))
         gate_ref[place, 0] = proj[:128, :128].T.astype(BF16)
         gate_ref[place, 1] = proj[128:, :128].T.astype(BF16)
+    for p in range(16):
+        sig_ref[p, 32:, :] = pieces_ref[p]
 
 
 def mix_kernel(core_ref, got_ref, keep_ref, other_ref, base_ref, out_ref):
@@ -246,12 +288,14 @@
         out_ref[rb * 128 : rb * 128 + 128, :] = total.astype(BF16)
 
 
-def call(kernel, outs, specs, scratch, flops, args, mib=8):
+def call(kernel, outs, specs, scratch, flops, args, mib=8, out_specs=None):
+    if out_specs is None:
+        out_specs = jax.tree.map(lambda _: pl.BlockSpec(memory_space=pltpu.VMEM), outs)
     return pl.pallas_call(
         kernel,
         out_shape=outs,
         in_specs=specs,
-        out_specs=jax.tree.map(lambda _: pl.BlockSpec(memory_space=pltpu.VMEM), outs),
+        out_specs=out_specs,
         scratch_shapes=scratch,
         compiler_params=pltpu.CompilerParams(vmem_limit_bytes=mib * 2**20),
         cost_estimate=pl.CostEstimate(flops=flops, bytes_accessed=4 * 2**20, transcendentals=0),
@@ -299,8 +343,8 @@
     first = call(
         first_kernel,
         shape((512, 128), BF16),
-        [SCALARS] + whole(3),
-        [],
+        [SCALARS, ANYWHERE] + whole(1) + [ANYWHERE],
+        [pltpu.VMEM((3, 64, 256), BF16), pltpu.VMEM((32, 512), BF16), pltpu.SemaphoreType.DMA((2,))],
         10**5,
         (core_at, w_in, lax.ppermute(w_in, "ctx", PERM_CORE), w_out),
     )
@@ -322,25 +366,38 @@
     taps_got = lax.ppermute(taps, "ctx", PERM_CORE)
 
     at = jnp.stack([(ctx // 8) % 4, (ctx // 2) % 4, core, z]).astype(jnp.int32)
-    gained, scale, sums = call(
+    gained, scale = call(
+        norm_kernel,
+        (shape((2, 256, 4096), BF16), shape((2, 256, 128), F32)),
+        [ANYWHERE, ANYWHERE] + whole(1),
+        [
+            pltpu.VMEM((2, 256, 4096), BF16),
+            pltpu.VMEM((2, 256, 4096), BF16),
+            pltpu.SemaphoreType.DMA((2, 2, 4)),
+        ],
+        10**7,
+        (tokens_in, beside, pre_gain.reshape(1, 4096)),
+        mib=16,
+        out_specs=(ANYWHERE, whole(1)[0]),
+    )
+    sums, terms, pieces = call(
         near_kernel,
-        (shape((2, 256, 4096), BF16), shape((2, 256, 128), F32), shape((2, 256, 384), F32)),
-        [SCALARS] + [pl.BlockSpec(memory_space=pl.ANY)] * 2 + whole(2),
-        [pltpu.VMEM((2, 256, 4096), BF16), pltpu.SemaphoreType.DMA((2, 4))],
+        (shape((2, 256, 384), F32), shape((8, 32, 128), BF16), shape((16, 32, 128), BF16)),
+        [SCALARS] + [ANYWHERE] * 3 + whole(2),
+        [pltpu.VMEM((2, 256, 2048), BF16), pltpu.VMEM((2, 256, 256), BF16), pltpu.SemaphoreType.DMA((4,))],
         8 * 10**8,
-        (at, tokens_in, beside, pre_gain.reshape(1, 4096), near),
+        (at, gained, taps, taps_got, near, w_unembed),
     )
     signal, gate = call(
         proj_kernel,
         (shape((16, 64, 128), BF16), shape((2, 2, 128, 128), BF16)),
-        [SCALARS] + whole(9),
-        [],
+        [SCALARS, ANYWHERE] + whole(3) + [ANYWHERE] * 4,
+        [pltpu.VMEM((2, 256, 2048), BF16), pltpu.VMEM((4, 4, 384, 128), BF16), pltpu.SemaphoreType.DMA((6,))],
         8 * 10**8,
-        (at, gained, scale, sums, taps, taps_got, *fars),
+        (at, gained, scale, sums, pieces, *fars),
     )
     got = lax.all_to_all(signal, "ctx", 0, 0, axis_index_groups=GROUPS_CORE, tiled=True)
     before = lax.ppermute(got, "ctx", PERM_Z_UP)
-    terms = call(product_kernel, shape((8, 32, 128), BF16), whole(2), [], 4 * 10**7, (near, w_unembed))
     terms, _ = lax.optimization_barrier((terms, got))
     terms = lax.all_to_all(terms, "tp", 0, 0, tiled=True)
     gate_keep = lax.dynamic_index_in_dim(gate, core, 0, False)

time: 179 us -> 179 us (level)
  waiting for transfers between devices: 41.3 us -> 34.6 us
  Pallas kernels: 11.6 us -> 14.5 us
  starting transfers between devices: 81.4 us -> 84 us
    all_to_all x1, waiting for transfers between devices: 9.9 us -> 3.87 us  [per_device(): lax.all_to_all(near, 'ctx', 0, 0, axis_index_groups=GROUPS_Y, tiled=True)]
    pallas_call x9, Pallas kernels: 11.6 us -> 14.5 us  [call(): pl.pallas_call(kernel, out_shape=outs, in_specs=specs, out_specs=out_spec...]
    ppermute x1, waiting for transfers between devices: 10.6 us -> 8.32 us  [per_device(): far = lax.ppermute(logits, 'tp', [(i, i ^ 4) for i in range(8)])]
    ppermute x1, starting transfers between devices: 2.66 us -> 4.94 us  [per_device(): far = lax.ppermute(logits, 'tp', [(i, i ^ 4) for i in range(8)])]
    unnamed x30 -> x26, local copies, waits for them, and re-layouts: 4.98 us -> 6.53 us
where the time goes in v14:
time: 179 us; the launch traced here: 177 us
  starting transfers between devices  84 us (47%)
  waiting for transfers between devices  34.6 us (19%)
  blocking collectives  32 us (18%)
  Pallas kernels  14.5 us (8%)
  local copies, waits for them, and re-layouts  8.02 us (4%)
  other arithmetic  2.55 us (1%)
    ppermute x1, starting transfers between devices, per_device(): far = lax.ppermute(first, 'ctx', PERM_Z)  15.7 us
    pallas_call x9, Pallas kernels, call(): pl.pallas_call(kernel, out_shape=outs, in_specs=specs, out_specs=out_spec...  14.5 us
    all_to_all x1, starting transfers between devices, per_device(): terms = lax.all_to_all(terms, 'tp', 0, 0, tiled=True)  13.1 us
    all_to_all x1, blocking collectives, per_device(): lax.all_to_all(logits.reshape(4, 64, 512), 'tp', 0, 0, axis_index_groups=...  12.7 us
    all_to_all x1, blocking collectives, per_device(): lax.all_to_all(signal, 'ctx', 0, 0, axis_index_groups=GROUPS_CORE, tiled=...  11.5 us
    all_to_all x1, waiting for transfers between devices, per_device(): terms = lax.all_to_all(terms, 'tp', 0, 0, tiled=True)  11.4 us
    ppermute x3, starting transfers between devices, per_device(): lax.ppermute(far, 'ctx', PERM_Y[k])  10.3 us
    ppermute x1, starting transfers between devices, per_device(): before = lax.ppermute(got, 'ctx', PERM_Z_UP)  8.81 us
  transfers between devices with their start and end apart: 17, of which 7 were waited for; matrix products, arithmetic and copies ran while one was open for 2% of the time, Pallas kernels for 5%

profile of v14, /device:TPU:6, one launch (start us, length us, event | category | flops | bytes accessed | tf_op | source)
XLA Modules:
  0.0 177.5 jit_solution(17193673096766739161)
XLA Ops:
  0.0 1.9 %collective-permute-start = (bf16[3,64,256]{2,1,0:T(8,128)(2,1)}, bf16[3,64,256]{2,1,0:T(8,128)(2,1)S(1)}, u32[]{:S(2)}, u32[]{:S(2)}) collective-permute-start(bf16[3,64,256]{2,1,0:T(8,128)(2,1)} %bitcast.24), channel_id=1, source_target_pairs={{0,8},{8,0},{16,24},{24,16},{32,40},{40,32},{48,56},{56,48},{64,72... | collective-permute-start | bytes 294920 | tf_op jit(solution)/shard_map/ppermute | solution.py:349
  5.2 15.7 %collective-permute-start.2 = (bf16[512,128]{1,0:T(8,128)(2,1)S(1)}, bf16[512,128]{1,0:T(8,128)(2,1)S(1)}, u32[]{:S(2)}, u32[]{:S(2)}) collective-permute-start(bf16[512,128]{1,0:T(8,128)(2,1)S(1)} %shard_map.118.first_ref), channel_id=1, source_target_pairs={{0,256},{8,264},{16,272},{24,280},{32,288},{40,296},{48,304},{56,3... | collective-permute-start | bytes 393224 | tf_op jit(solution)/shard_map/ppermute | solution.py:355
  21.8 1.9 %collective-permute-start.1 = (bf16[256,4096]{1,0:T(8,128)(2,1)}, bf16[256,4096]{1,0:T(8,128)(2,1)}, u32[]{:S(2)}, u32[]{:S(2)}) collective-permute-start(bf16[256,4096]{1,0:T(8,128)(2,1)} %own_hbm.1), channel_id=1, source_target_pairs={{0,8},{8,0},{16,24},{24,16},{32,40},{40,32},{48,56},{56,48},{64,72... | collective-permute-start | bytes 6291464 | tf_op jit(solution)/shard_map/ppermute | solution.py:353
  23.7 4.8 %all-to-all-start = ((bf16[4,384,128]{2,1,0:T(8,128)(2,1)}), bf16[4,384,128]{2,1,0:T(8,128)(2,1)S(1)}, u32[]{:S(2)}, u32[]{:S(2)}) async-start(bf16[4,384,128]{2,1,0:T(8,128)(2,1)} %shard_map.119), calls=%async_computation | async-start | bytes 786432 | tf_op jit(solution)/shard_map/all_to_all | solution.py:354
  28.5 4.9 %collective-permute-start.5 = (bf16[384,128]{1,0:T(8,128)(2,1)S(1)}, bf16[384,128]{1,0:T(8,128)(2,1)S(1)}, u32[]{:S(2)}, u32[]{:S(2)}) collective-permute-start(bf16[384,128]{1,0:T(8,128)(2,1)S(1)} %get-tuple-element.42), channel_id=1, source_target_pairs={{0,192},{8,200},{16,208},{24,216},{32,224},{40,232},{48,240},{56,2... | collective-permute-start | bytes 294920 | tf_op jit(solution)/shard_map/ppermute | solution.py:359
  33.4 2.5 %collective-permute-start.4 = (bf16[384,128]{1,0:T(8,128)(2,1)S(1)}, bf16[384,128]{1,0:T(8,128)(2,1)S(1)}, u32[]{:S(2)}, u32[]{:S(2)}) collective-permute-start(bf16[384,128]{1,0:T(8,128)(2,1)S(1)} %get-tuple-element.42), channel_id=1, source_target_pairs={{0,128},{8,136},{16,144},{24,152},{32,160},{40,168},{48,176},{56,1... | collective-permute-start | bytes 294920 | tf_op jit(solution)/shard_map/ppermute | solution.py:359
  36.0 2.9 %collective-permute-start.3 = (bf16[384,128]{1,0:T(8,128)(2,1)S(1)}, bf16[384,128]{1,0:T(8,128)(2,1)S(1)}, u32[]{:S(2)}, u32[]{:S(2)}) collective-permute-start(bf16[384,128]{1,0:T(8,128)(2,1)S(1)} %get-tuple-element.42), channel_id=1, source_target_pairs={{0,64},{8,72},{16,80},{24,88},{32,96},{40,104},{48,112},{56,120},{... | collective-permute-start | bytes 294920 | tf_op jit(solution)/shard_map/ppermute | solution.py:359
  38.9 3.0 %collective-permute-done.4 = bf16[384,128]{1,0:T(8,128)(2,1)S(1)} collective-permute-done((bf16[384,128]{1,0:T(8,128)(2,1)S(1)}, bf16[384,128]{1,0:T(8,128)(2,1)S(1)}, u32[]{:S(2)}, u32[]{:S(2)}) %collective-permute-start.4) | collective-permute-done | bytes 98336 | tf_op jit(solution)/shard_map/ppermute | solution.py:359
  41.9 1.8 collective-permute-done.3
  45.3 3.7 %all-to-all-start.1 = ((bf16[4,1600,128]{2,1,0:T(8,128)(2,1)}), bf16[4,1600,128]{2,1,0:T(8,128)(2,1)S(1)}, u32[]{:S(2)}, u32[]{:S(2)}) async-start(bf16[4,1600,128]{2,1,0:T(8,128)(2,1)} %pad_maximum_fusion), calls=%async_computation.1 | async-start | bytes 3276800 | tf_op jit(solution)/shard_map/all_to_all | solution.py:364
  49.0 1.9 %collective-permute-start.7 = (bf16[4,384,128]{2,1,0:T(8,128)(2,1)S(1)}, bf16[4,384,128]{2,1,0:T(8,128)(2,1)S(1)}, u32[]{:S(2)}, u32[]{:S(2)}) collective-permute-start(bf16[4,384,128]{2,1,0:T(8,128)(2,1)S(1)} %pad_maximum_fusion.1.f0), channel_id=1, source_target_pairs={{0,16},{8,24},{16,32},{24,40},{32,48},{40,56},{48,0},{56,8},{64,80... | collective-permute-start | bytes 1179656 | tf_op jit(solution)/shard_map/ppermute | solution.py:365
  50.9 4.8 %collective-permute-start.8 = (bf16[4,384,128]{2,1,0:T(8,128)(2,1)S(1)}, bf16[4,384,128]{2,1,0:T(8,128)(2,1)S(1)}, u32[]{:S(2)}, u32[]{:S(2)}) collective-permute-start(bf16[4,384,128]{2,1,0:T(8,128)(2,1)S(1)} %pad_maximum_fusion.1.f0), channel_id=1, source_target_pairs={{0,32},{8,40},{16,48},{24,56},{32,0},{40,8},{48,16},{56,24},{64,96... | collective-permute-start | bytes 1179656 | tf_op jit(solution)/shard_map/ppermute | solution.py:365
  55.7 1.9 %collective-permute-start.9 = (bf16[4,384,128]{2,1,0:T(8,128)(2,1)S(1)}, bf16[4,384,128]{2,1,0:T(8,128)(2,1)}, u32[]{:S(2)}, u32[]{:S(2)}) collective-permute-start(bf16[4,384,128]{2,1,0:T(8,128)(2,1)S(1)} %pad_maximum_fusion.1.f0), channel_id=1, source_target_pairs={{0,48},{8,56},{16,0},{24,8},{32,16},{40,24},{48,32},{56,40},{64,11... | collective-permute-start | bytes 1179656 | tf_op jit(solution)/shard_map/ppermute | solution.py:365
  57.7 1.9 %collective-permute-start.6 = (bf16[256,256]{1,0:T(8,128)(2,1)S(1)}, bf16[256,256]{1,0:T(8,128)(2,1)}, u32[]{:S(2)}, u32[]{:S(2)}) collective-permute-start(bf16[256,256]{1,0:T(8,128)(2,1)S(1)} %copy-done.7), channel_id=1, source_target_pairs={{0,8},{8,0},{16,24},{24,16},{32,40},{40,32},{48,56},{56,48},{64,72... | collective-permute-start | bytes 393224 | tf_op jit(solution)/shard_map/ppermute | solution.py:366
  59.8 3.1 %shard_map.120 = (bf16[2,256,4096]{2,1,0:T(8,128)(2,1)S(1)}, f32[2,256,128]{2,1,0:T(8,128)S(1)}) custom-call(bf16[256,4096]{1,0:T(8,128)(2,1)} %own_hbm.1, bf16[256,4096]{1,0:T(8,128)(2,1)} %collective-permute-done.1.beside_hbm, bf16[1,4096]{1,0:T(2,128)(2,1)S(1)} %reshape.28.gain_ref), custom_call_target="tpu_custom_call" | custom-call | flops 10000000 | bytes 4194304 | tf_op jit(solution)/shard_map/pallas_call | solution.py:294
  62.9 1.9 %copy-done = bf16[2,256,4096]{2,1,0:T(8,128)(2,1)} copy-done((bf16[2,256,4096]{2,1,0:T(8,128)(2,1)}, bf16[2,256,4096]{2,1,0:T(8,128)(2,1)S(1)}, u32[]{:S(2)}) %copy-start) | copy-done | bytes 4194328
  65.6 3.9 %all-to-all-done.1.near_ref = bf16[4,1600,128]{2,1,0:T(8,128)(2,1)S(1)} async-done(((bf16[4,1600,128]{2,1,0:T(8,128)(2,1)}), bf16[4,1600,128]{2,1,0:T(8,128)(2,1)S(1)}, u32[]{:S(2)}, u32[]{:S(2)}) %all-to-all-start.1) | async-done | bytes 1638432 | tf_op jit(solution)/shard_map/all_to_all | solution.py:364
  69.5 2.2 %copy-done.1 = bf16[2,256,4096]{2,1,0:T(8,128)(2,1)S(1)} copy-done((bf16[2,256,4096]{2,1,0:T(8,128)(2,1)S(1)}, bf16[2,256,4096]{2,1,0:T(8,128)(2,1)}, u32[]{:S(2)}) %copy-start.1) | copy-done | bytes 4194328
  71.7 3.3 %shard_map.121 = (f32[2,256,384]{2,1,0:T(8,128)S(1)}, bf16[8,32,128]{2,1,0:T(8,128)(2,1)}, bf16[16,32,128]{2,1,0:T(8,128)(2,1)S(1)}) custom-call(s32[4]{0:T(128)S(1)} %pad_add_fusion.at_ref, bf16[2,256,4096]{2,1,0:T(8,128)(2,1)S(1)} %copy-done.1, bf16[256,256]{1,0:T(8,128)(2,1)S(1)} %copy-done.7, bf16[256,256]{1,0:T(8,128)(2,1)} %collective-permute-done.6.got_taps, ...), custom_call_target="tpu_custom_call" | custom-call | flops 800000000 | bytes 4194304 | tf_op jit(solution)/shard_map/pallas_call | solution.py:294
  75.0 3.4 %shard_map.122 = (bf16[16,64,128]{2,1,0:T(8,128)(2,1)S(1)}, bf16[2,2,128,128]{3,2,1,0:T(8,128)(2,1)S(1)}) custom-call(s32[4]{0:T(128)S(1)} %pad_add_fusion.at_ref, bf16[2,256,4096]{2,1,0:T(8,128)(2,1)S(1)} %copy-done.1, f32[2,256,128]{2,1,0:T(8,128)S(1)} %copy-done.5, f32[2,256,384]{2,1,0:T(8,128)S(1)} %get-tuple-element.28.near_ref, ...), custom_call_target="tpu_custom_call" | custom-call | flops 800000000 | bytes 4194304 | tf_op jit(solution)/shard_map/pallas_call | solution.py:294
  78.5 11.5 %all_to_all.36.got_ref = bf16[16,64,128]{2,1,0:T(8,128)(2,1)S(1)} all-to-all(bf16[16,64,128]{2,1,0:T(8,128)(2,1)S(1)} %get-tuple-element.31), channel_id=1, replica_groups={{0,16,32,48,64,80,96,112,128,144,160,176,192,208,224,240},{8,24,40,56,7..., dimensions={0} | all-to-all | bytes 524288 | tf_op jit(solution)/shard_map/all_to_all | solution.py:399
  90.0 8.8 %collective-permute-start.10 = (bf16[16,64,128]{2,1,0:T(8,128)(2,1)S(1)}, bf16[16,64,128]{2,1,0:T(8,128)(2,1)S(1)}, u32[]{:S(2)}, u32[]{:S(2)}) collective-permute-start(bf16[16,64,128]{2,1,0:T(8,128)(2,1)S(1)} %all_to_all.36.got_ref), channel_id=1, source_target_pairs={{0,256},{8,264},{16,272},{24,280},{32,288},{40,296},{48,304},{56,3... | collective-permute-start | bytes 786440 | tf_op jit(solution)/shard_map/ppermute | solution.py:400
  98.8 13.1 %all-to-all-start.3 = ((bf16[8,32,128]{2,1,0:T(8,128)(2,1)}), bf16[8,32,128]{2,1,0:T(8,128)(2,1)S(1)}, u32[]{:S(2)}, u32[]{:S(2)}) async-start(bf16[8,32,128]{2,1,0:T(8,128)(2,1)} %get-tuple-element.35), calls=%async_computation.3 | async-start | bytes 131072 | tf_op jit(solution)/shard_map/all_to_all | solution.py:402
  112.9 1.5 shard_map.124.conv_ref
  114.5 11.4 %all-to-all-done.3.terms_ref = bf16[8,32,128]{2,1,0:T(8,128)(2,1)S(1)} async-done(((bf16[8,32,128]{2,1,0:T(8,128)(2,1)}), bf16[8,32,128]{2,1,0:T(8,128)(2,1)S(1)}, u32[]{:S(2)}, u32[]{:S(2)}) %all-to-all-start.3) | async-done | bytes 65568 | tf_op jit(solution)/shard_map/all_to_all | solution.py:402
  126.6 6.2 %all-to-all-start.4 = ((bf16[32,48,128]{2,1,0:T(8,128)(2,1)}), bf16[32,48,128]{2,1,0:T(8,128)(2,1)S(1)}, u32[]{:S(2)}, u32[]{:S(2)}) async-start(bf16[32,48,128]{2,1,0:T(8,128)(2,1)} %shard_map.125), calls=%async_computation.4 | async-start | bytes 786432 | tf_op jit(solution)/shard_map/all_to_all | solution.py:408
  132.9 2.1 %collective-permute-start.11 = (bf16[2,128,128]{2,1,0:T(8,128)(2,1)S(1)}, bf16[2,128,128]{2,1,0:T(8,128)(2,1)S(1)}, u32[]{:S(2)}, u32[]{:S(2)}) collective-permute-start(bf16[2,128,128]{2,1,0:T(8,128)(2,1)S(1)} %get-tuple-element.39), channel_id=1, source_target_pairs={{0,8},{8,0},{16,24},{24,16},{32,40},{40,32},{48,56},{56,48},{64,72... | collective-permute-start | bytes 196616 | tf_op jit(solution)/shard_map/ppermute | solution.py:404
  136.2 4.7 %all-to-all-done.4.got_ref = bf16[32,48,128]{2,1,0:T(8,128)(2,1)S(1)} async-done(((bf16[32,48,128]{2,1,0:T(8,128)(2,1)}), bf16[32,48,128]{2,1,0:T(8,128)(2,1)S(1)}, u32[]{:S(2)}, u32[]{:S(2)}) %all-to-all-start.4) | async-done | bytes 393248 | tf_op jit(solution)/shard_map/all_to_all | solution.py:408
  141.3 12.7 %all_to_all.37 = bf16[4,64,512]{2,1,0:T(8,128)(2,1)S(1)} all-to-all(bf16[4,64,512]{2,1,0:T(8,128)(2,1)S(1)} %bitcast.23), channel_id=1, replica_groups={{0,1,2,3},{4,5,6,7},{8,9,10,11},{12,13,14,15},{16,17,18,19},{20,21,22,2..., dimensions={0} | all-to-all | bytes 524288 | tf_op jit(solution)/shard_map/all_to_all | solution.py:420
  154.0 4.9 %collective-permute-start.12 = (bf16[64,512]{1,0:T(8,128)(2,1)S(1)}, bf16[64,512]{1,0:T(8,128)(2,1)S(1)}, u32[]{:S(2)}, u32[]{:S(2)}) collective-permute-start(bf16[64,512]{1,0:T(8,128)(2,1)S(1)} %reduce_sum.30), channel_id=1, source_target_pairs={{0,4},{1,5},{2,6},{3,7},{4,0},{5,1},{6,2},{7,3},{8,12},{9,13},{10,... | collective-permute-start | bytes 196616 | tf_op jit(solution)/shard_map/ppermute | solution.py:422
  159.0 8.3 %collective-permute-done.12 = bf16[64,512]{1,0:T(8,128)(2,1)S(1)} collective-permute-done((bf16[64,512]{1,0:T(8,128)(2,1)S(1)}, bf16[64,512]{1,0:T(8,128)(2,1)S(1)}, u32[]{:S(2)}, u32[]{:S(2)}) %collective-permute-start.12) | collective-permute-done | bytes 65568 | tf_op jit(solution)/shard_map/ppermute | solution.py:422
  167.8 7.9 %all_to_all.38 = f32[4,1,64]{2,1,0:T(1,128)S(1)} all-to-all(f32[4,1,64]{2,1,0:T(1,128)S(1)} %broadcast_in_dim.22), channel_id=1, replica_groups={{0,1,2,3},{4,5,6,7},{8,9,10,11},{12,13,14,15},{16,17,18,19},{20,21,22,2..., dimensions={0} | all-to-all | bytes 2048 | tf_op jit(solution)/shard_map/all_to_all | solution.py:433
  (61 shorter events, 12.2 us)
Async XLA Ops:
  0.0 3.4 %collective-permute-start = (bf16[3,64,256]{2,1,0:T(8,128)(2,1)}, bf16[3,64,256]{2,1,0:T(8,128)(2,1)S(1)}, u32[]{:S(2)}, u32[]{:S(2)}) collective-permute-start(bf16[3,64,256]{2,1,0:T(8,128)(2,1)} %bitcast.24), channel_id=1, source_target_pairs={{0,8},{8,0},{16,24},{24,16},{32,40},{40,32},{48,56},{56,48},{64,72... | collective-permute-start | bytes 294920 | tf_op jit(solution)/shard_map/ppermute | solution.py:349
  3.4 0.9 copy-start.8
  4.3 0.8 copy-start.9
  5.2 23.2 %collective-permute-start.2 = (bf16[512,128]{1,0:T(8,128)(2,1)S(1)}, bf16[512,128]{1,0:T(8,128)(2,1)S(1)}, u32[]{:S(2)}, u32[]{:S(2)}) collective-permute-start(bf16[512,128]{1,0:T(8,128)(2,1)S(1)} %shard_map.118.first_ref), channel_id=1, source_target_pairs={{0,256},{8,264},{16,272},{24,280},{32,288},{40,296},{48,304},{56,3... | collective-permute-start | bytes 393224 | tf_op jit(solution)/shard_map/ppermute | solution.py:355
  21.8 38.0 %collective-permute-start.1 = (bf16[256,4096]{1,0:T(8,128)(2,1)}, bf16[256,4096]{1,0:T(8,128)(2,1)}, u32[]{:S(2)}, u32[]{:S(2)}) collective-permute-start(bf16[256,4096]{1,0:T(8,128)(2,1)} %own_hbm.1), channel_id=1, source_target_pairs={{0,8},{8,0},{16,24},{24,16},{32,40},{40,32},{48,56},{56,48},{64,72... | collective-permute-start | bytes 6291464 | tf_op jit(solution)/shard_map/ppermute | solution.py:353
  23.7 20.1 %all-to-all-start = ((bf16[4,384,128]{2,1,0:T(8,128)(2,1)}), bf16[4,384,128]{2,1,0:T(8,128)(2,1)S(1)}, u32[]{:S(2)}, u32[]{:S(2)}) async-start(bf16[4,384,128]{2,1,0:T(8,128)(2,1)} %shard_map.119), calls=%async_computation | async-start | bytes 786432 | tf_op jit(solution)/shard_map/all_to_all | solution.py:354
  28.5 10.4 %collective-permute-start.5 = (bf16[384,128]{1,0:T(8,128)(2,1)S(1)}, bf16[384,128]{1,0:T(8,128)(2,1)S(1)}, u32[]{:S(2)}, u32[]{:S(2)}) collective-permute-start(bf16[384,128]{1,0:T(8,128)(2,1)S(1)} %get-tuple-element.42), channel_id=1, source_target_pairs={{0,192},{8,200},{16,208},{24,216},{32,224},{40,232},{48,240},{56,2... | collective-permute-start | bytes 294920 | tf_op jit(solution)/shard_map/ppermute | solution.py:359
  33.4 8.5 %collective-permute-start.4 = (bf16[384,128]{1,0:T(8,128)(2,1)S(1)}, bf16[384,128]{1,0:T(8,128)(2,1)S(1)}, u32[]{:S(2)}, u32[]{:S(2)}) collective-permute-start(bf16[384,128]{1,0:T(8,128)(2,1)S(1)} %get-tuple-element.42), channel_id=1, source_target_pairs={{0,128},{8,136},{16,144},{24,152},{32,160},{40,168},{48,176},{56,1... | collective-permute-start | bytes 294920 | tf_op jit(solution)/shard_map/ppermute | solution.py:359
  36.0 7.7 %collective-permute-start.3 = (bf16[384,128]{1,0:T(8,128)(2,1)S(1)}, bf16[384,128]{1,0:T(8,128)(2,1)S(1)}, u32[]{:S(2)}, u32[]{:S(2)}) collective-permute-start(bf16[384,128]{1,0:T(8,128)(2,1)S(1)} %get-tuple-element.42), channel_id=1, source_target_pairs={{0,64},{8,72},{16,80},{24,88},{32,96},{40,104},{48,112},{56,120},{... | collective-permute-start | bytes 294920 | tf_op jit(solution)/shard_map/ppermute | solution.py:359
  45.3 12.4 %copy-start.7 = (bf16[256,256]{1,0:T(8,128)(2,1)S(1)}, bf16[256,256]{1,0:T(8,128)(2,1)}, u32[]{:S(2)}) copy-start(bf16[256,256]{1,0:T(8,128)(2,1)} %own_taps) | copy-start | bytes 393220
  45.3 14.4 %copy-start.10 = (bf16[4096]{0:T(1024)(128)(2,1)S(1)}, bf16[4096]{0:T(1024)(128)(2,1)}, u32[]{:S(2)}) copy-start(bf16[4096]{0:T(1024)(128)(2,1)} %param.13) | copy-start | bytes 24580
  45.3 24.2 %all-to-all-start.1 = ((bf16[4,1600,128]{2,1,0:T(8,128)(2,1)}), bf16[4,1600,128]{2,1,0:T(8,128)(2,1)S(1)}, u32[]{:S(2)}, u32[]{:S(2)}) async-start(bf16[4,1600,128]{2,1,0:T(8,128)(2,1)} %pad_maximum_fusion), calls=%async_computation.1 | async-start | bytes 3276800 | tf_op jit(solution)/shard_map/all_to_all | solution.py:364
  49.0 26.0 %collective-permute-start.7 = (bf16[4,384,128]{2,1,0:T(8,128)(2,1)S(1)}, bf16[4,384,128]{2,1,0:T(8,128)(2,1)S(1)}, u32[]{:S(2)}, u32[]{:S(2)}) collective-permute-start(bf16[4,384,128]{2,1,0:T(8,128)(2,1)S(1)} %pad_maximum_fusion.1.f0), channel_id=1, source_target_pairs={{0,16},{8,24},{16,32},{24,40},{32,48},{40,56},{48,0},{56,8},{64,80... | collective-permute-start | bytes 1179656 | tf_op jit(solution)/shard_map/ppermute | solution.py:365
  50.9 24.1 %collective-permute-start.8 = (bf16[4,384,128]{2,1,0:T(8,128)(2,1)S(1)}, bf16[4,384,128]{2,1,0:T(8,128)(2,1)S(1)}, u32[]{:S(2)}, u32[]{:S(2)}) collective-permute-start(bf16[4,384,128]{2,1,0:T(8,128)(2,1)S(1)} %pad_maximum_fusion.1.f0), channel_id=1, source_target_pairs={{0,32},{8,40},{16,48},{24,56},{32,0},{40,8},{48,16},{56,24},{64,96... | collective-permute-start | bytes 1179656 | tf_op jit(solution)/shard_map/ppermute | solution.py:365
  55.7 19.3 %collective-permute-start.9 = (bf16[4,384,128]{2,1,0:T(8,128)(2,1)S(1)}, bf16[4,384,128]{2,1,0:T(8,128)(2,1)}, u32[]{:S(2)}, u32[]{:S(2)}) collective-permute-start(bf16[4,384,128]{2,1,0:T(8,128)(2,1)S(1)} %pad_maximum_fusion.1.f0), channel_id=1, source_target_pairs={{0,48},{8,56},{16,0},{24,8},{32,16},{40,24},{48,32},{56,40},{64,11... | collective-permute-start | bytes 1179656 | tf_op jit(solution)/shard_map/ppermute | solution.py:365
  57.7 7.9 %collective-permute-start.6 = (bf16[256,256]{1,0:T(8,128)(2,1)S(1)}, bf16[256,256]{1,0:T(8,128)(2,1)}, u32[]{:S(2)}, u32[]{:S(2)}) collective-permute-start(bf16[256,256]{1,0:T(8,128)(2,1)S(1)} %copy-done.7), channel_id=1, source_target_pairs={{0,8},{8,0},{16,24},{24,16},{32,40},{40,32},{48,56},{56,48},{64,72... | collective-permute-start | bytes 393224 | tf_op jit(solution)/shard_map/ppermute | solution.py:366
  59.8 9.7 %copy-start.2 = (bf16[512,512]{1,0:T(8,128)(2,1)S(1)}, bf16[512,512]{1,0:T(8,128)(2,1)}, u32[]{:S(2)}) copy-start(bf16[512,512]{1,0:T(8,128)(2,1)} %unembed_ref.1) | copy-start | bytes 1572868
  62.9 2.0 %copy-start = (bf16[2,256,4096]{2,1,0:T(8,128)(2,1)}, bf16[2,256,4096]{2,1,0:T(8,128)(2,1)S(1)}, u32[]{:S(2)}) copy-start(bf16[2,256,4096]{2,1,0:T(8,128)(2,1)S(1)} %get-tuple-element.22.gained_hbm) | copy-start | bytes 12582916
  64.9 0.7 copy-start.4
  69.5 2.2 %copy-start.1 = (bf16[2,256,4096]{2,1,0:T(8,128)(2,1)S(1)}, bf16[2,256,4096]{2,1,0:T(8,128)(2,1)}, u32[]{:S(2)}) copy-start(bf16[2,256,4096]{2,1,0:T(8,128)(2,1)} %copy-done) | copy-start | bytes 12582916
  71.7 3.4 %copy-start.5 = (f32[2,256,128]{2,1,0:T(8,128)S(1)}, f32[2,256,128]{2,1,0:T(8,128)}, u32[]{:S(2)}) copy-start(f32[2,256,128]{2,1,0:T(8,128)} %copy-done.4) | copy-start | bytes 786436
  75.0 36.9 %copy-start.3 = (bf16[832,256]{1,0:T(8,128)(2,1)S(1)}, bf16[832,256]{1,0:T(8,128)(2,1)}, u32[]{:S(2)}) copy-start(bf16[832,256]{1,0:T(8,128)(2,1)} %constant.101.clone.matrices) | copy-start | bytes 1277956
  75.0 36.9 %copy-start.6 = (f32[128,256]{1,0:T(8,128)S(1)}, f32[128,256]{1,0:T(8,128)}, u32[]{:S(2)}) copy-start(f32[128,256]{1,0:T(8,128)} %constant.102.clone.twiddles) | copy-start | bytes 393220
  90.0 22.9 %collective-permute-start.10 = (bf16[16,64,128]{2,1,0:T(8,128)(2,1)S(1)}, bf16[16,64,128]{2,1,0:T(8,128)(2,1)S(1)}, u32[]{:S(2)}, u32[]{:S(2)}) collective-permute-start(bf16[16,64,128]{2,1,0:T(8,128)(2,1)S(1)} %all_to_all.36.got_ref), channel_id=1, source_target_pairs={{0,256},{8,264},{16,272},{24,280},{32,288},{40,296},{48,304},{56,3... | collective-permute-start | bytes 786440 | tf_op jit(solution)/shard_map/ppermute | solution.py:400
  98.8 27.0 %all-to-all-start.3 = ((bf16[8,32,128]{2,1,0:T(8,128)(2,1)}), bf16[8,32,128]{2,1,0:T(8,128)(2,1)S(1)}, u32[]{:S(2)}, u32[]{:S(2)}) async-start(bf16[8,32,128]{2,1,0:T(8,128)(2,1)} %get-tuple-element.35), calls=%async_computation.3 | async-start | bytes 131072 | tf_op jit(solution)/shard_map/all_to_all | solution.py:402
  126.6 32.3 %copy-start.12 = (s32[256]{0:T(256)S(1)}, s32[256]{0:T(256)}, u32[]{:S(2)}) copy-start(s32[256]{0:T(256)} %param.18) | copy-start | bytes 3076
  126.6 14.3 %all-to-all-start.4 = ((bf16[32,48,128]{2,1,0:T(8,128)(2,1)}), bf16[32,48,128]{2,1,0:T(8,128)(2,1)S(1)}, u32[]{:S(2)}, u32[]{:S(2)}) async-start(bf16[32,48,128]{2,1,0:T(8,128)(2,1)} %shard_map.125), calls=%async_computation.4 | async-start | bytes 786432 | tf_op jit(solution)/shard_map/all_to_all | solution.py:408
  132.8 34.9 %copy-start.11 = (s32[256]{0:T(256)S(1)}, s32[256]{0:T(256)}, u32[]{:S(2)}) copy-start(s32[256]{0:T(256)} %param.19) | copy-start | bytes 3076
  132.9 3.3 %collective-permute-start.11 = (bf16[2,128,128]{2,1,0:T(8,128)(2,1)S(1)}, bf16[2,128,128]{2,1,0:T(8,128)(2,1)S(1)}, u32[]{:S(2)}, u32[]{:S(2)}) collective-permute-start(bf16[2,128,128]{2,1,0:T(8,128)(2,1)S(1)} %get-tuple-element.39), channel_id=1, source_target_pairs={{0,8},{8,0},{16,24},{24,16},{32,40},{40,32},{48,56},{56,48},{64,72... | collective-permute-start | bytes 196616 | tf_op jit(solution)/shard_map/ppermute | solution.py:404
  154.0 13.4 %collective-permute-start.12 = (bf16[64,512]{1,0:T(8,128)(2,1)S(1)}, bf16[64,512]{1,0:T(8,128)(2,1)S(1)}, u32[]{:S(2)}, u32[]{:S(2)}) collective-permute-start(bf16[64,512]{1,0:T(8,128)(2,1)S(1)} %reduce_sum.30), channel_id=1, source_target_pairs={{0,4},{1,5},{2,6},{3,7},{4,0},{5,1},{6,2},{7,3},{8,12},{9,13},{10,... | collective-permute-start | bytes 196616 | tf_op jit(solution)/shard_map/ppermute | solution.py:422

commit v15 on v14

--- a/solution.py
+++ b/solution.py
@@ -65,7 +65,7 @@
 
 
 SCALARS = pl.BlockSpec(memory_space=pltpu.SMEM)
-ANYWHERE = pl.BlockSpec(memory_space=pl.ANY)
+IN_HBM = pl.BlockSpec(memory_space=pltpu.HBM)
 
 
 def spectrum(scratch, matrices, twiddles):
@@ -343,7 +343,7 @@
     first = call(
         first_kernel,
         shape((512, 128), BF16),
-        [SCALARS, ANYWHERE] + whole(1) + [ANYWHERE],
+        [SCALARS, IN_HBM] + whole(1) + [IN_HBM],
         [pltpu.VMEM((3, 64, 256), BF16), pltpu.VMEM((32, 512), BF16), pltpu.SemaphoreType.DMA((2,))],
         10**5,
         (core_at, w_in, lax.ppermute(w_in, "ctx", PERM_CORE), w_out),
@@ -369,7 +369,7 @@
     gained, scale = call(
         norm_kernel,
         (shape((2, 256, 4096), BF16), shape((2, 256, 128), F32)),
-        [ANYWHERE, ANYWHERE] + whole(1),
+        [IN_HBM, IN_HBM] + whole(1),
         [
             pltpu.VMEM((2, 256, 4096), BF16),
             pltpu.VMEM((2, 256, 4096), BF16),
@@ -378,12 +378,12 @@
         10**7,
         (tokens_in, beside, pre_gain.reshape(1, 4096)),
         mib=16,
-        out_specs=(ANYWHERE, whole(1)[0]),
+        out_specs=(IN_HBM, whole(1)[0]),
     )
     sums, terms, pieces = call(
         near_kernel,
         (shape((2, 256, 384), F32), shape((8, 32, 128), BF16), shape((16, 32, 128), BF16)),
-        [SCALARS] + [ANYWHERE] * 3 + whole(2),
+        [SCALARS] + [IN_HBM] * 3 + whole(2),
         [pltpu.VMEM((2, 256, 2048), BF16), pltpu.VMEM((2, 256, 256), BF16), pltpu.SemaphoreType.DMA((4,))],
         8 * 10**8,
         (at, gained, taps, taps_got, near, w_unembed),
@@ -391,7 +391,7 @@
     signal, gate = call(
         proj_kernel,
         (shape((16, 64, 128), BF16), shape((2, 2, 128, 128), BF16)),
-        [SCALARS, ANYWHERE] + whole(3) + [ANYWHERE] * 4,
+        [SCALARS, IN_HBM] + whole(3) + [IN_HBM] * 4,
         [pltpu.VMEM((2, 256, 2048), BF16), pltpu.VMEM((4, 4, 384, 128), BF16), pltpu.SemaphoreType.DMA((6,))],
         8 * 10**8,
         (at, gained, scale, sums, pieces, *fars),

time: 179 us -> 179 us (level)
  no operation moved by 1% of the time
where the time goes in v15:
time: 179 us; the launch traced here: 177 us
  starting transfers between devices  84 us (47%)
  waiting for transfers between devices  34.6 us (19%)
  blocking collectives  32 us (18%)
  Pallas kernels  14.5 us (8%)
  local copies, waits for them, and re-layouts  8.02 us (4%)
  other arithmetic  2.55 us (1%)
    ppermute x1, starting transfers between devices, per_device(): far = lax.ppermute(first, 'ctx', PERM_Z)  15.7 us
    pallas_call x9, Pallas kernels, call(): pl.pallas_call(kernel, out_shape=outs, in_specs=specs, out_specs=out_spec...  14.5 us
    all_to_all x1, starting transfers between devices, per_device(): terms = lax.all_to_all(terms, 'tp', 0, 0, tiled=True)  13.1 us
    all_to_all x1, blocking collectives, per_device(): lax.all_to_all(logits.reshape(4, 64, 512), 'tp', 0, 0, axis_index_groups=...  12.7 us
    all_to_all x1, blocking collectives, per_device(): lax.all_to_all(signal, 'ctx', 0, 0, axis_index_groups=GROUPS_CORE, tiled=...  11.5 us
    all_to_all x1, waiting for transfers between devices, per_device(): terms = lax.all_to_all(terms, 'tp', 0, 0, tiled=True)  11.4 us
    ppermute x3, starting transfers between devices, per_device(): lax.ppermute(far, 'ctx', PERM_Y[k])  10.3 us
    ppermute x1, starting transfers between devices, per_device(): before = lax.ppermute(got, 'ctx', PERM_Z_UP)  8.81 us
  transfers between devices with their start and end apart: 17, of which 7 were waited for; matrix products, arithmetic and copies ran while one was open for 2% of the time, Pallas kernels for 5%

profile of v15, /device:TPU:6, one launch (start us, length us, event | category | flops | bytes accessed | tf_op | source)
XLA Modules:
  0.0 177.5 jit_solution(17193673096766739161)
XLA Ops:
  0.0 1.9 %collective-permute-start = (bf16[3,64,256]{2,1,0:T(8,128)(2,1)}, bf16[3,64,256]{2,1,0:T(8,128)(2,1)S(1)}, u32[]{:S(2)}, u32[]{:S(2)}) collective-permute-start(bf16[3,64,256]{2,1,0:T(8,128)(2,1)} %bitcast.24), channel_id=1, source_target_pairs={{0,8},{8,0},{16,24},{24,16},{32,40},{40,32},{48,56},{56,48},{64,72... | collective-permute-start | bytes 294920 | tf_op jit(solution)/shard_map/ppermute | solution.py:349
  5.2 15.7 %collective-permute-start.2 = (bf16[512,128]{1,0:T(8,128)(2,1)S(1)}, bf16[512,128]{1,0:T(8,128)(2,1)S(1)}, u32[]{:S(2)}, u32[]{:S(2)}) collective-permute-start(bf16[512,128]{1,0:T(8,128)(2,1)S(1)} %shard_map.118.first_ref), channel_id=1, source_target_pairs={{0,256},{8,264},{16,272},{24,280},{32,288},{40,296},{48,304},{56,3... | collective-permute-start | bytes 393224 | tf_op jit(solution)/shard_map/ppermute | solution.py:355
  21.8 1.9 %collective-permute-start.1 = (bf16[256,4096]{1,0:T(8,128)(2,1)}, bf16[256,4096]{1,0:T(8,128)(2,1)}, u32[]{:S(2)}, u32[]{:S(2)}) collective-permute-start(bf16[256,4096]{1,0:T(8,128)(2,1)} %own_hbm.1), channel_id=1, source_target_pairs={{0,8},{8,0},{16,24},{24,16},{32,40},{40,32},{48,56},{56,48},{64,72... | collective-permute-start | bytes 6291464 | tf_op jit(solution)/shard_map/ppermute | solution.py:353
  23.7 4.8 %all-to-all-start = ((bf16[4,384,128]{2,1,0:T(8,128)(2,1)}), bf16[4,384,128]{2,1,0:T(8,128)(2,1)S(1)}, u32[]{:S(2)}, u32[]{:S(2)}) async-start(bf16[4,384,128]{2,1,0:T(8,128)(2,1)} %shard_map.119), calls=%async_computation | async-start | bytes 786432 | tf_op jit(solution)/shard_map/all_to_all | solution.py:354
  28.5 4.9 %collective-permute-start.5 = (bf16[384,128]{1,0:T(8,128)(2,1)S(1)}, bf16[384,128]{1,0:T(8,128)(2,1)S(1)}, u32[]{:S(2)}, u32[]{:S(2)}) collective-permute-start(bf16[384,128]{1,0:T(8,128)(2,1)S(1)} %get-tuple-element.42), channel_id=1, source_target_pairs={{0,192},{8,200},{16,208},{24,216},{32,224},{40,232},{48,240},{56,2... | collective-permute-start | bytes 294920 | tf_op jit(solution)/shard_map/ppermute | solution.py:359
  33.4 2.5 %collective-permute-start.4 = (bf16[384,128]{1,0:T(8,128)(2,1)S(1)}, bf16[384,128]{1,0:T(8,128)(2,1)S(1)}, u32[]{:S(2)}, u32[]{:S(2)}) collective-permute-start(bf16[384,128]{1,0:T(8,128)(2,1)S(1)} %get-tuple-element.42), channel_id=1, source_target_pairs={{0,128},{8,136},{16,144},{24,152},{32,160},{40,168},{48,176},{56,1... | collective-permute-start | bytes 294920 | tf_op jit(solution)/shard_map/ppermute | solution.py:359
  36.0 2.9 %collective-permute-start.3 = (bf16[384,128]{1,0:T(8,128)(2,1)S(1)}, bf16[384,128]{1,0:T(8,128)(2,1)S(1)}, u32[]{:S(2)}, u32[]{:S(2)}) collective-permute-start(bf16[384,128]{1,0:T(8,128)(2,1)S(1)} %get-tuple-element.42), channel_id=1, source_target_pairs={{0,64},{8,72},{16,80},{24,88},{32,96},{40,104},{48,112},{56,120},{... | collective-permute-start | bytes 294920 | tf_op jit(solution)/shard_map/ppermute | solution.py:359
  38.9 3.0 %collective-permute-done.4 = bf16[384,128]{1,0:T(8,128)(2,1)S(1)} collective-permute-done((bf16[384,128]{1,0:T(8,128)(2,1)S(1)}, bf16[384,128]{1,0:T(8,128)(2,1)S(1)}, u32[]{:S(2)}, u32[]{:S(2)}) %collective-permute-start.4) | collective-permute-done | bytes 98336 | tf_op jit(solution)/shard_map/ppermute | solution.py:359
  41.9 1.8 collective-permute-done.3
  45.3 3.7 %all-to-all-start.1 = ((bf16[4,1600,128]{2,1,0:T(8,128)(2,1)}), bf16[4,1600,128]{2,1,0:T(8,128)(2,1)S(1)}, u32[]{:S(2)}, u32[]{:S(2)}) async-start(bf16[4,1600,128]{2,1,0:T(8,128)(2,1)} %pad_maximum_fusion), calls=%async_computation.1 | async-start | bytes 3276800 | tf_op jit(solution)/shard_map/all_to_all | solution.py:364
  49.0 1.9 %collective-permute-start.7 = (bf16[4,384,128]{2,1,0:T(8,128)(2,1)S(1)}, bf16[4,384,128]{2,1,0:T(8,128)(2,1)S(1)}, u32[]{:S(2)}, u32[]{:S(2)}) collective-permute-start(bf16[4,384,128]{2,1,0:T(8,128)(2,1)S(1)} %pad_maximum_fusion.1.f0), channel_id=1, source_target_pairs={{0,16},{8,24},{16,32},{24,40},{32,48},{40,56},{48,0},{56,8},{64,80... | collective-permute-start | bytes 1179656 | tf_op jit(solution)/shard_map/ppermute | solution.py:365
  50.9 4.8 %collective-permute-start.8 = (bf16[4,384,128]{2,1,0:T(8,128)(2,1)S(1)}, bf16[4,384,128]{2,1,0:T(8,128)(2,1)S(1)}, u32[]{:S(2)}, u32[]{:S(2)}) collective-permute-start(bf16[4,384,128]{2,1,0:T(8,128)(2,1)S(1)} %pad_maximum_fusion.1.f0), channel_id=1, source_target_pairs={{0,32},{8,40},{16,48},{24,56},{32,0},{40,8},{48,16},{56,24},{64,96... | collective-permute-start | bytes 1179656 | tf_op jit(solution)/shard_map/ppermute | solution.py:365
  55.7 1.9 %collective-permute-start.9 = (bf16[4,384,128]{2,1,0:T(8,128)(2,1)S(1)}, bf16[4,384,128]{2,1,0:T(8,128)(2,1)}, u32[]{:S(2)}, u32[]{:S(2)}) collective-permute-start(bf16[4,384,128]{2,1,0:T(8,128)(2,1)S(1)} %pad_maximum_fusion.1.f0), channel_id=1, source_target_pairs={{0,48},{8,56},{16,0},{24,8},{32,16},{40,24},{48,32},{56,40},{64,11... | collective-permute-start | bytes 1179656 | tf_op jit(solution)/shard_map/ppermute | solution.py:365
  57.7 1.9 %collective-permute-start.6 = (bf16[256,256]{1,0:T(8,128)(2,1)S(1)}, bf16[256,256]{1,0:T(8,128)(2,1)}, u32[]{:S(2)}, u32[]{:S(2)}) collective-permute-start(bf16[256,256]{1,0:T(8,128)(2,1)S(1)} %copy-done.7), channel_id=1, source_target_pairs={{0,8},{8,0},{16,24},{24,16},{32,40},{40,32},{48,56},{56,48},{64,72... | collective-permute-start | bytes 393224 | tf_op jit(solution)/shard_map/ppermute | solution.py:366
  59.8 3.1 %shard_map.120 = (bf16[2,256,4096]{2,1,0:T(8,128)(2,1)S(1)}, f32[2,256,128]{2,1,0:T(8,128)S(1)}) custom-call(bf16[256,4096]{1,0:T(8,128)(2,1)} %own_hbm.1, bf16[256,4096]{1,0:T(8,128)(2,1)} %collective-permute-done.1.beside_hbm, bf16[1,4096]{1,0:T(2,128)(2,1)S(1)} %reshape.28.gain_ref), custom_call_target="tpu_custom_call" | custom-call | flops 10000000 | bytes 4194304 | tf_op jit(solution)/shard_map/pallas_call | solution.py:294
  62.9 1.9 %copy-done = bf16[2,256,4096]{2,1,0:T(8,128)(2,1)} copy-done((bf16[2,256,4096]{2,1,0:T(8,128)(2,1)}, bf16[2,256,4096]{2,1,0:T(8,128)(2,1)S(1)}, u32[]{:S(2)}) %copy-start) | copy-done | bytes 4194328
  65.6 3.9 %all-to-all-done.1.near_ref = bf16[4,1600,128]{2,1,0:T(8,128)(2,1)S(1)} async-done(((bf16[4,1600,128]{2,1,0:T(8,128)(2,1)}), bf16[4,1600,128]{2,1,0:T(8,128)(2,1)S(1)}, u32[]{:S(2)}, u32[]{:S(2)}) %all-to-all-start.1) | async-done | bytes 1638432 | tf_op jit(solution)/shard_map/all_to_all | solution.py:364
  69.5 2.2 %copy-done.1 = bf16[2,256,4096]{2,1,0:T(8,128)(2,1)S(1)} copy-done((bf16[2,256,4096]{2,1,0:T(8,128)(2,1)S(1)}, bf16[2,256,4096]{2,1,0:T(8,128)(2,1)}, u32[]{:S(2)}) %copy-start.1) | copy-done | bytes 4194328
  71.7 3.3 %shard_map.121 = (f32[2,256,384]{2,1,0:T(8,128)S(1)}, bf16[8,32,128]{2,1,0:T(8,128)(2,1)}, bf16[16,32,128]{2,1,0:T(8,128)(2,1)S(1)}) custom-call(s32[4]{0:T(128)S(1)} %pad_add_fusion.at_ref, bf16[2,256,4096]{2,1,0:T(8,128)(2,1)S(1)} %copy-done.1, bf16[256,256]{1,0:T(8,128)(2,1)S(1)} %copy-done.7, bf16[256,256]{1,0:T(8,128)(2,1)} %collective-permute-done.6.got_taps, ...), custom_call_target="tpu_custom_call" | custom-call | flops 800000000 | bytes 4194304 | tf_op jit(solution)/shard_map/pallas_call | solution.py:294
  75.0 3.4 %shard_map.122 = (bf16[16,64,128]{2,1,0:T(8,128)(2,1)S(1)}, bf16[2,2,128,128]{3,2,1,0:T(8,128)(2,1)S(1)}) custom-call(s32[4]{0:T(128)S(1)} %pad_add_fusion.at_ref, bf16[2,256,4096]{2,1,0:T(8,128)(2,1)S(1)} %copy-done.1, f32[2,256,128]{2,1,0:T(8,128)S(1)} %copy-done.5, f32[2,256,384]{2,1,0:T(8,128)S(1)} %get-tuple-element.28.near_ref, ...), custom_call_target="tpu_custom_call" | custom-call | flops 800000000 | bytes 4194304 | tf_op jit(solution)/shard_map/pallas_call | solution.py:294
  78.5 11.5 %all_to_all.36.got_ref = bf16[16,64,128]{2,1,0:T(8,128)(2,1)S(1)} all-to-all(bf16[16,64,128]{2,1,0:T(8,128)(2,1)S(1)} %get-tuple-element.31), channel_id=1, replica_groups={{0,16,32,48,64,80,96,112,128,144,160,176,192,208,224,240},{8,24,40,56,7..., dimensions={0} | all-to-all | bytes 524288 | tf_op jit(solution)/shard_map/all_to_all | solution.py:399
  90.0 8.8 %collective-permute-start.10 = (bf16[16,64,128]{2,1,0:T(8,128)(2,1)S(1)}, bf16[16,64,128]{2,1,0:T(8,128)(2,1)S(1)}, u32[]{:S(2)}, u32[]{:S(2)}) collective-permute-start(bf16[16,64,128]{2,1,0:T(8,128)(2,1)S(1)} %all_to_all.36.got_ref), channel_id=1, source_target_pairs={{0,256},{8,264},{16,272},{24,280},{32,288},{40,296},{48,304},{56,3... | collective-permute-start | bytes 786440 | tf_op jit(solution)/shard_map/ppermute | solution.py:400
  98.8 13.1 %all-to-all-start.3 = ((bf16[8,32,128]{2,1,0:T(8,128)(2,1)}), bf16[8,32,128]{2,1,0:T(8,128)(2,1)S(1)}, u32[]{:S(2)}, u32[]{:S(2)}) async-start(bf16[8,32,128]{2,1,0:T(8,128)(2,1)} %get-tuple-element.35), calls=%async_computation.3 | async-start | bytes 131072 | tf_op jit(solution)/shard_map/all_to_all | solution.py:402
  112.9 1.5 shard_map.124.conv_ref
  114.5 11.4 %all-to-all-done.3.terms_ref = bf16[8,32,128]{2,1,0:T(8,128)(2,1)S(1)} async-done(((bf16[8,32,128]{2,1,0:T(8,128)(2,1)}), bf16[8,32,128]{2,1,0:T(8,128)(2,1)S(1)}, u32[]{:S(2)}, u32[]{:S(2)}) %all-to-all-start.3) | async-done | bytes 65568 | tf_op jit(solution)/shard_map/all_to_all | solution.py:402
  126.6 6.2 %all-to-all-start.4 = ((bf16[32,48,128]{2,1,0:T(8,128)(2,1)}), bf16[32,48,128]{2,1,0:T(8,128)(2,1)S(1)}, u32[]{:S(2)}, u32[]{:S(2)}) async-start(bf16[32,48,128]{2,1,0:T(8,128)(2,1)} %shard_map.125), calls=%async_computation.4 | async-start | bytes 786432 | tf_op jit(solution)/shard_map/all_to_all | solution.py:408
  132.9 2.1 %collective-permute-start.11 = (bf16[2,128,128]{2,1,0:T(8,128)(2,1)S(1)}, bf16[2,128,128]{2,1,0:T(8,128)(2,1)S(1)}, u32[]{:S(2)}, u32[]{:S(2)}) collective-permute-start(bf16[2,128,128]{2,1,0:T(8,128)(2,1)S(1)} %get-tuple-element.39), channel_id=1, source_target_pairs={{0,8},{8,0},{16,24},{24,16},{32,40},{40,32},{48,56},{56,48},{64,72... | collective-permute-start | bytes 196616 | tf_op jit(solution)/shard_map/ppermute | solution.py:404
  136.2 4.7 %all-to-all-done.4.got_ref = bf16[32,48,128]{2,1,0:T(8,128)(2,1)S(1)} async-done(((bf16[32,48,128]{2,1,0:T(8,128)(2,1)}), bf16[32,48,128]{2,1,0:T(8,128)(2,1)S(1)}, u32[]{:S(2)}, u32[]{:S(2)}) %all-to-all-start.4) | async-done | bytes 393248 | tf_op jit(solution)/shard_map/all_to_all | solution.py:408
  141.3 12.7 %all_to_all.37 = bf16[4,64,512]{2,1,0:T(8,128)(2,1)S(1)} all-to-all(bf16[4,64,512]{2,1,0:T(8,128)(2,1)S(1)} %bitcast.23), channel_id=1, replica_groups={{0,1,2,3},{4,5,6,7},{8,9,10,11},{12,13,14,15},{16,17,18,19},{20,21,22,2..., dimensions={0} | all-to-all | bytes 524288 | tf_op jit(solution)/shard_map/all_to_all | solution.py:420
  154.0 4.9 %collective-permute-start.12 = (bf16[64,512]{1,0:T(8,128)(2,1)S(1)}, bf16[64,512]{1,0:T(8,128)(2,1)S(1)}, u32[]{:S(2)}, u32[]{:S(2)}) collective-permute-start(bf16[64,512]{1,0:T(8,128)(2,1)S(1)} %reduce_sum.30), channel_id=1, source_target_pairs={{0,4},{1,5},{2,6},{3,7},{4,0},{5,1},{6,2},{7,3},{8,12},{9,13},{10,... | collective-permute-start | bytes 196616 | tf_op jit(solution)/shard_map/ppermute | solution.py:422
  159.0 8.3 %collective-permute-done.12 = bf16[64,512]{1,0:T(8,128)(2,1)S(1)} collective-permute-done((bf16[64,512]{1,0:T(8,128)(2,1)S(1)}, bf16[64,512]{1,0:T(8,128)(2,1)S(1)}, u32[]{:S(2)}, u32[]{:S(2)}) %collective-permute-start.12) | collective-permute-done | bytes 65568 | tf_op jit(solution)/shard_map/ppermute | solution.py:422
  167.8 7.9 %all_to_all.38 = f32[4,1,64]{2,1,0:T(1,128)S(1)} all-to-all(f32[4,1,64]{2,1,0:T(1,128)S(1)} %broadcast_in_dim.22), channel_id=1, replica_groups={{0,1,2,3},{4,5,6,7},{8,9,10,11},{12,13,14,15},{16,17,18,19},{20,21,22,2..., dimensions={0} | all-to-all | bytes 2048 | tf_op jit(solution)/shard_map/all_to_all | solution.py:433
  (61 shorter events, 12.2 us)
Async XLA Ops:
  0.0 3.4 %collective-permute-start = (bf16[3,64,256]{2,1,0:T(8,128)(2,1)}, bf16[3,64,256]{2,1,0:T(8,128)(2,1)S(1)}, u32[]{:S(2)}, u32[]{:S(2)}) collective-permute-start(bf16[3,64,256]{2,1,0:T(8,128)(2,1)} %bitcast.24), channel_id=1, source_target_pairs={{0,8},{8,0},{16,24},{24,16},{32,40},{40,32},{48,56},{56,48},{64,72... | collective-permute-start | bytes 294920 | tf_op jit(solution)/shard_map/ppermute | solution.py:349
  3.4 0.9 copy-start.8
  4.3 0.8 copy-start.9
  5.2 23.2 %collective-permute-start.2 = (bf16[512,128]{1,0:T(8,128)(2,1)S(1)}, bf16[512,128]{1,0:T(8,128)(2,1)S(1)}, u32[]{:S(2)}, u32[]{:S(2)}) collective-permute-start(bf16[512,128]{1,0:T(8,128)(2,1)S(1)} %shard_map.118.first_ref), channel_id=1, source_target_pairs={{0,256},{8,264},{16,272},{24,280},{32,288},{40,296},{48,304},{56,3... | collective-permute-start | bytes 393224 | tf_op jit(solution)/shard_map/ppermute | solution.py:355
  21.8 38.0 %collective-permute-start.1 = (bf16[256,4096]{1,0:T(8,128)(2,1)}, bf16[256,4096]{1,0:T(8,128)(2,1)}, u32[]{:S(2)}, u32[]{:S(2)}) collective-permute-start(bf16[256,4096]{1,0:T(8,128)(2,1)} %own_hbm.1), channel_id=1, source_target_pairs={{0,8},{8,0},{16,24},{24,16},{32,40},{40,32},{48,56},{56,48},{64,72... | collective-permute-start | bytes 6291464 | tf_op jit(solution)/shard_map/ppermute | solution.py:353
  23.7 20.1 %all-to-all-start = ((bf16[4,384,128]{2,1,0:T(8,128)(2,1)}), bf16[4,384,128]{2,1,0:T(8,128)(2,1)S(1)}, u32[]{:S(2)}, u32[]{:S(2)}) async-start(bf16[4,384,128]{2,1,0:T(8,128)(2,1)} %shard_map.119), calls=%async_computation | async-start | bytes 786432 | tf_op jit(solution)/shard_map/all_to_all | solution.py:354
  28.5 10.4 %collective-permute-start.5 = (bf16[384,128]{1,0:T(8,128)(2,1)S(1)}, bf16[384,128]{1,0:T(8,128)(2,1)S(1)}, u32[]{:S(2)}, u32[]{:S(2)}) collective-permute-start(bf16[384,128]{1,0:T(8,128)(2,1)S(1)} %get-tuple-element.42), channel_id=1, source_target_pairs={{0,192},{8,200},{16,208},{24,216},{32,224},{40,232},{48,240},{56,2... | collective-permute-start | bytes 294920 | tf_op jit(solution)/shard_map/ppermute | solution.py:359
  33.4 8.5 %collective-permute-start.4 = (bf16[384,128]{1,0:T(8,128)(2,1)S(1)}, bf16[384,128]{1,0:T(8,128)(2,1)S(1)}, u32[]{:S(2)}, u32[]{:S(2)}) collective-permute-start(bf16[384,128]{1,0:T(8,128)(2,1)S(1)} %get-tuple-element.42), channel_id=1, source_target_pairs={{0,128},{8,136},{16,144},{24,152},{32,160},{40,168},{48,176},{56,1... | collective-permute-start | bytes 294920 | tf_op jit(solution)/shard_map/ppermute | solution.py:359
  36.0 7.7 %collective-permute-start.3 = (bf16[384,128]{1,0:T(8,128)(2,1)S(1)}, bf16[384,128]{1,0:T(8,128)(2,1)S(1)}, u32[]{:S(2)}, u32[]{:S(2)}) collective-permute-start(bf16[384,128]{1,0:T(8,128)(2,1)S(1)} %get-tuple-element.42), channel_id=1, source_target_pairs={{0,64},{8,72},{16,80},{24,88},{32,96},{40,104},{48,112},{56,120},{... | collective-permute-start | bytes 294920 | tf_op jit(solution)/shard_map/ppermute | solution.py:359
  45.3 12.4 %copy-start.7 = (bf16[256,256]{1,0:T(8,128)(2,1)S(1)}, bf16[256,256]{1,0:T(8,128)(2,1)}, u32[]{:S(2)}) copy-start(bf16[256,256]{1,0:T(8,128)(2,1)} %own_taps) | copy-start | bytes 393220
  45.3 14.4 %copy-start.10 = (bf16[4096]{0:T(1024)(128)(2,1)S(1)}, bf16[4096]{0:T(1024)(128)(2,1)}, u32[]{:S(2)}) copy-start(bf16[4096]{0:T(1024)(128)(2,1)} %param.13) | copy-start | bytes 24580
  45.3 24.2 %all-to-all-start.1 = ((bf16[4,1600,128]{2,1,0:T(8,128)(2,1)}), bf16[4,1600,128]{2,1,0:T(8,128)(2,1)S(1)}, u32[]{:S(2)}, u32[]{:S(2)}) async-start(bf16[4,1600,128]{2,1,0:T(8,128)(2,1)} %pad_maximum_fusion), calls=%async_computation.1 | async-start | bytes 3276800 | tf_op jit(solution)/shard_map/all_to_all | solution.py:364
  49.0 26.0 %collective-permute-start.7 = (bf16[4,384,128]{2,1,0:T(8,128)(2,1)S(1)}, bf16[4,384,128]{2,1,0:T(8,128)(2,1)S(1)}, u32[]{:S(2)}, u32[]{:S(2)}) collective-permute-start(bf16[4,384,128]{2,1,0:T(8,128)(2,1)S(1)} %pad_maximum_fusion.1.f0), channel_id=1, source_target_pairs={{0,16},{8,24},{16,32},{24,40},{32,48},{40,56},{48,0},{56,8},{64,80... | collective-permute-start | bytes 1179656 | tf_op jit(solution)/shard_map/ppermute | solution.py:365
  50.9 24.1 %collective-permute-start.8 = (bf16[4,384,128]{2,1,0:T(8,128)(2,1)S(1)}, bf16[4,384,128]{2,1,0:T(8,128)(2,1)S(1)}, u32[]{:S(2)}, u32[]{:S(2)}) collective-permute-start(bf16[4,384,128]{2,1,0:T(8,128)(2,1)S(1)} %pad_maximum_fusion.1.f0), channel_id=1, source_target_pairs={{0,32},{8,40},{16,48},{24,56},{32,0},{40,8},{48,16},{56,24},{64,96... | collective-permute-start | bytes 1179656 | tf_op jit(solution)/shard_map/ppermute | solution.py:365
  55.7 19.3 %collective-permute-start.9 = (bf16[4,384,128]{2,1,0:T(8,128)(2,1)S(1)}, bf16[4,384,128]{2,1,0:T(8,128)(2,1)}, u32[]{:S(2)}, u32[]{:S(2)}) collective-permute-start(bf16[4,384,128]{2,1,0:T(8,128)(2,1)S(1)} %pad_maximum_fusion.1.f0), channel_id=1, source_target_pairs={{0,48},{8,56},{16,0},{24,8},{32,16},{40,24},{48,32},{56,40},{64,11... | collective-permute-start | bytes 1179656 | tf_op jit(solution)/shard_map/ppermute | solution.py:365
  57.7 7.9 %collective-permute-start.6 = (bf16[256,256]{1,0:T(8,128)(2,1)S(1)}, bf16[256,256]{1,0:T(8,128)(2,1)}, u32[]{:S(2)}, u32[]{:S(2)}) collective-permute-start(bf16[256,256]{1,0:T(8,128)(2,1)S(1)} %copy-done.7), channel_id=1, source_target_pairs={{0,8},{8,0},{16,24},{24,16},{32,40},{40,32},{48,56},{56,48},{64,72... | collective-permute-start | bytes 393224 | tf_op jit(solution)/shard_map/ppermute | solution.py:366
  59.8 9.7 %copy-start.2 = (bf16[512,512]{1,0:T(8,128)(2,1)S(1)}, bf16[512,512]{1,0:T(8,128)(2,1)}, u32[]{:S(2)}) copy-start(bf16[512,512]{1,0:T(8,128)(2,1)} %unembed_ref.1) | copy-start | bytes 1572868
  62.9 2.0 %copy-start = (bf16[2,256,4096]{2,1,0:T(8,128)(2,1)}, bf16[2,256,4096]{2,1,0:T(8,128)(2,1)S(1)}, u32[]{:S(2)}) copy-start(bf16[2,256,4096]{2,1,0:T(8,128)(2,1)S(1)} %get-tuple-element.22.gained_hbm) | copy-start | bytes 12582916
  64.9 0.7 copy-start.4
  69.5 2.2 %copy-start.1 = (bf16[2,256,4096]{2,1,0:T(8,128)(2,1)S(1)}, bf16[2,256,4096]{2,1,0:T(8,128)(2,1)}, u32[]{:S(2)}) copy-start(bf16[2,256,4096]{2,1,0:T(8,128)(2,1)} %copy-done) | copy-start | bytes 12582916
  71.7 3.4 %copy-start.5 = (f32[2,256,128]{2,1,0:T(8,128)S(1)}, f32[2,256,128]{2,1,0:T(8,128)}, u32[]{:S(2)}) copy-start(f32[2,256,128]{2,1,0:T(8,128)} %copy-done.4) | copy-start | bytes 786436
  75.0 36.9 %copy-start.3 = (bf16[832,256]{1,0:T(8,128)(2,1)S(1)}, bf16[832,256]{1,0:T(8,128)(2,1)}, u32[]{:S(2)}) copy-start(bf16[832,256]{1,0:T(8,128)(2,1)} %constant.101.clone.matrices) | copy-start | bytes 1277956
  75.0 36.9 %copy-start.6 = (f32[128,256]{1,0:T(8,128)S(1)}, f32[128,256]{1,0:T(8,128)}, u32[]{:S(2)}) copy-start(f32[128,256]{1,0:T(8,128)} %constant.102.clone.twiddles) | copy-start | bytes 393220
  90.0 22.9 %collective-permute-start.10 = (bf16[16,64,128]{2,1,0:T(8,128)(2,1)S(1)}, bf16[16,64,128]{2,1,0:T(8,128)(2,1)S(1)}, u32[]{:S(2)}, u32[]{:S(2)}) collective-permute-start(bf16[16,64,128]{2,1,0:T(8,128)(2,1)S(1)} %all_to_all.36.got_ref), channel_id=1, source_target_pairs={{0,256},{8,264},{16,272},{24,280},{32,288},{40,296},{48,304},{56,3... | collective-permute-start | bytes 786440 | tf_op jit(solution)/shard_map/ppermute | solution.py:400
  98.8 27.0 %all-to-all-start.3 = ((bf16[8,32,128]{2,1,0:T(8,128)(2,1)}), bf16[8,32,128]{2,1,0:T(8,128)(2,1)S(1)}, u32[]{:S(2)}, u32[]{:S(2)}) async-start(bf16[8,32,128]{2,1,0:T(8,128)(2,1)} %get-tuple-element.35), calls=%async_computation.3 | async-start | bytes 131072 | tf_op jit(solution)/shard_map/all_to_all | solution.py:402
  126.6 32.3 %copy-start.12 = (s32[256]{0:T(256)S(1)}, s32[256]{0:T(256)}, u32[]{:S(2)}) copy-start(s32[256]{0:T(256)} %param.18) | copy-start | bytes 3076
  126.6 14.3 %all-to-all-start.4 = ((bf16[32,48,128]{2,1,0:T(8,128)(2,1)}), bf16[32,48,128]{2,1,0:T(8,128)(2,1)S(1)}, u32[]{:S(2)}, u32[]{:S(2)}) async-start(bf16[32,48,128]{2,1,0:T(8,128)(2,1)} %shard_map.125), calls=%async_computation.4 | async-start | bytes 786432 | tf_op jit(solution)/shard_map/all_to_all | solution.py:408
  132.8 34.9 %copy-start.11 = (s32[256]{0:T(256)S(1)}, s32[256]{0:T(256)}, u32[]{:S(2)}) copy-start(s32[256]{0:T(256)} %param.19) | copy-start | bytes 3076
  132.9 3.3 %collective-permute-start.11 = (bf16[2,128,128]{2,1,0:T(8,128)(2,1)S(1)}, bf16[2,128,128]{2,1,0:T(8,128)(2,1)S(1)}, u32[]{:S(2)}, u32[]{:S(2)}) collective-permute-start(bf16[2,128,128]{2,1,0:T(8,128)(2,1)S(1)} %get-tuple-element.39), channel_id=1, source_target_pairs={{0,8},{8,0},{16,24},{24,16},{32,40},{40,32},{48,56},{56,48},{64,72... | collective-permute-start | bytes 196616 | tf_op jit(solution)/shard_map/ppermute | solution.py:404
  154.0 13.4 %collective-permute-start.12 = (bf16[64,512]{1,0:T(8,128)(2,1)S(1)}, bf16[64,512]{1,0:T(8,128)(2,1)S(1)}, u32[]{:S(2)}, u32[]{:S(2)}) collective-permute-start(bf16[64,512]{1,0:T(8,128)(2,1)S(1)} %reduce_sum.30), channel_id=1, source_target_pairs={{0,4},{1,5},{2,6},{3,7},{4,0},{5,1},{6,2},{7,3},{8,12},{9,13},{10,... | collective-permute-start | bytes 196616 | tf_op jit(solution)/shard_map/ppermute | solution.py:422

commit v16 on v12

--- a/solution.py
+++ b/solution.py
@@ -65,6 +65,7 @@
 
 
 SCALARS = pl.BlockSpec(memory_space=pltpu.SMEM)
+IN_HBM = pl.BlockSpec(memory_space=pltpu.HBM)
 
 
 def spectrum(scratch, matrices, twiddles):
@@ -137,12 +138,10 @@
     core = core_ref[0]
     half = pl.ds(pl.multiple_of(core * 128, 128), 128)
     for g in range(3):
-        own, got = own_ref[g, :, half], got_ref[g, :, half]
+        own, got = own_ref[g], got_ref[g, :, half]
         out_ref[g * 128 : g * 128 + 64] = jnp.where(core == 0, own, got)
         out_ref[g * 128 + 64 : g * 128 + 128] = jnp.where(core == 0, got, own)
-    rows = rows_ref[...].astype(F32)
-    blocks = [rows[y * 8 : y * 8 + 8, v * 128 : v * 128 + 128] for y in range(4) for v in range(4)]
-    out_ref[384:] = jnp.concatenate(blocks, axis=0).astype(BF16)
+    out_ref[384:] = rows_ref[...]
 
 
 def copies_kernel(first_ref, out_ref):
@@ -150,22 +149,55 @@
         out_ref[k] = first_ref[:384]
 
 
+def spread_kernel(z_ref, near_ref, first_ref, far_ref, out_hbm, sems):
+    z = z_ref[0]
+    copies = []
+    for y in range(4):
+        copies.append(pltpu.make_async_copy(near_ref, out_hbm.at[y, pl.ds(0, 1536)], sems.at[y, 0]))
+        rows = pl.ds(384 + y * 32, 32)
+        for k, (ref, place) in enumerate(((first_ref, z), (far_ref, 1 - z))):
+            to = pl.ds(pl.multiple_of(1536 + place * 32, 32), 32)
+            copies.append(pltpu.make_async_copy(ref.at[rows], out_hbm.at[y, to], sems.at[y, k + 1]))
+    for copy in copies:
+        copy.start()
+    for copy in copies:
+        copy.wait()
+
+
+def last_kernel(scores_ref, out_ref):
+    out_ref[...] = jnp.concatenate([scores_ref[k] for k in range(4)], axis=1)
+
+
 def weight_block(ref, lead, row):
     return jnp.concatenate([ref[lead, row + 128 * g : row + 128 * g + 128, :] for g in range(3)], axis=1)
 
 
 def near_kernel(
-    at_ref, own_hbm, beside_hbm, gain_ref, near_ref, gained_ref, scale_ref, out_ref, tokens, sems
+    at_ref, own_hbm, beside_hbm, gain_ref, own_taps, got_taps, near_ref, unembed_ref,
+    gained_ref, scale_ref, out_ref, terms_ref, pieces_ref, tokens, taps, sems,
 ):
-    start = at_ref[3] * 2048
+    core, start = at_ref[2], at_ref[3] * 2048
     gain = gain_ref[...]
     copies = []
     for part, ref in enumerate((own_hbm, beside_hbm)):
         for i in range(4):
-            rows = slice(i * 64, i * 64 + 64)
+            rows = pl.ds(i * 64, 64)
             copies.append(pltpu.make_async_copy(ref.at[rows], tokens.at[part, rows], sems.at[part, i]))
+    copies.append(pltpu.make_async_copy(own_taps, taps.at[0], sems.at[2, 0]))
+    copies.append(pltpu.make_async_copy(got_taps, taps.at[1], sems.at[2, 1]))
     for copy in copies:
         copy.start()
+
+    blocks = []
+    for plane in range(2):
+        for y in range(4):
+            block = near_ref[y, 1536 + plane * 32 : 1568 + plane * 32, :].astype(F32)
+            blocks.append(jnp.concatenate([block[v * 8 : v * 8 + 8] for v in range(4)], axis=1))
+    terms = mm(jnp.concatenate(blocks, axis=0).astype(BF16), unembed_ref[...])
+    for j in range(8):
+        parts = [terms[j * 8 : j * 8 + 8, v * 128 : v * 128 + 128] for v in range(4)]
+        terms_ref[j] = jnp.concatenate(parts, axis=0).astype(BF16)
+
     for part in range(2):
         for i in range(4):
             copies[part * 4 + i].wait()
@@ -183,18 +215,10 @@
                 right = [weight_block(near_ref, y, x * 384), weight_block(near_ref, y, x * 384 + 384)]
                 total += mm(left, jnp.concatenate(right, axis=0))
         out_ref[part] = total
-
-
-def product_kernel(rows_ref, unembed_ref, out_ref):
-    blocks = []
-    for z in range(2):
-        for y in range(4):
-            block = rows_ref[y, 1536 + z * 32 : 1568 + z * 32, :].astype(F32)
-            blocks.append(jnp.concatenate([block[v * 8 : v * 8 + 8] for v in range(4)], axis=1))
-    terms = mm(jnp.concatenate(blocks, axis=0).astype(BF16), unembed_ref[...])
-    for j in range(8):
-        parts = [terms[j * 8 : j * 8 + 8, v * 128 : v * 128 + 128] for v in range(4)]
-        out_ref[j] = jnp.concatenate(parts, axis=0).astype(BF16)
+    half = pl.ds(pl.multiple_of(core * 128, 128), 128)
+    for part in range(2):
+        copies[8 + part].wait()
+        put_pieces(pieces_ref, 0, core if part == 0 else 1 - core, taps[part, :, half].astype(F32))
 
 
 def put_pieces(ref, row, place, block):
@@ -205,26 +229,31 @@
         ref[p, pl.ds(pl.multiple_of(row + place * 16, 16), 16), :] = rows
 
 
-def proj_kernel(at_ref, gained_ref, scale_ref, near_ref, own_taps, got_taps, f0, f1, f2, f3, sig_ref, gate_ref):
+def proj_kernel(at_ref, gained_ref, scale_ref, near_ref, pieces_ref, f0, f1, f2, f3, sig_ref, gate_ref, fars, sems):
     y_at, x_at, core = at_ref[0], at_ref[1], at_ref[2]
     start = 2048 - at_ref[3] * 2048
-    half = pl.ds(pl.multiple_of(core * 128, 128), 128)
+    copies = [pltpu.make_async_copy(f, fars.at[k], sems.at[k]) for k, f in enumerate((f0, f1, f2, f3))]
+    for copy in copies:
+        copy.start()
     for part in range(2):
         total = near_ref[part]
-        for step, ref in enumerate((f0, f1, f2, f3)):
+        for step in range(4):
+            if part == 0:
+                copies[step].wait()
             x = lax.rem(x_at + 4 - step, 4)
             for k in (0, 2):
                 starts = [start + (lax.rem(y_at + 4 - j, 4) * 4 + x) * 128 for j in (k, k + 1)]
                 left = [gained_ref[part, :, pl.ds(pl.multiple_of(at, 128), 128)] for at in starts]
-                right = [weight_block(ref, k, 0), weight_block(ref, k + 1, 0)]
+                right = [weight_block(fars.at[step], k, 0), weight_block(fars.at[step], k + 1, 0)]
                 total += mm(jnp.concatenate(left, axis=1), jnp.concatenate(right, axis=0))
         scale = scale_ref[part]
         proj = (total * jnp.concatenate([scale, scale, scale], axis=1)).astype(BF16).astype(F32)
         place = core if part == 0 else 1 - core
         put_pieces(sig_ref, 0, place, proj[:, 128:256] * proj[:, 256:])
-        put_pieces(sig_ref, 32, place, (own_taps if part == 0 else got_taps)[:, half].astype(F32))
         gate_ref[place, 0] = proj[:128, :128].T.astype(BF16)
         gate_ref[place, 1] = proj[128:, :128].T.astype(BF16)
+    for p in range(16):
+        sig_ref[p, 32:, :] = pieces_ref[p]
 
 
 def mix_kernel(core_ref, got_ref, keep_ref, other_ref, base_ref, out_ref):
@@ -246,12 +275,14 @@
         out_ref[rb * 128 : rb * 128 + 128, :] = total.astype(BF16)
 
 
-def call(kernel, outs, specs, scratch, flops, args, mib=8):
+def call(kernel, outs, specs, scratch, flops, args, mib=8, out_specs=None):
+    if out_specs is None:
+        out_specs = jax.tree.map(lambda _: pl.BlockSpec(memory_space=pltpu.VMEM), outs)
     return pl.pallas_call(
         kernel,
         out_shape=outs,
         in_specs=specs,
-        out_specs=jax.tree.map(lambda _: pl.BlockSpec(memory_space=pltpu.VMEM), outs),
+        out_specs=out_specs,
         scratch_shapes=scratch,
         compiler_params=pltpu.CompilerParams(vmem_limit_bytes=mib * 2**20),
         cost_estimate=pl.CostEstimate(flops=flops, bytes_accessed=4 * 2**20, transcendentals=0),
@@ -296,13 +327,15 @@
 
     core_at = core.reshape(1).astype(jnp.int32)
     w_in = w_in.transpose(1, 0, 2)
+    keep = lax.dynamic_slice_in_dim(w_in, core * 128, 128, 2)
+    rows = w_out.reshape(4, 8, 4, 128).transpose(0, 2, 1, 3).reshape(128, 128)
     first = call(
         first_kernel,
         shape((512, 128), BF16),
         [SCALARS] + whole(3),
         [],
         10**5,
-        (core_at, w_in, lax.ppermute(w_in, "ctx", PERM_CORE), w_out),
+        (core_at, keep, lax.ppermute(w_in, "ctx", PERM_CORE), rows),
     )
     near = call(copies_kernel, shape((4, 384, 128), BF16), whole(1), [], 10**10, (first,))
     near, tokens = lax.optimization_barrier((near, tokens_in))
@@ -310,37 +343,50 @@
     near = lax.all_to_all(near, "ctx", 0, 0, axis_index_groups=GROUPS_X, tiled=True)
     far = lax.ppermute(first, "ctx", PERM_Z)
 
-    rows = by_position(first[384:].reshape(4, 32, 128), far[384:].reshape(4, 32, 128), z)
-    far = far[:384]
-    far = jnp.stack([far] + [lax.ppermute(far, "ctx", PERM_Y[k]) for k in (1, 2, 3)])
-    near, far, rows, taps = lax.optimization_barrier((near, far, rows, long_filter))
-
-    near = jnp.broadcast_to(near.reshape(1, 1536, 128), (4, 1536, 128))
-    near = jnp.concatenate([near, rows[0], rows[1]], axis=1)
+    along = far[:384]
+    along = jnp.stack([along] + [lax.ppermute(along, "ctx", PERM_Y[k]) for k in (1, 2, 3)])
+    near, along, far, taps = lax.optimization_barrier((near, along, far, long_filter))
+
+    near = call(
+        spread_kernel,
+        shape((4, 1600, 128), BF16),
+        [SCALARS] + whole(3),
+        [pltpu.SemaphoreType.DMA((4, 3))],
+        10**5,
+        (z_at, near.reshape(1536, 128), first, far),
+        out_specs=IN_HBM,
+    )
     near = lax.all_to_all(near, "ctx", 0, 0, axis_index_groups=GROUPS_Y, tiled=True)
+    far = along
     fars = [far] + [lax.ppermute(far, "ctx", PERM_X[k]) for k in (1, 2, 3)]
     taps_got = lax.ppermute(taps, "ctx", PERM_CORE)
 
     at = jnp.stack([(ctx // 8) % 4, (ctx // 2) % 4, core, z]).astype(jnp.int32)
-    gained, scale, sums = call(
+    gained, scale, sums, terms, pieces = call(
         near_kernel,
-        (shape((2, 256, 4096), BF16), shape((2, 256, 128), F32), shape((2, 256, 384), F32)),
-        [SCALARS] + [pl.BlockSpec(memory_space=pl.ANY)] * 2 + whole(2),
-        [pltpu.VMEM((2, 256, 4096), BF16), pltpu.SemaphoreType.DMA((2, 4))],
+        (
+            shape((2, 256, 4096), BF16),
+            shape((2, 256, 128), F32),
+            shape((2, 256, 384), F32),
+            shape((8, 32, 128), BF16),
+            shape((16, 32, 128), BF16),
+        ),
+        [SCALARS, IN_HBM, IN_HBM] + whole(1) + [IN_HBM, IN_HBM] + whole(2),
+        [pltpu.VMEM((2, 256, 4096), BF16), pltpu.VMEM((2, 256, 256), BF16), pltpu.SemaphoreType.DMA((3, 4))],
         8 * 10**8,
-        (at, tokens_in, beside, pre_gain.reshape(1, 4096), near),
+        (at, tokens_in, beside, pre_gain.reshape(1, 4096), taps, taps_got, near, w_unembed),
+        mib=12,
     )
     signal, gate = call(
         proj_kernel,
         (shape((16, 64, 128), BF16), shape((2, 2, 128, 128), BF16)),
-        [SCALARS] + whole(9),
-        [],
+        [SCALARS] + whole(4) + [IN_HBM] * 4,
+        [pltpu.VMEM((4, 4, 384, 128), BF16), pltpu.SemaphoreType.DMA((4,))],
         8 * 10**8,
-        (at, gained, scale, sums, taps, taps_got, *fars),
+        (at, gained, scale, sums, pieces, *fars),
     )
     got = lax.all_to_all(signal, "ctx", 0, 0, axis_index_groups=GROUPS_CORE, tiled=True)
     before = lax.ppermute(got, "ctx", PERM_Z_UP)
-    terms = call(product_kernel, shape((8, 32, 128), BF16), whole(2), [], 4 * 10**7, (near, w_unembed))
     terms, _ = lax.optimization_barrier((terms, got))
     terms = lax.all_to_all(terms, "tp", 0, 0, tiled=True)
     gate_keep = lax.dynamic_index_in_dim(gate, core, 0, False)
@@ -372,9 +418,9 @@
     vocab_index = lax.broadcasted_iota(jnp.int32, (64, 512), 1)
     picked = jnp.sum(jnp.where(vocab_index == ids[:, None], logits, 0.0), axis=1)
     scores = (picked - log_total) * mask.astype(F32)
-    scores = jnp.broadcast_to(scores[None, :], (4, 64))
+    scores = jnp.broadcast_to(scores[None, None, :], (4, 1, 64))
     scores = lax.all_to_all(scores, "tp", 0, 0, axis_index_groups=GROUPS_TP, tiled=True)
-    return scores.reshape(256)
+    return call(last_kernel, shape((1, 256), F32), whole(1), [], 10**3, (scores,)).reshape(256)
 
 
 def solution(mesh):

time: 179 us -> 178 us (level)
  starting transfers between devices: 81.4 us -> 87.5 us
  local copies, waits for them, and re-layouts: 6.48 us -> 1.73 us
  Pallas kernels: 11.6 us -> 14.7 us
  waiting for transfers between devices: 41.3 us -> 38.4 us
  other arithmetic: 2.52 us -> 0.57 us
    ppermute x1, starting transfers between devices: 7.89 us -> 12.1 us  [per_device(): before = lax.ppermute(got, 'ctx', PERM_Z_UP)]
    unnamed x30 -> x16, local copies, waits for them, and re-layouts: 4.98 us -> 0.8 us
    pallas_call x9 -> x10, Pallas kernels: 11.6 us -> 14.7 us  [call(): pl.pallas_call(kernel, out_shape=outs, in_specs=specs, out_specs=out_spec...]
    all_to_all x1, waiting for transfers between devices: 9.9 us -> 7.31 us  [per_device(): lax.all_to_all(near, 'ctx', 0, 0, axis_index_groups=GROUPS_Y, tiled=True)]
  transfers between devices with their start and end apart: 17 -> 17, of which waited for: 7 -> 7; matrix products, arithmetic and copies ran while one was open for 2% -> 1% of each run, Pallas kernels for 5% -> 5%
where the time goes in v16:
time: 178 us; the launch traced here: 177 us
  starting transfers between devices  87.5 us (49%)
  waiting for transfers between devices  38.4 us (22%)
  blocking collectives  32.2 us (18%)
  Pallas kernels  14.7 us (8%)
    ppermute x1, starting transfers between devices, per_device(): far = lax.ppermute(first, 'ctx', PERM_Z)  15.7 us
    pallas_call x10, Pallas kernels, call(): pl.pallas_call(kernel, out_shape=outs, in_specs=specs, out_specs=out_spec...  14.7 us
    all_to_all x1, blocking collectives, per_device(): lax.all_to_all(logits.reshape(4, 64, 512), 'tp', 0, 0, axis_index_groups=...  12.7 us
    all_to_all x1, starting transfers between devices, per_device(): terms = lax.all_to_all(terms, 'tp', 0, 0, tiled=True)  12.5 us
    ppermute x1, starting transfers between devices, per_device(): before = lax.ppermute(got, 'ctx', PERM_Z_UP)  12.1 us
    all_to_all x1, waiting for transfers between devices, per_device(): terms = lax.all_to_all(terms, 'tp', 0, 0, tiled=True)  12 us
    all_to_all x1, blocking collectives, per_device(): lax.all_to_all(signal, 'ctx', 0, 0, axis_index_groups=GROUPS_CORE, tiled=...  11.7 us
    ppermute x3, starting transfers between devices, per_device(): lax.ppermute(along, 'ctx', PERM_Y[k])  11.6 us
  transfers between devices with their start and end apart: 17, of which 7 were waited for; matrix products, arithmetic and copies ran while one was open for 1% of the time, Pallas kernels for 5%

profile of v16, /device:TPU:6, one launch (start us, length us, event | category | flops | bytes accessed | tf_op | source)
XLA Modules:
  0.0 176.8 jit_solution(16523004639884400052)
XLA Ops:
  0.0 1.9 %collective-permute-start = (bf16[3,64,256]{2,1,0:T(8,128)(2,1)}, bf16[3,64,256]{2,1,0:T(8,128)(2,1)S(1)}, u32[]{:S(2)}, u32[]{:S(2)}) collective-permute-start(bf16[3,64,256]{2,1,0:T(8,128)(2,1)} %bitcast.31), channel_id=1, source_target_pairs={{0,8},{8,0},{16,24},{24,16},{32,40},{40,32},{48,56},{56,48},{64,72... | collective-permute-start | bytes 294920 | tf_op jit(solution)/shard_map/ppermute | solution.py:338
  5.0 2.1 %collective-permute-start.1 = (bf16[256,4096]{1,0:T(8,128)(2,1)}, bf16[256,4096]{1,0:T(8,128)(2,1)}, u32[]{:S(2)}, u32[]{:S(2)}) collective-permute-start(bf16[256,4096]{1,0:T(8,128)(2,1)} %own_hbm.1), channel_id=1, source_target_pairs={{0,8},{8,0},{16,24},{24,16},{32,40},{40,32},{48,56},{56,48},{64,72... | collective-permute-start | bytes 6291464 | tf_op jit(solution)/shard_map/ppermute | solution.py:342
  7.0 15.7 %collective-permute-start.2 = (bf16[512,128]{1,0:T(8,128)(2,1)S(1)}, bf16[512,128]{1,0:T(8,128)(2,1)S(1)}, u32[]{:S(2)}, u32[]{:S(2)}) collective-permute-start(bf16[512,128]{1,0:T(8,128)(2,1)S(1)} %shard_map.118.first_ref), channel_id=1, source_target_pairs={{0,256},{8,264},{16,272},{24,280},{32,288},{40,296},{48,304},{56,3... | collective-permute-start | bytes 393224 | tf_op jit(solution)/shard_map/ppermute | solution.py:344
  22.8 4.8 %all-to-all-start = ((bf16[4,384,128]{2,1,0:T(8,128)(2,1)}), bf16[4,384,128]{2,1,0:T(8,128)(2,1)S(1)}, u32[]{:S(2)}, u32[]{:S(2)}) async-start(bf16[4,384,128]{2,1,0:T(8,128)(2,1)} %shard_map.119), calls=%async_computation | async-start | bytes 786432 | tf_op jit(solution)/shard_map/all_to_all | solution.py:343
  27.6 3.5 %collective-permute-start.3 = (bf16[384,128]{1,0:T(8,128)(2,1)S(1)}, bf16[384,128]{1,0:T(8,128)(2,1)S(1)}, u32[]{:S(2)}, u32[]{:S(2)}) collective-permute-start(bf16[384,128]{1,0:T(8,128)(2,1)S(1)} %get-tuple-element.42), channel_id=1, source_target_pairs={{0,64},{8,72},{16,80},{24,88},{32,96},{40,104},{48,112},{56,120},{... | collective-permute-start | bytes 294920 | tf_op jit(solution)/shard_map/ppermute | solution.py:347
  31.1 4.8 %collective-permute-start.4 = (bf16[384,128]{1,0:T(8,128)(2,1)S(1)}, bf16[384,128]{1,0:T(8,128)(2,1)S(1)}, u32[]{:S(2)}, u32[]{:S(2)}) collective-permute-start(bf16[384,128]{1,0:T(8,128)(2,1)S(1)} %get-tuple-element.42), channel_id=1, source_target_pairs={{0,128},{8,136},{16,144},{24,152},{32,160},{40,168},{48,176},{56,1... | collective-permute-start | bytes 294920 | tf_op jit(solution)/shard_map/ppermute | solution.py:347
  35.9 3.3 %collective-permute-start.5 = (bf16[384,128]{1,0:T(8,128)(2,1)S(1)}, bf16[384,128]{1,0:T(8,128)(2,1)S(1)}, u32[]{:S(2)}, u32[]{:S(2)}) collective-permute-start(bf16[384,128]{1,0:T(8,128)(2,1)S(1)} %get-tuple-element.42), channel_id=1, source_target_pairs={{0,192},{8,200},{16,208},{24,216},{32,224},{40,232},{48,240},{56,2... | collective-permute-start | bytes 294920 | tf_op jit(solution)/shard_map/ppermute | solution.py:347
  39.2 3.2 %collective-permute-done.5 = bf16[384,128]{1,0:T(8,128)(2,1)S(1)} collective-permute-done((bf16[384,128]{1,0:T(8,128)(2,1)S(1)}, bf16[384,128]{1,0:T(8,128)(2,1)S(1)}, u32[]{:S(2)}, u32[]{:S(2)}) %collective-permute-start.5) | collective-permute-done | bytes 98336 | tf_op jit(solution)/shard_map/ppermute | solution.py:347
  42.5 1.3 shard_map.120
  43.8 4.0 %all-to-all-start.1 = ((bf16[4,1600,128]{2,1,0:T(8,128)(2,1)}), bf16[4,1600,128]{2,1,0:T(8,128)(2,1)S(1)}, u32[]{:S(2)}, u32[]{:S(2)}) async-start(bf16[4,1600,128]{2,1,0:T(8,128)(2,1)} %shard_map.120), calls=%async_computation.1 | async-start | bytes 3276800 | tf_op jit(solution)/shard_map/all_to_all | solution.py:359
  47.8 1.9 %collective-permute-start.7 = (bf16[4,384,128]{2,1,0:T(8,128)(2,1)S(1)}, bf16[4,384,128]{2,1,0:T(8,128)(2,1)S(1)}, u32[]{:S(2)}, u32[]{:S(2)}) collective-permute-start(bf16[4,384,128]{2,1,0:T(8,128)(2,1)S(1)} %pad_maximum_fusion.f0), channel_id=1, source_target_pairs={{0,16},{8,24},{16,32},{24,40},{32,48},{40,56},{48,0},{56,8},{64,80... | collective-permute-start | bytes 1179656 | tf_op jit(solution)/shard_map/ppermute | solution.py:361
  49.7 4.8 %collective-permute-start.8 = (bf16[4,384,128]{2,1,0:T(8,128)(2,1)S(1)}, bf16[4,384,128]{2,1,0:T(8,128)(2,1)S(1)}, u32[]{:S(2)}, u32[]{:S(2)}) collective-permute-start(bf16[4,384,128]{2,1,0:T(8,128)(2,1)S(1)} %pad_maximum_fusion.f0), channel_id=1, source_target_pairs={{0,32},{8,40},{16,48},{24,56},{32,0},{40,8},{48,16},{56,24},{64,96... | collective-permute-start | bytes 1179656 | tf_op jit(solution)/shard_map/ppermute | solution.py:361
  54.5 1.9 %collective-permute-start.9 = (bf16[4,384,128]{2,1,0:T(8,128)(2,1)S(1)}, bf16[4,384,128]{2,1,0:T(8,128)(2,1)}, u32[]{:S(2)}, u32[]{:S(2)}) collective-permute-start(bf16[4,384,128]{2,1,0:T(8,128)(2,1)S(1)} %pad_maximum_fusion.f0), channel_id=1, source_target_pairs={{0,48},{8,56},{16,0},{24,8},{32,16},{40,24},{48,32},{56,40},{64,11... | collective-permute-start | bytes 1179656 | tf_op jit(solution)/shard_map/ppermute | solution.py:361
  56.4 1.9 %collective-permute-start.6 = (bf16[256,256]{1,0:T(8,128)(2,1)S(1)}, bf16[256,256]{1,0:T(8,128)(2,1)}, u32[]{:S(2)}, u32[]{:S(2)}) collective-permute-start(bf16[256,256]{1,0:T(8,128)(2,1)S(1)} %copy-done.3), channel_id=1, source_target_pairs={{0,8},{8,0},{16,24},{24,16},{32,40},{40,32},{48,56},{56,48},{64,72... | collective-permute-start | bytes 393224 | tf_op jit(solution)/shard_map/ppermute | solution.py:362
  58.5 1.3 collective-permute-done.6.got_taps
  59.8 7.3 %all-to-all-done.1.near_ref = bf16[4,1600,128]{2,1,0:T(8,128)(2,1)S(1)} async-done(((bf16[4,1600,128]{2,1,0:T(8,128)(2,1)}), bf16[4,1600,128]{2,1,0:T(8,128)(2,1)S(1)}, u32[]{:S(2)}, u32[]{:S(2)}) %all-to-all-start.1) | async-done | bytes 1638432 | tf_op jit(solution)/shard_map/all_to_all | solution.py:359
  67.1 5.2 %shard_map.121 = (bf16[2,256,4096]{2,1,0:T(8,128)(2,1)S(1)}, f32[2,256,128]{2,1,0:T(8,128)S(1)}, f32[2,256,384]{2,1,0:T(8,128)S(1)}, bf16[8,32,128]{2,1,0:T(8,128)(2,1)}, bf16[16,32,128]{2,1,0:T(8,128)(2,1)S(1)}) custom-call(s32[4]{0:T(128)S(1)} %pad_add_fusion.at_ref, bf16[256,4096]{1,0:T(8,128)(2,1)} %own_hbm.1, ...), custom_call_target="tpu_custom_call" | custom-call | flops 800000000 | bytes 4194304 | tf_op jit(solution)/shard_map/pallas_call | solution.py:281
  72.4 3.1 %shard_map.122 = (bf16[16,64,128]{2,1,0:T(8,128)(2,1)S(1)}, bf16[2,2,128,128]{3,2,1,0:T(8,128)(2,1)S(1)}) custom-call(s32[4]{0:T(128)S(1)} %pad_add_fusion.at_ref, bf16[2,256,4096]{2,1,0:T(8,128)(2,1)S(1)} %get-tuple-element.26.gained_ref, f32[2,256,128]{2,1,0:T(8,128)S(1)} %get-tuple-element.27.scale_ref, f32[2,256,384]{2,1,0:T(8,128)S(1)} %get-tuple-element.28.near_ref, ...), custom_call_target="tpu_custom_call" | custom-call | flops 800000000 | bytes 4194304 | tf_op jit(solution)/shard_map/pallas_call | solution.py:281
  75.5 11.7 %all_to_all.35.got_ref = bf16[16,64,128]{2,1,0:T(8,128)(2,1)S(1)} all-to-all(bf16[16,64,128]{2,1,0:T(8,128)(2,1)S(1)} %get-tuple-element.31), channel_id=1, replica_groups={{0,16,32,48,64,80,96,112,128,144,160,176,192,208,224,240},{8,24,40,56,7..., dimensions={0} | all-to-all | bytes 524288 | tf_op jit(solution)/shard_map/all_to_all | solution.py:388
  87.1 12.1 %collective-permute-start.10 = (bf16[16,64,128]{2,1,0:T(8,128)(2,1)S(1)}, bf16[16,64,128]{2,1,0:T(8,128)(2,1)S(1)}, u32[]{:S(2)}, u32[]{:S(2)}) collective-permute-start(bf16[16,64,128]{2,1,0:T(8,128)(2,1)S(1)} %all_to_all.35.got_ref), channel_id=1, source_target_pairs={{0,256},{8,264},{16,272},{24,280},{32,288},{40,296},{48,304},{56,3... | collective-permute-start | bytes 786440 | tf_op jit(solution)/shard_map/ppermute | solution.py:389
  99.3 12.5 %all-to-all-start.3 = ((bf16[8,32,128]{2,1,0:T(8,128)(2,1)}), bf16[8,32,128]{2,1,0:T(8,128)(2,1)S(1)}, u32[]{:S(2)}, u32[]{:S(2)}) async-start(bf16[8,32,128]{2,1,0:T(8,128)(2,1)} %get-tuple-element.35), calls=%async_computation.3 | async-start | bytes 131072 | tf_op jit(solution)/shard_map/all_to_all | solution.py:391
  111.7 1.0 shard_map.123
  112.7 1.6 shard_map.124.conv_ref
  114.3 12.0 %all-to-all-done.3.terms_ref = bf16[8,32,128]{2,1,0:T(8,128)(2,1)S(1)} async-done(((bf16[8,32,128]{2,1,0:T(8,128)(2,1)}), bf16[8,32,128]{2,1,0:T(8,128)(2,1)S(1)}, u32[]{:S(2)}, u32[]{:S(2)}) %all-to-all-start.3) | async-done | bytes 65568 | tf_op jit(solution)/shard_map/all_to_all | solution.py:391
  127.1 6.2 %all-to-all-start.4 = ((bf16[32,48,128]{2,1,0:T(8,128)(2,1)}), bf16[32,48,128]{2,1,0:T(8,128)(2,1)S(1)}, u32[]{:S(2)}, u32[]{:S(2)}) async-start(bf16[32,48,128]{2,1,0:T(8,128)(2,1)} %shard_map.125), calls=%async_computation.4 | async-start | bytes 786432 | tf_op jit(solution)/shard_map/all_to_all | solution.py:397
  133.3 2.1 %collective-permute-start.11 = (bf16[2,128,128]{2,1,0:T(8,128)(2,1)S(1)}, bf16[2,128,128]{2,1,0:T(8,128)(2,1)S(1)}, u32[]{:S(2)}, u32[]{:S(2)}) collective-permute-start(bf16[2,128,128]{2,1,0:T(8,128)(2,1)S(1)} %get-tuple-element.39), channel_id=1, source_target_pairs={{0,8},{8,0},{16,24},{24,16},{32,40},{40,32},{48,56},{56,48},{64,72... | collective-permute-start | bytes 196616 | tf_op jit(solution)/shard_map/ppermute | solution.py:393
  135.4 1.2 fusion.base_ref
  136.7 4.7 %all-to-all-done.4.got_ref = bf16[32,48,128]{2,1,0:T(8,128)(2,1)S(1)} async-done(((bf16[32,48,128]{2,1,0:T(8,128)(2,1)}), bf16[32,48,128]{2,1,0:T(8,128)(2,1)S(1)}, u32[]{:S(2)}, u32[]{:S(2)}) %all-to-all-start.4) | async-done | bytes 393248 | tf_op jit(solution)/shard_map/all_to_all | solution.py:397
  141.8 12.7 %all_to_all.36 = bf16[4,64,512]{2,1,0:T(8,128)(2,1)S(1)} all-to-all(bf16[4,64,512]{2,1,0:T(8,128)(2,1)S(1)} %bitcast.26), channel_id=1, replica_groups={{0,1,2,3},{4,5,6,7},{8,9,10,11},{12,13,14,15},{16,17,18,19},{20,21,22,2..., dimensions={0} | all-to-all | bytes 524288 | tf_op jit(solution)/shard_map/all_to_all | solution.py:409
  154.5 4.1 %collective-permute-start.12 = (bf16[64,512]{1,0:T(8,128)(2,1)S(1)}, bf16[64,512]{1,0:T(8,128)(2,1)S(1)}, u32[]{:S(2)}, u32[]{:S(2)}) collective-permute-start(bf16[64,512]{1,0:T(8,128)(2,1)S(1)} %reduce_sum.30), channel_id=1, source_target_pairs={{0,4},{1,5},{2,6},{3,7},{4,0},{5,1},{6,2},{7,3},{8,12},{9,13},{10,... | collective-permute-start | bytes 196616 | tf_op jit(solution)/shard_map/ppermute | solution.py:411
  158.7 9.2 %collective-permute-done.12 = bf16[64,512]{1,0:T(8,128)(2,1)S(1)} collective-permute-done((bf16[64,512]{1,0:T(8,128)(2,1)S(1)}, bf16[64,512]{1,0:T(8,128)(2,1)S(1)}, u32[]{:S(2)}, u32[]{:S(2)}) %collective-permute-start.12) | collective-permute-done | bytes 65568 | tf_op jit(solution)/shard_map/ppermute | solution.py:411
  168.2 7.9 %all_to_all.37.scores_ref = f32[4,1,64]{2,1,0:T(1,128)S(1)} all-to-all(f32[4,1,64]{2,1,0:T(1,128)S(1)} %broadcast_in_dim.7), channel_id=1, replica_groups={{0,1,2,3},{4,5,6,7},{8,9,10,11},{12,13,14,15},{16,17,18,19},{20,21,22,2..., dimensions={0} | all-to-all | bytes 2048 | tf_op jit(solution)/shard_map/all_to_all | solution.py:422
  (44 shorter events, 5.6 us)
Async XLA Ops:
  0.0 3.4 %collective-permute-start = (bf16[3,64,256]{2,1,0:T(8,128)(2,1)}, bf16[3,64,256]{2,1,0:T(8,128)(2,1)S(1)}, u32[]{:S(2)}, u32[]{:S(2)}) collective-permute-start(bf16[3,64,256]{2,1,0:T(8,128)(2,1)} %bitcast.31), channel_id=1, source_target_pairs={{0,8},{8,0},{16,24},{24,16},{32,40},{40,32},{48,56},{56,48},{64,72... | collective-permute-start | bytes 294920 | tf_op jit(solution)/shard_map/ppermute | solution.py:338
  3.4 0.8 copy-start.4
  5.0 62.2 %collective-permute-start.1 = (bf16[256,4096]{1,0:T(8,128)(2,1)}, bf16[256,4096]{1,0:T(8,128)(2,1)}, u32[]{:S(2)}, u32[]{:S(2)}) collective-permute-start(bf16[256,4096]{1,0:T(8,128)(2,1)} %own_hbm.1), channel_id=1, source_target_pairs={{0,8},{8,0},{16,24},{24,16},{32,40},{40,32},{48,56},{56,48},{64,72... | collective-permute-start | bytes 6291464 | tf_op jit(solution)/shard_map/ppermute | solution.py:342
  7.0 20.5 %collective-permute-start.2 = (bf16[512,128]{1,0:T(8,128)(2,1)S(1)}, bf16[512,128]{1,0:T(8,128)(2,1)S(1)}, u32[]{:S(2)}, u32[]{:S(2)}) collective-permute-start(bf16[512,128]{1,0:T(8,128)(2,1)S(1)} %shard_map.118.first_ref), channel_id=1, source_target_pairs={{0,256},{8,264},{16,272},{24,280},{32,288},{40,296},{48,304},{56,3... | collective-permute-start | bytes 393224 | tf_op jit(solution)/shard_map/ppermute | solution.py:344
  22.8 19.7 %all-to-all-start = ((bf16[4,384,128]{2,1,0:T(8,128)(2,1)}), bf16[4,384,128]{2,1,0:T(8,128)(2,1)S(1)}, u32[]{:S(2)}, u32[]{:S(2)}) async-start(bf16[4,384,128]{2,1,0:T(8,128)(2,1)} %shard_map.119), calls=%async_computation | async-start | bytes 786432 | tf_op jit(solution)/shard_map/all_to_all | solution.py:343
  27.6 11.6 %collective-permute-start.3 = (bf16[384,128]{1,0:T(8,128)(2,1)S(1)}, bf16[384,128]{1,0:T(8,128)(2,1)S(1)}, u32[]{:S(2)}, u32[]{:S(2)}) collective-permute-start(bf16[384,128]{1,0:T(8,128)(2,1)S(1)} %get-tuple-element.42), channel_id=1, source_target_pairs={{0,64},{8,72},{16,80},{24,88},{32,96},{40,104},{48,112},{56,120},{... | collective-permute-start | bytes 294920 | tf_op jit(solution)/shard_map/ppermute | solution.py:347
  31.1 8.1 %collective-permute-start.4 = (bf16[384,128]{1,0:T(8,128)(2,1)S(1)}, bf16[384,128]{1,0:T(8,128)(2,1)S(1)}, u32[]{:S(2)}, u32[]{:S(2)}) collective-permute-start(bf16[384,128]{1,0:T(8,128)(2,1)S(1)} %get-tuple-element.42), channel_id=1, source_target_pairs={{0,128},{8,136},{16,144},{24,152},{32,160},{40,168},{48,176},{56,1... | collective-permute-start | bytes 294920 | tf_op jit(solution)/shard_map/ppermute | solution.py:347
  35.9 6.5 %collective-permute-start.5 = (bf16[384,128]{1,0:T(8,128)(2,1)S(1)}, bf16[384,128]{1,0:T(8,128)(2,1)S(1)}, u32[]{:S(2)}, u32[]{:S(2)}) collective-permute-start(bf16[384,128]{1,0:T(8,128)(2,1)S(1)} %get-tuple-element.42), channel_id=1, source_target_pairs={{0,192},{8,200},{16,208},{24,216},{32,224},{40,232},{48,240},{56,2... | collective-permute-start | bytes 294920 | tf_op jit(solution)/shard_map/ppermute | solution.py:347
  43.7 12.7 %copy-start.3 = (bf16[256,256]{1,0:T(8,128)(2,1)S(1)}, bf16[256,256]{1,0:T(8,128)(2,1)}, u32[]{:S(2)}) copy-start(bf16[256,256]{1,0:T(8,128)(2,1)} %own_taps) | copy-start | bytes 393220
  43.8 14.7 %copy-start.5 = (bf16[4096]{0:T(1024)(128)(2,1)S(1)}, bf16[4096]{0:T(1024)(128)(2,1)}, u32[]{:S(2)}) copy-start(bf16[4096]{0:T(1024)(128)(2,1)} %param.13) | copy-start | bytes 24580
  43.8 23.4 %copy-start = (bf16[512,512]{1,0:T(8,128)(2,1)S(1)}, bf16[512,512]{1,0:T(8,128)(2,1)}, u32[]{:S(2)}) copy-start(bf16[512,512]{1,0:T(8,128)(2,1)} %unembed_ref.1) | copy-start | bytes 1572868
  43.8 23.3 %all-to-all-start.1 = ((bf16[4,1600,128]{2,1,0:T(8,128)(2,1)}), bf16[4,1600,128]{2,1,0:T(8,128)(2,1)S(1)}, u32[]{:S(2)}, u32[]{:S(2)}) async-start(bf16[4,1600,128]{2,1,0:T(8,128)(2,1)} %shard_map.120), calls=%async_computation.1 | async-start | bytes 3276800 | tf_op jit(solution)/shard_map/all_to_all | solution.py:359
  47.8 24.6 %collective-permute-start.7 = (bf16[4,384,128]{2,1,0:T(8,128)(2,1)S(1)}, bf16[4,384,128]{2,1,0:T(8,128)(2,1)S(1)}, u32[]{:S(2)}, u32[]{:S(2)}) collective-permute-start(bf16[4,384,128]{2,1,0:T(8,128)(2,1)S(1)} %pad_maximum_fusion.f0), channel_id=1, source_target_pairs={{0,16},{8,24},{16,32},{24,40},{32,48},{40,56},{48,0},{56,8},{64,80... | collective-permute-start | bytes 1179656 | tf_op jit(solution)/shard_map/ppermute | solution.py:361
  49.7 22.6 %collective-permute-start.8 = (bf16[4,384,128]{2,1,0:T(8,128)(2,1)S(1)}, bf16[4,384,128]{2,1,0:T(8,128)(2,1)S(1)}, u32[]{:S(2)}, u32[]{:S(2)}) collective-permute-start(bf16[4,384,128]{2,1,0:T(8,128)(2,1)S(1)} %pad_maximum_fusion.f0), channel_id=1, source_target_pairs={{0,32},{8,40},{16,48},{24,56},{32,0},{40,8},{48,16},{56,24},{64,96... | collective-permute-start | bytes 1179656 | tf_op jit(solution)/shard_map/ppermute | solution.py:361
  54.5 17.8 %collective-permute-start.9 = (bf16[4,384,128]{2,1,0:T(8,128)(2,1)S(1)}, bf16[4,384,128]{2,1,0:T(8,128)(2,1)}, u32[]{:S(2)}, u32[]{:S(2)}) collective-permute-start(bf16[4,384,128]{2,1,0:T(8,128)(2,1)S(1)} %pad_maximum_fusion.f0), channel_id=1, source_target_pairs={{0,48},{8,56},{16,0},{24,8},{32,16},{40,24},{48,32},{56,40},{64,11... | collective-permute-start | bytes 1179656 | tf_op jit(solution)/shard_map/ppermute | solution.py:361
  56.4 3.4 %collective-permute-start.6 = (bf16[256,256]{1,0:T(8,128)(2,1)S(1)}, bf16[256,256]{1,0:T(8,128)(2,1)}, u32[]{:S(2)}, u32[]{:S(2)}) collective-permute-start(bf16[256,256]{1,0:T(8,128)(2,1)S(1)} %copy-done.3), channel_id=1, source_target_pairs={{0,8},{8,0},{16,24},{24,16},{32,40},{40,32},{48,56},{56,48},{64,72... | collective-permute-start | bytes 393224 | tf_op jit(solution)/shard_map/ppermute | solution.py:362
  72.3 39.4 %copy-start.1 = (bf16[832,256]{1,0:T(8,128)(2,1)S(1)}, bf16[832,256]{1,0:T(8,128)(2,1)}, u32[]{:S(2)}) copy-start(bf16[832,256]{1,0:T(8,128)(2,1)} %constant.103.clone.matrices) | copy-start | bytes 1277956
  72.3 39.4 %copy-start.2 = (f32[128,256]{1,0:T(8,128)S(1)}, f32[128,256]{1,0:T(8,128)}, u32[]{:S(2)}) copy-start(f32[128,256]{1,0:T(8,128)} %constant.104.clone.twiddles) | copy-start | bytes 393220
  87.1 25.6 %collective-permute-start.10 = (bf16[16,64,128]{2,1,0:T(8,128)(2,1)S(1)}, bf16[16,64,128]{2,1,0:T(8,128)(2,1)S(1)}, u32[]{:S(2)}, u32[]{:S(2)}) collective-permute-start(bf16[16,64,128]{2,1,0:T(8,128)(2,1)S(1)} %all_to_all.35.got_ref), channel_id=1, source_target_pairs={{0,256},{8,264},{16,272},{24,280},{32,288},{40,296},{48,304},{56,3... | collective-permute-start | bytes 786440 | tf_op jit(solution)/shard_map/ppermute | solution.py:389
  99.3 27.1 %all-to-all-start.3 = ((bf16[8,32,128]{2,1,0:T(8,128)(2,1)}), bf16[8,32,128]{2,1,0:T(8,128)(2,1)S(1)}, u32[]{:S(2)}, u32[]{:S(2)}) async-start(bf16[8,32,128]{2,1,0:T(8,128)(2,1)} %get-tuple-element.35), calls=%async_computation.3 | async-start | bytes 131072 | tf_op jit(solution)/shard_map/all_to_all | solution.py:391
  127.1 31.5 %copy-start.7 = (s32[256]{0:T(256)S(1)}, s32[256]{0:T(256)}, u32[]{:S(2)}) copy-start(s32[256]{0:T(256)} %param.18) | copy-start | bytes 3076
  127.1 14.3 %all-to-all-start.4 = ((bf16[32,48,128]{2,1,0:T(8,128)(2,1)}), bf16[32,48,128]{2,1,0:T(8,128)(2,1)S(1)}, u32[]{:S(2)}, u32[]{:S(2)}) async-start(bf16[32,48,128]{2,1,0:T(8,128)(2,1)} %shard_map.125), calls=%async_computation.4 | async-start | bytes 786432 | tf_op jit(solution)/shard_map/all_to_all | solution.py:397
  133.3 34.9 %copy-start.6 = (s32[256]{0:T(256)S(1)}, s32[256]{0:T(256)}, u32[]{:S(2)}) copy-start(s32[256]{0:T(256)} %param.19) | copy-start | bytes 3076
  133.3 3.3 %collective-permute-start.11 = (bf16[2,128,128]{2,1,0:T(8,128)(2,1)S(1)}, bf16[2,128,128]{2,1,0:T(8,128)(2,1)S(1)}, u32[]{:S(2)}, u32[]{:S(2)}) collective-permute-start(bf16[2,128,128]{2,1,0:T(8,128)(2,1)S(1)} %get-tuple-element.39), channel_id=1, source_target_pairs={{0,8},{8,0},{16,24},{24,16},{32,40},{40,32},{48,56},{56,48},{64,72... | collective-permute-start | bytes 196616 | tf_op jit(solution)/shard_map/ppermute | solution.py:393
  154.5 13.4 %collective-permute-start.12 = (bf16[64,512]{1,0:T(8,128)(2,1)S(1)}, bf16[64,512]{1,0:T(8,128)(2,1)S(1)}, u32[]{:S(2)}, u32[]{:S(2)}) collective-permute-start(bf16[64,512]{1,0:T(8,128)(2,1)S(1)} %reduce_sum.30), channel_id=1, source_target_pairs={{0,4},{1,5},{2,6},{3,7},{4,0},{5,1},{6,2},{7,3},{8,12},{9,13},{10,... | collective-permute-start | bytes 196616 | tf_op jit(solution)/shard_map/ppermute | solution.py:411

commit v17 on v16

--- a/solution.py
+++ b/solution.py
@@ -89,23 +89,24 @@
         scratch[p * 32 : p * 32 + 32] = ref[p, at : at + 32].astype(F32)
 
 
-def spectra_kernel(got_ref, matrices, twiddles, signal_ref, filter_ref, scratch):
+def spectra_kernel(z_ref, got_ref, matrices, twiddles, signal_ref, low_ref, all_ref, scratch):
+    upper = z_ref[0] == 1
     rows_of(scratch, got_ref, 0)
     signal_ref[...] = spectrum(scratch, matrices, twiddles)
     rows_of(scratch, got_ref, 32)
-    filter_ref[...] = spectrum(scratch, matrices, twiddles)
-
-
-def conv_kernel(z_ref, signal_ref, filter_ref, before_ref, matrices, twiddles, out_ref, scratch):
-    upper = z_ref[0] == 1
+    high = spectrum(scratch, matrices, twiddles)
+    rows_of(scratch, got_ref, 64)
+    low = jnp.where(upper, spectrum(scratch, matrices, twiddles), high)
+    low_ref[...] = low
+    odd = lax.broadcasted_iota(jnp.int32, (1024, 256), 0) & 1
+    all_ref[...] = jnp.where(odd == 1, -low, low) + high
+
+
+def conv_kernel(z_ref, signal_ref, low_ref, all_ref, before_ref, matrices, twiddles, out_ref, scratch):
     cos_tw, sin_tw = twiddles[:, :128], twiddles[:, 128:]
-    own, high = signal_ref[...], filter_ref[...]
-    rows_of(scratch, before_ref, 0)
-    old = jnp.where(upper, spectrum(scratch, matrices, twiddles), 0.0)
-    rows_of(scratch, before_ref, 32)
-    low = jnp.where(upper, spectrum(scratch, matrices, twiddles), high)
-    odd = lax.broadcasted_iota(jnp.int32, (1024, 256), 0) & 1
-    every = jnp.where(odd == 1, -low, low) + high
+    own, low, every = signal_ref[...], low_ref[...], all_ref[...]
+    scratch[...] = before_ref[...].astype(F32)
+    old = jnp.where(z_ref[0] == 1, spectrum(scratch, matrices, twiddles), 0.0)
     own_r, own_i, old_r, old_i = own[:, :128], own[:, 128:], old[:, :128], old[:, 128:]
     low_r, low_i, all_r, all_i = low[:, :128], low[:, 128:], every[:, :128], every[:, 128:]
     real = own_r * low_r - own_i * low_i + old_r * all_r - old_i * all_i
@@ -134,14 +135,16 @@
         out_ref[d, 16:] = piece
 
 
-def first_kernel(core_ref, own_ref, got_ref, rows_ref, out_ref):
+def first_kernel(core_ref, own_ref, got_ref, rows_ref, taps_ref, out_ref):
     core = core_ref[0]
     half = pl.ds(pl.multiple_of(core * 128, 128), 128)
     for g in range(3):
         own, got = own_ref[g], got_ref[g, :, half]
         out_ref[g * 128 : g * 128 + 64] = jnp.where(core == 0, own, got)
         out_ref[g * 128 + 64 : g * 128 + 128] = jnp.where(core == 0, got, own)
-    out_ref[384:] = rows_ref[...]
+    out_ref[384:512] = rows_ref[...]
+    out_ref[512:768] = taps_ref[:, :128]
+    out_ref[768:] = taps_ref[:, 128:]
 
 
 def copies_kernel(first_ref, out_ref):
@@ -215,10 +218,11 @@
                 right = [weight_block(near_ref, y, x * 384), weight_block(near_ref, y, x * 384 + 384)]
                 total += mm(left, jnp.concatenate(right, axis=0))
         out_ref[part] = total
-    half = pl.ds(pl.multiple_of(core * 128, 128), 128)
     for part in range(2):
         copies[8 + part].wait()
-        put_pieces(pieces_ref, 0, core if part == 0 else 1 - core, taps[part, :, half].astype(F32))
+        for plane in range(2):
+            place = core if part == 0 else 1 - core
+            put_pieces(pieces_ref, plane * 32, place, taps[part, plane].astype(F32))
 
 
 def put_pieces(ref, row, place, block):
@@ -297,25 +301,26 @@
     return jnp.where(place == 0, jnp.stack([own, other]), jnp.stack([other, own]))
 
 
-def spectra(got):
+def spectra(z, got):
     return call(
         spectra_kernel,
-        (shape((1024, 256), F32), shape((1024, 256), F32)),
-        whole(3),
+        (shape((1024, 256), F32), shape((1024, 256), F32), shape((1024, 256), F32)),
+        [SCALARS] + whole(3),
         [pltpu.VMEM((512, 128), F32)],
         4 * 10**8,
-        (got, jnp.asarray(MATRICES, BF16), jnp.asarray(TWIDDLES, F32)),
-    )
-
-
-def convolve(z, signal, taps, before):
+        (z, got, jnp.asarray(MATRICES, BF16), jnp.asarray(TWIDDLES, F32)),
+        mib=16,
+    )
+
+
+def convolve(z, signal, low, every, before):
     return call(
         conv_kernel,
         shape((32, 16, 128), BF16),
-        [SCALARS] + whole(5),
+        [SCALARS] + whole(6),
         [pltpu.VMEM((512, 128), F32)],
         6 * 10**8,
-        (z, signal, taps, before, jnp.asarray(MATRICES, BF16), jnp.asarray(TWIDDLES, F32)),
+        (z, signal, low, every, before, jnp.asarray(MATRICES, BF16), jnp.asarray(TWIDDLES, F32)),
         mib=16,
     )
 
@@ -331,11 +336,11 @@
     rows = w_out.reshape(4, 8, 4, 128).transpose(0, 2, 1, 3).reshape(128, 128)
     first = call(
         first_kernel,
-        shape((512, 128), BF16),
-        [SCALARS] + whole(3),
+        shape((1024, 128), BF16),
+        [SCALARS] + whole(4),
         [],
         10**5,
-        (core_at, keep, lax.ppermute(w_in, "ctx", PERM_CORE), rows),
+        (core_at, keep, lax.ppermute(w_in, "ctx", PERM_CORE), rows, long_filter),
     )
     near = call(copies_kernel, shape((4, 384, 128), BF16), whole(1), [], 10**10, (first,))
     near, tokens = lax.optimization_barrier((near, tokens_in))
@@ -345,7 +350,7 @@
 
     along = far[:384]
     along = jnp.stack([along] + [lax.ppermute(along, "ctx", PERM_Y[k]) for k in (1, 2, 3)])
-    near, along, far, taps = lax.optimization_barrier((near, along, far, long_filter))
+    near, along, far = lax.optimization_barrier((near, along, far))
 
     near = call(
         spread_kernel,
@@ -357,9 +362,12 @@
         out_specs=IN_HBM,
     )
     near = lax.all_to_all(near, "ctx", 0, 0, axis_index_groups=GROUPS_Y, tiled=True)
+    taps = far[512:].reshape(2, 256, 128)
     far = along
     fars = [far] + [lax.ppermute(far, "ctx", PERM_X[k]) for k in (1, 2, 3)]
-    taps_got = lax.ppermute(taps, "ctx", PERM_CORE)
+    taps = jnp.stack([first[512:].reshape(2, 256, 128), taps])
+    taps_got = lax.ppermute(lax.dynamic_index_in_dim(taps, 1 - core, 1, False), "ctx", PERM_CORE)
+    taps = lax.dynamic_index_in_dim(taps, core, 1, False)
 
     at = jnp.stack([(ctx // 8) % 4, (ctx // 2) % 4, core, z]).astype(jnp.int32)
     gained, scale, sums, terms, pieces = call(
@@ -369,30 +377,30 @@
             shape((2, 256, 128), F32),
             shape((2, 256, 384), F32),
             shape((8, 32, 128), BF16),
-            shape((16, 32, 128), BF16),
+            shape((16, 64, 128), BF16),
         ),
         [SCALARS, IN_HBM, IN_HBM] + whole(1) + [IN_HBM, IN_HBM] + whole(2),
-        [pltpu.VMEM((2, 256, 4096), BF16), pltpu.VMEM((2, 256, 256), BF16), pltpu.SemaphoreType.DMA((3, 4))],
+        [pltpu.VMEM((2, 256, 4096), BF16), pltpu.VMEM((2, 2, 256, 128), BF16), pltpu.SemaphoreType.DMA((3, 4))],
         8 * 10**8,
         (at, tokens_in, beside, pre_gain.reshape(1, 4096), taps, taps_got, near, w_unembed),
         mib=12,
     )
     signal, gate = call(
         proj_kernel,
-        (shape((16, 64, 128), BF16), shape((2, 2, 128, 128), BF16)),
+        (shape((16, 96, 128), BF16), shape((2, 2, 128, 128), BF16)),
         [SCALARS] + whole(4) + [IN_HBM] * 4,
         [pltpu.VMEM((4, 4, 384, 128), BF16), pltpu.SemaphoreType.DMA((4,))],
         8 * 10**8,
         (at, gained, scale, sums, pieces, *fars),
     )
     got = lax.all_to_all(signal, "ctx", 0, 0, axis_index_groups=GROUPS_CORE, tiled=True)
-    before = lax.ppermute(got, "ctx", PERM_Z_UP)
+    before = lax.ppermute(got[:, :32].reshape(512, 128), "ctx", PERM_Z_UP)
     terms, _ = lax.optimization_barrier((terms, got))
     terms = lax.all_to_all(terms, "tp", 0, 0, tiled=True)
     gate_keep = lax.dynamic_index_in_dim(gate, core, 0, False)
     gate_got = lax.ppermute(lax.dynamic_index_in_dim(gate, 1 - core, 0, False), "ctx", PERM_CORE)
 
-    conv = convolve(z_at, *spectra(got), before)
+    conv = convolve(z_at, *spectra(z_at, got), before)
     conv = call(pack_kernel, shape((32, 48, 128), BF16), whole(2), [], 10**5, (conv, terms))
     conv = lax.all_to_all(conv, "ctx", 0, 0, axis_index_groups=GROUPS_PLANE, tiled=True)
 

time: 178 us -> 188 us (1.056)
  blocking collectives: 32.2 us -> 42.6 us
  waiting for transfers between devices: 38.4 us -> 28 us
  starting transfers between devices: 87.5 us -> 95.7 us
    all_to_all x1, waiting for transfers between devices: 12 us -> 0.01 us  [per_device(): terms = lax.all_to_all(terms, 'tp', 0, 0, tiled=True)]
    all_to_all x1, blocking collectives: 12.7 us -> 20.1 us  [per_device(): lax.all_to_all(logits.reshape(4, 64, 512), 'tp', 0, 0, axis_index_groups=...]
    ppermute x3, waiting for transfers between devices: 0.01 us -> 5.17 us  [per_device(): fars = [far] + [lax.ppermute(far, 'ctx', PERM_X[k]) for k in (1, 2, 3)]]
    ppermute x3, starting transfers between devices: 8.65 us -> 12.7 us  [per_device(): fars = [far] + [lax.ppermute(far, 'ctx', PERM_X[k]) for k in (1, 2, 3)]]
    all_to_all x1, waiting for transfers between devices: 7.31 us -> 3.25 us  [per_device(): lax.all_to_all(near, 'ctx', 0, 0, axis_index_groups=GROUPS_Y, tiled=True)]
    all_to_all x1, starting transfers between devices: 12.5 us -> 16.5 us  [per_device(): terms = lax.all_to_all(terms, 'tp', 0, 0, tiled=True)]
    all_to_all x1, blocking collectives: 11.7 us -> 14.6 us  [per_device(): lax.all_to_all(signal, 'ctx', 0, 0, axis_index_groups=GROUPS_CORE, tiled=...]
    ppermute x1, waiting for transfers between devices: 9.16 us -> 6.33 us  [per_device(): far = lax.ppermute(logits, 'tp', [(i, i ^ 4) for i in range(8)])]
  transfers between devices with their start and end apart: 17 -> 17, of which waited for: 7 -> 9; matrix products, arithmetic and copies ran while one was open for 1% -> 1% of each run, Pallas kernels for 5% -> 5%
where the time goes in v17:
time: 188 us; the launch traced here: 186 us
  starting transfers between devices  95.7 us (51%)
  blocking collectives  42.6 us (23%)
  waiting for transfers between devices  28 us (15%)
  Pallas kernels  14.6 us (8%)
  local copies, waits for them, and re-layouts  2.66 us (1%)
    all_to_all x1, blocking collectives, per_device(): lax.all_to_all(logits.reshape(4, 64, 512), 'tp', 0, 0, axis_index_groups=...  20.1 us
    all_to_all x1, starting transfers between devices, per_device(): terms = lax.all_to_all(terms, 'tp', 0, 0, tiled=True)  16.5 us
    ppermute x1, starting transfers between devices, per_device(): far = lax.ppermute(first, 'ctx', PERM_Z)  15.7 us
    all_to_all x1, blocking collectives, per_device(): lax.all_to_all(signal, 'ctx', 0, 0, axis_index_groups=GROUPS_CORE, tiled=...  14.6 us
    pallas_call x10, Pallas kernels, call(): pl.pallas_call(kernel, out_shape=outs, in_specs=specs, out_specs=out_spec...  14.6 us
    ppermute x3, starting transfers between devices, per_device(): fars = [far] + [lax.ppermute(far, 'ctx', PERM_X[k]) for k in (1, 2, 3)]  12.7 us
    ppermute x3, starting transfers between devices, per_device(): lax.ppermute(along, 'ctx', PERM_Y[k])  11.6 us
    ppermute x1, starting transfers between devices, per_device(): before = lax.ppermute(got[:, :32].reshape(512, 128), 'ctx', PERM_Z_UP)  9.44 us
  transfers between devices with their start and end apart: 17, of which 9 were waited for; matrix products, arithmetic and copies ran while one was open for 1% of the time, Pallas kernels for 5%

profile of v17, /device:TPU:6, one launch (start us, length us, event | category | flops | bytes accessed | tf_op | source)
XLA Modules:
  0.0 185.9 jit_solution(6828630317574238579)
XLA Ops:
  0.0 1.9 %collective-permute-start = (bf16[3,64,256]{2,1,0:T(8,128)(2,1)}, bf16[3,64,256]{2,1,0:T(8,128)(2,1)S(1)}, u32[]{:S(2)}, u32[]{:S(2)}) collective-permute-start(bf16[3,64,256]{2,1,0:T(8,128)(2,1)} %bitcast.41), channel_id=1, source_target_pairs={{0,8},{8,0},{16,24},{24,16},{32,40},{40,32},{48,56},{56,48},{64,72... | collective-permute-start | bytes 294920 | tf_op jit(solution)/shard_map/ppermute | solution.py:343
  5.9 2.1 %collective-permute-start.1 = (bf16[256,4096]{1,0:T(8,128)(2,1)}, bf16[256,4096]{1,0:T(8,128)(2,1)}, u32[]{:S(2)}, u32[]{:S(2)}) collective-permute-start(bf16[256,4096]{1,0:T(8,128)(2,1)} %own_hbm.1), channel_id=1, source_target_pairs={{0,8},{8,0},{16,24},{24,16},{32,40},{40,32},{48,56},{56,48},{64,72... | collective-permute-start | bytes 6291464 | tf_op jit(solution)/shard_map/ppermute | solution.py:347
  8.0 15.7 %collective-permute-start.2 = (bf16[1024,128]{1,0:T(8,128)(2,1)S(1)}, bf16[1024,128]{1,0:T(8,128)(2,1)S(1)}, u32[]{:S(2)}, u32[]{:S(2)}) collective-permute-start(bf16[1024,128]{1,0:T(8,128)(2,1)S(1)} %shard_map.118.first_ref), channel_id=1, source_target_pairs={{0,256},{8,264},{16,272},{24,280},{32,288},{40,296},{48,304},{56,3... | collective-permute-start | bytes 786440 | tf_op jit(solution)/shard_map/ppermute | solution.py:349
  23.7 4.8 %all-to-all-start = ((bf16[4,384,128]{2,1,0:T(8,128)(2,1)}), bf16[4,384,128]{2,1,0:T(8,128)(2,1)S(1)}, u32[]{:S(2)}, u32[]{:S(2)}) async-start(bf16[4,384,128]{2,1,0:T(8,128)(2,1)} %shard_map.119), calls=%async_computation | async-start | bytes 786432 | tf_op jit(solution)/shard_map/all_to_all | solution.py:348
  28.5 2.3 %collective-permute-done.2.far_ref = bf16[1024,128]{1,0:T(8,128)(2,1)S(1)} collective-permute-done((bf16[1024,128]{1,0:T(8,128)(2,1)S(1)}, bf16[1024,128]{1,0:T(8,128)(2,1)S(1)}, u32[]{:S(2)}, u32[]{:S(2)}) %collective-permute-start.2) | collective-permute-done | bytes 262176 | tf_op jit(solution)/shard_map/ppermute | solution.py:349
  30.8 3.5 %collective-permute-start.3 = (bf16[384,128]{1,0:T(8,128)(2,1)S(1)}, bf16[384,128]{1,0:T(8,128)(2,1)S(1)}, u32[]{:S(2)}, u32[]{:S(2)}) collective-permute-start(bf16[384,128]{1,0:T(8,128)(2,1)S(1)} %get-tuple-element.42), channel_id=1, source_target_pairs={{0,64},{8,72},{16,80},{24,88},{32,96},{40,104},{48,112},{56,120},{... | collective-permute-start | bytes 294920 | tf_op jit(solution)/shard_map/ppermute | solution.py:352
  34.3 4.8 %collective-permute-start.4 = (bf16[384,128]{1,0:T(8,128)(2,1)S(1)}, bf16[384,128]{1,0:T(8,128)(2,1)S(1)}, u32[]{:S(2)}, u32[]{:S(2)}) collective-permute-start(bf16[384,128]{1,0:T(8,128)(2,1)S(1)} %get-tuple-element.42), channel_id=1, source_target_pairs={{0,128},{8,136},{16,144},{24,152},{32,160},{40,168},{48,176},{56,1... | collective-permute-start | bytes 294920 | tf_op jit(solution)/shard_map/ppermute | solution.py:352
  39.1 3.3 %collective-permute-start.5 = (bf16[384,128]{1,0:T(8,128)(2,1)S(1)}, bf16[384,128]{1,0:T(8,128)(2,1)S(1)}, u32[]{:S(2)}, u32[]{:S(2)}) collective-permute-start(bf16[384,128]{1,0:T(8,128)(2,1)S(1)} %get-tuple-element.42), channel_id=1, source_target_pairs={{0,192},{8,200},{16,208},{24,216},{32,224},{40,232},{48,240},{56,2... | collective-permute-start | bytes 294920 | tf_op jit(solution)/shard_map/ppermute | solution.py:352
  42.4 3.2 %collective-permute-done.5 = bf16[384,128]{1,0:T(8,128)(2,1)S(1)} collective-permute-done((bf16[384,128]{1,0:T(8,128)(2,1)S(1)}, bf16[384,128]{1,0:T(8,128)(2,1)S(1)}, u32[]{:S(2)}, u32[]{:S(2)}) %collective-permute-start.5) | collective-permute-done | bytes 98336 | tf_op jit(solution)/shard_map/ppermute | solution.py:352
  45.7 1.3 shard_map.120
  47.0 4.0 %all-to-all-start.1 = ((bf16[4,1600,128]{2,1,0:T(8,128)(2,1)}), bf16[4,1600,128]{2,1,0:T(8,128)(2,1)S(1)}, u32[]{:S(2)}, u32[]{:S(2)}) async-start(bf16[4,1600,128]{2,1,0:T(8,128)(2,1)} %shard_map.120), calls=%async_computation.1 | async-start | bytes 3276800 | tf_op jit(solution)/shard_map/all_to_all | solution.py:364
  51.0 8.1 %collective-permute-start.7 = (bf16[4,384,128]{2,1,0:T(8,128)(2,1)S(1)}, bf16[4,384,128]{2,1,0:T(8,128)(2,1)S(1)}, u32[]{:S(2)}, u32[]{:S(2)}) collective-permute-start(bf16[4,384,128]{2,1,0:T(8,128)(2,1)S(1)} %pad_maximum_fusion.f0), channel_id=1, source_target_pairs={{0,16},{8,24},{16,32},{24,40},{32,48},{40,56},{48,0},{56,8},{64,80... | collective-permute-start | bytes 1179656 | tf_op jit(solution)/shard_map/ppermute | solution.py:367
  59.1 1.9 %collective-permute-start.8 = (bf16[4,384,128]{2,1,0:T(8,128)(2,1)S(1)}, bf16[4,384,128]{2,1,0:T(8,128)(2,1)}, u32[]{:S(2)}, u32[]{:S(2)}) collective-permute-start(bf16[4,384,128]{2,1,0:T(8,128)(2,1)S(1)} %pad_maximum_fusion.f0), channel_id=1, source_target_pairs={{0,32},{8,40},{16,48},{24,56},{32,0},{40,8},{48,16},{56,24},{64,96... | collective-permute-start | bytes 1179656 | tf_op jit(solution)/shard_map/ppermute | solution.py:367
  61.0 2.8 %collective-permute-start.9 = (bf16[4,384,128]{2,1,0:T(8,128)(2,1)S(1)}, bf16[4,384,128]{2,1,0:T(8,128)(2,1)}, u32[]{:S(2)}, u32[]{:S(2)}) collective-permute-start(bf16[4,384,128]{2,1,0:T(8,128)(2,1)S(1)} %pad_maximum_fusion.f0), channel_id=1, source_target_pairs={{0,48},{8,56},{16,0},{24,8},{32,16},{40,24},{48,32},{56,40},{64,11... | collective-permute-start | bytes 1179656 | tf_op jit(solution)/shard_map/ppermute | solution.py:367
  63.9 1.9 %collective-permute-start.6 = (bf16[2,256,128]{2,1,0:T(8,128)(2,1)S(1)}, bf16[2,256,128]{2,1,0:T(8,128)(2,1)S(1)}, u32[]{:S(2)}, u32[]{:S(2)}) collective-permute-start(bf16[2,256,128]{2,1,0:T(8,128)(2,1)S(1)} %get-tuple-element.39), channel_id=1, source_target_pairs={{0,8},{8,0},{16,24},{24,16},{32,40},{40,32},{48,56},{56,48},{64,72... | collective-permute-start | bytes 393224 | tf_op jit(solution)/shard_map/ppermute | solution.py:369
  67.1 3.3 %all-to-all-done.1.near_ref = bf16[4,1600,128]{2,1,0:T(8,128)(2,1)S(1)} async-done(((bf16[4,1600,128]{2,1,0:T(8,128)(2,1)}), bf16[4,1600,128]{2,1,0:T(8,128)(2,1)S(1)}, u32[]{:S(2)}, u32[]{:S(2)}) %all-to-all-start.1) | async-done | bytes 1638432 | tf_op jit(solution)/shard_map/all_to_all | solution.py:364
  70.4 5.2 %shard_map.121 = (bf16[2,256,4096]{2,1,0:T(8,128)(2,1)S(1)}, f32[2,256,128]{2,1,0:T(8,128)S(1)}, f32[2,256,384]{2,1,0:T(8,128)S(1)}, bf16[8,32,128]{2,1,0:T(8,128)(2,1)}, bf16[16,64,128]{2,1,0:T(8,128)(2,1)S(1)}) custom-call(s32[4]{0:T(128)S(1)} %pad_add_fusion.at_ref, bf16[256,4096]{1,0:T(8,128)(2,1)} %own_hbm.1, ...), custom_call_target="tpu_custom_call" | custom-call | flops 800000000 | bytes 4194304 | tf_op jit(solution)/shard_map/pallas_call | solution.py:285
  75.6 5.2 %collective-permute-done.9.f3 = bf16[4,384,128]{2,1,0:T(8,128)(2,1)} collective-permute-done((bf16[4,384,128]{2,1,0:T(8,128)(2,1)S(1)}, bf16[4,384,128]{2,1,0:T(8,128)(2,1)}, u32[]{:S(2)}, u32[]{:S(2)}) %collective-permute-start.9) | collective-permute-done | bytes 393248 | tf_op jit(solution)/shard_map/ppermute | solution.py:367
  80.7 3.2 %shard_map.122 = (bf16[16,96,128]{2,1,0:T(8,128)(2,1)S(1)}, bf16[2,2,128,128]{3,2,1,0:T(8,128)(2,1)S(1)}) custom-call(s32[4]{0:T(128)S(1)} %pad_add_fusion.at_ref, bf16[2,256,4096]{2,1,0:T(8,128)(2,1)S(1)} %get-tuple-element.25.gained_ref, f32[2,256,128]{2,1,0:T(8,128)S(1)} %get-tuple-element.26.scale_ref, f32[2,256,384]{2,1,0:T(8,128)S(1)} %get-tuple-element.27.near_ref, ...), custom_call_target="tpu_custom_call" | custom-call | flops 800000000 | bytes 4194304 | tf_op jit(solution)/shard_map/pallas_call | solution.py:285
  83.9 14.6 %all_to_all.35.got_ref = bf16[16,96,128]{2,1,0:T(8,128)(2,1)S(1)} all-to-all(bf16[16,96,128]{2,1,0:T(8,128)(2,1)S(1)} %get-tuple-element.30), channel_id=1, replica_groups={{0,16,32,48,64,80,96,112,128,144,160,176,192,208,224,240},{8,24,40,56,7..., dimensions={0} | all-to-all | bytes 786432 | tf_op jit(solution)/shard_map/all_to_all | solution.py:396
  98.6 16.5 %all-to-all-start.3 = ((bf16[8,32,128]{2,1,0:T(8,128)(2,1)}), bf16[8,32,128]{2,1,0:T(8,128)(2,1)S(1)}, u32[]{:S(2)}, u32[]{:S(2)}) async-start(bf16[8,32,128]{2,1,0:T(8,128)(2,1)} %get-tuple-element.35), calls=%async_computation.3 | async-start | bytes 131072 | tf_op jit(solution)/shard_map/all_to_all | solution.py:399
  115.1 9.4 %collective-permute-start.10 = (bf16[512,128]{1,0:T(8,128)(2,1)S(1)}, bf16[512,128]{1,0:T(8,128)(2,1)S(1)}, u32[]{:S(2)}, u32[]{:S(2)}) collective-permute-start(bf16[512,128]{1,0:T(8,128)(2,1)S(1)} %bitcast.37), channel_id=1, source_target_pairs={{0,256},{8,264},{16,272},{24,280},{32,288},{40,296},{48,304},{56,3... | collective-permute-start | bytes 393224 | tf_op jit(solution)/shard_map/ppermute | solution.py:397
  124.5 1.3 shard_map.123
  125.8 1.2 collective-permute-done.10.before_ref
  128.9 6.4 %all-to-all-start.4 = ((bf16[32,48,128]{2,1,0:T(8,128)(2,1)}), bf16[32,48,128]{2,1,0:T(8,128)(2,1)S(1)}, u32[]{:S(2)}, u32[]{:S(2)}) async-start(bf16[32,48,128]{2,1,0:T(8,128)(2,1)} %shard_map.125), calls=%async_computation.4 | async-start | bytes 786432 | tf_op jit(solution)/shard_map/all_to_all | solution.py:405
  135.3 2.1 %collective-permute-start.11 = (bf16[2,128,128]{2,1,0:T(8,128)(2,1)S(1)}, bf16[2,128,128]{2,1,0:T(8,128)(2,1)S(1)}, u32[]{:S(2)}, u32[]{:S(2)}) collective-permute-start(bf16[2,128,128]{2,1,0:T(8,128)(2,1)S(1)} %get-tuple-element.43), channel_id=1, source_target_pairs={{0,8},{8,0},{16,24},{24,16},{32,40},{40,32},{48,56},{56,48},{64,72... | collective-permute-start | bytes 196616 | tf_op jit(solution)/shard_map/ppermute | solution.py:401
  137.3 1.2 fusion.base_ref
  138.6 4.8 %all-to-all-done.4.got_ref = bf16[32,48,128]{2,1,0:T(8,128)(2,1)S(1)} async-done(((bf16[32,48,128]{2,1,0:T(8,128)(2,1)}), bf16[32,48,128]{2,1,0:T(8,128)(2,1)S(1)}, u32[]{:S(2)}, u32[]{:S(2)}) %all-to-all-start.4) | async-done | bytes 393248 | tf_op jit(solution)/shard_map/all_to_all | solution.py:405
  143.7 20.1 %all_to_all.36 = bf16[4,64,512]{2,1,0:T(8,128)(2,1)S(1)} all-to-all(bf16[4,64,512]{2,1,0:T(8,128)(2,1)S(1)} %bitcast.33), channel_id=1, replica_groups={{0,1,2,3},{4,5,6,7},{8,9,10,11},{12,13,14,15},{16,17,18,19},{20,21,22,2..., dimensions={0} | all-to-all | bytes 524288 | tf_op jit(solution)/shard_map/all_to_all | solution.py:417
  163.9 6.7 %collective-permute-start.12 = (bf16[64,512]{1,0:T(8,128)(2,1)S(1)}, bf16[64,512]{1,0:T(8,128)(2,1)S(1)}, u32[]{:S(2)}, u32[]{:S(2)}) collective-permute-start(bf16[64,512]{1,0:T(8,128)(2,1)S(1)} %reduce_sum.30), channel_id=1, source_target_pairs={{0,4},{1,5},{2,6},{3,7},{4,0},{5,1},{6,2},{7,3},{8,12},{9,13},{10,... | collective-permute-start | bytes 196616 | tf_op jit(solution)/shard_map/ppermute | solution.py:419
  170.6 6.3 %collective-permute-done.12 = bf16[64,512]{1,0:T(8,128)(2,1)S(1)} collective-permute-done((bf16[64,512]{1,0:T(8,128)(2,1)S(1)}, bf16[64,512]{1,0:T(8,128)(2,1)S(1)}, u32[]{:S(2)}, u32[]{:S(2)}) %collective-permute-start.12) | collective-permute-done | bytes 65568 | tf_op jit(solution)/shard_map/ppermute | solution.py:419
  177.4 7.9 %all_to_all.37.scores_ref = f32[4,1,64]{2,1,0:T(1,128)S(1)} all-to-all(f32[4,1,64]{2,1,0:T(1,128)S(1)} %broadcast_in_dim.7), channel_id=1, replica_groups={{0,1,2,3},{4,5,6,7},{8,9,10,11},{12,13,14,15},{16,17,18,19},{20,21,22,2..., dimensions={0} | all-to-all | bytes 2048 | tf_op jit(solution)/shard_map/all_to_all | solution.py:430
  (48 shorter events, 8.7 us)
Async XLA Ops:
  0.0 3.4 %collective-permute-start = (bf16[3,64,256]{2,1,0:T(8,128)(2,1)}, bf16[3,64,256]{2,1,0:T(8,128)(2,1)S(1)}, u32[]{:S(2)}, u32[]{:S(2)}) collective-permute-start(bf16[3,64,256]{2,1,0:T(8,128)(2,1)} %bitcast.41), channel_id=1, source_target_pairs={{0,8},{8,0},{16,24},{24,16},{32,40},{40,32},{48,56},{56,48},{64,72... | collective-permute-start | bytes 294920 | tf_op jit(solution)/shard_map/ppermute | solution.py:343
  3.4 0.9 copy-start.3
  4.3 0.8 copy-start.4
  5.9 64.4 %collective-permute-start.1 = (bf16[256,4096]{1,0:T(8,128)(2,1)}, bf16[256,4096]{1,0:T(8,128)(2,1)}, u32[]{:S(2)}, u32[]{:S(2)}) collective-permute-start(bf16[256,4096]{1,0:T(8,128)(2,1)} %own_hbm.1), channel_id=1, source_target_pairs={{0,8},{8,0},{16,24},{24,16},{32,40},{40,32},{48,56},{56,48},{64,72... | collective-permute-start | bytes 6291464 | tf_op jit(solution)/shard_map/ppermute | solution.py:347
  8.0 22.8 %collective-permute-start.2 = (bf16[1024,128]{1,0:T(8,128)(2,1)S(1)}, bf16[1024,128]{1,0:T(8,128)(2,1)S(1)}, u32[]{:S(2)}, u32[]{:S(2)}) collective-permute-start(bf16[1024,128]{1,0:T(8,128)(2,1)S(1)} %shard_map.118.first_ref), channel_id=1, source_target_pairs={{0,256},{8,264},{16,272},{24,280},{32,288},{40,296},{48,304},{56,3... | collective-permute-start | bytes 786440 | tf_op jit(solution)/shard_map/ppermute | solution.py:349
  23.7 22.0 %all-to-all-start = ((bf16[4,384,128]{2,1,0:T(8,128)(2,1)}), bf16[4,384,128]{2,1,0:T(8,128)(2,1)S(1)}, u32[]{:S(2)}, u32[]{:S(2)}) async-start(bf16[4,384,128]{2,1,0:T(8,128)(2,1)} %shard_map.119), calls=%async_computation | async-start | bytes 786432 | tf_op jit(solution)/shard_map/all_to_all | solution.py:348
  30.8 11.6 %collective-permute-start.3 = (bf16[384,128]{1,0:T(8,128)(2,1)S(1)}, bf16[384,128]{1,0:T(8,128)(2,1)S(1)}, u32[]{:S(2)}, u32[]{:S(2)}) collective-permute-start(bf16[384,128]{1,0:T(8,128)(2,1)S(1)} %get-tuple-element.42), channel_id=1, source_target_pairs={{0,64},{8,72},{16,80},{24,88},{32,96},{40,104},{48,112},{56,120},{... | collective-permute-start | bytes 294920 | tf_op jit(solution)/shard_map/ppermute | solution.py:352
  34.3 8.1 %collective-permute-start.4 = (bf16[384,128]{1,0:T(8,128)(2,1)S(1)}, bf16[384,128]{1,0:T(8,128)(2,1)S(1)}, u32[]{:S(2)}, u32[]{:S(2)}) collective-permute-start(bf16[384,128]{1,0:T(8,128)(2,1)S(1)} %get-tuple-element.42), channel_id=1, source_target_pairs={{0,128},{8,136},{16,144},{24,152},{32,160},{40,168},{48,176},{56,1... | collective-permute-start | bytes 294920 | tf_op jit(solution)/shard_map/ppermute | solution.py:352
  39.1 6.5 %collective-permute-start.5 = (bf16[384,128]{1,0:T(8,128)(2,1)S(1)}, bf16[384,128]{1,0:T(8,128)(2,1)S(1)}, u32[]{:S(2)}, u32[]{:S(2)}) collective-permute-start(bf16[384,128]{1,0:T(8,128)(2,1)S(1)} %get-tuple-element.42), channel_id=1, source_target_pairs={{0,192},{8,200},{16,208},{24,216},{32,224},{40,232},{48,240},{56,2... | collective-permute-start | bytes 294920 | tf_op jit(solution)/shard_map/ppermute | solution.py:352
  47.0 18.8 %copy-start.5 = (bf16[4096]{0:T(1024)(128)(2,1)S(1)}, bf16[4096]{0:T(1024)(128)(2,1)}, u32[]{:S(2)}) copy-start(bf16[4096]{0:T(1024)(128)(2,1)} %param.13) | copy-start | bytes 24580
  47.0 23.3 %copy-start = (bf16[512,512]{1,0:T(8,128)(2,1)S(1)}, bf16[512,512]{1,0:T(8,128)(2,1)}, u32[]{:S(2)}) copy-start(bf16[512,512]{1,0:T(8,128)(2,1)} %unembed_ref.1) | copy-start | bytes 1572868
  47.0 23.3 %all-to-all-start.1 = ((bf16[4,1600,128]{2,1,0:T(8,128)(2,1)}), bf16[4,1600,128]{2,1,0:T(8,128)(2,1)S(1)}, u32[]{:S(2)}, u32[]{:S(2)}) async-start(bf16[4,1600,128]{2,1,0:T(8,128)(2,1)} %shard_map.120), calls=%async_computation.1 | async-start | bytes 3276800 | tf_op jit(solution)/shard_map/all_to_all | solution.py:364
  51.0 24.6 %collective-permute-start.7 = (bf16[4,384,128]{2,1,0:T(8,128)(2,1)S(1)}, bf16[4,384,128]{2,1,0:T(8,128)(2,1)S(1)}, u32[]{:S(2)}, u32[]{:S(2)}) collective-permute-start(bf16[4,384,128]{2,1,0:T(8,128)(2,1)S(1)} %pad_maximum_fusion.f0), channel_id=1, source_target_pairs={{0,16},{8,24},{16,32},{24,40},{32,48},{40,56},{48,0},{56,8},{64,80... | collective-permute-start | bytes 1179656 | tf_op jit(solution)/shard_map/ppermute | solution.py:367
  59.1 16.5 %collective-permute-start.8 = (bf16[4,384,128]{2,1,0:T(8,128)(2,1)S(1)}, bf16[4,384,128]{2,1,0:T(8,128)(2,1)}, u32[]{:S(2)}, u32[]{:S(2)}) collective-permute-start(bf16[4,384,128]{2,1,0:T(8,128)(2,1)S(1)} %pad_maximum_fusion.f0), channel_id=1, source_target_pairs={{0,32},{8,40},{16,48},{24,56},{32,0},{40,8},{48,16},{56,24},{64,96... | collective-permute-start | bytes 1179656 | tf_op jit(solution)/shard_map/ppermute | solution.py:367
  61.0 19.7 %collective-permute-start.9 = (bf16[4,384,128]{2,1,0:T(8,128)(2,1)S(1)}, bf16[4,384,128]{2,1,0:T(8,128)(2,1)}, u32[]{:S(2)}, u32[]{:S(2)}) collective-permute-start(bf16[4,384,128]{2,1,0:T(8,128)(2,1)S(1)} %pad_maximum_fusion.f0), channel_id=1, source_target_pairs={{0,48},{8,56},{16,0},{24,8},{32,16},{40,24},{48,32},{56,40},{64,11... | collective-permute-start | bytes 1179656 | tf_op jit(solution)/shard_map/ppermute | solution.py:367
  63.9 3.2 %collective-permute-start.6 = (bf16[2,256,128]{2,1,0:T(8,128)(2,1)S(1)}, bf16[2,256,128]{2,1,0:T(8,128)(2,1)S(1)}, u32[]{:S(2)}, u32[]{:S(2)}) collective-permute-start(bf16[2,256,128]{2,1,0:T(8,128)(2,1)S(1)} %get-tuple-element.39), channel_id=1, source_target_pairs={{0,8},{8,0},{16,24},{24,16},{32,40},{40,32},{48,56},{56,48},{64,72... | collective-permute-start | bytes 393224 | tf_op jit(solution)/shard_map/ppermute | solution.py:369
  80.7 43.8 %copy-start.1 = (bf16[832,256]{1,0:T(8,128)(2,1)S(1)}, bf16[832,256]{1,0:T(8,128)(2,1)}, u32[]{:S(2)}) copy-start(bf16[832,256]{1,0:T(8,128)(2,1)} %constant.109.clone.matrices) | copy-start | bytes 1277956
  80.7 43.8 %copy-start.2 = (f32[128,256]{1,0:T(8,128)S(1)}, f32[128,256]{1,0:T(8,128)}, u32[]{:S(2)}) copy-start(f32[128,256]{1,0:T(8,128)} %constant.110.clone.twiddles) | copy-start | bytes 393220
  98.6 29.5 %all-to-all-start.3 = ((bf16[8,32,128]{2,1,0:T(8,128)(2,1)}), bf16[8,32,128]{2,1,0:T(8,128)(2,1)S(1)}, u32[]{:S(2)}, u32[]{:S(2)}) async-start(bf16[8,32,128]{2,1,0:T(8,128)(2,1)} %get-tuple-element.35), calls=%async_computation.3 | async-start | bytes 131072 | tf_op jit(solution)/shard_map/all_to_all | solution.py:399
  115.1 11.9 %collective-permute-start.10 = (bf16[512,128]{1,0:T(8,128)(2,1)S(1)}, bf16[512,128]{1,0:T(8,128)(2,1)S(1)}, u32[]{:S(2)}, u32[]{:S(2)}) collective-permute-start(bf16[512,128]{1,0:T(8,128)(2,1)S(1)} %bitcast.37), channel_id=1, source_target_pairs={{0,256},{8,264},{16,272},{24,280},{32,288},{40,296},{48,304},{56,3... | collective-permute-start | bytes 393224 | tf_op jit(solution)/shard_map/ppermute | solution.py:397
  128.9 41.7 %copy-start.7 = (s32[256]{0:T(256)S(1)}, s32[256]{0:T(256)}, u32[]{:S(2)}) copy-start(s32[256]{0:T(256)} %param.18) | copy-start | bytes 3076
  128.9 14.5 %all-to-all-start.4 = ((bf16[32,48,128]{2,1,0:T(8,128)(2,1)}), bf16[32,48,128]{2,1,0:T(8,128)(2,1)S(1)}, u32[]{:S(2)}, u32[]{:S(2)}) async-start(bf16[32,48,128]{2,1,0:T(8,128)(2,1)} %shard_map.125), calls=%async_computation.4 | async-start | bytes 786432 | tf_op jit(solution)/shard_map/all_to_all | solution.py:405
  135.2 42.1 %copy-start.6 = (s32[256]{0:T(256)S(1)}, s32[256]{0:T(256)}, u32[]{:S(2)}) copy-start(s32[256]{0:T(256)} %param.19) | copy-start | bytes 3076
  135.3 3.3 %collective-permute-start.11 = (bf16[2,128,128]{2,1,0:T(8,128)(2,1)S(1)}, bf16[2,128,128]{2,1,0:T(8,128)(2,1)S(1)}, u32[]{:S(2)}, u32[]{:S(2)}) collective-permute-start(bf16[2,128,128]{2,1,0:T(8,128)(2,1)S(1)} %get-tuple-element.43), channel_id=1, source_target_pairs={{0,8},{8,0},{16,24},{24,16},{32,40},{40,32},{48,56},{56,48},{64,72... | collective-permute-start | bytes 196616 | tf_op jit(solution)/shard_map/ppermute | solution.py:401
  163.9 13.1 %collective-permute-start.12 = (bf16[64,512]{1,0:T(8,128)(2,1)S(1)}, bf16[64,512]{1,0:T(8,128)(2,1)S(1)}, u32[]{:S(2)}, u32[]{:S(2)}) collective-permute-start(bf16[64,512]{1,0:T(8,128)(2,1)S(1)} %reduce_sum.30), channel_id=1, source_target_pairs={{0,4},{1,5},{2,6},{3,7},{4,0},{5,1},{6,2},{7,3},{8,12},{9,13},{10,... | collective-permute-start | bytes 196616 | tf_op jit(solution)/shard_map/ppermute | solution.py:419

commit v18 on v16

--- a/solution.py
+++ b/solution.py
@@ -337,9 +337,8 @@
         10**5,
         (core_at, keep, lax.ppermute(w_in, "ctx", PERM_CORE), rows),
     )
-    near = call(copies_kernel, shape((4, 384, 128), BF16), whole(1), [], 10**10, (first,))
-    near, tokens = lax.optimization_barrier((near, tokens_in))
-    beside = lax.ppermute(tokens, "ctx", PERM_CORE)
+    near = call(copies_kernel, shape((4, 384, 128), BF16), whole(1), [], 10**5, (first,))
+    beside = lax.ppermute(tokens_in, "ctx", PERM_CORE)
     near = lax.all_to_all(near, "ctx", 0, 0, axis_index_groups=GROUPS_X, tiled=True)
     far = lax.ppermute(first, "ctx", PERM_Z)
 

time: 178 us -> 178 us (level)
  no operation moved by 1% of the time
where the time goes in v18:
time: 178 us; the launch traced here: 177 us
  starting transfers between devices  86.8 us (49%)
  waiting for transfers between devices  38 us (21%)
  blocking collectives  32.1 us (18%)
  Pallas kernels  14.2 us (8%)
  local copies, waits for them, and re-layouts  3.32 us (2%)
    ppermute x1, starting transfers between devices, per_device(): far = lax.ppermute(first, 'ctx', PERM_Z)  15.7 us
    pallas_call x10, Pallas kernels, call(): pl.pallas_call(kernel, out_shape=outs, in_specs=specs, out_specs=out_spec...  14.2 us
    all_to_all x1, starting transfers between devices, per_device(): terms = lax.all_to_all(terms, 'tp', 0, 0, tiled=True)  12.9 us
    all_to_all x1, blocking collectives, per_device(): lax.all_to_all(logits.reshape(4, 64, 512), 'tp', 0, 0, axis_index_groups=...  12.7 us
    ppermute x3, starting transfers between devices, per_device(): lax.ppermute(along, 'ctx', PERM_Y[k])  11.6 us
    all_to_all x1, blocking collectives, per_device(): lax.all_to_all(signal, 'ctx', 0, 0, axis_index_groups=GROUPS_CORE, tiled=...  11.5 us
    all_to_all x1, waiting for transfers between devices, per_device(): terms = lax.all_to_all(terms, 'tp', 0, 0, tiled=True)  11.3 us
    ppermute x1, starting transfers between devices, per_device(): before = lax.ppermute(got, 'ctx', PERM_Z_UP)  10.6 us
  transfers between devices with their start and end apart: 17, of which 7 were waited for; matrix products, arithmetic and copies ran while one was open for 1% of the time, Pallas kernels for 5%

profile of v18, /device:TPU:6, one launch (start us, length us, event | category | flops | bytes accessed | tf_op | source)
XLA Modules:
  0.0 176.6 jit_solution(13653288774044495292)
XLA Ops:
  0.0 1.9 %collective-permute-start = (bf16[256,4096]{1,0:T(8,128)(2,1)}, bf16[256,4096]{1,0:T(8,128)(2,1)}, u32[]{:S(2)}, u32[]{:S(2)}) collective-permute-start(bf16[256,4096]{1,0:T(8,128)(2,1)} %own_hbm.1), channel_id=1, source_target_pairs={{0,8},{8,0},{16,24},{24,16},{32,40},{40,32},{48,56},{56,48},{64,72... | collective-permute-start | bytes 6291464 | tf_op jit(solution)/shard_map/ppermute | solution.py:341
  1.9 2.4 %collective-permute-start.1 = (bf16[3,64,256]{2,1,0:T(8,128)(2,1)}, bf16[3,64,256]{2,1,0:T(8,128)(2,1)S(1)}, u32[]{:S(2)}, u32[]{:S(2)}) collective-permute-start(bf16[3,64,256]{2,1,0:T(8,128)(2,1)} %bitcast.31), channel_id=1, source_target_pairs={{0,8},{8,0},{16,24},{24,16},{32,40},{40,32},{48,56},{56,48},{64,72... | collective-permute-start | bytes 294920 | tf_op jit(solution)/shard_map/ppermute | solution.py:338
  7.2 15.7 %collective-permute-start.2 = (bf16[512,128]{1,0:T(8,128)(2,1)S(1)}, bf16[512,128]{1,0:T(8,128)(2,1)S(1)}, u32[]{:S(2)}, u32[]{:S(2)}) collective-permute-start(bf16[512,128]{1,0:T(8,128)(2,1)S(1)} %shard_map.118.first_ref), channel_id=1, source_target_pairs={{0,256},{8,264},{16,272},{24,280},{32,288},{40,296},{48,304},{56,3... | collective-permute-start | bytes 393224 | tf_op jit(solution)/shard_map/ppermute | solution.py:343
  23.7 4.8 %all-to-all-start = ((bf16[4,384,128]{2,1,0:T(8,128)(2,1)}), bf16[4,384,128]{2,1,0:T(8,128)(2,1)S(1)}, u32[]{:S(2)}, u32[]{:S(2)}) async-start(bf16[4,384,128]{2,1,0:T(8,128)(2,1)} %shard_map.119), calls=%async_computation | async-start | bytes 786432 | tf_op jit(solution)/shard_map/all_to_all | solution.py:342
  28.5 3.5 %collective-permute-start.3 = (bf16[384,128]{1,0:T(8,128)(2,1)S(1)}, bf16[384,128]{1,0:T(8,128)(2,1)S(1)}, u32[]{:S(2)}, u32[]{:S(2)}) collective-permute-start(bf16[384,128]{1,0:T(8,128)(2,1)S(1)} %get-tuple-element.38), channel_id=1, source_target_pairs={{0,64},{8,72},{16,80},{24,88},{32,96},{40,104},{48,112},{56,120},{... | collective-permute-start | bytes 294920 | tf_op jit(solution)/shard_map/ppermute | solution.py:346
  32.0 4.8 %collective-permute-start.4 = (bf16[384,128]{1,0:T(8,128)(2,1)S(1)}, bf16[384,128]{1,0:T(8,128)(2,1)S(1)}, u32[]{:S(2)}, u32[]{:S(2)}) collective-permute-start(bf16[384,128]{1,0:T(8,128)(2,1)S(1)} %get-tuple-element.38), channel_id=1, source_target_pairs={{0,128},{8,136},{16,144},{24,152},{32,160},{40,168},{48,176},{56,1... | collective-permute-start | bytes 294920 | tf_op jit(solution)/shard_map/ppermute | solution.py:346
  36.8 3.3 %collective-permute-start.5 = (bf16[384,128]{1,0:T(8,128)(2,1)S(1)}, bf16[384,128]{1,0:T(8,128)(2,1)S(1)}, u32[]{:S(2)}, u32[]{:S(2)}) collective-permute-start(bf16[384,128]{1,0:T(8,128)(2,1)S(1)} %get-tuple-element.38), channel_id=1, source_target_pairs={{0,192},{8,200},{16,208},{24,216},{32,224},{40,232},{48,240},{56,2... | collective-permute-start | bytes 294920 | tf_op jit(solution)/shard_map/ppermute | solution.py:346
  40.1 3.2 %collective-permute-done.5 = bf16[384,128]{1,0:T(8,128)(2,1)S(1)} collective-permute-done((bf16[384,128]{1,0:T(8,128)(2,1)S(1)}, bf16[384,128]{1,0:T(8,128)(2,1)S(1)}, u32[]{:S(2)}, u32[]{:S(2)}) %collective-permute-start.5) | collective-permute-done | bytes 98336 | tf_op jit(solution)/shard_map/ppermute | solution.py:346
  43.4 1.3 shard_map.120
  44.7 4.0 %all-to-all-start.1 = ((bf16[4,1600,128]{2,1,0:T(8,128)(2,1)}), bf16[4,1600,128]{2,1,0:T(8,128)(2,1)S(1)}, u32[]{:S(2)}, u32[]{:S(2)}) async-start(bf16[4,1600,128]{2,1,0:T(8,128)(2,1)} %shard_map.120), calls=%async_computation.1 | async-start | bytes 3276800 | tf_op jit(solution)/shard_map/all_to_all | solution.py:358
  48.7 1.9 %collective-permute-start.7 = (bf16[4,384,128]{2,1,0:T(8,128)(2,1)S(1)}, bf16[4,384,128]{2,1,0:T(8,128)(2,1)S(1)}, u32[]{:S(2)}, u32[]{:S(2)}) collective-permute-start(bf16[4,384,128]{2,1,0:T(8,128)(2,1)S(1)} %pad_maximum_fusion.f0), channel_id=1, source_target_pairs={{0,16},{8,24},{16,32},{24,40},{32,48},{40,56},{48,0},{56,8},{64,80... | collective-permute-start | bytes 1179656 | tf_op jit(solution)/shard_map/ppermute | solution.py:360
  50.6 4.8 %collective-permute-start.8 = (bf16[4,384,128]{2,1,0:T(8,128)(2,1)S(1)}, bf16[4,384,128]{2,1,0:T(8,128)(2,1)S(1)}, u32[]{:S(2)}, u32[]{:S(2)}) collective-permute-start(bf16[4,384,128]{2,1,0:T(8,128)(2,1)S(1)} %pad_maximum_fusion.f0), channel_id=1, source_target_pairs={{0,32},{8,40},{16,48},{24,56},{32,0},{40,8},{48,16},{56,24},{64,96... | collective-permute-start | bytes 1179656 | tf_op jit(solution)/shard_map/ppermute | solution.py:360
  55.4 1.9 %collective-permute-start.9 = (bf16[4,384,128]{2,1,0:T(8,128)(2,1)S(1)}, bf16[4,384,128]{2,1,0:T(8,128)(2,1)}, u32[]{:S(2)}, u32[]{:S(2)}) collective-permute-start(bf16[4,384,128]{2,1,0:T(8,128)(2,1)S(1)} %pad_maximum_fusion.f0), channel_id=1, source_target_pairs={{0,48},{8,56},{16,0},{24,8},{32,16},{40,24},{48,32},{56,40},{64,11... | collective-permute-start | bytes 1179656 | tf_op jit(solution)/shard_map/ppermute | solution.py:360
  57.4 1.9 %collective-permute-start.6 = (bf16[256,256]{1,0:T(8,128)(2,1)S(1)}, bf16[256,256]{1,0:T(8,128)(2,1)}, u32[]{:S(2)}, u32[]{:S(2)}) collective-permute-start(bf16[256,256]{1,0:T(8,128)(2,1)S(1)} %copy-done.4), channel_id=1, source_target_pairs={{0,8},{8,0},{16,24},{24,16},{32,40},{40,32},{48,56},{56,48},{64,72... | collective-permute-start | bytes 393224 | tf_op jit(solution)/shard_map/ppermute | solution.py:361
  59.5 1.3 collective-permute-done.6.got_taps
  60.7 7.1 %all-to-all-done.1.near_ref = bf16[4,1600,128]{2,1,0:T(8,128)(2,1)S(1)} async-done(((bf16[4,1600,128]{2,1,0:T(8,128)(2,1)}), bf16[4,1600,128]{2,1,0:T(8,128)(2,1)S(1)}, u32[]{:S(2)}, u32[]{:S(2)}) %all-to-all-start.1) | async-done | bytes 1638432 | tf_op jit(solution)/shard_map/all_to_all | solution.py:358
  67.9 1.6 copy-done
  69.4 4.7 %shard_map.121 = (bf16[2,256,4096]{2,1,0:T(8,128)(2,1)S(1)}, f32[2,256,128]{2,1,0:T(8,128)S(1)}, f32[2,256,384]{2,1,0:T(8,128)S(1)}, bf16[8,32,128]{2,1,0:T(8,128)(2,1)}, bf16[16,32,128]{2,1,0:T(8,128)(2,1)S(1)}) custom-call(s32[4]{0:T(128)S(1)} %pad_add_fusion.at_ref, bf16[256,4096]{1,0:T(8,128)(2,1)S(1)} %copy-done, ...), custom_call_target="tpu_custom_call" | custom-call | flops 800000000 | bytes 4194304 | tf_op jit(solution)/shard_map/pallas_call | solution.py:281
  74.2 3.1 %shard_map.122 = (bf16[16,64,128]{2,1,0:T(8,128)(2,1)S(1)}, bf16[2,2,128,128]{3,2,1,0:T(8,128)(2,1)S(1)}) custom-call(s32[4]{0:T(128)S(1)} %pad_add_fusion.at_ref, bf16[2,256,4096]{2,1,0:T(8,128)(2,1)S(1)} %get-tuple-element.22.gained_ref, f32[2,256,128]{2,1,0:T(8,128)S(1)} %get-tuple-element.23.scale_ref, f32[2,256,384]{2,1,0:T(8,128)S(1)} %get-tuple-element.24.near_ref, ...), custom_call_target="tpu_custom_call" | custom-call | flops 800000000 | bytes 4194304 | tf_op jit(solution)/shard_map/pallas_call | solution.py:281
  77.3 11.5 %all_to_all.35.got_ref = bf16[16,64,128]{2,1,0:T(8,128)(2,1)S(1)} all-to-all(bf16[16,64,128]{2,1,0:T(8,128)(2,1)S(1)} %get-tuple-element.27), channel_id=1, replica_groups={{0,16,32,48,64,80,96,112,128,144,160,176,192,208,224,240},{8,24,40,56,7..., dimensions={0} | all-to-all | bytes 524288 | tf_op jit(solution)/shard_map/all_to_all | solution.py:387
  88.8 10.6 %collective-permute-start.10 = (bf16[16,64,128]{2,1,0:T(8,128)(2,1)S(1)}, bf16[16,64,128]{2,1,0:T(8,128)(2,1)S(1)}, u32[]{:S(2)}, u32[]{:S(2)}) collective-permute-start(bf16[16,64,128]{2,1,0:T(8,128)(2,1)S(1)} %all_to_all.35.got_ref), channel_id=1, source_target_pairs={{0,256},{8,264},{16,272},{24,280},{32,288},{40,296},{48,304},{56,3... | collective-permute-start | bytes 786440 | tf_op jit(solution)/shard_map/ppermute | solution.py:388
  99.4 12.9 %all-to-all-start.3 = ((bf16[8,32,128]{2,1,0:T(8,128)(2,1)}), bf16[8,32,128]{2,1,0:T(8,128)(2,1)S(1)}, u32[]{:S(2)}, u32[]{:S(2)}) async-start(bf16[8,32,128]{2,1,0:T(8,128)(2,1)} %get-tuple-element.31), calls=%async_computation.3 | async-start | bytes 131072 | tf_op jit(solution)/shard_map/all_to_all | solution.py:390
  113.4 1.6 shard_map.124.conv_ref
  114.9 11.3 %all-to-all-done.3.terms_ref = bf16[8,32,128]{2,1,0:T(8,128)(2,1)S(1)} async-done(((bf16[8,32,128]{2,1,0:T(8,128)(2,1)}), bf16[8,32,128]{2,1,0:T(8,128)(2,1)S(1)}, u32[]{:S(2)}, u32[]{:S(2)}) %all-to-all-start.3) | async-done | bytes 65568 | tf_op jit(solution)/shard_map/all_to_all | solution.py:390
  127.0 6.2 %all-to-all-start.4 = ((bf16[32,48,128]{2,1,0:T(8,128)(2,1)}), bf16[32,48,128]{2,1,0:T(8,128)(2,1)S(1)}, u32[]{:S(2)}, u32[]{:S(2)}) async-start(bf16[32,48,128]{2,1,0:T(8,128)(2,1)} %shard_map.125), calls=%async_computation.4 | async-start | bytes 786432 | tf_op jit(solution)/shard_map/all_to_all | solution.py:396
  133.2 2.1 %collective-permute-start.11 = (bf16[2,128,128]{2,1,0:T(8,128)(2,1)S(1)}, bf16[2,128,128]{2,1,0:T(8,128)(2,1)S(1)}, u32[]{:S(2)}, u32[]{:S(2)}) collective-permute-start(bf16[2,128,128]{2,1,0:T(8,128)(2,1)S(1)} %get-tuple-element.35), channel_id=1, source_target_pairs={{0,8},{8,0},{16,24},{24,16},{32,40},{40,32},{48,56},{56,48},{64,72... | collective-permute-start | bytes 196616 | tf_op jit(solution)/shard_map/ppermute | solution.py:392
  135.3 1.2 fusion.base_ref
  136.6 4.7 %all-to-all-done.4.got_ref = bf16[32,48,128]{2,1,0:T(8,128)(2,1)S(1)} async-done(((bf16[32,48,128]{2,1,0:T(8,128)(2,1)}), bf16[32,48,128]{2,1,0:T(8,128)(2,1)S(1)}, u32[]{:S(2)}, u32[]{:S(2)}) %all-to-all-start.4) | async-done | bytes 393248 | tf_op jit(solution)/shard_map/all_to_all | solution.py:396
  141.6 12.7 %all_to_all.36 = bf16[4,64,512]{2,1,0:T(8,128)(2,1)S(1)} all-to-all(bf16[4,64,512]{2,1,0:T(8,128)(2,1)S(1)} %bitcast.26), channel_id=1, replica_groups={{0,1,2,3},{4,5,6,7},{8,9,10,11},{12,13,14,15},{16,17,18,19},{20,21,22,2..., dimensions={0} | all-to-all | bytes 524288 | tf_op jit(solution)/shard_map/all_to_all | solution.py:408
  154.3 4.1 %collective-permute-start.12 = (bf16[64,512]{1,0:T(8,128)(2,1)S(1)}, bf16[64,512]{1,0:T(8,128)(2,1)S(1)}, u32[]{:S(2)}, u32[]{:S(2)}) collective-permute-start(bf16[64,512]{1,0:T(8,128)(2,1)S(1)} %reduce_sum.30), channel_id=1, source_target_pairs={{0,4},{1,5},{2,6},{3,7},{4,0},{5,1},{6,2},{7,3},{8,12},{9,13},{10,... | collective-permute-start | bytes 196616 | tf_op jit(solution)/shard_map/ppermute | solution.py:410
  158.6 9.1 %collective-permute-done.12 = bf16[64,512]{1,0:T(8,128)(2,1)S(1)} collective-permute-done((bf16[64,512]{1,0:T(8,128)(2,1)S(1)}, bf16[64,512]{1,0:T(8,128)(2,1)S(1)}, u32[]{:S(2)}, u32[]{:S(2)}) %collective-permute-start.12) | collective-permute-done | bytes 65568 | tf_op jit(solution)/shard_map/ppermute | solution.py:410
  168.1 7.9 %all_to_all.37.scores_ref = f32[4,1,64]{2,1,0:T(1,128)S(1)} all-to-all(f32[4,1,64]{2,1,0:T(1,128)S(1)} %broadcast_in_dim.7), channel_id=1, replica_groups={{0,1,2,3},{4,5,6,7},{8,9,10,11},{12,13,14,15},{16,17,18,19},{20,21,22,2..., dimensions={0} | all-to-all | bytes 2048 | tf_op jit(solution)/shard_map/all_to_all | solution.py:421
  (46 shorter events, 7.1 us)
Async XLA Ops:
  0.0 67.8 %collective-permute-start = (bf16[256,4096]{1,0:T(8,128)(2,1)}, bf16[256,4096]{1,0:T(8,128)(2,1)}, u32[]{:S(2)}, u32[]{:S(2)}) collective-permute-start(bf16[256,4096]{1,0:T(8,128)(2,1)} %own_hbm.1), channel_id=1, source_target_pairs={{0,8},{8,0},{16,24},{24,16},{32,40},{40,32},{48,56},{56,48},{64,72... | collective-permute-start | bytes 6291464 | tf_op jit(solution)/shard_map/ppermute | solution.py:341
  1.9 4.5 %collective-permute-start.1 = (bf16[3,64,256]{2,1,0:T(8,128)(2,1)}, bf16[3,64,256]{2,1,0:T(8,128)(2,1)S(1)}, u32[]{:S(2)}, u32[]{:S(2)}) collective-permute-start(bf16[3,64,256]{2,1,0:T(8,128)(2,1)} %bitcast.31), channel_id=1, source_target_pairs={{0,8},{8,0},{16,24},{24,16},{32,40},{40,32},{48,56},{56,48},{64,72... | collective-permute-start | bytes 294920 | tf_op jit(solution)/shard_map/ppermute | solution.py:338
  6.4 0.8 copy-start.5
  7.2 21.3 %collective-permute-start.2 = (bf16[512,128]{1,0:T(8,128)(2,1)S(1)}, bf16[512,128]{1,0:T(8,128)(2,1)S(1)}, u32[]{:S(2)}, u32[]{:S(2)}) collective-permute-start(bf16[512,128]{1,0:T(8,128)(2,1)S(1)} %shard_map.118.first_ref), channel_id=1, source_target_pairs={{0,256},{8,264},{16,272},{24,280},{32,288},{40,296},{48,304},{56,3... | collective-permute-start | bytes 393224 | tf_op jit(solution)/shard_map/ppermute | solution.py:343
  23.7 19.7 %all-to-all-start = ((bf16[4,384,128]{2,1,0:T(8,128)(2,1)}), bf16[4,384,128]{2,1,0:T(8,128)(2,1)S(1)}, u32[]{:S(2)}, u32[]{:S(2)}) async-start(bf16[4,384,128]{2,1,0:T(8,128)(2,1)} %shard_map.119), calls=%async_computation | async-start | bytes 786432 | tf_op jit(solution)/shard_map/all_to_all | solution.py:342
  28.5 11.6 %collective-permute-start.3 = (bf16[384,128]{1,0:T(8,128)(2,1)S(1)}, bf16[384,128]{1,0:T(8,128)(2,1)S(1)}, u32[]{:S(2)}, u32[]{:S(2)}) collective-permute-start(bf16[384,128]{1,0:T(8,128)(2,1)S(1)} %get-tuple-element.38), channel_id=1, source_target_pairs={{0,64},{8,72},{16,80},{24,88},{32,96},{40,104},{48,112},{56,120},{... | collective-permute-start | bytes 294920 | tf_op jit(solution)/shard_map/ppermute | solution.py:346
  32.0 8.1 %collective-permute-start.4 = (bf16[384,128]{1,0:T(8,128)(2,1)S(1)}, bf16[384,128]{1,0:T(8,128)(2,1)S(1)}, u32[]{:S(2)}, u32[]{:S(2)}) collective-permute-start(bf16[384,128]{1,0:T(8,128)(2,1)S(1)} %get-tuple-element.38), channel_id=1, source_target_pairs={{0,128},{8,136},{16,144},{24,152},{32,160},{40,168},{48,176},{56,1... | collective-permute-start | bytes 294920 | tf_op jit(solution)/shard_map/ppermute | solution.py:346
  36.8 6.5 %collective-permute-start.5 = (bf16[384,128]{1,0:T(8,128)(2,1)S(1)}, bf16[384,128]{1,0:T(8,128)(2,1)S(1)}, u32[]{:S(2)}, u32[]{:S(2)}) collective-permute-start(bf16[384,128]{1,0:T(8,128)(2,1)S(1)} %get-tuple-element.38), channel_id=1, source_target_pairs={{0,192},{8,200},{16,208},{24,216},{32,224},{40,232},{48,240},{56,2... | collective-permute-start | bytes 294920 | tf_op jit(solution)/shard_map/ppermute | solution.py:346
  44.7 12.7 %copy-start.4 = (bf16[256,256]{1,0:T(8,128)(2,1)S(1)}, bf16[256,256]{1,0:T(8,128)(2,1)}, u32[]{:S(2)}) copy-start(bf16[256,256]{1,0:T(8,128)(2,1)} %own_taps) | copy-start | bytes 393220
  44.7 14.7 %copy-start.6 = (bf16[4096]{0:T(1024)(128)(2,1)S(1)}, bf16[4096]{0:T(1024)(128)(2,1)}, u32[]{:S(2)}) copy-start(bf16[4096]{0:T(1024)(128)(2,1)} %param.13) | copy-start | bytes 24580
  44.7 23.2 %copy-start.1 = (bf16[512,512]{1,0:T(8,128)(2,1)S(1)}, bf16[512,512]{1,0:T(8,128)(2,1)}, u32[]{:S(2)}) copy-start(bf16[512,512]{1,0:T(8,128)(2,1)} %unembed_ref.1) | copy-start | bytes 1572868
  44.7 23.1 %all-to-all-start.1 = ((bf16[4,1600,128]{2,1,0:T(8,128)(2,1)}), bf16[4,1600,128]{2,1,0:T(8,128)(2,1)S(1)}, u32[]{:S(2)}, u32[]{:S(2)}) async-start(bf16[4,1600,128]{2,1,0:T(8,128)(2,1)} %shard_map.120), calls=%async_computation.1 | async-start | bytes 3276800 | tf_op jit(solution)/shard_map/all_to_all | solution.py:358
  48.7 25.4 %collective-permute-start.7 = (bf16[4,384,128]{2,1,0:T(8,128)(2,1)S(1)}, bf16[4,384,128]{2,1,0:T(8,128)(2,1)S(1)}, u32[]{:S(2)}, u32[]{:S(2)}) collective-permute-start(bf16[4,384,128]{2,1,0:T(8,128)(2,1)S(1)} %pad_maximum_fusion.f0), channel_id=1, source_target_pairs={{0,16},{8,24},{16,32},{24,40},{32,48},{40,56},{48,0},{56,8},{64,80... | collective-permute-start | bytes 1179656 | tf_op jit(solution)/shard_map/ppermute | solution.py:360
  50.6 23.5 %collective-permute-start.8 = (bf16[4,384,128]{2,1,0:T(8,128)(2,1)S(1)}, bf16[4,384,128]{2,1,0:T(8,128)(2,1)S(1)}, u32[]{:S(2)}, u32[]{:S(2)}) collective-permute-start(bf16[4,384,128]{2,1,0:T(8,128)(2,1)S(1)} %pad_maximum_fusion.f0), channel_id=1, source_target_pairs={{0,32},{8,40},{16,48},{24,56},{32,0},{40,8},{48,16},{56,24},{64,96... | collective-permute-start | bytes 1179656 | tf_op jit(solution)/shard_map/ppermute | solution.py:360
  55.4 18.7 %collective-permute-start.9 = (bf16[4,384,128]{2,1,0:T(8,128)(2,1)S(1)}, bf16[4,384,128]{2,1,0:T(8,128)(2,1)}, u32[]{:S(2)}, u32[]{:S(2)}) collective-permute-start(bf16[4,384,128]{2,1,0:T(8,128)(2,1)S(1)} %pad_maximum_fusion.f0), channel_id=1, source_target_pairs={{0,48},{8,56},{16,0},{24,8},{32,16},{40,24},{48,32},{56,40},{64,11... | collective-permute-start | bytes 1179656 | tf_op jit(solution)/shard_map/ppermute | solution.py:360
  57.4 3.4 %collective-permute-start.6 = (bf16[256,256]{1,0:T(8,128)(2,1)S(1)}, bf16[256,256]{1,0:T(8,128)(2,1)}, u32[]{:S(2)}, u32[]{:S(2)}) collective-permute-start(bf16[256,256]{1,0:T(8,128)(2,1)S(1)} %copy-done.4), channel_id=1, source_target_pairs={{0,8},{8,0},{16,24},{24,16},{32,40},{40,32},{48,56},{56,48},{64,72... | collective-permute-start | bytes 393224 | tf_op jit(solution)/shard_map/ppermute | solution.py:361
  67.9 1.6 copy-start
  74.1 38.2 %copy-start.2 = (bf16[832,256]{1,0:T(8,128)(2,1)S(1)}, bf16[832,256]{1,0:T(8,128)(2,1)}, u32[]{:S(2)}) copy-start(bf16[832,256]{1,0:T(8,128)(2,1)} %constant.103.clone.matrices) | copy-start | bytes 1277956
  74.2 38.2 %copy-start.3 = (f32[128,256]{1,0:T(8,128)S(1)}, f32[128,256]{1,0:T(8,128)}, u32[]{:S(2)}) copy-start(f32[128,256]{1,0:T(8,128)} %constant.104.clone.twiddles) | copy-start | bytes 393220
  88.8 24.6 %collective-permute-start.10 = (bf16[16,64,128]{2,1,0:T(8,128)(2,1)S(1)}, bf16[16,64,128]{2,1,0:T(8,128)(2,1)S(1)}, u32[]{:S(2)}, u32[]{:S(2)}) collective-permute-start(bf16[16,64,128]{2,1,0:T(8,128)(2,1)S(1)} %all_to_all.35.got_ref), channel_id=1, source_target_pairs={{0,256},{8,264},{16,272},{24,280},{32,288},{40,296},{48,304},{56,3... | collective-permute-start | bytes 786440 | tf_op jit(solution)/shard_map/ppermute | solution.py:388
  99.4 26.8 %all-to-all-start.3 = ((bf16[8,32,128]{2,1,0:T(8,128)(2,1)}), bf16[8,32,128]{2,1,0:T(8,128)(2,1)S(1)}, u32[]{:S(2)}, u32[]{:S(2)}) async-start(bf16[8,32,128]{2,1,0:T(8,128)(2,1)} %get-tuple-element.31), calls=%async_computation.3 | async-start | bytes 131072 | tf_op jit(solution)/shard_map/all_to_all | solution.py:390
  127.0 31.5 %copy-start.8 = (s32[256]{0:T(256)S(1)}, s32[256]{0:T(256)}, u32[]{:S(2)}) copy-start(s32[256]{0:T(256)} %param.18) | copy-start | bytes 3076
  127.0 14.3 %all-to-all-start.4 = ((bf16[32,48,128]{2,1,0:T(8,128)(2,1)}), bf16[32,48,128]{2,1,0:T(8,128)(2,1)S(1)}, u32[]{:S(2)}, u32[]{:S(2)}) async-start(bf16[32,48,128]{2,1,0:T(8,128)(2,1)} %shard_map.125), calls=%async_computation.4 | async-start | bytes 786432 | tf_op jit(solution)/shard_map/all_to_all | solution.py:396
  133.2 34.9 %copy-start.7 = (s32[256]{0:T(256)S(1)}, s32[256]{0:T(256)}, u32[]{:S(2)}) copy-start(s32[256]{0:T(256)} %param.19) | copy-start | bytes 3076
  133.2 3.3 %collective-permute-start.11 = (bf16[2,128,128]{2,1,0:T(8,128)(2,1)S(1)}, bf16[2,128,128]{2,1,0:T(8,128)(2,1)S(1)}, u32[]{:S(2)}, u32[]{:S(2)}) collective-permute-start(bf16[2,128,128]{2,1,0:T(8,128)(2,1)S(1)} %get-tuple-element.35), channel_id=1, source_target_pairs={{0,8},{8,0},{16,24},{24,16},{32,40},{40,32},{48,56},{56,48},{64,72... | collective-permute-start | bytes 196616 | tf_op jit(solution)/shard_map/ppermute | solution.py:392
  154.3 13.4 %collective-permute-start.12 = (bf16[64,512]{1,0:T(8,128)(2,1)S(1)}, bf16[64,512]{1,0:T(8,128)(2,1)S(1)}, u32[]{:S(2)}, u32[]{:S(2)}) collective-permute-start(bf16[64,512]{1,0:T(8,128)(2,1)S(1)} %reduce_sum.30), channel_id=1, source_target_pairs={{0,4},{1,5},{2,6},{3,7},{4,0},{5,1},{6,2},{7,3},{8,12},{9,13},{10,... | collective-permute-start | bytes 196616 | tf_op jit(solution)/shard_map/ppermute | solution.py:410

commit v19 on v18

--- a/solution.py
+++ b/solution.py
@@ -172,9 +172,27 @@
     return jnp.concatenate([ref[lead, row + 128 * g : row + 128 * g + 128, :] for g in range(3)], axis=1)
 
 
+def scale_kernel(own_hbm, beside_hbm, scale_ref, tokens, sems):
+    copies = []
+    for part, ref in enumerate((own_hbm, beside_hbm)):
+        for i in range(4):
+            rows = pl.ds(i * 64, 64)
+            copies.append(pltpu.make_async_copy(ref.at[rows], tokens.at[part, rows], sems.at[part, i]))
+    for copy in copies:
+        copy.start()
+    for k in range(8):
+        copies[k].wait()
+        part, i = k // 4, k % 4
+        for half in range(2):
+            rows = slice(i * 64 + half * 32, i * 64 + half * 32 + 32)
+            stream = tokens[part, rows, :].astype(F32)
+            mean = jnp.mean(stream * stream, axis=1, keepdims=True)
+            scale_ref[part, rows, :] = jnp.broadcast_to(lax.rsqrt(mean + NORM_EPS), (32, 128))
+
+
 def near_kernel(
     at_ref, own_hbm, beside_hbm, gain_ref, own_taps, got_taps, near_ref, unembed_ref,
-    gained_ref, scale_ref, out_ref, terms_ref, pieces_ref, tokens, taps, sems,
+    gained_ref, out_ref, terms_ref, pieces_ref, tokens, taps, sems,
 ):
     core, start = at_ref[2], at_ref[3] * 2048
     gain = gain_ref[...]
@@ -201,13 +219,8 @@
     for part in range(2):
         for i in range(4):
             copies[part * 4 + i].wait()
-            for half in range(2):
-                rows = slice(i * 64 + half * 32, i * 64 + half * 32 + 32)
-                block = tokens[part, rows, :]
-                stream = block.astype(F32)
-                mean = jnp.mean(stream * stream, axis=1, keepdims=True)
-                scale_ref[part, rows, :] = jnp.broadcast_to(lax.rsqrt(mean + NORM_EPS), (32, 128))
-                gained_ref[part, rows, :] = block * gain
+            rows = slice(i * 64, i * 64 + 64)
+            gained_ref[part, rows, :] = tokens[part, rows, :] * gain
         total = jnp.zeros((256, 384), F32)
         for y in range(4):
             for x in (0, 2):
@@ -229,10 +242,13 @@
         ref[p, pl.ds(pl.multiple_of(row + place * 16, 16), 16), :] = rows
 
 
-def proj_kernel(at_ref, gained_ref, scale_ref, near_ref, pieces_ref, f0, f1, f2, f3, sig_ref, gate_ref, fars, sems):
+def proj_kernel(
+    at_ref, gained_ref, near_ref, pieces_ref, scale_hbm, f0, f1, f2, f3, sig_ref, gate_ref, fars, scales, sems
+):
     y_at, x_at, core = at_ref[0], at_ref[1], at_ref[2]
     start = 2048 - at_ref[3] * 2048
     copies = [pltpu.make_async_copy(f, fars.at[k], sems.at[k]) for k, f in enumerate((f0, f1, f2, f3))]
+    copies.append(pltpu.make_async_copy(scale_hbm, scales, sems.at[4]))
     for copy in copies:
         copy.start()
     for part in range(2):
@@ -246,7 +262,9 @@
                 left = [gained_ref[part, :, pl.ds(pl.multiple_of(at, 128), 128)] for at in starts]
                 right = [weight_block(fars.at[step], k, 0), weight_block(fars.at[step], k + 1, 0)]
                 total += mm(jnp.concatenate(left, axis=1), jnp.concatenate(right, axis=0))
-        scale = scale_ref[part]
+        if part == 0:
+            copies[4].wait()
+        scale = scales[part]
         proj = (total * jnp.concatenate([scale, scale, scale], axis=1)).astype(BF16).astype(F32)
         place = core if part == 0 else 1 - core
         put_pieces(sig_ref, 0, place, proj[:, 128:256] * proj[:, 256:])
@@ -361,11 +379,18 @@
     taps_got = lax.ppermute(taps, "ctx", PERM_CORE)
 
     at = jnp.stack([(ctx // 8) % 4, (ctx // 2) % 4, core, z]).astype(jnp.int32)
-    gained, scale, sums, terms, pieces = call(
+    scale = call(
+        scale_kernel,
+        shape((2, 256, 128), F32),
+        [IN_HBM, IN_HBM],
+        [pltpu.VMEM((2, 256, 4096), BF16), pltpu.SemaphoreType.DMA((2, 4))],
+        10**7,
+        (tokens_in, beside),
+    )
+    gained, sums, terms, pieces = call(
         near_kernel,
         (
             shape((2, 256, 4096), BF16),
-            shape((2, 256, 128), F32),
             shape((2, 256, 384), F32),
             shape((8, 32, 128), BF16),
             shape((16, 32, 128), BF16),
@@ -379,10 +404,10 @@
     signal, gate = call(
         proj_kernel,
         (shape((16, 64, 128), BF16), shape((2, 2, 128, 128), BF16)),
-        [SCALARS] + whole(4) + [IN_HBM] * 4,
-        [pltpu.VMEM((4, 4, 384, 128), BF16), pltpu.SemaphoreType.DMA((4,))],
+        [SCALARS] + whole(3) + [IN_HBM] * 5,
+        [pltpu.VMEM((4, 4, 384, 128), BF16), pltpu.VMEM((2, 256, 128), F32), pltpu.SemaphoreType.DMA((5,))],
         8 * 10**8,
-        (at, gained, scale, sums, pieces, *fars),
+        (at, gained, sums, pieces, scale, *fars),
     )
     got = lax.all_to_all(signal, "ctx", 0, 0, axis_index_groups=GROUPS_CORE, tiled=True)
     before = lax.ppermute(got, "ctx", PERM_Z_UP)

time: 178 us -> 182 us (1.022)
  local copies, waits for them, and re-layouts: 3.32 us -> 8.54 us
  waiting for transfers between devices: 38 us -> 33.2 us
  Pallas kernels: 14.2 us -> 16.7 us
    unnamed x18 -> x36, local copies, waits for them, and re-layouts: 2.39 us -> 6.97 us
    pallas_call x10 -> x11, Pallas kernels: 14.2 us -> 16.7 us  [call(): pl.pallas_call(kernel, out_shape=outs, in_specs=specs, out_specs=out_spec...]
  transfers between devices with their start and end apart: 17 -> 17, of which waited for: 7 -> 7; matrix products, arithmetic and copies ran while one was open for 1% -> 1% of each run, Pallas kernels for 5% -> 6%
where the time goes in v19:
time: 182 us; the launch traced here: 181 us
  starting transfers between devices  87.6 us (48%)
  waiting for transfers between devices  33.2 us (18%)
  blocking collectives  33 us (18%)
  Pallas kernels  16.7 us (9%)
  local copies, waits for them, and re-layouts  8.54 us (5%)
    pallas_call x11, Pallas kernels, call(): pl.pallas_call(kernel, out_shape=outs, in_specs=specs, out_specs=out_spec...  16.7 us
    ppermute x1, starting transfers between devices, per_device(): far = lax.ppermute(first, 'ctx', PERM_Z)  15.7 us
    all_to_all x1, blocking collectives, per_device(): lax.all_to_all(logits.reshape(4, 64, 512), 'tp', 0, 0, axis_index_groups=...  13.2 us
    all_to_all x1, starting transfers between devices, per_device(): terms = lax.all_to_all(terms, 'tp', 0, 0, tiled=True)  12.3 us
    all_to_all x1, blocking collectives, per_device(): lax.all_to_all(signal, 'ctx', 0, 0, axis_index_groups=GROUPS_CORE, tiled=...  12 us
    ppermute x3, starting transfers between devices, per_device(): lax.ppermute(along, 'ctx', PERM_Y[k])  11.6 us
    ppermute x1, starting transfers between devices, per_device(): before = lax.ppermute(got, 'ctx', PERM_Z_UP)  11.2 us
    all_to_all x1, waiting for transfers between devices, per_device(): terms = lax.all_to_all(terms, 'tp', 0, 0, tiled=True)  9.59 us
  transfers between devices with their start and end apart: 17, of which 7 were waited for; matrix products, arithmetic and copies ran while one was open for 1% of the time, Pallas kernels for 6%

profile of v19, /device:TPU:6, one launch (start us, length us, event | category | flops | bytes accessed | tf_op | source)
XLA Modules:
  0.0 181.0 jit_solution(7188268790125238063)
XLA Ops:
  0.0 1.9 %collective-permute-start = (bf16[256,4096]{1,0:T(8,128)(2,1)}, bf16[256,4096]{1,0:T(8,128)(2,1)}, u32[]{:S(2)}, u32[]{:S(2)}) collective-permute-start(bf16[256,4096]{1,0:T(8,128)(2,1)} %own_hbm.3), channel_id=1, source_target_pairs={{0,8},{8,0},{16,24},{24,16},{32,40},{40,32},{48,56},{56,48},{64,72... | collective-permute-start | bytes 6291464 | tf_op jit(solution)/shard_map/ppermute | solution.py:359
  1.9 2.4 %collective-permute-start.1 = (bf16[3,64,256]{2,1,0:T(8,128)(2,1)}, bf16[3,64,256]{2,1,0:T(8,128)(2,1)S(1)}, u32[]{:S(2)}, u32[]{:S(2)}) collective-permute-start(bf16[3,64,256]{2,1,0:T(8,128)(2,1)} %bitcast.31), channel_id=1, source_target_pairs={{0,8},{8,0},{16,24},{24,16},{32,40},{40,32},{48,56},{56,48},{64,72... | collective-permute-start | bytes 294920 | tf_op jit(solution)/shard_map/ppermute | solution.py:356
  5.2 1.2 collective-permute-done.1.got_ref
  7.2 15.7 %collective-permute-start.2 = (bf16[512,128]{1,0:T(8,128)(2,1)S(1)}, bf16[512,128]{1,0:T(8,128)(2,1)S(1)}, u32[]{:S(2)}, u32[]{:S(2)}) collective-permute-start(bf16[512,128]{1,0:T(8,128)(2,1)S(1)} %shard_map.118.first_ref), channel_id=1, source_target_pairs={{0,256},{8,264},{16,272},{24,280},{32,288},{40,296},{48,304},{56,3... | collective-permute-start | bytes 393224 | tf_op jit(solution)/shard_map/ppermute | solution.py:361
  23.7 4.8 %all-to-all-start = ((bf16[4,384,128]{2,1,0:T(8,128)(2,1)}), bf16[4,384,128]{2,1,0:T(8,128)(2,1)S(1)}, u32[]{:S(2)}, u32[]{:S(2)}) async-start(bf16[4,384,128]{2,1,0:T(8,128)(2,1)} %shard_map.119), calls=%async_computation | async-start | bytes 786432 | tf_op jit(solution)/shard_map/all_to_all | solution.py:360
  28.5 3.5 %collective-permute-start.3 = (bf16[384,128]{1,0:T(8,128)(2,1)S(1)}, bf16[384,128]{1,0:T(8,128)(2,1)S(1)}, u32[]{:S(2)}, u32[]{:S(2)}) collective-permute-start(bf16[384,128]{1,0:T(8,128)(2,1)S(1)} %get-tuple-element.36), channel_id=1, source_target_pairs={{0,64},{8,72},{16,80},{24,88},{32,96},{40,104},{48,112},{56,120},{... | collective-permute-start | bytes 294920 | tf_op jit(solution)/shard_map/ppermute | solution.py:364
  32.0 4.8 %collective-permute-start.4 = (bf16[384,128]{1,0:T(8,128)(2,1)S(1)}, bf16[384,128]{1,0:T(8,128)(2,1)S(1)}, u32[]{:S(2)}, u32[]{:S(2)}) collective-permute-start(bf16[384,128]{1,0:T(8,128)(2,1)S(1)} %get-tuple-element.36), channel_id=1, source_target_pairs={{0,128},{8,136},{16,144},{24,152},{32,160},{40,168},{48,176},{56,1... | collective-permute-start | bytes 294920 | tf_op jit(solution)/shard_map/ppermute | solution.py:364
  36.8 3.3 %collective-permute-start.5 = (bf16[384,128]{1,0:T(8,128)(2,1)S(1)}, bf16[384,128]{1,0:T(8,128)(2,1)S(1)}, u32[]{:S(2)}, u32[]{:S(2)}) collective-permute-start(bf16[384,128]{1,0:T(8,128)(2,1)S(1)} %get-tuple-element.36), channel_id=1, source_target_pairs={{0,192},{8,200},{16,208},{24,216},{32,224},{40,232},{48,240},{56,2... | collective-permute-start | bytes 294920 | tf_op jit(solution)/shard_map/ppermute | solution.py:364
  40.1 3.2 %collective-permute-done.5 = bf16[384,128]{1,0:T(8,128)(2,1)S(1)} collective-permute-done((bf16[384,128]{1,0:T(8,128)(2,1)S(1)}, bf16[384,128]{1,0:T(8,128)(2,1)S(1)}, u32[]{:S(2)}, u32[]{:S(2)}) %collective-permute-start.5) | collective-permute-done | bytes 98336 | tf_op jit(solution)/shard_map/ppermute | solution.py:364
  44.4 1.2 copy-done.1
  45.6 4.5 %all-to-all-start.1 = ((bf16[4,1600,128]{2,1,0:T(8,128)(2,1)}), bf16[4,1600,128]{2,1,0:T(8,128)(2,1)}, u32[]{:S(2)}, u32[]{:S(2)}) async-start(bf16[4,1600,128]{2,1,0:T(8,128)(2,1)} %copy-done.1), calls=%async_computation.1 | async-start | bytes 3276800 | tf_op jit(solution)/shard_map/all_to_all | solution.py:376
  50.1 1.9 %collective-permute-start.7 = (bf16[4,384,128]{2,1,0:T(8,128)(2,1)S(1)}, bf16[4,384,128]{2,1,0:T(8,128)(2,1)}, u32[]{:S(2)}, u32[]{:S(2)}) collective-permute-start(bf16[4,384,128]{2,1,0:T(8,128)(2,1)S(1)} %pad_maximum_fusion.f0), channel_id=1, source_target_pairs={{0,16},{8,24},{16,32},{24,40},{32,48},{40,56},{48,0},{56,8},{64,80... | collective-permute-start | bytes 1179656 | tf_op jit(solution)/shard_map/ppermute | solution.py:378
  52.0 4.8 %collective-permute-start.8 = (bf16[4,384,128]{2,1,0:T(8,128)(2,1)S(1)}, bf16[4,384,128]{2,1,0:T(8,128)(2,1)}, u32[]{:S(2)}, u32[]{:S(2)}) collective-permute-start(bf16[4,384,128]{2,1,0:T(8,128)(2,1)S(1)} %pad_maximum_fusion.f0), channel_id=1, source_target_pairs={{0,32},{8,40},{16,48},{24,56},{32,0},{40,8},{48,16},{56,24},{64,96... | collective-permute-start | bytes 1179656 | tf_op jit(solution)/shard_map/ppermute | solution.py:378
  56.8 1.9 %collective-permute-start.9 = (bf16[4,384,128]{2,1,0:T(8,128)(2,1)S(1)}, bf16[4,384,128]{2,1,0:T(8,128)(2,1)}, u32[]{:S(2)}, u32[]{:S(2)}) collective-permute-start(bf16[4,384,128]{2,1,0:T(8,128)(2,1)S(1)} %pad_maximum_fusion.f0), channel_id=1, source_target_pairs={{0,48},{8,56},{16,0},{24,8},{32,16},{40,24},{48,32},{56,40},{64,11... | collective-permute-start | bytes 1179656 | tf_op jit(solution)/shard_map/ppermute | solution.py:378
  58.8 1.9 %collective-permute-start.6 = (bf16[256,256]{1,0:T(8,128)(2,1)S(1)}, bf16[256,256]{1,0:T(8,128)(2,1)S(1)}, u32[]{:S(2)}, u32[]{:S(2)}) collective-permute-start(bf16[256,256]{1,0:T(8,128)(2,1)S(1)} %copy-done.9), channel_id=1, source_target_pairs={{0,8},{8,0},{16,24},{24,16},{32,40},{40,32},{48,56},{56,48},{64,72... | collective-permute-start | bytes 393224 | tf_op jit(solution)/shard_map/ppermute | solution.py:379
  61.5 2.1 %shard_map.122.scale_hbm = f32[2,256,128]{2,1,0:T(8,128)S(1)} custom-call(bf16[256,4096]{1,0:T(8,128)(2,1)S(1)} %copy-done, bf16[256,4096]{1,0:T(8,128)(2,1)} %collective-permute-done.beside_hbm), custom_call_target="tpu_custom_call" | custom-call | flops 10000000 | bytes 4194304 | tf_op jit(solution)/shard_map/pallas_call | solution.py:299
  63.6 6.0 %all-to-all-done.1.near_ref = bf16[4,1600,128]{2,1,0:T(8,128)(2,1)} async-done(((bf16[4,1600,128]{2,1,0:T(8,128)(2,1)}), bf16[4,1600,128]{2,1,0:T(8,128)(2,1)}, u32[]{:S(2)}, u32[]{:S(2)}) %all-to-all-start.1) | async-done | bytes 1638432 | tf_op jit(solution)/shard_map/all_to_all | solution.py:376
  70.3 4.2 %shard_map.121 = (bf16[2,256,4096]{2,1,0:T(8,128)(2,1)S(1)}, f32[2,256,384]{2,1,0:T(8,128)S(1)}, bf16[8,32,128]{2,1,0:T(8,128)(2,1)S(1)}, bf16[16,32,128]{2,1,0:T(8,128)(2,1)S(1)}) custom-call(s32[4]{0:T(128)S(1)} %copy-done.14, bf16[256,4096]{1,0:T(8,128)(2,1)S(1)} %copy-done, bf16[256,4096]{1,0:T(8,128)(2,1)} %collective-permute-done.beside_hbm, ...), custom_call_target="tpu_custom_call" | custom-call | flops 800000000 | bytes 4194304 | tf_op jit(solution)/shard_map/pallas_call | solution.py:299
  74.5 3.4 %shard_map.123 = (bf16[16,64,128]{2,1,0:T(8,128)(2,1)S(1)}, bf16[2,2,128,128]{3,2,1,0:T(8,128)(2,1)S(1)}) custom-call(s32[4]{0:T(128)S(1)} %copy-done.14, bf16[2,256,4096]{2,1,0:T(8,128)(2,1)S(1)} %get-tuple-element.21.gained_ref, f32[2,256,384]{2,1,0:T(8,128)S(1)} %get-tuple-element.22.near_ref, bf16[16,32,128]{2,1,0:T(8,128)(2,1)S(1)} %get-tuple-element.23.pieces_ref, ...), custom_call_target="tpu_custom_call" | custom-call | flops 800000000 | bytes 4194304 | tf_op jit(solution)/shard_map/pallas_call | solution.py:299
  78.0 12.0 %all_to_all.35.got_ref = bf16[16,64,128]{2,1,0:T(8,128)(2,1)} all-to-all(bf16[16,64,128]{2,1,0:T(8,128)(2,1)S(1)} %get-tuple-element.25), channel_id=1, replica_groups={{0,16,32,48,64,80,96,112,128,144,160,176,192,208,224,240},{8,24,40,56,7..., dimensions={0} | all-to-all | bytes 524288 | tf_op jit(solution)/shard_map/all_to_all | solution.py:412
  90.0 11.2 %collective-permute-start.10 = (bf16[16,64,128]{2,1,0:T(8,128)(2,1)}, bf16[16,64,128]{2,1,0:T(8,128)(2,1)S(1)}, u32[]{:S(2)}, u32[]{:S(2)}) collective-permute-start(bf16[16,64,128]{2,1,0:T(8,128)(2,1)} %all_to_all.35.got_ref), channel_id=1, source_target_pairs={{0,256},{8,264},{16,272},{24,280},{32,288},{40,296},{48,304},{56,3... | collective-permute-start | bytes 786440 | tf_op jit(solution)/shard_map/ppermute | solution.py:413
  101.2 12.3 %all-to-all-start.3 = ((bf16[8,32,128]{2,1,0:T(8,128)(2,1)}), bf16[8,32,128]{2,1,0:T(8,128)(2,1)S(1)}, u32[]{:S(2)}, u32[]{:S(2)}) async-start(bf16[8,32,128]{2,1,0:T(8,128)(2,1)} %copy-done.12), calls=%async_computation.3 | async-start | bytes 131072 | tf_op jit(solution)/shard_map/all_to_all | solution.py:415
  114.6 1.9 %shard_map.124 = (f32[1024,256]{1,0:T(8,128)S(1)}, f32[1024,256]{1,0:T(8,128)S(1)}) custom-call(bf16[16,64,128]{2,1,0:T(8,128)(2,1)} %all_to_all.35.got_ref, bf16[832,256]{1,0:T(8,128)(2,1)S(1)} %copy-done.3, f32[128,256]{1,0:T(8,128)S(1)} %copy-done.6), custom_call_target="tpu_custom_call" | custom-call | flops 400000000 | bytes 4194304 | tf_op jit(solution)/shard_map/pallas_call | solution.py:299
  117.5 1.5 shard_map.125.conv_ref
  119.0 9.6 %all-to-all-done.3.terms_ref = bf16[8,32,128]{2,1,0:T(8,128)(2,1)S(1)} async-done(((bf16[8,32,128]{2,1,0:T(8,128)(2,1)}), bf16[8,32,128]{2,1,0:T(8,128)(2,1)S(1)}, u32[]{:S(2)}, u32[]{:S(2)}) %all-to-all-start.3) | async-done | bytes 65568 | tf_op jit(solution)/shard_map/all_to_all | solution.py:415
  129.4 6.2 %all-to-all-start.4 = ((bf16[32,48,128]{2,1,0:T(8,128)(2,1)}), bf16[32,48,128]{2,1,0:T(8,128)(2,1)S(1)}, u32[]{:S(2)}, u32[]{:S(2)}) async-start(bf16[32,48,128]{2,1,0:T(8,128)(2,1)} %shard_map.126), calls=%async_computation.4 | async-start | bytes 786432 | tf_op jit(solution)/shard_map/all_to_all | solution.py:421
  136.3 2.0 %collective-permute-start.11 = (bf16[2,128,128]{2,1,0:T(8,128)(2,1)S(1)}, bf16[2,128,128]{2,1,0:T(8,128)(2,1)S(1)}, u32[]{:S(2)}, u32[]{:S(2)}) collective-permute-start(bf16[2,128,128]{2,1,0:T(8,128)(2,1)S(1)} %get-tuple-element.33), channel_id=1, source_target_pairs={{0,8},{8,0},{16,24},{24,16},{32,40},{40,32},{48,56},{56,48},{64,72... | collective-permute-start | bytes 196616 | tf_op jit(solution)/shard_map/ppermute | solution.py:417
  140.1 3.7 %all-to-all-done.4.got_ref = bf16[32,48,128]{2,1,0:T(8,128)(2,1)S(1)} async-done(((bf16[32,48,128]{2,1,0:T(8,128)(2,1)}), bf16[32,48,128]{2,1,0:T(8,128)(2,1)S(1)}, u32[]{:S(2)}, u32[]{:S(2)}) %all-to-all-start.4) | async-done | bytes 393248 | tf_op jit(solution)/shard_map/all_to_all | solution.py:421
  145.8 13.2 %all_to_all.36 = bf16[4,64,512]{2,1,0:T(8,128)(2,1)S(1)} all-to-all(bf16[4,64,512]{2,1,0:T(8,128)(2,1)S(1)} %bitcast.26), channel_id=1, replica_groups={{0,1,2,3},{4,5,6,7},{8,9,10,11},{12,13,14,15},{16,17,18,19},{20,21,22,2..., dimensions={0} | all-to-all | bytes 524288 | tf_op jit(solution)/shard_map/all_to_all | solution.py:433
  159.0 4.3 %collective-permute-start.12 = (bf16[64,512]{1,0:T(8,128)(2,1)S(1)}, bf16[64,512]{1,0:T(8,128)(2,1)S(1)}, u32[]{:S(2)}, u32[]{:S(2)}) collective-permute-start(bf16[64,512]{1,0:T(8,128)(2,1)S(1)} %reduce_sum.30), channel_id=1, source_target_pairs={{0,4},{1,5},{2,6},{3,7},{4,0},{5,1},{6,2},{7,3},{8,12},{9,13},{10,... | collective-permute-start | bytes 196616 | tf_op jit(solution)/shard_map/ppermute | solution.py:435
  163.4 8.7 %collective-permute-done.12 = bf16[64,512]{1,0:T(8,128)(2,1)S(1)} collective-permute-done((bf16[64,512]{1,0:T(8,128)(2,1)S(1)}, bf16[64,512]{1,0:T(8,128)(2,1)S(1)}, u32[]{:S(2)}, u32[]{:S(2)}) %collective-permute-start.12) | collective-permute-done | bytes 65568 | tf_op jit(solution)/shard_map/ppermute | solution.py:435
  172.5 7.9 %all_to_all.37.scores_ref = f32[4,1,64]{2,1,0:T(1,128)S(1)} all-to-all(f32[4,1,64]{2,1,0:T(1,128)S(1)} %broadcast_in_dim.7), channel_id=1, replica_groups={{0,1,2,3},{4,5,6,7},{8,9,10,11},{12,13,14,15},{16,17,18,19},{20,21,22,2..., dimensions={0} | all-to-all | bytes 2048 | tf_op jit(solution)/shard_map/all_to_all | solution.py:446
  (65 shorter events, 13.2 us)
Async XLA Ops:
  0.0 61.5 %collective-permute-start = (bf16[256,4096]{1,0:T(8,128)(2,1)}, bf16[256,4096]{1,0:T(8,128)(2,1)}, u32[]{:S(2)}, u32[]{:S(2)}) collective-permute-start(bf16[256,4096]{1,0:T(8,128)(2,1)} %own_hbm.3), channel_id=1, source_target_pairs={{0,8},{8,0},{16,24},{24,16},{32,40},{40,32},{48,56},{56,48},{64,72... | collective-permute-start | bytes 6291464 | tf_op jit(solution)/shard_map/ppermute | solution.py:359
  1.9 4.5 %collective-permute-start.1 = (bf16[3,64,256]{2,1,0:T(8,128)(2,1)}, bf16[3,64,256]{2,1,0:T(8,128)(2,1)S(1)}, u32[]{:S(2)}, u32[]{:S(2)}) collective-permute-start(bf16[3,64,256]{2,1,0:T(8,128)(2,1)} %bitcast.31), channel_id=1, source_target_pairs={{0,8},{8,0},{16,24},{24,16},{32,40},{40,32},{48,56},{56,48},{64,72... | collective-permute-start | bytes 294920 | tf_op jit(solution)/shard_map/ppermute | solution.py:356
  7.2 21.3 %collective-permute-start.2 = (bf16[512,128]{1,0:T(8,128)(2,1)S(1)}, bf16[512,128]{1,0:T(8,128)(2,1)S(1)}, u32[]{:S(2)}, u32[]{:S(2)}) collective-permute-start(bf16[512,128]{1,0:T(8,128)(2,1)S(1)} %shard_map.118.first_ref), channel_id=1, source_target_pairs={{0,256},{8,264},{16,272},{24,280},{32,288},{40,296},{48,304},{56,3... | collective-permute-start | bytes 393224 | tf_op jit(solution)/shard_map/ppermute | solution.py:361
  23.7 19.7 %all-to-all-start = ((bf16[4,384,128]{2,1,0:T(8,128)(2,1)}), bf16[4,384,128]{2,1,0:T(8,128)(2,1)S(1)}, u32[]{:S(2)}, u32[]{:S(2)}) async-start(bf16[4,384,128]{2,1,0:T(8,128)(2,1)} %shard_map.119), calls=%async_computation | async-start | bytes 786432 | tf_op jit(solution)/shard_map/all_to_all | solution.py:360
  28.5 11.6 %collective-permute-start.3 = (bf16[384,128]{1,0:T(8,128)(2,1)S(1)}, bf16[384,128]{1,0:T(8,128)(2,1)S(1)}, u32[]{:S(2)}, u32[]{:S(2)}) collective-permute-start(bf16[384,128]{1,0:T(8,128)(2,1)S(1)} %get-tuple-element.36), channel_id=1, source_target_pairs={{0,64},{8,72},{16,80},{24,88},{32,96},{40,104},{48,112},{56,120},{... | collective-permute-start | bytes 294920 | tf_op jit(solution)/shard_map/ppermute | solution.py:364
  32.0 8.1 %collective-permute-start.4 = (bf16[384,128]{1,0:T(8,128)(2,1)S(1)}, bf16[384,128]{1,0:T(8,128)(2,1)S(1)}, u32[]{:S(2)}, u32[]{:S(2)}) collective-permute-start(bf16[384,128]{1,0:T(8,128)(2,1)S(1)} %get-tuple-element.36), channel_id=1, source_target_pairs={{0,128},{8,136},{16,144},{24,152},{32,160},{40,168},{48,176},{56,1... | collective-permute-start | bytes 294920 | tf_op jit(solution)/shard_map/ppermute | solution.py:364
  36.8 6.5 %collective-permute-start.5 = (bf16[384,128]{1,0:T(8,128)(2,1)S(1)}, bf16[384,128]{1,0:T(8,128)(2,1)S(1)}, u32[]{:S(2)}, u32[]{:S(2)}) collective-permute-start(bf16[384,128]{1,0:T(8,128)(2,1)S(1)} %get-tuple-element.36), channel_id=1, source_target_pairs={{0,192},{8,200},{16,208},{24,216},{32,224},{40,232},{48,240},{56,2... | collective-permute-start | bytes 294920 | tf_op jit(solution)/shard_map/ppermute | solution.py:364
  44.4 1.2 copy-start.1
  45.6 13.2 %copy-start.9 = (bf16[256,256]{1,0:T(8,128)(2,1)S(1)}, bf16[256,256]{1,0:T(8,128)(2,1)}, u32[]{:S(2)}) copy-start(bf16[256,256]{1,0:T(8,128)(2,1)} %own_taps) | copy-start | bytes 393220
  45.6 15.2 %copy-start.15 = (bf16[4096]{0:T(1024)(128)(2,1)S(1)}, bf16[4096]{0:T(1024)(128)(2,1)}, u32[]{:S(2)}) copy-start(bf16[4096]{0:T(1024)(128)(2,1)} %param.13) | copy-start | bytes 24580
  45.6 15.9 %copy-start = (bf16[256,4096]{1,0:T(8,128)(2,1)S(1)}, bf16[256,4096]{1,0:T(8,128)(2,1)}, u32[]{:S(2)}) copy-start(bf16[256,4096]{1,0:T(8,128)(2,1)} %own_hbm.3) | copy-start | bytes 6291460
  45.6 24.0 %all-to-all-start.1 = ((bf16[4,1600,128]{2,1,0:T(8,128)(2,1)}), bf16[4,1600,128]{2,1,0:T(8,128)(2,1)}, u32[]{:S(2)}, u32[]{:S(2)}) async-start(bf16[4,1600,128]{2,1,0:T(8,128)(2,1)} %copy-done.1), calls=%async_computation.1 | async-start | bytes 3276800 | tf_op jit(solution)/shard_map/all_to_all | solution.py:376
  50.1 24.4 %collective-permute-start.7 = (bf16[4,384,128]{2,1,0:T(8,128)(2,1)S(1)}, bf16[4,384,128]{2,1,0:T(8,128)(2,1)}, u32[]{:S(2)}, u32[]{:S(2)}) collective-permute-start(bf16[4,384,128]{2,1,0:T(8,128)(2,1)S(1)} %pad_maximum_fusion.f0), channel_id=1, source_target_pairs={{0,16},{8,24},{16,32},{24,40},{32,48},{40,56},{48,0},{56,8},{64,80... | collective-permute-start | bytes 1179656 | tf_op jit(solution)/shard_map/ppermute | solution.py:378
  52.0 22.5 %collective-permute-start.8 = (bf16[4,384,128]{2,1,0:T(8,128)(2,1)S(1)}, bf16[4,384,128]{2,1,0:T(8,128)(2,1)}, u32[]{:S(2)}, u32[]{:S(2)}) collective-permute-start(bf16[4,384,128]{2,1,0:T(8,128)(2,1)S(1)} %pad_maximum_fusion.f0), channel_id=1, source_target_pairs={{0,32},{8,40},{16,48},{24,56},{32,0},{40,8},{48,16},{56,24},{64,96... | collective-permute-start | bytes 1179656 | tf_op jit(solution)/shard_map/ppermute | solution.py:378
  56.8 17.7 %collective-permute-start.9 = (bf16[4,384,128]{2,1,0:T(8,128)(2,1)S(1)}, bf16[4,384,128]{2,1,0:T(8,128)(2,1)}, u32[]{:S(2)}, u32[]{:S(2)}) collective-permute-start(bf16[4,384,128]{2,1,0:T(8,128)(2,1)S(1)} %pad_maximum_fusion.f0), channel_id=1, source_target_pairs={{0,48},{8,56},{16,0},{24,8},{32,16},{40,24},{48,32},{56,40},{64,11... | collective-permute-start | bytes 1179656 | tf_op jit(solution)/shard_map/ppermute | solution.py:378
  58.8 4.8 %collective-permute-start.6 = (bf16[256,256]{1,0:T(8,128)(2,1)S(1)}, bf16[256,256]{1,0:T(8,128)(2,1)S(1)}, u32[]{:S(2)}, u32[]{:S(2)}) collective-permute-start(bf16[256,256]{1,0:T(8,128)(2,1)S(1)} %copy-done.9), channel_id=1, source_target_pairs={{0,8},{8,0},{16,24},{24,16},{32,40},{40,32},{48,56},{56,48},{64,72... | collective-permute-start | bytes 393224 | tf_op jit(solution)/shard_map/ppermute | solution.py:379
  61.5 8.1 %copy-start.2 = (bf16[512,512]{1,0:T(8,128)(2,1)S(1)}, bf16[512,512]{1,0:T(8,128)(2,1)}, u32[]{:S(2)}) copy-start(bf16[512,512]{1,0:T(8,128)(2,1)} %unembed_ref.1) | copy-start | bytes 1572868
  74.5 26.7 %copy-start.12 = (bf16[8,32,128]{2,1,0:T(8,128)(2,1)}, bf16[8,32,128]{2,1,0:T(8,128)(2,1)S(1)}, u32[]{:S(2)}) copy-start(bf16[8,32,128]{2,1,0:T(8,128)(2,1)S(1)} %get-tuple-element.29) | copy-start | bytes 196612
  74.5 39.0 %copy-start.6 = (f32[128,256]{1,0:T(8,128)S(1)}, f32[128,256]{1,0:T(8,128)}, u32[]{:S(2)}) copy-start(f32[128,256]{1,0:T(8,128)} %constant.104.clone.twiddles) | copy-start | bytes 393220
  78.0 23.2 %copy-start.7 = (bf16[2,2,128,128]{3,2,1,0:T(8,128)(2,1)}, bf16[2,2,128,128]{3,2,1,0:T(8,128)(2,1)S(1)}, u32[]{:S(2)}) copy-start(bf16[2,2,128,128]{3,2,1,0:T(8,128)(2,1)S(1)} %get-tuple-element.30) | copy-start | bytes 393220
  90.0 26.5 %collective-permute-start.10 = (bf16[16,64,128]{2,1,0:T(8,128)(2,1)}, bf16[16,64,128]{2,1,0:T(8,128)(2,1)S(1)}, u32[]{:S(2)}, u32[]{:S(2)}) collective-permute-start(bf16[16,64,128]{2,1,0:T(8,128)(2,1)} %all_to_all.35.got_ref), channel_id=1, source_target_pairs={{0,256},{8,264},{16,272},{24,280},{32,288},{40,296},{48,304},{56,3... | collective-permute-start | bytes 786440 | tf_op jit(solution)/shard_map/ppermute | solution.py:413
  101.2 27.4 %all-to-all-start.3 = ((bf16[8,32,128]{2,1,0:T(8,128)(2,1)}), bf16[8,32,128]{2,1,0:T(8,128)(2,1)S(1)}, u32[]{:S(2)}, u32[]{:S(2)}) async-start(bf16[8,32,128]{2,1,0:T(8,128)(2,1)} %copy-done.12), calls=%async_computation.3 | async-start | bytes 131072 | tf_op jit(solution)/shard_map/all_to_all | solution.py:415
  113.5 1.0 copy-start.3
  116.5 1.0 copy-start.4
  117.5 18.1 %copy-start.8 = (bf16[2,2,128,128]{3,2,1,0:T(8,128)(2,1)S(1)}, bf16[2,2,128,128]{3,2,1,0:T(8,128)(2,1)}, u32[]{:S(2)}) copy-start(bf16[2,2,128,128]{3,2,1,0:T(8,128)(2,1)} %copy-done.7) | copy-start | bytes 393220
  129.4 33.9 %copy-start.17 = (s32[256]{0:T(256)S(1)}, s32[256]{0:T(256)}, u32[]{:S(2)}) copy-start(s32[256]{0:T(256)} %param.18) | copy-start | bytes 3076
  129.4 14.3 %all-to-all-start.4 = ((bf16[32,48,128]{2,1,0:T(8,128)(2,1)}), bf16[32,48,128]{2,1,0:T(8,128)(2,1)S(1)}, u32[]{:S(2)}, u32[]{:S(2)}) async-start(bf16[32,48,128]{2,1,0:T(8,128)(2,1)} %shard_map.126), calls=%async_computation.4 | async-start | bytes 786432 | tf_op jit(solution)/shard_map/all_to_all | solution.py:421
  135.6 36.8 %copy-start.16 = (s32[256]{0:T(256)S(1)}, s32[256]{0:T(256)}, u32[]{:S(2)}) copy-start(s32[256]{0:T(256)} %param.19) | copy-start | bytes 3076
  136.3 3.1 %collective-permute-start.11 = (bf16[2,128,128]{2,1,0:T(8,128)(2,1)S(1)}, bf16[2,128,128]{2,1,0:T(8,128)(2,1)S(1)}, u32[]{:S(2)}, u32[]{:S(2)}) collective-permute-start(bf16[2,128,128]{2,1,0:T(8,128)(2,1)S(1)} %get-tuple-element.33), channel_id=1, source_target_pairs={{0,8},{8,0},{16,24},{24,16},{32,40},{40,32},{48,56},{56,48},{64,72... | collective-permute-start | bytes 196616 | tf_op jit(solution)/shard_map/ppermute | solution.py:417
  143.7 0.8 copy-start.5
  144.6 0.8 copy-start.11
  159.0 13.1 %collective-permute-start.12 = (bf16[64,512]{1,0:T(8,128)(2,1)S(1)}, bf16[64,512]{1,0:T(8,128)(2,1)S(1)}, u32[]{:S(2)}, u32[]{:S(2)}) collective-permute-start(bf16[64,512]{1,0:T(8,128)(2,1)S(1)} %reduce_sum.30), channel_id=1, source_target_pairs={{0,4},{1,5},{2,6},{3,7},{4,0},{5,1},{6,2},{7,3},{8,12},{9,13},{10,... | collective-permute-start | bytes 196616 | tf_op jit(solution)/shard_map/ppermute | solution.py:435
  (3 other events, 2.1 us)

commit v20 on v18

--- a/solution.py
+++ b/solution.py
@@ -174,7 +174,7 @@
 
 def near_kernel(
     at_ref, own_hbm, beside_hbm, gain_ref, own_taps, got_taps, near_ref, unembed_ref,
-    gained_ref, scale_ref, out_ref, terms_ref, pieces_ref, tokens, taps, sems,
+    gained_ref, scale_ref, out_ref, terms_ref, pieces_ref, tokens, taps, sems, spare,
 ):
     core, start = at_ref[2], at_ref[3] * 2048
     gain = gain_ref[...]
@@ -371,10 +371,15 @@
             shape((16, 32, 128), BF16),
         ),
         [SCALARS, IN_HBM, IN_HBM] + whole(1) + [IN_HBM, IN_HBM] + whole(2),
-        [pltpu.VMEM((2, 256, 4096), BF16), pltpu.VMEM((2, 256, 256), BF16), pltpu.SemaphoreType.DMA((3, 4))],
+        [
+            pltpu.VMEM((2, 256, 4096), BF16),
+            pltpu.VMEM((2, 256, 256), BF16),
+            pltpu.SemaphoreType.DMA((3, 4)),
+            pltpu.VMEM((40, 2048, 256), BF16),
+        ],
         8 * 10**8,
         (at, tokens_in, beside, pre_gain.reshape(1, 4096), taps, taps_got, near, w_unembed),
-        mib=12,
+        mib=56,
     )
     signal, gate = call(
         proj_kernel,

time: 178 us -> 185 us (1.039)
  local copies, waits for them, and re-layouts: 3.32 us -> 7.5 us
  Pallas kernels: 14.2 us -> 17.6 us
    unnamed x18 -> x28, local copies, waits for them, and re-layouts: 2.39 us -> 5.97 us
    pallas_call x10, Pallas kernels: 14.2 us -> 17.6 us  [call(): pl.pallas_call(kernel, out_shape=outs, in_specs=specs, out_specs=out_spec...]
  transfers between devices with their start and end apart: 17 -> 17, of which waited for: 7 -> 6; matrix products, arithmetic and copies ran while one was open for 1% -> 2% of each run, Pallas kernels for 5% -> 7%
where the time goes in v20:
time: 185 us; the launch traced here: 183 us
  starting transfers between devices  86.7 us (47%)
  waiting for transfers between devices  36.8 us (20%)
  blocking collectives  32 us (17%)
  Pallas kernels  17.6 us (10%)
  local copies, waits for them, and re-layouts  7.5 us (4%)
    pallas_call x10, Pallas kernels, call(): pl.pallas_call(kernel, out_shape=outs, in_specs=specs, out_specs=out_spec...  17.6 us
    ppermute x1, starting transfers between devices, per_device(): far = lax.ppermute(first, 'ctx', PERM_Z)  15.7 us
    all_to_all x1, starting transfers between devices, per_device(): terms = lax.all_to_all(terms, 'tp', 0, 0, tiled=True)  12.9 us
    all_to_all x1, blocking collectives, per_device(): lax.all_to_all(logits.reshape(4, 64, 512), 'tp', 0, 0, axis_index_groups=...  12.7 us
    ppermute x3, starting transfers between devices, per_device(): lax.ppermute(along, 'ctx', PERM_Y[k])  11.6 us
    all_to_all x1, blocking collectives, per_device(): lax.all_to_all(signal, 'ctx', 0, 0, axis_index_groups=GROUPS_CORE, tiled=...  11.5 us
    ppermute x1, starting transfers between devices, per_device(): before = lax.ppermute(got, 'ctx', PERM_Z_UP)  10.6 us
    all_to_all x1, waiting for transfers between devices, per_device(): terms = lax.all_to_all(terms, 'tp', 0, 0, tiled=True)  10.2 us
  transfers between devices with their start and end apart: 17, of which 6 were waited for; matrix products, arithmetic and copies ran while one was open for 2% of the time, Pallas kernels for 7%

profile of v20, /device:TPU:6, one launch (start us, length us, event | category | flops | bytes accessed | tf_op | source)
XLA Modules:
  0.0 183.5 jit_solution(12066335491559290044)
XLA Ops:
  0.0 1.9 %collective-permute-start = (bf16[256,4096]{1,0:T(8,128)(2,1)}, bf16[256,4096]{1,0:T(8,128)(2,1)}, u32[]{:S(2)}, u32[]{:S(2)}) collective-permute-start(bf16[256,4096]{1,0:T(8,128)(2,1)} %own_hbm.1), channel_id=1, source_target_pairs={{0,8},{8,0},{16,24},{24,16},{32,40},{40,32},{48,56},{56,48},{64,72... | collective-permute-start | bytes 6291464 | tf_op jit(solution)/shard_map/ppermute | solution.py:341
  1.9 2.4 %collective-permute-start.1 = (bf16[3,64,256]{2,1,0:T(8,128)(2,1)}, bf16[3,64,256]{2,1,0:T(8,128)(2,1)S(1)}, u32[]{:S(2)}, u32[]{:S(2)}) collective-permute-start(bf16[3,64,256]{2,1,0:T(8,128)(2,1)} %bitcast.31), channel_id=1, source_target_pairs={{0,8},{8,0},{16,24},{24,16},{32,40},{40,32},{48,56},{56,48},{64,72... | collective-permute-start | bytes 294920 | tf_op jit(solution)/shard_map/ppermute | solution.py:338
  5.2 1.2 collective-permute-done.1.got_ref
  7.2 15.7 %collective-permute-start.2 = (bf16[512,128]{1,0:T(8,128)(2,1)S(1)}, bf16[512,128]{1,0:T(8,128)(2,1)S(1)}, u32[]{:S(2)}, u32[]{:S(2)}) collective-permute-start(bf16[512,128]{1,0:T(8,128)(2,1)S(1)} %shard_map.118.first_ref), channel_id=1, source_target_pairs={{0,256},{8,264},{16,272},{24,280},{32,288},{40,296},{48,304},{56,3... | collective-permute-start | bytes 393224 | tf_op jit(solution)/shard_map/ppermute | solution.py:343
  23.7 4.8 %all-to-all-start = ((bf16[4,384,128]{2,1,0:T(8,128)(2,1)}), bf16[4,384,128]{2,1,0:T(8,128)(2,1)S(1)}, u32[]{:S(2)}, u32[]{:S(2)}) async-start(bf16[4,384,128]{2,1,0:T(8,128)(2,1)} %shard_map.119), calls=%async_computation | async-start | bytes 786432 | tf_op jit(solution)/shard_map/all_to_all | solution.py:342
  28.5 3.5 %collective-permute-start.3 = (bf16[384,128]{1,0:T(8,128)(2,1)S(1)}, bf16[384,128]{1,0:T(8,128)(2,1)S(1)}, u32[]{:S(2)}, u32[]{:S(2)}) collective-permute-start(bf16[384,128]{1,0:T(8,128)(2,1)S(1)} %get-tuple-element.38), channel_id=1, source_target_pairs={{0,64},{8,72},{16,80},{24,88},{32,96},{40,104},{48,112},{56,120},{... | collective-permute-start | bytes 294920 | tf_op jit(solution)/shard_map/ppermute | solution.py:346
  32.0 4.8 %collective-permute-start.4 = (bf16[384,128]{1,0:T(8,128)(2,1)S(1)}, bf16[384,128]{1,0:T(8,128)(2,1)S(1)}, u32[]{:S(2)}, u32[]{:S(2)}) collective-permute-start(bf16[384,128]{1,0:T(8,128)(2,1)S(1)} %get-tuple-element.38), channel_id=1, source_target_pairs={{0,128},{8,136},{16,144},{24,152},{32,160},{40,168},{48,176},{56,1... | collective-permute-start | bytes 294920 | tf_op jit(solution)/shard_map/ppermute | solution.py:346
  36.8 3.3 %collective-permute-start.5 = (bf16[384,128]{1,0:T(8,128)(2,1)S(1)}, bf16[384,128]{1,0:T(8,128)(2,1)S(1)}, u32[]{:S(2)}, u32[]{:S(2)}) collective-permute-start(bf16[384,128]{1,0:T(8,128)(2,1)S(1)} %get-tuple-element.38), channel_id=1, source_target_pairs={{0,192},{8,200},{16,208},{24,216},{32,224},{40,232},{48,240},{56,2... | collective-permute-start | bytes 294920 | tf_op jit(solution)/shard_map/ppermute | solution.py:346
  40.1 3.2 %collective-permute-done.5 = bf16[384,128]{1,0:T(8,128)(2,1)S(1)} collective-permute-done((bf16[384,128]{1,0:T(8,128)(2,1)S(1)}, bf16[384,128]{1,0:T(8,128)(2,1)S(1)}, u32[]{:S(2)}, u32[]{:S(2)}) %collective-permute-start.5) | collective-permute-done | bytes 98336 | tf_op jit(solution)/shard_map/ppermute | solution.py:346
  43.4 1.3 shard_map.120
  44.7 4.5 %all-to-all-start.1 = ((bf16[4,1600,128]{2,1,0:T(8,128)(2,1)}), bf16[4,1600,128]{2,1,0:T(8,128)(2,1)}, u32[]{:S(2)}, u32[]{:S(2)}) async-start(bf16[4,1600,128]{2,1,0:T(8,128)(2,1)} %shard_map.120), calls=%async_computation.1 | async-start | bytes 3276800 | tf_op jit(solution)/shard_map/all_to_all | solution.py:358
  49.3 1.9 %collective-permute-start.7 = (bf16[4,384,128]{2,1,0:T(8,128)(2,1)S(1)}, bf16[4,384,128]{2,1,0:T(8,128)(2,1)S(1)}, u32[]{:S(2)}, u32[]{:S(2)}) collective-permute-start(bf16[4,384,128]{2,1,0:T(8,128)(2,1)S(1)} %pad_maximum_fusion.f0), channel_id=1, source_target_pairs={{0,16},{8,24},{16,32},{24,40},{32,48},{40,56},{48,0},{56,8},{64,80... | collective-permute-start | bytes 1179656 | tf_op jit(solution)/shard_map/ppermute | solution.py:360
  51.2 4.8 %collective-permute-start.8 = (bf16[4,384,128]{2,1,0:T(8,128)(2,1)S(1)}, bf16[4,384,128]{2,1,0:T(8,128)(2,1)S(1)}, u32[]{:S(2)}, u32[]{:S(2)}) collective-permute-start(bf16[4,384,128]{2,1,0:T(8,128)(2,1)S(1)} %pad_maximum_fusion.f0), channel_id=1, source_target_pairs={{0,32},{8,40},{16,48},{24,56},{32,0},{40,8},{48,16},{56,24},{64,96... | collective-permute-start | bytes 1179656 | tf_op jit(solution)/shard_map/ppermute | solution.py:360
  56.0 1.9 %collective-permute-start.9 = (bf16[4,384,128]{2,1,0:T(8,128)(2,1)S(1)}, bf16[4,384,128]{2,1,0:T(8,128)(2,1)S(1)}, u32[]{:S(2)}, u32[]{:S(2)}) collective-permute-start(bf16[4,384,128]{2,1,0:T(8,128)(2,1)S(1)} %pad_maximum_fusion.f0), channel_id=1, source_target_pairs={{0,48},{8,56},{16,0},{24,8},{32,16},{40,24},{48,32},{56,40},{64,11... | collective-permute-start | bytes 1179656 | tf_op jit(solution)/shard_map/ppermute | solution.py:360
  58.0 1.9 %collective-permute-start.6 = (bf16[256,256]{1,0:T(8,128)(2,1)S(1)}, bf16[256,256]{1,0:T(8,128)(2,1)S(1)}, u32[]{:S(2)}, u32[]{:S(2)}) collective-permute-start(bf16[256,256]{1,0:T(8,128)(2,1)S(1)} %copy-done.9), channel_id=1, source_target_pairs={{0,8},{8,0},{16,24},{24,16},{32,40},{40,32},{48,56},{56,48},{64,72... | collective-permute-start | bytes 393224 | tf_op jit(solution)/shard_map/ppermute | solution.py:361
  61.2 7.6 %all-to-all-done.1.near_ref = bf16[4,1600,128]{2,1,0:T(8,128)(2,1)} async-done(((bf16[4,1600,128]{2,1,0:T(8,128)(2,1)}), bf16[4,1600,128]{2,1,0:T(8,128)(2,1)}, u32[]{:S(2)}, u32[]{:S(2)}) %all-to-all-start.1) | async-done | bytes 1638432 | tf_op jit(solution)/shard_map/all_to_all | solution.py:358
  68.8 8.0 %shard_map.121 = (bf16[2,256,4096]{2,1,0:T(8,128)(2,1)}, f32[2,256,128]{2,1,0:T(8,128)}, f32[2,256,384]{2,1,0:T(8,128)}, bf16[8,32,128]{2,1,0:T(8,128)(2,1)}, bf16[16,32,128]{2,1,0:T(8,128)(2,1)}) custom-call(s32[4]{0:T(128)} %pad_add_fusion.at_ref, bf16[256,4096]{1,0:T(8,128)(2,1)} %own_hbm.1, bf16[256,4096]{1,0:T(8,128)(2,1)} %collective-permute-done.beside_hbm, ...), custom_call_target="tpu_custom_call" | custom-call | flops 800000000 | bytes 4194304 | tf_op jit(solution)/shard_map/pallas_call | solution.py:281
  76.9 2.2 %copy-done = bf16[2,256,4096]{2,1,0:T(8,128)(2,1)S(1)} copy-done((bf16[2,256,4096]{2,1,0:T(8,128)(2,1)S(1)}, bf16[2,256,4096]{2,1,0:T(8,128)(2,1)}, u32[]{:S(2)}) %copy-start) | copy-done | bytes 4194328
  82.0 3.1 %shard_map.122 = (bf16[16,64,128]{2,1,0:T(8,128)(2,1)S(1)}, bf16[2,2,128,128]{3,2,1,0:T(8,128)(2,1)S(1)}) custom-call(s32[4]{0:T(128)S(1)} %copy-done.7, bf16[2,256,4096]{2,1,0:T(8,128)(2,1)S(1)} %copy-done, f32[2,256,128]{2,1,0:T(8,128)S(1)} %copy-done.3, f32[2,256,384]{2,1,0:T(8,128)S(1)} %copy-done.1, bf16[16,32,128]{2,1,0:T(8,128)(2,1)S(1)} %copy-done.5, ...), custom_call_target="tpu_custom_call" | custom-call | flops 800000000 | bytes 4194304 | tf_op jit(solution)/shard_map/pallas_call | solution.py:281
  85.2 11.5 %all_to_all.35.got_ref = bf16[16,64,128]{2,1,0:T(8,128)(2,1)S(1)} all-to-all(bf16[16,64,128]{2,1,0:T(8,128)(2,1)S(1)} %get-tuple-element.27), channel_id=1, replica_groups={{0,16,32,48,64,80,96,112,128,144,160,176,192,208,224,240},{8,24,40,56,7..., dimensions={0} | all-to-all | bytes 524288 | tf_op jit(solution)/shard_map/all_to_all | solution.py:392
  96.7 10.6 %collective-permute-start.10 = (bf16[16,64,128]{2,1,0:T(8,128)(2,1)S(1)}, bf16[16,64,128]{2,1,0:T(8,128)(2,1)S(1)}, u32[]{:S(2)}, u32[]{:S(2)}) collective-permute-start(bf16[16,64,128]{2,1,0:T(8,128)(2,1)S(1)} %all_to_all.35.got_ref), channel_id=1, source_target_pairs={{0,256},{8,264},{16,272},{24,280},{32,288},{40,296},{48,304},{56,3... | collective-permute-start | bytes 786440 | tf_op jit(solution)/shard_map/ppermute | solution.py:393
  107.3 12.9 %all-to-all-start.3 = ((bf16[8,32,128]{2,1,0:T(8,128)(2,1)}), bf16[8,32,128]{2,1,0:T(8,128)(2,1)S(1)}, u32[]{:S(2)}, u32[]{:S(2)}) async-start(bf16[8,32,128]{2,1,0:T(8,128)(2,1)} %get-tuple-element.31), calls=%async_computation.3 | async-start | bytes 131072 | tf_op jit(solution)/shard_map/all_to_all | solution.py:395
  121.3 1.5 shard_map.124.conv_ref
  122.8 10.2 %all-to-all-done.3.terms_ref = bf16[8,32,128]{2,1,0:T(8,128)(2,1)S(1)} async-done(((bf16[8,32,128]{2,1,0:T(8,128)(2,1)}), bf16[8,32,128]{2,1,0:T(8,128)(2,1)S(1)}, u32[]{:S(2)}, u32[]{:S(2)}) %all-to-all-start.3) | async-done | bytes 65568 | tf_op jit(solution)/shard_map/all_to_all | solution.py:395
  133.8 6.2 %all-to-all-start.4 = ((bf16[32,48,128]{2,1,0:T(8,128)(2,1)}), bf16[32,48,128]{2,1,0:T(8,128)(2,1)S(1)}, u32[]{:S(2)}, u32[]{:S(2)}) async-start(bf16[32,48,128]{2,1,0:T(8,128)(2,1)} %shard_map.125), calls=%async_computation.4 | async-start | bytes 786432 | tf_op jit(solution)/shard_map/all_to_all | solution.py:401
  140.0 2.1 %collective-permute-start.11 = (bf16[2,128,128]{2,1,0:T(8,128)(2,1)S(1)}, bf16[2,128,128]{2,1,0:T(8,128)(2,1)S(1)}, u32[]{:S(2)}, u32[]{:S(2)}) collective-permute-start(bf16[2,128,128]{2,1,0:T(8,128)(2,1)S(1)} %get-tuple-element.35), channel_id=1, source_target_pairs={{0,8},{8,0},{16,24},{24,16},{32,40},{40,32},{48,56},{56,48},{64,72... | collective-permute-start | bytes 196616 | tf_op jit(solution)/shard_map/ppermute | solution.py:397
  142.1 1.2 fusion.base_ref
  143.4 4.7 %all-to-all-done.4.got_ref = bf16[32,48,128]{2,1,0:T(8,128)(2,1)S(1)} async-done(((bf16[32,48,128]{2,1,0:T(8,128)(2,1)}), bf16[32,48,128]{2,1,0:T(8,128)(2,1)S(1)}, u32[]{:S(2)}, u32[]{:S(2)}) %all-to-all-start.4) | async-done | bytes 393248 | tf_op jit(solution)/shard_map/all_to_all | solution.py:401
  148.5 12.7 %all_to_all.36 = bf16[4,64,512]{2,1,0:T(8,128)(2,1)S(1)} all-to-all(bf16[4,64,512]{2,1,0:T(8,128)(2,1)S(1)} %bitcast.26), channel_id=1, replica_groups={{0,1,2,3},{4,5,6,7},{8,9,10,11},{12,13,14,15},{16,17,18,19},{20,21,22,2..., dimensions={0} | all-to-all | bytes 524288 | tf_op jit(solution)/shard_map/all_to_all | solution.py:413
  161.2 3.5 %collective-permute-start.12 = (bf16[64,512]{1,0:T(8,128)(2,1)S(1)}, bf16[64,512]{1,0:T(8,128)(2,1)S(1)}, u32[]{:S(2)}, u32[]{:S(2)}) collective-permute-start(bf16[64,512]{1,0:T(8,128)(2,1)S(1)} %reduce_sum.30), channel_id=1, source_target_pairs={{0,4},{1,5},{2,6},{3,7},{4,0},{5,1},{6,2},{7,3},{8,12},{9,13},{10,... | collective-permute-start | bytes 196616 | tf_op jit(solution)/shard_map/ppermute | solution.py:415
  164.8 9.7 %collective-permute-done.12 = bf16[64,512]{1,0:T(8,128)(2,1)S(1)} collective-permute-done((bf16[64,512]{1,0:T(8,128)(2,1)S(1)}, bf16[64,512]{1,0:T(8,128)(2,1)S(1)}, u32[]{:S(2)}, u32[]{:S(2)}) %collective-permute-start.12) | collective-permute-done | bytes 65568 | tf_op jit(solution)/shard_map/ppermute | solution.py:415
  175.0 7.9 %all_to_all.37.scores_ref = f32[4,1,64]{2,1,0:T(1,128)S(1)} all-to-all(f32[4,1,64]{2,1,0:T(1,128)S(1)} %broadcast_in_dim.7), channel_id=1, replica_groups={{0,1,2,3},{4,5,6,7},{8,9,10,11},{12,13,14,15},{16,17,18,19},{20,21,22,2..., dimensions={0} | all-to-all | bytes 2048 | tf_op jit(solution)/shard_map/all_to_all | solution.py:426
  (56 shorter events, 10.1 us)
Async XLA Ops:
  0.0 68.8 %collective-permute-start = (bf16[256,4096]{1,0:T(8,128)(2,1)}, bf16[256,4096]{1,0:T(8,128)(2,1)}, u32[]{:S(2)}, u32[]{:S(2)}) collective-permute-start(bf16[256,4096]{1,0:T(8,128)(2,1)} %own_hbm.1), channel_id=1, source_target_pairs={{0,8},{8,0},{16,24},{24,16},{32,40},{40,32},{48,56},{56,48},{64,72... | collective-permute-start | bytes 6291464 | tf_op jit(solution)/shard_map/ppermute | solution.py:341
  1.9 4.5 %collective-permute-start.1 = (bf16[3,64,256]{2,1,0:T(8,128)(2,1)}, bf16[3,64,256]{2,1,0:T(8,128)(2,1)S(1)}, u32[]{:S(2)}, u32[]{:S(2)}) collective-permute-start(bf16[3,64,256]{2,1,0:T(8,128)(2,1)} %bitcast.31), channel_id=1, source_target_pairs={{0,8},{8,0},{16,24},{24,16},{32,40},{40,32},{48,56},{56,48},{64,72... | collective-permute-start | bytes 294920 | tf_op jit(solution)/shard_map/ppermute | solution.py:338
  6.4 0.8 copy-start.6
  7.2 21.3 %collective-permute-start.2 = (bf16[512,128]{1,0:T(8,128)(2,1)S(1)}, bf16[512,128]{1,0:T(8,128)(2,1)S(1)}, u32[]{:S(2)}, u32[]{:S(2)}) collective-permute-start(bf16[512,128]{1,0:T(8,128)(2,1)S(1)} %shard_map.118.first_ref), channel_id=1, source_target_pairs={{0,256},{8,264},{16,272},{24,280},{32,288},{40,296},{48,304},{56,3... | collective-permute-start | bytes 393224 | tf_op jit(solution)/shard_map/ppermute | solution.py:343
  23.7 19.7 %all-to-all-start = ((bf16[4,384,128]{2,1,0:T(8,128)(2,1)}), bf16[4,384,128]{2,1,0:T(8,128)(2,1)S(1)}, u32[]{:S(2)}, u32[]{:S(2)}) async-start(bf16[4,384,128]{2,1,0:T(8,128)(2,1)} %shard_map.119), calls=%async_computation | async-start | bytes 786432 | tf_op jit(solution)/shard_map/all_to_all | solution.py:342
  28.5 11.6 %collective-permute-start.3 = (bf16[384,128]{1,0:T(8,128)(2,1)S(1)}, bf16[384,128]{1,0:T(8,128)(2,1)S(1)}, u32[]{:S(2)}, u32[]{:S(2)}) collective-permute-start(bf16[384,128]{1,0:T(8,128)(2,1)S(1)} %get-tuple-element.38), channel_id=1, source_target_pairs={{0,64},{8,72},{16,80},{24,88},{32,96},{40,104},{48,112},{56,120},{... | collective-permute-start | bytes 294920 | tf_op jit(solution)/shard_map/ppermute | solution.py:346
  32.0 8.1 %collective-permute-start.4 = (bf16[384,128]{1,0:T(8,128)(2,1)S(1)}, bf16[384,128]{1,0:T(8,128)(2,1)S(1)}, u32[]{:S(2)}, u32[]{:S(2)}) collective-permute-start(bf16[384,128]{1,0:T(8,128)(2,1)S(1)} %get-tuple-element.38), channel_id=1, source_target_pairs={{0,128},{8,136},{16,144},{24,152},{32,160},{40,168},{48,176},{56,1... | collective-permute-start | bytes 294920 | tf_op jit(solution)/shard_map/ppermute | solution.py:346
  36.8 6.5 %collective-permute-start.5 = (bf16[384,128]{1,0:T(8,128)(2,1)S(1)}, bf16[384,128]{1,0:T(8,128)(2,1)S(1)}, u32[]{:S(2)}, u32[]{:S(2)}) collective-permute-start(bf16[384,128]{1,0:T(8,128)(2,1)S(1)} %get-tuple-element.38), channel_id=1, source_target_pairs={{0,192},{8,200},{16,208},{24,216},{32,224},{40,232},{48,240},{56,2... | collective-permute-start | bytes 294920 | tf_op jit(solution)/shard_map/ppermute | solution.py:346
  44.7 13.2 %copy-start.9 = (bf16[256,256]{1,0:T(8,128)(2,1)S(1)}, bf16[256,256]{1,0:T(8,128)(2,1)}, u32[]{:S(2)}) copy-start(bf16[256,256]{1,0:T(8,128)(2,1)} %own_taps) | copy-start | bytes 393220
  44.7 15.2 %copy-start.11 = (bf16[4096]{0:T(1024)(128)(2,1)S(1)}, bf16[4096]{0:T(1024)(128)(2,1)}, u32[]{:S(2)}) copy-start(bf16[4096]{0:T(1024)(128)(2,1)} %param.13) | copy-start | bytes 24580
  44.7 24.0 %all-to-all-start.1 = ((bf16[4,1600,128]{2,1,0:T(8,128)(2,1)}), bf16[4,1600,128]{2,1,0:T(8,128)(2,1)}, u32[]{:S(2)}, u32[]{:S(2)}) async-start(bf16[4,1600,128]{2,1,0:T(8,128)(2,1)} %shard_map.120), calls=%async_computation.1 | async-start | bytes 3276800 | tf_op jit(solution)/shard_map/all_to_all | solution.py:358
  49.3 27.5 %collective-permute-start.7 = (bf16[4,384,128]{2,1,0:T(8,128)(2,1)S(1)}, bf16[4,384,128]{2,1,0:T(8,128)(2,1)S(1)}, u32[]{:S(2)}, u32[]{:S(2)}) collective-permute-start(bf16[4,384,128]{2,1,0:T(8,128)(2,1)S(1)} %pad_maximum_fusion.f0), channel_id=1, source_target_pairs={{0,16},{8,24},{16,32},{24,40},{32,48},{40,56},{48,0},{56,8},{64,80... | collective-permute-start | bytes 1179656 | tf_op jit(solution)/shard_map/ppermute | solution.py:360
  51.2 25.6 %collective-permute-start.8 = (bf16[4,384,128]{2,1,0:T(8,128)(2,1)S(1)}, bf16[4,384,128]{2,1,0:T(8,128)(2,1)S(1)}, u32[]{:S(2)}, u32[]{:S(2)}) collective-permute-start(bf16[4,384,128]{2,1,0:T(8,128)(2,1)S(1)} %pad_maximum_fusion.f0), channel_id=1, source_target_pairs={{0,32},{8,40},{16,48},{24,56},{32,0},{40,8},{48,16},{56,24},{64,96... | collective-permute-start | bytes 1179656 | tf_op jit(solution)/shard_map/ppermute | solution.py:360
  56.0 20.8 %collective-permute-start.9 = (bf16[4,384,128]{2,1,0:T(8,128)(2,1)S(1)}, bf16[4,384,128]{2,1,0:T(8,128)(2,1)S(1)}, u32[]{:S(2)}, u32[]{:S(2)}) collective-permute-start(bf16[4,384,128]{2,1,0:T(8,128)(2,1)S(1)} %pad_maximum_fusion.f0), channel_id=1, source_target_pairs={{0,48},{8,56},{16,0},{24,8},{32,16},{40,24},{48,32},{56,40},{64,11... | collective-permute-start | bytes 1179656 | tf_op jit(solution)/shard_map/ppermute | solution.py:360
  58.0 3.2 %collective-permute-start.6 = (bf16[256,256]{1,0:T(8,128)(2,1)S(1)}, bf16[256,256]{1,0:T(8,128)(2,1)S(1)}, u32[]{:S(2)}, u32[]{:S(2)}) collective-permute-start(bf16[256,256]{1,0:T(8,128)(2,1)S(1)} %copy-done.9), channel_id=1, source_target_pairs={{0,8},{8,0},{16,24},{24,16},{32,40},{40,32},{48,56},{56,48},{64,72... | collective-permute-start | bytes 393224 | tf_op jit(solution)/shard_map/ppermute | solution.py:361
  61.1 15.7 %copy-start.7 = (s32[4]{0:T(128)S(1)}, s32[4]{0:T(128)}, u32[]{:S(2)}) copy-start(s32[4]{0:T(128)} %pad_add_fusion.at_ref) | copy-start | bytes 52
  61.2 7.6 %copy-start.10 = (bf16[256,256]{1,0:T(8,128)(2,1)}, bf16[256,256]{1,0:T(8,128)(2,1)S(1)}, u32[]{:S(2)}) copy-start(bf16[256,256]{1,0:T(8,128)(2,1)S(1)} %collective-permute-done.6.got_taps) | copy-start | bytes 393220
  76.8 2.2 %copy-start = (bf16[2,256,4096]{2,1,0:T(8,128)(2,1)S(1)}, bf16[2,256,4096]{2,1,0:T(8,128)(2,1)}, u32[]{:S(2)}) copy-start(bf16[2,256,4096]{2,1,0:T(8,128)(2,1)} %get-tuple-element.22.gained_ref) | copy-start | bytes 12582916
  79.0 1.1 copy-start.1
  80.2 0.9 copy-start.3
  81.1 0.9 copy-start.5
  82.0 38.2 %copy-start.2 = (bf16[832,256]{1,0:T(8,128)(2,1)S(1)}, bf16[832,256]{1,0:T(8,128)(2,1)}, u32[]{:S(2)}) copy-start(bf16[832,256]{1,0:T(8,128)(2,1)} %constant.103.clone.matrices) | copy-start | bytes 1277956
  82.0 38.2 %copy-start.4 = (f32[128,256]{1,0:T(8,128)S(1)}, f32[128,256]{1,0:T(8,128)}, u32[]{:S(2)}) copy-start(f32[128,256]{1,0:T(8,128)} %constant.104.clone.twiddles) | copy-start | bytes 393220
  96.7 24.6 %collective-permute-start.10 = (bf16[16,64,128]{2,1,0:T(8,128)(2,1)S(1)}, bf16[16,64,128]{2,1,0:T(8,128)(2,1)S(1)}, u32[]{:S(2)}, u32[]{:S(2)}) collective-permute-start(bf16[16,64,128]{2,1,0:T(8,128)(2,1)S(1)} %all_to_all.35.got_ref), channel_id=1, source_target_pairs={{0,256},{8,264},{16,272},{24,280},{32,288},{40,296},{48,304},{56,3... | collective-permute-start | bytes 786440 | tf_op jit(solution)/shard_map/ppermute | solution.py:393
  107.3 25.7 %all-to-all-start.3 = ((bf16[8,32,128]{2,1,0:T(8,128)(2,1)}), bf16[8,32,128]{2,1,0:T(8,128)(2,1)S(1)}, u32[]{:S(2)}, u32[]{:S(2)}) async-start(bf16[8,32,128]{2,1,0:T(8,128)(2,1)} %get-tuple-element.31), calls=%async_computation.3 | async-start | bytes 131072 | tf_op jit(solution)/shard_map/all_to_all | solution.py:395
  121.2 20.9 %copy-start.8 = (bf16[512,512]{1,0:T(8,128)(2,1)S(1)}, bf16[512,512]{1,0:T(8,128)(2,1)}, u32[]{:S(2)}) copy-start(bf16[512,512]{1,0:T(8,128)(2,1)} %unembed_ref.1) | copy-start | bytes 1572868
  133.8 30.9 %copy-start.13 = (s32[256]{0:T(256)S(1)}, s32[256]{0:T(256)}, u32[]{:S(2)}) copy-start(s32[256]{0:T(256)} %param.18) | copy-start | bytes 3076
  133.8 14.3 %all-to-all-start.4 = ((bf16[32,48,128]{2,1,0:T(8,128)(2,1)}), bf16[32,48,128]{2,1,0:T(8,128)(2,1)S(1)}, u32[]{:S(2)}, u32[]{:S(2)}) async-start(bf16[32,48,128]{2,1,0:T(8,128)(2,1)} %shard_map.125), calls=%async_computation.4 | async-start | bytes 786432 | tf_op jit(solution)/shard_map/all_to_all | solution.py:401
  140.0 34.9 %copy-start.12 = (s32[256]{0:T(256)S(1)}, s32[256]{0:T(256)}, u32[]{:S(2)}) copy-start(s32[256]{0:T(256)} %param.19) | copy-start | bytes 3076
  140.0 3.3 %collective-permute-start.11 = (bf16[2,128,128]{2,1,0:T(8,128)(2,1)S(1)}, bf16[2,128,128]{2,1,0:T(8,128)(2,1)S(1)}, u32[]{:S(2)}, u32[]{:S(2)}) collective-permute-start(bf16[2,128,128]{2,1,0:T(8,128)(2,1)S(1)} %get-tuple-element.35), channel_id=1, source_target_pairs={{0,8},{8,0},{16,24},{24,16},{32,40},{40,32},{48,56},{56,48},{64,72... | collective-permute-start | bytes 196616 | tf_op jit(solution)/shard_map/ppermute | solution.py:397
  161.2 13.4 %collective-permute-start.12 = (bf16[64,512]{1,0:T(8,128)(2,1)S(1)}, bf16[64,512]{1,0:T(8,128)(2,1)S(1)}, u32[]{:S(2)}, u32[]{:S(2)}) collective-permute-start(bf16[64,512]{1,0:T(8,128)(2,1)S(1)} %reduce_sum.30), channel_id=1, source_target_pairs={{0,4},{1,5},{2,6},{3,7},{4,0},{5,1},{6,2},{7,3},{8,12},{9,13},{10,... | collective-permute-start | bytes 196616 | tf_op jit(solution)/shard_map/ppermute | solution.py:415
